TPU v7x, 32 devices: a whole 2x2x4 slice. The times are simulated.
32 devices in a mesh: tm: 4 (over x, core), tile: 8 (over z, y).
Axes of the slice: x: 2, y: 2, z: 4, core: 2. Of those that a mesh axis runs over, the one named last changes fastest.
Arguments:
- gains: bfloat16 [32, 768, 768], P('tm', 'tile'), may hold values from -1.5 to 1.5
- increments: float32 [32, 768, 768], P('tm', 'tile'), may hold values from -2 to 5
- terminal: float32 [768, 768], P('tile'), may hold values from -3 to 6
Outputs:
- smoothed: float32 [32, 768, 768], P('tm', 'tile')
All inputs are finite; a program needn't handle non-finite values.
Results may differ from a plain program's by a relative error of at most 0.04.
Values may be sent and summed in bfloat16 or wider, within the bound.
No kernel may reach another device: no remote copies, remote signals or barrier semaphores. Data moves between devices by JAX's collectives and lax.ppermute only.
A program may use at most 576 MiB of HBM per device.

v0:
```python
import jax
import jax.numpy as jnp
from jax import lax
from jax.sharding import PartitionSpec as P


def carried_in(array, axis, join, neutral):
    count = lax.axis_size(axis)
    place = lax.axis_index(axis)
    ahead = count - 1 - place
    gathered = jax.tree.map(
        lambda a, kind: lax.all_gather(a.astype(kind), axis),
        array,
        jax.tree.map(lambda a: jnp.bfloat16 if a.dtype == jnp.float32 else a.dtype, array),
    )
    state = jax.tree.map(lambda a, e: jnp.zeros_like(a) + jnp.asarray(e, a.dtype), array, neutral)

    def carried_one(turn, state):
        source = count - 1 - turn
        return join(
            state,
            jax.tree.map(
                lambda a, own: lax.dynamic_index_in_dim(a, source, 0, False).astype(own.dtype),
                gathered,
                array,
            ),
        )

    return lax.fori_loop(0, ahead, carried_one, state)


def spread(value, axis, source):
    kept = jnp.where(lax.axis_index(axis) == source, value, 0).astype(value.dtype)
    return lax.psum(kept, axis)


def prefix(part, axis, combine, identity):
    count = lax.axis_size(axis)
    place = lax.axis_index(axis)
    ahead = count - 1 - place
    gathered = jax.tree.map(lambda a: lax.all_gather(a, axis), part)
    state = jax.tree.map(lambda a, e: jnp.zeros_like(a) + jnp.asarray(e, a.dtype), part, identity)

    def prefix_one(turn, state):
        source = count - 1 - turn
        return combine(
            state, jax.tree.map(lambda a: lax.dynamic_index_in_dim(a, source, 0, False), gathered)
        )

    return lax.fori_loop(0, ahead, prefix_one, state)


def transpose_dot(left, right):
    return lax.dot_general(
        left, right, (((1,), (1,)), ((), ())), preferred_element_type=jnp.float32
    )


def combine_affine_pair(earlier, later):
    high_factor, high_covariance = earlier
    low_factor, lower_covariance = later
    factor = jnp.dot(low_factor, high_factor, preferred_element_type=jnp.float32).astype(
        jnp.bfloat16
    )
    product = jnp.dot(low_factor, high_covariance, preferred_element_type=jnp.float32).astype(
        jnp.bfloat16
    )
    covariance = (transpose_dot(product, low_factor) + lower_covariance.astype(jnp.float32)).astype(
        jnp.bfloat16
    )
    return (factor, covariance)


def local(gains, increments, terminal):
    whole_gains = lax.all_to_all(gains, "tile", split_axis=0, concat_axis=1, tiled=True)
    whole_increments = lax.all_to_all(
        increments.astype(jnp.bfloat16), "tile", split_axis=0, concat_axis=1, tiled=True
    ).astype(increments.dtype)
    cell_count = whole_gains.shape[0]
    state_width = whole_gains.shape[1]
    element = (whole_gains[cell_count - 1], whole_increments[cell_count - 1].astype(jnp.bfloat16))
    identity = (
        jnp.eye(state_width, dtype=jnp.bfloat16),
        jnp.zeros((state_width, state_width), jnp.bfloat16),
    )
    inside = carried_in(element, "tile", combine_affine_pair, identity)
    block_map = jnp.stack(combine_affine_pair(inside, element))
    block_map = spread(block_map, "tile", 0)
    exterior_part = prefix((block_map[0], block_map[1]), "tm", combine_affine_pair, identity)
    before = combine_affine_pair(exterior_part, inside)
    full_terminal = lax.all_gather(terminal.astype(jnp.bfloat16), "tile", axis=0, tiled=True)
    prior_factor, prior_covariance = before
    carried = jnp.dot(prior_factor, full_terminal, preferred_element_type=jnp.float32).astype(
        jnp.bfloat16
    )
    covariance = transpose_dot(carried, prior_factor) + prior_covariance.astype(jnp.float32)
    factor = whole_gains[0]
    product = jnp.dot(
        factor, covariance.astype(jnp.bfloat16), preferred_element_type=jnp.float32
    ).astype(jnp.bfloat16)
    covariance = transpose_dot(product, factor) + whole_increments[0]
    results = [covariance]
    smoothed_cells = jnp.stack(results[::-1])
    return lax.all_to_all(
        smoothed_cells.astype(jnp.bfloat16), "tile", split_axis=1, concat_axis=0, tiled=True
    ).astype(smoothed_cells.dtype)


def solution(mesh):
    return jax.shard_map(
        local,
        mesh=mesh,
        in_specs=(P("tm", "tile", None), P("tm", "tile", None), P("tile", None)),
        out_specs=P("tm", "tile", None),
        check_vma=False,
    )
```

profile of v0, /device:TPU:0, one launch (start us, length us, event | category | flops | bytes accessed | tf_op | source)
XLA Modules:
  0.0 691.1 jit_solution(1448490414244777398)
XLA Ops:
  6.5 1.8 convert_element_type.131
  8.3 36.1 %all_to_all.33 = bf16[8,96,768]{2,1,0:T(8,128)(2,1)} all-to-all(bf16[8,96,768]{2,1,0:T(8,128)(2,1)S(1)} %convert_element_type.131), channel_id=1, replica_groups=mesh['tm'=4,'tile'=8] {'tile'}, dimensions={0} | all-to-all | bytes 2359296 | tf_op jit(solution)/shard_map/all_to_all | solution.py:76
  44.5 1.2 copy-done.11
  45.7 60.3 %all_to_all.34 = bf16[8,96,768]{2,1,0:T(8,128)(2,1)} all-to-all(bf16[8,96,768]{2,1,0:T(8,128)(2,1)S(1)} %copy-done.11), channel_id=1, replica_groups=mesh['tm'=4,'tile'=8] {'tile'}, dimensions={0} | all-to-all | bytes 2359296 | tf_op jit(solution)/shard_map/all_to_all | solution.py:75
  108.0 1.7 bitcast_convert_fusion
  109.6 3.0 copy.15
  112.7 89.3 %all-gather.8.cloned.1.call-done = bf16[8,768,768]{2,1,0:T(8,128)(2,1)} async-done(((bf16[1,768,768]{2,1,0:T(8,128)(2,1)}), bf16[8,768,768]{2,1,0:T(8,128)(2,1)}) %all-gather.8.cloned.1.call-update) | async-done | bytes 9437200 | tf_op jit(solution)/shard_map/all_gather | solution.py:12
  201.9 138.5 %all-gather.6.cloned.1.call-done = bf16[8,768,768]{2,1,0:T(8,128)(2,1)} async-done(((bf16[1,768,768]{2,1,0:T(8,128)(2,1)}), bf16[8,768,768]{2,1,0:T(8,128)(2,1)}) %all-gather.6.cloned.1.call-update) | async-done | bytes 9437200 | tf_op jit(solution)/shard_map/all_gather | solution.py:12
  340.5 46.9 %while.28 = (s32[]{:T(128)}, bf16[768,768]{1,0:T(8,128)(2,1)S(1)}, bf16[768,768]{1,0:T(8,128)(2,1)S(1)}, s32[]{:T(128)}, bf16[8,768,768]{2,1,0:T(8,128)(2,1)}, /...) while((s32[]{:T(128)}, bf16[768,768]{1,0:T(8,128)(2,1)S(1)}, ...), condition=%wide.region_1.2_spmd, body=%wide.region_0.1_spmd.sunk | while | flops 2720858112 | bytes 14157463 | solution.py:29
  340.6 4.2 fusion.66
  344.8 2.4 convolution_convert_fusion.12
  347.3 4.1 fusion.66
  351.6 2.4 convolution_convert_fusion.12
  354.0 4.1 fusion.66
  358.2 2.4 convolution_convert_fusion.12
  360.7 4.1 fusion.66
  364.9 2.4 convolution_convert_fusion.12
  367.4 4.2 fusion.66
  371.6 2.4 convolution_convert_fusion.12
  374.1 4.2 fusion.66
  378.4 2.4 convolution_convert_fusion.12
  380.8 4.1 fusion.66
  385.0 2.4 convolution_convert_fusion.12
  387.4 4.3 fusion.27
  391.8 4.8 fusion.25
  396.6 3.0 maximum_select_fusion
  399.6 106.1 %all-reduce.2.cloned.1.call-done = bf16[2,768,768]{1,2,0:T(8,128)(2,1)} async-done(((bf16[2,768,768]{1,2,0:T(8,128)(2,1)}), bf16[2,768,768]{1,2,0:T(8,128)(2,1)}) %all-reduce.2.cloned.1.call-update) | async-done | bytes 2359312 | tf_op jit(solution)/shard_map/psum | solution.py:34
  505.7 1.8 fusion.28
  507.5 1.5 copy.16
  509.0 1.5 copy.17
  512.2 33.5 %all-gather.10.cloned.1.call-done = bf16[4,768,768]{2,1,0:T(8,128)(2,1)} async-done(((bf16[1,768,768]{2,1,0:T(8,128)(2,1)}), bf16[4,768,768]{2,1,0:T(8,128)(2,1)}) %all-gather.10.cloned.1.call-update) | async-done | bytes 4718608 | tf_op jit(solution)/shard_map/all_gather | solution.py:41
  545.6 39.0 %all-gather.12.cloned.1.call-done = bf16[4,768,768]{2,1,0:T(8,128)(2,1)} async-done(((bf16[1,768,768]{2,1,0:T(8,128)(2,1)}), bf16[4,768,768]{2,1,0:T(8,128)(2,1)}) %all-gather.12.cloned.1.call-update) | async-done | bytes 4718608 | tf_op jit(solution)/shard_map/all_gather | solution.py:41
  584.7 24.3 %while.29 = (s32[]{:T(128)}, bf16[768,768]{1,0:T(8,128)(2,1)S(1)}, bf16[768,768]{1,0:T(8,128)(2,1)S(1)}, s32[]{:T(128)}, bf16[4,768,768]{2,1,0:T(8,128)(2,1)}, /...) while((s32[]{:T(128)}, bf16[768,768]{1,0:T(8,128)(2,1)S(1)}, ...), condition=%wide.region_4.5_spmd, body=%wide.region_3.4_spmd.sunk | while | flops 2720858112 | bytes 14157463 | solution.py:50
  585.8 4.6 fusion.72
  590.4 2.4 convolution_convert_fusion.13
  593.9 4.5 fusion.72
  598.5 2.4 convolution_convert_fusion.13
  601.9 4.5 fusion.72
  606.4 2.4 convolution_convert_fusion.13
  609.0 2.1 convolution_convert_fusion.7
  611.1 4.5 add_convert_fusion.2
  615.7 12.3 %all-gather.14.cloned.1.call-done = bf16[768,768]{1,0:T(8,128)(2,1)} async-done(((bf16[96,768]{1,0:T(8,128)(2,1)}), bf16[768,768]{1,0:T(8,128)(2,1)}) %all-gather.14.cloned.1.call-update) | async-done | bytes 1179664 | tf_op jit(solution)/shard_map/all_gather | solution.py:91
  628.0 5.5 add_convert_fusion.1
  633.5 4.9 fusion.26
  638.4 3.1 copy.22
  642.0 8.0 %reduce = bf16[768,768]{1,0:T(8,128)(2,1)S(1)} reduce(bf16[768,1,768]{2,1,0:T(2,128)(2,1)S(1)} %bitcast.89, bf16[]{:T(256)} %broadcast), dimensions={1}, to_apply=%bitcast.63.reduce_sub_computation | reduce | bytes 2359298
  650.4 30.9 %all_to_all.35 = bf16[8,2,36864]{2,1,0:T(2,128)(2,1)S(1)} all-to-all(bf16[8,2,36864]{2,1,0:T(2,128)(2,1)S(1)} %reshape.30), channel_id=1, replica_groups=mesh['tm'=4,'tile'=8] {'tile'}, dimensions={0} | all-to-all | bytes 2359296 | tf_op jit(solution)/shard_map/all_to_all | solution.py:104
  682.6 1.6 convert.7
  (65 shorter events, 10.4 us)
Async XLA Ops:
  6.5 195.4 %all-gather.8.cloned.1.call-start = ((), (), s32[]{:S(2)}) async-start(), calls=%async_computation.4 | async-start | bytes 10616832 | tf_op jit(solution)/shard_map/all_gather | solution.py:12
  44.5 1.3 copy-start.11
  44.5 295.9 %all-gather.6.cloned.1.call-start = ((), (), s32[]{:S(2)}) async-start(), calls=%async_computation.3 | async-start | bytes 10616832 | tf_op jit(solution)/shard_map/all_gather | solution.py:12
  106.1 399.6 %all-reduce.2.cloned.1.call-start = ((), (), s32[]{:S(2)}) async-start(), calls=%async_computation.5 | async-start | bytes 4718592 | tf_op jit(solution)/shard_map/psum | solution.py:34
  106.3 1.1 copy-start
  106.3 1.7 copy-start.6
  112.7 227.8 %copy-start.4 = (bf16[768,768]{1,0:T(8,128)(2,1)S(1)}, bf16[768,768]{1,0:T(8,128)(2,1)}, u32[]{:S(2)}) copy-start(bf16[768,768]{1,0:T(8,128)(2,1)} %copy-done) | copy-start | bytes 3538948
  387.4 4.4 copy-start.2
  387.4 4.3 copy-start.5
  387.4 4.3 copy-start.8
  391.8 4.8 copy-start.10
  399.6 146.1 %all-gather.10.cloned.1.call-start = ((), (), s32[]{:S(2)}) async-start(), calls=%async_computation.6 | async-start | bytes 5898240 | tf_op jit(solution)/shard_map/all_gather | solution.py:41
  509.0 75.6 %all-gather.12.cloned.1.call-start = ((), (), s32[]{:S(2)}) async-start(), calls=%async_computation.7 | async-start | bytes 5898240 | tf_op jit(solution)/shard_map/all_gather | solution.py:41
  510.5 1.0 copy-start.12
  510.5 74.2 %copy-start.1 = (bf16[768,768]{1,0:T(8,128)(2,1)S(1)}, bf16[768,768]{1,0:T(8,128)(2,1)}, u32[]{:S(2)}) copy-start(bf16[768,768]{1,0:T(8,128)(2,1)} %copy-done) | copy-start | bytes 3538948
  510.5 117.4 %all-gather.14.cloned.1.call-start = ((), (), s32[]{:S(2)}) async-start(), calls=%async_computation.8 | async-start | bytes 1327104 | tf_op jit(solution)/shard_map/all_gather | solution.py:91
  584.7 24.3 %copy-start.3 = (bf16[768,768]{1,0:T(8,128)(2,1)S(1)}, bf16[768,768]{1,0:T(8,128)(2,1)}, u32[]{:S(2)}) copy-start(bf16[768,768]{1,0:T(8,128)(2,1)} %copy-done.2) | copy-start | bytes 3538948
  615.7 17.8 %copy-start.7 = (f32[768,768]{1,0:T(8,128)S(1)}, f32[768,768]{1,0:T(8,128)}, u32[]{:S(2)}) copy-start(f32[768,768]{1,0:T(8,128)} %bitcast_convert_fusion) | copy-start | bytes 7077892
  615.7 17.8 %copy-start.9 = (bf16[8,96,768]{2,1,0:T(8,128)(2,1)S(1)}, bf16[8,96,768]{2,1,0:T(8,128)(2,1)}, u32[]{:S(2)}) copy-start(bf16[8,96,768]{2,1,0:T(8,128)(2,1)} %all_to_all.34) | copy-start | bytes 3538948
Sparse Core Ops, SparseCore 0:
  44.6 157.2 all-gather.7
  204.1 136.2 all-gather.5
  399.7 105.9 all-reduce.1
  509.1 36.5 all-gather.9
  547.1 37.4 all-gather.11
  586.9 41.0 all-gather.13
where the time goes:
time: 692 us; the launch traced here: 691 us
  waiting for transfers between devices  419 us (61%)
  blocking collectives  127 us (18%)
  matrix products  92.3 us (13%)
  local copies, waits for them, and re-layouts  21.3 us (3%)
  other arithmetic  16.8 us (2%)
  between operations  13.7 us (2%)
    all_gather x2, waiting for transfers between devices, carried_in(): lax.all_gather(a.astype(kind), axis)  228 us
    psum x1, waiting for transfers between devices, spread(): return lax.psum(kept, axis)  106 us
    all_gather x2, waiting for transfers between devices, prefix(): gathered = jax.tree.map(lambda a: lax.all_gather(a, axis), part)  72.5 us
    dot_general x14, matrix products, transpose_dot(): lax.dot_general(left, right, (((1,), (1,)), ((), ())), preferred_element_...  62.3 us
    all_to_all x1, blocking collectives, local(): lax.all_to_all(gains, 'tile', split_axis=0, concat_axis=1, tiled=True)  60.3 us
    all_to_all x1, blocking collectives, local(): lax.all_to_all(increments.astype(jnp.bfloat16), 'tile', split_axis=0, con...  36.1 us
    all_to_all x1, blocking collectives, local(): lax.all_to_all(smoothed_cells.astype(jnp.bfloat16), 'tile', split_axis=1,...  30.9 us
    dot_general x12, matrix products, combine_affine_pair(): jnp.dot(low_factor, high_factor, preferred_element_type=jnp.float32)  30 us
  transfers between devices with their start and end apart: 6, of which 6 were waited for; matrix products, arithmetic and copies ran while one was open for 5% of the time, Pallas kernels for 0%

commit v1 on v0

v1 whole, which is shorter than its diff:
```python
import functools

import jax
import jax.numpy as jnp
from jax import lax
from jax.experimental import pallas as pl
from jax.experimental.pallas import tpu as pltpu
from jax.sharding import PartitionSpec as P

BF16 = jnp.bfloat16
F32 = jnp.float32
LANES = 128
TILE = 256
VMEM_LIMIT = 48 * 1024 * 1024


def params(steps=None):
    return pltpu.CompilerParams(vmem_limit_bytes=VMEM_LIMIT)


def half_width(rows, count):
    used = (count // 2 + 1) * rows
    return used, -(-used // LANES) * LANES


def nt(left, right):
    return lax.dot_general(left, right, (((1,), (1,)), ((), ())), preferred_element_type=F32)


def pack_kernel(count, place_ref, gain_ref, increment_ref, packed_ref):
    rows, width = gain_ref.shape[1:]
    used, half = half_width(rows, count)
    packed_ref[0, :, :width] = gain_ref[0]
    shift = lax.rem(width - place_ref[0] * rows, width)
    turned = pltpu.roll(increment_ref[0], shift, 1)[:, :half]
    column = lax.broadcasted_iota(jnp.int32, turned.shape, 1)
    halved = (column < rows) | (column >= used - rows)
    weight = jnp.where(column < used, jnp.where(halved, 0.5, 1.0), 0.0)
    packed_ref[0, :, width:] = (turned * weight).astype(BF16)


def pack(place, gains, increments, count):
    steps, rows, width = gains.shape
    _, half = half_width(rows, count)
    return pl.pallas_call(
        functools.partial(pack_kernel, count),
        grid_spec=pltpu.PrefetchScalarGridSpec(
            num_scalar_prefetch=1,
            grid=(steps,),
            in_specs=[
                pl.BlockSpec((1, rows, width), lambda i, p: (i, 0, 0)),
                pl.BlockSpec((1, rows, width), lambda i, p: (i, 0, 0)),
            ],
            out_specs=pl.BlockSpec((1, rows, width + half), lambda i, p: (i, 0, 0)),
        ),
        out_shape=jax.ShapeDtypeStruct((steps, rows, width + half), BF16),
        compiler_params=params(),
        name="pack",
    )(place, gains, increments)


def compose_kernel(first, last, place_ref, packed_ref, *refs):
    if first:
        factor_out, own_out, factor_end, half_end, factor, half, middle, total = refs
    else:
        factor_in, half_in, factor_out, own_out, factor_end, half_end, factor, half, middle, total = refs
    count, _, rows, _ = packed_ref.shape
    width = factor.shape[0]
    turn = pl.program_id(0)
    gain = packed_ref[:, 0, :, :width].reshape(width, width)

    def add_increment(block):
        piece = packed_ref[block, 0, :, width:].astype(F32)
        rest = width - piece.shape[1]
        wide = jnp.concatenate([piece, jnp.zeros((rows, rest), F32)], axis=1) if rest else piece
        return pltpu.roll(wide, block * rows, 1) if block else wide

    if first:

        @pl.when(turn == 0)
        def _():
            factor[...] = gain
            for block in range(count):
                half[block * rows:(block + 1) * rows, :] = add_increment(block).astype(BF16)

    else:

        @pl.when(turn == 0)
        def _():
            factor[...] = factor_in[...]
            half[...] = half_in[...]

    def step():
        for j in range(0, width, TILE):
            cols = slice(j, j + TILE)
            middle[:, cols] = jnp.dot(gain, half[:, cols], preferred_element_type=F32).astype(BF16)
            factor[:, cols] = jnp.dot(gain, factor[:, cols], preferred_element_type=F32).astype(BF16)
        for j in range(0, width, TILE):
            total[:, j:j + TILE] = nt(middle[...], gain[j:j + TILE, :])
        for block in range(count):
            span = slice(block * rows, (block + 1) * rows)
            half[span, :] = (total[span, :] + add_increment(block)).astype(BF16)

    if first:
        pl.when(turn > 0)(step)
    else:
        step()

    start = pl.multiple_of(place_ref[0] * rows, 16)
    picked = lax.broadcasted_iota(jnp.int32, (rows, width), 1) == start + lax.broadcasted_iota(
        jnp.int32, (rows, width), 0
    )
    own = half[pl.ds(start, rows), :].astype(F32)
    own_out[0] = own + nt(picked.astype(F32).astype(BF16), half[...])
    factor_out[0] = factor[...]

    @pl.when(turn == pl.num_programs(0) - 1)
    def _():
        factor_end[...] = factor[...]
        if last:
            for j in range(0, width, TILE):
                cols = slice(j, j + TILE)
                whole = half[:, cols].astype(F32) + jnp.swapaxes(half[cols, :].astype(F32), 0, 1)
                half_end[:, cols] = whole
        else:
            half_end[...] = half[...]


def compose(place, packed, state, last):
    count, steps, rows, total_width = packed.shape
    width = count * rows
    first = state is None
    whole = pl.BlockSpec((width, width), lambda i, p: (0, 0))
    in_specs = [pl.BlockSpec((count, 1, rows, total_width), lambda i, p: (0, steps - 1 - i, 0, 0))]
    if not first:
        in_specs += [whole, whole]
    return pl.pallas_call(
        functools.partial(compose_kernel, first, last),
        grid_spec=pltpu.PrefetchScalarGridSpec(
            num_scalar_prefetch=1,
            grid=(steps,),
            in_specs=in_specs,
            out_specs=[
                pl.BlockSpec((1, width, width), lambda i, p: (steps - 1 - i, 0, 0)),
                pl.BlockSpec((1, rows, width), lambda i, p: (steps - 1 - i, 0, 0)),
                whole,
                whole,
            ],
            scratch_shapes=[
                pltpu.VMEM((width, width), BF16),
                pltpu.VMEM((width, width), BF16),
                pltpu.VMEM((width, width), BF16),
                pltpu.VMEM((width, width), F32),
            ],
        ),
        out_shape=[
            jax.ShapeDtypeStruct((steps, width, width), BF16),
            jax.ShapeDtypeStruct((steps, rows, width), F32),
            jax.ShapeDtypeStruct((width, width), BF16),
            jax.ShapeDtypeStruct((width, width), F32 if last else BF16),
        ],
        compiler_params=params(),
        cost_estimate=pl.CostEstimate(
            flops=6 * steps * width**3, bytes_accessed=8 * steps * width * width, transcendentals=0
        ),
        name="compose",
    )(place, packed, *(() if first else state))


def hop_kernel(arrived, factor_ref, increment_ref, *refs):
    covariances, out_ref, covariance, middle = refs[:arrived], refs[arrived], refs[arrived + 1], refs[arrived + 2]
    width = factor_ref.shape[0]
    value = covariances[0][...]
    for extra in covariances[1:]:
        value = value + extra[...]
    covariance[...] = value
    for j in range(0, width, TILE):
        cols = slice(j, j + TILE)
        middle[:, cols] = jnp.dot(factor_ref[...], covariance[:, cols], preferred_element_type=F32).astype(BF16)
    for j in range(0, width, TILE):
        cols = slice(j, j + TILE)
        out_ref[:, cols] = (nt(middle[...], factor_ref[cols, :]) + increment_ref[:, cols]).astype(BF16)


def hop(factor, increment, covariances):
    width = factor.shape[0]
    return pl.pallas_call(
        functools.partial(hop_kernel, len(covariances)),
        out_shape=jax.ShapeDtypeStruct((width, width), BF16),
        scratch_shapes=[pltpu.VMEM((width, width), BF16), pltpu.VMEM((width, width), BF16)],
        compiler_params=params(),
        cost_estimate=pl.CostEstimate(flops=4 * width**3, bytes_accessed=10 * width * width, transcendentals=0),
        name="hop",
    )(factor, increment, *covariances)


def finish_kernel(arrived, place_ref, factor_ref, own_ref, *refs):
    covariances, out_ref, covariance = refs[:arrived], refs[arrived], refs[arrived + 1]
    rows = own_ref.shape[1]

    @pl.when(pl.program_id(0) == 0)
    def _():
        value = covariances[0][...]
        for extra in covariances[1:]:
            value = value + extra[...]
        covariance[...] = value

    start = pl.multiple_of(place_ref[0] * rows, 16)
    mine = factor_ref[0, pl.ds(start, rows), :]
    middle = jnp.dot(mine, covariance[...], preferred_element_type=F32).astype(BF16)
    out_ref[0] = nt(middle, factor_ref[0]) + own_ref[0]


def finish(place, factors, own, covariances):
    steps, rows, width = own.shape
    whole = pl.BlockSpec((width, width), lambda i, p: (0, 0))
    return pl.pallas_call(
        functools.partial(finish_kernel, len(covariances)),
        grid_spec=pltpu.PrefetchScalarGridSpec(
            num_scalar_prefetch=1,
            grid=(steps,),
            in_specs=[
                pl.BlockSpec((1, width, width), lambda i, p: (i, 0, 0)),
                pl.BlockSpec((1, rows, width), lambda i, p: (i, 0, 0)),
            ]
            + [whole] * len(covariances),
            out_specs=pl.BlockSpec((1, rows, width), lambda i, p: (i, 0, 0)),
            scratch_shapes=[pltpu.VMEM((width, width), BF16)],
        ),
        out_shape=jax.ShapeDtypeStruct((steps, rows, width), F32),
        compiler_params=params(),
        name="finish",
    )(place, factors, own, *covariances)


def local(gains, increments, terminal):
    count = lax.axis_size("tile")
    blocks = lax.axis_size("tm")
    steps = gains.shape[0]
    place = lax.axis_index("tile").astype(jnp.int32).reshape(1)
    block = lax.axis_index("tm")
    packed = pack(place, gains, increments, count)
    cut = steps - steps * 5 // 8
    late = lax.all_gather(packed[cut:], "tile")
    early = lax.all_gather(packed[:cut], "tile")
    full_terminal = lax.all_gather(terminal.astype(BF16), "tile", axis=0, tiled=True)
    late_factors, late_own, factor, half = compose(place, late, None, False)
    early_factors, early_own, factor, increment = compose(place, early, (factor, half), True)
    covariances = [jnp.where(block == blocks - 1, full_terminal, jnp.zeros_like(full_terminal))]
    for turn in range(blocks - 1, 0, -1):
        covariances.append(lax.ppermute(hop(factor, increment, covariances), "tm", [(turn, turn - 1)]))
    return jnp.concatenate(
        [
            finish(place, early_factors, early_own, covariances),
            finish(place, late_factors, late_own, covariances),
        ]
    )


def solution(mesh):
    return jax.shard_map(
        local,
        mesh=mesh,
        in_specs=(P("tm", "tile", None), P("tm", "tile", None), P("tile", None)),
        out_specs=P("tm", "tile", None),
        check_vma=False,
    )
```

time: 692 us -> 365 us (0.53)
  waiting for transfers between devices: 419 us -> 280 us
  blocking collectives: 127 us -> 0 us
  matrix products: 92.3 us -> 0 us
  Pallas kernels: 0 us -> 55 us
  other arithmetic: 16.8 us -> 3.28 us
  local copies, waits for them, and re-layouts: 21.3 us -> 10 us
    all_to_all x3 -> x0, blocking collectives: 127 us -> none  [the longest x1 60.3 us: local(): lax.all_to_all(gains, 'tile', split_axis=0, concat_axis=1, tiled=True)]
    psum x1 -> x0, waiting for transfers between devices: 106 us -> none  [spread(): return lax.psum(kept, axis)]
    dot_general x26 -> x0, matrix products: 92.3 us -> none  [the longest x14 62.3 us: transpose_dot(): lax.dot_general(left, right, (((1,), (1,)), ((), ())), preferred_element_...]
    pallas_call x0 -> x8, Pallas kernels: none -> 55 us  [the longest x2 32.8 us: compose(): pl.pallas_call(functools.partial(compose_kernel, first, last), grid_spec=...]
    all_gather x5 -> x3, waiting for transfers between devices: 312 us -> 258 us  [the longest x1 144 us: local(): late = lax.all_gather(packed[cut:], 'tile')]
    ppermute x0 -> x3, waiting for transfers between devices: none -> 22.1 us  [local(): lax.ppermute(hop(factor, increment, covariances), 'tm', [(turn, turn - 1)])]
    unnamed x1 -> x0, other arithmetic: 8.05 us -> none
  transfers between devices with their start and end apart: 6 -> 6, of which waited for: 6 -> 4; matrix products, arithmetic and copies ran while one was open for 5% -> 1% of each run, Pallas kernels for 0% -> 5%
where the time goes in v1:
time: 365 us
  waiting for transfers between devices  280 us (77%)
  Pallas kernels  55 us (15%)
  between operations  13.2 us (4%)
  local copies, waits for them, and re-layouts  10 us (3%)
    all_gather x1, waiting for transfers between devices, local(): late = lax.all_gather(packed[cut:], 'tile')  144 us
    all_gather x1, waiting for transfers between devices, local(): early = lax.all_gather(packed[:cut], 'tile')  75.8 us
    all_gather x1, waiting for transfers between devices, local(): lax.all_gather(terminal.astype(BF16), 'tile', axis=0, tiled=True)  38.5 us
    pallas_call x2, Pallas kernels, compose(): pl.pallas_call(functools.partial(compose_kernel, first, last), grid_spec=...  32.8 us
    ppermute x3, waiting for transfers between devices, local(): lax.ppermute(hop(factor, increment, covariances), 'tm', [(turn, turn - 1)])  22.1 us
    pallas_call x2, Pallas kernels, finish(): pl.pallas_call(functools.partial(finish_kernel, len(covariances)), grid_s...  11 us
    pallas_call x3, Pallas kernels, hop(): pl.pallas_call(functools.partial(hop_kernel, len(covariances)), out_shape...  9.69 us
    unnamed x12, local copies, waits for them, and re-layouts  7.99 us
  transfers between devices with their start and end apart: 6, of which 4 were waited for; matrix products, arithmetic and copies ran while one was open for 1% of the time, Pallas kernels for 5%

profile of v1, /device:TPU:0, one launch (start us, length us, event | category | flops | bytes accessed | tf_op | source)
XLA Modules:
  0.0 364.8 jit_solution(12800241096914772979)
XLA Ops:
  6.5 0.0 all-gather.6.cloned.1.call-start
  6.5 1.6 convert_element_type.3
  8.2 0.0 all-gather.6.cloned.1.call-update
  8.2 0.0 all-gather.10.cloned.1.call-start
  8.3 0.0 copy-start.3
  8.3 1.7 copy-done.3
  9.9 0.0 copy-start.5
  9.9 1.3 copy-done.5
  11.2 1.5 pack.1
  12.7 1.1 slice.9
  13.8 0.0 all-gather.10.cloned.1.call-update
  13.8 0.0 all-gather.8.cloned.1.call-start
  13.9 0.9 slice.8
  14.8 0.0 all-gather.8.cloned.1.call-update
  14.8 38.5 %all-gather.6.cloned.1.call-done = bf16[768,768]{1,0:T(8,128)(2,1)} async-done(((bf16[96,768]{1,0:T(8,128)(2,1)}), bf16[768,768]{1,0:T(8,128)(2,1)}) %all-gather.6.cloned.1.call-update) | async-done | bytes 1179664 | tf_op jit(solution)/shard_map/all_gather | solution.py:246
  53.3 0.1 broadcast_select_fusion.refs_0_
  53.4 143.8 %all-gather.10.cloned.1.call-done = bf16[40,96,1280]{2,1,0:T(8,128)(2,1)} async-done(((bf16[5,96,1280]{2,1,0:T(8,128)(2,1)}), bf16[40,96,1280]{2,1,0:T(8,128)(2,1)}) %all-gather.10.cloned.1.call-update) | async-done | bytes 9830416 | tf_op jit(solution)/shard_map/all_gather | solution.py:244
  197.2 17.7 %compose.2 = (bf16[5,768,768]{2,1,0:T(8,128)(2,1)}, f32[5,96,768]{2,1,0:T(8,128)S(1)}, bf16[768,768]{1,0:T(8,128)(2,1)S(1)}, bf16[768,768]{1,0:T(8,128)(2,1)S(1)}) custom-call(s32[1]{0:T(128)} %bitcast.place_ref, bf16[8,5,96,1280]{3,2,1,0:T(8,128)(2,1)} %bitcast.3), custom_call_target="tpu_custom_call" | custom-call | flops 13589544960 | bytes 23592960 | tf_op jit(solution)/shard_map/compose/pallas_call | solution.py:137
  214.9 0.0 copy-start.4
  214.9 1.1 copy-done.4
  216.0 75.8 %all-gather.8.cloned.1.call-done = bf16[24,96,1280]{2,1,0:T(8,128)(2,1)} async-done(((bf16[3,96,1280]{2,1,0:T(8,128)(2,1)}), bf16[24,96,1280]{2,1,0:T(8,128)(2,1)}) %all-gather.8.cloned.1.call-update) | async-done | bytes 5898256 | tf_op jit(solution)/shard_map/all_gather | solution.py:245
  291.8 15.1 %compose.3 = (bf16[3,768,768]{2,1,0:T(8,128)(2,1)}, f32[3,96,768]{2,1,0:T(8,128)S(1)}, bf16[768,768]{1,0:T(8,128)(2,1)S(1)}, f32[768,768]{1,0:T(8,128)}) custom-call(s32[1]{0:T(128)} %bitcast.place_ref, bf16[8,3,96,1280]{3,2,1,0:T(8,128)(2,1)} %bitcast.4, bf16[768,768]{1,0:T(8,128)(2,1)S(1)} %get-tuple-element.13.refs_0_, ...), custom_call_target="tpu_custom_call" | custom-call | flops 8153726976 | bytes 14155776 | tf_op jit(solution)/shard_map/compose/pallas_call | solution.py:137
  306.9 0.0 copy-start
  306.9 1.7 copy-done
  308.6 2.1 hop.3
  310.7 0.7 collective-permute-start
  311.5 0.0 collective-permute-done.refs_1_
  311.5 3.8 %hop.4 = bf16[768,768]{1,0:T(8,128)(2,1)S(1)} custom-call(bf16[768,768]{1,0:T(8,128)(2,1)S(1)} %get-tuple-element.17.factor_ref, f32[768,768]{1,0:T(8,128)} %get-tuple-element.18.increment_ref, bf16[768,768]{1,0:T(8,128)(2,1)S(1)} %broadcast_select_fusion.refs_0_, bf16[768,768]{1,0:T(8,128)(2,1)S(1)} %collective-permute-done.refs_1_), custom_call_target="tpu_custom_call" | custom-call | flops 1811939328 | bytes 5898240 | tf_op jit(solution)/shard_map/hop/pallas_call | solution.py:187
  315.3 0.9 collective-permute-start.1
  316.2 0.0 collective-permute-done.1.refs_2_
  316.2 3.8 %hop.5 = bf16[768,768]{1,0:T(8,128)(2,1)S(1)} custom-call(bf16[768,768]{1,0:T(8,128)(2,1)S(1)} %get-tuple-element.17.factor_ref, f32[768,768]{1,0:T(8,128)} %get-tuple-element.18.increment_ref, bf16[768,768]{1,0:T(8,128)(2,1)S(1)} %broadcast_select_fusion.refs_0_, bf16[768,768]{1,0:T(8,128)(2,1)S(1)} %collective-permute-done.refs_1_, ...), custom_call_target="tpu_custom_call" | custom-call | flops 1811939328 | bytes 5898240 | tf_op jit(solution)/shard_map/hop/pallas_call | solution.py:187
  320.0 1.3 collective-permute-start.2
  321.3 22.1 %collective-permute-done.2.refs_3_ = bf16[768,768]{1,0:T(8,128)(2,1)S(1)} collective-permute-done((bf16[768,768]{1,0:T(8,128)(2,1)S(1)}, bf16[768,768]{1,0:T(8,128)(2,1)S(1)}, u32[]{:S(2)}, u32[]{:S(2)}) %collective-permute-start.2) | collective-permute-done | bytes 1179680 | tf_op jit(solution)/shard_map/ppermute | solution.py:251
  343.4 0.0 copy-start.1
  343.4 1.0 copy-done.1
  344.4 4.6 %finish.2 = f32[3,96,768]{2,1,0:T(8,128)S(1)} custom-call(s32[1]{0:T(128)} %bitcast.place_ref, bf16[3,768,768]{2,1,0:T(8,128)(2,1)} %get-tuple-element.15.factor_ref, f32[3,96,768]{2,1,0:T(8,128)S(1)} %get-tuple-element.16.own_ref, bf16[768,768]{1,0:T(8,128)(2,1)S(1)} %broadcast_select_fusion.refs_0_, bf16[768,768]{1,0:T(8,128)(2,1)S(1)} %collective-permute-done.refs_1_, ...), custom_call_target="tpu_custom_call" | custom-call | tf_op jit(solution)/shard_map/finish/pallas_call | solution.py:217
  349.0 0.0 copy-start.2
  349.0 1.3 copy-done.2
  350.3 6.4 %finish.3 = f32[5,96,768]{2,1,0:T(8,128)S(1)} custom-call(s32[1]{0:T(128)} %bitcast.place_ref, bf16[5,768,768]{2,1,0:T(8,128)(2,1)} %get-tuple-element.19.factor_ref, f32[5,96,768]{2,1,0:T(8,128)} %copy-done.4, bf16[768,768]{1,0:T(8,128)(2,1)S(1)} %broadcast_select_fusion.refs_0_, bf16[768,768]{1,0:T(8,128)(2,1)S(1)} %collective-permute-done.refs_1_, ...), custom_call_target="tpu_custom_call" | custom-call | tf_op jit(solution)/shard_map/finish/pallas_call | solution.py:217
  356.7 1.6 pad_maximum_fusion
Async XLA Ops:
  6.5 46.8 %all-gather.6.cloned.1.call-start = ((), (), s32[]{:S(2)}) async-start(), calls=%async_computation | async-start | bytes 1327104 | tf_op jit(solution)/shard_map/all_gather | solution.py:246
  8.2 189.0 %all-gather.10.cloned.1.call-start = ((), (), s32[]{:S(2)}) async-start(), calls=%async_computation.2 | async-start | bytes 11059200 | tf_op jit(solution)/shard_map/all_gather | solution.py:244
  8.3 1.7 copy-start.3
  9.9 1.3 copy-start.5
  13.8 278.0 %all-gather.8.cloned.1.call-start = ((), (), s32[]{:S(2)}) async-start(), calls=%async_computation.1 | async-start | bytes 6635520 | tf_op jit(solution)/shard_map/all_gather | solution.py:245
  214.9 1.1 copy-start.4
  306.9 1.7 copy-start
  310.7 0.7 collective-permute-start
  315.3 0.9 collective-permute-start.1
  320.0 23.4 %collective-permute-start.2 = (bf16[768,768]{1,0:T(8,128)(2,1)S(1)}, bf16[768,768]{1,0:T(8,128)(2,1)S(1)}, u32[]{:S(2)}, u32[]{:S(2)}) collective-permute-start(bf16[768,768]{1,0:T(8,128)(2,1)S(1)} %hop.5), channel_id=1, source_target_pairs={{8,0},{9,1},{10,2},{11,3},{12,4},{13,5},{14,6},{15,7}} | collective-permute-start | bytes 3538952 | tf_op jit(solution)/shard_map/ppermute | solution.py:251
  343.4 1.0 copy-start.1
  349.0 1.3 copy-start.2
Sparse Core Ops, SparseCore 0:
  9.5 43.7 all-gather.5
  55.5 141.6 all-gather.9
  199.4 92.4 all-gather.7

commit v2 on v1

v2 whole, which is shorter than its diff:
```python
import functools
import math

import jax
import jax.numpy as jnp
from jax import lax
from jax.experimental import pallas as pl
from jax.experimental.pallas import tpu as pltpu
from jax.sharding import PartitionSpec as P

BF16 = jnp.bfloat16
F32 = jnp.float32
LANES = 128
TILE = 256
LINE = 4
MIB = 1024 * 1024


def half_width(rows, count):
    used = (count // 2 + 1) * rows
    return used, -(-used // LANES) * LANES


def nt(left, right):
    return lax.dot_general(left, right, (((1,), (1,)), ((), ())), preferred_element_type=F32)


def pack_kernel(count, place_ref, gain_ref, increment_ref, packed_ref):
    rows, width = gain_ref.shape[1:]
    used, half = half_width(rows, count)
    packed_ref[0, :, :width] = gain_ref[0]
    shift = lax.rem(width - place_ref[0] * rows, width)
    turned = pltpu.roll(increment_ref[0], shift, 1)[:, :half]
    column = lax.broadcasted_iota(jnp.int32, turned.shape, 1)
    halved = (column < rows) | (column >= used - rows)
    weight = jnp.where(column < used, jnp.where(halved, 0.5, 1.0), 0.0)
    packed_ref[0, :, width:] = (turned * weight).astype(BF16)


def pack(places, gains, increments, low, high):
    count = places.shape[0]
    steps, rows, width = gains.shape
    _, half = half_width(rows, count)
    return pl.pallas_call(
        functools.partial(pack_kernel, count),
        grid_spec=pltpu.PrefetchScalarGridSpec(
            num_scalar_prefetch=1,
            grid=(high - low,),
            in_specs=[
                pl.BlockSpec((1, rows, width), lambda i, p: (low + i, 0, 0)),
                pl.BlockSpec((1, rows, width), lambda i, p: (low + i, 0, 0)),
            ],
            out_specs=pl.BlockSpec((1, rows, width + half), lambda i, p: (i, 0, 0)),
        ),
        out_shape=jax.ShapeDtypeStruct((high - low, rows, width + half), BF16),
        compiler_params=pltpu.CompilerParams(vmem_limit_bytes=8 * MIB),
        name="pack",
    )(places, gains, increments)


def compose_kernel(count, first, places_ref, *refs):
    shards, refs = refs[:count], refs[count:]
    if not first:
        factor_in, half_in, refs = refs[0], refs[1], refs[4:]
    factor_out, own_out, factor_end, half_end, gain, factor, half, middle, total = refs
    rows = shards[0].shape[1]
    width = factor.shape[0]
    turn = pl.program_id(0)
    starts = [pl.multiple_of(places_ref[i] * rows, 16) for i in range(count)]
    for start, shard in zip(starts, shards):
        gain[pl.ds(start, rows), :] = shard[0, :, :width]

    def increment(start, shard):
        piece = shard[0, :, width:].astype(F32)
        rest = width - piece.shape[1]
        wide = jnp.concatenate([piece, jnp.zeros((rows, rest), F32)], axis=1) if rest else piece
        return pltpu.roll(wide, start, 1)

    @pl.when(turn == 0)
    def _():
        if first:
            factor[...] = gain[...]
            for start, shard in zip(starts, shards):
                half[pl.ds(start, rows), :] = increment(start, shard).astype(BF16)
        else:
            factor[...] = factor_in[...]
            half[...] = half_in[...]

    def step():
        for j in range(0, width, TILE):
            cols = slice(j, j + TILE)
            middle[:, cols] = jnp.dot(gain[...], half[:, cols], preferred_element_type=F32).astype(BF16)
            factor[:, cols] = jnp.dot(gain[...], factor[:, cols], preferred_element_type=F32).astype(BF16)
        for j in range(0, width, TILE):
            total[:, j:j + TILE] = nt(middle[...], gain[j:j + TILE, :])
        for start, shard in zip(starts, shards):
            span = pl.ds(start, rows)
            half[span, :] = (total[span, :] + increment(start, shard)).astype(BF16)

    if first:
        pl.when(turn > 0)(step)
    else:
        step()

    picked = lax.broadcasted_iota(jnp.int32, (rows, width), 1) == starts[0] + lax.broadcasted_iota(
        jnp.int32, (rows, width), 0
    )
    own = half[pl.ds(starts[0], rows), :].astype(F32)
    own_out[0] = own + nt(jnp.where(picked, 1.0, 0.0).astype(BF16), half[...])
    factor_out[0] = factor[...]

    @pl.when(turn == pl.num_programs(0) - 1)
    def _():
        factor_end[...] = factor[...]
        half_end[...] = half[...]


def compose(places, shards, state, low, steps):
    count = len(shards)
    turns, rows, packed_width = shards[0].shape
    width = count * rows
    first = state is None
    whole = pl.BlockSpec((width, width), lambda i, p: (0, 0))
    anywhere = pl.BlockSpec(memory_space=pl.ANY)
    in_specs = [pl.BlockSpec((1, rows, packed_width), lambda i, p: (turns - 1 - i, 0, 0))] * count
    if not first:
        in_specs += [whole, whole, anywhere, anywhere]
    return pl.pallas_call(
        functools.partial(compose_kernel, count, first),
        grid_spec=pltpu.PrefetchScalarGridSpec(
            num_scalar_prefetch=1,
            grid=(turns,),
            in_specs=in_specs,
            out_specs=[
                pl.BlockSpec((1, width, width), lambda i, p: (low + turns - 1 - i, 0, 0)),
                pl.BlockSpec((1, rows, width), lambda i, p: (low + turns - 1 - i, 0, 0)),
                whole,
                whole,
            ],
            scratch_shapes=[pltpu.VMEM((width, width), BF16) for _ in range(4)]
            + [pltpu.VMEM((width, width), F32)],
        ),
        out_shape=[
            jax.ShapeDtypeStruct((steps, width, width), BF16),
            jax.ShapeDtypeStruct((steps, rows, width), F32),
            jax.ShapeDtypeStruct((width, width), BF16),
            jax.ShapeDtypeStruct((width, width), BF16),
        ],
        input_output_aliases={} if first else {count + 3: 0, count + 4: 1},
        compiler_params=pltpu.CompilerParams(vmem_limit_bytes=32 * MIB),
        cost_estimate=pl.CostEstimate(
            flops=6 * turns * width**3, bytes_accessed=8 * turns * width * width, transcendentals=0
        ),
        name="compose",
    )(places, *shards, *(() if first else (state[2], state[3], state[0], state[1])))


def arrived_sum(refs):
    value = refs[0][...]
    for extra in refs[1:]:
        value = value + extra[...]
    return value


def hop_kernel(arrived, factor_ref, half_ref, *refs):
    out_ref, covariance, middle = refs[arrived:]
    width = factor_ref.shape[0]
    covariance[...] = arrived_sum(refs[:arrived])
    for j in range(0, width, TILE):
        cols = slice(j, j + TILE)
        middle[:, cols] = jnp.dot(factor_ref[...], covariance[:, cols], preferred_element_type=F32).astype(BF16)
    for j in range(0, width, TILE):
        cols = slice(j, j + TILE)
        out_ref[:, cols] = (nt(middle[...], factor_ref[cols, :]) + half_ref[:, cols].astype(F32)).astype(BF16)


def hop(factor, half, halves):
    width = factor.shape[0]
    return pl.pallas_call(
        functools.partial(hop_kernel, len(halves)),
        out_shape=jax.ShapeDtypeStruct((width, width), BF16),
        scratch_shapes=[pltpu.VMEM((width, width), BF16), pltpu.VMEM((width, width), BF16)],
        compiler_params=pltpu.CompilerParams(vmem_limit_bytes=20 * MIB),
        cost_estimate=pl.CostEstimate(flops=4 * width**3, bytes_accessed=10 * width * width, transcendentals=0),
        name="hop",
    )(factor, half, *halves)


def finish_kernel(arrived, places_ref, factor_ref, own_ref, *refs):
    out_ref, half, identity, covariance = refs[arrived:]
    rows = own_ref.shape[1]
    width = covariance.shape[0]

    @pl.when(pl.program_id(0) == 0)
    def _():
        half[...] = arrived_sum(refs[:arrived])
        row = lax.broadcasted_iota(jnp.int32, (width, width), 0)
        column = lax.broadcasted_iota(jnp.int32, (width, width), 1)
        identity[...] = jnp.where(row == column, 1.0, 0.0).astype(BF16)
        for j in range(0, width, TILE):
            cols = slice(j, j + TILE)
            turned = nt(identity[...], half[cols, :])
            covariance[:, cols] = (half[:, cols].astype(F32) + turned).astype(BF16)

    start = pl.multiple_of(places_ref[0] * rows, 16)
    mine = factor_ref[0, pl.ds(start, rows), :]
    middle = jnp.dot(mine, covariance[...], preferred_element_type=F32).astype(BF16)
    out_ref[0] = nt(middle, factor_ref[0]) + own_ref[0]


def finish(places, factors, own, halves):
    steps, rows, width = own.shape
    whole = pl.BlockSpec((width, width), lambda i, p: (0, 0))
    return pl.pallas_call(
        functools.partial(finish_kernel, len(halves)),
        grid_spec=pltpu.PrefetchScalarGridSpec(
            num_scalar_prefetch=1,
            grid=(steps,),
            in_specs=[
                pl.BlockSpec((1, width, width), lambda i, p: (i, 0, 0)),
                pl.BlockSpec((1, rows, width), lambda i, p: (i, 0, 0)),
            ]
            + [whole] * len(halves),
            out_specs=pl.BlockSpec((1, rows, width), lambda i, p: (i, 0, 0)),
            scratch_shapes=[pltpu.VMEM((width, width), BF16)] * 3,
        ),
        out_shape=jax.ShapeDtypeStruct((steps, rows, width), F32),
        compiler_params=pltpu.CompilerParams(vmem_limit_bytes=24 * MIB),
        name="finish",
    )(places, factors, own, *halves)


def pieces(steps):
    if steps < 8:
        return [(0, steps, False)]
    bulk = (steps - steps // 4) // 2
    rest = steps - 2 * bulk
    return [
        (steps - bulk, steps, False),
        (rest, rest + bulk, False),
        (rest // 2, rest, True),
        (0, rest // 2, False),
    ]


def local(gains, increments, terminal):
    count = lax.axis_size("tile")
    blocks = lax.axis_size("tm")
    line = math.gcd(count, LINE)
    across = count // line
    steps = gains.shape[0]
    place = lax.axis_index("tile").astype(jnp.int32)
    block = lax.axis_index("tm")

    def shifted(array, along, over):
        pairs = [
            (a * across + b, (a + along) % line * across + (b + over) % across)
            for a in range(line)
            for b in range(across)
        ]
        return lax.ppermute(array, "tile", pairs)

    places = jnp.stack(
        [
            (place // across - i + line) % line * across + (place % across - j + across) % across
            for i in range(line)
            for j in range(across)
        ]
    )
    full_terminal = lax.all_gather(terminal.astype(BF16), "tile", axis=0, tiled=True)
    state = None
    for low, high, across_first in pieces(steps):
        own = pack(places, gains, increments, low, high)
        shards = {}
        if across_first:
            for j in range(across):
                shards[0, j] = shifted(own, 0, j) if j else own
            for i in range(1, line):
                for j in range(across):
                    shards[i, j] = shifted(shards[0, j], i, 0)
        else:
            for i in range(line):
                shards[i, 0] = shifted(own, i, 0) if i else own
                for j in range(1, across):
                    shards[i, j] = shifted(shards[i, 0], 0, j)
        ordered = [shards[i, j] for i in range(line) for j in range(across)]
        state = compose(places, ordered, state, low, steps)
    factors, own, factor, half = state
    halves = [jnp.where(block == blocks - 1, 0.5, 0.0).astype(BF16) * full_terminal]
    for turn in range(blocks - 1, 0, -1):
        halves.append(lax.ppermute(hop(factor, half, halves), "tm", [(turn, turn - 1)]))
    return finish(places, factors, own, halves)


def solution(mesh):
    return jax.shard_map(
        local,
        mesh=mesh,
        in_specs=(P("tm", "tile", None), P("tm", "tile", None), P("tile", None)),
        out_specs=P("tm", "tile", None),
        check_vma=False,
    )
```

time: 365 us -> 351 us (0.962)
  waiting for transfers between devices: 280 us -> 145 us
  starting transfers between devices: 3.03 us -> 116 us
  local copies, waits for them, and re-layouts: 10 us -> 16.5 us
    all_gather x2 -> x0, waiting for transfers between devices: 220 us -> none  [the longest x1 144 us: local(): late = lax.all_gather(packed[cut:], 'tile')]
    ppermute x3 -> x31, waiting for transfers between devices: 22.1 us -> 145 us  [the longest x28 123 us: shifted(): return lax.ppermute(array, 'tile', pairs)]
    ppermute x3 -> x31, starting transfers between devices: 2.95 us -> 116 us  [the longest x28 113 us: shifted(): return lax.ppermute(array, 'tile', pairs)]
    all_gather x1, waiting for transfers between devices: 38.5 us -> 0.01 us  [local(): lax.all_gather(terminal.astype(BF16), 'tile', axis=0, tiled=True)]
    unnamed x12 -> x58, local copies, waits for them, and re-layouts: 7.99 us -> 16.4 us
    pallas_call x7 -> x8, Pallas kernels: 53.5 us -> 51.9 us  [the longest x4 37.1 us: compose(): pl.pallas_call(functools.partial(compose_kernel, count, first), grid_spec...]
  transfers between devices with their start and end apart: 6 -> 32, of which waited for: 4 -> 12; matrix products, arithmetic and copies ran while one was open for 1% -> 0% of each run, Pallas kernels for 5% -> 12%
where the time goes in v2:
time: 351 us; the launch traced here: 350 us
  waiting for transfers between devices  145 us (41%)
  starting transfers between devices  116 us (33%)
  Pallas kernels  56.7 us (16%)
  local copies, waits for them, and re-layouts  16.5 us (5%)
  between operations  13.7 us (4%)
    ppermute x28, waiting for transfers between devices, shifted(): return lax.ppermute(array, 'tile', pairs)  123 us
    ppermute x28, starting transfers between devices, shifted(): return lax.ppermute(array, 'tile', pairs)  113 us
    pallas_call x4, Pallas kernels, compose(): pl.pallas_call(functools.partial(compose_kernel, count, first), grid_spec...  37.1 us
    ppermute x3, waiting for transfers between devices, local(): lax.ppermute(hop(factor, half, halves), 'tm', [(turn, turn - 1)])  22.1 us
    unnamed x58, local copies, waits for them, and re-layouts  16.4 us
    pallas_call x1, Pallas kernels, finish(): pl.pallas_call(functools.partial(finish_kernel, len(halves)), grid_spec=p...  8.34 us
  transfers between devices with their start and end apart: 32, of which 12 were waited for; matrix products, arithmetic and copies ran while one was open for 0% of the time, Pallas kernels for 12%

profile of v2, /device:TPU:0, one launch (start us, length us, event | category | flops | bytes accessed | tf_op | source)
XLA Modules:
  0.0 350.1 jit_solution(6109066103403167326)
XLA Ops:
  6.6 1.7 copy-done.1
  8.3 1.3 copy-done.5
  10.3 3.0 collective-permute-start.7
  13.3 2.6 collective-permute-start.10
  15.9 1.3 collective-permute-start.12
  17.9 1.1 pack.7.refs_0_
  19.1 1.6 collective-permute-start.22
  20.7 2.3 pack.6.refs_0_
  23.0 2.1 collective-permute-start.24
  25.2 38.5 %collective-permute-done.10.refs_4_ = bf16[1,96,1280]{2,1,0:T(8,128)(2,1)S(1)} collective-permute-done((bf16[1,96,1280]{2,1,0:T(8,128)(2,1)S(1)}, bf16[1,96,1280]{2,1,0:T(8,128)(2,1)S(1)}, u32[]{:S(2)}, u32[]{:S(2)}) %collective-permute-start.10) | collective-permute-done | bytes 245792 | tf_op jit(solution)/shard_map/ppermute | solution.py:261
  65.8 6.9 %collective-permute-start.15 = (bf16[3,96,1280]{2,1,0:T(8,128)(2,1)}, bf16[3,96,1280]{2,1,0:T(8,128)(2,1)}, u32[]{:S(2)}, u32[]{:S(2)}) collective-permute-start(bf16[3,96,1280]{2,1,0:T(8,128)(2,1)} %pack.6.refs_0_), channel_id=1, source_target_pairs={{0,2},{1,3},{2,4},{3,5},{4,6},{5,7},{6,0},{7,1},{8,10},{9,11},{10,... | collective-permute-start | bytes 2211848 | tf_op jit(solution)/shard_map/ppermute | solution.py:261
  72.7 15.0 %collective-permute-start.17 = (bf16[3,96,1280]{2,1,0:T(8,128)(2,1)}, bf16[3,96,1280]{2,1,0:T(8,128)(2,1)}, u32[]{:S(2)}, u32[]{:S(2)}) collective-permute-start(bf16[3,96,1280]{2,1,0:T(8,128)(2,1)} %pack.6.refs_0_), channel_id=1, source_target_pairs={{0,4},{1,5},{2,6},{3,7},{4,0},{5,1},{6,2},{7,3},{8,12},{9,13},{10,... | collective-permute-start | bytes 2211848 | tf_op jit(solution)/shard_map/ppermute | solution.py:261
  87.7 30.1 %collective-permute-done.24.refs_4_ = bf16[3,96,1280]{2,1,0:T(8,128)(2,1)} collective-permute-done((bf16[3,96,1280]{2,1,0:T(8,128)(2,1)S(1)}, bf16[3,96,1280]{2,1,0:T(8,128)(2,1)}, u32[]{:S(2)}, u32[]{:S(2)}) %collective-permute-start.24) | collective-permute-done | bytes 737312 | tf_op jit(solution)/shard_map/ppermute | solution.py:261
  117.8 2.4 collective-permute-start.19
  121.6 1.5 collective-permute-start.25
  125.8 23.6 %collective-permute-done.17.refs_4_ = bf16[3,96,1280]{2,1,0:T(8,128)(2,1)} collective-permute-done((bf16[3,96,1280]{2,1,0:T(8,128)(2,1)}, bf16[3,96,1280]{2,1,0:T(8,128)(2,1)}, u32[]{:S(2)}, u32[]{:S(2)}) %collective-permute-start.17) | collective-permute-done | bytes 737312 | tf_op jit(solution)/shard_map/ppermute | solution.py:261
  150.1 18.4 %collective-permute-start.1 = (bf16[1,96,1280]{2,1,0:T(8,128)(2,1)}, bf16[1,96,1280]{2,1,0:T(8,128)(2,1)S(1)}, u32[]{:S(2)}, u32[]{:S(2)}) collective-permute-start(bf16[1,96,1280]{2,1,0:T(8,128)(2,1)} %copy-done.11), channel_id=1, source_target_pairs={{0,2},{1,3},{2,4},{3,5},{4,6},{5,7},{6,0},{7,1},{8,10},{9,11},{10,... | collective-permute-start | bytes 737288 | tf_op jit(solution)/shard_map/ppermute | solution.py:261
  168.5 1.7 collective-permute-start.16
  170.5 2.6 collective-permute-done.27.refs_7_
  173.6 1.1 copy-done.14
  174.7 1.1 copy-done.24
  175.9 11.5 %compose.4 = (bf16[8,768,768]{2,1,0:T(8,128)(2,1)S(1)}, f32[8,96,768]{2,1,0:T(8,128)S(1)}, bf16[768,768]{1,0:T(8,128)(2,1)S(1)}, bf16[768,768]{1,0:T(8,128)(2,1)S(1)}) custom-call(s32[8]{0:T(128)S(1)} %stack.35.place_ref.places_ref, bf16[3,96,1280]{2,1,0:T(8,128)(2,1)S(1)} %copy-done.14, bf16[3,96,1280]{2,1,0:T(8,128)(2,1)S(1)} %copy-done.24, ...), custom_call_target="tpu_custom_call" | custom-call | flops 8153726976 | bytes 14155776 | tf_op jit(solution)/shard_map/compose/pallas_call | solution.py:128
  187.4 17.2 %collective-permute-start.3 = (bf16[1,96,1280]{2,1,0:T(8,128)(2,1)S(1)}, bf16[1,96,1280]{2,1,0:T(8,128)(2,1)S(1)}, u32[]{:S(2)}, u32[]{:S(2)}) collective-permute-start(bf16[1,96,1280]{2,1,0:T(8,128)(2,1)S(1)} %copy-done.12), channel_id=1, source_target_pairs={{0,4},{1,5},{2,6},{3,7},{4,0},{5,1},{6,2},{7,3},{8,12},{9,13},{10,... | collective-permute-start | bytes 737288 | tf_op jit(solution)/shard_map/ppermute | solution.py:261
  204.5 5.4 %collective-permute-start.5 = (bf16[1,96,1280]{2,1,0:T(8,128)(2,1)S(1)}, bf16[1,96,1280]{2,1,0:T(8,128)(2,1)S(1)}, u32[]{:S(2)}, u32[]{:S(2)}) collective-permute-start(bf16[1,96,1280]{2,1,0:T(8,128)(2,1)S(1)} %copy-done.12), channel_id=1, source_target_pairs={{0,6},{1,7},{2,0},{3,1},{4,2},{5,3},{6,4},{7,5},{8,14},{9,15},{10,... | collective-permute-start | bytes 737288 | tf_op jit(solution)/shard_map/ppermute | solution.py:261
  210.9 12.8 %collective-permute-start.11 = (bf16[1,96,1280]{2,1,0:T(8,128)(2,1)S(1)}, bf16[1,96,1280]{2,1,0:T(8,128)(2,1)S(1)}, u32[]{:S(2)}, u32[]{:S(2)}) collective-permute-start(bf16[1,96,1280]{2,1,0:T(8,128)(2,1)S(1)} %copy-done.16), channel_id=1, source_target_pairs={{0,4},{1,5},{2,6},{3,7},{4,0},{5,1},{6,2},{7,3},{8,12},{9,13},{10,... | collective-permute-start | bytes 737288 | tf_op jit(solution)/shard_map/ppermute | solution.py:261
  223.8 3.0 collective-permute-done.18.refs_5_
  226.7 1.8 collective-permute-start.13
  228.5 12.7 %collective-permute-done.20.refs_7_ = bf16[3,96,1280]{2,1,0:T(8,128)(2,1)S(1)} collective-permute-done((bf16[3,96,1280]{2,1,0:T(8,128)(2,1)}, bf16[3,96,1280]{2,1,0:T(8,128)(2,1)S(1)}, u32[]{:S(2)}, u32[]{:S(2)}) %collective-permute-start.20) | collective-permute-done | bytes 737312 | tf_op jit(solution)/shard_map/ppermute | solution.py:261
  241.2 12.1 %collective-permute-start.9 = (bf16[1,96,1280]{2,1,0:T(8,128)(2,1)S(1)}, bf16[1,96,1280]{2,1,0:T(8,128)(2,1)S(1)}, u32[]{:S(2)}, u32[]{:S(2)}) collective-permute-start(bf16[1,96,1280]{2,1,0:T(8,128)(2,1)S(1)} %copy-done.16), channel_id=1, source_target_pairs={{0,2},{1,3},{2,4},{3,5},{4,6},{5,7},{6,0},{7,1},{8,10},{9,11},{10,... | collective-permute-start | bytes 737288 | tf_op jit(solution)/shard_map/ppermute | solution.py:261
  253.3 15.7 %compose.5 = (bf16[8,768,768]{2,1,0:T(8,128)(2,1)S(1)}, f32[8,96,768]{2,1,0:T(8,128)S(1)}, bf16[768,768]{1,0:T(8,128)(2,1)S(1)}, bf16[768,768]{1,0:T(8,128)(2,1)S(1)}) custom-call(s32[8]{0:T(128)S(1)} %stack.35.place_ref.places_ref, bf16[3,96,1280]{2,1,0:T(8,128)(2,1)} %pack.6.refs_0_, ...), custom_call_target="tpu_custom_call", output_to_operand_aliasing={{0}: (11, {}), {1}: (12, {})} | custom-call | flops 8153726976 | bytes 14155776 | tf_op jit(solution)/shard_map/compose/pallas_call | solution.py:128
  269.5 1.6 collective-permute-start.2
  271.5 1.6 collective-permute-start.6
  273.1 5.0 %compose.6 = (bf16[8,768,768]{2,1,0:T(8,128)(2,1)S(1)}, f32[8,96,768]{2,1,0:T(8,128)S(1)}, bf16[768,768]{1,0:T(8,128)(2,1)S(1)}, bf16[768,768]{1,0:T(8,128)(2,1)S(1)}) custom-call(s32[8]{0:T(128)S(1)} %stack.35.place_ref.places_ref, bf16[1,96,1280]{2,1,0:T(8,128)(2,1)S(1)} %copy-done.10, ...), custom_call_target="tpu_custom_call", output_to_operand_aliasing={{0}: (11, {}), {1}: (12, {})} | custom-call | flops 2717908992 | bytes 4718592 | tf_op jit(solution)/shard_map/compose/pallas_call | solution.py:128
  278.1 5.1 %collective-permute-done.2.refs_3_ = bf16[1,96,1280]{2,1,0:T(8,128)(2,1)S(1)} collective-permute-done((bf16[1,96,1280]{2,1,0:T(8,128)(2,1)S(1)}, bf16[1,96,1280]{2,1,0:T(8,128)(2,1)S(1)}, u32[]{:S(2)}, u32[]{:S(2)}) %collective-permute-start.2) | collective-permute-done | bytes 245792 | tf_op jit(solution)/shard_map/ppermute | solution.py:261
  283.2 3.4 collective-permute-done.4.refs_5_
  286.6 2.6 collective-permute-done.6.refs_7_
  289.3 5.0 %compose.7 = (bf16[8,768,768]{2,1,0:T(8,128)(2,1)S(1)}, f32[8,96,768]{2,1,0:T(8,128)S(1)}, bf16[768,768]{1,0:T(8,128)(2,1)S(1)}, bf16[768,768]{1,0:T(8,128)(2,1)S(1)}) custom-call(s32[8]{0:T(128)S(1)} %stack.35.place_ref.places_ref, bf16[1,96,1280]{2,1,0:T(8,128)(2,1)S(1)} %copy-done.12, ...), custom_call_target="tpu_custom_call", output_to_operand_aliasing={{0}: (11, {}), {1}: (12, {})} | custom-call | flops 2717908992 | bytes 4718592 | tf_op jit(solution)/shard_map/compose/pallas_call | solution.py:128
  294.3 3.7 %copy-done = bf16[8,768,768]{2,1,0:T(8,128)(2,1)} copy-done((bf16[8,768,768]{2,1,0:T(8,128)(2,1)}, bf16[8,768,768]{2,1,0:T(8,128)(2,1)S(1)}, u32[]{:S(2)}) %copy-start) | copy-done | bytes 9437208
  297.9 1.4 copy-done.3
  300.4 1.5 broadcast_multiply_fusion.refs_0_
  301.9 1.4 copy-done.8
  303.3 2.1 hop.3
  305.4 1.1 collective-permute-start.28
  306.5 2.1 hop.4
  309.4 2.2 hop.5
  311.6 1.3 collective-permute-start.30
  312.9 22.1 %collective-permute-done.30.refs_3_ = bf16[768,768]{1,0:T(8,128)(2,1)S(1)} collective-permute-done((bf16[768,768]{1,0:T(8,128)(2,1)S(1)}, bf16[768,768]{1,0:T(8,128)(2,1)S(1)}, u32[]{:S(2)}, u32[]{:S(2)}) %collective-permute-start.30) | collective-permute-done | bytes 1179680 | tf_op jit(solution)/shard_map/ppermute | solution.py:291
  335.0 8.3 %finish.1 = f32[8,96,768]{2,1,0:T(8,128)} custom-call(s32[8]{0:T(128)S(1)} %stack.35.place_ref.places_ref, bf16[8,768,768]{2,1,0:T(8,128)(2,1)S(1)} %bitcast.9, f32[8,96,768]{2,1,0:T(8,128)S(1)} %copy-done.4, bf16[768,768]{1,0:T(8,128)(2,1)S(1)} %broadcast_multiply_fusion.refs_0_, bf16[768,768]{1,0:T(8,128)(2,1)S(1)} %collective-permute-done.28.refs_1_, ...), custom_call_target="tpu_custom_call" | custom-call | tf_op jit(solution)/shard_map/finish/pallas_call | solution.py:214
  (91 shorter events, 12.9 us)
Async XLA Ops:
  6.5 293.8 %all-gather.2.cloned.1.call-start = ((), (), s32[]{:S(2)}) async-start(), calls=%async_computation | async-start | bytes 1327104 | tf_op jit(solution)/shard_map/all_gather | solution.py:270
  10.3 8.8 %copy-start.9 = (bf16[1,96,1280]{2,1,0:T(8,128)(2,1)}, bf16[1,96,1280]{2,1,0:T(8,128)(2,1)S(1)}, u32[]{:S(2)}) copy-start(bf16[1,96,1280]{2,1,0:T(8,128)(2,1)S(1)} %pack.5.refs_0_) | copy-start | bytes 737284
  10.3 12.7 %collective-permute-start.7 = (bf16[1,96,1280]{2,1,0:T(8,128)(2,1)S(1)}, bf16[1,96,1280]{2,1,0:T(8,128)(2,1)S(1)}, u32[]{:S(2)}, u32[]{:S(2)}) collective-permute-start(bf16[1,96,1280]{2,1,0:T(8,128)(2,1)S(1)} %pack.5.refs_0_), channel_id=1, source_target_pairs={{0,1},{1,0},{2,3},{3,2},{4,5},{5,4},{6,7},{7,6},{8,9},{9,8},{10,11... | collective-permute-start | bytes 737288 | tf_op jit(solution)/shard_map/ppermute | solution.py:261
  13.3 50.3 %collective-permute-start.10 = (bf16[1,96,1280]{2,1,0:T(8,128)(2,1)S(1)}, bf16[1,96,1280]{2,1,0:T(8,128)(2,1)S(1)}, u32[]{:S(2)}, u32[]{:S(2)}) collective-permute-start(bf16[1,96,1280]{2,1,0:T(8,128)(2,1)S(1)} %pack.5.refs_0_), channel_id=1, source_target_pairs={{0,4},{1,5},{2,6},{3,7},{4,0},{5,1},{6,2},{7,3},{8,12},{9,13},{10,... | collective-permute-start | bytes 737288 | tf_op jit(solution)/shard_map/ppermute | solution.py:261
  15.9 48.4 %collective-permute-start.12 = (bf16[1,96,1280]{2,1,0:T(8,128)(2,1)S(1)}, bf16[1,96,1280]{2,1,0:T(8,128)(2,1)S(1)}, u32[]{:S(2)}, u32[]{:S(2)}) collective-permute-start(bf16[1,96,1280]{2,1,0:T(8,128)(2,1)S(1)} %pack.5.refs_0_), channel_id=1, source_target_pairs={{0,6},{1,7},{2,0},{3,1},{4,2},{5,3},{6,4},{7,5},{8,14},{9,15},{10,... | collective-permute-start | bytes 737288 | tf_op jit(solution)/shard_map/ppermute | solution.py:261
  17.3 47.8 %collective-permute-start.8 = (bf16[1,96,1280]{2,1,0:T(8,128)(2,1)S(1)}, bf16[1,96,1280]{2,1,0:T(8,128)(2,1)S(1)}, u32[]{:S(2)}, u32[]{:S(2)}) collective-permute-start(bf16[1,96,1280]{2,1,0:T(8,128)(2,1)S(1)} %pack.5.refs_0_), channel_id=1, source_target_pairs={{0,2},{1,3},{2,4},{3,5},{4,6},{5,7},{6,0},{7,1},{8,10},{9,11},{10,... | collective-permute-start | bytes 737288 | tf_op jit(solution)/shard_map/ppermute | solution.py:261
  19.1 45.3 %copy-start.13 = (bf16[3,96,1280]{2,1,0:T(8,128)(2,1)}, bf16[3,96,1280]{2,1,0:T(8,128)(2,1)S(1)}, u32[]{:S(2)}) copy-start(bf16[3,96,1280]{2,1,0:T(8,128)(2,1)S(1)} %pack.7.refs_0_) | copy-start | bytes 2211844
  19.1 104.6 %copy-start.25 = (f32[96,768]{1,0:T(8,128)S(1)}, f32[96,768]{1,0:T(8,128)}, u32[]{:S(2)}) copy-start(f32[96,768]{1,0:T(8,128)} %param.5) | copy-start | bytes 884740
  19.1 53.6 %collective-permute-start.22 = (bf16[3,96,1280]{2,1,0:T(8,128)(2,1)S(1)}, bf16[3,96,1280]{2,1,0:T(8,128)(2,1)}, u32[]{:S(2)}, u32[]{:S(2)}) collective-permute-start(bf16[3,96,1280]{2,1,0:T(8,128)(2,1)S(1)} %pack.7.refs_0_), channel_id=1, source_target_pairs={{0,2},{1,3},{2,4},{3,5},{4,6},{5,7},{6,0},{7,1},{8,10},{9,11},{10,... | collective-permute-start | bytes 2211848 | tf_op jit(solution)/shard_map/ppermute | solution.py:261
  20.7 103.7 %copy-start.2 = (f32[8,96,768]{2,1,0:T(8,128)S(1)}, f32[8,96,768]{2,1,0:T(8,128)}, u32[]{:S(2)}) copy-start(f32[8,96,768]{2,1,0:T(8,128)} %increment_ref.7) | copy-start | bytes 7077892
  20.7 103.7 %copy-start.6 = (bf16[8,96,768]{2,1,0:T(8,128)(2,1)S(1)}, bf16[8,96,768]{2,1,0:T(8,128)(2,1)}, u32[]{:S(2)}) copy-start(bf16[8,96,768]{2,1,0:T(8,128)(2,1)} %gain_ref.7) | copy-start | bytes 3538948
  23.0 97.7 %copy-start.15 = (bf16[1,96,1280]{2,1,0:T(8,128)(2,1)}, bf16[1,96,1280]{2,1,0:T(8,128)(2,1)S(1)}, u32[]{:S(2)}) copy-start(bf16[1,96,1280]{2,1,0:T(8,128)(2,1)S(1)} %collective-permute-done.7.refs_1_) | copy-start | bytes 737284
  23.0 94.8 %collective-permute-start.24 = (bf16[3,96,1280]{2,1,0:T(8,128)(2,1)S(1)}, bf16[3,96,1280]{2,1,0:T(8,128)(2,1)}, u32[]{:S(2)}, u32[]{:S(2)}) collective-permute-start(bf16[3,96,1280]{2,1,0:T(8,128)(2,1)S(1)} %pack.7.refs_0_), channel_id=1, source_target_pairs={{0,4},{1,5},{2,6},{3,7},{4,0},{5,1},{6,2},{7,3},{8,12},{9,13},{10,... | collective-permute-start | bytes 2211848 | tf_op jit(solution)/shard_map/ppermute | solution.py:261
  64.3 55.9 %collective-permute-start.26 = (bf16[3,96,1280]{2,1,0:T(8,128)(2,1)S(1)}, bf16[3,96,1280]{2,1,0:T(8,128)(2,1)}, u32[]{:S(2)}, u32[]{:S(2)}) collective-permute-start(bf16[3,96,1280]{2,1,0:T(8,128)(2,1)S(1)} %pack.7.refs_0_), channel_id=1, source_target_pairs={{0,6},{1,7},{2,0},{3,1},{4,2},{5,3},{6,4},{7,5},{8,14},{9,15},{10,... | collective-permute-start | bytes 2211848 | tf_op jit(solution)/shard_map/ppermute | solution.py:261
  65.1 55.7 %collective-permute-start.21 = (bf16[3,96,1280]{2,1,0:T(8,128)(2,1)S(1)}, bf16[3,96,1280]{2,1,0:T(8,128)(2,1)S(1)}, u32[]{:S(2)}, u32[]{:S(2)}) collective-permute-start(bf16[3,96,1280]{2,1,0:T(8,128)(2,1)S(1)} %pack.7.refs_0_), channel_id=1, source_target_pairs={{0,1},{1,0},{2,3},{3,2},{4,5},{5,4},{6,7},{7,6},{8,9},{9,8},{10,11... | collective-permute-start | bytes 2211848 | tf_op jit(solution)/shard_map/ppermute | solution.py:261
  65.8 57.4 %collective-permute-start.15 = (bf16[3,96,1280]{2,1,0:T(8,128)(2,1)}, bf16[3,96,1280]{2,1,0:T(8,128)(2,1)}, u32[]{:S(2)}, u32[]{:S(2)}) collective-permute-start(bf16[3,96,1280]{2,1,0:T(8,128)(2,1)} %pack.6.refs_0_), channel_id=1, source_target_pairs={{0,2},{1,3},{2,4},{3,5},{4,6},{5,7},{6,0},{7,1},{8,10},{9,11},{10,... | collective-permute-start | bytes 2211848 | tf_op jit(solution)/shard_map/ppermute | solution.py:261
  72.7 76.8 %collective-permute-start.17 = (bf16[3,96,1280]{2,1,0:T(8,128)(2,1)}, bf16[3,96,1280]{2,1,0:T(8,128)(2,1)}, u32[]{:S(2)}, u32[]{:S(2)}) collective-permute-start(bf16[3,96,1280]{2,1,0:T(8,128)(2,1)} %pack.6.refs_0_), channel_id=1, source_target_pairs={{0,4},{1,5},{2,6},{3,7},{4,0},{5,1},{6,2},{7,3},{8,12},{9,13},{10,... | collective-permute-start | bytes 2211848 | tf_op jit(solution)/shard_map/ppermute | solution.py:261
  117.8 32.3 %collective-permute-start.19 = (bf16[3,96,1280]{2,1,0:T(8,128)(2,1)}, bf16[3,96,1280]{2,1,0:T(8,128)(2,1)}, u32[]{:S(2)}, u32[]{:S(2)}) collective-permute-start(bf16[3,96,1280]{2,1,0:T(8,128)(2,1)} %pack.6.refs_0_), channel_id=1, source_target_pairs={{0,6},{1,7},{2,0},{3,1},{4,2},{5,3},{6,4},{7,5},{8,14},{9,15},{10,... | collective-permute-start | bytes 2211848 | tf_op jit(solution)/shard_map/ppermute | solution.py:261
  120.2 48.3 %collective-permute-start.23 = (bf16[3,96,1280]{2,1,0:T(8,128)(2,1)}, bf16[3,96,1280]{2,1,0:T(8,128)(2,1)}, u32[]{:S(2)}, u32[]{:S(2)}) collective-permute-start(bf16[3,96,1280]{2,1,0:T(8,128)(2,1)} %collective-permute-done.22.refs_2_), channel_id=1, source_target_pairs={{0,1},{1,0},{2,3},{3,2},{4,5},{5,4},{6,7},{7,6},{8,9},{9,8},{10,11... | collective-permute-start | bytes 2211848 | tf_op jit(solution)/shard_map/ppermute | solution.py:261
  121.6 48.6 %collective-permute-start.25 = (bf16[3,96,1280]{2,1,0:T(8,128)(2,1)}, bf16[3,96,1280]{2,1,0:T(8,128)(2,1)}, u32[]{:S(2)}, u32[]{:S(2)}) collective-permute-start(bf16[3,96,1280]{2,1,0:T(8,128)(2,1)} %collective-permute-done.24.refs_4_), channel_id=1, source_target_pairs={{0,1},{1,0},{2,3},{3,2},{4,5},{5,4},{6,7},{7,6},{8,9},{9,8},{10,11... | collective-permute-start | bytes 2211848 | tf_op jit(solution)/shard_map/ppermute | solution.py:261
  123.2 49.9 %collective-permute-start.27 = (bf16[3,96,1280]{2,1,0:T(8,128)(2,1)}, bf16[3,96,1280]{2,1,0:T(8,128)(2,1)}, u32[]{:S(2)}, u32[]{:S(2)}) collective-permute-start(bf16[3,96,1280]{2,1,0:T(8,128)(2,1)} %collective-permute-done.26.refs_6_), channel_id=1, source_target_pairs={{0,1},{1,0},{2,3},{3,2},{4,5},{5,4},{6,7},{7,6},{8,9},{9,8},{10,11... | collective-permute-start | bytes 2211848 | tf_op jit(solution)/shard_map/ppermute | solution.py:261
  125.8 61.5 %copy-start.12 = (bf16[1,96,1280]{2,1,0:T(8,128)(2,1)S(1)}, bf16[1,96,1280]{2,1,0:T(8,128)(2,1)}, u32[]{:S(2)}) copy-start(bf16[1,96,1280]{2,1,0:T(8,128)(2,1)} %copy-done.11) | copy-start | bytes 737284
  149.4 55.1 %collective-permute-start.14 = (bf16[3,96,1280]{2,1,0:T(8,128)(2,1)}, bf16[3,96,1280]{2,1,0:T(8,128)(2,1)S(1)}, u32[]{:S(2)}, u32[]{:S(2)}) collective-permute-start(bf16[3,96,1280]{2,1,0:T(8,128)(2,1)} %pack.6.refs_0_), channel_id=1, source_target_pairs={{0,1},{1,0},{2,3},{3,2},{4,5},{5,4},{6,7},{7,6},{8,9},{9,8},{10,11... | collective-permute-start | bytes 2211848 | tf_op jit(solution)/shard_map/ppermute | solution.py:261
  150.1 37.3 %collective-permute-start.1 = (bf16[1,96,1280]{2,1,0:T(8,128)(2,1)}, bf16[1,96,1280]{2,1,0:T(8,128)(2,1)S(1)}, u32[]{:S(2)}, u32[]{:S(2)}) collective-permute-start(bf16[1,96,1280]{2,1,0:T(8,128)(2,1)} %copy-done.11), channel_id=1, source_target_pairs={{0,2},{1,3},{2,4},{3,5},{4,6},{5,7},{6,0},{7,1},{8,10},{9,11},{10,... | collective-permute-start | bytes 737288 | tf_op jit(solution)/shard_map/ppermute | solution.py:261
  168.5 42.4 %collective-permute-start.16 = (bf16[3,96,1280]{2,1,0:T(8,128)(2,1)}, bf16[3,96,1280]{2,1,0:T(8,128)(2,1)S(1)}, u32[]{:S(2)}, u32[]{:S(2)}) collective-permute-start(bf16[3,96,1280]{2,1,0:T(8,128)(2,1)} %collective-permute-done.15.refs_2_), channel_id=1, source_target_pairs={{0,1},{1,0},{2,3},{3,2},{4,5},{5,4},{6,7},{7,6},{8,9},{9,8},{10,11... | collective-permute-start | bytes 2211848 | tf_op jit(solution)/shard_map/ppermute | solution.py:261
  170.2 56.5 %collective-permute-start.18 = (bf16[3,96,1280]{2,1,0:T(8,128)(2,1)}, bf16[3,96,1280]{2,1,0:T(8,128)(2,1)S(1)}, u32[]{:S(2)}, u32[]{:S(2)}) collective-permute-start(bf16[3,96,1280]{2,1,0:T(8,128)(2,1)} %collective-permute-done.17.refs_4_), channel_id=1, source_target_pairs={{0,1},{1,0},{2,3},{3,2},{4,5},{5,4},{6,7},{7,6},{8,9},{9,8},{10,11... | collective-permute-start | bytes 2211848 | tf_op jit(solution)/shard_map/ppermute | solution.py:261
  173.1 68.0 %collective-permute-start.20 = (bf16[3,96,1280]{2,1,0:T(8,128)(2,1)}, bf16[3,96,1280]{2,1,0:T(8,128)(2,1)S(1)}, u32[]{:S(2)}, u32[]{:S(2)}) collective-permute-start(bf16[3,96,1280]{2,1,0:T(8,128)(2,1)} %collective-permute-done.19.refs_6_), channel_id=1, source_target_pairs={{0,1},{1,0},{2,3},{3,2},{4,5},{5,4},{6,7},{7,6},{8,9},{9,8},{10,11... | collective-permute-start | bytes 2211848 | tf_op jit(solution)/shard_map/ppermute | solution.py:261
  175.9 35.1 %copy-start.16 = (bf16[1,96,1280]{2,1,0:T(8,128)(2,1)S(1)}, bf16[1,96,1280]{2,1,0:T(8,128)(2,1)}, u32[]{:S(2)}) copy-start(bf16[1,96,1280]{2,1,0:T(8,128)(2,1)} %copy-done.15) | copy-start | bytes 737284
  187.4 81.6 %collective-permute-start.3 = (bf16[1,96,1280]{2,1,0:T(8,128)(2,1)S(1)}, bf16[1,96,1280]{2,1,0:T(8,128)(2,1)S(1)}, u32[]{:S(2)}, u32[]{:S(2)}) collective-permute-start(bf16[1,96,1280]{2,1,0:T(8,128)(2,1)S(1)} %copy-done.12), channel_id=1, source_target_pairs={{0,4},{1,5},{2,6},{3,7},{4,0},{5,1},{6,2},{7,3},{8,12},{9,13},{10,... | collective-permute-start | bytes 737288 | tf_op jit(solution)/shard_map/ppermute | solution.py:261
  204.5 64.9 %collective-permute-start.5 = (bf16[1,96,1280]{2,1,0:T(8,128)(2,1)S(1)}, bf16[1,96,1280]{2,1,0:T(8,128)(2,1)S(1)}, u32[]{:S(2)}, u32[]{:S(2)}) collective-permute-start(bf16[1,96,1280]{2,1,0:T(8,128)(2,1)S(1)} %copy-done.12), channel_id=1, source_target_pairs={{0,6},{1,7},{2,0},{3,1},{4,2},{5,3},{6,4},{7,5},{8,14},{9,15},{10,... | collective-permute-start | bytes 737288 | tf_op jit(solution)/shard_map/ppermute | solution.py:261
  210.9 60.1 %collective-permute-start.11 = (bf16[1,96,1280]{2,1,0:T(8,128)(2,1)S(1)}, bf16[1,96,1280]{2,1,0:T(8,128)(2,1)S(1)}, u32[]{:S(2)}, u32[]{:S(2)}) collective-permute-start(bf16[1,96,1280]{2,1,0:T(8,128)(2,1)S(1)} %copy-done.16), channel_id=1, source_target_pairs={{0,4},{1,5},{2,6},{3,7},{4,0},{5,1},{6,2},{7,3},{8,12},{9,13},{10,... | collective-permute-start | bytes 737288 | tf_op jit(solution)/shard_map/ppermute | solution.py:261
  226.7 44.8 %collective-permute-start.13 = (bf16[1,96,1280]{2,1,0:T(8,128)(2,1)S(1)}, bf16[1,96,1280]{2,1,0:T(8,128)(2,1)S(1)}, u32[]{:S(2)}, u32[]{:S(2)}) collective-permute-start(bf16[1,96,1280]{2,1,0:T(8,128)(2,1)S(1)} %copy-done.16), channel_id=1, source_target_pairs={{0,6},{1,7},{2,0},{3,1},{4,2},{5,3},{6,4},{7,5},{8,14},{9,15},{10,... | collective-permute-start | bytes 737288 | tf_op jit(solution)/shard_map/ppermute | solution.py:261
  241.2 31.9 %collective-permute-start.9 = (bf16[1,96,1280]{2,1,0:T(8,128)(2,1)S(1)}, bf16[1,96,1280]{2,1,0:T(8,128)(2,1)S(1)}, u32[]{:S(2)}, u32[]{:S(2)}) collective-permute-start(bf16[1,96,1280]{2,1,0:T(8,128)(2,1)S(1)} %copy-done.16), channel_id=1, source_target_pairs={{0,2},{1,3},{2,4},{3,5},{4,6},{5,7},{6,0},{7,1},{8,10},{9,11},{10,... | collective-permute-start | bytes 737288 | tf_op jit(solution)/shard_map/ppermute | solution.py:261
  253.2 19.8 %copy-start.10 = (bf16[1,96,1280]{2,1,0:T(8,128)(2,1)S(1)}, bf16[1,96,1280]{2,1,0:T(8,128)(2,1)}, u32[]{:S(2)}) copy-start(bf16[1,96,1280]{2,1,0:T(8,128)(2,1)} %copy-done.9) | copy-start | bytes 737284
  253.2 19.8 %copy-start.18 = (bf16[1,96,1280]{2,1,0:T(8,128)(2,1)S(1)}, bf16[1,96,1280]{2,1,0:T(8,128)(2,1)}, u32[]{:S(2)}) copy-start(bf16[1,96,1280]{2,1,0:T(8,128)(2,1)} %copy-done.17) | copy-start | bytes 737284
  253.2 19.8 %copy-start.20 = (bf16[1,96,1280]{2,1,0:T(8,128)(2,1)S(1)}, bf16[1,96,1280]{2,1,0:T(8,128)(2,1)}, u32[]{:S(2)}) copy-start(bf16[1,96,1280]{2,1,0:T(8,128)(2,1)} %copy-done.19) | copy-start | bytes 737284
  253.3 19.8 %copy-start.22 = (bf16[1,96,1280]{2,1,0:T(8,128)(2,1)S(1)}, bf16[1,96,1280]{2,1,0:T(8,128)(2,1)}, u32[]{:S(2)}) copy-start(bf16[1,96,1280]{2,1,0:T(8,128)(2,1)} %copy-done.21) | copy-start | bytes 737284
  268.9 9.2 %collective-permute-start = (bf16[1,96,1280]{2,1,0:T(8,128)(2,1)S(1)}, bf16[1,96,1280]{2,1,0:T(8,128)(2,1)S(1)}, u32[]{:S(2)}, u32[]{:S(2)}) collective-permute-start(bf16[1,96,1280]{2,1,0:T(8,128)(2,1)S(1)} %copy-done.12), channel_id=1, source_target_pairs={{0,1},{1,0},{2,3},{3,2},{4,5},{5,4},{6,7},{7,6},{8,9},{9,8},{10,11... | collective-permute-start | bytes 737288 | tf_op jit(solution)/shard_map/ppermute | solution.py:261
  269.5 13.7 %collective-permute-start.2 = (bf16[1,96,1280]{2,1,0:T(8,128)(2,1)S(1)}, bf16[1,96,1280]{2,1,0:T(8,128)(2,1)S(1)}, u32[]{:S(2)}, u32[]{:S(2)}) collective-permute-start(bf16[1,96,1280]{2,1,0:T(8,128)(2,1)S(1)} %collective-permute-done.1.refs_2_), channel_id=1, source_target_pairs={{0,1},{1,0},{2,3},{3,2},{4,5},{5,4},{6,7},{7,6},{8,9},{9,8},{10,11... | collective-permute-start | bytes 737288 | tf_op jit(solution)/shard_map/ppermute | solution.py:261
  271.0 15.6 %collective-permute-start.4 = (bf16[1,96,1280]{2,1,0:T(8,128)(2,1)S(1)}, bf16[1,96,1280]{2,1,0:T(8,128)(2,1)S(1)}, u32[]{:S(2)}, u32[]{:S(2)}) collective-permute-start(bf16[1,96,1280]{2,1,0:T(8,128)(2,1)S(1)} %collective-permute-done.3.refs_4_), channel_id=1, source_target_pairs={{0,1},{1,0},{2,3},{3,2},{4,5},{5,4},{6,7},{7,6},{8,9},{9,8},{10,11... | collective-permute-start | bytes 737288 | tf_op jit(solution)/shard_map/ppermute | solution.py:261
  271.5 17.8 %collective-permute-start.6 = (bf16[1,96,1280]{2,1,0:T(8,128)(2,1)S(1)}, bf16[1,96,1280]{2,1,0:T(8,128)(2,1)S(1)}, u32[]{:S(2)}, u32[]{:S(2)}) collective-permute-start(bf16[1,96,1280]{2,1,0:T(8,128)(2,1)S(1)} %collective-permute-done.5.refs_6_), channel_id=1, source_target_pairs={{0,1},{1,0},{2,3},{3,2},{4,5},{5,4},{6,7},{7,6},{8,9},{9,8},{10,11... | collective-permute-start | bytes 737288 | tf_op jit(solution)/shard_map/ppermute | solution.py:261
  300.4 34.6 %slice-start = ((s8[9437184]{0:T(1024)(128)(4,1)}), s8[4194304]{0:T(1024)(128)(4,1)S(1)}, s32[]{:S(2)}) async-start(s8[9437184]{0:T(1024)(128)(4,1)} %bitcast.8), calls=%async_computation.1 | async-start | bytes 8388608
  303.2 31.7 %slice-start.1 = ((s8[9437184]{0:T(1024)(128)(4,1)}), s8[4194304]{0:T(1024)(128)(4,1)S(1)}, s32[]{:S(2)}) async-start(s8[9437184]{0:T(1024)(128)(4,1)} %bitcast.8), calls=%async_computation.2 | async-start | bytes 8388608
  305.4 29.6 %slice-start.2 = ((s8[9437184]{0:T(1024)(128)(4,1)}), s8[1048576]{0:T(1024)(128)(4,1)S(1)}, s32[]{:S(2)}) async-start(s8[9437184]{0:T(1024)(128)(4,1)} %bitcast.8), calls=%async_computation.3 | async-start | bytes 2097152
  305.4 1.1 collective-permute-start.28
  308.6 0.7 collective-permute-start.29
  309.4 25.6 %copy-start.4 = (f32[8,96,768]{2,1,0:T(8,128)S(1)}, f32[8,96,768]{2,1,0:T(8,128)}, u32[]{:S(2)}) copy-start(f32[8,96,768]{2,1,0:T(8,128)} %copy-done.3) | copy-start | bytes 7077892
  311.6 23.4 %collective-permute-start.30 = (bf16[768,768]{1,0:T(8,128)(2,1)S(1)}, bf16[768,768]{1,0:T(8,128)(2,1)S(1)}, u32[]{:S(2)}, u32[]{:S(2)}) collective-permute-start(bf16[768,768]{1,0:T(8,128)(2,1)S(1)} %hop.5), channel_id=1, source_target_pairs={{8,0},{9,1},{10,2},{11,3},{12,4},{13,5},{14,6},{15,7}} | collective-permute-start | bytes 3538952 | tf_op jit(solution)/shard_map/ppermute | solution.py:291
  (13 other events, 16.4 us)
Sparse Core Ops, SparseCore 0:
  124.5 76.4 all-gather.1

commit v3 on v2

--- a/solution.py
+++ b/solution.py
@@ -25,20 +25,30 @@
     return lax.dot_general(left, right, (((1,), (1,)), ((), ())), preferred_element_type=F32)
 
 
-def pack_kernel(count, place_ref, gain_ref, increment_ref, packed_ref):
-    rows, width = gain_ref.shape[1:]
+def packed_half(increment, place, count):
+    rows, width = increment.shape
     used, half = half_width(rows, count)
-    packed_ref[0, :, :width] = gain_ref[0]
-    shift = lax.rem(width - place_ref[0] * rows, width)
-    turned = pltpu.roll(increment_ref[0], shift, 1)[:, :half]
+    turned = pltpu.roll(increment, lax.rem(width - place * rows, width), 1)[:, :half]
     column = lax.broadcasted_iota(jnp.int32, turned.shape, 1)
     halved = (column < rows) | (column >= used - rows)
     weight = jnp.where(column < used, jnp.where(halved, 0.5, 1.0), 0.0)
-    packed_ref[0, :, width:] = (turned * weight).astype(BF16)
-
-
-def pack(places, gains, increments, low, high):
-    count = places.shape[0]
+    return (turned * weight).astype(BF16)
+
+
+def unpacked_half(piece, start, width):
+    piece = piece.astype(F32)
+    rest = width - piece.shape[1]
+    wide = jnp.concatenate([piece, jnp.zeros((piece.shape[0], rest), F32)], axis=1) if rest else piece
+    return pltpu.roll(wide, start, 1)
+
+
+def pack_kernel(count, place_ref, gain_ref, increment_ref, packed_ref):
+    width = gain_ref.shape[2]
+    packed_ref[0, :, :width] = gain_ref[0]
+    packed_ref[0, :, width:] = packed_half(increment_ref[0], place_ref[0], count)
+
+
+def pack(place, gains, increments, count, low, high):
     steps, rows, width = gains.shape
     _, half = half_width(rows, count)
     return pl.pallas_call(
@@ -55,57 +65,75 @@
         out_shape=jax.ShapeDtypeStruct((high - low, rows, width + half), BF16),
         compiler_params=pltpu.CompilerParams(vmem_limit_bytes=8 * MIB),
         name="pack",
-    )(places, gains, increments)
-
-
-def compose_kernel(count, first, places_ref, *refs):
-    shards, refs = refs[:count], refs[count:]
-    if not first:
+    )(place, gains, increments)
+
+
+def pack_terminal_kernel(count, place_ref, terminal_ref, packed_ref):
+    packed_ref[...] = packed_half(terminal_ref[...], place_ref[0], count)
+
+
+def pack_terminal(place, terminal, count):
+    rows, width = terminal.shape
+    _, half = half_width(rows, count)
+    return pl.pallas_call(
+        functools.partial(pack_terminal_kernel, count),
+        in_specs=[pl.BlockSpec(memory_space=pltpu.SMEM), pl.BlockSpec(memory_space=pltpu.VMEM)],
+        out_shape=jax.ShapeDtypeStruct((rows, half), BF16),
+        name="pack_terminal",
+    )(place, terminal)
+
+
+def compose_kernel(groups, first, last_ref, places_ref, *refs):
+    blocks, refs = refs[:groups], refs[groups:]
+    if first:
+        ends, refs = refs[:groups], refs[groups:]
+    else:
         factor_in, half_in, refs = refs[0], refs[1], refs[4:]
     factor_out, own_out, factor_end, half_end, gain, factor, half, middle, total = refs
-    rows = shards[0].shape[1]
+    line, _, rows, _ = blocks[0].shape
     width = factor.shape[0]
     turn = pl.program_id(0)
-    starts = [pl.multiple_of(places_ref[i] * rows, 16) for i in range(count)]
-    for start, shard in zip(starts, shards):
-        gain[pl.ds(start, rows), :] = shard[0, :, :width]
-
-    def increment(start, shard):
-        piece = shard[0, :, width:].astype(F32)
-        rest = width - piece.shape[1]
-        wide = jnp.concatenate([piece, jnp.zeros((rows, rest), F32)], axis=1) if rest else piece
-        return pltpu.roll(wide, start, 1)
+    starts = [
+        [pl.multiple_of(places_ref[1 + j * line + i] * rows, 16) for i in range(line)] for j in range(groups)
+    ]
+    spots = [(j, i, starts[j][i]) for j in range(groups) for i in range(line)]
+    for j, i, start in spots:
+        gain[pl.ds(start, rows), :] = blocks[j][i, 0, :, :width]
 
     @pl.when(turn == 0)
     def _():
         if first:
             factor[...] = gain[...]
-            for start, shard in zip(starts, shards):
-                half[pl.ds(start, rows), :] = increment(start, shard).astype(BF16)
+            scale = jnp.where(last_ref[0] == 1, 1.0, 0.0)
+            for j, i, start in spots:
+                half[pl.ds(start, rows), :] = (unpacked_half(ends[j][i], start, width) * scale).astype(BF16)
         else:
             factor[...] = factor_in[...]
             half[...] = half_in[...]
 
-    def step():
+    def extend():
         for j in range(0, width, TILE):
             cols = slice(j, j + TILE)
-            middle[:, cols] = jnp.dot(gain[...], half[:, cols], preferred_element_type=F32).astype(BF16)
             factor[:, cols] = jnp.dot(gain[...], factor[:, cols], preferred_element_type=F32).astype(BF16)
-        for j in range(0, width, TILE):
-            total[:, j:j + TILE] = nt(middle[...], gain[j:j + TILE, :])
-        for start, shard in zip(starts, shards):
-            span = pl.ds(start, rows)
-            half[span, :] = (total[span, :] + increment(start, shard)).astype(BF16)
 
     if first:
-        pl.when(turn > 0)(step)
+        pl.when(turn > 0)(extend)
     else:
-        step()
-
-    picked = lax.broadcasted_iota(jnp.int32, (rows, width), 1) == starts[0] + lax.broadcasted_iota(
+        extend()
+    for j in range(0, width, TILE):
+        cols = slice(j, j + TILE)
+        middle[:, cols] = jnp.dot(gain[...], half[:, cols], preferred_element_type=F32).astype(BF16)
+    for j in range(0, width, TILE):
+        total[:, j:j + TILE] = nt(middle[...], gain[j:j + TILE, :])
+    for j, i, start in spots:
+        span = pl.ds(start, rows)
+        half[span, :] = (total[span, :] + unpacked_half(blocks[j][i, 0, :, width:], start, width)).astype(BF16)
+
+    mine = pl.multiple_of(places_ref[0] * rows, 16)
+    picked = lax.broadcasted_iota(jnp.int32, (rows, width), 1) == mine + lax.broadcasted_iota(
         jnp.int32, (rows, width), 0
     )
-    own = half[pl.ds(starts[0], rows), :].astype(F32)
+    own = half[pl.ds(mine, rows), :].astype(F32)
     own_out[0] = own + nt(jnp.where(picked, 1.0, 0.0).astype(BF16), half[...])
     factor_out[0] = factor[...]
 
@@ -115,25 +143,27 @@
         half_end[...] = half[...]
 
 
-def compose(places, shards, state, low, steps):
-    count = len(shards)
-    turns, rows, packed_width = shards[0].shape
-    width = count * rows
+def compose(last, places, blocks, ends, state, low, steps):
+    groups = len(blocks)
+    line, turns, rows, packed_width = blocks[0].shape
+    width = line * groups * rows
     first = state is None
-    whole = pl.BlockSpec((width, width), lambda i, p: (0, 0))
+    whole = pl.BlockSpec((width, width), lambda i, *p: (0, 0))
     anywhere = pl.BlockSpec(memory_space=pl.ANY)
-    in_specs = [pl.BlockSpec((1, rows, packed_width), lambda i, p: (turns - 1 - i, 0, 0))] * count
-    if not first:
+    in_specs = [pl.BlockSpec((line, 1, rows, packed_width), lambda i, *p: (0, turns - 1 - i, 0, 0))] * groups
+    if first:
+        in_specs += [pl.BlockSpec(ends[0].shape, lambda i, *p: (0, 0, 0))] * groups
+    else:
         in_specs += [whole, whole, anywhere, anywhere]
     return pl.pallas_call(
-        functools.partial(compose_kernel, count, first),
+        functools.partial(compose_kernel, groups, first),
         grid_spec=pltpu.PrefetchScalarGridSpec(
-            num_scalar_prefetch=1,
+            num_scalar_prefetch=2,
             grid=(turns,),
             in_specs=in_specs,
             out_specs=[
-                pl.BlockSpec((1, width, width), lambda i, p: (low + turns - 1 - i, 0, 0)),
-                pl.BlockSpec((1, rows, width), lambda i, p: (low + turns - 1 - i, 0, 0)),
+                pl.BlockSpec((1, width, width), lambda i, *p: (low + turns - 1 - i, 0, 0)),
+                pl.BlockSpec((1, rows, width), lambda i, *p: (low + turns - 1 - i, 0, 0)),
                 whole,
                 whole,
             ],
@@ -146,13 +176,13 @@
             jax.ShapeDtypeStruct((width, width), BF16),
             jax.ShapeDtypeStruct((width, width), BF16),
         ],
-        input_output_aliases={} if first else {count + 3: 0, count + 4: 1},
+        input_output_aliases={} if first else {groups + 4: 0, groups + 5: 1},
         compiler_params=pltpu.CompilerParams(vmem_limit_bytes=32 * MIB),
         cost_estimate=pl.CostEstimate(
             flops=6 * turns * width**3, bytes_accessed=8 * turns * width * width, transcendentals=0
         ),
         name="compose",
-    )(places, *shards, *(() if first else (state[2], state[3], state[0], state[1])))
+    )(last, places, *blocks, *(ends if first else (state[2], state[3], state[0], state[1])))
 
 
 def arrived_sum(refs):
@@ -233,14 +263,9 @@
 def pieces(steps):
     if steps < 8:
         return [(0, steps, False)]
-    bulk = (steps - steps // 4) // 2
-    rest = steps - 2 * bulk
-    return [
-        (steps - bulk, steps, False),
-        (rest, rest + bulk, False),
-        (rest // 2, rest, True),
-        (0, rest // 2, False),
-    ]
+    small = steps // 8
+    cuts = [steps, 6 * small, 4 * small, 2 * small, small, 0]
+    return [(low, high, turn == 3) for turn, (high, low) in enumerate(zip(cuts, cuts[1:]))]
 
 
 def local(gains, increments, terminal):
@@ -250,46 +275,38 @@
     across = count // line
     steps = gains.shape[0]
     place = lax.axis_index("tile").astype(jnp.int32)
-    block = lax.axis_index("tm")
-
-    def shifted(array, along, over):
+    last = (lax.axis_index("tm") == blocks - 1).astype(jnp.int32).reshape(1)
+    lines = [[a * across + b for a in range(line)] for b in range(across)]
+
+    def shifted(array, over):
         pairs = [
-            (a * across + b, (a + along) % line * across + (b + over) % across)
-            for a in range(line)
-            for b in range(across)
+            (a * across + b, a * across + (b + over) % across) for a in range(line) for b in range(across)
         ]
         return lax.ppermute(array, "tile", pairs)
 
+    def gathered(array):
+        return lax.all_gather(array, "tile", axis_index_groups=lines)
+
+    def both(array, across_first):
+        if across_first:
+            return [gathered(shifted(array, j) if j else array) for j in range(across)]
+        whole = gathered(array)
+        return [shifted(whole, j) if j else whole for j in range(across)]
+
     places = jnp.stack(
-        [
-            (place // across - i + line) % line * across + (place % across - j + across) % across
-            for i in range(line)
-            for j in range(across)
-        ]
+        [place]
+        + [i * across + (place % across - j + across) % across for j in range(across) for i in range(line)]
     )
-    full_terminal = lax.all_gather(terminal.astype(BF16), "tile", axis=0, tiled=True)
+    ends = both(pack_terminal(place.reshape(1), terminal, count), False)
     state = None
     for low, high, across_first in pieces(steps):
-        own = pack(places, gains, increments, low, high)
-        shards = {}
-        if across_first:
-            for j in range(across):
-                shards[0, j] = shifted(own, 0, j) if j else own
-            for i in range(1, line):
-                for j in range(across):
-                    shards[i, j] = shifted(shards[0, j], i, 0)
-        else:
-            for i in range(line):
-                shards[i, 0] = shifted(own, i, 0) if i else own
-                for j in range(1, across):
-                    shards[i, j] = shifted(shards[i, 0], 0, j)
-        ordered = [shards[i, j] for i in range(line) for j in range(across)]
-        state = compose(places, ordered, state, low, steps)
+        own = pack(place.reshape(1), gains, increments, count, low, high)
+        state = compose(last, places, both(own, across_first), ends, state, low, steps)
     factors, own, factor, half = state
-    halves = [jnp.where(block == blocks - 1, 0.5, 0.0).astype(BF16) * full_terminal]
-    for turn in range(blocks - 1, 0, -1):
+    halves = [lax.ppermute(half, "tm", [(blocks - 1, blocks - 2)])]
+    for turn in range(blocks - 2, 0, -1):
         halves.append(lax.ppermute(hop(factor, half, halves), "tm", [(turn, turn - 1)]))
-    return finish(places, factors, own, halves)
+    return finish(place.reshape(1), factors, own, halves)
 
 
 def solution(mesh):

time: 351 us -> 299 us (0.85)
  starting transfers between devices: 116 us -> 10.7 us
  blocking collectives: 0 us -> 78 us
  waiting for transfers between devices: 145 us -> 130 us
  local copies, waits for them, and re-layouts: 16.5 us -> 8.52 us
    ppermute x28 -> x6, waiting for transfers between devices: 123 us -> 0.02 us  [shifted(): return lax.ppermute(array, 'tile', pairs)]
    all_gather x1 -> x3, waiting for transfers between devices: 0.01 us -> 107 us  [gathered(): return lax.all_gather(array, 'tile', axis_index_groups=lines)]
    ppermute x28 -> x6, starting transfers between devices: 113 us -> 7.82 us  [shifted(): return lax.ppermute(array, 'tile', pairs)]
    all_gather x0 -> x4, blocking collectives: none -> 78 us  [gathered(): return lax.all_gather(array, 'tile', axis_index_groups=lines)]
    unnamed x58 -> x22, local copies, waits for them, and re-layouts: 16.4 us -> 8.43 us
    pallas_call x4 -> x6, Pallas kernels: 37.1 us -> 44.6 us  [the longest x5 42.8 us: compose(): pl.pallas_call(functools.partial(compose_kernel, groups, first), grid_spe...]
    ppermute x3 -> x2, waiting for transfers between devices: 22.1 us -> 22.5 us  [local(): lax.ppermute(hop(factor, half, halves), 'tm', [(turn, turn - 1)])]
  transfers between devices with their start and end apart: 32 -> 12, of which waited for: 12 -> 4; matrix products, arithmetic and copies ran while one was open for 0% -> 0% of each run, Pallas kernels for 12% -> 14%
where the time goes in v3:
time: 299 us
  waiting for transfers between devices  130 us (43%)
  blocking collectives  78 us (26%)
  Pallas kernels  58.9 us (20%)
  between operations  13.3 us (4%)
  starting transfers between devices  10.7 us (4%)
  local copies, waits for them, and re-layouts  8.52 us (3%)
    all_gather x3, waiting for transfers between devices, gathered(): return lax.all_gather(array, 'tile', axis_index_groups=lines)  107 us
    all_gather x4, blocking collectives, gathered(): return lax.all_gather(array, 'tile', axis_index_groups=lines)  78 us
    pallas_call x5, Pallas kernels, compose(): pl.pallas_call(functools.partial(compose_kernel, groups, first), grid_spe...  42.8 us
    ppermute x2, waiting for transfers between devices, local(): lax.ppermute(hop(factor, half, halves), 'tm', [(turn, turn - 1)])  22.5 us
    unnamed x22, local copies, waits for them, and re-layouts  8.43 us
    ppermute x6, starting transfers between devices, shifted(): return lax.ppermute(array, 'tile', pairs)  7.82 us
    pallas_call x1, Pallas kernels, finish(): pl.pallas_call(functools.partial(finish_kernel, len(halves)), grid_spec=p...  7.81 us
  transfers between devices with their start and end apart: 12, of which 4 were waited for; matrix products, arithmetic and copies ran while one was open for 0% of the time, Pallas kernels for 14%

profile of v3, /device:TPU:0, one launch (start us, length us, event | category | flops | bytes accessed | tf_op | source)
XLA Modules:
  0.0 299.1 jit_solution(17411425586150744307)
XLA Ops:
  6.5 1.7 copy-done
  8.2 1.3 copy-done.2
  9.5 0.4 pack.9
  9.9 0.8 copy-done.5
  10.6 0.0 all-gather.15.cloned.1.call-update
  10.7 0.0 all-gather.13.cloned.1.call-start
  10.7 0.6 copy-done.1
  11.3 0.3 copy-done.3
  11.6 0.4 pack.8
  12.0 0.8 copy-done.6
  12.8 0.0 all-gather.13.cloned.1.call-update
  12.8 0.0 all-gather.11.cloned.1.call-start
  12.9 0.4 pack.7
  13.3 0.0 copy-start.4
  13.3 0.8 copy-done.4
  14.1 0.0 all-gather.11.cloned.1.call-update
  14.1 43.0 %all-gather.15.cloned.1.call-done = bf16[8,96,1280]{2,1,0:T(8,128)(2,1)} async-done(((bf16[2,96,1280]{2,1,0:T(8,128)(2,1)}), bf16[8,96,1280]{2,1,0:T(8,128)(2,1)}) %all-gather.15.cloned.1.call-update) | async-done | bytes 1966096 | tf_op jit(solution)/shard_map/all_gather | solution.py:288
  57.1 1.5 collective-permute-start.4
  58.6 42.5 %all-gather.13.cloned.1.call-done = bf16[8,96,1280]{2,1,0:T(8,128)(2,1)} async-done(((bf16[2,96,1280]{2,1,0:T(8,128)(2,1)}), bf16[8,96,1280]{2,1,0:T(8,128)(2,1)}) %all-gather.13.cloned.1.call-update) | async-done | bytes 1966096 | tf_op jit(solution)/shard_map/all_gather | solution.py:288
  101.1 1.5 collective-permute-start.3
  102.6 1.8 pack_terminal.1
  104.3 18.5 %all-gather.6 = bf16[384,512]{1,0:T(8,128)(2,1)} all-gather(bf16[96,512]{1,0:T(8,128)(2,1)} %pack_terminal.1), channel_id=8, replica_groups={{0,2,4,6},{1,3,5,7},{8,10,12,14},{9,11,13,15},{16,18,20,22},{17,19,21,2..., dimensions={0}, use_global_device_ids=true | all-gather | bytes 491520 | tf_op jit(solution)/shard_map/all_gather | solution.py:288
  122.9 0.0 collective-permute-start.5
  122.9 0.9 pack.6
  123.7 2.0 collective-permute-start.1
  125.8 0.2 pack.5
  126.0 0.7 copy-done.7
  126.6 21.7 %all-gather.11.cloned.1.call-done = bf16[8,96,1280]{2,1,0:T(8,128)(2,1)} async-done(((bf16[2,96,1280]{2,1,0:T(8,128)(2,1)}), bf16[8,96,1280]{2,1,0:T(8,128)(2,1)}) %all-gather.11.cloned.1.call-update) | async-done | bytes 1966096 | tf_op jit(solution)/shard_map/all_gather | solution.py:288
  148.3 1.4 collective-permute-start.2
  149.7 20.5 %all-gather.1 = bf16[4,96,1280]{2,1,0:T(8,128)(2,1)S(1)} all-gather(bf16[1,96,1280]{2,1,0:T(8,128)(2,1)} %pack.6), channel_id=3, replica_groups={{0,2,4,6},{1,3,5,7},{8,10,12,14},{9,11,13,15},{16,18,20,22},{17,19,21,2..., dimensions={0}, use_global_device_ids=true | all-gather | bytes 1228800 | tf_op jit(solution)/shard_map/all_gather | solution.py:288
  170.2 20.1 %all-gather = bf16[4,96,1280]{2,1,0:T(8,128)(2,1)S(1)} all-gather(bf16[1,96,1280]{2,1,0:T(8,128)(2,1)} %copy-done.7), channel_id=2, replica_groups={{0,2,4,6},{1,3,5,7},{8,10,12,14},{9,11,13,15},{16,18,20,22},{17,19,21,2..., dimensions={0}, use_global_device_ids=true | all-gather | bytes 1228800 | tf_op jit(solution)/shard_map/all_gather | solution.py:288
  190.3 0.1 stack.36.places_ref
  190.4 0.0 collective-permute-done.1
  190.4 1.5 collective-permute-start
  191.9 18.9 %all-gather.2 = bf16[4,96,1280]{2,1,0:T(8,128)(2,1)S(1)} all-gather(bf16[1,96,1280]{2,1,0:T(8,128)(2,1)} %collective-permute-done.1), channel_id=4, replica_groups={{0,2,4,6},{1,3,5,7},{8,10,12,14},{9,11,13,15},{16,18,20,22},{17,19,21,2..., dimensions={0}, use_global_device_ids=true | all-gather | bytes 1228800 | tf_op jit(solution)/shard_map/all_gather | solution.py:288
  210.7 1.5 copy-done.10
  212.3 10.4 %compose.5 = (bf16[8,768,768]{2,1,0:T(8,128)(2,1)S(1)}, f32[8,96,768]{2,1,0:T(8,128)S(1)}, bf16[768,768]{1,0:T(8,128)(2,1)S(1)}, bf16[768,768]{1,0:T(8,128)(2,1)S(1)}) custom-call(s32[1]{0:T(128)} %bitcast.1.last_ref, s32[9]{0:T(128)S(1)} %stack.36.places_ref, bf16[4,2,96,1280]{3,2,1,0:T(8,128)(2,1)S(1)} %bitcast.26, ...), custom_call_target="tpu_custom_call" | custom-call | flops 5435817984 | bytes 9437184 | tf_op jit(solution)/shard_map/compose/pallas_call | solution.py:158
  222.7 11.1 %compose.6 = (bf16[8,768,768]{2,1,0:T(8,128)(2,1)S(1)}, f32[8,96,768]{2,1,0:T(8,128)S(1)}, bf16[768,768]{1,0:T(8,128)(2,1)S(1)}, bf16[768,768]{1,0:T(8,128)(2,1)S(1)}) custom-call(s32[1]{0:T(128)} %bitcast.1.last_ref, s32[9]{0:T(128)S(1)} %stack.36.places_ref, bf16[4,2,96,1280]{3,2,1,0:T(8,128)(2,1)S(1)} %bitcast.24, ...), custom_call_target="tpu_custom_call", output_to_operand_aliasing={{0}: (6, {}), {1}: (7, {})} | custom-call | flops 5435817984 | bytes 9437184 | tf_op jit(solution)/shard_map/compose/pallas_call | solution.py:158
  233.9 11.3 %compose.7 = (bf16[8,768,768]{2,1,0:T(8,128)(2,1)S(1)}, f32[8,96,768]{2,1,0:T(8,128)S(1)}, bf16[768,768]{1,0:T(8,128)(2,1)S(1)}, bf16[768,768]{1,0:T(8,128)(2,1)S(1)}) custom-call(s32[1]{0:T(128)} %bitcast.1.last_ref, s32[9]{0:T(128)S(1)} %stack.36.places_ref, bf16[4,2,96,1280]{3,2,1,0:T(8,128)(2,1)S(1)} %bitcast.22, ...), custom_call_target="tpu_custom_call", output_to_operand_aliasing={{0}: (6, {}), {1}: (7, {})} | custom-call | flops 5435817984 | bytes 9437184 | tf_op jit(solution)/shard_map/compose/pallas_call | solution.py:158
  245.2 5.0 %compose.8 = (bf16[8,768,768]{2,1,0:T(8,128)(2,1)S(1)}, f32[8,96,768]{2,1,0:T(8,128)S(1)}, bf16[768,768]{1,0:T(8,128)(2,1)S(1)}, bf16[768,768]{1,0:T(8,128)(2,1)S(1)}) custom-call(s32[1]{0:T(128)} %bitcast.1.last_ref, s32[9]{0:T(128)S(1)} %stack.36.places_ref, bf16[4,1,96,1280]{3,2,1,0:T(8,128)(2,1)S(1)} %bitcast.19, ...), custom_call_target="tpu_custom_call", output_to_operand_aliasing={{0}: (6, {}), {1}: (7, {})} | custom-call | flops 2717908992 | bytes 4718592 | tf_op jit(solution)/shard_map/compose/pallas_call | solution.py:158
  250.2 5.0 %compose.9 = (bf16[8,768,768]{2,1,0:T(8,128)(2,1)S(1)}, f32[8,96,768]{2,1,0:T(8,128)S(1)}, bf16[768,768]{1,0:T(8,128)(2,1)S(1)}, bf16[768,768]{1,0:T(8,128)(2,1)S(1)}) custom-call(s32[1]{0:T(128)} %bitcast.1.last_ref, s32[9]{0:T(128)S(1)} %stack.36.places_ref, bf16[4,1,96,1280]{3,2,1,0:T(8,128)(2,1)S(1)} %bitcast.18, ...), custom_call_target="tpu_custom_call", output_to_operand_aliasing={{0}: (6, {}), {1}: (7, {})} | custom-call | flops 2717908992 | bytes 4718592 | tf_op jit(solution)/shard_map/compose/pallas_call | solution.py:158
  255.2 0.7 collective-permute-start.6
  256.0 2.1 hop.2
  258.1 0.7 collective-permute-start.7
  258.9 2.1 hop.3
  261.0 1.3 collective-permute-start.8
  262.3 22.5 %collective-permute-done.8.refs_2_ = bf16[768,768]{1,0:T(8,128)(2,1)S(1)} collective-permute-done((bf16[768,768]{1,0:T(8,128)(2,1)S(1)}, bf16[768,768]{1,0:T(8,128)(2,1)S(1)}, u32[]{:S(2)}, u32[]{:S(2)}) %collective-permute-start.8) | collective-permute-done | bytes 1179680 | tf_op jit(solution)/shard_map/ppermute | solution.py:308
  284.8 7.8 %finish.1 = f32[8,96,768]{2,1,0:T(8,128)} custom-call(s32[1]{0:T(128)} %bitcast.place_ref.places_ref, bf16[8,768,768]{2,1,0:T(8,128)(2,1)S(1)} %get-tuple-element.41.factor_ref, f32[8,96,768]{2,1,0:T(8,128)S(1)} %get-tuple-element.42.own_ref, bf16[768,768]{1,0:T(8,128)(2,1)S(1)} %collective-permute-done.6.refs_0_, ...), custom_call_target="tpu_custom_call" | custom-call | tf_op jit(solution)/shard_map/finish/pallas_call | solution.py:244
  (20 shorter events, 0.0 us)
Async XLA Ops:
  6.5 50.6 %all-gather.15.cloned.1.call-start = ((), (), s32[]{:S(2)}) async-start(), calls=%async_computation.2 | async-start | bytes 2457600 | tf_op jit(solution)/shard_map/all_gather | solution.py:288
  6.5 1.7 copy-start
  8.2 1.3 copy-start.2
  9.5 1.8 copy-start.1
  9.5 2.2 copy-start.3
  9.9 0.8 copy-start.5
  10.7 90.4 %all-gather.13.cloned.1.call-start = ((), (), s32[]{:S(2)}) async-start(), calls=%async_computation.1 | async-start | bytes 2457600 | tf_op jit(solution)/shard_map/all_gather | solution.py:288
  12.0 0.8 copy-start.6
  12.8 135.5 %all-gather.11.cloned.1.call-start = ((), (), s32[]{:S(2)}) async-start(), calls=%async_computation | async-start | bytes 2457600 | tf_op jit(solution)/shard_map/all_gather | solution.py:288
  13.3 0.8 copy-start.4
  57.1 153.6 %collective-permute-start.4 = (bf16[4,2,96,1280]{3,2,1,0:T(8,128)(2,1)}, bf16[4,2,96,1280]{3,2,1,0:T(8,128)(2,1)}, u32[]{:S(2)}, u32[]{:S(2)}) collective-permute-start(bf16[4,2,96,1280]{3,2,1,0:T(8,128)(2,1)} %bitcast.25), channel_id=1, source_target_pairs={{0,1},{1,0},{2,3},{3,2},{4,5},{5,4},{6,7},{7,6},{8,9},{9,8},{10,11... | collective-permute-start | bytes 5898248 | tf_op jit(solution)/shard_map/ppermute | solution.py:285
  101.1 121.6 %collective-permute-start.3 = (bf16[4,2,96,1280]{3,2,1,0:T(8,128)(2,1)}, bf16[4,2,96,1280]{3,2,1,0:T(8,128)(2,1)}, u32[]{:S(2)}, u32[]{:S(2)}) collective-permute-start(bf16[4,2,96,1280]{3,2,1,0:T(8,128)(2,1)} %bitcast.23), channel_id=1, source_target_pairs={{0,1},{1,0},{2,3},{3,2},{4,5},{5,4},{6,7},{7,6},{8,9},{9,8},{10,11... | collective-permute-start | bytes 5898248 | tf_op jit(solution)/shard_map/ppermute | solution.py:285
  122.9 87.9 %collective-permute-start.5 = (bf16[4,96,512]{2,1,0:T(8,128)(2,1)}, bf16[4,96,512]{2,1,0:T(8,128)(2,1)}, u32[]{:S(2)}, u32[]{:S(2)}) collective-permute-start(bf16[4,96,512]{2,1,0:T(8,128)(2,1)} %bitcast.16.refs_2_), channel_id=1, source_target_pairs={{0,1},{1,0},{2,3},{3,2},{4,5},{5,4},{6,7},{7,6},{8,9},{9,8},{10,11... | collective-permute-start | bytes 1179656 | tf_op jit(solution)/shard_map/ppermute | solution.py:285
  123.7 66.6 %collective-permute-start.1 = (bf16[1,96,1280]{2,1,0:T(8,128)(2,1)}, bf16[1,96,1280]{2,1,0:T(8,128)(2,1)}, u32[]{:S(2)}, u32[]{:S(2)}) collective-permute-start(bf16[1,96,1280]{2,1,0:T(8,128)(2,1)} %pack.6), channel_id=1, source_target_pairs={{0,1},{1,0},{2,3},{3,2},{4,5},{5,4},{6,7},{7,6},{8,9},{9,8},{10,11... | collective-permute-start | bytes 737288 | tf_op jit(solution)/shard_map/ppermute | solution.py:285
  125.9 0.7 copy-start.7
  148.3 85.5 %collective-permute-start.2 = (bf16[4,2,96,1280]{3,2,1,0:T(8,128)(2,1)}, bf16[4,2,96,1280]{3,2,1,0:T(8,128)(2,1)}, u32[]{:S(2)}, u32[]{:S(2)}) collective-permute-start(bf16[4,2,96,1280]{3,2,1,0:T(8,128)(2,1)} %bitcast.21), channel_id=1, source_target_pairs={{0,1},{1,0},{2,3},{3,2},{4,5},{5,4},{6,7},{7,6},{8,9},{9,8},{10,11... | collective-permute-start | bytes 5898248 | tf_op jit(solution)/shard_map/ppermute | solution.py:285
  190.4 59.8 %collective-permute-start = (bf16[4,1,96,1280]{3,2,1,0:T(8,128)(2,1)S(1)}, bf16[4,1,96,1280]{3,2,1,0:T(8,128)(2,1)S(1)}, u32[]{:S(2)}, u32[]{:S(2)}) collective-permute-start(bf16[4,1,96,1280]{3,2,1,0:T(8,128)(2,1)S(1)} %bitcast.17), channel_id=1, source_target_pairs={{0,1},{1,0},{2,3},{3,2},{4,5},{5,4},{6,7},{7,6},{8,9},{9,8},{10,11... | collective-permute-start | bytes 2949128 | tf_op jit(solution)/shard_map/ppermute | solution.py:285
  210.7 1.5 copy-start.10
  212.3 10.4 %copy-start.9 = (bf16[8,96,1280]{2,1,0:T(8,128)(2,1)S(1)}, bf16[8,96,1280]{2,1,0:T(8,128)(2,1)}, u32[]{:S(2)}) copy-start(bf16[8,96,1280]{2,1,0:T(8,128)(2,1)} %all-gather.13.cloned.1.call-done) | copy-start | bytes 5898244
  222.7 11.1 %copy-start.8 = (bf16[8,96,1280]{2,1,0:T(8,128)(2,1)S(1)}, bf16[8,96,1280]{2,1,0:T(8,128)(2,1)}, u32[]{:S(2)}) copy-start(bf16[8,96,1280]{2,1,0:T(8,128)(2,1)} %all-gather.11.cloned.1.call-done) | copy-start | bytes 5898244
  255.2 0.7 collective-permute-start.6
  258.1 0.7 collective-permute-start.7
  261.0 23.8 %collective-permute-start.8 = (bf16[768,768]{1,0:T(8,128)(2,1)S(1)}, bf16[768,768]{1,0:T(8,128)(2,1)S(1)}, u32[]{:S(2)}, u32[]{:S(2)}) collective-permute-start(bf16[768,768]{1,0:T(8,128)(2,1)S(1)} %hop.3), channel_id=1, source_target_pairs={{8,0},{9,1},{10,2},{11,3},{12,4},{13,5},{14,6},{15,7}} | collective-permute-start | bytes 3538952 | tf_op jit(solution)/shard_map/ppermute | solution.py:308
Sparse Core Ops, SparseCore 0:
  10.8 46.2 all-gather.14
  58.7 42.3 all-gather.12
  102.7 45.6 all-gather.10

commit v4 on v3

v4 whole, which is shorter than its diff:
```python
import functools
import math

import jax
import jax.numpy as jnp
from jax import lax
from jax.experimental import pallas as pl
from jax.experimental.pallas import tpu as pltpu
from jax.sharding import PartitionSpec as P

BF16 = jnp.bfloat16
F32 = jnp.float32
LANES = 128
TILE = 256
LINE = 4
MIB = 1024 * 1024


def half_width(rows, count):
    used = (count // 2 + 1) * rows
    return used, -(-used // LANES) * LANES


def nt(left, right):
    return lax.dot_general(left, right, (((1,), (1,)), ((), ())), preferred_element_type=F32)


def packed_half(increment, place, count):
    rows, width = increment.shape
    used, half = half_width(rows, count)
    turned = pltpu.roll(increment, lax.rem(width - place * rows, width), 1)[:, :half]
    column = lax.broadcasted_iota(jnp.int32, turned.shape, 1)
    halved = (column < rows) | (column >= used - rows)
    weight = jnp.where(column < used, jnp.where(halved, 0.5, 1.0), 0.0)
    return (turned * weight).astype(BF16)


def unpacked_half(piece, start, width):
    piece = piece.astype(F32)
    rest = width - piece.shape[1]
    wide = jnp.concatenate([piece, jnp.zeros((piece.shape[0], rest), F32)], axis=1) if rest else piece
    return pltpu.roll(wide, start, 1)


def pack_kernel(count, low, high, place_ref, gain_ref, increment_ref, *refs):
    packed_ref = refs[-1]
    width = gain_ref.shape[2]
    stride = width + half_width(gain_ref.shape[1], count)[1]
    for step in range(high - low):
        base = step * stride
        packed_ref[:, base:base + width] = gain_ref[step]
        packed_ref[:, base + width:base + stride] = packed_half(increment_ref[step], place_ref[0], count)
    if len(refs) > 1:
        packed_ref[:, (high - low) * stride:] = packed_half(refs[0][...], place_ref[0], count)


def pack(place, gains, increments, terminal, count, low, high):
    rows, width = gains.shape[1:]
    half = half_width(rows, count)[1]
    ends = [] if terminal is None else [terminal]
    lanes = (high - low) * (width + half) + half * len(ends)
    return pl.pallas_call(
        functools.partial(pack_kernel, count, low, high),
        in_specs=[pl.BlockSpec(memory_space=pltpu.SMEM)] + [pl.BlockSpec(memory_space=pltpu.VMEM)] * (2 + len(ends)),
        out_specs=pl.BlockSpec(memory_space=pltpu.VMEM),
        out_shape=jax.ShapeDtypeStruct((rows, lanes), BF16),
        compiler_params=pltpu.CompilerParams(vmem_limit_bytes=24 * MIB),
        name="pack",
    )(place, gains[low:high], increments[low:high], *ends)


def compose_kernel(lines, parts, first, last_ref, places_ref, *refs):
    sizes = [lines[j] for j in range(len(lines))]
    blocks = []
    for size in sizes:
        blocks.append(refs[:size])
        refs = refs[size:]
    ends = []
    if first:
        for _ in range(parts):
            ends.append([])
            for size in sizes:
                ends[-1].append(refs[:size])
                refs = refs[size:]
    else:
        factor_in, half_in, refs = refs[0], refs[1], refs[5:]
    factor_out, own_out, mine_out, factor_end, half_end, gain, factor, half, middle, total = refs
    width = factor.shape[0]
    turn = pl.program_id(0)
    spots = []
    for j, group in enumerate(blocks):
        for n, ref in enumerate(group):
            inner = ref.shape[0] if len(ref.shape) == 3 else 1
            for i in range(inner):
                spots.append((j, n, i, len(ref.shape) == 3))
    rows = width // len(spots)
    starts = [pl.multiple_of(places_ref[1 + k] * rows, 16) for k in range(len(spots))]

    def lanes(refs_of, spot, cut):
        j, n, i, stacked = spot
        return refs_of[j][n][i, :, cut] if stacked else refs_of[j][n][:, cut]

    for spot, start in zip(spots, starts):
        gain[pl.ds(start, rows), :] = lanes(blocks, spot, slice(0, width))

    @pl.when(turn == 0)
    def _():
        if first:
            factor[...] = gain[...]
            scale = jnp.where(last_ref[0] == 1, 1.0, 0.0)
            for spot, start in zip(spots, starts):
                piece = jnp.concatenate([lanes(end, spot, slice(None)) for end in ends], axis=1)
                half[pl.ds(start, rows), :] = (unpacked_half(piece, start, width) * scale).astype(BF16)
        else:
            factor[...] = factor_in[...]
            half[...] = half_in[...]

    def extend():
        for j in range(0, width, TILE):
            cols = slice(j, j + TILE)
            factor[:, cols] = jnp.dot(gain[...], factor[:, cols], preferred_element_type=F32).astype(BF16)

    if first:
        pl.when(turn > 0)(extend)
    else:
        extend()
    for j in range(0, width, TILE):
        cols = slice(j, j + TILE)
        middle[:, cols] = jnp.dot(gain[...], half[:, cols], preferred_element_type=F32).astype(BF16)
    for j in range(0, width, TILE):
        total[:, j:j + TILE] = nt(middle[...], gain[j:j + TILE, :])
    for spot, start in zip(spots, starts):
        span = pl.ds(start, rows)
        piece = lanes(blocks, spot, slice(width, None))
        half[span, :] = (total[span, :] + unpacked_half(piece, start, width)).astype(BF16)

    mine = pl.multiple_of(places_ref[0] * rows, 16)
    picked = lax.broadcasted_iota(jnp.int32, (rows, width), 1) == mine + lax.broadcasted_iota(
        jnp.int32, (rows, width), 0
    )
    own = half[pl.ds(mine, rows), :].astype(F32)
    own_out[0] = own + nt(jnp.where(picked, 1.0, 0.0).astype(BF16), half[...])
    mine_out[0] = factor[pl.ds(mine, rows), :]
    factor_out[0] = factor[...]

    @pl.when(turn == pl.num_programs(0) - 1)
    def _():
        factor_end[...] = factor[...]
        half_end[...] = half[...]


def compose(last, places, blocks, state, low, turns, steps):
    lines = [len(group) for group in blocks]
    flat = [block for group in blocks for block in group]
    rows = flat[0].shape[-2]
    width = rows * sum(block.shape[0] if block.ndim == 3 else 1 for block in flat)
    half = half_width(rows, width // rows)[1]
    stride = width + half
    first = state is None
    whole = pl.BlockSpec((width, width), lambda i, *p: (0, 0))
    anywhere = pl.BlockSpec(memory_space=pl.ANY)

    def spec(block, size, place):
        if block.ndim == 3:
            return pl.BlockSpec((block.shape[0], rows, size), lambda i, *p: (0, 0, place(i)))
        return pl.BlockSpec((rows, size), lambda i, *p: (0, place(i)))

    in_specs = [spec(block, stride, lambda i: turns - 1 - i) for block in flat]
    args = list(flat)
    parts = half // math.gcd(turns * stride, half)
    if first:
        for n in range(parts):
            at = turns * stride * parts // half + n
            in_specs += [spec(block, half // parts, lambda i, at=at: at) for block in flat]
            args += flat
    else:
        in_specs += [whole, whole, anywhere, anywhere, anywhere]
        args += [state[3], state[4], state[0], state[1], state[2]]
    base = 2 + len(flat) + 2
    return pl.pallas_call(
        functools.partial(compose_kernel, lines, parts, first),
        grid_spec=pltpu.PrefetchScalarGridSpec(
            num_scalar_prefetch=2,
            grid=(turns,),
            in_specs=in_specs,
            out_specs=[
                pl.BlockSpec((1, width, width), lambda i, *p: (low + turns - 1 - i, 0, 0)),
                pl.BlockSpec((1, rows, width), lambda i, *p: (low + turns - 1 - i, 0, 0)),
                pl.BlockSpec((1, rows, width), lambda i, *p: (low + turns - 1 - i, 0, 0)),
                whole,
                whole,
            ],
            scratch_shapes=[pltpu.VMEM((width, width), BF16) for _ in range(4)]
            + [pltpu.VMEM((width, width), F32)],
        ),
        out_shape=[
            jax.ShapeDtypeStruct((steps, width, width), BF16),
            jax.ShapeDtypeStruct((steps, rows, width), F32),
            jax.ShapeDtypeStruct((steps, rows, width), BF16),
            jax.ShapeDtypeStruct((width, width), BF16),
            jax.ShapeDtypeStruct((width, width), BF16),
        ],
        input_output_aliases={} if first else {base: 0, base + 1: 1, base + 2: 2},
        compiler_params=pltpu.CompilerParams(vmem_limit_bytes=32 * MIB),
        cost_estimate=pl.CostEstimate(
            flops=6 * turns * width**3, bytes_accessed=8 * turns * width * width, transcendentals=0
        ),
        name="compose",
    )(last, places, *args)


def upper_blocks(width):
    return [(a, b) for a in range(0, width, TILE) for b in range(a, width, TILE)]


def identity(size):
    row = lax.broadcasted_iota(jnp.int32, (size, size), 0)
    column = lax.broadcasted_iota(jnp.int32, (size, size), 1)
    return jnp.where(row == column, 1.0, 0.0).astype(BF16)


def fold(half_ref, packed_ref):
    one = identity(TILE)
    for n, (a, b) in enumerate(upper_blocks(half_ref.shape[0])):
        block = half_ref[a:a + TILE, b:b + TILE]
        if a != b:
            block = block.astype(F32) + nt(one, half_ref[b:b + TILE, a:a + TILE])
        packed_ref[n] = block.astype(BF16)


def arrived_sum(refs, n):
    value = refs[0][n]
    for extra in refs[1:]:
        value = value + extra[n]
    return value


def fold_kernel(half_ref, packed_ref):
    fold(half_ref, packed_ref)


def hop_kernel(arrived, factor_ref, half_ref, *refs):
    out_ref, covariance, middle, ahead = refs[arrived:]
    width = factor_ref.shape[0]
    for n, (a, b) in enumerate(upper_blocks(width)):
        covariance[a:a + TILE, b:b + TILE] = arrived_sum(refs[:arrived], n)
    for j in range(0, width, TILE):
        cols = slice(j, j + TILE)
        middle[:, cols] = jnp.dot(
            factor_ref[:, :j + TILE], covariance[:j + TILE, cols], preferred_element_type=F32
        ).astype(BF16)
    for j in range(0, width, TILE):
        cols = slice(j, j + TILE)
        ahead[:, cols] = (nt(middle[...], factor_ref[cols, :]) + half_ref[:, cols].astype(F32)).astype(BF16)
    fold(ahead, out_ref)


def hop(factor, half, packed):
    width = factor.shape[0]
    shape = (len(upper_blocks(width)), TILE, TILE)
    square = pltpu.VMEM((width, width), BF16)
    if not packed:
        return pl.pallas_call(
            fold_kernel,
            out_shape=jax.ShapeDtypeStruct(shape, BF16),
            compiler_params=pltpu.CompilerParams(vmem_limit_bytes=16 * MIB),
            name="fold",
        )(half)
    return pl.pallas_call(
        functools.partial(hop_kernel, len(packed)),
        out_shape=jax.ShapeDtypeStruct(shape, BF16),
        scratch_shapes=[square, square, square],
        compiler_params=pltpu.CompilerParams(vmem_limit_bytes=20 * MIB),
        cost_estimate=pl.CostEstimate(flops=4 * width**3, bytes_accessed=10 * width * width, transcendentals=0),
        name="hop",
    )(factor, half, *packed)


def finish_kernel(arrived, factor_ref, own_ref, mine_ref, *refs):
    out_ref, covariance, middle = refs[arrived:]
    turn = pl.program_id(0)
    rows = own_ref.shape[1]
    steps = mine_ref.shape[0]
    width = covariance.shape[0]

    @pl.when(turn == 0)
    def _():
        one = identity(TILE)
        for n, (a, b) in enumerate(upper_blocks(width)):
            block = arrived_sum(refs[:arrived], n)
            turned = nt(one, block)
            if a == b:
                covariance[a:a + TILE, b:b + TILE] = (block.astype(F32) + turned).astype(BF16)
            else:
                covariance[a:a + TILE, b:b + TILE] = block
                covariance[b:b + TILE, a:a + TILE] = turned.astype(BF16)
        mine = mine_ref[...].reshape(steps * rows, width)
        for j in range(0, width, TILE):
            cols = slice(j, j + TILE)
            middle[:, cols] = jnp.dot(mine, covariance[:, cols], preferred_element_type=F32).astype(BF16)

    left = middle[pl.ds(pl.multiple_of(turn * rows, 16), rows), :]
    out_ref[0] = nt(left, factor_ref[0]) + own_ref[0]


def finish(factors, own, mine, packed):
    steps, rows, width = own.shape
    whole = pl.BlockSpec(packed[0].shape, lambda i: (0, 0, 0))
    return pl.pallas_call(
        functools.partial(finish_kernel, len(packed)),
        grid=(steps,),
        in_specs=[
            pl.BlockSpec((1, width, width), lambda i: (i, 0, 0)),
            pl.BlockSpec((1, rows, width), lambda i: (i, 0, 0)),
            pl.BlockSpec(mine.shape, lambda i: (0, 0, 0)),
        ]
        + [whole] * len(packed),
        out_specs=pl.BlockSpec((1, rows, width), lambda i: (i, 0, 0)),
        scratch_shapes=[pltpu.VMEM((width, width), BF16), pltpu.VMEM((steps * rows, width), BF16)],
        out_shape=jax.ShapeDtypeStruct((steps, rows, width), F32),
        compiler_params=pltpu.CompilerParams(vmem_limit_bytes=24 * MIB),
        name="finish",
    )(factors, own, mine, *packed)


def pieces(steps):
    small = max(steps // 8, 1)
    low = steps - 3 * small
    return [
        (low, steps, "shifts"),
        (low - 2 * small, low, "lines"),
        (low - 4 * small, low - 2 * small, "lines"),
        (0, low - 4 * small, "across"),
    ]


def local(gains, increments, terminal):
    count = lax.axis_size("tile")
    blocks = lax.axis_size("tm")
    line = math.gcd(count, LINE)
    across = count // line
    steps = gains.shape[0]
    place = lax.axis_index("tile").astype(jnp.int32)
    last = (lax.axis_index("tm") == blocks - 1).astype(jnp.int32).reshape(1)
    lines = [[a * across + b for a in range(line)] for b in range(across)]

    def shifted(array, along, over):
        pairs = [
            (a * across + b, (a + along) % line * across + (b + over) % across)
            for a in range(line)
            for b in range(across)
        ]
        return lax.ppermute(array, "tile", pairs) if along or over else array

    def gathered(array):
        return lax.all_gather(array, "tile", axis_index_groups=lines)

    def spread(array, kind):
        if kind == "shifts":
            along = [shifted(array, i, 0) for i in range(line)]
            return [[shifted(part, 0, j) for part in along] for j in range(across)]
        if kind == "lines":
            whole = gathered(array)
            return [[shifted(whole, 0, j)] for j in range(across)]
        return [[gathered(shifted(array, 0, j))] for j in range(across)]

    def order(kind):
        found = [place]
        for j in range(across):
            for i in range(line):
                along = (place // across - i + line) % line if kind == "shifts" else i
                found.append(along * across + (place % across - j + across) % across)
        return jnp.stack(found)

    state = None
    for low, high, kind in pieces(steps):
        own = pack(place.reshape(1), gains, increments, terminal if state is None else None, count, low, high)
        state = compose(last, order(kind), spread(own, kind), state, low, high - low, steps)
    factors, own, mine, factor, half = state
    packed = []
    for turn in range(blocks - 1, 0, -1):
        packed.append(lax.ppermute(hop(factor, half, packed), "tm", [(turn, turn - 1)]))
    return finish(factors, own, mine, packed)


def solution(mesh):
    return jax.shard_map(
        local,
        mesh=mesh,
        in_specs=(P("tm", "tile", None), P("tm", "tile", None), P("tile", None)),
        out_specs=P("tm", "tile", None),
        check_vma=False,
    )
```

time: 299 us -> 298 us (level)
  blocking collectives: 78 us -> 40.8 us
  waiting for transfers between devices: 130 us -> 164 us
  starting transfers between devices: 10.7 us -> 17.5 us
  Pallas kernels: 58.9 us -> 54 us
    all_gather x4 -> x2, blocking collectives: 78 us -> 40.8 us  [gathered(): return lax.all_gather(array, 'tile', axis_index_groups=lines)]
    ppermute x9 -> x13, waiting for transfers between devices: 22.5 us -> 59.2 us  [the longest x10 42.2 us: shifted(): return lax.ppermute(array, 'tile', pairs) if along or over else array]
    unnamed x22 -> x8, local copies, waits for them, and re-layouts: 8.43 us -> 0.22 us
    ppermute x9 -> x13, starting transfers between devices: 10.6 us -> 17.4 us  [the longest x10 14.7 us: shifted(): return lax.ppermute(array, 'tile', pairs) if along or over else array]
    slice x0 -> x6, local copies, waits for them, and re-layouts: none -> 5.63 us  [the longest x3 3.62 us: pack(): increments[low:high]]
    pallas_call x14 -> x12, Pallas kernels: 58.9 us -> 54 us  [the longest x4 40.7 us: compose(): pl.pallas_call(functools.partial(compose_kernel, lines, parts, first), gr...]
    all_gather x3 -> x2, waiting for transfers between devices: 107 us -> 105 us  [gathered(): return lax.all_gather(array, 'tile', axis_index_groups=lines)]
  transfers between devices with their start and end apart: 12 -> 15, of which waited for: 4 -> 6; matrix products, arithmetic and copies ran while one was open for 0% -> 1% of each run, Pallas kernels for 14% -> 9%
where the time goes in v4:
time: 298 us; the launch traced here: 296 us
  waiting for transfers between devices  164 us (55%)
  Pallas kernels  54 us (18%)
  blocking collectives  40.8 us (14%)
  starting transfers between devices  17.5 us (6%)
  between operations  13.6 us (5%)
  local copies, waits for them, and re-layouts  6.02 us (2%)
    all_gather x2, waiting for transfers between devices, gathered(): return lax.all_gather(array, 'tile', axis_index_groups=lines)  105 us
    ppermute x10, waiting for transfers between devices, shifted(): return lax.ppermute(array, 'tile', pairs) if along or over else array  42.2 us
    all_gather x2, blocking collectives, gathered(): return lax.all_gather(array, 'tile', axis_index_groups=lines)  40.8 us
    pallas_call x4, Pallas kernels, compose(): pl.pallas_call(functools.partial(compose_kernel, lines, parts, first), gr...  40.7 us
    ppermute x3, waiting for transfers between devices, local(): lax.ppermute(hop(factor, half, packed), 'tm', [(turn, turn - 1)])  17 us
    ppermute x10, starting transfers between devices, shifted(): return lax.ppermute(array, 'tile', pairs) if along or over else array  14.7 us
    pallas_call x1, Pallas kernels, finish(): pl.pallas_call(functools.partial(finish_kernel, len(packed)), grid=(steps...  6.73 us
  transfers between devices with their start and end apart: 15, of which 6 were waited for; matrix products, arithmetic and copies ran while one was open for 1% of the time, Pallas kernels for 9%

profile of v4, /device:TPU:0, one launch (start us, length us, event | category | flops | bytes accessed | tf_op | source)
XLA Modules:
  0.0 296.1 jit_solution(4095996917920641865)
XLA Ops:
  6.5 1.4 fusion
  8.0 0.2 copy-done.3
  8.2 1.0 pack.6
  9.2 0.0 all-gather.9.cloned.1.call-update
  9.3 0.0 all-gather.7.cloned.1.call-start
  9.3 0.0 copy-start
  9.3 1.0 pack.5
  10.4 0.0 all-gather.7.cloned.1.call-update
  10.4 1.2 slice.31.increment_ref
  11.6 1.0 slice.30.gain_ref
  12.7 0.4 pack.7.refs_0_.refs_8_.refs_16_
  13.1 3.1 %collective-permute-start.3 = (bf16[96,4352]{1,0:T(8,128)(2,1)S(1)}, bf16[96,4352]{1,0:T(8,128)(2,1)}, u32[]{:S(2)}, u32[]{:S(2)}) collective-permute-start(bf16[96,4352]{1,0:T(8,128)(2,1)S(1)} %pack.7.refs_0_.refs_8_.refs_16_), channel_id=1, source_target_pairs={{0,2},{1,3},{2,4},{3,5},{4,6},{5,7},{6,0},{7,1},{8,10},{9,11},{10,... | collective-permute-start | bytes 2506760 | tf_op jit(solution)/shard_map/ppermute | solution.py:353
  16.2 2.6 collective-permute-start.4
  18.8 1.3 collective-permute-start.5
  20.1 1.5 collective-permute-start.6
  21.6 1.0 slice.25.increment_ref
  22.6 0.9 slice.24.gain_ref
  23.5 0.2 pack.4
  23.7 0.6 collective-permute-start
  24.3 20.6 %collective-permute-done = bf16[96,1280]{1,0:T(8,128)(2,1)S(1)} collective-permute-done((bf16[96,1280]{1,0:T(8,128)(2,1)S(1)}, bf16[96,1280]{1,0:T(8,128)(2,1)S(1)}, u32[]{:S(2)}, u32[]{:S(2)}) %collective-permute-start) | collective-permute-done | bytes 245792 | tf_op jit(solution)/shard_map/ppermute | solution.py:353
  44.9 57.7 %all-gather.9.cloned.1.call-done = bf16[384,2560]{1,0:T(8,128)(2,1)} async-done(((bf16[96,2560]{1,0:T(8,128)(2,1)}), bf16[384,2560]{1,0:T(8,128)(2,1)}) %all-gather.9.cloned.1.call-update) | async-done | bytes 1966096 | tf_op jit(solution)/shard_map/all_gather | solution.py:356
  102.6 1.5 collective-permute-start.2
  104.1 0.0 collective-permute-done.3.refs_1_.refs_9_.refs_17_
  104.1 0.5 collective-permute-start.7
  104.6 0.0 collective-permute-done.4.refs_2_.refs_10_.refs_18_
  104.6 1.5 collective-permute-start.8
  106.2 0.0 collective-permute-done.5.refs_3_.refs_11_.refs_19_
  106.2 0.5 collective-permute-start.9
  106.7 0.1 stack.96.places_ref
  106.8 0.1 stack.87.places_ref
  106.9 47.3 %all-gather.7.cloned.1.call-done = bf16[384,2560]{1,0:T(8,128)(2,1)} async-done(((bf16[96,2560]{1,0:T(8,128)(2,1)}), bf16[384,2560]{1,0:T(8,128)(2,1)}) %all-gather.7.cloned.1.call-update) | async-done | bytes 1966096 | tf_op jit(solution)/shard_map/all_gather | solution.py:356
  154.1 1.5 collective-permute-start.1
  155.7 20.2 %all-gather = bf16[384,1280]{1,0:T(8,128)(2,1)S(1)} all-gather(bf16[96,1280]{1,0:T(8,128)(2,1)S(1)} %pack.4), channel_id=2, replica_groups={{0,2,4,6},{1,3,5,7},{8,10,12,14},{9,11,13,15},{16,18,20,22},{17,19,21,2..., dimensions={0}, use_global_device_ids=true | all-gather | bytes 1228800 | tf_op jit(solution)/shard_map/all_gather | solution.py:356
  175.9 20.6 %all-gather.1 = bf16[384,1280]{1,0:T(8,128)(2,1)S(1)} all-gather(bf16[96,1280]{1,0:T(8,128)(2,1)S(1)} %collective-permute-done), channel_id=3, replica_groups={{0,2,4,6},{1,3,5,7},{8,10,12,14},{9,11,13,15},{16,18,20,22},{17,19,21,2..., dimensions={0}, use_global_device_ids=true | all-gather | bytes 1228800 | tf_op jit(solution)/shard_map/all_gather | solution.py:356
  196.5 5.8 %collective-permute-done.9.refs_7_.refs_15_.refs_23_ = bf16[96,4352]{1,0:T(8,128)(2,1)} collective-permute-done((bf16[96,4352]{1,0:T(8,128)(2,1)}, bf16[96,4352]{1,0:T(8,128)(2,1)}, u32[]{:S(2)}, u32[]{:S(2)}) %collective-permute-start.9) | collective-permute-done | bytes 835616 | tf_op jit(solution)/shard_map/ppermute | solution.py:353
  202.3 15.2 %compose.4 = (bf16[8,768,768]{2,1,0:T(8,128)(2,1)S(1)}, f32[8,96,768]{2,1,0:T(8,128)S(1)}, bf16[8,96,768]{2,1,0:T(8,128)(2,1)S(1)}, bf16[768,768]{1,0:T(8,128)(2,1)S(1)}, bf16[768,768]{1,0:T(8,128)(2,1)S(1)}) custom-call(s32[1]{0:T(128)} %bitcast.last_ref, s32[9]{0:T(128)S(1)} %stack.96.places_ref, bf16[96,4352]{1,0:T(8,128)(2,1)S(1)} %pack.7.refs_0_.refs_8_.refs_16_, ...), custom_call_target="tpu_custom_call" | custom-call | flops 8153726976 | bytes 14155776 | tf_op jit(solution)/shard_map/compose/pallas_call | solution.py:180
  217.6 10.1 %compose.5 = (bf16[8,768,768]{2,1,0:T(8,128)(2,1)S(1)}, f32[8,96,768]{2,1,0:T(8,128)S(1)}, bf16[8,96,768]{2,1,0:T(8,128)(2,1)S(1)}, bf16[768,768]{1,0:T(8,128)(2,1)S(1)}, bf16[768,768]{1,0:T(8,128)(2,1)S(1)}) custom-call(s32[1]{0:T(128)} %bitcast.last_ref, s32[9]{0:T(128)S(1)} %stack.87.places_ref, ...), custom_call_target="tpu_custom_call", output_to_operand_aliasing={{0}: (6, {}), {1}: (7, {}), {2}: (8, {})} | custom-call | flops 5435817984 | bytes 9437184 | tf_op jit(solution)/shard_map/compose/pallas_call | solution.py:180
  227.7 15.7 %collective-permute-done.1.refs_1_ = bf16[4,96,2560]{2,1,0:T(8,128)(2,1)S(1)} collective-permute-done((bf16[4,96,2560]{2,1,0:T(8,128)(2,1)}, bf16[4,96,2560]{2,1,0:T(8,128)(2,1)S(1)}, u32[]{:S(2)}, u32[]{:S(2)}) %collective-permute-start.1) | collective-permute-done | bytes 1966112 | tf_op jit(solution)/shard_map/ppermute | solution.py:353
  243.5 10.4 %compose.6 = (bf16[8,768,768]{2,1,0:T(8,128)(2,1)S(1)}, f32[8,96,768]{2,1,0:T(8,128)S(1)}, bf16[8,96,768]{2,1,0:T(8,128)(2,1)S(1)}, bf16[768,768]{1,0:T(8,128)(2,1)S(1)}, bf16[768,768]{1,0:T(8,128)(2,1)S(1)}) custom-call(s32[1]{0:T(128)} %bitcast.last_ref, s32[9]{0:T(128)S(1)} %stack.87.places_ref, ...), custom_call_target="tpu_custom_call", output_to_operand_aliasing={{0}: (6, {}), {1}: (7, {}), {2}: (8, {})} | custom-call | flops 5435817984 | bytes 9437184 | tf_op jit(solution)/shard_map/compose/pallas_call | solution.py:180
  253.8 5.0 %compose.7 = (bf16[8,768,768]{2,1,0:T(8,128)(2,1)S(1)}, f32[8,96,768]{2,1,0:T(8,128)S(1)}, bf16[8,96,768]{2,1,0:T(8,128)(2,1)S(1)}, bf16[768,768]{1,0:T(8,128)(2,1)S(1)}, bf16[768,768]{1,0:T(8,128)(2,1)S(1)}) custom-call(s32[1]{0:T(128)} %bitcast.last_ref, s32[9]{0:T(128)S(1)} %stack.87.places_ref, ...), custom_call_target="tpu_custom_call", output_to_operand_aliasing={{0}: (6, {}), {1}: (7, {}), {2}: (8, {})} | custom-call | flops 2717908992 | bytes 4718592 | tf_op jit(solution)/shard_map/compose/pallas_call | solution.py:180
  258.8 0.3 fold.1
  259.2 0.7 collective-permute-start.10
  259.9 1.8 hop.2
  261.7 0.7 collective-permute-start.11
  262.4 1.8 hop.3
  264.2 1.3 collective-permute-start.12
  265.5 17.0 %collective-permute-done.12.refs_2_ = bf16[6,256,256]{2,1,0:T(8,128)(2,1)S(1)} collective-permute-done((bf16[6,256,256]{2,1,0:T(8,128)(2,1)S(1)}, bf16[6,256,256]{2,1,0:T(8,128)(2,1)S(1)}, u32[]{:S(2)}, u32[]{:S(2)}) %collective-permute-start.12) | collective-permute-done | bytes 786464 | tf_op jit(solution)/shard_map/ppermute | solution.py:382
  282.6 6.7 %finish.1 = f32[8,96,768]{2,1,0:T(8,128)} custom-call(bf16[8,768,768]{2,1,0:T(8,128)(2,1)S(1)} %get-tuple-element.40.factor_ref, f32[8,96,768]{2,1,0:T(8,128)S(1)} %get-tuple-element.41.own_ref, bf16[8,96,768]{2,1,0:T(8,128)(2,1)S(1)} %get-tuple-element.42.mine_ref, bf16[6,256,256]{2,1,0:T(8,128)(2,1)S(1)} %collective-permute-done.10.refs_0_, ...), custom_call_target="tpu_custom_call" | custom-call | tf_op jit(solution)/shard_map/finish/pallas_call | solution.py:309
  (14 shorter events, 0.1 us)
Async XLA Ops:
  6.5 1.6 copy-start.3
  6.5 96.1 %all-gather.9.cloned.1.call-start = ((), (), s32[]{:S(2)}) async-start(), calls=%async_computation.1 | async-start | bytes 2457600 | tf_op jit(solution)/shard_map/all_gather | solution.py:356
  9.3 144.9 %all-gather.7.cloned.1.call-start = ((), (), s32[]{:S(2)}) async-start(), calls=%async_computation | async-start | bytes 2457600 | tf_op jit(solution)/shard_map/all_gather | solution.py:356
  9.3 3.4 %copy-start = (f32[96,768]{1,0:T(8,128)S(1)}, f32[96,768]{1,0:T(8,128)}, u32[]{:S(2)}) copy-start(f32[96,768]{1,0:T(8,128)} %refs_0_.1) | copy-start | bytes 884740
  13.1 91.0 %collective-permute-start.3 = (bf16[96,4352]{1,0:T(8,128)(2,1)S(1)}, bf16[96,4352]{1,0:T(8,128)(2,1)}, u32[]{:S(2)}, u32[]{:S(2)}) collective-permute-start(bf16[96,4352]{1,0:T(8,128)(2,1)S(1)} %pack.7.refs_0_.refs_8_.refs_16_), channel_id=1, source_target_pairs={{0,2},{1,3},{2,4},{3,5},{4,6},{5,7},{6,0},{7,1},{8,10},{9,11},{10,... | collective-permute-start | bytes 2506760 | tf_op jit(solution)/shard_map/ppermute | solution.py:353
  16.2 88.5 %collective-permute-start.4 = (bf16[96,4352]{1,0:T(8,128)(2,1)S(1)}, bf16[96,4352]{1,0:T(8,128)(2,1)}, u32[]{:S(2)}, u32[]{:S(2)}) collective-permute-start(bf16[96,4352]{1,0:T(8,128)(2,1)S(1)} %pack.7.refs_0_.refs_8_.refs_16_), channel_id=1, source_target_pairs={{0,4},{1,5},{2,6},{3,7},{4,0},{5,1},{6,2},{7,3},{8,12},{9,13},{10,... | collective-permute-start | bytes 2506760 | tf_op jit(solution)/shard_map/ppermute | solution.py:353
  18.8 87.4 %collective-permute-start.5 = (bf16[96,4352]{1,0:T(8,128)(2,1)S(1)}, bf16[96,4352]{1,0:T(8,128)(2,1)}, u32[]{:S(2)}, u32[]{:S(2)}) collective-permute-start(bf16[96,4352]{1,0:T(8,128)(2,1)S(1)} %pack.7.refs_0_.refs_8_.refs_16_), channel_id=1, source_target_pairs={{0,6},{1,7},{2,0},{3,1},{4,2},{5,3},{6,4},{7,5},{8,14},{9,15},{10,... | collective-permute-start | bytes 2506760 | tf_op jit(solution)/shard_map/ppermute | solution.py:353
  20.1 86.7 %collective-permute-start.6 = (bf16[96,4352]{1,0:T(8,128)(2,1)S(1)}, bf16[96,4352]{1,0:T(8,128)(2,1)}, u32[]{:S(2)}, u32[]{:S(2)}) collective-permute-start(bf16[96,4352]{1,0:T(8,128)(2,1)S(1)} %pack.7.refs_0_.refs_8_.refs_16_), channel_id=1, source_target_pairs={{0,1},{1,0},{2,3},{3,2},{4,5},{5,4},{6,7},{7,6},{8,9},{9,8},{10,11... | collective-permute-start | bytes 2506760 | tf_op jit(solution)/shard_map/ppermute | solution.py:353
  23.7 21.1 %collective-permute-start = (bf16[96,1280]{1,0:T(8,128)(2,1)S(1)}, bf16[96,1280]{1,0:T(8,128)(2,1)S(1)}, u32[]{:S(2)}, u32[]{:S(2)}) collective-permute-start(bf16[96,1280]{1,0:T(8,128)(2,1)S(1)} %pack.4), channel_id=1, source_target_pairs={{0,1},{1,0},{2,3},{3,2},{4,5},{5,4},{6,7},{7,6},{8,9},{9,8},{10,11... | collective-permute-start | bytes 737288 | tf_op jit(solution)/shard_map/ppermute | solution.py:353
  102.6 114.9 %collective-permute-start.2 = (bf16[4,96,2560]{2,1,0:T(8,128)(2,1)}, bf16[4,96,2560]{2,1,0:T(8,128)(2,1)S(1)}, u32[]{:S(2)}, u32[]{:S(2)}) collective-permute-start(bf16[4,96,2560]{2,1,0:T(8,128)(2,1)} %bitcast.26), channel_id=1, source_target_pairs={{0,1},{1,0},{2,3},{3,2},{4,5},{5,4},{6,7},{7,6},{8,9},{9,8},{10,11... | collective-permute-start | bytes 5898248 | tf_op jit(solution)/shard_map/ppermute | solution.py:353
  104.1 92.3 %collective-permute-start.7 = (bf16[96,4352]{1,0:T(8,128)(2,1)}, bf16[96,4352]{1,0:T(8,128)(2,1)}, u32[]{:S(2)}, u32[]{:S(2)}) collective-permute-start(bf16[96,4352]{1,0:T(8,128)(2,1)} %collective-permute-done.3.refs_1_.refs_9_.refs_17_), channel_id=1, source_target_pairs={{0,1},{1,0},{2,3},{3,2},{4,5},{5,4},{6,7},{7,6},{8,9},{9,8},{10,11... | collective-permute-start | bytes 2506760 | tf_op jit(solution)/shard_map/ppermute | solution.py:353
  104.6 91.8 %collective-permute-start.8 = (bf16[96,4352]{1,0:T(8,128)(2,1)}, bf16[96,4352]{1,0:T(8,128)(2,1)}, u32[]{:S(2)}, u32[]{:S(2)}) collective-permute-start(bf16[96,4352]{1,0:T(8,128)(2,1)} %collective-permute-done.4.refs_2_.refs_10_.refs_18_), channel_id=1, source_target_pairs={{0,1},{1,0},{2,3},{3,2},{4,5},{5,4},{6,7},{7,6},{8,9},{9,8},{10,11... | collective-permute-start | bytes 2506760 | tf_op jit(solution)/shard_map/ppermute | solution.py:353
  106.2 96.2 %collective-permute-start.9 = (bf16[96,4352]{1,0:T(8,128)(2,1)}, bf16[96,4352]{1,0:T(8,128)(2,1)}, u32[]{:S(2)}, u32[]{:S(2)}) collective-permute-start(bf16[96,4352]{1,0:T(8,128)(2,1)} %collective-permute-done.5.refs_3_.refs_11_.refs_19_), channel_id=1, source_target_pairs={{0,1},{1,0},{2,3},{3,2},{4,5},{5,4},{6,7},{7,6},{8,9},{9,8},{10,11... | collective-permute-start | bytes 2506760 | tf_op jit(solution)/shard_map/ppermute | solution.py:353
  154.1 89.3 %collective-permute-start.1 = (bf16[4,96,2560]{2,1,0:T(8,128)(2,1)}, bf16[4,96,2560]{2,1,0:T(8,128)(2,1)S(1)}, u32[]{:S(2)}, u32[]{:S(2)}) collective-permute-start(bf16[4,96,2560]{2,1,0:T(8,128)(2,1)} %bitcast.24), channel_id=1, source_target_pairs={{0,1},{1,0},{2,3},{3,2},{4,5},{5,4},{6,7},{7,6},{8,9},{9,8},{10,11... | collective-permute-start | bytes 5898248 | tf_op jit(solution)/shard_map/ppermute | solution.py:353
  202.3 15.2 %copy-start.2 = (bf16[384,2560]{1,0:T(8,128)(2,1)S(1)}, bf16[384,2560]{1,0:T(8,128)(2,1)}, u32[]{:S(2)}) copy-start(bf16[384,2560]{1,0:T(8,128)(2,1)} %all-gather.9.cloned.1.call-done) | copy-start | bytes 5898244
  217.6 25.9 %copy-start.1 = (bf16[384,2560]{1,0:T(8,128)(2,1)S(1)}, bf16[384,2560]{1,0:T(8,128)(2,1)}, u32[]{:S(2)}) copy-start(bf16[384,2560]{1,0:T(8,128)(2,1)} %all-gather.7.cloned.1.call-done) | copy-start | bytes 5898244
  259.2 0.7 collective-permute-start.10
  261.7 0.7 collective-permute-start.11
  264.2 18.3 %collective-permute-start.12 = (bf16[6,256,256]{2,1,0:T(8,128)(2,1)S(1)}, bf16[6,256,256]{2,1,0:T(8,128)(2,1)S(1)}, u32[]{:S(2)}, u32[]{:S(2)}) collective-permute-start(bf16[6,256,256]{2,1,0:T(8,128)(2,1)S(1)} %hop.3), channel_id=1, source_target_pairs={{8,0},{9,1},{10,2},{11,3},{12,4},{13,5},{14,6},{15,7}} | collective-permute-start | bytes 2359304 | tf_op jit(solution)/shard_map/ppermute | solution.py:382
Sparse Core Ops, SparseCore 0:
  9.4 93.1 all-gather.8
  104.2 49.9 all-gather.6

commit v5 on v4

--- a/solution.py
+++ b/solution.py
@@ -42,31 +42,32 @@
     return pltpu.roll(wide, start, 1)
 
 
-def pack_kernel(count, low, high, place_ref, gain_ref, increment_ref, *refs):
-    packed_ref = refs[-1]
-    width = gain_ref.shape[2]
-    stride = width + half_width(gain_ref.shape[1], count)[1]
-    for step in range(high - low):
+def pack_kernel(count, ranges, place_ref, gain_ref, increment_ref, terminal_ref, whole_ref, *piece_refs):
+    steps, rows, width = gain_ref.shape
+    stride = width + half_width(rows, count)[1]
+    place = place_ref[0]
+    for step in range(steps):
         base = step * stride
-        packed_ref[:, base:base + width] = gain_ref[step]
-        packed_ref[:, base + width:base + stride] = packed_half(increment_ref[step], place_ref[0], count)
-    if len(refs) > 1:
-        packed_ref[:, (high - low) * stride:] = packed_half(refs[0][...], place_ref[0], count)
-
-
-def pack(place, gains, increments, terminal, count, low, high):
-    rows, width = gains.shape[1:]
+        whole_ref[:, base:base + width] = gain_ref[step]
+        whole_ref[:, base + width:base + stride] = packed_half(increment_ref[step], place, count)
+    whole_ref[:, steps * stride:] = packed_half(terminal_ref[...], place, count)
+    for (low, high), piece_ref in zip(ranges, piece_refs):
+        piece_ref[...] = whole_ref[:, low * stride:low * stride + piece_ref.shape[1]]
+
+
+def pack(place, gains, increments, terminal, count, ranges):
+    steps, rows, width = gains.shape
     half = half_width(rows, count)[1]
-    ends = [] if terminal is None else [terminal]
-    lanes = (high - low) * (width + half) + half * len(ends)
+    lanes = [(high - low) * (width + half) + half * (high == steps) for low, high in [(0, steps)] + ranges]
+    vmem = pl.BlockSpec(memory_space=pltpu.VMEM)
     return pl.pallas_call(
-        functools.partial(pack_kernel, count, low, high),
-        in_specs=[pl.BlockSpec(memory_space=pltpu.SMEM)] + [pl.BlockSpec(memory_space=pltpu.VMEM)] * (2 + len(ends)),
-        out_specs=pl.BlockSpec(memory_space=pltpu.VMEM),
-        out_shape=jax.ShapeDtypeStruct((rows, lanes), BF16),
+        functools.partial(pack_kernel, count, ranges),
+        in_specs=[pl.BlockSpec(memory_space=pltpu.SMEM), vmem, vmem, vmem],
+        out_specs=[vmem] * len(lanes),
+        out_shape=[jax.ShapeDtypeStruct((rows, size), BF16) for size in lanes],
         compiler_params=pltpu.CompilerParams(vmem_limit_bytes=24 * MIB),
         name="pack",
-    )(place, gains[low:high], increments[low:high], *ends)
+    )(place, gains, increments, terminal)
 
 
 def compose_kernel(lines, parts, first, last_ref, places_ref, *refs):
@@ -152,8 +153,8 @@
 def compose(last, places, blocks, state, low, turns, steps):
     lines = [len(group) for group in blocks]
     flat = [block for group in blocks for block in group]
-    rows = flat[0].shape[-2]
-    width = rows * sum(block.shape[0] if block.ndim == 3 else 1 for block in flat)
+    rows = flat[0][0].shape[-2]
+    width = rows * sum(block.shape[0] if block.ndim == 3 else 1 for block, _ in flat)
     half = half_width(rows, width // rows)[1]
     stride = width + half
     first = state is None
@@ -165,15 +166,16 @@
             return pl.BlockSpec((block.shape[0], rows, size), lambda i, *p: (0, 0, place(i)))
         return pl.BlockSpec((rows, size), lambda i, *p: (0, place(i)))
 
-    in_specs = [spec(block, stride, lambda i: turns - 1 - i) for block in flat]
-    args = list(flat)
-    parts = half // math.gcd(turns * stride, half)
-    if first:
-        for n in range(parts):
-            at = turns * stride * parts // half + n
-            in_specs += [spec(block, half // parts, lambda i, at=at: at) for block in flat]
-            args += flat
-    else:
+    in_specs = [spec(block, stride, lambda i, begin=begin: low + turns - 1 - i - begin) for block, begin in flat]
+    args = [block for block, _ in flat]
+    size = math.gcd(stride, half)
+    parts = half // size if first else 0
+    for n in range(parts):
+        in_specs += [
+            spec(block, size, lambda i, at=(steps - begin) * stride // size + n: at) for block, begin in flat
+        ]
+        args += [block for block, _ in flat]
+    if not first:
         in_specs += [whole, whole, anywhere, anywhere, anywhere]
         args += [state[3], state[4], state[0], state[1], state[2]]
     base = 2 + len(flat) + 2
@@ -325,13 +327,8 @@
 
 def pieces(steps):
     small = max(steps // 8, 1)
-    low = steps - 3 * small
-    return [
-        (low, steps, "shifts"),
-        (low - 2 * small, low, "lines"),
-        (low - 4 * small, low - 2 * small, "lines"),
-        (0, low - 4 * small, "across"),
-    ]
+    cuts = [0, small, 2 * small, 4 * small, 6 * small, steps]
+    return list(zip(cuts, cuts[1:]))[::-1]
 
 
 def local(gains, increments, terminal):
@@ -342,7 +339,6 @@
     steps = gains.shape[0]
     place = lax.axis_index("tile").astype(jnp.int32)
     last = (lax.axis_index("tm") == blocks - 1).astype(jnp.int32).reshape(1)
-    lines = [[a * across + b for a in range(line)] for b in range(across)]
 
     def shifted(array, along, over):
         pairs = [
@@ -352,30 +348,38 @@
         ]
         return lax.ppermute(array, "tile", pairs) if along or over else array
 
-    def gathered(array):
-        return lax.all_gather(array, "tile", axis_index_groups=lines)
-
-    def spread(array, kind):
-        if kind == "shifts":
-            along = [shifted(array, i, 0) for i in range(line)]
-            return [[shifted(part, 0, j) for part in along] for j in range(across)]
-        if kind == "lines":
-            whole = gathered(array)
-            return [[shifted(whole, 0, j)] for j in range(across)]
-        return [[gathered(shifted(array, 0, j))] for j in range(across)]
-
-    def order(kind):
-        found = [place]
-        for j in range(across):
-            for i in range(line):
-                along = (place // across - i + line) % line if kind == "shifts" else i
-                found.append(along * across + (place % across - j + across) % across)
-        return jnp.stack(found)
-
+    places = jnp.stack(
+        [place]
+        + [
+            (place // across - i + line) % line * across + (place % across - j + across) % across
+            for j in range(across)
+            for i in range(line)
+        ]
+    )
+    ranges = pieces(steps)
+    whole, *own = pack(place.reshape(1), gains, increments, terminal, count, ranges)
+    passing = [shifted(whole, 0, j) for j in range(1, across)]
+    crossed = [whole] + passing
     state = None
-    for low, high, kind in pieces(steps):
-        own = pack(place.reshape(1), gains, increments, terminal if state is None else None, count, low, high)
-        state = compose(last, order(kind), spread(own, kind), state, low, high - low, steps)
+    stages = []
+    for (low, high), array in zip(ranges, own):
+        if stages:
+            array, passing, parts = lax.optimization_barrier((array, passing, parts))
+            if len(stages) == 1:
+                crossed = [whole] + passing
+            else:
+                stages[-2][3][1:] = passing
+            stages[-1][3][0] = jnp.stack(parts)
+            passing = [shifted(stages[-1][3][0], 0, j) for j in range(1, across)]
+        parts = [shifted(array, i, 0) for i in range(1, line)]
+        stages.append((low, high, array, [None] * across))
+    last_parts, passing = lax.optimization_barrier((parts, passing))
+    stages[-2][3][1:] = passing
+    stacked = jnp.stack(last_parts)
+    stages[-1][3][:] = [shifted(stacked, 0, j) for j in range(across)]
+    for low, high, _, stacks in stages:
+        groups = [[(crossed[j], 0), (stacks[j], low)] for j in range(across)]
+        state = compose(last, places, groups, state, low, high - low, steps)
     factors, own, mine, factor, half = state
     packed = []
     for turn in range(blocks - 1, 0, -1):

time: 298 us -> 285 us (0.956)
  starting transfers between devices: 17.5 us -> 73.8 us
  blocking collectives: 40.8 us -> 0 us
  waiting for transfers between devices: 164 us -> 135 us
  between operations: 13.6 us -> 0.16 us
  local copies, waits for them, and re-layouts: 6.02 us -> 12.8 us
  Pallas kernels: 54 us -> 57.4 us
    all_gather x2 -> x0, waiting for transfers between devices: 105 us -> none  [gathered(): return lax.all_gather(array, 'tile', axis_index_groups=lines)]
    ppermute x10 -> x21, waiting for transfers between devices: 42.2 us -> 118 us  [shifted(): return lax.ppermute(array, 'tile', pairs) if along or over else array]
    ppermute x10 -> x21, starting transfers between devices: 14.7 us -> 71 us  [shifted(): return lax.ppermute(array, 'tile', pairs) if along or over else array]
    all_gather x2 -> x0, blocking collectives: 40.8 us -> none  [gathered(): return lax.all_gather(array, 'tile', axis_index_groups=lines)]
    unnamed x8 -> x32, local copies, waits for them, and re-layouts: 0.22 us -> 12.8 us
    slice x6 -> x0, local copies, waits for them, and re-layouts: 5.63 us -> none  [the longest x3 3.62 us: pack(): increments[low:high]]
    pallas_call x4 -> x5, Pallas kernels: 40.7 us -> 45.1 us  [compose(): pl.pallas_call(functools.partial(compose_kernel, lines, parts, first), gr...]
  transfers between devices with their start and end apart: 15 -> 24, of which waited for: 6 -> 13; matrix products, arithmetic and copies ran while one was open for 1% -> 0% of each run, Pallas kernels for 9% -> 14%
where the time goes in v5:
time: 285 us; the launch traced here: 281 us
  waiting for transfers between devices  135 us (47%)
  starting transfers between devices  73.8 us (26%)
  Pallas kernels  57.4 us (20%)
  local copies, waits for them, and re-layouts  12.8 us (4%)
    ppermute x21, waiting for transfers between devices, shifted(): return lax.ppermute(array, 'tile', pairs) if along or over else array  118 us
    ppermute x21, starting transfers between devices, shifted(): return lax.ppermute(array, 'tile', pairs) if along or over else array  71 us
    pallas_call x5, Pallas kernels, compose(): pl.pallas_call(functools.partial(compose_kernel, lines, parts, first), gr...  45.1 us
    ppermute x3, waiting for transfers between devices, local(): lax.ppermute(hop(factor, half, packed), 'tm', [(turn, turn - 1)])  17.2 us
    unnamed x32, local copies, waits for them, and re-layouts  12.8 us
    pallas_call x1, Pallas kernels, finish(): pl.pallas_call(functools.partial(finish_kernel, len(packed)), grid=(steps...  6.75 us
  transfers between devices with their start and end apart: 24, of which 13 were waited for; matrix products, arithmetic and copies ran while one was open for 0% of the time, Pallas kernels for 14%

profile of v5, /device:TPU:0, one launch (start us, length us, event | category | flops | bytes accessed | tf_op | source)
XLA Modules:
  0.0 281.2 jit_solution(16634156991283513904)
XLA Ops:
  0.0 1.7 copy-done.9
  1.7 1.3 copy-done.12
  2.9 1.0 copy-done.13
  3.9 1.6 pack.1
  6.2 3.0 %collective-permute-start = (bf16[96,10752]{1,0:T(8,128)(2,1)S(1)}, bf16[96,10752]{1,0:T(8,128)(2,1)S(1)}, u32[]{:S(2)}, u32[]{:S(2)}) collective-permute-start(bf16[96,10752]{1,0:T(8,128)(2,1)S(1)} %get-tuple-element.60.refs_0_.refs_4_.refs_8_), channel_id=1, source_target_pairs={{0,1},{1,0},{2,3},{3,2},{4,5},{5,4},{6,7},{7,6},{8,9},{9,8},{10,11... | collective-permute-start | bytes 6193160 | tf_op jit(solution)/shard_map/ppermute | solution.py:349
  9.2 1.6 collective-permute-start.1
  10.8 2.6 collective-permute-start.2
  13.3 1.3 collective-permute-start.3
  14.7 12.7 %collective-permute-done.1 = bf16[96,3072]{1,0:T(8,128)(2,1)S(1)} collective-permute-done((bf16[96,3072]{1,0:T(8,128)(2,1)S(1)}, bf16[96,3072]{1,0:T(8,128)(2,1)S(1)}, u32[]{:S(2)}, u32[]{:S(2)}) %collective-permute-start.1) | collective-permute-done | bytes 589856 | tf_op jit(solution)/shard_map/ppermute | solution.py:349
  27.4 23.9 %collective-permute-done.2 = bf16[96,3072]{1,0:T(8,128)(2,1)S(1)} collective-permute-done((bf16[96,3072]{1,0:T(8,128)(2,1)S(1)}, bf16[96,3072]{1,0:T(8,128)(2,1)S(1)}, u32[]{:S(2)}, u32[]{:S(2)}) %collective-permute-start.2) | collective-permute-done | bytes 589856 | tf_op jit(solution)/shard_map/ppermute | solution.py:349
  51.2 2.9 %collective-permute-done.refs_2_.refs_6_.refs_10_ = bf16[96,10752]{1,0:T(8,128)(2,1)S(1)} collective-permute-done((bf16[96,10752]{1,0:T(8,128)(2,1)S(1)}, bf16[96,10752]{1,0:T(8,128)(2,1)S(1)}, u32[]{:S(2)}, u32[]{:S(2)}) %collective-permute-start) | collective-permute-done | bytes 2064416 | tf_op jit(solution)/shard_map/ppermute | solution.py:349
  54.1 1.3 copy-done.1
  55.6 1.8 collective-permute-start.4
  57.4 9.0 %collective-permute-start.5 = (bf16[96,2560]{1,0:T(8,128)(2,1)S(1)}, bf16[96,2560]{1,0:T(8,128)(2,1)S(1)}, u32[]{:S(2)}, u32[]{:S(2)}) collective-permute-start(bf16[96,2560]{1,0:T(8,128)(2,1)S(1)} %get-tuple-element.69), channel_id=1, source_target_pairs={{0,2},{1,3},{2,4},{3,5},{4,6},{5,7},{6,0},{7,1},{8,10},{9,11},{10,... | collective-permute-start | bytes 1474568 | tf_op jit(solution)/shard_map/ppermute | solution.py:349
  66.4 1.6 collective-permute-start.6
  68.8 10.9 %collective-permute-done.5 = bf16[96,2560]{1,0:T(8,128)(2,1)S(1)} collective-permute-done((bf16[96,2560]{1,0:T(8,128)(2,1)S(1)}, bf16[96,2560]{1,0:T(8,128)(2,1)S(1)}, u32[]{:S(2)}, u32[]{:S(2)}) %collective-permute-start.5) | collective-permute-done | bytes 491552 | tf_op jit(solution)/shard_map/ppermute | solution.py:349
  79.7 18.7 %collective-permute-done.6 = bf16[96,2560]{1,0:T(8,128)(2,1)S(1)} collective-permute-done((bf16[96,2560]{1,0:T(8,128)(2,1)S(1)}, bf16[96,2560]{1,0:T(8,128)(2,1)S(1)}, u32[]{:S(2)}, u32[]{:S(2)}) %collective-permute-start.6) | collective-permute-done | bytes 491552 | tf_op jit(solution)/shard_map/ppermute | solution.py:349
  98.4 1.2 copy-done.5
  99.8 1.6 collective-permute-start.8
  101.4 10.0 %collective-permute-start.10 = (bf16[96,2560]{1,0:T(8,128)(2,1)S(1)}, bf16[96,2560]{1,0:T(8,128)(2,1)S(1)}, u32[]{:S(2)}, u32[]{:S(2)}) collective-permute-start(bf16[96,2560]{1,0:T(8,128)(2,1)S(1)} %get-tuple-element.73), channel_id=1, source_target_pairs={{0,4},{1,5},{2,6},{3,7},{4,0},{5,1},{6,2},{7,3},{8,12},{9,13},{10,... | collective-permute-start | bytes 1474568 | tf_op jit(solution)/shard_map/ppermute | solution.py:349
  111.4 3.4 %collective-permute-start.11 = (bf16[96,2560]{1,0:T(8,128)(2,1)S(1)}, bf16[96,2560]{1,0:T(8,128)(2,1)S(1)}, u32[]{:S(2)}, u32[]{:S(2)}) collective-permute-start(bf16[96,2560]{1,0:T(8,128)(2,1)S(1)} %get-tuple-element.73), channel_id=1, source_target_pairs={{0,6},{1,7},{2,0},{3,1},{4,2},{5,3},{6,4},{7,5},{8,14},{9,15},{10,... | collective-permute-start | bytes 1474568 | tf_op jit(solution)/shard_map/ppermute | solution.py:349
  115.1 18.9 %collective-permute-done.10 = bf16[96,2560]{1,0:T(8,128)(2,1)S(1)} collective-permute-done((bf16[96,2560]{1,0:T(8,128)(2,1)S(1)}, bf16[96,2560]{1,0:T(8,128)(2,1)S(1)}, u32[]{:S(2)}, u32[]{:S(2)}) %collective-permute-start.10) | collective-permute-done | bytes 491552 | tf_op jit(solution)/shard_map/ppermute | solution.py:349
  134.0 12.8 %collective-permute-done.9 = bf16[96,2560]{1,0:T(8,128)(2,1)S(1)} collective-permute-done((bf16[96,2560]{1,0:T(8,128)(2,1)S(1)}, bf16[96,2560]{1,0:T(8,128)(2,1)S(1)}, u32[]{:S(2)}, u32[]{:S(2)}) %collective-permute-start.9) | collective-permute-done | bytes 491552 | tf_op jit(solution)/shard_map/ppermute | solution.py:349
  146.8 1.1 copy-done.10
  148.7 13.1 %collective-permute-start.13 = (bf16[96,1280]{1,0:T(8,128)(2,1)}, bf16[96,1280]{1,0:T(8,128)(2,1)}, u32[]{:S(2)}, u32[]{:S(2)}) collective-permute-start(bf16[96,1280]{1,0:T(8,128)(2,1)} %get-tuple-element.77), channel_id=1, source_target_pairs={{0,2},{1,3},{2,4},{3,5},{4,6},{5,7},{6,0},{7,1},{8,10},{9,11},{10,... | collective-permute-start | bytes 737288 | tf_op jit(solution)/shard_map/ppermute | solution.py:349
  161.8 2.4 collective-permute-start.15
  164.2 4.3 %collective-permute-done.13 = bf16[96,1280]{1,0:T(8,128)(2,1)} collective-permute-done((bf16[96,1280]{1,0:T(8,128)(2,1)}, bf16[96,1280]{1,0:T(8,128)(2,1)}, u32[]{:S(2)}, u32[]{:S(2)}) %collective-permute-start.13) | collective-permute-done | bytes 245792 | tf_op jit(solution)/shard_map/ppermute | solution.py:349
  168.5 6.0 %collective-permute-done.14 = bf16[96,1280]{1,0:T(8,128)(2,1)} collective-permute-done((bf16[96,1280]{1,0:T(8,128)(2,1)}, bf16[96,1280]{1,0:T(8,128)(2,1)}, u32[]{:S(2)}, u32[]{:S(2)}) %collective-permute-start.14) | collective-permute-done | bytes 245792 | tf_op jit(solution)/shard_map/ppermute | solution.py:349
  174.6 2.4 collective-permute-done.15
  177.0 4.3 %collective-permute-done.12.refs_3_ = bf16[3,96,2560]{2,1,0:T(8,128)(2,1)} collective-permute-done((bf16[3,96,2560]{2,1,0:T(8,128)(2,1)S(1)}, bf16[3,96,2560]{2,1,0:T(8,128)(2,1)}, u32[]{:S(2)}, u32[]{:S(2)}) %collective-permute-start.12) | collective-permute-done | bytes 1474592 | tf_op jit(solution)/shard_map/ppermute | solution.py:349
  181.3 1.3 pad_maximum_fusion.3.refs_1_
  183.1 1.6 copy-done.2
  184.7 1.5 copy-done.4
  186.2 1.5 copy-done.6
  187.7 10.8 %compose.5 = (bf16[8,768,768]{2,1,0:T(8,128)(2,1)}, f32[8,96,768]{2,1,0:T(8,128)S(1)}, bf16[8,96,768]{2,1,0:T(8,128)(2,1)S(1)}, bf16[768,768]{1,0:T(8,128)(2,1)S(1)}, bf16[768,768]{1,0:T(8,128)(2,1)S(1)}) custom-call(s32[1]{0:T(128)} %bitcast.last_ref, s32[9]{0:T(128)S(1)} %stack.99.places_ref, ...), custom_call_target="tpu_custom_call" | custom-call | flops 5435817984 | bytes 9437184 | tf_op jit(solution)/shard_map/compose/pallas_call | solution.py:182
  198.4 13.5 %collective-permute-start.16 = (bf16[96,1280]{1,0:T(8,128)(2,1)S(1)}, bf16[96,1280]{1,0:T(8,128)(2,1)S(1)}, u32[]{:S(2)}, u32[]{:S(2)}) collective-permute-start(bf16[96,1280]{1,0:T(8,128)(2,1)S(1)} %copy-done.15), channel_id=1, source_target_pairs={{0,2},{1,3},{2,4},{3,5},{4,6},{5,7},{6,0},{7,1},{8,10},{9,11},{10,... | collective-permute-start | bytes 737288 | tf_op jit(solution)/shard_map/ppermute | solution.py:349
  211.9 2.4 collective-permute-start.18
  214.3 11.4 %compose.6 = (bf16[8,768,768]{2,1,0:T(8,128)(2,1)}, f32[8,96,768]{2,1,0:T(8,128)S(1)}, bf16[8,96,768]{2,1,0:T(8,128)(2,1)S(1)}, bf16[768,768]{1,0:T(8,128)(2,1)S(1)}, bf16[768,768]{1,0:T(8,128)(2,1)S(1)}) custom-call(s32[1]{0:T(128)} %bitcast.last_ref, s32[9]{0:T(128)S(1)} %stack.99.places_ref, ...), custom_call_target="tpu_custom_call", output_to_operand_aliasing={{0}: (8, {}), {1}: (9, {}), {2}: (10, {})} | custom-call | flops 5435817984 | bytes 9437184 | tf_op jit(solution)/shard_map/compose/pallas_call | solution.py:182
  225.9 1.6 collective-permute-start.20
  227.5 12.1 %compose.7 = (bf16[8,768,768]{2,1,0:T(8,128)(2,1)}, f32[8,96,768]{2,1,0:T(8,128)S(1)}, bf16[8,96,768]{2,1,0:T(8,128)(2,1)S(1)}, bf16[768,768]{1,0:T(8,128)(2,1)S(1)}, bf16[768,768]{1,0:T(8,128)(2,1)S(1)}) custom-call(s32[1]{0:T(128)} %bitcast.last_ref, s32[9]{0:T(128)S(1)} %stack.99.places_ref, ...), custom_call_target="tpu_custom_call", output_to_operand_aliasing={{0}: (8, {}), {1}: (9, {}), {2}: (10, {})} | custom-call | flops 5435817984 | bytes 9437184 | tf_op jit(solution)/shard_map/compose/pallas_call | solution.py:182
  239.6 5.3 %compose.8 = (bf16[8,768,768]{2,1,0:T(8,128)(2,1)}, f32[8,96,768]{2,1,0:T(8,128)S(1)}, bf16[8,96,768]{2,1,0:T(8,128)(2,1)S(1)}, bf16[768,768]{1,0:T(8,128)(2,1)S(1)}, bf16[768,768]{1,0:T(8,128)(2,1)S(1)}) custom-call(s32[1]{0:T(128)} %bitcast.last_ref, s32[9]{0:T(128)S(1)} %stack.99.places_ref, ...), custom_call_target="tpu_custom_call", output_to_operand_aliasing={{0}: (8, {}), {1}: (9, {}), {2}: (10, {})} | custom-call | flops 2717908992 | bytes 4718592 | tf_op jit(solution)/shard_map/compose/pallas_call | solution.py:182
  244.9 5.5 %compose.9 = (bf16[8,768,768]{2,1,0:T(8,128)(2,1)}, f32[8,96,768]{2,1,0:T(8,128)S(1)}, bf16[8,96,768]{2,1,0:T(8,128)(2,1)S(1)}, bf16[768,768]{1,0:T(8,128)(2,1)S(1)}, bf16[768,768]{1,0:T(8,128)(2,1)S(1)}) custom-call(s32[1]{0:T(128)} %bitcast.last_ref, s32[9]{0:T(128)S(1)} %stack.99.places_ref, ...), custom_call_target="tpu_custom_call", output_to_operand_aliasing={{0}: (8, {}), {1}: (9, {}), {2}: (10, {})} | custom-call | flops 2717908992 | bytes 4718592 | tf_op jit(solution)/shard_map/compose/pallas_call | solution.py:182
  251.5 1.8 hop.2
  253.3 0.8 collective-permute-start.22
  254.2 1.8 hop.3
  256.0 1.3 collective-permute-start.23
  257.3 17.2 %collective-permute-done.23.refs_2_ = bf16[6,256,256]{2,1,0:T(8,128)(2,1)S(1)} collective-permute-done((bf16[6,256,256]{2,1,0:T(8,128)(2,1)S(1)}, bf16[6,256,256]{2,1,0:T(8,128)(2,1)S(1)}, u32[]{:S(2)}, u32[]{:S(2)}) %collective-permute-start.23) | collective-permute-done | bytes 786464 | tf_op jit(solution)/shard_map/ppermute | solution.py:386
  274.5 6.8 %finish.1 = f32[8,96,768]{2,1,0:T(8,128)} custom-call(bf16[8,768,768]{2,1,0:T(8,128)(2,1)S(1)} %copy-done, f32[8,96,768]{2,1,0:T(8,128)S(1)} %get-tuple-element.111.own_ref, bf16[8,96,768]{2,1,0:T(8,128)(2,1)S(1)} %get-tuple-element.112.mine_ref, bf16[6,256,256]{2,1,0:T(8,128)(2,1)S(1)} %collective-permute-done.21.refs_0_, ...), custom_call_target="tpu_custom_call" | custom-call | tf_op jit(solution)/shard_map/finish/pallas_call | solution.py:311
  (48 shorter events, 4.8 us)
Async XLA Ops:
  0.0 1.7 copy-start.9
  1.7 1.3 copy-start.12
  2.9 1.0 copy-start.13
  5.5 0.7 copy-start.14
  6.2 47.9 %collective-permute-start = (bf16[96,10752]{1,0:T(8,128)(2,1)S(1)}, bf16[96,10752]{1,0:T(8,128)(2,1)S(1)}, u32[]{:S(2)}, u32[]{:S(2)}) collective-permute-start(bf16[96,10752]{1,0:T(8,128)(2,1)S(1)} %get-tuple-element.60.refs_0_.refs_4_.refs_8_), channel_id=1, source_target_pairs={{0,1},{1,0},{2,3},{3,2},{4,5},{5,4},{6,7},{7,6},{8,9},{9,8},{10,11... | collective-permute-start | bytes 6193160 | tf_op jit(solution)/shard_map/ppermute | solution.py:349
  9.2 18.2 %collective-permute-start.1 = (bf16[96,3072]{1,0:T(8,128)(2,1)S(1)}, bf16[96,3072]{1,0:T(8,128)(2,1)S(1)}, u32[]{:S(2)}, u32[]{:S(2)}) collective-permute-start(bf16[96,3072]{1,0:T(8,128)(2,1)S(1)} %get-tuple-element.65), channel_id=1, source_target_pairs={{0,2},{1,3},{2,4},{3,5},{4,6},{5,7},{6,0},{7,1},{8,10},{9,11},{10,... | collective-permute-start | bytes 1769480 | tf_op jit(solution)/shard_map/ppermute | solution.py:349
  10.8 40.5 %collective-permute-start.2 = (bf16[96,3072]{1,0:T(8,128)(2,1)S(1)}, bf16[96,3072]{1,0:T(8,128)(2,1)S(1)}, u32[]{:S(2)}, u32[]{:S(2)}) collective-permute-start(bf16[96,3072]{1,0:T(8,128)(2,1)S(1)} %get-tuple-element.65), channel_id=1, source_target_pairs={{0,4},{1,5},{2,6},{3,7},{4,0},{5,1},{6,2},{7,3},{8,12},{9,13},{10,... | collective-permute-start | bytes 1769480 | tf_op jit(solution)/shard_map/ppermute | solution.py:349
  13.3 37.9 %collective-permute-start.3 = (bf16[96,3072]{1,0:T(8,128)(2,1)S(1)}, bf16[96,3072]{1,0:T(8,128)(2,1)S(1)}, u32[]{:S(2)}, u32[]{:S(2)}) collective-permute-start(bf16[96,3072]{1,0:T(8,128)(2,1)S(1)} %get-tuple-element.65), channel_id=1, source_target_pairs={{0,6},{1,7},{2,0},{3,1},{4,2},{5,3},{6,4},{7,5},{8,14},{9,15},{10,... | collective-permute-start | bytes 1769480 | tf_op jit(solution)/shard_map/ppermute | solution.py:349
  54.1 1.3 copy-start.1
  55.6 44.2 %copy-start.3 = (bf16[3,96,3072]{2,1,0:T(8,128)(2,1)}, bf16[3,96,3072]{2,1,0:T(8,128)(2,1)S(1)}, u32[]{:S(2)}) copy-start(bf16[3,96,3072]{2,1,0:T(8,128)(2,1)S(1)} %pad_maximum_fusion.refs_1_.refs_5_.refs_9_) | copy-start | bytes 5308420
  55.6 42.8 %collective-permute-start.4 = (bf16[3,96,3072]{2,1,0:T(8,128)(2,1)S(1)}, bf16[3,96,3072]{2,1,0:T(8,128)(2,1)S(1)}, u32[]{:S(2)}, u32[]{:S(2)}) collective-permute-start(bf16[3,96,3072]{2,1,0:T(8,128)(2,1)S(1)} %pad_maximum_fusion.refs_1_.refs_5_.refs_9_), channel_id=1, source_target_pairs={{0,1},{1,0},{2,3},{3,2},{4,5},{5,4},{6,7},{7,6},{8,9},{9,8},{10,11... | collective-permute-start | bytes 5308424 | tf_op jit(solution)/shard_map/ppermute | solution.py:349
  57.4 22.3 %collective-permute-start.5 = (bf16[96,2560]{1,0:T(8,128)(2,1)S(1)}, bf16[96,2560]{1,0:T(8,128)(2,1)S(1)}, u32[]{:S(2)}, u32[]{:S(2)}) collective-permute-start(bf16[96,2560]{1,0:T(8,128)(2,1)S(1)} %get-tuple-element.69), channel_id=1, source_target_pairs={{0,2},{1,3},{2,4},{3,5},{4,6},{5,7},{6,0},{7,1},{8,10},{9,11},{10,... | collective-permute-start | bytes 1474568 | tf_op jit(solution)/shard_map/ppermute | solution.py:349
  66.4 32.0 %collective-permute-start.6 = (bf16[96,2560]{1,0:T(8,128)(2,1)S(1)}, bf16[96,2560]{1,0:T(8,128)(2,1)S(1)}, u32[]{:S(2)}, u32[]{:S(2)}) collective-permute-start(bf16[96,2560]{1,0:T(8,128)(2,1)S(1)} %get-tuple-element.69), channel_id=1, source_target_pairs={{0,4},{1,5},{2,6},{3,7},{4,0},{5,1},{6,2},{7,3},{8,12},{9,13},{10,... | collective-permute-start | bytes 1474568 | tf_op jit(solution)/shard_map/ppermute | solution.py:349
  68.0 30.4 %collective-permute-start.7 = (bf16[96,2560]{1,0:T(8,128)(2,1)S(1)}, bf16[96,2560]{1,0:T(8,128)(2,1)S(1)}, u32[]{:S(2)}, u32[]{:S(2)}) collective-permute-start(bf16[96,2560]{1,0:T(8,128)(2,1)S(1)} %get-tuple-element.69), channel_id=1, source_target_pairs={{0,6},{1,7},{2,0},{3,1},{4,2},{5,3},{6,4},{7,5},{8,14},{9,15},{10,... | collective-permute-start | bytes 1474568 | tf_op jit(solution)/shard_map/ppermute | solution.py:349
  98.4 1.2 copy-start.5
  99.8 48.3 %copy-start.7 = (bf16[3,96,2560]{2,1,0:T(8,128)(2,1)}, bf16[3,96,2560]{2,1,0:T(8,128)(2,1)S(1)}, u32[]{:S(2)}) copy-start(bf16[3,96,2560]{2,1,0:T(8,128)(2,1)S(1)} %pad_maximum_fusion.1.refs_1_) | copy-start | bytes 4423684
  99.8 47.0 %collective-permute-start.8 = (bf16[3,96,2560]{2,1,0:T(8,128)(2,1)S(1)}, bf16[3,96,2560]{2,1,0:T(8,128)(2,1)S(1)}, u32[]{:S(2)}, u32[]{:S(2)}) collective-permute-start(bf16[3,96,2560]{2,1,0:T(8,128)(2,1)S(1)} %pad_maximum_fusion.1.refs_1_), channel_id=1, source_target_pairs={{0,1},{1,0},{2,3},{3,2},{4,5},{5,4},{6,7},{7,6},{8,9},{9,8},{10,11... | collective-permute-start | bytes 4423688 | tf_op jit(solution)/shard_map/ppermute | solution.py:349
  101.4 32.6 %collective-permute-start.10 = (bf16[96,2560]{1,0:T(8,128)(2,1)S(1)}, bf16[96,2560]{1,0:T(8,128)(2,1)S(1)}, u32[]{:S(2)}, u32[]{:S(2)}) collective-permute-start(bf16[96,2560]{1,0:T(8,128)(2,1)S(1)} %get-tuple-element.73), channel_id=1, source_target_pairs={{0,4},{1,5},{2,6},{3,7},{4,0},{5,1},{6,2},{7,3},{8,12},{9,13},{10,... | collective-permute-start | bytes 1474568 | tf_op jit(solution)/shard_map/ppermute | solution.py:349
  111.4 22.6 %collective-permute-start.11 = (bf16[96,2560]{1,0:T(8,128)(2,1)S(1)}, bf16[96,2560]{1,0:T(8,128)(2,1)S(1)}, u32[]{:S(2)}, u32[]{:S(2)}) collective-permute-start(bf16[96,2560]{1,0:T(8,128)(2,1)S(1)} %get-tuple-element.73), channel_id=1, source_target_pairs={{0,6},{1,7},{2,0},{3,1},{4,2},{5,3},{6,4},{7,5},{8,14},{9,15},{10,... | collective-permute-start | bytes 1474568 | tf_op jit(solution)/shard_map/ppermute | solution.py:349
  114.7 32.1 %collective-permute-start.9 = (bf16[96,2560]{1,0:T(8,128)(2,1)S(1)}, bf16[96,2560]{1,0:T(8,128)(2,1)S(1)}, u32[]{:S(2)}, u32[]{:S(2)}) collective-permute-start(bf16[96,2560]{1,0:T(8,128)(2,1)S(1)} %get-tuple-element.73), channel_id=1, source_target_pairs={{0,2},{1,3},{2,4},{3,5},{4,6},{5,7},{6,0},{7,1},{8,10},{9,11},{10,... | collective-permute-start | bytes 1474568 | tf_op jit(solution)/shard_map/ppermute | solution.py:349
  146.8 1.1 copy-start.10
  148.1 33.2 %collective-permute-start.12 = (bf16[3,96,2560]{2,1,0:T(8,128)(2,1)S(1)}, bf16[3,96,2560]{2,1,0:T(8,128)(2,1)}, u32[]{:S(2)}, u32[]{:S(2)}) collective-permute-start(bf16[3,96,2560]{2,1,0:T(8,128)(2,1)S(1)} %pad_maximum_fusion.2.refs_1_), channel_id=1, source_target_pairs={{0,1},{1,0},{2,3},{3,2},{4,5},{5,4},{6,7},{7,6},{8,9},{9,8},{10,11... | collective-permute-start | bytes 4423688 | tf_op jit(solution)/shard_map/ppermute | solution.py:349
  148.7 19.8 %collective-permute-start.13 = (bf16[96,1280]{1,0:T(8,128)(2,1)}, bf16[96,1280]{1,0:T(8,128)(2,1)}, u32[]{:S(2)}, u32[]{:S(2)}) collective-permute-start(bf16[96,1280]{1,0:T(8,128)(2,1)} %get-tuple-element.77), channel_id=1, source_target_pairs={{0,2},{1,3},{2,4},{3,5},{4,6},{5,7},{6,0},{7,1},{8,10},{9,11},{10,... | collective-permute-start | bytes 737288 | tf_op jit(solution)/shard_map/ppermute | solution.py:349
  161.8 12.8 %collective-permute-start.14 = (bf16[96,1280]{1,0:T(8,128)(2,1)}, bf16[96,1280]{1,0:T(8,128)(2,1)}, u32[]{:S(2)}, u32[]{:S(2)}) collective-permute-start(bf16[96,1280]{1,0:T(8,128)(2,1)} %get-tuple-element.77), channel_id=1, source_target_pairs={{0,4},{1,5},{2,6},{3,7},{4,0},{5,1},{6,2},{7,3},{8,12},{9,13},{10,... | collective-permute-start | bytes 737288 | tf_op jit(solution)/shard_map/ppermute | solution.py:349
  161.8 15.2 %collective-permute-start.15 = (bf16[96,1280]{1,0:T(8,128)(2,1)}, bf16[96,1280]{1,0:T(8,128)(2,1)}, u32[]{:S(2)}, u32[]{:S(2)}) collective-permute-start(bf16[96,1280]{1,0:T(8,128)(2,1)} %get-tuple-element.77), channel_id=1, source_target_pairs={{0,6},{1,7},{2,0},{3,1},{4,2},{5,3},{6,4},{7,5},{8,14},{9,15},{10,... | collective-permute-start | bytes 737288 | tf_op jit(solution)/shard_map/ppermute | solution.py:349
  182.6 43.2 %collective-permute-start.19 = (bf16[3,96,1280]{2,1,0:T(8,128)(2,1)S(1)}, bf16[3,96,1280]{2,1,0:T(8,128)(2,1)S(1)}, u32[]{:S(2)}, u32[]{:S(2)}) collective-permute-start(bf16[3,96,1280]{2,1,0:T(8,128)(2,1)S(1)} %pad_maximum_fusion.3.refs_1_), channel_id=1, source_target_pairs={{0,1},{1,0},{2,3},{3,2},{4,5},{5,4},{6,7},{7,6},{8,9},{9,8},{10,11... | collective-permute-start | bytes 2211848 | tf_op jit(solution)/shard_map/ppermute | solution.py:349
  183.1 1.6 copy-start.2
  184.7 1.5 copy-start.4
  186.2 1.5 copy-start.6
  187.7 10.8 %copy-start.15 = (bf16[96,1280]{1,0:T(8,128)(2,1)S(1)}, bf16[96,1280]{1,0:T(8,128)(2,1)}, u32[]{:S(2)}) copy-start(bf16[96,1280]{1,0:T(8,128)(2,1)} %copy-done.14) | copy-start | bytes 737284
  187.7 26.6 %copy-start.8 = (bf16[3,96,2560]{2,1,0:T(8,128)(2,1)S(1)}, bf16[3,96,2560]{2,1,0:T(8,128)(2,1)}, u32[]{:S(2)}) copy-start(bf16[3,96,2560]{2,1,0:T(8,128)(2,1)} %copy-done.7) | copy-start | bytes 4423684
  187.7 26.6 %copy-start.11 = (bf16[3,96,2560]{2,1,0:T(8,128)(2,1)S(1)}, bf16[3,96,2560]{2,1,0:T(8,128)(2,1)}, u32[]{:S(2)}) copy-start(bf16[3,96,2560]{2,1,0:T(8,128)(2,1)} %copy-done.10) | copy-start | bytes 4423684
  198.4 27.2 %collective-permute-start.16 = (bf16[96,1280]{1,0:T(8,128)(2,1)S(1)}, bf16[96,1280]{1,0:T(8,128)(2,1)S(1)}, u32[]{:S(2)}, u32[]{:S(2)}) collective-permute-start(bf16[96,1280]{1,0:T(8,128)(2,1)S(1)} %copy-done.15), channel_id=1, source_target_pairs={{0,2},{1,3},{2,4},{3,5},{4,6},{5,7},{6,0},{7,1},{8,10},{9,11},{10,... | collective-permute-start | bytes 737288 | tf_op jit(solution)/shard_map/ppermute | solution.py:349
  211.9 13.7 %collective-permute-start.17 = (bf16[96,1280]{1,0:T(8,128)(2,1)S(1)}, bf16[96,1280]{1,0:T(8,128)(2,1)S(1)}, u32[]{:S(2)}, u32[]{:S(2)}) collective-permute-start(bf16[96,1280]{1,0:T(8,128)(2,1)S(1)} %copy-done.15), channel_id=1, source_target_pairs={{0,4},{1,5},{2,6},{3,7},{4,0},{5,1},{6,2},{7,3},{8,12},{9,13},{10,... | collective-permute-start | bytes 737288 | tf_op jit(solution)/shard_map/ppermute | solution.py:349
  211.9 13.9 %collective-permute-start.18 = (bf16[96,1280]{1,0:T(8,128)(2,1)S(1)}, bf16[96,1280]{1,0:T(8,128)(2,1)S(1)}, u32[]{:S(2)}, u32[]{:S(2)}) collective-permute-start(bf16[96,1280]{1,0:T(8,128)(2,1)S(1)} %copy-done.15), channel_id=1, source_target_pairs={{0,6},{1,7},{2,0},{3,1},{4,2},{5,3},{6,4},{7,5},{8,14},{9,15},{10,... | collective-permute-start | bytes 737288 | tf_op jit(solution)/shard_map/ppermute | solution.py:349
  225.9 19.1 %collective-permute-start.20 = (bf16[3,96,1280]{2,1,0:T(8,128)(2,1)S(1)}, bf16[3,96,1280]{2,1,0:T(8,128)(2,1)S(1)}, u32[]{:S(2)}, u32[]{:S(2)}) collective-permute-start(bf16[3,96,1280]{2,1,0:T(8,128)(2,1)S(1)} %pad_maximum_fusion.4.refs_1_), channel_id=1, source_target_pairs={{0,1},{1,0},{2,3},{3,2},{4,5},{5,4},{6,7},{7,6},{8,9},{9,8},{10,11... | collective-permute-start | bytes 2211848 | tf_op jit(solution)/shard_map/ppermute | solution.py:349
  250.8 0.7 collective-permute-start.21
  251.5 23.0 %copy-start = (bf16[8,768,768]{2,1,0:T(8,128)(2,1)S(1)}, bf16[8,768,768]{2,1,0:T(8,128)(2,1)}, u32[]{:S(2)}) copy-start(bf16[8,768,768]{2,1,0:T(8,128)(2,1)} %get-tuple-element.110.factor_ref) | copy-start | bytes 28311556
  253.3 0.9 collective-permute-start.22
  256.0 18.5 %collective-permute-start.23 = (bf16[6,256,256]{2,1,0:T(8,128)(2,1)S(1)}, bf16[6,256,256]{2,1,0:T(8,128)(2,1)S(1)}, u32[]{:S(2)}, u32[]{:S(2)}) collective-permute-start(bf16[6,256,256]{2,1,0:T(8,128)(2,1)S(1)} %hop.3), channel_id=1, source_target_pairs={{8,0},{9,1},{10,2},{11,3},{12,4},{13,5},{14,6},{15,7}} | collective-permute-start | bytes 2359304 | tf_op jit(solution)/shard_map/ppermute | solution.py:386

commit v6 on v5

--- a/solution.py
+++ b/solution.py
@@ -13,6 +13,7 @@
 LANES = 128
 TILE = 256
 LINE = 4
+GATE = 3
 MIB = 1024 * 1024
 
 
@@ -42,23 +43,22 @@
     return pltpu.roll(wide, start, 1)
 
 
-def pack_kernel(count, ranges, place_ref, gain_ref, increment_ref, terminal_ref, whole_ref, *piece_refs):
-    steps, rows, width = gain_ref.shape
-    stride = width + half_width(rows, count)[1]
+def pack_kernel(count, ranges, place_ref, gain_ref, increment_ref, terminal_ref, *packed_refs):
+    width = gain_ref.shape[2]
+    stride = width + half_width(gain_ref.shape[1], count)[1]
     place = place_ref[0]
-    for step in range(steps):
-        base = step * stride
-        whole_ref[:, base:base + width] = gain_ref[step]
-        whole_ref[:, base + width:base + stride] = packed_half(increment_ref[step], place, count)
-    whole_ref[:, steps * stride:] = packed_half(terminal_ref[...], place, count)
-    for (low, high), piece_ref in zip(ranges, piece_refs):
-        piece_ref[...] = whole_ref[:, low * stride:low * stride + piece_ref.shape[1]]
+    for (low, high), packed_ref in zip(ranges, packed_refs):
+        for step in range(low, high):
+            base = (step - low) * stride
+            packed_ref[:, base:base + width] = gain_ref[step]
+            packed_ref[:, base + width:base + stride] = packed_half(increment_ref[step], place, count)
+    packed_refs[-1][...] = packed_half(terminal_ref[...], place, count)
 
 
 def pack(place, gains, increments, terminal, count, ranges):
-    steps, rows, width = gains.shape
+    rows, width = gains.shape[1:]
     half = half_width(rows, count)[1]
-    lanes = [(high - low) * (width + half) + half * (high == steps) for low, high in [(0, steps)] + ranges]
+    lanes = [(high - low) * (width + half) for low, high in ranges] + [half]
     vmem = pl.BlockSpec(memory_space=pltpu.VMEM)
     return pl.pallas_call(
         functools.partial(pack_kernel, count, ranges),
@@ -70,48 +70,27 @@
     )(place, gains, increments, terminal)
 
 
-def compose_kernel(lines, parts, first, last_ref, places_ref, *refs):
-    sizes = [lines[j] for j in range(len(lines))]
-    blocks = []
-    for size in sizes:
-        blocks.append(refs[:size])
-        refs = refs[size:]
-    ends = []
+def compose_kernel(count, first, last_ref, places_ref, *refs):
+    blocks, refs = refs[:count], refs[count:]
     if first:
-        for _ in range(parts):
-            ends.append([])
-            for size in sizes:
-                ends[-1].append(refs[:size])
-                refs = refs[size:]
+        end, refs = refs[0], refs[1:]
     else:
         factor_in, half_in, refs = refs[0], refs[1], refs[5:]
     factor_out, own_out, mine_out, factor_end, half_end, gain, factor, half, middle, total = refs
     width = factor.shape[0]
+    rows = width // count
     turn = pl.program_id(0)
-    spots = []
-    for j, group in enumerate(blocks):
-        for n, ref in enumerate(group):
-            inner = ref.shape[0] if len(ref.shape) == 3 else 1
-            for i in range(inner):
-                spots.append((j, n, i, len(ref.shape) == 3))
-    rows = width // len(spots)
-    starts = [pl.multiple_of(places_ref[1 + k] * rows, 16) for k in range(len(spots))]
-
-    def lanes(refs_of, spot, cut):
-        j, n, i, stacked = spot
-        return refs_of[j][n][i, :, cut] if stacked else refs_of[j][n][:, cut]
-
-    for spot, start in zip(spots, starts):
-        gain[pl.ds(start, rows), :] = lanes(blocks, spot, slice(0, width))
+    starts = [pl.multiple_of(places_ref[n] * rows, 16) for n in range(count)]
+    for start, block in zip(starts, blocks):
+        gain[pl.ds(start, rows), :] = block[:, :width]
 
     @pl.when(turn == 0)
     def _():
         if first:
             factor[...] = gain[...]
             scale = jnp.where(last_ref[0] == 1, 1.0, 0.0)
-            for spot, start in zip(spots, starts):
-                piece = jnp.concatenate([lanes(end, spot, slice(None)) for end in ends], axis=1)
-                half[pl.ds(start, rows), :] = (unpacked_half(piece, start, width) * scale).astype(BF16)
+            for n in range(count):
+                half[n * rows:(n + 1) * rows, :] = (unpacked_half(end[n], n * rows, width) * scale).astype(BF16)
         else:
             factor[...] = factor_in[...]
             half[...] = half_in[...]
@@ -130,12 +109,11 @@
         middle[:, cols] = jnp.dot(gain[...], half[:, cols], preferred_element_type=F32).astype(BF16)
     for j in range(0, width, TILE):
         total[:, j:j + TILE] = nt(middle[...], gain[j:j + TILE, :])
-    for spot, start in zip(spots, starts):
+    for start, block in zip(starts, blocks):
         span = pl.ds(start, rows)
-        piece = lanes(blocks, spot, slice(width, None))
-        half[span, :] = (total[span, :] + unpacked_half(piece, start, width)).astype(BF16)
-
-    mine = pl.multiple_of(places_ref[0] * rows, 16)
+        half[span, :] = (total[span, :] + unpacked_half(block[:, width:], start, width)).astype(BF16)
+
+    mine = starts[0]
     picked = lax.broadcasted_iota(jnp.int32, (rows, width), 1) == mine + lax.broadcasted_iota(
         jnp.int32, (rows, width), 0
     )
@@ -150,37 +128,24 @@
         half_end[...] = half[...]
 
 
-def compose(last, places, blocks, state, low, turns, steps):
-    lines = [len(group) for group in blocks]
-    flat = [block for group in blocks for block in group]
-    rows = flat[0][0].shape[-2]
-    width = rows * sum(block.shape[0] if block.ndim == 3 else 1 for block, _ in flat)
-    half = half_width(rows, width // rows)[1]
-    stride = width + half
+def compose(last, places, blocks, end, state, low, turns, steps):
+    count = len(blocks)
+    rows = blocks[0].shape[0]
+    width = rows * count
+    stride = width + half_width(rows, count)[1]
     first = state is None
     whole = pl.BlockSpec((width, width), lambda i, *p: (0, 0))
     anywhere = pl.BlockSpec(memory_space=pl.ANY)
-
-    def spec(block, size, place):
-        if block.ndim == 3:
-            return pl.BlockSpec((block.shape[0], rows, size), lambda i, *p: (0, 0, place(i)))
-        return pl.BlockSpec((rows, size), lambda i, *p: (0, place(i)))
-
-    in_specs = [spec(block, stride, lambda i, begin=begin: low + turns - 1 - i - begin) for block, begin in flat]
-    args = [block for block, _ in flat]
-    size = math.gcd(stride, half)
-    parts = half // size if first else 0
-    for n in range(parts):
-        in_specs += [
-            spec(block, size, lambda i, at=(steps - begin) * stride // size + n: at) for block, begin in flat
-        ]
-        args += [block for block, _ in flat]
-    if not first:
+    in_specs = [pl.BlockSpec((rows, stride), lambda i, *p: (0, turns - 1 - i))] * count
+    if first:
+        in_specs += [pl.BlockSpec(end.shape, lambda i, *p: (0, 0, 0))]
+        args = [*blocks, end]
+    else:
         in_specs += [whole, whole, anywhere, anywhere, anywhere]
-        args += [state[3], state[4], state[0], state[1], state[2]]
-    base = 2 + len(flat) + 2
+        args = [*blocks, state[3], state[4], state[0], state[1], state[2]]
+    base = 2 + count + 2
     return pl.pallas_call(
-        functools.partial(compose_kernel, lines, parts, first),
+        functools.partial(compose_kernel, count, first),
         grid_spec=pltpu.PrefetchScalarGridSpec(
             num_scalar_prefetch=2,
             grid=(turns,),
@@ -325,9 +290,17 @@
     )(factors, own, mine, *packed)
 
 
+def ring_order(line, across):
+    cycle = []
+    for a in range(line):
+        columns = list(range(1, across))
+        cycle += [a * across + b for b in (columns if a % 2 == 0 else columns[::-1])]
+    return cycle + [a * across for a in reversed(range(line))]
+
+
 def pieces(steps):
     small = max(steps // 8, 1)
-    cuts = [0, small, 2 * small, 4 * small, 6 * small, steps]
+    cuts = [0, small, 2 * small, (steps + 2 * small) // 2, steps]
     return list(zip(cuts, cuts[1:]))[::-1]
 
 
@@ -335,51 +308,37 @@
     count = lax.axis_size("tile")
     blocks = lax.axis_size("tm")
     line = math.gcd(count, LINE)
-    across = count // line
     steps = gains.shape[0]
     place = lax.axis_index("tile").astype(jnp.int32)
     last = (lax.axis_index("tm") == blocks - 1).astype(jnp.int32).reshape(1)
-
-    def shifted(array, along, over):
-        pairs = [
-            (a * across + b, (a + along) % line * across + (b + over) % across)
-            for a in range(line)
-            for b in range(across)
-        ]
-        return lax.ppermute(array, "tile", pairs) if along or over else array
-
-    places = jnp.stack(
-        [place]
-        + [
-            (place // across - i + line) % line * across + (place % across - j + across) % across
-            for j in range(across)
-            for i in range(line)
-        ]
-    )
+    cycle = ring_order(line, count // line)
+
+    def passed(array, way):
+        return lax.ppermute(array, "tile", [(cycle[n], cycle[(n + way) % count]) for n in range(count)])
+
+    def origins(way):
+        table = [[cycle[(cycle.index(d) - way * hop) % count] for hop in range(count)] for d in range(count)]
+        return jnp.asarray(table, jnp.int32)[place]
+
     ranges = pieces(steps)
-    whole, *own = pack(place.reshape(1), gains, increments, terminal, count, ranges)
-    passing = [shifted(whole, 0, j) for j in range(1, across)]
-    crossed = [whole] + passing
+    *own, end = pack(place.reshape(1), gains, increments, terminal, count, ranges)
+    end = lax.all_gather(end, "tile")
+    arrived = []
+    for turn, array in enumerate(own):
+        way = 1 if turn % 2 == 0 else -1
+        if turn >= 2:
+            before = arrived[turn - 2]
+            array, before[GATE] = lax.optimization_barrier((array, before[GATE]))
+            for hop_count in range(GATE + 1, count):
+                before[hop_count] = passed(before[hop_count - 1], way)
+        found = [array]
+        for hop_count in range(1, count):
+            found.append(passed(found[-1], way))
+        arrived.append(found)
     state = None
-    stages = []
-    for (low, high), array in zip(ranges, own):
-        if stages:
-            array, passing, parts = lax.optimization_barrier((array, passing, parts))
-            if len(stages) == 1:
-                crossed = [whole] + passing
-            else:
-                stages[-2][3][1:] = passing
-            stages[-1][3][0] = jnp.stack(parts)
-            passing = [shifted(stages[-1][3][0], 0, j) for j in range(1, across)]
-        parts = [shifted(array, i, 0) for i in range(1, line)]
-        stages.append((low, high, array, [None] * across))
-    last_parts, passing = lax.optimization_barrier((parts, passing))
-    stages[-2][3][1:] = passing
-    stacked = jnp.stack(last_parts)
-    stages[-1][3][:] = [shifted(stacked, 0, j) for j in range(across)]
-    for low, high, _, stacks in stages:
-        groups = [[(crossed[j], 0), (stacks[j], low)] for j in range(across)]
-        state = compose(last, places, groups, state, low, high - low, steps)
+    for turn, (low, high) in enumerate(ranges):
+        places = origins(1 if turn % 2 == 0 else -1)
+        state = compose(last, places, arrived[turn], end, state, low, high - low, steps)
     factors, own, mine, factor, half = state
     packed = []
     for turn in range(blocks - 1, 0, -1):

time: 285 us -> 291 us (1.021)
  starting transfers between devices: 73.8 us -> 31.6 us
  blocking collectives: 0 us -> 35 us
  local copies, waits for them, and re-layouts: 12.8 us -> 40 us
  Pallas kernels: 57.4 us -> 52.8 us
  waiting for transfers between devices: 135 us -> 131 us
    ppermute x21 -> x28, starting transfers between devices: 71 us -> 28.7 us  [passed(): lax.ppermute(array, 'tile', [(cycle[n], cycle[(n + way) % count]) for n i...]
    all_gather x0 -> x1, blocking collectives: none -> 35 us  [local(): end = lax.all_gather(end, 'tile')]
    unnamed x32 -> x62, local copies, waits for them, and re-layouts: 12.8 us -> 38.6 us
    ppermute x21 -> x28, waiting for transfers between devices: 118 us -> 113 us  [passed(): lax.ppermute(array, 'tile', [(cycle[n], cycle[(n + way) % count]) for n i...]
    pallas_call x5 -> x4, Pallas kernels: 45.1 us -> 41.3 us  [compose(): pl.pallas_call(functools.partial(compose_kernel, count, first), grid_spec...]
  transfers between devices with their start and end apart: 24 -> 31, of which waited for: 13 -> 11; matrix products, arithmetic and copies ran while one was open for 0% -> 0% of each run, Pallas kernels for 14% -> 12%
where the time goes in v6:
time: 291 us; the launch traced here: 290 us
  waiting for transfers between devices  131 us (45%)
  Pallas kernels  52.8 us (18%)
  local copies, waits for them, and re-layouts  40 us (14%)
  blocking collectives  35 us (12%)
  starting transfers between devices  31.6 us (11%)
    ppermute x28, waiting for transfers between devices, passed(): lax.ppermute(array, 'tile', [(cycle[n], cycle[(n + way) % count]) for n i...  113 us
    pallas_call x4, Pallas kernels, compose(): pl.pallas_call(functools.partial(compose_kernel, count, first), grid_spec...  41.3 us
    unnamed x62, local copies, waits for them, and re-layouts  38.6 us
    all_gather x1, blocking collectives, local(): end = lax.all_gather(end, 'tile')  35 us
    ppermute x28, starting transfers between devices, passed(): lax.ppermute(array, 'tile', [(cycle[n], cycle[(n + way) % count]) for n i...  28.7 us
    ppermute x3, waiting for transfers between devices, local(): lax.ppermute(hop(factor, half, packed), 'tm', [(turn, turn - 1)])  17.1 us
    pallas_call x1, Pallas kernels, finish(): pl.pallas_call(functools.partial(finish_kernel, len(packed)), grid=(steps...  6.76 us
  transfers between devices with their start and end apart: 31, of which 11 were waited for; matrix products, arithmetic and copies ran while one was open for 0% of the time, Pallas kernels for 12%

profile of v6, /device:TPU:0, one launch (start us, length us, event | category | flops | bytes accessed | tf_op | source)
XLA Modules:
  0.0 290.1 jit_solution(7355535798788481699)
XLA Ops:
  0.0 1.7 copy-done.6
  1.7 1.3 copy-done.7
  2.9 1.0 copy-done.8
  4.8 3.0 %collective-permute-start.10 = (bf16[96,3840]{1,0:T(8,128)(2,1)S(1)}, bf16[96,3840]{1,0:T(8,128)(2,1)S(1)}, u32[]{:S(2)}, u32[]{:S(2)}) collective-permute-start(bf16[96,3840]{1,0:T(8,128)(2,1)S(1)} %get-tuple-element.38.refs_0_), channel_id=1, source_target_pairs={{1,3},{3,5},{5,7},{7,6},{6,4},{4,2},{2,0},{0,1},{9,11},{11,13},{13... | collective-permute-start | bytes 2211848 | tf_op jit(solution)/shard_map/ppermute | solution.py:317
  9.6 14.7 %collective-permute-done.10.refs_1_ = bf16[96,3840]{1,0:T(8,128)(2,1)S(1)} collective-permute-done((bf16[96,3840]{1,0:T(8,128)(2,1)S(1)}, bf16[96,3840]{1,0:T(8,128)(2,1)S(1)}, u32[]{:S(2)}, u32[]{:S(2)}) %collective-permute-start.10) | collective-permute-done | bytes 737312 | tf_op jit(solution)/shard_map/ppermute | solution.py:317
  24.3 1.7 collective-permute-start.11
  28.1 13.9 %collective-permute-done.11.refs_2_ = bf16[96,3840]{1,0:T(8,128)(2,1)S(1)} collective-permute-done((bf16[96,3840]{1,0:T(8,128)(2,1)S(1)}, bf16[96,3840]{1,0:T(8,128)(2,1)S(1)}, u32[]{:S(2)}, u32[]{:S(2)}) %collective-permute-start.11) | collective-permute-done | bytes 737312 | tf_op jit(solution)/shard_map/ppermute | solution.py:317
  42.0 1.4 collective-permute-start.12
  45.7 13.0 %collective-permute-done.12.refs_3_ = bf16[96,3840]{1,0:T(8,128)(2,1)S(1)} collective-permute-done((bf16[96,3840]{1,0:T(8,128)(2,1)S(1)}, bf16[96,3840]{1,0:T(8,128)(2,1)S(1)}, u32[]{:S(2)}, u32[]{:S(2)}) %collective-permute-start.12) | collective-permute-done | bytes 737312 | tf_op jit(solution)/shard_map/ppermute | solution.py:317
  58.7 1.3 collective-permute-start.24
  62.6 12.8 %collective-permute-done.24.refs_4_ = bf16[96,3840]{1,0:T(8,128)(2,1)S(1)} collective-permute-done((bf16[96,3840]{1,0:T(8,128)(2,1)S(1)}, bf16[96,3840]{1,0:T(8,128)(2,1)S(1)}, u32[]{:S(2)}, u32[]{:S(2)}) %collective-permute-start.24) | collective-permute-done | bytes 737312 | tf_op jit(solution)/shard_map/ppermute | solution.py:317
  75.4 1.3 collective-permute-start.25
  77.5 1.6 collective-permute-start.13
  81.2 13.6 %collective-permute-done.25.refs_5_ = bf16[96,3840]{1,0:T(8,128)(2,1)S(1)} collective-permute-done((bf16[96,3840]{1,0:T(8,128)(2,1)S(1)}, bf16[96,3840]{1,0:T(8,128)(2,1)S(1)}, u32[]{:S(2)}, u32[]{:S(2)}) %collective-permute-start.25) | collective-permute-done | bytes 737312 | tf_op jit(solution)/shard_map/ppermute | solution.py:317
  94.8 1.3 collective-permute-start.26
  97.0 3.1 %collective-permute-done.13.refs_1_ = bf16[96,1280]{1,0:T(8,128)(2,1)S(1)} collective-permute-done((bf16[96,1280]{1,0:T(8,128)(2,1)S(1)}, bf16[96,1280]{1,0:T(8,128)(2,1)S(1)}, u32[]{:S(2)}, u32[]{:S(2)}) %collective-permute-start.13) | collective-permute-done | bytes 245792 | tf_op jit(solution)/shard_map/ppermute | solution.py:317
  100.1 1.3 collective-permute-start.14
  102.1 16.2 %collective-permute-done.14.refs_2_ = bf16[96,1280]{1,0:T(8,128)(2,1)S(1)} collective-permute-done((bf16[96,1280]{1,0:T(8,128)(2,1)S(1)}, bf16[96,1280]{1,0:T(8,128)(2,1)S(1)}, u32[]{:S(2)}, u32[]{:S(2)}) %collective-permute-start.14) | collective-permute-done | bytes 245792 | tf_op jit(solution)/shard_map/ppermute | solution.py:317
  118.3 1.3 collective-permute-start.15
  120.3 6.8 %collective-permute-done.15.refs_3_ = bf16[96,1280]{1,0:T(8,128)(2,1)S(1)} collective-permute-done((bf16[96,1280]{1,0:T(8,128)(2,1)S(1)}, bf16[96,1280]{1,0:T(8,128)(2,1)S(1)}, u32[]{:S(2)}, u32[]{:S(2)}) %collective-permute-start.15) | collective-permute-done | bytes 245792 | tf_op jit(solution)/shard_map/ppermute | solution.py:317
  127.1 1.3 collective-permute-start.16
  129.1 1.3 collective-permute-start.22
  131.2 4.8 %collective-permute-done.16.refs_4_ = bf16[96,1280]{1,0:T(8,128)(2,1)S(1)} collective-permute-done((bf16[96,1280]{1,0:T(8,128)(2,1)S(1)}, bf16[96,1280]{1,0:T(8,128)(2,1)S(1)}, u32[]{:S(2)}, u32[]{:S(2)}) %collective-permute-start.16) | collective-permute-done | bytes 245792 | tf_op jit(solution)/shard_map/ppermute | solution.py:317
  136.0 1.3 collective-permute-start.17
  139.4 14.5 %collective-permute-done.17.refs_5_ = bf16[96,1280]{1,0:T(8,128)(2,1)S(1)} collective-permute-done((bf16[96,1280]{1,0:T(8,128)(2,1)S(1)}, bf16[96,1280]{1,0:T(8,128)(2,1)S(1)}, u32[]{:S(2)}, u32[]{:S(2)}) %collective-permute-start.17) | collective-permute-done | bytes 245792 | tf_op jit(solution)/shard_map/ppermute | solution.py:317
  153.9 1.5 collective-permute-start.18
  155.9 35.0 %all-gather = bf16[768,512]{1,0:T(8,128)(2,1)S(1)} all-gather(bf16[96,512]{1,0:T(8,128)(2,1)S(1)} %get-tuple-element.42), channel_id=2, replica_groups=mesh['tm'=4,'tile'=8] {'tile'}, dimensions={0}, use_global_device_ids=true | all-gather | bytes 884736 | tf_op jit(solution)/shard_map/all_gather | solution.py:325
  190.9 2.0 collective-permute-start.9
  193.0 1.1 copy-done.14
  194.1 1.1 copy-done.18
  195.2 1.1 copy-done.20
  196.4 1.1 copy-done.24
  197.5 1.1 copy-done.28
  198.6 1.1 copy-done.30
  199.7 14.5 %compose.4 = (bf16[8,768,768]{2,1,0:T(8,128)(2,1)S(1)}, f32[8,96,768]{2,1,0:T(8,128)S(1)}, bf16[8,96,768]{2,1,0:T(8,128)(2,1)S(1)}, bf16[768,768]{1,0:T(8,128)(2,1)S(1)}, bf16[768,768]{1,0:T(8,128)(2,1)S(1)}) custom-call(s32[1]{0:T(128)} %bitcast.last_ref, s32[8]{0:T(128)S(1)} %dynamic-slice_bitcast_fusion.places_ref, bf16[96,3840]{1,0:T(8,128)(2,1)S(1)} %copy-done.14, ...), custom_call_target="tpu_custom_call" | custom-call | flops 8153726976 | bytes 14155776 | tf_op jit(solution)/shard_map/compose/pallas_call | solution.py:147
  214.3 3.6 %copy-done = bf16[8,768,768]{2,1,0:T(8,128)(2,1)} copy-done((bf16[8,768,768]{2,1,0:T(8,128)(2,1)}, bf16[8,768,768]{2,1,0:T(8,128)(2,1)S(1)}, u32[]{:S(2)}) %copy-start) | copy-done | bytes 9437208
  218.0 16.7 %compose.5 = (bf16[8,768,768]{2,1,0:T(8,128)(2,1)}, f32[8,96,768]{2,1,0:T(8,128)S(1)}, bf16[8,96,768]{2,1,0:T(8,128)(2,1)S(1)}, bf16[768,768]{1,0:T(8,128)(2,1)S(1)}, bf16[768,768]{1,0:T(8,128)(2,1)S(1)}) custom-call(s32[1]{0:T(128)} %bitcast.last_ref, ...), custom_call_target="tpu_custom_call", output_to_operand_aliasing={{0}: (12, {}), {1}: (13, {}), {2}: (14, {})} | custom-call | flops 8153726976 | bytes 14155776 | tf_op jit(solution)/shard_map/compose/pallas_call | solution.py:147
  234.7 3.7 %copy-done.1 = bf16[8,768,768]{2,1,0:T(8,128)(2,1)S(1)} copy-done((bf16[8,768,768]{2,1,0:T(8,128)(2,1)S(1)}, bf16[8,768,768]{2,1,0:T(8,128)(2,1)}, u32[]{:S(2)}) %copy-start.1) | copy-done | bytes 9437208
  238.3 5.0 %compose.6 = (bf16[8,768,768]{2,1,0:T(8,128)(2,1)S(1)}, f32[8,96,768]{2,1,0:T(8,128)S(1)}, bf16[8,96,768]{2,1,0:T(8,128)(2,1)S(1)}, bf16[768,768]{1,0:T(8,128)(2,1)S(1)}, bf16[768,768]{1,0:T(8,128)(2,1)S(1)}) custom-call(s32[1]{0:T(128)} %bitcast.last_ref, ...), custom_call_target="tpu_custom_call", output_to_operand_aliasing={{0}: (12, {}), {1}: (13, {}), {2}: (14, {})} | custom-call | flops 2717908992 | bytes 4718592 | tf_op jit(solution)/shard_map/compose/pallas_call | solution.py:147
  243.4 3.7 %copy-done.2 = bf16[8,768,768]{2,1,0:T(8,128)(2,1)} copy-done((bf16[8,768,768]{2,1,0:T(8,128)(2,1)}, bf16[8,768,768]{2,1,0:T(8,128)(2,1)S(1)}, u32[]{:S(2)}) %copy-start.2) | copy-done | bytes 9437208
  247.0 3.7 %copy-done.3 = bf16[8,768,768]{2,1,0:T(8,128)(2,1)S(1)} copy-done((bf16[8,768,768]{2,1,0:T(8,128)(2,1)S(1)}, bf16[8,768,768]{2,1,0:T(8,128)(2,1)}, u32[]{:S(2)}) %copy-start.3) | copy-done | bytes 9437208
  250.7 5.0 %compose.7 = (bf16[8,768,768]{2,1,0:T(8,128)(2,1)S(1)}, f32[8,96,768]{2,1,0:T(8,128)S(1)}, bf16[8,96,768]{2,1,0:T(8,128)(2,1)S(1)}, bf16[768,768]{1,0:T(8,128)(2,1)S(1)}, bf16[768,768]{1,0:T(8,128)(2,1)S(1)}) custom-call(s32[1]{0:T(128)} %bitcast.last_ref, ...), custom_call_target="tpu_custom_call", output_to_operand_aliasing={{0}: (12, {}), {1}: (13, {}), {2}: (14, {})} | custom-call | flops 2717908992 | bytes 4718592 | tf_op jit(solution)/shard_map/compose/pallas_call | solution.py:147
  255.7 3.7 %copy-done.4 = bf16[8,768,768]{2,1,0:T(8,128)(2,1)} copy-done((bf16[8,768,768]{2,1,0:T(8,128)(2,1)}, bf16[8,768,768]{2,1,0:T(8,128)(2,1)S(1)}, u32[]{:S(2)}) %copy-start.4) | copy-done | bytes 9437208
  260.4 1.8 hop.2
  263.1 1.8 hop.3
  265.0 1.3 collective-permute-start.30
  266.3 17.0 %collective-permute-done.30.refs_2_ = bf16[6,256,256]{2,1,0:T(8,128)(2,1)S(1)} collective-permute-done((bf16[6,256,256]{2,1,0:T(8,128)(2,1)S(1)}, bf16[6,256,256]{2,1,0:T(8,128)(2,1)S(1)}, u32[]{:S(2)}, u32[]{:S(2)}) %collective-permute-start.30) | collective-permute-done | bytes 786464 | tf_op jit(solution)/shard_map/ppermute | solution.py:345
  283.3 6.8 %finish.1 = f32[8,96,768]{2,1,0:T(8,128)} custom-call(bf16[8,768,768]{2,1,0:T(8,128)(2,1)S(1)} %copy-done.5, f32[8,96,768]{2,1,0:T(8,128)S(1)} %get-tuple-element.59.own_ref, bf16[8,96,768]{2,1,0:T(8,128)(2,1)S(1)} %get-tuple-element.60.mine_ref, bf16[6,256,256]{2,1,0:T(8,128)(2,1)S(1)} %collective-permute-done.28.refs_0_, ...), custom_call_target="tpu_custom_call" | custom-call | tf_op jit(solution)/shard_map/finish/pallas_call | solution.py:276
  (88 shorter events, 21.2 us)
Async XLA Ops:
  0.0 1.7 copy-start.6
  1.7 1.3 copy-start.7
  4.8 19.6 %collective-permute-start.10 = (bf16[96,3840]{1,0:T(8,128)(2,1)S(1)}, bf16[96,3840]{1,0:T(8,128)(2,1)S(1)}, u32[]{:S(2)}, u32[]{:S(2)}) collective-permute-start(bf16[96,3840]{1,0:T(8,128)(2,1)S(1)} %get-tuple-element.38.refs_0_), channel_id=1, source_target_pairs={{1,3},{3,5},{5,7},{7,6},{6,4},{4,2},{2,0},{0,1},{9,11},{11,13},{13... | collective-permute-start | bytes 2211848 | tf_op jit(solution)/shard_map/ppermute | solution.py:317
  8.7 18.2 %collective-permute-start = (bf16[96,3840]{1,0:T(8,128)(2,1)S(1)}, bf16[96,3840]{1,0:T(8,128)(2,1)S(1)}, u32[]{:S(2)}, u32[]{:S(2)}) collective-permute-start(bf16[96,3840]{1,0:T(8,128)(2,1)S(1)} %get-tuple-element.35.refs_0_), channel_id=1, source_target_pairs={{1,0},{3,1},{5,3},{7,5},{6,7},{4,6},{2,4},{0,2},{9,8},{11,9},{13,1... | collective-permute-start | bytes 2211848 | tf_op jit(solution)/shard_map/ppermute | solution.py:317
  24.3 17.7 %collective-permute-start.11 = (bf16[96,3840]{1,0:T(8,128)(2,1)S(1)}, bf16[96,3840]{1,0:T(8,128)(2,1)S(1)}, u32[]{:S(2)}, u32[]{:S(2)}) collective-permute-start(bf16[96,3840]{1,0:T(8,128)(2,1)S(1)} %collective-permute-done.10.refs_1_), channel_id=1, source_target_pairs={{1,3},{3,5},{5,7},{7,6},{6,4},{4,2},{2,0},{0,1},{9,11},{11,13},{13... | collective-permute-start | bytes 2211848 | tf_op jit(solution)/shard_map/ppermute | solution.py:317
  26.9 17.4 %collective-permute-start.1 = (bf16[96,3840]{1,0:T(8,128)(2,1)S(1)}, bf16[96,3840]{1,0:T(8,128)(2,1)S(1)}, u32[]{:S(2)}, u32[]{:S(2)}) collective-permute-start(bf16[96,3840]{1,0:T(8,128)(2,1)S(1)} %collective-permute-done.refs_1_), channel_id=1, source_target_pairs={{1,0},{3,1},{5,3},{7,5},{6,7},{4,6},{2,4},{0,2},{9,8},{11,9},{13,1... | collective-permute-start | bytes 2211848 | tf_op jit(solution)/shard_map/ppermute | solution.py:317
  42.0 16.8 %collective-permute-start.12 = (bf16[96,3840]{1,0:T(8,128)(2,1)S(1)}, bf16[96,3840]{1,0:T(8,128)(2,1)S(1)}, u32[]{:S(2)}, u32[]{:S(2)}) collective-permute-start(bf16[96,3840]{1,0:T(8,128)(2,1)S(1)} %collective-permute-done.11.refs_2_), channel_id=1, source_target_pairs={{1,3},{3,5},{5,7},{7,6},{6,4},{4,2},{2,0},{0,1},{9,11},{11,13},{13... | collective-permute-start | bytes 2211848 | tf_op jit(solution)/shard_map/ppermute | solution.py:317
  44.2 16.7 %collective-permute-start.2 = (bf16[96,3840]{1,0:T(8,128)(2,1)S(1)}, bf16[96,3840]{1,0:T(8,128)(2,1)S(1)}, u32[]{:S(2)}, u32[]{:S(2)}) collective-permute-start(bf16[96,3840]{1,0:T(8,128)(2,1)S(1)} %collective-permute-done.1.refs_2_), channel_id=1, source_target_pairs={{1,0},{3,1},{5,3},{7,5},{6,7},{4,6},{2,4},{0,2},{9,8},{11,9},{13,1... | collective-permute-start | bytes 2211848 | tf_op jit(solution)/shard_map/ppermute | solution.py:317
  58.7 16.7 %collective-permute-start.24 = (bf16[96,3840]{1,0:T(8,128)(2,1)S(1)}, bf16[96,3840]{1,0:T(8,128)(2,1)S(1)}, u32[]{:S(2)}, u32[]{:S(2)}) collective-permute-start(bf16[96,3840]{1,0:T(8,128)(2,1)S(1)} %collective-permute-done.12.refs_3_), channel_id=1, source_target_pairs={{1,3},{3,5},{5,7},{7,6},{6,4},{4,2},{2,0},{0,1},{9,11},{11,13},{13... | collective-permute-start | bytes 2211848 | tf_op jit(solution)/shard_map/ppermute | solution.py:317
  60.9 18.7 %collective-permute-start.20 = (bf16[96,3840]{1,0:T(8,128)(2,1)S(1)}, bf16[96,3840]{1,0:T(8,128)(2,1)S(1)}, u32[]{:S(2)}, u32[]{:S(2)}) collective-permute-start(bf16[96,3840]{1,0:T(8,128)(2,1)S(1)} %collective-permute-done.2.refs_3_), channel_id=1, source_target_pairs={{1,0},{3,1},{5,3},{7,5},{6,7},{4,6},{2,4},{0,2},{9,8},{11,9},{13,1... | collective-permute-start | bytes 2211848 | tf_op jit(solution)/shard_map/ppermute | solution.py:317
  75.4 19.4 %collective-permute-start.25 = (bf16[96,3840]{1,0:T(8,128)(2,1)S(1)}, bf16[96,3840]{1,0:T(8,128)(2,1)S(1)}, u32[]{:S(2)}, u32[]{:S(2)}) collective-permute-start(bf16[96,3840]{1,0:T(8,128)(2,1)S(1)} %collective-permute-done.24.refs_4_), channel_id=1, source_target_pairs={{1,3},{3,5},{5,7},{7,6},{6,4},{4,2},{2,0},{0,1},{9,11},{11,13},{13... | collective-permute-start | bytes 2211848 | tf_op jit(solution)/shard_map/ppermute | solution.py:317
  77.5 22.6 %collective-permute-start.13 = (bf16[96,1280]{1,0:T(8,128)(2,1)S(1)}, bf16[96,1280]{1,0:T(8,128)(2,1)S(1)}, u32[]{:S(2)}, u32[]{:S(2)}) collective-permute-start(bf16[96,1280]{1,0:T(8,128)(2,1)S(1)} %get-tuple-element.39.refs_0_), channel_id=1, source_target_pairs={{1,3},{3,5},{5,7},{7,6},{6,4},{4,2},{2,0},{0,1},{9,11},{11,13},{13... | collective-permute-start | bytes 737288 | tf_op jit(solution)/shard_map/ppermute | solution.py:317
  79.1 22.3 %collective-permute-start.3 = (bf16[96,1280]{1,0:T(8,128)(2,1)S(1)}, bf16[96,1280]{1,0:T(8,128)(2,1)S(1)}, u32[]{:S(2)}, u32[]{:S(2)}) collective-permute-start(bf16[96,1280]{1,0:T(8,128)(2,1)S(1)} %get-tuple-element.36.refs_0_), channel_id=1, source_target_pairs={{1,0},{3,1},{5,3},{7,5},{6,7},{4,6},{2,4},{0,2},{9,8},{11,9},{13,1... | collective-permute-start | bytes 737288 | tf_op jit(solution)/shard_map/ppermute | solution.py:317
  79.6 49.6 %collective-permute-start.21 = (bf16[96,3840]{1,0:T(8,128)(2,1)S(1)}, bf16[96,3840]{1,0:T(8,128)(2,1)}, u32[]{:S(2)}, u32[]{:S(2)}) collective-permute-start(bf16[96,3840]{1,0:T(8,128)(2,1)S(1)} %collective-permute-done.20.refs_4_), channel_id=1, source_target_pairs={{1,0},{3,1},{5,3},{7,5},{6,7},{4,6},{2,4},{0,2},{9,8},{11,9},{13,1... | collective-permute-start | bytes 2211848 | tf_op jit(solution)/shard_map/ppermute | solution.py:317
  94.8 35.6 %collective-permute-start.26 = (bf16[96,3840]{1,0:T(8,128)(2,1)S(1)}, bf16[96,3840]{1,0:T(8,128)(2,1)}, u32[]{:S(2)}, u32[]{:S(2)}) collective-permute-start(bf16[96,3840]{1,0:T(8,128)(2,1)S(1)} %collective-permute-done.25.refs_5_), channel_id=1, source_target_pairs={{1,3},{3,5},{5,7},{7,6},{6,4},{4,2},{2,0},{0,1},{9,11},{11,13},{13... | collective-permute-start | bytes 2211848 | tf_op jit(solution)/shard_map/ppermute | solution.py:317
  100.1 18.2 %collective-permute-start.14 = (bf16[96,1280]{1,0:T(8,128)(2,1)S(1)}, bf16[96,1280]{1,0:T(8,128)(2,1)S(1)}, u32[]{:S(2)}, u32[]{:S(2)}) collective-permute-start(bf16[96,1280]{1,0:T(8,128)(2,1)S(1)} %collective-permute-done.13.refs_1_), channel_id=1, source_target_pairs={{1,3},{3,5},{5,7},{7,6},{6,4},{4,2},{2,0},{0,1},{9,11},{11,13},{13... | collective-permute-start | bytes 737288 | tf_op jit(solution)/shard_map/ppermute | solution.py:317
  101.4 18.2 %collective-permute-start.4 = (bf16[96,1280]{1,0:T(8,128)(2,1)S(1)}, bf16[96,1280]{1,0:T(8,128)(2,1)S(1)}, u32[]{:S(2)}, u32[]{:S(2)}) collective-permute-start(bf16[96,1280]{1,0:T(8,128)(2,1)S(1)} %collective-permute-done.3.refs_1_), channel_id=1, source_target_pairs={{1,0},{3,1},{5,3},{7,5},{6,7},{4,6},{2,4},{0,2},{9,8},{11,9},{13,1... | collective-permute-start | bytes 737288 | tf_op jit(solution)/shard_map/ppermute | solution.py:317
  118.3 8.8 %collective-permute-start.15 = (bf16[96,1280]{1,0:T(8,128)(2,1)S(1)}, bf16[96,1280]{1,0:T(8,128)(2,1)S(1)}, u32[]{:S(2)}, u32[]{:S(2)}) collective-permute-start(bf16[96,1280]{1,0:T(8,128)(2,1)S(1)} %collective-permute-done.14.refs_2_), channel_id=1, source_target_pairs={{1,3},{3,5},{5,7},{7,6},{6,4},{4,2},{2,0},{0,1},{9,11},{11,13},{13... | collective-permute-start | bytes 737288 | tf_op jit(solution)/shard_map/ppermute | solution.py:317
  119.6 8.8 %collective-permute-start.5 = (bf16[96,1280]{1,0:T(8,128)(2,1)S(1)}, bf16[96,1280]{1,0:T(8,128)(2,1)S(1)}, u32[]{:S(2)}, u32[]{:S(2)}) collective-permute-start(bf16[96,1280]{1,0:T(8,128)(2,1)S(1)} %collective-permute-done.4.refs_2_), channel_id=1, source_target_pairs={{1,0},{3,1},{5,3},{7,5},{6,7},{4,6},{2,4},{0,2},{9,8},{11,9},{13,1... | collective-permute-start | bytes 737288 | tf_op jit(solution)/shard_map/ppermute | solution.py:317
  127.1 8.9 %collective-permute-start.16 = (bf16[96,1280]{1,0:T(8,128)(2,1)S(1)}, bf16[96,1280]{1,0:T(8,128)(2,1)S(1)}, u32[]{:S(2)}, u32[]{:S(2)}) collective-permute-start(bf16[96,1280]{1,0:T(8,128)(2,1)S(1)} %collective-permute-done.15.refs_3_), channel_id=1, source_target_pairs={{1,3},{3,5},{5,7},{7,6},{6,4},{4,2},{2,0},{0,1},{9,11},{11,13},{13... | collective-permute-start | bytes 737288 | tf_op jit(solution)/shard_map/ppermute | solution.py:317
  128.4 8.9 %collective-permute-start.6 = (bf16[96,1280]{1,0:T(8,128)(2,1)S(1)}, bf16[96,1280]{1,0:T(8,128)(2,1)S(1)}, u32[]{:S(2)}, u32[]{:S(2)}) collective-permute-start(bf16[96,1280]{1,0:T(8,128)(2,1)S(1)} %collective-permute-done.5.refs_3_), channel_id=1, source_target_pairs={{1,0},{3,1},{5,3},{7,5},{6,7},{4,6},{2,4},{0,2},{9,8},{11,9},{13,1... | collective-permute-start | bytes 737288 | tf_op jit(solution)/shard_map/ppermute | solution.py:317
  129.1 63.8 %collective-permute-start.22 = (bf16[96,3840]{1,0:T(8,128)(2,1)}, bf16[96,3840]{1,0:T(8,128)(2,1)}, u32[]{:S(2)}, u32[]{:S(2)}) collective-permute-start(bf16[96,3840]{1,0:T(8,128)(2,1)} %collective-permute-done.21.refs_5_), channel_id=1, source_target_pairs={{1,0},{3,1},{5,3},{7,5},{6,7},{4,6},{2,4},{0,2},{9,8},{11,9},{13,1... | collective-permute-start | bytes 2211848 | tf_op jit(solution)/shard_map/ppermute | solution.py:317
  130.5 62.5 %collective-permute-start.27 = (bf16[96,3840]{1,0:T(8,128)(2,1)}, bf16[96,3840]{1,0:T(8,128)(2,1)}, u32[]{:S(2)}, u32[]{:S(2)}) collective-permute-start(bf16[96,3840]{1,0:T(8,128)(2,1)} %collective-permute-done.26.refs_6_), channel_id=1, source_target_pairs={{1,3},{3,5},{5,7},{7,6},{6,4},{4,2},{2,0},{0,1},{9,11},{11,13},{13... | collective-permute-start | bytes 2211848 | tf_op jit(solution)/shard_map/ppermute | solution.py:317
  136.0 17.9 %collective-permute-start.17 = (bf16[96,1280]{1,0:T(8,128)(2,1)S(1)}, bf16[96,1280]{1,0:T(8,128)(2,1)S(1)}, u32[]{:S(2)}, u32[]{:S(2)}) collective-permute-start(bf16[96,1280]{1,0:T(8,128)(2,1)S(1)} %collective-permute-done.16.refs_4_), channel_id=1, source_target_pairs={{1,3},{3,5},{5,7},{7,6},{6,4},{4,2},{2,0},{0,1},{9,11},{11,13},{13... | collective-permute-start | bytes 737288 | tf_op jit(solution)/shard_map/ppermute | solution.py:317
  137.3 18.2 %collective-permute-start.7 = (bf16[96,1280]{1,0:T(8,128)(2,1)S(1)}, bf16[96,1280]{1,0:T(8,128)(2,1)S(1)}, u32[]{:S(2)}, u32[]{:S(2)}) collective-permute-start(bf16[96,1280]{1,0:T(8,128)(2,1)S(1)} %collective-permute-done.6.refs_4_), channel_id=1, source_target_pairs={{1,0},{3,1},{5,3},{7,5},{6,7},{4,6},{2,4},{0,2},{9,8},{11,9},{13,1... | collective-permute-start | bytes 737288 | tf_op jit(solution)/shard_map/ppermute | solution.py:317
  153.9 37.0 %collective-permute-start.18 = (bf16[96,1280]{1,0:T(8,128)(2,1)S(1)}, bf16[96,1280]{1,0:T(8,128)(2,1)S(1)}, u32[]{:S(2)}, u32[]{:S(2)}) collective-permute-start(bf16[96,1280]{1,0:T(8,128)(2,1)S(1)} %collective-permute-done.17.refs_5_), channel_id=1, source_target_pairs={{1,3},{3,5},{5,7},{7,6},{6,4},{4,2},{2,0},{0,1},{9,11},{11,13},{13... | collective-permute-start | bytes 737288 | tf_op jit(solution)/shard_map/ppermute | solution.py:317
  155.4 35.5 %collective-permute-start.8 = (bf16[96,1280]{1,0:T(8,128)(2,1)S(1)}, bf16[96,1280]{1,0:T(8,128)(2,1)S(1)}, u32[]{:S(2)}, u32[]{:S(2)}) collective-permute-start(bf16[96,1280]{1,0:T(8,128)(2,1)S(1)} %collective-permute-done.7.refs_5_), channel_id=1, source_target_pairs={{1,0},{3,1},{5,3},{7,5},{6,7},{4,6},{2,4},{0,2},{9,8},{11,9},{13,1... | collective-permute-start | bytes 737288 | tf_op jit(solution)/shard_map/ppermute | solution.py:317
  190.9 43.8 %collective-permute-start.19 = (bf16[96,1280]{1,0:T(8,128)(2,1)S(1)}, bf16[96,1280]{1,0:T(8,128)(2,1)S(1)}, u32[]{:S(2)}, u32[]{:S(2)}) collective-permute-start(bf16[96,1280]{1,0:T(8,128)(2,1)S(1)} %collective-permute-done.18.refs_6_), channel_id=1, source_target_pairs={{1,3},{3,5},{5,7},{7,6},{6,4},{4,2},{2,0},{0,1},{9,11},{11,13},{13... | collective-permute-start | bytes 737288 | tf_op jit(solution)/shard_map/ppermute | solution.py:317
  190.9 56.1 %collective-permute-start.9 = (bf16[96,1280]{1,0:T(8,128)(2,1)S(1)}, bf16[96,1280]{1,0:T(8,128)(2,1)S(1)}, u32[]{:S(2)}, u32[]{:S(2)}) collective-permute-start(bf16[96,1280]{1,0:T(8,128)(2,1)S(1)} %collective-permute-done.8.refs_6_), channel_id=1, source_target_pairs={{1,0},{3,1},{5,3},{7,5},{6,7},{4,6},{2,4},{0,2},{9,8},{11,9},{13,1... | collective-permute-start | bytes 737288 | tf_op jit(solution)/shard_map/ppermute | solution.py:317
  192.9 25.0 %collective-permute-start.23 = (bf16[96,3840]{1,0:T(8,128)(2,1)}, bf16[96,3840]{1,0:T(8,128)(2,1)S(1)}, u32[]{:S(2)}, u32[]{:S(2)}) collective-permute-start(bf16[96,3840]{1,0:T(8,128)(2,1)} %collective-permute-done.22.refs_6_), channel_id=1, source_target_pairs={{1,0},{3,1},{5,3},{7,5},{6,7},{4,6},{2,4},{0,2},{9,8},{11,9},{13,1... | collective-permute-start | bytes 2211848 | tf_op jit(solution)/shard_map/ppermute | solution.py:317
  193.0 1.1 copy-start.14
  194.1 1.1 copy-start.18
  195.2 1.1 copy-start.20
  196.3 1.1 copy-start.24
  199.7 18.2 %copy-start.10 = (bf16[96,3840]{1,0:T(8,128)(2,1)S(1)}, bf16[96,3840]{1,0:T(8,128)(2,1)}, u32[]{:S(2)}) copy-start(bf16[96,3840]{1,0:T(8,128)(2,1)} %copy-done.9) | copy-start | bytes 2211844
  199.7 18.2 %copy-start.12 = (bf16[96,3840]{1,0:T(8,128)(2,1)S(1)}, bf16[96,3840]{1,0:T(8,128)(2,1)}, u32[]{:S(2)}) copy-start(bf16[96,3840]{1,0:T(8,128)(2,1)} %copy-done.11) | copy-start | bytes 2211844
  199.7 18.2 %copy-start.16 = (bf16[96,3840]{1,0:T(8,128)(2,1)S(1)}, bf16[96,3840]{1,0:T(8,128)(2,1)}, u32[]{:S(2)}) copy-start(bf16[96,3840]{1,0:T(8,128)(2,1)} %copy-done.15) | copy-start | bytes 2211844
  199.7 18.2 %copy-start.22 = (bf16[96,3840]{1,0:T(8,128)(2,1)S(1)}, bf16[96,3840]{1,0:T(8,128)(2,1)}, u32[]{:S(2)}) copy-start(bf16[96,3840]{1,0:T(8,128)(2,1)} %copy-done.21) | copy-start | bytes 2211844
  199.7 18.2 %copy-start.26 = (bf16[96,3840]{1,0:T(8,128)(2,1)S(1)}, bf16[96,3840]{1,0:T(8,128)(2,1)}, u32[]{:S(2)}) copy-start(bf16[96,3840]{1,0:T(8,128)(2,1)} %copy-done.25) | copy-start | bytes 2211844
  214.3 3.7 %copy-start = (bf16[8,768,768]{2,1,0:T(8,128)(2,1)}, bf16[8,768,768]{2,1,0:T(8,128)(2,1)S(1)}, u32[]{:S(2)}) copy-start(bf16[8,768,768]{2,1,0:T(8,128)(2,1)S(1)} %get-tuple-element.45.refs_10_) | copy-start | bytes 28311556
  234.7 3.7 %copy-start.1 = (bf16[8,768,768]{2,1,0:T(8,128)(2,1)S(1)}, bf16[8,768,768]{2,1,0:T(8,128)(2,1)}, u32[]{:S(2)}) copy-start(bf16[8,768,768]{2,1,0:T(8,128)(2,1)} %get-tuple-element.50.refs_10_) | copy-start | bytes 28311556
  243.4 3.7 %copy-start.2 = (bf16[8,768,768]{2,1,0:T(8,128)(2,1)}, bf16[8,768,768]{2,1,0:T(8,128)(2,1)S(1)}, u32[]{:S(2)}) copy-start(bf16[8,768,768]{2,1,0:T(8,128)(2,1)S(1)} %get-tuple-element.55.refs_10_) | copy-start | bytes 28311556
  247.0 3.7 %copy-start.3 = (bf16[8,768,768]{2,1,0:T(8,128)(2,1)S(1)}, bf16[8,768,768]{2,1,0:T(8,128)(2,1)}, u32[]{:S(2)}) copy-start(bf16[8,768,768]{2,1,0:T(8,128)(2,1)} %copy-done.2) | copy-start | bytes 28311556
  255.7 3.7 %copy-start.4 = (bf16[8,768,768]{2,1,0:T(8,128)(2,1)}, bf16[8,768,768]{2,1,0:T(8,128)(2,1)S(1)}, u32[]{:S(2)}) copy-start(bf16[8,768,768]{2,1,0:T(8,128)(2,1)S(1)} %get-tuple-element.58.factor_ref) | copy-start | bytes 28311556
  259.7 0.7 collective-permute-start.28
  260.4 22.9 %copy-start.5 = (bf16[8,768,768]{2,1,0:T(8,128)(2,1)S(1)}, bf16[8,768,768]{2,1,0:T(8,128)(2,1)}, u32[]{:S(2)}) copy-start(bf16[8,768,768]{2,1,0:T(8,128)(2,1)} %copy-done.4) | copy-start | bytes 28311556
  262.3 0.9 collective-permute-start.29
  265.0 18.3 %collective-permute-start.30 = (bf16[6,256,256]{2,1,0:T(8,128)(2,1)S(1)}, bf16[6,256,256]{2,1,0:T(8,128)(2,1)S(1)}, u32[]{:S(2)}, u32[]{:S(2)}) collective-permute-start(bf16[6,256,256]{2,1,0:T(8,128)(2,1)S(1)} %hop.3), channel_id=1, source_target_pairs={{8,0},{9,1},{10,2},{11,3},{12,4},{13,5},{14,6},{15,7}} | collective-permute-start | bytes 2359304 | tf_op jit(solution)/shard_map/ppermute | solution.py:345
  (14 other events, 12.9 us)

commit v7 on v6

--- a/solution.py
+++ b/solution.py
@@ -43,7 +43,7 @@
     return pltpu.roll(wide, start, 1)
 
 
-def pack_kernel(count, ranges, place_ref, gain_ref, increment_ref, terminal_ref, *packed_refs):
+def pack_kernel(count, ranges, place_ref, gain_ref, increment_ref, *packed_refs):
     width = gain_ref.shape[2]
     stride = width + half_width(gain_ref.shape[1], count)[1]
     place = place_ref[0]
@@ -52,22 +52,21 @@
             base = (step - low) * stride
             packed_ref[:, base:base + width] = gain_ref[step]
             packed_ref[:, base + width:base + stride] = packed_half(increment_ref[step], place, count)
-    packed_refs[-1][...] = packed_half(terminal_ref[...], place, count)
-
-
-def pack(place, gains, increments, terminal, count, ranges):
+
+
+def pack(place, gains, increments, count, ranges):
     rows, width = gains.shape[1:]
     half = half_width(rows, count)[1]
-    lanes = [(high - low) * (width + half) for low, high in ranges] + [half]
+    lanes = [(high - low) * (width + half) for low, high in ranges]
     vmem = pl.BlockSpec(memory_space=pltpu.VMEM)
     return pl.pallas_call(
         functools.partial(pack_kernel, count, ranges),
-        in_specs=[pl.BlockSpec(memory_space=pltpu.SMEM), vmem, vmem, vmem],
+        in_specs=[pl.BlockSpec(memory_space=pltpu.SMEM), vmem, vmem],
         out_specs=[vmem] * len(lanes),
         out_shape=[jax.ShapeDtypeStruct((rows, size), BF16) for size in lanes],
-        compiler_params=pltpu.CompilerParams(vmem_limit_bytes=24 * MIB),
+        compiler_params=pltpu.CompilerParams(vmem_limit_bytes=12 * MIB),
         name="pack",
-    )(place, gains, increments, terminal)
+    )(place, gains, increments)
 
 
 def compose_kernel(count, first, last_ref, places_ref, *refs):
@@ -75,8 +74,8 @@
     if first:
         end, refs = refs[0], refs[1:]
     else:
-        factor_in, half_in, refs = refs[0], refs[1], refs[5:]
-    factor_out, own_out, mine_out, factor_end, half_end, gain, factor, half, middle, total = refs
+        half_in, factor_in, refs = refs[0], refs[1], refs[4:]
+    factor_out, own_out, mine_out, half_end, gain, factor, half, middle, total = refs
     width = factor.shape[0]
     rows = width // count
     turn = pl.program_id(0)
@@ -88,11 +87,10 @@
     def _():
         if first:
             factor[...] = gain[...]
-            scale = jnp.where(last_ref[0] == 1, 1.0, 0.0)
-            for n in range(count):
-                half[n * rows:(n + 1) * rows, :] = (unpacked_half(end[n], n * rows, width) * scale).astype(BF16)
+            scale = jnp.where(last_ref[0] == 1, 0.5, 0.0)
+            half[...] = (end[...].astype(F32) * scale).astype(BF16)
         else:
-            factor[...] = factor_in[...]
+            factor[...] = factor_in[0]
             half[...] = half_in[...]
 
     def extend():
@@ -124,7 +122,6 @@
 
     @pl.when(turn == pl.num_programs(0) - 1)
     def _():
-        factor_end[...] = factor[...]
         half_end[...] = half[...]
 
 
@@ -138,12 +135,13 @@
     anywhere = pl.BlockSpec(memory_space=pl.ANY)
     in_specs = [pl.BlockSpec((rows, stride), lambda i, *p: (0, turns - 1 - i))] * count
     if first:
-        in_specs += [pl.BlockSpec(end.shape, lambda i, *p: (0, 0, 0))]
+        in_specs += [whole]
         args = [*blocks, end]
     else:
-        in_specs += [whole, whole, anywhere, anywhere, anywhere]
-        args = [*blocks, state[3], state[4], state[0], state[1], state[2]]
-    base = 2 + count + 2
+        after = pl.BlockSpec((1, width, width), lambda i, *p: (low + turns, 0, 0))
+        in_specs += [whole, after, anywhere, anywhere]
+        args = [*blocks, state[3], state[0], state[1], state[2]]
+    base = 2 + count + 1
     return pl.pallas_call(
         functools.partial(compose_kernel, count, first),
         grid_spec=pltpu.PrefetchScalarGridSpec(
@@ -155,7 +153,6 @@
                 pl.BlockSpec((1, rows, width), lambda i, *p: (low + turns - 1 - i, 0, 0)),
                 pl.BlockSpec((1, rows, width), lambda i, *p: (low + turns - 1 - i, 0, 0)),
                 whole,
-                whole,
             ],
             scratch_shapes=[pltpu.VMEM((width, width), BF16) for _ in range(4)]
             + [pltpu.VMEM((width, width), F32)],
@@ -165,10 +162,9 @@
             jax.ShapeDtypeStruct((steps, rows, width), F32),
             jax.ShapeDtypeStruct((steps, rows, width), BF16),
             jax.ShapeDtypeStruct((width, width), BF16),
-            jax.ShapeDtypeStruct((width, width), BF16),
         ],
         input_output_aliases={} if first else {base: 0, base + 1: 1, base + 2: 2},
-        compiler_params=pltpu.CompilerParams(vmem_limit_bytes=32 * MIB),
+        compiler_params=pltpu.CompilerParams(vmem_limit_bytes=25 * MIB),
         cost_estimate=pl.CostEstimate(
             flops=6 * turns * width**3, bytes_accessed=8 * turns * width * width, transcendentals=0
         ),
@@ -208,39 +204,47 @@
 
 def hop_kernel(arrived, factor_ref, half_ref, *refs):
     out_ref, covariance, middle, ahead = refs[arrived:]
-    width = factor_ref.shape[0]
+    width = factor_ref.shape[1]
     for n, (a, b) in enumerate(upper_blocks(width)):
         covariance[a:a + TILE, b:b + TILE] = arrived_sum(refs[:arrived], n)
     for j in range(0, width, TILE):
         cols = slice(j, j + TILE)
         middle[:, cols] = jnp.dot(
-            factor_ref[:, :j + TILE], covariance[:j + TILE, cols], preferred_element_type=F32
+            factor_ref[0, :, :j + TILE], covariance[:j + TILE, cols], preferred_element_type=F32
         ).astype(BF16)
     for j in range(0, width, TILE):
         cols = slice(j, j + TILE)
-        ahead[:, cols] = (nt(middle[...], factor_ref[cols, :]) + half_ref[:, cols].astype(F32)).astype(BF16)
+        ahead[:, cols] = (nt(middle[...], factor_ref[0, cols, :]) + half_ref[:, cols].astype(F32)).astype(BF16)
     fold(ahead, out_ref)
 
 
-def hop(factor, half, packed):
-    width = factor.shape[0]
+def hop(factors, half, packed):
+    width = half.shape[0]
     shape = (len(upper_blocks(width)), TILE, TILE)
     square = pltpu.VMEM((width, width), BF16)
     if not packed:
         return pl.pallas_call(
             fold_kernel,
             out_shape=jax.ShapeDtypeStruct(shape, BF16),
-            compiler_params=pltpu.CompilerParams(vmem_limit_bytes=16 * MIB),
+            compiler_params=pltpu.CompilerParams(vmem_limit_bytes=12 * MIB),
             name="fold",
         )(half)
+    blocks = pl.BlockSpec(shape, lambda i: (0, 0, 0))
     return pl.pallas_call(
         functools.partial(hop_kernel, len(packed)),
+        grid=(1,),
+        in_specs=[
+            pl.BlockSpec((1, width, width), lambda i: (0, 0, 0)),
+            pl.BlockSpec((width, width), lambda i: (0, 0)),
+        ]
+        + [blocks] * len(packed),
+        out_specs=blocks,
         out_shape=jax.ShapeDtypeStruct(shape, BF16),
         scratch_shapes=[square, square, square],
         compiler_params=pltpu.CompilerParams(vmem_limit_bytes=20 * MIB),
         cost_estimate=pl.CostEstimate(flops=4 * width**3, bytes_accessed=10 * width * width, transcendentals=0),
         name="hop",
-    )(factor, half, *packed)
+    )(factors, half, *packed)
 
 
 def finish_kernel(arrived, factor_ref, own_ref, mine_ref, *refs):
@@ -300,7 +304,7 @@
 
 def pieces(steps):
     small = max(steps // 8, 1)
-    cuts = [0, small, 2 * small, (steps + 2 * small) // 2, steps]
+    cuts = [0, 2 * small, 4 * small, 6 * small, steps]
     return list(zip(cuts, cuts[1:]))[::-1]
 
 
@@ -321,8 +325,8 @@
         return jnp.asarray(table, jnp.int32)[place]
 
     ranges = pieces(steps)
-    *own, end = pack(place.reshape(1), gains, increments, terminal, count, ranges)
-    end = lax.all_gather(end, "tile")
+    own = pack(place.reshape(1), gains, increments, count, ranges)
+    end = lax.all_gather(terminal.astype(BF16), "tile", axis=0, tiled=True)
     arrived = []
     for turn, array in enumerate(own):
         way = 1 if turn % 2 == 0 else -1
@@ -339,10 +343,10 @@
     for turn, (low, high) in enumerate(ranges):
         places = origins(1 if turn % 2 == 0 else -1)
         state = compose(last, places, arrived[turn], end, state, low, high - low, steps)
-    factors, own, mine, factor, half = state
+    factors, own, mine, half = state
     packed = []
     for turn in range(blocks - 1, 0, -1):
-        packed.append(lax.ppermute(hop(factor, half, packed), "tm", [(turn, turn - 1)]))
+        packed.append(lax.ppermute(hop(factors, half, packed), "tm", [(turn, turn - 1)]))
     return finish(factors, own, mine, packed)
 
 

time: 291 us -> 254 us (0.87)
  blocking collectives: 35 us -> 0 us
  local copies, waits for them, and re-layouts: 40 us -> 20.5 us
  between operations: 0.22 us -> 13.6 us
    all_gather x1 -> x0, blocking collectives: 35 us -> none  [local(): end = lax.all_gather(end, 'tile')]
    unnamed x62 -> x52, local copies, waits for them, and re-layouts: 38.6 us -> 19.1 us
  transfers between devices with their start and end apart: 31 -> 32, of which waited for: 11 -> 14; matrix products, arithmetic and copies ran while one was open for 0% -> 1% of each run, Pallas kernels for 12% -> 13%
where the time goes in v7:
time: 254 us; the launch traced here: 253 us
  waiting for transfers between devices  133 us (52%)
  Pallas kernels  54.2 us (21%)
  starting transfers between devices  30.8 us (12%)
  local copies, waits for them, and re-layouts  20.5 us (8%)
  between operations  13.6 us (5%)
    ppermute x28, waiting for transfers between devices, passed(): lax.ppermute(array, 'tile', [(cycle[n], cycle[(n + way) % count]) for n i...  116 us
    pallas_call x4, Pallas kernels, compose(): pl.pallas_call(functools.partial(compose_kernel, count, first), grid_spec...  42.8 us
    ppermute x28, starting transfers between devices, passed(): lax.ppermute(array, 'tile', [(cycle[n], cycle[(n + way) % count]) for n i...  28.1 us
    unnamed x52, local copies, waits for them, and re-layouts  19.1 us
    ppermute x3, waiting for transfers between devices, local(): lax.ppermute(hop(factors, half, packed), 'tm', [(turn, turn - 1)])  17 us
    pallas_call x1, Pallas kernels, finish(): pl.pallas_call(functools.partial(finish_kernel, len(packed)), grid=(steps...  6.73 us
  transfers between devices with their start and end apart: 32, of which 14 were waited for; matrix products, arithmetic and copies ran while one was open for 1% of the time, Pallas kernels for 13%

profile of v7, /device:TPU:0, one launch (start us, length us, event | category | flops | bytes accessed | tf_op | source)
XLA Modules:
  0.0 252.8 jit_solution(15179012386662447753)
XLA Ops:
  6.5 1.7 copy-done
  8.2 1.3 copy-done.1
  10.2 3.0 %collective-permute-start.10 = (bf16[96,2560]{1,0:T(8,128)(2,1)S(1)}, bf16[96,2560]{1,0:T(8,128)(2,1)S(1)}, u32[]{:S(2)}, u32[]{:S(2)}) collective-permute-start(bf16[96,2560]{1,0:T(8,128)(2,1)S(1)} %get-tuple-element.33.refs_0_), channel_id=1, source_target_pairs={{1,3},{3,5},{5,7},{7,6},{6,4},{4,2},{2,0},{0,1},{9,11},{11,13},{13... | collective-permute-start | bytes 1474568 | tf_op jit(solution)/shard_map/ppermute | solution.py:321
  14.1 10.4 %collective-permute-done.10.refs_1_ = bf16[96,2560]{1,0:T(8,128)(2,1)S(1)} collective-permute-done((bf16[96,2560]{1,0:T(8,128)(2,1)S(1)}, bf16[96,2560]{1,0:T(8,128)(2,1)S(1)}, u32[]{:S(2)}, u32[]{:S(2)}) %collective-permute-start.10) | collective-permute-done | bytes 491552 | tf_op jit(solution)/shard_map/ppermute | solution.py:321
  24.5 1.7 collective-permute-start.11
  26.2 0.8 copy-done.9
  27.4 9.6 %collective-permute-done.11.refs_2_ = bf16[96,2560]{1,0:T(8,128)(2,1)S(1)} collective-permute-done((bf16[96,2560]{1,0:T(8,128)(2,1)S(1)}, bf16[96,2560]{1,0:T(8,128)(2,1)S(1)}, u32[]{:S(2)}, u32[]{:S(2)}) %collective-permute-start.11) | collective-permute-done | bytes 491552 | tf_op jit(solution)/shard_map/ppermute | solution.py:321
  36.9 1.4 collective-permute-start.12
  39.7 8.7 %collective-permute-done.12.refs_3_ = bf16[96,2560]{1,0:T(8,128)(2,1)S(1)} collective-permute-done((bf16[96,2560]{1,0:T(8,128)(2,1)S(1)}, bf16[96,2560]{1,0:T(8,128)(2,1)S(1)}, u32[]{:S(2)}, u32[]{:S(2)}) %collective-permute-start.12) | collective-permute-done | bytes 491552 | tf_op jit(solution)/shard_map/ppermute | solution.py:321
  49.2 1.0 collective-permute-start.13
  51.8 1.0 collective-permute-start.3
  52.7 7.9 %collective-permute-done.13.refs_1_ = bf16[96,2560]{1,0:T(8,128)(2,1)S(1)} collective-permute-done((bf16[96,2560]{1,0:T(8,128)(2,1)S(1)}, bf16[96,2560]{1,0:T(8,128)(2,1)S(1)}, u32[]{:S(2)}, u32[]{:S(2)}) %collective-permute-start.13) | collective-permute-done | bytes 491552 | tf_op jit(solution)/shard_map/ppermute | solution.py:321
  60.6 1.0 collective-permute-start.14
  61.6 1.6 collective-permute-start.24
  64.2 2.5 collective-permute-start.4
  66.7 11.3 %collective-permute-done.14.refs_2_ = bf16[96,2560]{1,0:T(8,128)(2,1)S(1)} collective-permute-done((bf16[96,2560]{1,0:T(8,128)(2,1)S(1)}, bf16[96,2560]{1,0:T(8,128)(2,1)S(1)}, u32[]{:S(2)}, u32[]{:S(2)}) %collective-permute-start.14) | collective-permute-done | bytes 491552 | tf_op jit(solution)/shard_map/ppermute | solution.py:321
  78.8 18.4 %collective-permute-done.24.refs_4_ = bf16[96,2560]{1,0:T(8,128)(2,1)S(1)} collective-permute-done((bf16[96,2560]{1,0:T(8,128)(2,1)}, bf16[96,2560]{1,0:T(8,128)(2,1)S(1)}, u32[]{:S(2)}, u32[]{:S(2)}) %collective-permute-start.24) | collective-permute-done | bytes 491552 | tf_op jit(solution)/shard_map/ppermute | solution.py:321
  97.2 0.8 copy-done.21
  98.1 2.0 collective-permute-start.21
  102.0 6.6 %collective-permute-done.15.refs_3_ = bf16[96,2560]{1,0:T(8,128)(2,1)S(1)} collective-permute-done((bf16[96,2560]{1,0:T(8,128)(2,1)S(1)}, bf16[96,2560]{1,0:T(8,128)(2,1)S(1)}, u32[]{:S(2)}, u32[]{:S(2)}) %collective-permute-start.15) | collective-permute-done | bytes 491552 | tf_op jit(solution)/shard_map/ppermute | solution.py:321
  108.6 0.8 copy-done.17
  109.4 9.7 %collective-permute-done.25.refs_5_ = bf16[96,2560]{1,0:T(8,128)(2,1)S(1)} collective-permute-done((bf16[96,2560]{1,0:T(8,128)(2,1)S(1)}, bf16[96,2560]{1,0:T(8,128)(2,1)S(1)}, u32[]{:S(2)}, u32[]{:S(2)}) %collective-permute-start.25) | collective-permute-done | bytes 491552 | tf_op jit(solution)/shard_map/ppermute | solution.py:321
  119.9 2.0 collective-permute-start.22
  121.9 1.5 collective-permute-start.6
  123.4 6.3 %collective-permute-done.16.refs_4_ = bf16[96,2560]{1,0:T(8,128)(2,1)} collective-permute-done((bf16[96,2560]{1,0:T(8,128)(2,1)S(1)}, bf16[96,2560]{1,0:T(8,128)(2,1)}, u32[]{:S(2)}, u32[]{:S(2)}) %collective-permute-start.16) | collective-permute-done | bytes 491552 | tf_op jit(solution)/shard_map/ppermute | solution.py:321
  129.7 10.5 %collective-permute-done.26.refs_6_ = bf16[96,2560]{1,0:T(8,128)(2,1)} collective-permute-done((bf16[96,2560]{1,0:T(8,128)(2,1)S(1)}, bf16[96,2560]{1,0:T(8,128)(2,1)}, u32[]{:S(2)}, u32[]{:S(2)}) %collective-permute-start.26) | collective-permute-done | bytes 491552 | tf_op jit(solution)/shard_map/ppermute | solution.py:321
  141.7 2.0 collective-permute-start.23
  143.7 1.5 collective-permute-start.7
  145.2 5.6 %collective-permute-done.17.refs_5_ = bf16[96,2560]{1,0:T(8,128)(2,1)} collective-permute-done((bf16[96,2560]{1,0:T(8,128)(2,1)}, bf16[96,2560]{1,0:T(8,128)(2,1)}, u32[]{:S(2)}, u32[]{:S(2)}) %collective-permute-start.17) | collective-permute-done | bytes 491552 | tf_op jit(solution)/shard_map/ppermute | solution.py:321
  150.8 10.5 %collective-permute-done.27.refs_7_ = bf16[96,2560]{1,0:T(8,128)(2,1)} collective-permute-done((bf16[96,2560]{1,0:T(8,128)(2,1)}, bf16[96,2560]{1,0:T(8,128)(2,1)}, u32[]{:S(2)}, u32[]{:S(2)}) %collective-permute-start.27) | collective-permute-done | bytes 491552 | tf_op jit(solution)/shard_map/ppermute | solution.py:321
  161.3 1.3 copy-done.2
  162.6 1.0 copy-done.4
  163.6 1.0 copy-done.10
  164.7 1.0 copy-done.14
  165.7 1.0 copy-done.16
  166.7 1.0 copy-done.22
  167.8 1.0 copy-done.24
  168.8 9.6 %compose.4 = (bf16[8,768,768]{2,1,0:T(8,128)(2,1)S(1)}, f32[8,96,768]{2,1,0:T(8,128)S(1)}, bf16[8,96,768]{2,1,0:T(8,128)(2,1)S(1)}, bf16[768,768]{1,0:T(8,128)(2,1)S(1)}) custom-call(s32[1]{0:T(128)} %bitcast.last_ref, s32[8]{0:T(128)S(1)} %dynamic-slice_bitcast_fusion.places_ref, bf16[96,2560]{1,0:T(8,128)(2,1)S(1)} %copy-done.4, ...), custom_call_target="tpu_custom_call" | custom-call | flops 5435817984 | bytes 9437184 | tf_op jit(solution)/shard_map/compose/pallas_call | solution.py:145
  178.4 1.6 collective-permute-start.8
  180.5 11.1 %compose.5 = (bf16[8,768,768]{2,1,0:T(8,128)(2,1)S(1)}, f32[8,96,768]{2,1,0:T(8,128)S(1)}, bf16[8,96,768]{2,1,0:T(8,128)(2,1)S(1)}, bf16[768,768]{1,0:T(8,128)(2,1)S(1)}) custom-call(s32[1]{0:T(128)} %bitcast.last_ref, s32[8]{0:T(128)S(1)} %dynamic-slice_bitcast_fusion.1.places_ref, ...), custom_call_target="tpu_custom_call", output_to_operand_aliasing={{0}: (11, {}), {1}: (12, {}), {2}: (13, {})} | custom-call | flops 5435817984 | bytes 9437184 | tf_op jit(solution)/shard_map/compose/pallas_call | solution.py:145
  191.6 1.8 collective-permute-start.9
  193.4 11.1 %compose.6 = (bf16[8,768,768]{2,1,0:T(8,128)(2,1)S(1)}, f32[8,96,768]{2,1,0:T(8,128)S(1)}, bf16[8,96,768]{2,1,0:T(8,128)(2,1)S(1)}, bf16[768,768]{1,0:T(8,128)(2,1)S(1)}) custom-call(s32[1]{0:T(128)} %bitcast.last_ref, s32[8]{0:T(128)S(1)} %dynamic-slice_bitcast_fusion.places_ref, ...), custom_call_target="tpu_custom_call", output_to_operand_aliasing={{0}: (11, {}), {1}: (12, {}), {2}: (13, {})} | custom-call | flops 5435817984 | bytes 9437184 | tf_op jit(solution)/shard_map/compose/pallas_call | solution.py:145
  204.5 11.0 %compose.7 = (bf16[8,768,768]{2,1,0:T(8,128)(2,1)S(1)}, f32[8,96,768]{2,1,0:T(8,128)S(1)}, bf16[8,96,768]{2,1,0:T(8,128)(2,1)S(1)}, bf16[768,768]{1,0:T(8,128)(2,1)S(1)}) custom-call(s32[1]{0:T(128)} %bitcast.last_ref, s32[8]{0:T(128)S(1)} %dynamic-slice_bitcast_fusion.1.places_ref, ...), custom_call_target="tpu_custom_call", output_to_operand_aliasing={{0}: (11, {}), {1}: (12, {}), {2}: (13, {})} | custom-call | flops 5435817984 | bytes 9437184 | tf_op jit(solution)/shard_map/compose/pallas_call | solution.py:145
  216.6 1.8 hop.2
  219.1 1.8 hop.3
  220.9 1.3 collective-permute-start.30
  222.2 17.0 %collective-permute-done.30.refs_2_ = bf16[6,256,256]{2,1,0:T(8,128)(2,1)S(1)} collective-permute-done((bf16[6,256,256]{2,1,0:T(8,128)(2,1)S(1)}, bf16[6,256,256]{2,1,0:T(8,128)(2,1)S(1)}, u32[]{:S(2)}, u32[]{:S(2)}) %collective-permute-start.30) | collective-permute-done | bytes 786464 | tf_op jit(solution)/shard_map/ppermute | solution.py:349
  239.2 6.7 %finish.1 = f32[8,96,768]{2,1,0:T(8,128)} custom-call(bf16[8,768,768]{2,1,0:T(8,128)(2,1)S(1)} %get-tuple-element.49.factor_ref, f32[8,96,768]{2,1,0:T(8,128)S(1)} %get-tuple-element.50.own_ref, bf16[8,96,768]{2,1,0:T(8,128)(2,1)S(1)} %get-tuple-element.51.mine_ref, bf16[6,256,256]{2,1,0:T(8,128)(2,1)S(1)} %collective-permute-done.28.refs_0_, ...), custom_call_target="tpu_custom_call" | custom-call | tf_op jit(solution)/shard_map/finish/pallas_call | solution.py:280
  (81 shorter events, 13.9 us)
Async XLA Ops:
  6.5 144.3 %all-gather.2.cloned.1.call-start = ((), (), s32[]{:S(2)}) async-start(), calls=%async_computation | async-start | bytes 1327104 | tf_op jit(solution)/shard_map/all_gather | solution.py:329
  6.5 1.7 copy-start
  8.2 1.3 copy-start.1
  9.5 40.8 %copy-start.25 = (f32[96,768]{1,0:T(8,128)S(1)}, f32[96,768]{1,0:T(8,128)}, u32[]{:S(2)}) copy-start(f32[96,768]{1,0:T(8,128)} %param.9) | copy-start | bytes 884740
  10.2 14.3 %collective-permute-start.10 = (bf16[96,2560]{1,0:T(8,128)(2,1)S(1)}, bf16[96,2560]{1,0:T(8,128)(2,1)S(1)}, u32[]{:S(2)}, u32[]{:S(2)}) collective-permute-start(bf16[96,2560]{1,0:T(8,128)(2,1)S(1)} %get-tuple-element.33.refs_0_), channel_id=1, source_target_pairs={{1,3},{3,5},{5,7},{7,6},{6,4},{4,2},{2,0},{0,1},{9,11},{11,13},{13... | collective-permute-start | bytes 1474568 | tf_op jit(solution)/shard_map/ppermute | solution.py:321
  14.0 13.0 %collective-permute-start = (bf16[96,2560]{1,0:T(8,128)(2,1)S(1)}, bf16[96,2560]{1,0:T(8,128)(2,1)S(1)}, u32[]{:S(2)}, u32[]{:S(2)}) collective-permute-start(bf16[96,2560]{1,0:T(8,128)(2,1)S(1)} %get-tuple-element.30.refs_0_), channel_id=1, source_target_pairs={{1,0},{3,1},{5,3},{7,5},{6,7},{4,6},{2,4},{0,2},{9,8},{11,9},{13,1... | collective-permute-start | bytes 1474568 | tf_op jit(solution)/shard_map/ppermute | solution.py:321
  24.5 12.4 %collective-permute-start.11 = (bf16[96,2560]{1,0:T(8,128)(2,1)S(1)}, bf16[96,2560]{1,0:T(8,128)(2,1)S(1)}, u32[]{:S(2)}, u32[]{:S(2)}) collective-permute-start(bf16[96,2560]{1,0:T(8,128)(2,1)S(1)} %collective-permute-done.10.refs_1_), channel_id=1, source_target_pairs={{1,3},{3,5},{5,7},{7,6},{6,4},{4,2},{2,0},{0,1},{9,11},{11,13},{13... | collective-permute-start | bytes 1474568 | tf_op jit(solution)/shard_map/ppermute | solution.py:321
  27.0 12.1 %collective-permute-start.1 = (bf16[96,2560]{1,0:T(8,128)(2,1)S(1)}, bf16[96,2560]{1,0:T(8,128)(2,1)S(1)}, u32[]{:S(2)}, u32[]{:S(2)}) collective-permute-start(bf16[96,2560]{1,0:T(8,128)(2,1)S(1)} %collective-permute-done.refs_1_), channel_id=1, source_target_pairs={{1,0},{3,1},{5,3},{7,5},{6,7},{4,6},{2,4},{0,2},{9,8},{11,9},{13,1... | collective-permute-start | bytes 1474568 | tf_op jit(solution)/shard_map/ppermute | solution.py:321
  36.9 11.5 %collective-permute-start.12 = (bf16[96,2560]{1,0:T(8,128)(2,1)S(1)}, bf16[96,2560]{1,0:T(8,128)(2,1)S(1)}, u32[]{:S(2)}, u32[]{:S(2)}) collective-permute-start(bf16[96,2560]{1,0:T(8,128)(2,1)S(1)} %collective-permute-done.11.refs_2_), channel_id=1, source_target_pairs={{1,3},{3,5},{5,7},{7,6},{6,4},{4,2},{2,0},{0,1},{9,11},{11,13},{13... | collective-permute-start | bytes 1474568 | tf_op jit(solution)/shard_map/ppermute | solution.py:321
  39.1 11.9 %collective-permute-start.2 = (bf16[96,2560]{1,0:T(8,128)(2,1)S(1)}, bf16[96,2560]{1,0:T(8,128)(2,1)S(1)}, u32[]{:S(2)}, u32[]{:S(2)}) collective-permute-start(bf16[96,2560]{1,0:T(8,128)(2,1)S(1)} %collective-permute-done.1.refs_2_), channel_id=1, source_target_pairs={{1,0},{3,1},{5,3},{7,5},{6,7},{4,6},{2,4},{0,2},{9,8},{11,9},{13,1... | collective-permute-start | bytes 1474568 | tf_op jit(solution)/shard_map/ppermute | solution.py:321
  49.2 11.4 %collective-permute-start.13 = (bf16[96,2560]{1,0:T(8,128)(2,1)S(1)}, bf16[96,2560]{1,0:T(8,128)(2,1)S(1)}, u32[]{:S(2)}, u32[]{:S(2)}) collective-permute-start(bf16[96,2560]{1,0:T(8,128)(2,1)S(1)} %get-tuple-element.34.refs_0_), channel_id=1, source_target_pairs={{1,3},{3,5},{5,7},{7,6},{6,4},{4,2},{2,0},{0,1},{9,11},{11,13},{13... | collective-permute-start | bytes 1474568 | tf_op jit(solution)/shard_map/ppermute | solution.py:321
  51.8 12.5 %collective-permute-start.3 = (bf16[96,2560]{1,0:T(8,128)(2,1)S(1)}, bf16[96,2560]{1,0:T(8,128)(2,1)S(1)}, u32[]{:S(2)}, u32[]{:S(2)}) collective-permute-start(bf16[96,2560]{1,0:T(8,128)(2,1)S(1)} %get-tuple-element.31.refs_0_), channel_id=1, source_target_pairs={{1,0},{3,1},{5,3},{7,5},{6,7},{4,6},{2,4},{0,2},{9,8},{11,9},{13,1... | collective-permute-start | bytes 1474568 | tf_op jit(solution)/shard_map/ppermute | solution.py:321
  60.6 17.4 %collective-permute-start.14 = (bf16[96,2560]{1,0:T(8,128)(2,1)S(1)}, bf16[96,2560]{1,0:T(8,128)(2,1)S(1)}, u32[]{:S(2)}, u32[]{:S(2)}) collective-permute-start(bf16[96,2560]{1,0:T(8,128)(2,1)S(1)} %collective-permute-done.13.refs_1_), channel_id=1, source_target_pairs={{1,3},{3,5},{5,7},{7,6},{6,4},{4,2},{2,0},{0,1},{9,11},{11,13},{13... | collective-permute-start | bytes 1474568 | tf_op jit(solution)/shard_map/ppermute | solution.py:321
  61.6 35.6 %collective-permute-start.24 = (bf16[96,2560]{1,0:T(8,128)(2,1)}, bf16[96,2560]{1,0:T(8,128)(2,1)S(1)}, u32[]{:S(2)}, u32[]{:S(2)}) collective-permute-start(bf16[96,2560]{1,0:T(8,128)(2,1)} %copy-done.15), channel_id=1, source_target_pairs={{1,3},{3,5},{5,7},{7,6},{6,4},{4,2},{2,0},{0,1},{9,11},{11,13},{13... | collective-permute-start | bytes 1474568 | tf_op jit(solution)/shard_map/ppermute | solution.py:321
  63.2 34.9 %collective-permute-start.20 = (bf16[96,2560]{1,0:T(8,128)(2,1)}, bf16[96,2560]{1,0:T(8,128)(2,1)S(1)}, u32[]{:S(2)}, u32[]{:S(2)}) collective-permute-start(bf16[96,2560]{1,0:T(8,128)(2,1)} %copy-done.7), channel_id=1, source_target_pairs={{1,0},{3,1},{5,3},{7,5},{6,7},{4,6},{2,4},{0,2},{9,8},{11,9},{13,1... | collective-permute-start | bytes 1474568 | tf_op jit(solution)/shard_map/ppermute | solution.py:321
  64.2 36.7 %collective-permute-start.4 = (bf16[96,2560]{1,0:T(8,128)(2,1)S(1)}, bf16[96,2560]{1,0:T(8,128)(2,1)S(1)}, u32[]{:S(2)}, u32[]{:S(2)}) collective-permute-start(bf16[96,2560]{1,0:T(8,128)(2,1)S(1)} %collective-permute-done.3.refs_1_), channel_id=1, source_target_pairs={{1,0},{3,1},{5,3},{7,5},{6,7},{4,6},{2,4},{0,2},{9,8},{11,9},{13,1... | collective-permute-start | bytes 1474568 | tf_op jit(solution)/shard_map/ppermute | solution.py:321
  78.0 30.5 %collective-permute-start.15 = (bf16[96,2560]{1,0:T(8,128)(2,1)S(1)}, bf16[96,2560]{1,0:T(8,128)(2,1)S(1)}, u32[]{:S(2)}, u32[]{:S(2)}) collective-permute-start(bf16[96,2560]{1,0:T(8,128)(2,1)S(1)} %collective-permute-done.14.refs_2_), channel_id=1, source_target_pairs={{1,3},{3,5},{5,7},{7,6},{6,4},{4,2},{2,0},{0,1},{9,11},{11,13},{13... | collective-permute-start | bytes 1474568 | tf_op jit(solution)/shard_map/ppermute | solution.py:321
  97.2 21.9 %collective-permute-start.25 = (bf16[96,2560]{1,0:T(8,128)(2,1)S(1)}, bf16[96,2560]{1,0:T(8,128)(2,1)S(1)}, u32[]{:S(2)}, u32[]{:S(2)}) collective-permute-start(bf16[96,2560]{1,0:T(8,128)(2,1)S(1)} %collective-permute-done.24.refs_4_), channel_id=1, source_target_pairs={{1,3},{3,5},{5,7},{7,6},{6,4},{4,2},{2,0},{0,1},{9,11},{11,13},{13... | collective-permute-start | bytes 1474568 | tf_op jit(solution)/shard_map/ppermute | solution.py:321
  97.2 0.8 copy-start.21
  98.1 21.8 %collective-permute-start.21 = (bf16[96,2560]{1,0:T(8,128)(2,1)S(1)}, bf16[96,2560]{1,0:T(8,128)(2,1)}, u32[]{:S(2)}, u32[]{:S(2)}) collective-permute-start(bf16[96,2560]{1,0:T(8,128)(2,1)S(1)} %collective-permute-done.20.refs_4_), channel_id=1, source_target_pairs={{1,0},{3,1},{5,3},{7,5},{6,7},{4,6},{2,4},{0,2},{9,8},{11,9},{13,1... | collective-permute-start | bytes 1474568 | tf_op jit(solution)/shard_map/ppermute | solution.py:321
  100.9 21.0 %collective-permute-start.5 = (bf16[96,2560]{1,0:T(8,128)(2,1)S(1)}, bf16[96,2560]{1,0:T(8,128)(2,1)}, u32[]{:S(2)}, u32[]{:S(2)}) collective-permute-start(bf16[96,2560]{1,0:T(8,128)(2,1)S(1)} %collective-permute-done.4.refs_2_), channel_id=1, source_target_pairs={{1,0},{3,1},{5,3},{7,5},{6,7},{4,6},{2,4},{0,2},{9,8},{11,9},{13,1... | collective-permute-start | bytes 1474568 | tf_op jit(solution)/shard_map/ppermute | solution.py:321
  108.6 21.2 %collective-permute-start.16 = (bf16[96,2560]{1,0:T(8,128)(2,1)S(1)}, bf16[96,2560]{1,0:T(8,128)(2,1)}, u32[]{:S(2)}, u32[]{:S(2)}) collective-permute-start(bf16[96,2560]{1,0:T(8,128)(2,1)S(1)} %collective-permute-done.15.refs_3_), channel_id=1, source_target_pairs={{1,3},{3,5},{5,7},{7,6},{6,4},{4,2},{2,0},{0,1},{9,11},{11,13},{13... | collective-permute-start | bytes 1474568 | tf_op jit(solution)/shard_map/ppermute | solution.py:321
  119.1 21.2 %collective-permute-start.26 = (bf16[96,2560]{1,0:T(8,128)(2,1)S(1)}, bf16[96,2560]{1,0:T(8,128)(2,1)}, u32[]{:S(2)}, u32[]{:S(2)}) collective-permute-start(bf16[96,2560]{1,0:T(8,128)(2,1)S(1)} %collective-permute-done.25.refs_5_), channel_id=1, source_target_pairs={{1,3},{3,5},{5,7},{7,6},{6,4},{4,2},{2,0},{0,1},{9,11},{11,13},{13... | collective-permute-start | bytes 1474568 | tf_op jit(solution)/shard_map/ppermute | solution.py:321
  119.9 21.8 %collective-permute-start.22 = (bf16[96,2560]{1,0:T(8,128)(2,1)}, bf16[96,2560]{1,0:T(8,128)(2,1)}, u32[]{:S(2)}, u32[]{:S(2)}) collective-permute-start(bf16[96,2560]{1,0:T(8,128)(2,1)} %collective-permute-done.21.refs_5_), channel_id=1, source_target_pairs={{1,0},{3,1},{5,3},{7,5},{6,7},{4,6},{2,4},{0,2},{9,8},{11,9},{13,1... | collective-permute-start | bytes 1474568 | tf_op jit(solution)/shard_map/ppermute | solution.py:321
  121.9 21.8 %collective-permute-start.6 = (bf16[96,2560]{1,0:T(8,128)(2,1)}, bf16[96,2560]{1,0:T(8,128)(2,1)}, u32[]{:S(2)}, u32[]{:S(2)}) collective-permute-start(bf16[96,2560]{1,0:T(8,128)(2,1)} %collective-permute-done.5.refs_3_), channel_id=1, source_target_pairs={{1,0},{3,1},{5,3},{7,5},{6,7},{4,6},{2,4},{0,2},{9,8},{11,9},{13,1... | collective-permute-start | bytes 1474568 | tf_op jit(solution)/shard_map/ppermute | solution.py:321
  129.7 21.1 %collective-permute-start.17 = (bf16[96,2560]{1,0:T(8,128)(2,1)}, bf16[96,2560]{1,0:T(8,128)(2,1)}, u32[]{:S(2)}, u32[]{:S(2)}) collective-permute-start(bf16[96,2560]{1,0:T(8,128)(2,1)} %collective-permute-done.16.refs_4_), channel_id=1, source_target_pairs={{1,3},{3,5},{5,7},{7,6},{6,4},{4,2},{2,0},{0,1},{9,11},{11,13},{13... | collective-permute-start | bytes 1474568 | tf_op jit(solution)/shard_map/ppermute | solution.py:321
  140.3 21.1 %collective-permute-start.27 = (bf16[96,2560]{1,0:T(8,128)(2,1)}, bf16[96,2560]{1,0:T(8,128)(2,1)}, u32[]{:S(2)}, u32[]{:S(2)}) collective-permute-start(bf16[96,2560]{1,0:T(8,128)(2,1)} %collective-permute-done.26.refs_6_), channel_id=1, source_target_pairs={{1,3},{3,5},{5,7},{7,6},{6,4},{4,2},{2,0},{0,1},{9,11},{11,13},{13... | collective-permute-start | bytes 1474568 | tf_op jit(solution)/shard_map/ppermute | solution.py:321
  141.7 38.8 %collective-permute-start.23 = (bf16[96,2560]{1,0:T(8,128)(2,1)}, bf16[96,2560]{1,0:T(8,128)(2,1)}, u32[]{:S(2)}, u32[]{:S(2)}) collective-permute-start(bf16[96,2560]{1,0:T(8,128)(2,1)} %collective-permute-done.22.refs_6_), channel_id=1, source_target_pairs={{1,0},{3,1},{5,3},{7,5},{6,7},{4,6},{2,4},{0,2},{9,8},{11,9},{13,1... | collective-permute-start | bytes 1474568 | tf_op jit(solution)/shard_map/ppermute | solution.py:321
  143.7 34.7 %collective-permute-start.7 = (bf16[96,2560]{1,0:T(8,128)(2,1)}, bf16[96,2560]{1,0:T(8,128)(2,1)}, u32[]{:S(2)}, u32[]{:S(2)}) collective-permute-start(bf16[96,2560]{1,0:T(8,128)(2,1)} %collective-permute-done.6.refs_4_), channel_id=1, source_target_pairs={{1,0},{3,1},{5,3},{7,5},{6,7},{4,6},{2,4},{0,2},{9,8},{11,9},{13,1... | collective-permute-start | bytes 1474568 | tf_op jit(solution)/shard_map/ppermute | solution.py:321
  150.8 29.2 %collective-permute-start.18 = (bf16[96,2560]{1,0:T(8,128)(2,1)}, bf16[96,2560]{1,0:T(8,128)(2,1)}, u32[]{:S(2)}, u32[]{:S(2)}) collective-permute-start(bf16[96,2560]{1,0:T(8,128)(2,1)} %collective-permute-done.17.refs_5_), channel_id=1, source_target_pairs={{1,3},{3,5},{5,7},{7,6},{6,4},{4,2},{2,0},{0,1},{9,11},{11,13},{13... | collective-permute-start | bytes 1474568 | tf_op jit(solution)/shard_map/ppermute | solution.py:321
  161.3 1.3 copy-start.2
  162.6 1.0 copy-start.4
  163.6 1.0 copy-start.10
  164.7 1.0 copy-start.14
  165.7 1.0 copy-start.16
  166.7 1.0 copy-start.22
  167.8 1.0 copy-start.24
  168.8 11.7 %copy-start.8 = (bf16[96,2560]{1,0:T(8,128)(2,1)S(1)}, bf16[96,2560]{1,0:T(8,128)(2,1)}, u32[]{:S(2)}) copy-start(bf16[96,2560]{1,0:T(8,128)(2,1)} %copy-done.7) | copy-start | bytes 1474564
  168.8 11.7 %copy-start.20 = (bf16[96,2560]{1,0:T(8,128)(2,1)S(1)}, bf16[96,2560]{1,0:T(8,128)(2,1)}, u32[]{:S(2)}) copy-start(bf16[96,2560]{1,0:T(8,128)(2,1)} %copy-done.19) | copy-start | bytes 1474564
  178.4 13.2 %collective-permute-start.8 = (bf16[96,2560]{1,0:T(8,128)(2,1)}, bf16[96,2560]{1,0:T(8,128)(2,1)S(1)}, u32[]{:S(2)}, u32[]{:S(2)}) collective-permute-start(bf16[96,2560]{1,0:T(8,128)(2,1)} %collective-permute-done.7.refs_5_), channel_id=1, source_target_pairs={{1,0},{3,1},{5,3},{7,5},{6,7},{4,6},{2,4},{0,2},{9,8},{11,9},{13,1... | collective-permute-start | bytes 1474568 | tf_op jit(solution)/shard_map/ppermute | solution.py:321
  180.0 13.4 %collective-permute-start.19 = (bf16[96,2560]{1,0:T(8,128)(2,1)}, bf16[96,2560]{1,0:T(8,128)(2,1)S(1)}, u32[]{:S(2)}, u32[]{:S(2)}) collective-permute-start(bf16[96,2560]{1,0:T(8,128)(2,1)} %collective-permute-done.18.refs_6_), channel_id=1, source_target_pairs={{1,3},{3,5},{5,7},{7,6},{6,4},{4,2},{2,0},{0,1},{9,11},{11,13},{13... | collective-permute-start | bytes 1474568 | tf_op jit(solution)/shard_map/ppermute | solution.py:321
  180.5 12.9 %copy-start.12 = (bf16[96,2560]{1,0:T(8,128)(2,1)S(1)}, bf16[96,2560]{1,0:T(8,128)(2,1)}, u32[]{:S(2)}) copy-start(bf16[96,2560]{1,0:T(8,128)(2,1)} %copy-done.11) | copy-start | bytes 1474564
  180.5 12.9 %copy-start.18 = (bf16[96,2560]{1,0:T(8,128)(2,1)S(1)}, bf16[96,2560]{1,0:T(8,128)(2,1)}, u32[]{:S(2)}) copy-start(bf16[96,2560]{1,0:T(8,128)(2,1)} %copy-done.17) | copy-start | bytes 1474564
  191.6 12.9 %collective-permute-start.9 = (bf16[96,2560]{1,0:T(8,128)(2,1)S(1)}, bf16[96,2560]{1,0:T(8,128)(2,1)S(1)}, u32[]{:S(2)}, u32[]{:S(2)}) collective-permute-start(bf16[96,2560]{1,0:T(8,128)(2,1)S(1)} %collective-permute-done.8.refs_6_), channel_id=1, source_target_pairs={{1,0},{3,1},{5,3},{7,5},{6,7},{4,6},{2,4},{0,2},{9,8},{11,9},{13,1... | collective-permute-start | bytes 1474568 | tf_op jit(solution)/shard_map/ppermute | solution.py:321
  193.4 11.1 %copy-start.6 = (bf16[96,2560]{1,0:T(8,128)(2,1)S(1)}, bf16[96,2560]{1,0:T(8,128)(2,1)}, u32[]{:S(2)}) copy-start(bf16[96,2560]{1,0:T(8,128)(2,1)} %copy-done.5) | copy-start | bytes 1474564
  215.9 0.7 collective-permute-start.28
  218.4 0.7 collective-permute-start.29
  220.9 18.3 %collective-permute-start.30 = (bf16[6,256,256]{2,1,0:T(8,128)(2,1)S(1)}, bf16[6,256,256]{2,1,0:T(8,128)(2,1)S(1)}, u32[]{:S(2)}, u32[]{:S(2)}) collective-permute-start(bf16[6,256,256]{2,1,0:T(8,128)(2,1)S(1)} %hop.3), channel_id=1, source_target_pairs={{8,0},{9,1},{10,2},{11,3},{12,4},{13,5},{14,6},{15,7}} | collective-permute-start | bytes 2359304 | tf_op jit(solution)/shard_map/ppermute | solution.py:349
  (10 other events, 7.9 us)
Sparse Core Ops, SparseCore 0:
  51.1 49.1 all-gather.1

commit v8 on v7

--- a/solution.py
+++ b/solution.py
@@ -69,78 +69,85 @@
     )(place, gains, increments)
 
 
-def compose_kernel(count, first, last_ref, places_ref, *refs):
-    blocks, refs = refs[:count], refs[count:]
-    if first:
-        end, refs = refs[0], refs[1:]
-    else:
-        half_in, factor_in, refs = refs[0], refs[1], refs[4:]
-    factor_out, own_out, mine_out, half_end, gain, factor, half, middle, total = refs
-    width = factor.shape[0]
-    rows = width // count
-    turn = pl.program_id(0)
-    starts = [pl.multiple_of(places_ref[n] * rows, 16) for n in range(count)]
+def assemble(starts, blocks, gain, fresh):
+    rows = blocks[0].shape[0]
+    width = gain.shape[0]
     for start, block in zip(starts, blocks):
         gain[pl.ds(start, rows), :] = block[:, :width]
-
-    @pl.when(turn == 0)
-    def _():
-        if first:
-            factor[...] = gain[...]
-            scale = jnp.where(last_ref[0] == 1, 0.5, 0.0)
-            half[...] = (end[...].astype(F32) * scale).astype(BF16)
-        else:
-            factor[...] = factor_in[0]
-            half[...] = half_in[...]
-
-    def extend():
-        for j in range(0, width, TILE):
-            cols = slice(j, j + TILE)
-            factor[:, cols] = jnp.dot(gain[...], factor[:, cols], preferred_element_type=F32).astype(BF16)
-
-    if first:
-        pl.when(turn > 0)(extend)
-    else:
-        extend()
+        fresh[pl.ds(start, rows), :] = unpacked_half(block[:, width:], start, width).astype(BF16)
+
+
+def advance(gain, half, fresh, middle):
+    width = half.shape[0]
     for j in range(0, width, TILE):
         cols = slice(j, j + TILE)
         middle[:, cols] = jnp.dot(gain[...], half[:, cols], preferred_element_type=F32).astype(BF16)
     for j in range(0, width, TILE):
-        total[:, j:j + TILE] = nt(middle[...], gain[j:j + TILE, :])
-    for start, block in zip(starts, blocks):
-        span = pl.ds(start, rows)
-        half[span, :] = (total[span, :] + unpacked_half(block[:, width:], start, width)).astype(BF16)
-
-    mine = starts[0]
-    picked = lax.broadcasted_iota(jnp.int32, (rows, width), 1) == mine + lax.broadcasted_iota(
-        jnp.int32, (rows, width), 0
+        cols = slice(j, j + TILE)
+        half[:, cols] = (nt(middle[...], gain[cols, :]) + fresh[:, cols].astype(F32)).astype(BF16)
+
+
+def extend(gain, factor):
+    for j in range(0, factor.shape[0], TILE):
+        cols = slice(j, j + TILE)
+        factor[:, cols] = jnp.dot(gain[...], factor[:, cols], preferred_element_type=F32).astype(BF16)
+
+
+def whole_rows(half, mine, rows):
+    picked = lax.broadcasted_iota(jnp.int32, (rows, half.shape[0]), 1) == mine + lax.broadcasted_iota(
+        jnp.int32, (rows, half.shape[0]), 0
     )
     own = half[pl.ds(mine, rows), :].astype(F32)
-    own_out[0] = own + nt(jnp.where(picked, 1.0, 0.0).astype(BF16), half[...])
-    mine_out[0] = factor[pl.ds(mine, rows), :]
+    return own + nt(jnp.where(picked, 1.0, 0.0).astype(BF16), half[...])
+
+
+def compose_kernel(count, first, last_ref, places_ref, *refs):
+    blocks, refs = refs[:count], refs[count:]
+    half_in, refs = refs[0], refs[1:]
+    if not first:
+        factor_in, refs = refs[0], refs[3:]
+    factor_out, own_out, mine_out, half, gain, factor, fresh, middle = refs
+    rows = blocks[0].shape[0]
+    starts = [pl.multiple_of(places_ref[n] * rows, 16) for n in range(count)]
+    assemble(starts, blocks, gain, fresh)
+
+    @pl.when(pl.program_id(0) == 0)
+    def _():
+        if first:
+            factor[...] = gain[...]
+            half[...] = (half_in[...].astype(F32) * jnp.where(last_ref[0] == 1, 0.5, 0.0)).astype(BF16)
+        else:
+            factor[...] = factor_in[0]
+            half[...] = half_in[...]
+
+    if first:
+        pl.when(pl.program_id(0) > 0)(lambda: extend(gain, factor))
+    else:
+        extend(gain, factor)
+    advance(gain, half, fresh, middle)
+    own_out[0] = whole_rows(half, starts[0], rows)
+    mine_out[0] = factor[pl.ds(starts[0], rows), :]
     factor_out[0] = factor[...]
 
-    @pl.when(turn == pl.num_programs(0) - 1)
-    def _():
-        half_end[...] = half[...]
-
-
-def compose(last, places, blocks, end, state, low, turns, steps):
+
+def square(width, place=None):
+    if place is None:
+        return pl.BlockSpec((width, width), lambda i, *p: (0, 0), pipeline_mode=pl.Buffered(1))
+    return pl.BlockSpec((1, width, width), lambda i, *p: (place(i), 0, 0))
+
+
+def compose(last, places, blocks, half, state, low, turns, steps):
     count = len(blocks)
     rows = blocks[0].shape[0]
     width = rows * count
     stride = width + half_width(rows, count)[1]
     first = state is None
-    whole = pl.BlockSpec((width, width), lambda i, *p: (0, 0))
     anywhere = pl.BlockSpec(memory_space=pl.ANY)
-    in_specs = [pl.BlockSpec((rows, stride), lambda i, *p: (0, turns - 1 - i))] * count
-    if first:
-        in_specs += [whole]
-        args = [*blocks, end]
-    else:
-        after = pl.BlockSpec((1, width, width), lambda i, *p: (low + turns, 0, 0))
-        in_specs += [whole, after, anywhere, anywhere]
-        args = [*blocks, state[3], state[0], state[1], state[2]]
+    in_specs = [pl.BlockSpec((rows, stride), lambda i, *p: (0, turns - 1 - i))] * count + [square(width)]
+    if not first:
+        after = pl.BlockSpec((1, width, width), lambda i, *p: (low + turns, 0, 0), pipeline_mode=pl.Buffered(1))
+        in_specs += [after, anywhere, anywhere]
+    band = pl.BlockSpec((1, rows, width), lambda i, *p: (low + turns - 1 - i, 0, 0))
     base = 2 + count + 1
     return pl.pallas_call(
         functools.partial(compose_kernel, count, first),
@@ -148,14 +155,8 @@
             num_scalar_prefetch=2,
             grid=(turns,),
             in_specs=in_specs,
-            out_specs=[
-                pl.BlockSpec((1, width, width), lambda i, *p: (low + turns - 1 - i, 0, 0)),
-                pl.BlockSpec((1, rows, width), lambda i, *p: (low + turns - 1 - i, 0, 0)),
-                pl.BlockSpec((1, rows, width), lambda i, *p: (low + turns - 1 - i, 0, 0)),
-                whole,
-            ],
-            scratch_shapes=[pltpu.VMEM((width, width), BF16) for _ in range(4)]
-            + [pltpu.VMEM((width, width), F32)],
+            out_specs=[square(width, lambda i: low + turns - 1 - i), band, band, square(width)],
+            scratch_shapes=[pltpu.VMEM((width, width), BF16) for _ in range(4)],
         ),
         out_shape=[
             jax.ShapeDtypeStruct((steps, width, width), BF16),
@@ -164,12 +165,134 @@
             jax.ShapeDtypeStruct((width, width), BF16),
         ],
         input_output_aliases={} if first else {base: 0, base + 1: 1, base + 2: 2},
-        compiler_params=pltpu.CompilerParams(vmem_limit_bytes=25 * MIB),
+        compiler_params=pltpu.CompilerParams(vmem_limit_bytes=18 * MIB),
         cost_estimate=pl.CostEstimate(
             flops=6 * turns * width**3, bytes_accessed=8 * turns * width * width, transcendentals=0
         ),
         name="compose",
-    )(last, places, *args)
+    )(last, places, *blocks, half, *(() if first else state))
+
+
+def chain_kernel(count, places_ref, *refs):
+    blocks, refs = refs[:count], refs[count:]
+    half_in, refs = refs[0], refs[-6:]
+    gain_out, half_out, gain, half, fresh, middle = refs
+    rows = blocks[0].shape[0]
+    starts = [pl.multiple_of(places_ref[n] * rows, 16) for n in range(count)]
+    assemble(starts, blocks, gain, fresh)
+
+    @pl.when(pl.program_id(0) == 0)
+    def _():
+        half[...] = half_in[...].reshape(half.shape)
+
+    gain_out[0] = gain[...]
+    advance(gain, half, fresh, middle)
+    half_out[0] = half[...]
+
+
+def chain(places, blocks, half, state, low, turns, steps):
+    count = len(blocks)
+    rows = blocks[0].shape[0]
+    width = rows * count
+    stride = width + half_width(rows, count)[1]
+    anywhere = pl.BlockSpec(memory_space=pl.ANY)
+    in_specs = [pl.BlockSpec((rows, stride), lambda i, *p: (0, turns - 1 - i))] * count
+    if state is None:
+        in_specs += [square(width)]
+        args = [half]
+    else:
+        in_specs += [
+            pl.BlockSpec((1, width, width), lambda i, *p: (low + turns, 0, 0), pipeline_mode=pl.Buffered(1)),
+            anywhere,
+        ]
+        args = [state[1], state[0]]
+    whole = square(width, lambda i: low + turns - 1 - i)
+    return pl.pallas_call(
+        functools.partial(chain_kernel, count),
+        grid_spec=pltpu.PrefetchScalarGridSpec(
+            num_scalar_prefetch=1,
+            grid=(turns,),
+            in_specs=in_specs,
+            out_specs=[whole, whole],
+            scratch_shapes=[pltpu.VMEM((width, width), BF16) for _ in range(4)],
+        ),
+        out_shape=[jax.ShapeDtypeStruct((steps, width, width), BF16)] * 2,
+        input_output_aliases={} if state is None else {1 + count + 1: 0, 1 + count: 1},
+        compiler_params=pltpu.CompilerParams(vmem_limit_bytes=18 * MIB),
+        cost_estimate=pl.CostEstimate(
+            flops=4 * turns * width**3, bytes_accessed=8 * turns * width * width, transcendentals=0
+        ),
+        name="chain",
+    )(places, *blocks, *args)
+
+
+def factors_kernel(place_ref, gain_ref, factor_in, mine_ref, factor_out, mine_out, factor):
+    del mine_ref
+    rows = mine_out.shape[1]
+
+    @pl.when(pl.program_id(0) == 0)
+    def _():
+        factor[...] = factor_in[0]
+
+    extend(gain_ref.at[0], factor)
+    mine_out[0] = factor[pl.ds(pl.multiple_of(place_ref[0] * rows, 16), rows), :]
+    factor_out[0] = factor[...]
+
+
+def extend_factors(place, gains, factors, mine):
+    turns, width, _ = gains.shape
+    steps, rows, _ = mine.shape
+    anywhere = pl.BlockSpec(memory_space=pl.ANY)
+    return pl.pallas_call(
+        factors_kernel,
+        grid_spec=pltpu.PrefetchScalarGridSpec(
+            num_scalar_prefetch=1,
+            grid=(turns,),
+            in_specs=[square(width, lambda i: turns - 1 - i), square(width, lambda i: turns), anywhere],
+            out_specs=[
+                square(width, lambda i: turns - 1 - i),
+                pl.BlockSpec((1, rows, width), lambda i, *p: (turns - 1 - i, 0, 0)),
+            ],
+            scratch_shapes=[pltpu.VMEM((width, width), BF16)],
+        ),
+        out_shape=[
+            jax.ShapeDtypeStruct((steps, width, width), BF16),
+            jax.ShapeDtypeStruct((steps, rows, width), BF16),
+        ],
+        input_output_aliases={2: 0, 3: 1},
+        compiler_params=pltpu.CompilerParams(vmem_limit_bytes=12 * MIB),
+        cost_estimate=pl.CostEstimate(
+            flops=2 * turns * width**3, bytes_accessed=4 * turns * width * width, transcendentals=0
+        ),
+        name="extend_factors",
+    )(place, gains, factors, mine)
+
+
+def rows_kernel(place_ref, half_ref, own_ref, own_out):
+    del own_ref
+    rows = own_out.shape[1]
+    own_out[0] = whole_rows(half_ref.at[0], pl.multiple_of(place_ref[0] * rows, 16), rows)
+
+
+def own_rows(place, halves, own):
+    turns, width, _ = halves.shape
+    steps, rows, _ = own.shape
+    return pl.pallas_call(
+        rows_kernel,
+        grid_spec=pltpu.PrefetchScalarGridSpec(
+            num_scalar_prefetch=1,
+            grid=(turns,),
+            in_specs=[square(width, lambda i: i), pl.BlockSpec(memory_space=pl.ANY)],
+            out_specs=pl.BlockSpec((1, rows, width), lambda i, *p: (i, 0, 0)),
+        ),
+        out_shape=jax.ShapeDtypeStruct((steps, rows, width), F32),
+        input_output_aliases={2: 0},
+        compiler_params=pltpu.CompilerParams(vmem_limit_bytes=8 * MIB),
+        cost_estimate=pl.CostEstimate(
+            flops=2 * turns * rows * width**2, bytes_accessed=2 * turns * width * width, transcendentals=0
+        ),
+        name="own_rows",
+    )(place, halves, own)
 
 
 def upper_blocks(width):
@@ -199,7 +322,7 @@
 
 
 def fold_kernel(half_ref, packed_ref):
-    fold(half_ref, packed_ref)
+    fold(half_ref.at[0], packed_ref)
 
 
 def hop_kernel(arrived, factor_ref, half_ref, *refs):
@@ -214,37 +337,36 @@
         ).astype(BF16)
     for j in range(0, width, TILE):
         cols = slice(j, j + TILE)
-        ahead[:, cols] = (nt(middle[...], factor_ref[0, cols, :]) + half_ref[:, cols].astype(F32)).astype(BF16)
+        ahead[:, cols] = (nt(middle[...], factor_ref[0, cols, :]) + half_ref[0, :, cols].astype(F32)).astype(BF16)
     fold(ahead, out_ref)
 
 
-def hop(factors, half, packed):
-    width = half.shape[0]
+def hop(factors, halves, packed):
+    width = halves.shape[1]
     shape = (len(upper_blocks(width)), TILE, TILE)
-    square = pltpu.VMEM((width, width), BF16)
+    blocks = pl.BlockSpec(shape, lambda i: (0, 0, 0), pipeline_mode=pl.Buffered(1))
+    whole = pl.BlockSpec((1, width, width), lambda i: (0, 0, 0), pipeline_mode=pl.Buffered(1))
     if not packed:
         return pl.pallas_call(
             fold_kernel,
+            grid=(1,),
+            in_specs=[whole],
+            out_specs=blocks,
             out_shape=jax.ShapeDtypeStruct(shape, BF16),
-            compiler_params=pltpu.CompilerParams(vmem_limit_bytes=12 * MIB),
+            compiler_params=pltpu.CompilerParams(vmem_limit_bytes=8 * MIB),
             name="fold",
-        )(half)
-    blocks = pl.BlockSpec(shape, lambda i: (0, 0, 0))
+        )(halves)
     return pl.pallas_call(
         functools.partial(hop_kernel, len(packed)),
         grid=(1,),
-        in_specs=[
-            pl.BlockSpec((1, width, width), lambda i: (0, 0, 0)),
-            pl.BlockSpec((width, width), lambda i: (0, 0)),
-        ]
-        + [blocks] * len(packed),
+        in_specs=[whole, whole] + [blocks] * len(packed),
         out_specs=blocks,
         out_shape=jax.ShapeDtypeStruct(shape, BF16),
-        scratch_shapes=[square, square, square],
-        compiler_params=pltpu.CompilerParams(vmem_limit_bytes=20 * MIB),
+        scratch_shapes=[pltpu.VMEM((width, width), BF16)] * 3,
+        compiler_params=pltpu.CompilerParams(vmem_limit_bytes=16 * MIB),
         cost_estimate=pl.CostEstimate(flops=4 * width**3, bytes_accessed=10 * width * width, transcendentals=0),
         name="hop",
-    )(factors, half, *packed)
+    )(factors, halves, *packed)
 
 
 def finish_kernel(arrived, factor_ref, own_ref, mine_ref, *refs):
@@ -276,20 +398,20 @@
 
 def finish(factors, own, mine, packed):
     steps, rows, width = own.shape
-    whole = pl.BlockSpec(packed[0].shape, lambda i: (0, 0, 0))
+    whole = pl.BlockSpec(packed[0].shape, lambda i: (0, 0, 0), pipeline_mode=pl.Buffered(1))
     return pl.pallas_call(
         functools.partial(finish_kernel, len(packed)),
         grid=(steps,),
         in_specs=[
             pl.BlockSpec((1, width, width), lambda i: (i, 0, 0)),
             pl.BlockSpec((1, rows, width), lambda i: (i, 0, 0)),
-            pl.BlockSpec(mine.shape, lambda i: (0, 0, 0)),
+            pl.BlockSpec(mine.shape, lambda i: (0, 0, 0), pipeline_mode=pl.Buffered(1)),
         ]
         + [whole] * len(packed),
         out_specs=pl.BlockSpec((1, rows, width), lambda i: (i, 0, 0)),
         scratch_shapes=[pltpu.VMEM((width, width), BF16), pltpu.VMEM((steps * rows, width), BF16)],
         out_shape=jax.ShapeDtypeStruct((steps, rows, width), F32),
-        compiler_params=pltpu.CompilerParams(vmem_limit_bytes=24 * MIB),
+        compiler_params=pltpu.CompilerParams(vmem_limit_bytes=20 * MIB),
         name="finish",
     )(factors, own, mine, *packed)
 
@@ -326,7 +448,8 @@
 
     ranges = pieces(steps)
     own = pack(place.reshape(1), gains, increments, count, ranges)
-    end = lax.all_gather(terminal.astype(BF16), "tile", axis=0, tiled=True)
+    own, end = lax.optimization_barrier((own, terminal.astype(BF16)))
+    end = lax.all_gather(end, "tile", axis=0, tiled=True)
     arrived = []
     for turn, array in enumerate(own):
         way = 1 if turn % 2 == 0 else -1
@@ -335,18 +458,28 @@
             array, before[GATE] = lax.optimization_barrier((array, before[GATE]))
             for hop_count in range(GATE + 1, count):
                 before[hop_count] = passed(before[hop_count - 1], way)
+                if hop_count == GATE + 1:
+                    before[hop_count], end = lax.optimization_barrier((before[hop_count], end))
         found = [array]
         for hop_count in range(1, count):
             found.append(passed(found[-1], way))
         arrived.append(found)
-    state = None
-    for turn, (low, high) in enumerate(ranges):
-        places = origins(1 if turn % 2 == 0 else -1)
-        state = compose(last, places, arrived[turn], end, state, low, high - low, steps)
-    factors, own, mine, half = state
+    state, half = None, end
+    for turn in range(2):
+        reached = count - 3 + turn
+        blocks_here, _ = lax.optimization_barrier((arrived[turn], (arrived[2][reached], arrived[3][reached])))
+        low, high = ranges[turn]
+        *state, half = compose(last, origins(1 - 2 * turn), blocks_here, half, state, low, high - low, steps)
+    factors, own, mine = state
+    early = None
+    for turn in range(2, 4):
+        low, high = ranges[turn]
+        early = chain(origins(5 - 2 * turn), arrived[turn], half, early, low, high - low, ranges[2][1])
+    factors, mine = extend_factors(place.reshape(1), early[0], factors, mine)
+    own = own_rows(place.reshape(1), early[1], own)
     packed = []
     for turn in range(blocks - 1, 0, -1):
-        packed.append(lax.ppermute(hop(factors, half, packed), "tm", [(turn, turn - 1)]))
+        packed.append(lax.ppermute(hop(factors, early[1], packed), "tm", [(turn, turn - 1)]))
     return finish(factors, own, mine, packed)
 
 

time: 254 us -> 245 us (0.965)
  local copies, waits for them, and re-layouts: 20.5 us -> 14.6 us
  starting transfers between devices: 30.8 us -> 26.1 us
  waiting for transfers between devices: 133 us -> 136 us
    pallas_call x4 -> x2, Pallas kernels: 42.8 us -> 19.8 us  [compose(): pl.pallas_call(functools.partial(compose_kernel, count, first), grid_spec...]
    pallas_call x1 -> x5, Pallas kernels: 0.3 us -> 22.1 us  [the longest x2 15.1 us: chain(): pl.pallas_call(functools.partial(chain_kernel, count), grid_spec=pltpu.Pr...]
    ppermute x28, waiting for transfers between devices: 116 us -> 124 us  [passed(): lax.ppermute(array, 'tile', [(cycle[n], cycle[(n + way) % count]) for n i...]
    unnamed x52 -> x30, local copies, waits for them, and re-layouts: 19.1 us -> 13.2 us
    ppermute x3, waiting for transfers between devices: 17 us -> 11.4 us  [local(): lax.ppermute(hop(factors, early[1], packed), 'tm', [(turn, turn - 1)])]
    ppermute x28, starting transfers between devices: 28.1 us -> 23.1 us  [passed(): lax.ppermute(array, 'tile', [(cycle[n], cycle[(n + way) % count]) for n i...]
  transfers between devices with their start and end apart: 32 -> 32, of which waited for: 14 -> 13; matrix products, arithmetic and copies ran while one was open for 1% -> 1% of each run, Pallas kernels for 13% -> 14%
where the time goes in v8:
time: 245 us; the launch traced here: 244 us
  waiting for transfers between devices  136 us (56%)
  Pallas kernels  53 us (22%)
  starting transfers between devices  26.1 us (11%)
  local copies, waits for them, and re-layouts  14.6 us (6%)
  between operations  13.6 us (6%)
    ppermute x28, waiting for transfers between devices, passed(): lax.ppermute(array, 'tile', [(cycle[n], cycle[(n + way) % count]) for n i...  124 us
    ppermute x28, starting transfers between devices, passed(): lax.ppermute(array, 'tile', [(cycle[n], cycle[(n + way) % count]) for n i...  23.1 us
    pallas_call x2, Pallas kernels, compose(): pl.pallas_call(functools.partial(compose_kernel, count, first), grid_spec...  19.8 us
    pallas_call x2, Pallas kernels, chain(): pl.pallas_call(functools.partial(chain_kernel, count), grid_spec=pltpu.Pr...  15.1 us
    unnamed x30, local copies, waits for them, and re-layouts  13.2 us
    ppermute x3, waiting for transfers between devices, local(): lax.ppermute(hop(factors, early[1], packed), 'tm', [(turn, turn - 1)])  11.4 us
    pallas_call x1, Pallas kernels, finish(): pl.pallas_call(functools.partial(finish_kernel, len(packed)), grid=(steps...  6.76 us
  transfers between devices with their start and end apart: 32, of which 13 were waited for; matrix products, arithmetic and copies ran while one was open for 1% of the time, Pallas kernels for 14%

profile of v8, /device:TPU:0, one launch (start us, length us, event | category | flops | bytes accessed | tf_op | source)
XLA Modules:
  0.0 244.5 jit_solution(15981187530217147026)
XLA Ops:
  6.5 1.6 convert_element_type.4
  8.2 1.7 copy-done
  9.8 1.3 copy-done.1
  11.9 3.0 %collective-permute-start.10 = (bf16[96,2560]{1,0:T(8,128)(2,1)S(1)}, bf16[96,2560]{1,0:T(8,128)(2,1)S(1)}, u32[]{:S(2)}, u32[]{:S(2)}) collective-permute-start(bf16[96,2560]{1,0:T(8,128)(2,1)S(1)} %get-tuple-element.76.refs_0_), channel_id=1, source_target_pairs={{1,3},{3,5},{5,7},{7,6},{6,4},{4,2},{2,0},{0,1},{9,11},{11,13},{13... | collective-permute-start | bytes 1474568 | tf_op jit(solution)/shard_map/ppermute | solution.py:443
  15.1 11.1 %collective-permute-done.10.refs_1_ = bf16[96,2560]{1,0:T(8,128)(2,1)S(1)} collective-permute-done((bf16[96,2560]{1,0:T(8,128)(2,1)S(1)}, bf16[96,2560]{1,0:T(8,128)(2,1)S(1)}, u32[]{:S(2)}, u32[]{:S(2)}) %collective-permute-start.10) | collective-permute-done | bytes 491552 | tf_op jit(solution)/shard_map/ppermute | solution.py:443
  26.2 1.7 collective-permute-start.11
  27.9 0.8 copy-done.3
  29.0 13.9 %collective-permute-done.11.refs_2_ = bf16[96,2560]{1,0:T(8,128)(2,1)S(1)} collective-permute-done((bf16[96,2560]{1,0:T(8,128)(2,1)S(1)}, bf16[96,2560]{1,0:T(8,128)(2,1)S(1)}, u32[]{:S(2)}, u32[]{:S(2)}) %collective-permute-start.11) | collective-permute-done | bytes 491552 | tf_op jit(solution)/shard_map/ppermute | solution.py:443
  42.9 0.8 copy-done.5
  43.7 2.0 collective-permute-start.2
  45.7 19.2 %collective-permute-done.12.refs_3_ = bf16[96,2560]{1,0:T(8,128)(2,1)S(1)} collective-permute-done((bf16[96,2560]{1,0:T(8,128)(2,1)S(1)}, bf16[96,2560]{1,0:T(8,128)(2,1)S(1)}, u32[]{:S(2)}, u32[]{:S(2)}) %collective-permute-start.12) | collective-permute-done | bytes 491552 | tf_op jit(solution)/shard_map/ppermute | solution.py:443
  64.9 2.0 collective-permute-start.3
  66.9 0.8 copy-done.7
  67.8 11.4 %collective-permute-done.13.refs_1_ = bf16[96,2560]{1,0:T(8,128)(2,1)} collective-permute-done((bf16[96,2560]{1,0:T(8,128)(2,1)S(1)}, bf16[96,2560]{1,0:T(8,128)(2,1)}, u32[]{:S(2)}, u32[]{:S(2)}) %collective-permute-start.13) | collective-permute-done | bytes 491552 | tf_op jit(solution)/shard_map/ppermute | solution.py:443
  79.2 2.0 collective-permute-start.4
  81.6 8.1 %collective-permute-done.21.refs_4_ = bf16[96,2560]{1,0:T(8,128)(2,1)} collective-permute-done((bf16[96,2560]{1,0:T(8,128)(2,1)S(1)}, bf16[96,2560]{1,0:T(8,128)(2,1)}, u32[]{:S(2)}, u32[]{:S(2)}) %collective-permute-start.21) | collective-permute-done | bytes 491552 | tf_op jit(solution)/shard_map/ppermute | solution.py:443
  89.7 10.5 %collective-permute-done.14.refs_2_ = bf16[96,2560]{1,0:T(8,128)(2,1)} collective-permute-done((bf16[96,2560]{1,0:T(8,128)(2,1)}, bf16[96,2560]{1,0:T(8,128)(2,1)}, u32[]{:S(2)}, u32[]{:S(2)}) %collective-permute-start.14) | collective-permute-done | bytes 491552 | tf_op jit(solution)/shard_map/ppermute | solution.py:443
  100.2 2.0 collective-permute-start.5
  102.7 8.0 %collective-permute-done.25.refs_5_ = bf16[96,2560]{1,0:T(8,128)(2,1)S(1)} collective-permute-done((bf16[96,2560]{1,0:T(8,128)(2,1)}, bf16[96,2560]{1,0:T(8,128)(2,1)S(1)}, u32[]{:S(2)}, u32[]{:S(2)}) %collective-permute-start.25) | collective-permute-done | bytes 491552 | tf_op jit(solution)/shard_map/ppermute | solution.py:443
  110.7 0.8 copy-done.13
  111.5 9.7 %collective-permute-done.15.refs_3_ = bf16[96,2560]{1,0:T(8,128)(2,1)S(1)} collective-permute-done((bf16[96,2560]{1,0:T(8,128)(2,1)}, bf16[96,2560]{1,0:T(8,128)(2,1)S(1)}, u32[]{:S(2)}, u32[]{:S(2)}) %collective-permute-start.15) | collective-permute-done | bytes 491552 | tf_op jit(solution)/shard_map/ppermute | solution.py:443
  121.2 0.8 copy-done.11
  122.0 2.0 collective-permute-start.6
  124.0 0.8 copy-done.9
  125.2 6.6 %collective-permute-done.26.refs_6_ = bf16[96,2560]{1,0:T(8,128)(2,1)} collective-permute-done((bf16[96,2560]{1,0:T(8,128)(2,1)S(1)}, bf16[96,2560]{1,0:T(8,128)(2,1)}, u32[]{:S(2)}, u32[]{:S(2)}) %collective-permute-start.26) | collective-permute-done | bytes 491552 | tf_op jit(solution)/shard_map/ppermute | solution.py:443
  131.8 10.5 %collective-permute-done.16.refs_4_ = bf16[96,2560]{1,0:T(8,128)(2,1)} collective-permute-done((bf16[96,2560]{1,0:T(8,128)(2,1)S(1)}, bf16[96,2560]{1,0:T(8,128)(2,1)}, u32[]{:S(2)}, u32[]{:S(2)}) %collective-permute-start.16) | collective-permute-done | bytes 491552 | tf_op jit(solution)/shard_map/ppermute | solution.py:443
  142.4 2.0 collective-permute-start.7
  146.2 6.7 %collective-permute-done.27.refs_7_ = bf16[96,2560]{1,0:T(8,128)(2,1)} collective-permute-done((bf16[96,2560]{1,0:T(8,128)(2,1)}, bf16[96,2560]{1,0:T(8,128)(2,1)}, u32[]{:S(2)}, u32[]{:S(2)}) %collective-permute-start.27) | collective-permute-done | bytes 491552 | tf_op jit(solution)/shard_map/ppermute | solution.py:443
  152.9 8.5 %collective-permute-done.17.refs_5_ = bf16[96,2560]{1,0:T(8,128)(2,1)} collective-permute-done((bf16[96,2560]{1,0:T(8,128)(2,1)}, bf16[96,2560]{1,0:T(8,128)(2,1)}, u32[]{:S(2)}, u32[]{:S(2)}) %collective-permute-start.17) | collective-permute-done | bytes 491552 | tf_op jit(solution)/shard_map/ppermute | solution.py:443
  161.7 1.7 collective-permute-start.8
  163.4 1.3 copy-done.2
  164.7 1.0 copy-done.4
  165.7 1.0 copy-done.6
  166.8 1.0 copy-done.8
  167.8 1.0 copy-done.14
  168.8 9.1 %compose.2 = (bf16[8,768,768]{2,1,0:T(8,128)(2,1)S(1)}, f32[8,96,768]{2,1,0:T(8,128)S(1)}, bf16[8,96,768]{2,1,0:T(8,128)(2,1)S(1)}, bf16[768,768]{1,0:T(8,128)(2,1)S(1)}) custom-call(s32[1]{0:T(128)} %bitcast.3.last_ref, s32[8]{0:T(128)S(1)} %dynamic-slice_bitcast_fusion.places_ref, bf16[96,2560]{1,0:T(8,128)(2,1)S(1)} %get-tuple-element.76.refs_0_, ...), custom_call_target="tpu_custom_call" | custom-call | flops 5435817984 | bytes 9437184 | tf_op jit(solution)/shard_map/compose/pallas_call | solution.py:152
  178.3 1.7 collective-permute-start.9
  180.1 10.6 %compose.3 = (bf16[8,768,768]{2,1,0:T(8,128)(2,1)S(1)}, f32[8,96,768]{2,1,0:T(8,128)S(1)}, bf16[8,96,768]{2,1,0:T(8,128)(2,1)S(1)}, bf16[768,768]{1,0:T(8,128)(2,1)S(1)}) custom-call(s32[1]{0:T(128)} %bitcast.3.last_ref, s32[8]{0:T(128)S(1)} %dynamic-slice_bitcast_fusion.1.places_ref, ...), custom_call_target="tpu_custom_call", output_to_operand_aliasing={{0}: (11, {}), {1}: (12, {}), {2}: (13, {})} | custom-call | flops 5435817984 | bytes 9437184 | tf_op jit(solution)/shard_map/compose/pallas_call | solution.py:152
  190.7 7.6 %chain.2 = (bf16[4,768,768]{2,1,0:T(8,128)(2,1)S(1)}, bf16[4,768,768]{2,1,0:T(8,128)(2,1)S(1)}) custom-call(s32[8]{0:T(128)S(1)} %dynamic-slice_bitcast_fusion.places_ref, bf16[96,2560]{1,0:T(8,128)(2,1)S(1)} %get-tuple-element.61.refs_0_, bf16[96,2560]{1,0:T(8,128)(2,1)} %collective-permute-done.13.refs_1_, ...), custom_call_target="tpu_custom_call" | custom-call | flops 3623878656 | bytes 9437184 | tf_op jit(solution)/shard_map/chain/pallas_call | solution.py:210
  198.4 7.5 %chain.3 = (bf16[4,768,768]{2,1,0:T(8,128)(2,1)S(1)}, bf16[4,768,768]{2,1,0:T(8,128)(2,1)S(1)}) custom-call(s32[8]{0:T(128)S(1)} %dynamic-slice_bitcast_fusion.1.places_ref, bf16[96,2560]{1,0:T(8,128)(2,1)S(1)} %get-tuple-element.58.refs_0_, bf16[96,2560]{1,0:T(8,128)(2,1)S(1)} %collective-permute-done.3.refs_1_, ...), custom_call_target="tpu_custom_call", output_to_operand_aliasing={{0}: (10, {}), {1}: (9, {})} | custom-call | flops 3623878656 | bytes 9437184 | tf_op jit(solution)/shard_map/chain/pallas_call | solution.py:210
  206.9 4.5 %extend_factors.1 = (bf16[8,768,768]{2,1,0:T(8,128)(2,1)S(1)}, bf16[8,96,768]{2,1,0:T(8,128)(2,1)S(1)}) custom-call(s32[1]{0:T(128)} %bitcast.place_ref, bf16[4,768,768]{2,1,0:T(8,128)(2,1)S(1)} %get-tuple-element.92.gain_ref, bf16[8,768,768]{2,1,0:T(8,128)(2,1)S(1)} %get-tuple-element.93.factor_in, ...), custom_call_target="tpu_custom_call", output_to_operand_aliasing={{0}: (2, {}), {1}: (3, {})} | custom-call | flops 3623878656 | bytes 9437184 | tf_op jit(solution)/shard_map/extend_factors/pallas_call | solution.py:246
  211.5 1.8 hop.2
  213.3 0.9 collective-permute-start.29
  214.2 1.8 hop.3
  216.1 1.3 collective-permute-start.30
  217.4 2.1 own_rows.1.own_ref
  219.5 11.4 %collective-permute-done.30.refs_2_ = bf16[6,256,256]{2,1,0:T(8,128)(2,1)S(1)} collective-permute-done((bf16[6,256,256]{2,1,0:T(8,128)(2,1)S(1)}, bf16[6,256,256]{2,1,0:T(8,128)(2,1)S(1)}, u32[]{:S(2)}, u32[]{:S(2)}) %collective-permute-start.30) | collective-permute-done | bytes 786464 | tf_op jit(solution)/shard_map/ppermute | solution.py:482
  230.9 6.8 %finish.1 = f32[8,96,768]{2,1,0:T(8,128)} custom-call(bf16[8,768,768]{2,1,0:T(8,128)(2,1)S(1)} %get-tuple-element.95.factor_ref, f32[8,96,768]{2,1,0:T(8,128)S(1)} %own_rows.1.own_ref, bf16[8,96,768]{2,1,0:T(8,128)(2,1)S(1)} %get-tuple-element.98.mine_ref, bf16[6,256,256]{2,1,0:T(8,128)(2,1)S(1)} %collective-permute-done.28.refs_0_, ...), custom_call_target="tpu_custom_call" | custom-call | tf_op jit(solution)/shard_map/finish/pallas_call | solution.py:402
  (61 shorter events, 6.0 us)
Async XLA Ops:
  6.5 83.2 %all-gather.2.cloned.1.call-start = ((), (), s32[]{:S(2)}) async-start(), calls=%async_computation | async-start | bytes 1327104 | tf_op jit(solution)/shard_map/all_gather | solution.py:452
  8.2 1.7 copy-start
  9.8 1.3 copy-start.1
  11.9 14.3 %collective-permute-start.10 = (bf16[96,2560]{1,0:T(8,128)(2,1)S(1)}, bf16[96,2560]{1,0:T(8,128)(2,1)S(1)}, u32[]{:S(2)}, u32[]{:S(2)}) collective-permute-start(bf16[96,2560]{1,0:T(8,128)(2,1)S(1)} %get-tuple-element.76.refs_0_), channel_id=1, source_target_pairs={{1,3},{3,5},{5,7},{7,6},{6,4},{4,2},{2,0},{0,1},{9,11},{11,13},{13... | collective-permute-start | bytes 1474568 | tf_op jit(solution)/shard_map/ppermute | solution.py:443
  14.9 13.8 %collective-permute-start = (bf16[96,2560]{1,0:T(8,128)(2,1)S(1)}, bf16[96,2560]{1,0:T(8,128)(2,1)S(1)}, u32[]{:S(2)}, u32[]{:S(2)}) collective-permute-start(bf16[96,2560]{1,0:T(8,128)(2,1)S(1)} %get-tuple-element.67.refs_0_), channel_id=1, source_target_pairs={{1,0},{3,1},{5,3},{7,5},{6,7},{4,6},{2,4},{0,2},{9,8},{11,9},{13,1... | collective-permute-start | bytes 1474568 | tf_op jit(solution)/shard_map/ppermute | solution.py:443
  26.2 16.7 %collective-permute-start.11 = (bf16[96,2560]{1,0:T(8,128)(2,1)S(1)}, bf16[96,2560]{1,0:T(8,128)(2,1)S(1)}, u32[]{:S(2)}, u32[]{:S(2)}) collective-permute-start(bf16[96,2560]{1,0:T(8,128)(2,1)S(1)} %collective-permute-done.10.refs_1_), channel_id=1, source_target_pairs={{1,3},{3,5},{5,7},{7,6},{6,4},{4,2},{2,0},{0,1},{9,11},{11,13},{13... | collective-permute-start | bytes 1474568 | tf_op jit(solution)/shard_map/ppermute | solution.py:443
  27.9 0.8 copy-start.3
  28.7 15.0 %collective-permute-start.1 = (bf16[96,2560]{1,0:T(8,128)(2,1)S(1)}, bf16[96,2560]{1,0:T(8,128)(2,1)S(1)}, u32[]{:S(2)}, u32[]{:S(2)}) collective-permute-start(bf16[96,2560]{1,0:T(8,128)(2,1)S(1)} %collective-permute-done.refs_1_), channel_id=1, source_target_pairs={{1,0},{3,1},{5,3},{7,5},{6,7},{4,6},{2,4},{0,2},{9,8},{11,9},{13,1... | collective-permute-start | bytes 1474568 | tf_op jit(solution)/shard_map/ppermute | solution.py:443
  42.9 22.0 %collective-permute-start.12 = (bf16[96,2560]{1,0:T(8,128)(2,1)S(1)}, bf16[96,2560]{1,0:T(8,128)(2,1)S(1)}, u32[]{:S(2)}, u32[]{:S(2)}) collective-permute-start(bf16[96,2560]{1,0:T(8,128)(2,1)S(1)} %collective-permute-done.11.refs_2_), channel_id=1, source_target_pairs={{1,3},{3,5},{5,7},{7,6},{6,4},{4,2},{2,0},{0,1},{9,11},{11,13},{13... | collective-permute-start | bytes 1474568 | tf_op jit(solution)/shard_map/ppermute | solution.py:443
  42.9 0.8 copy-start.5
  43.7 21.2 %collective-permute-start.2 = (bf16[96,2560]{1,0:T(8,128)(2,1)S(1)}, bf16[96,2560]{1,0:T(8,128)(2,1)}, u32[]{:S(2)}, u32[]{:S(2)}) collective-permute-start(bf16[96,2560]{1,0:T(8,128)(2,1)S(1)} %collective-permute-done.1.refs_2_), channel_id=1, source_target_pairs={{1,0},{3,1},{5,3},{7,5},{6,7},{4,6},{2,4},{0,2},{9,8},{11,9},{13,1... | collective-permute-start | bytes 1474568 | tf_op jit(solution)/shard_map/ppermute | solution.py:443
  64.9 14.3 %collective-permute-start.13 = (bf16[96,2560]{1,0:T(8,128)(2,1)S(1)}, bf16[96,2560]{1,0:T(8,128)(2,1)}, u32[]{:S(2)}, u32[]{:S(2)}) collective-permute-start(bf16[96,2560]{1,0:T(8,128)(2,1)S(1)} %get-tuple-element.61.refs_0_), channel_id=1, source_target_pairs={{1,3},{3,5},{5,7},{7,6},{6,4},{4,2},{2,0},{0,1},{9,11},{11,13},{13... | collective-permute-start | bytes 1474568 | tf_op jit(solution)/shard_map/ppermute | solution.py:443
  64.9 14.3 %collective-permute-start.3 = (bf16[96,2560]{1,0:T(8,128)(2,1)S(1)}, bf16[96,2560]{1,0:T(8,128)(2,1)S(1)}, u32[]{:S(2)}, u32[]{:S(2)}) collective-permute-start(bf16[96,2560]{1,0:T(8,128)(2,1)S(1)} %get-tuple-element.58.refs_0_), channel_id=1, source_target_pairs={{1,0},{3,1},{5,3},{7,5},{6,7},{4,6},{2,4},{0,2},{9,8},{11,9},{13,1... | collective-permute-start | bytes 1474568 | tf_op jit(solution)/shard_map/ppermute | solution.py:443
  66.9 22.8 %collective-permute-start.21 = (bf16[96,2560]{1,0:T(8,128)(2,1)S(1)}, bf16[96,2560]{1,0:T(8,128)(2,1)}, u32[]{:S(2)}, u32[]{:S(2)}) collective-permute-start(bf16[96,2560]{1,0:T(8,128)(2,1)S(1)} %collective-permute-done.12.refs_3_), channel_id=1, source_target_pairs={{1,3},{3,5},{5,7},{7,6},{6,4},{4,2},{2,0},{0,1},{9,11},{11,13},{13... | collective-permute-start | bytes 1474568 | tf_op jit(solution)/shard_map/ppermute | solution.py:443
  66.9 0.8 copy-start.7
  79.2 21.1 %collective-permute-start.14 = (bf16[96,2560]{1,0:T(8,128)(2,1)}, bf16[96,2560]{1,0:T(8,128)(2,1)}, u32[]{:S(2)}, u32[]{:S(2)}) collective-permute-start(bf16[96,2560]{1,0:T(8,128)(2,1)} %collective-permute-done.13.refs_1_), channel_id=1, source_target_pairs={{1,3},{3,5},{5,7},{7,6},{6,4},{4,2},{2,0},{0,1},{9,11},{11,13},{13... | collective-permute-start | bytes 1474568 | tf_op jit(solution)/shard_map/ppermute | solution.py:443
  79.2 21.1 %collective-permute-start.4 = (bf16[96,2560]{1,0:T(8,128)(2,1)S(1)}, bf16[96,2560]{1,0:T(8,128)(2,1)}, u32[]{:S(2)}, u32[]{:S(2)}) collective-permute-start(bf16[96,2560]{1,0:T(8,128)(2,1)S(1)} %collective-permute-done.3.refs_1_), channel_id=1, source_target_pairs={{1,0},{3,1},{5,3},{7,5},{6,7},{4,6},{2,4},{0,2},{9,8},{11,9},{13,1... | collective-permute-start | bytes 1474568 | tf_op jit(solution)/shard_map/ppermute | solution.py:443
  81.2 21.1 %collective-permute-start.20 = (bf16[96,2560]{1,0:T(8,128)(2,1)}, bf16[96,2560]{1,0:T(8,128)(2,1)}, u32[]{:S(2)}, u32[]{:S(2)}) collective-permute-start(bf16[96,2560]{1,0:T(8,128)(2,1)} %collective-permute-done.2.refs_3_), channel_id=1, source_target_pairs={{1,0},{3,1},{5,3},{7,5},{6,7},{4,6},{2,4},{0,2},{9,8},{11,9},{13,1... | collective-permute-start | bytes 1474568 | tf_op jit(solution)/shard_map/ppermute | solution.py:443
  89.7 21.0 %collective-permute-start.25 = (bf16[96,2560]{1,0:T(8,128)(2,1)}, bf16[96,2560]{1,0:T(8,128)(2,1)S(1)}, u32[]{:S(2)}, u32[]{:S(2)}) collective-permute-start(bf16[96,2560]{1,0:T(8,128)(2,1)} %collective-permute-done.21.refs_4_), channel_id=1, source_target_pairs={{1,3},{3,5},{5,7},{7,6},{6,4},{4,2},{2,0},{0,1},{9,11},{11,13},{13... | collective-permute-start | bytes 1474568 | tf_op jit(solution)/shard_map/ppermute | solution.py:443
  100.2 21.0 %collective-permute-start.15 = (bf16[96,2560]{1,0:T(8,128)(2,1)}, bf16[96,2560]{1,0:T(8,128)(2,1)S(1)}, u32[]{:S(2)}, u32[]{:S(2)}) collective-permute-start(bf16[96,2560]{1,0:T(8,128)(2,1)} %collective-permute-done.14.refs_2_), channel_id=1, source_target_pairs={{1,3},{3,5},{5,7},{7,6},{6,4},{4,2},{2,0},{0,1},{9,11},{11,13},{13... | collective-permute-start | bytes 1474568 | tf_op jit(solution)/shard_map/ppermute | solution.py:443
  100.2 21.8 %collective-permute-start.5 = (bf16[96,2560]{1,0:T(8,128)(2,1)}, bf16[96,2560]{1,0:T(8,128)(2,1)S(1)}, u32[]{:S(2)}, u32[]{:S(2)}) collective-permute-start(bf16[96,2560]{1,0:T(8,128)(2,1)} %collective-permute-done.4.refs_2_), channel_id=1, source_target_pairs={{1,0},{3,1},{5,3},{7,5},{6,7},{4,6},{2,4},{0,2},{9,8},{11,9},{13,1... | collective-permute-start | bytes 1474568 | tf_op jit(solution)/shard_map/ppermute | solution.py:443
  102.3 22.6 %collective-permute-start.22 = (bf16[96,2560]{1,0:T(8,128)(2,1)}, bf16[96,2560]{1,0:T(8,128)(2,1)}, u32[]{:S(2)}, u32[]{:S(2)}) collective-permute-start(bf16[96,2560]{1,0:T(8,128)(2,1)} %collective-permute-done.20.refs_4_), channel_id=1, source_target_pairs={{1,0},{3,1},{5,3},{7,5},{6,7},{4,6},{2,4},{0,2},{9,8},{11,9},{13,1... | collective-permute-start | bytes 1474568 | tf_op jit(solution)/shard_map/ppermute | solution.py:443
  110.6 21.2 %collective-permute-start.26 = (bf16[96,2560]{1,0:T(8,128)(2,1)S(1)}, bf16[96,2560]{1,0:T(8,128)(2,1)}, u32[]{:S(2)}, u32[]{:S(2)}) collective-permute-start(bf16[96,2560]{1,0:T(8,128)(2,1)S(1)} %collective-permute-done.25.refs_5_), channel_id=1, source_target_pairs={{1,3},{3,5},{5,7},{7,6},{6,4},{4,2},{2,0},{0,1},{9,11},{11,13},{13... | collective-permute-start | bytes 1474568 | tf_op jit(solution)/shard_map/ppermute | solution.py:443
  110.7 0.8 copy-start.13
  121.2 21.2 %collective-permute-start.16 = (bf16[96,2560]{1,0:T(8,128)(2,1)S(1)}, bf16[96,2560]{1,0:T(8,128)(2,1)}, u32[]{:S(2)}, u32[]{:S(2)}) collective-permute-start(bf16[96,2560]{1,0:T(8,128)(2,1)S(1)} %collective-permute-done.15.refs_3_), channel_id=1, source_target_pairs={{1,3},{3,5},{5,7},{7,6},{6,4},{4,2},{2,0},{0,1},{9,11},{11,13},{13... | collective-permute-start | bytes 1474568 | tf_op jit(solution)/shard_map/ppermute | solution.py:443
  121.2 0.8 copy-start.11
  122.0 20.3 %collective-permute-start.6 = (bf16[96,2560]{1,0:T(8,128)(2,1)S(1)}, bf16[96,2560]{1,0:T(8,128)(2,1)}, u32[]{:S(2)}, u32[]{:S(2)}) collective-permute-start(bf16[96,2560]{1,0:T(8,128)(2,1)S(1)} %collective-permute-done.5.refs_3_), channel_id=1, source_target_pairs={{1,0},{3,1},{5,3},{7,5},{6,7},{4,6},{2,4},{0,2},{9,8},{11,9},{13,1... | collective-permute-start | bytes 1474568 | tf_op jit(solution)/shard_map/ppermute | solution.py:443
  124.0 0.8 copy-start.9
  124.8 21.0 %collective-permute-start.23 = (bf16[96,2560]{1,0:T(8,128)(2,1)}, bf16[96,2560]{1,0:T(8,128)(2,1)}, u32[]{:S(2)}, u32[]{:S(2)}) collective-permute-start(bf16[96,2560]{1,0:T(8,128)(2,1)} %collective-permute-done.22.refs_5_), channel_id=1, source_target_pairs={{1,0},{3,1},{5,3},{7,5},{6,7},{4,6},{2,4},{0,2},{9,8},{11,9},{13,1... | collective-permute-start | bytes 1474568 | tf_op jit(solution)/shard_map/ppermute | solution.py:443
  131.8 21.1 %collective-permute-start.27 = (bf16[96,2560]{1,0:T(8,128)(2,1)}, bf16[96,2560]{1,0:T(8,128)(2,1)}, u32[]{:S(2)}, u32[]{:S(2)}) collective-permute-start(bf16[96,2560]{1,0:T(8,128)(2,1)} %collective-permute-done.26.refs_6_), channel_id=1, source_target_pairs={{1,3},{3,5},{5,7},{7,6},{6,4},{4,2},{2,0},{0,1},{9,11},{11,13},{13... | collective-permute-start | bytes 1474568 | tf_op jit(solution)/shard_map/ppermute | solution.py:443
  142.4 19.0 %collective-permute-start.17 = (bf16[96,2560]{1,0:T(8,128)(2,1)}, bf16[96,2560]{1,0:T(8,128)(2,1)}, u32[]{:S(2)}, u32[]{:S(2)}) collective-permute-start(bf16[96,2560]{1,0:T(8,128)(2,1)} %collective-permute-done.16.refs_4_), channel_id=1, source_target_pairs={{1,3},{3,5},{5,7},{7,6},{6,4},{4,2},{2,0},{0,1},{9,11},{11,13},{13... | collective-permute-start | bytes 1474568 | tf_op jit(solution)/shard_map/ppermute | solution.py:443
  142.4 19.0 %collective-permute-start.7 = (bf16[96,2560]{1,0:T(8,128)(2,1)}, bf16[96,2560]{1,0:T(8,128)(2,1)}, u32[]{:S(2)}, u32[]{:S(2)}) collective-permute-start(bf16[96,2560]{1,0:T(8,128)(2,1)} %collective-permute-done.6.refs_4_), channel_id=1, source_target_pairs={{1,0},{3,1},{5,3},{7,5},{6,7},{4,6},{2,4},{0,2},{9,8},{11,9},{13,1... | collective-permute-start | bytes 1474568 | tf_op jit(solution)/shard_map/ppermute | solution.py:443
  145.8 32.2 %collective-permute-start.24 = (bf16[96,2560]{1,0:T(8,128)(2,1)}, bf16[96,2560]{1,0:T(8,128)(2,1)S(1)}, u32[]{:S(2)}, u32[]{:S(2)}) collective-permute-start(bf16[96,2560]{1,0:T(8,128)(2,1)} %collective-permute-done.23.refs_6_), channel_id=1, source_target_pairs={{1,0},{3,1},{5,3},{7,5},{6,7},{4,6},{2,4},{0,2},{9,8},{11,9},{13,1... | collective-permute-start | bytes 1474568 | tf_op jit(solution)/shard_map/ppermute | solution.py:443
  161.4 16.6 %collective-permute-start.18 = (bf16[96,2560]{1,0:T(8,128)(2,1)}, bf16[96,2560]{1,0:T(8,128)(2,1)S(1)}, u32[]{:S(2)}, u32[]{:S(2)}) collective-permute-start(bf16[96,2560]{1,0:T(8,128)(2,1)} %collective-permute-done.17.refs_5_), channel_id=1, source_target_pairs={{1,3},{3,5},{5,7},{7,6},{6,4},{4,2},{2,0},{0,1},{9,11},{11,13},{13... | collective-permute-start | bytes 1474568 | tf_op jit(solution)/shard_map/ppermute | solution.py:443
  161.7 16.3 %collective-permute-start.8 = (bf16[96,2560]{1,0:T(8,128)(2,1)}, bf16[96,2560]{1,0:T(8,128)(2,1)S(1)}, u32[]{:S(2)}, u32[]{:S(2)}) collective-permute-start(bf16[96,2560]{1,0:T(8,128)(2,1)} %collective-permute-done.7.refs_5_), channel_id=1, source_target_pairs={{1,0},{3,1},{5,3},{7,5},{6,7},{4,6},{2,4},{0,2},{9,8},{11,9},{13,1... | collective-permute-start | bytes 1474568 | tf_op jit(solution)/shard_map/ppermute | solution.py:443
  163.4 1.3 copy-start.2
  164.7 1.0 copy-start.4
  165.7 1.0 copy-start.6
  166.8 1.0 copy-start.8
  167.8 1.0 copy-start.14
  178.0 12.7 %collective-permute-start.19 = (bf16[96,2560]{1,0:T(8,128)(2,1)S(1)}, bf16[96,2560]{1,0:T(8,128)(2,1)S(1)}, u32[]{:S(2)}, u32[]{:S(2)}) collective-permute-start(bf16[96,2560]{1,0:T(8,128)(2,1)S(1)} %collective-permute-done.18.refs_6_), channel_id=1, source_target_pairs={{1,3},{3,5},{5,7},{7,6},{6,4},{4,2},{2,0},{0,1},{9,11},{11,13},{13... | collective-permute-start | bytes 1474568 | tf_op jit(solution)/shard_map/ppermute | solution.py:443
  178.3 20.1 %collective-permute-start.9 = (bf16[96,2560]{1,0:T(8,128)(2,1)S(1)}, bf16[96,2560]{1,0:T(8,128)(2,1)S(1)}, u32[]{:S(2)}, u32[]{:S(2)}) collective-permute-start(bf16[96,2560]{1,0:T(8,128)(2,1)S(1)} %collective-permute-done.8.refs_6_), channel_id=1, source_target_pairs={{1,0},{3,1},{5,3},{7,5},{6,7},{4,6},{2,4},{0,2},{9,8},{11,9},{13,1... | collective-permute-start | bytes 1474568 | tf_op jit(solution)/shard_map/ppermute | solution.py:443
  180.1 10.7 %copy-start.12 = (bf16[96,2560]{1,0:T(8,128)(2,1)S(1)}, bf16[96,2560]{1,0:T(8,128)(2,1)}, u32[]{:S(2)}) copy-start(bf16[96,2560]{1,0:T(8,128)(2,1)} %copy-done.11) | copy-start | bytes 1474564
  190.7 7.7 %copy-start.10 = (bf16[96,2560]{1,0:T(8,128)(2,1)S(1)}, bf16[96,2560]{1,0:T(8,128)(2,1)}, u32[]{:S(2)}) copy-start(bf16[96,2560]{1,0:T(8,128)(2,1)} %copy-done.9) | copy-start | bytes 1474564
  206.2 5.3 %collective-permute-start.28 = (bf16[6,256,256]{2,1,0:T(8,128)(2,1)S(1)}, bf16[6,256,256]{2,1,0:T(8,128)(2,1)S(1)}, u32[]{:S(2)}, u32[]{:S(2)}) collective-permute-start(bf16[6,256,256]{2,1,0:T(8,128)(2,1)S(1)} %fold.1), channel_id=1, source_target_pairs={{24,16},{25,17},{26,18},{27,19},{28,20},{29,21},{30,22},{31,23}} | collective-permute-start | bytes 2359304 | tf_op jit(solution)/shard_map/ppermute | solution.py:482
  213.3 0.9 collective-permute-start.29
  216.1 14.8 %collective-permute-start.30 = (bf16[6,256,256]{2,1,0:T(8,128)(2,1)S(1)}, bf16[6,256,256]{2,1,0:T(8,128)(2,1)S(1)}, u32[]{:S(2)}, u32[]{:S(2)}) collective-permute-start(bf16[6,256,256]{2,1,0:T(8,128)(2,1)S(1)} %hop.3), channel_id=1, source_target_pairs={{8,0},{9,1},{10,2},{11,3},{12,4},{13,5},{14,6},{15,7}} | collective-permute-start | bytes 2359304 | tf_op jit(solution)/shard_map/ppermute | solution.py:482
Sparse Core Ops, SparseCore 0:
  15.2 49.7 all-gather.1

commit v9 on v8

--- a/solution.py
+++ b/solution.py
@@ -13,8 +13,9 @@
 LANES = 128
 TILE = 256
 LINE = 4
-GATE = 3
+GATE = 2
 MIB = 1024 * 1024
+CLAIM = 60 * MIB
 
 
 def half_width(rows, count):
@@ -40,41 +41,63 @@
     piece = piece.astype(F32)
     rest = width - piece.shape[1]
     wide = jnp.concatenate([piece, jnp.zeros((piece.shape[0], rest), F32)], axis=1) if rest else piece
-    return pltpu.roll(wide, start, 1)
-
-
-def pack_kernel(count, ranges, place_ref, gain_ref, increment_ref, *packed_refs):
+    return pltpu.roll(wide, start, 1) if start else wide
+
+
+def pack_kernel(count, ranges, place_ref, gain_ref, increment_ref, terminal_ref, *packed_refs):
     width = gain_ref.shape[2]
-    stride = width + half_width(gain_ref.shape[1], count)[1]
+    half = half_width(gain_ref.shape[1], count)[1]
+    stride = width + half
     place = place_ref[0]
     for (low, high), packed_ref in zip(ranges, packed_refs):
         for step in range(low, high):
             base = (step - low) * stride
             packed_ref[:, base:base + width] = gain_ref[step]
             packed_ref[:, base + width:base + stride] = packed_half(increment_ref[step], place, count)
-
-
-def pack(place, gains, increments, count, ranges):
+    end = packed_half(terminal_ref[...], place, count)
+    for turn in range(2):
+        base = (ranges[turn][1] - ranges[turn][0]) * stride
+        packed_refs[turn][:, base:] = end[:, turn * half // 2:(turn + 1) * half // 2]
+
+
+def pack(place, gains, increments, terminal, count, ranges):
     rows, width = gains.shape[1:]
     half = half_width(rows, count)[1]
-    lanes = [(high - low) * (width + half) for low, high in ranges]
+    lanes = [(high - low) * (width + half) + half // 2 * (n < 2) for n, (low, high) in enumerate(ranges)]
     vmem = pl.BlockSpec(memory_space=pltpu.VMEM)
     return pl.pallas_call(
         functools.partial(pack_kernel, count, ranges),
-        in_specs=[pl.BlockSpec(memory_space=pltpu.SMEM), vmem, vmem],
+        in_specs=[pl.BlockSpec(memory_space=pltpu.SMEM), vmem, vmem, vmem],
         out_specs=[vmem] * len(lanes),
         out_shape=[jax.ShapeDtypeStruct((rows, size), BF16) for size in lanes],
-        compiler_params=pltpu.CompilerParams(vmem_limit_bytes=12 * MIB),
+        compiler_params=pltpu.CompilerParams(vmem_limit_bytes=CLAIM),
         name="pack",
-    )(place, gains, increments)
-
-
-def assemble(starts, blocks, gain, fresh):
+    )(place, gains, increments, terminal)
+
+
+def unpack(raw, half):
+    count, rows, _ = raw.shape
+    for n in range(count):
+        half[n * rows:(n + 1) * rows, :] = unpacked_half(raw[n], n * rows, half.shape[1]).astype(BF16)
+
+
+def origins(place, cycle, way):
+    count = len(cycle)
+
+    def look(table, at):
+        return sum(jnp.where(at == n, value, 0) for n, value in enumerate(table))
+
+    spot = look([cycle.index(d) for d in range(count)], place)
+    return [look(cycle, lax.rem(spot - way * n + count, count)) for n in range(count)]
+
+
+def assemble(places, blocks, gain, fresh, raw):
     rows = blocks[0].shape[0]
     width = gain.shape[0]
-    for start, block in zip(starts, blocks):
-        gain[pl.ds(start, rows), :] = block[:, :width]
-        fresh[pl.ds(start, rows), :] = unpacked_half(block[:, width:], start, width).astype(BF16)
+    for place, block in zip(places, blocks):
+        gain[pl.ds(pl.multiple_of(place * rows, 16), rows), :] = block[:, :width]
+        raw[place] = block[:, width:]
+    unpack(raw, fresh)
 
 
 def advance(gain, half, fresh, middle):
@@ -101,32 +124,44 @@
     return own + nt(jnp.where(picked, 1.0, 0.0).astype(BF16), half[...])
 
 
-def compose_kernel(count, first, last_ref, places_ref, *refs):
+def compose_kernel(cycle, way, first, last_ref, place_ref, *refs):
+    count = len(cycle)
+    places = origins(place_ref[0], cycle, way)
     blocks, refs = refs[:count], refs[count:]
-    half_in, refs = refs[0], refs[1:]
-    if not first:
-        factor_in, refs = refs[0], refs[3:]
-    factor_out, own_out, mine_out, half, gain, factor, fresh, middle = refs
+    if first:
+        ends, refs = refs[:2 * count], refs[2 * count:]
+    else:
+        half_in, factor_in, refs = refs[0], refs[1], refs[4:]
+    factor_out, own_out, mine_out, half, gain, factor, fresh, middle, raw = refs
     rows = blocks[0].shape[0]
-    starts = [pl.multiple_of(places_ref[n] * rows, 16) for n in range(count)]
-    assemble(starts, blocks, gain, fresh)
 
     @pl.when(pl.program_id(0) == 0)
     def _():
         if first:
-            factor[...] = gain[...]
-            half[...] = (half_in[...].astype(F32) * jnp.where(last_ref[0] == 1, 0.5, 0.0)).astype(BF16)
+            scale = jnp.where(last_ref[0] == 1, 1.0, 0.0).astype(BF16)
+            cut = ends[0].shape[1]
+            for n, end in enumerate(ends):
+                spots = places if n < count else origins(place_ref[0], cycle, -way)
+                raw[spots[n % count], :, n // count * cut:(n // count + 1) * cut] = end[...] * scale
+            unpack(raw, half)
         else:
             factor[...] = factor_in[0]
             half[...] = half_in[...]
 
+    assemble(places, blocks, gain, fresh, raw)
     if first:
+
+        @pl.when(pl.program_id(0) == 0)
+        def _():
+            factor[...] = gain[...]
+
         pl.when(pl.program_id(0) > 0)(lambda: extend(gain, factor))
     else:
         extend(gain, factor)
     advance(gain, half, fresh, middle)
-    own_out[0] = whole_rows(half, starts[0], rows)
-    mine_out[0] = factor[pl.ds(starts[0], rows), :]
+    mine = pl.multiple_of(place_ref[0] * rows, 16)
+    own_out[0] = whole_rows(half, mine, rows)
+    mine_out[0] = factor[pl.ds(mine, rows), :]
     factor_out[0] = factor[...]
 
 
@@ -136,27 +171,35 @@
     return pl.BlockSpec((1, width, width), lambda i, *p: (place(i), 0, 0))
 
 
-def compose(last, places, blocks, half, state, low, turns, steps):
+def compose(last, place, cycle, way, blocks, ends, state, half, low, turns, steps):
     count = len(blocks)
     rows = blocks[0].shape[0]
     width = rows * count
-    stride = width + half_width(rows, count)[1]
+    lanes = half_width(rows, count)[1]
+    stride = width + lanes
     first = state is None
     anywhere = pl.BlockSpec(memory_space=pl.ANY)
-    in_specs = [pl.BlockSpec((rows, stride), lambda i, *p: (0, turns - 1 - i))] * count + [square(width)]
-    if not first:
+    in_specs = [pl.BlockSpec((rows, stride), lambda i, *p: (0, turns - 1 - i))] * count
+    if first:
+        at = turns * stride // (lanes // 2)
+        in_specs += [
+            pl.BlockSpec((rows, lanes // 2), lambda i, *p: (0, at), pipeline_mode=pl.Buffered(1))
+        ] * len(ends)
+        args = ends
+    else:
         after = pl.BlockSpec((1, width, width), lambda i, *p: (low + turns, 0, 0), pipeline_mode=pl.Buffered(1))
-        in_specs += [after, anywhere, anywhere]
+        in_specs += [square(width), after, anywhere, anywhere]
+        args = [half, *state]
     band = pl.BlockSpec((1, rows, width), lambda i, *p: (low + turns - 1 - i, 0, 0))
     base = 2 + count + 1
     return pl.pallas_call(
-        functools.partial(compose_kernel, count, first),
+        functools.partial(compose_kernel, cycle, way, first),
         grid_spec=pltpu.PrefetchScalarGridSpec(
             num_scalar_prefetch=2,
             grid=(turns,),
             in_specs=in_specs,
             out_specs=[square(width, lambda i: low + turns - 1 - i), band, band, square(width)],
-            scratch_shapes=[pltpu.VMEM((width, width), BF16) for _ in range(4)],
+            scratch_shapes=[pltpu.VMEM((width, width), BF16)] * 4 + [pltpu.VMEM((count, rows, lanes), BF16)],
         ),
         out_shape=[
             jax.ShapeDtypeStruct((steps, width, width), BF16),
@@ -170,33 +213,33 @@
             flops=6 * turns * width**3, bytes_accessed=8 * turns * width * width, transcendentals=0
         ),
         name="compose",
-    )(last, places, *blocks, half, *(() if first else state))
-
-
-def chain_kernel(count, places_ref, *refs):
+    )(last, place, *blocks, *args)
+
+
+def chain_kernel(cycle, way, place_ref, *refs):
+    count = len(cycle)
+    places = origins(place_ref[0], cycle, way)
     blocks, refs = refs[:count], refs[count:]
-    half_in, refs = refs[0], refs[-6:]
-    gain_out, half_out, gain, half, fresh, middle = refs
-    rows = blocks[0].shape[0]
-    starts = [pl.multiple_of(places_ref[n] * rows, 16) for n in range(count)]
-    assemble(starts, blocks, gain, fresh)
+    half_in, refs = refs[0], refs[-7:]
+    gain_out, half_out, gain, half, fresh, middle, raw = refs
 
     @pl.when(pl.program_id(0) == 0)
     def _():
         half[...] = half_in[...].reshape(half.shape)
 
+    assemble(places, blocks, gain, fresh, raw)
     gain_out[0] = gain[...]
     advance(gain, half, fresh, middle)
     half_out[0] = half[...]
 
 
-def chain(places, blocks, half, state, low, turns, steps):
+def chain(place, cycle, way, blocks, half, state, low, turns, steps):
     count = len(blocks)
     rows = blocks[0].shape[0]
     width = rows * count
-    stride = width + half_width(rows, count)[1]
+    lanes = half_width(rows, count)[1]
     anywhere = pl.BlockSpec(memory_space=pl.ANY)
-    in_specs = [pl.BlockSpec((rows, stride), lambda i, *p: (0, turns - 1 - i))] * count
+    in_specs = [pl.BlockSpec((rows, width + lanes), lambda i, *p: (0, turns - 1 - i))] * count
     if state is None:
         in_specs += [square(width)]
         args = [half]
@@ -208,13 +251,13 @@
         args = [state[1], state[0]]
     whole = square(width, lambda i: low + turns - 1 - i)
     return pl.pallas_call(
-        functools.partial(chain_kernel, count),
+        functools.partial(chain_kernel, cycle, way),
         grid_spec=pltpu.PrefetchScalarGridSpec(
             num_scalar_prefetch=1,
             grid=(turns,),
             in_specs=in_specs,
             out_specs=[whole, whole],
-            scratch_shapes=[pltpu.VMEM((width, width), BF16) for _ in range(4)],
+            scratch_shapes=[pltpu.VMEM((width, width), BF16)] * 4 + [pltpu.VMEM((count, rows, lanes), BF16)],
         ),
         out_shape=[jax.ShapeDtypeStruct((steps, width, width), BF16)] * 2,
         input_output_aliases={} if state is None else {1 + count + 1: 0, 1 + count: 1},
@@ -223,7 +266,7 @@
             flops=4 * turns * width**3, bytes_accessed=8 * turns * width * width, transcendentals=0
         ),
         name="chain",
-    )(places, *blocks, *args)
+    )(place, *blocks, *args)
 
 
 def factors_kernel(place_ref, gain_ref, factor_in, mine_ref, factor_out, mine_out, factor):
@@ -435,21 +478,16 @@
     blocks = lax.axis_size("tm")
     line = math.gcd(count, LINE)
     steps = gains.shape[0]
-    place = lax.axis_index("tile").astype(jnp.int32)
+    place = lax.axis_index("tile").astype(jnp.int32).reshape(1)
     last = (lax.axis_index("tm") == blocks - 1).astype(jnp.int32).reshape(1)
     cycle = ring_order(line, count // line)
 
     def passed(array, way):
         return lax.ppermute(array, "tile", [(cycle[n], cycle[(n + way) % count]) for n in range(count)])
 
-    def origins(way):
-        table = [[cycle[(cycle.index(d) - way * hop) % count] for hop in range(count)] for d in range(count)]
-        return jnp.asarray(table, jnp.int32)[place]
-
     ranges = pieces(steps)
-    own = pack(place.reshape(1), gains, increments, count, ranges)
-    own, end = lax.optimization_barrier((own, terminal.astype(BF16)))
-    end = lax.all_gather(end, "tile", axis=0, tiled=True)
+    own = pack(place, gains, increments, terminal, count, ranges)
+    own, last = lax.optimization_barrier((own, last))
     arrived = []
     for turn, array in enumerate(own):
         way = 1 if turn % 2 == 0 else -1
@@ -458,25 +496,24 @@
             array, before[GATE] = lax.optimization_barrier((array, before[GATE]))
             for hop_count in range(GATE + 1, count):
                 before[hop_count] = passed(before[hop_count - 1], way)
-                if hop_count == GATE + 1:
-                    before[hop_count], end = lax.optimization_barrier((before[hop_count], end))
         found = [array]
         for hop_count in range(1, count):
             found.append(passed(found[-1], way))
         arrived.append(found)
-    state, half = None, end
+    state, half = None, None
     for turn in range(2):
         reached = count - 3 + turn
-        blocks_here, _ = lax.optimization_barrier((arrived[turn], (arrived[2][reached], arrived[3][reached])))
+        arrived[:2], _ = lax.optimization_barrier((arrived[:2], (arrived[2][reached], arrived[3][reached])))
+        ends = [] if turn else arrived[0] + arrived[1]
         low, high = ranges[turn]
-        *state, half = compose(last, origins(1 - 2 * turn), blocks_here, half, state, low, high - low, steps)
+        *state, half = compose(last, place, cycle, 1 - 2 * turn, arrived[turn], ends, state, half, low, high - low, steps)
     factors, own, mine = state
     early = None
     for turn in range(2, 4):
         low, high = ranges[turn]
-        early = chain(origins(5 - 2 * turn), arrived[turn], half, early, low, high - low, ranges[2][1])
-    factors, mine = extend_factors(place.reshape(1), early[0], factors, mine)
-    own = own_rows(place.reshape(1), early[1], own)
+        early = chain(place, cycle, 5 - 2 * turn, arrived[turn], half, early, low, high - low, ranges[2][1])
+    factors, mine = extend_factors(place, early[0], factors, mine)
+    own = own_rows(place, early[1], own)
     packed = []
     for turn in range(blocks - 1, 0, -1):
         packed.append(lax.ppermute(hop(factors, early[1], packed), "tm", [(turn, turn - 1)]))

time: 245 us -> 212 us (0.87)
  between operations: 13.6 us -> 0.2 us
  local copies, waits for them, and re-layouts: 14.6 us -> 2.1 us
  waiting for transfers between devices: 136 us -> 128 us
  starting transfers between devices: 26.1 us -> 32.4 us
  Pallas kernels: 53 us -> 48.8 us
    unnamed x30 -> x10, local copies, waits for them, and re-layouts: 13.2 us -> 2.1 us
    ppermute x28, waiting for transfers between devices: 124 us -> 116 us  [passed(): lax.ppermute(array, 'tile', [(cycle[n], cycle[(n + way) % count]) for n i...]
    pallas_call x4, Pallas kernels: 34.9 us -> 27.2 us  [the longest x2 16.9 us: compose(): pl.pallas_call(functools.partial(compose_kernel, cycle, way, first), grid...]
    ppermute x28, starting transfers between devices: 23.1 us -> 29.4 us  [passed(): lax.ppermute(array, 'tile', [(cycle[n], cycle[(n + way) % count]) for n i...]
    pallas_call x1, Pallas kernels: 0.77 us -> 4.16 us  [pack(): pl.pallas_call(functools.partial(pack_kernel, count, ranges), in_specs=[p...]
  transfers between devices with their start and end apart: 32 -> 31, of which waited for: 13 -> 13; matrix products, arithmetic and copies ran while one was open for 1% -> 0% of each run, Pallas kernels for 14% -> 14%
where the time goes in v9:
time: 212 us; the launch traced here: 211 us
  waiting for transfers between devices  128 us (60%)
  Pallas kernels  48.8 us (23%)
  starting transfers between devices  32.4 us (15%)
    ppermute x28, waiting for transfers between devices, passed(): lax.ppermute(array, 'tile', [(cycle[n], cycle[(n + way) % count]) for n i...  116 us
    ppermute x28, starting transfers between devices, passed(): lax.ppermute(array, 'tile', [(cycle[n], cycle[(n + way) % count]) for n i...  29.4 us
    pallas_call x2, Pallas kernels, compose(): pl.pallas_call(functools.partial(compose_kernel, cycle, way, first), grid...  16.9 us
    ppermute x3, waiting for transfers between devices, local(): lax.ppermute(hop(factors, early[1], packed), 'tm', [(turn, turn - 1)])  11.8 us
    pallas_call x2, Pallas kernels, chain(): pl.pallas_call(functools.partial(chain_kernel, cycle, way), grid_spec=plt...  10.3 us
    pallas_call x1, Pallas kernels, finish(): pl.pallas_call(functools.partial(finish_kernel, len(packed)), grid=(steps...  6.79 us
    pallas_call x1, Pallas kernels, extend_factors(): pl.pallas_call(factors_kernel, grid_spec=pltpu.PrefetchScalarGridSpec(num...  4.55 us
  transfers between devices with their start and end apart: 31, of which 13 were waited for; matrix products, arithmetic and copies ran while one was open for 0% of the time, Pallas kernels for 14%

profile of v9, /device:TPU:0, one launch (start us, length us, event | category | flops | bytes accessed | tf_op | source)
XLA Modules:
  0.0 211.5 jit_solution(677567267943519781)
XLA Ops:
  0.0 4.2 %pack.1 = (bf16[96,2816]{1,0:T(8,128)(2,1)}, bf16[96,2816]{1,0:T(8,128)(2,1)}, bf16[96,2560]{1,0:T(8,128)(2,1)}, bf16[96,2560]{1,0:T(8,128)(2,1)}) custom-call(s32[1]{0:T(128)} %bitcast.place_ref, bf16[8,96,768]{2,1,0:T(8,128)(2,1)} %gain_ref.1, f32[8,96,768]{2,1,0:T(8,128)} %increment_ref.1, f32[96,768]{1,0:T(8,128)} %terminal_ref.1), custom_call_target="tpu_custom_call" | custom-call | tf_op jit(solution)/shard_map/pack/pallas_call | solution.py:68
  4.2 3.0 %collective-permute-start.9 = (bf16[96,2816]{1,0:T(8,128)(2,1)}, bf16[96,2816]{1,0:T(8,128)(2,1)S(1)}, u32[]{:S(2)}, u32[]{:S(2)}) collective-permute-start(bf16[96,2816]{1,0:T(8,128)(2,1)} %get-tuple-element.69.refs_0_.refs_8_), channel_id=1, source_target_pairs={{1,3},{3,5},{5,7},{7,6},{6,4},{4,2},{2,0},{0,1},{9,11},{11,13},{13... | collective-permute-start | bytes 1622024 | tf_op jit(solution)/shard_map/ppermute | solution.py:486
  7.2 12.5 %collective-permute-done.9.refs_1_.refs_9_ = bf16[96,2816]{1,0:T(8,128)(2,1)S(1)} collective-permute-done((bf16[96,2816]{1,0:T(8,128)(2,1)}, bf16[96,2816]{1,0:T(8,128)(2,1)S(1)}, u32[]{:S(2)}, u32[]{:S(2)}) %collective-permute-start.9) | collective-permute-done | bytes 540704 | tf_op jit(solution)/shard_map/ppermute | solution.py:486
  19.7 1.7 collective-permute-start.10
  21.7 11.4 %collective-permute-done.10.refs_2_.refs_10_ = bf16[96,2816]{1,0:T(8,128)(2,1)S(1)} collective-permute-done((bf16[96,2816]{1,0:T(8,128)(2,1)S(1)}, bf16[96,2816]{1,0:T(8,128)(2,1)S(1)}, u32[]{:S(2)}, u32[]{:S(2)}) %collective-permute-start.10) | collective-permute-done | bytes 540704 | tf_op jit(solution)/shard_map/ppermute | solution.py:486
  33.1 1.1 collective-permute-done.1.refs_18_.refs_2_
  34.2 1.6 collective-permute-start.18
  36.2 1.6 collective-permute-start.11
  38.3 11.2 %collective-permute-done.18.refs_3_.refs_11_ = bf16[96,2816]{1,0:T(8,128)(2,1)S(1)} collective-permute-done((bf16[96,2816]{1,0:T(8,128)(2,1)S(1)}, bf16[96,2816]{1,0:T(8,128)(2,1)S(1)}, u32[]{:S(2)}, u32[]{:S(2)}) %collective-permute-start.18) | collective-permute-done | bytes 540704 | tf_op jit(solution)/shard_map/ppermute | solution.py:486
  49.4 1.6 collective-permute-start.19
  51.0 0.5 collective-permute-start.24
  51.5 8.5 %collective-permute-done.11.refs_1_ = bf16[96,2560]{1,0:T(8,128)(2,1)S(1)} collective-permute-done((bf16[96,2560]{1,0:T(8,128)(2,1)}, bf16[96,2560]{1,0:T(8,128)(2,1)S(1)}, u32[]{:S(2)}, u32[]{:S(2)}) %collective-permute-start.11) | collective-permute-done | bytes 491552 | tf_op jit(solution)/shard_map/ppermute | solution.py:486
  60.0 1.6 collective-permute-start.12
  61.5 0.5 collective-permute-start.3
  62.0 9.6 %collective-permute-done.19.refs_4_.refs_12_ = bf16[96,2816]{1,0:T(8,128)(2,1)S(1)} collective-permute-done((bf16[96,2816]{1,0:T(8,128)(2,1)S(1)}, bf16[96,2816]{1,0:T(8,128)(2,1)S(1)}, u32[]{:S(2)}, u32[]{:S(2)}) %collective-permute-start.19) | collective-permute-done | bytes 540704 | tf_op jit(solution)/shard_map/ppermute | solution.py:486
  71.6 1.6 collective-permute-start.20
  73.1 0.5 collective-permute-start.25
  73.6 8.5 %collective-permute-done.12.refs_2_ = bf16[96,2560]{1,0:T(8,128)(2,1)S(1)} collective-permute-done((bf16[96,2560]{1,0:T(8,128)(2,1)S(1)}, bf16[96,2560]{1,0:T(8,128)(2,1)S(1)}, u32[]{:S(2)}, u32[]{:S(2)}) %collective-permute-start.12) | collective-permute-done | bytes 491552 | tf_op jit(solution)/shard_map/ppermute | solution.py:486
  82.1 1.6 collective-permute-start.13
  83.7 0.5 collective-permute-start.4
  84.1 9.6 %collective-permute-done.20.refs_5_.refs_13_ = bf16[96,2816]{1,0:T(8,128)(2,1)S(1)} collective-permute-done((bf16[96,2816]{1,0:T(8,128)(2,1)S(1)}, bf16[96,2816]{1,0:T(8,128)(2,1)S(1)}, u32[]{:S(2)}, u32[]{:S(2)}) %collective-permute-start.20) | collective-permute-done | bytes 540704 | tf_op jit(solution)/shard_map/ppermute | solution.py:486
  93.7 1.6 collective-permute-start.21
  95.3 0.5 collective-permute-start.26
  95.7 8.5 %collective-permute-done.13.refs_3_ = bf16[96,2560]{1,0:T(8,128)(2,1)S(1)} collective-permute-done((bf16[96,2560]{1,0:T(8,128)(2,1)S(1)}, bf16[96,2560]{1,0:T(8,128)(2,1)S(1)}, u32[]{:S(2)}, u32[]{:S(2)}) %collective-permute-start.13) | collective-permute-done | bytes 491552 | tf_op jit(solution)/shard_map/ppermute | solution.py:486
  104.2 1.6 collective-permute-start.14
  106.2 9.6 %collective-permute-done.21.refs_6_.refs_14_ = bf16[96,2816]{1,0:T(8,128)(2,1)S(1)} collective-permute-done((bf16[96,2816]{1,0:T(8,128)(2,1)S(1)}, bf16[96,2816]{1,0:T(8,128)(2,1)S(1)}, u32[]{:S(2)}, u32[]{:S(2)}) %collective-permute-start.21) | collective-permute-done | bytes 540704 | tf_op jit(solution)/shard_map/ppermute | solution.py:486
  115.8 1.6 collective-permute-start.22
  117.8 8.5 %collective-permute-done.14.refs_4_ = bf16[96,2560]{1,0:T(8,128)(2,1)S(1)} collective-permute-done((bf16[96,2560]{1,0:T(8,128)(2,1)S(1)}, bf16[96,2560]{1,0:T(8,128)(2,1)S(1)}, u32[]{:S(2)}, u32[]{:S(2)}) %collective-permute-start.14) | collective-permute-done | bytes 491552 | tf_op jit(solution)/shard_map/ppermute | solution.py:486
  126.3 1.6 collective-permute-start.15
  128.4 17.3 %collective-permute-done.15.refs_5_ = bf16[96,2560]{1,0:T(8,128)(2,1)S(1)} collective-permute-done((bf16[96,2560]{1,0:T(8,128)(2,1)S(1)}, bf16[96,2560]{1,0:T(8,128)(2,1)S(1)}, u32[]{:S(2)}, u32[]{:S(2)}) %collective-permute-start.15) | collective-permute-done | bytes 491552 | tf_op jit(solution)/shard_map/ppermute | solution.py:486
  145.7 1.6 collective-permute-start.16
  147.7 1.0 copy-done
  148.8 1.0 copy-done.2
  149.8 8.2 %compose.2 = (bf16[8,768,768]{2,1,0:T(8,128)(2,1)S(1)}, f32[8,96,768]{2,1,0:T(8,128)S(1)}, bf16[8,96,768]{2,1,0:T(8,128)(2,1)S(1)}, bf16[768,768]{1,0:T(8,128)(2,1)S(1)}) custom-call(s32[1]{0:T(128)} %bitcast.1.last_ref, s32[1]{0:T(128)} %bitcast.place_ref, bf16[96,2816]{1,0:T(8,128)(2,1)S(1)} %copy-done.2, ...), custom_call_target="tpu_custom_call" | custom-call | flops 5435817984 | bytes 9437184 | tf_op jit(solution)/shard_map/compose/pallas_call | solution.py:195
  158.0 1.6 collective-permute-start.17
  159.6 0.5 collective-permute-start.8
  160.1 8.7 %compose.3 = (bf16[8,768,768]{2,1,0:T(8,128)(2,1)S(1)}, f32[8,96,768]{2,1,0:T(8,128)S(1)}, bf16[8,96,768]{2,1,0:T(8,128)(2,1)S(1)}, bf16[768,768]{1,0:T(8,128)(2,1)S(1)}) custom-call(s32[1]{0:T(128)} %bitcast.1.last_ref, s32[1]{0:T(128)} %bitcast.place_ref, ...), custom_call_target="tpu_custom_call", output_to_operand_aliasing={{0}: (11, {}), {1}: (12, {}), {2}: (13, {})} | custom-call | flops 5435817984 | bytes 9437184 | tf_op jit(solution)/shard_map/compose/pallas_call | solution.py:195
  168.9 5.1 %chain.2 = (bf16[4,768,768]{2,1,0:T(8,128)(2,1)S(1)}, bf16[4,768,768]{2,1,0:T(8,128)(2,1)S(1)}) custom-call(s32[1]{0:T(128)} %bitcast.place_ref, bf16[96,2560]{1,0:T(8,128)(2,1)S(1)} %copy-done.4, bf16[96,2560]{1,0:T(8,128)(2,1)S(1)} %collective-permute-done.11.refs_1_, bf16[96,2560]{1,0:T(8,128)(2,1)S(1)} %collective-permute-done.12.refs_2_, ...), custom_call_target="tpu_custom_call" | custom-call | flops 3623878656 | bytes 9437184 | tf_op jit(solution)/shard_map/chain/pallas_call | solution.py:253
  174.1 5.1 %chain.3 = (bf16[4,768,768]{2,1,0:T(8,128)(2,1)S(1)}, bf16[4,768,768]{2,1,0:T(8,128)(2,1)S(1)}) custom-call(s32[1]{0:T(128)} %bitcast.place_ref, bf16[96,2560]{1,0:T(8,128)(2,1)S(1)} %copy-done.3, bf16[96,2560]{1,0:T(8,128)(2,1)S(1)} %collective-permute-done.2.refs_1_, ...), custom_call_target="tpu_custom_call", output_to_operand_aliasing={{0}: (10, {}), {1}: (9, {})} | custom-call | flops 3623878656 | bytes 9437184 | tf_op jit(solution)/shard_map/chain/pallas_call | solution.py:253
  179.5 0.7 collective-permute-start.28
  180.2 4.5 %extend_factors.1 = (bf16[8,768,768]{2,1,0:T(8,128)(2,1)S(1)}, bf16[8,96,768]{2,1,0:T(8,128)(2,1)S(1)}) custom-call(s32[1]{0:T(128)} %bitcast.place_ref, bf16[4,768,768]{2,1,0:T(8,128)(2,1)S(1)} %get-tuple-element.100.gain_ref, bf16[8,768,768]{2,1,0:T(8,128)(2,1)S(1)} %get-tuple-element.101.factor_in, ...), custom_call_target="tpu_custom_call", output_to_operand_aliasing={{0}: (2, {}), {1}: (3, {})} | custom-call | flops 3623878656 | bytes 9437184 | tf_op jit(solution)/shard_map/extend_factors/pallas_call | solution.py:289
  184.8 1.8 hop.2
  186.6 0.9 collective-permute-start.29
  187.6 1.8 hop.3
  189.4 1.3 collective-permute-start.30
  190.7 2.1 own_rows.1.own_ref
  192.8 11.8 %collective-permute-done.30.refs_2_ = bf16[6,256,256]{2,1,0:T(8,128)(2,1)S(1)} collective-permute-done((bf16[6,256,256]{2,1,0:T(8,128)(2,1)S(1)}, bf16[6,256,256]{2,1,0:T(8,128)(2,1)S(1)}, u32[]{:S(2)}, u32[]{:S(2)}) %collective-permute-start.30) | collective-permute-done | bytes 786464 | tf_op jit(solution)/shard_map/ppermute | solution.py:519
  204.7 6.8 %finish.1 = f32[8,96,768]{2,1,0:T(8,128)} custom-call(bf16[8,768,768]{2,1,0:T(8,128)(2,1)S(1)} %get-tuple-element.103.factor_ref, f32[8,96,768]{2,1,0:T(8,128)S(1)} %own_rows.1.own_ref, bf16[8,96,768]{2,1,0:T(8,128)(2,1)S(1)} %get-tuple-element.106.mine_ref, bf16[6,256,256]{2,1,0:T(8,128)(2,1)S(1)} %collective-permute-done.28.refs_0_, ...), custom_call_target="tpu_custom_call" | custom-call | tf_op jit(solution)/shard_map/finish/pallas_call | solution.py:445
  (35 shorter events, 3.5 us)
Async XLA Ops:
  4.2 15.5 %collective-permute-start.9 = (bf16[96,2816]{1,0:T(8,128)(2,1)}, bf16[96,2816]{1,0:T(8,128)(2,1)S(1)}, u32[]{:S(2)}, u32[]{:S(2)}) collective-permute-start(bf16[96,2816]{1,0:T(8,128)(2,1)} %get-tuple-element.69.refs_0_.refs_8_), channel_id=1, source_target_pairs={{1,3},{3,5},{5,7},{7,6},{6,4},{4,2},{2,0},{0,1},{9,11},{11,13},{13... | collective-permute-start | bytes 1622024 | tf_op jit(solution)/shard_map/ppermute | solution.py:486
  7.1 14.2 %collective-permute-start = (bf16[96,2816]{1,0:T(8,128)(2,1)}, bf16[96,2816]{1,0:T(8,128)(2,1)S(1)}, u32[]{:S(2)}, u32[]{:S(2)}) collective-permute-start(bf16[96,2816]{1,0:T(8,128)(2,1)} %get-tuple-element.85.refs_16_.refs_0_), channel_id=1, source_target_pairs={{1,0},{3,1},{5,3},{7,5},{6,7},{4,6},{2,4},{0,2},{9,8},{11,9},{13,1... | collective-permute-start | bytes 1622024 | tf_op jit(solution)/shard_map/ppermute | solution.py:486
  19.7 13.5 %collective-permute-start.10 = (bf16[96,2816]{1,0:T(8,128)(2,1)S(1)}, bf16[96,2816]{1,0:T(8,128)(2,1)S(1)}, u32[]{:S(2)}, u32[]{:S(2)}) collective-permute-start(bf16[96,2816]{1,0:T(8,128)(2,1)S(1)} %collective-permute-done.9.refs_1_.refs_9_), channel_id=1, source_target_pairs={{1,3},{3,5},{5,7},{7,6},{6,4},{4,2},{2,0},{0,1},{9,11},{11,13},{13... | collective-permute-start | bytes 1622024 | tf_op jit(solution)/shard_map/ppermute | solution.py:486
  21.4 12.9 %collective-permute-start.1 = (bf16[96,2816]{1,0:T(8,128)(2,1)S(1)}, bf16[96,2816]{1,0:T(8,128)(2,1)S(1)}, u32[]{:S(2)}, u32[]{:S(2)}) collective-permute-start(bf16[96,2816]{1,0:T(8,128)(2,1)S(1)} %collective-permute-done.refs_17_.refs_1_), channel_id=1, source_target_pairs={{1,0},{3,1},{5,3},{7,5},{6,7},{4,6},{2,4},{0,2},{9,8},{11,9},{13,1... | collective-permute-start | bytes 1622024 | tf_op jit(solution)/shard_map/ppermute | solution.py:486
  34.2 15.2 %collective-permute-start.18 = (bf16[96,2816]{1,0:T(8,128)(2,1)S(1)}, bf16[96,2816]{1,0:T(8,128)(2,1)S(1)}, u32[]{:S(2)}, u32[]{:S(2)}) collective-permute-start(bf16[96,2816]{1,0:T(8,128)(2,1)S(1)} %collective-permute-done.10.refs_2_.refs_10_), channel_id=1, source_target_pairs={{1,3},{3,5},{5,7},{7,6},{6,4},{4,2},{2,0},{0,1},{9,11},{11,13},{13... | collective-permute-start | bytes 1622024 | tf_op jit(solution)/shard_map/ppermute | solution.py:486
  35.8 15.2 %collective-permute-start.23 = (bf16[96,2816]{1,0:T(8,128)(2,1)S(1)}, bf16[96,2816]{1,0:T(8,128)(2,1)S(1)}, u32[]{:S(2)}, u32[]{:S(2)}) collective-permute-start(bf16[96,2816]{1,0:T(8,128)(2,1)S(1)} %collective-permute-done.1.refs_18_.refs_2_), channel_id=1, source_target_pairs={{1,0},{3,1},{5,3},{7,5},{6,7},{4,6},{2,4},{0,2},{9,8},{11,9},{13,1... | collective-permute-start | bytes 1622024 | tf_op jit(solution)/shard_map/ppermute | solution.py:486
  36.2 23.7 %collective-permute-start.11 = (bf16[96,2560]{1,0:T(8,128)(2,1)}, bf16[96,2560]{1,0:T(8,128)(2,1)S(1)}, u32[]{:S(2)}, u32[]{:S(2)}) collective-permute-start(bf16[96,2560]{1,0:T(8,128)(2,1)} %get-tuple-element.65.refs_0_), channel_id=1, source_target_pairs={{1,3},{3,5},{5,7},{7,6},{6,4},{4,2},{2,0},{0,1},{9,11},{11,13},{13... | collective-permute-start | bytes 1474568 | tf_op jit(solution)/shard_map/ppermute | solution.py:486
  37.8 23.7 %collective-permute-start.2 = (bf16[96,2560]{1,0:T(8,128)(2,1)}, bf16[96,2560]{1,0:T(8,128)(2,1)S(1)}, u32[]{:S(2)}, u32[]{:S(2)}) collective-permute-start(bf16[96,2560]{1,0:T(8,128)(2,1)} %get-tuple-element.62.refs_0_), channel_id=1, source_target_pairs={{1,0},{3,1},{5,3},{7,5},{6,7},{4,6},{2,4},{0,2},{9,8},{11,9},{13,1... | collective-permute-start | bytes 1474568 | tf_op jit(solution)/shard_map/ppermute | solution.py:486
  49.4 22.1 %collective-permute-start.19 = (bf16[96,2816]{1,0:T(8,128)(2,1)S(1)}, bf16[96,2816]{1,0:T(8,128)(2,1)S(1)}, u32[]{:S(2)}, u32[]{:S(2)}) collective-permute-start(bf16[96,2816]{1,0:T(8,128)(2,1)S(1)} %collective-permute-done.18.refs_3_.refs_11_), channel_id=1, source_target_pairs={{1,3},{3,5},{5,7},{7,6},{6,4},{4,2},{2,0},{0,1},{9,11},{11,13},{13... | collective-permute-start | bytes 1622024 | tf_op jit(solution)/shard_map/ppermute | solution.py:486
  51.0 22.1 %collective-permute-start.24 = (bf16[96,2816]{1,0:T(8,128)(2,1)S(1)}, bf16[96,2816]{1,0:T(8,128)(2,1)S(1)}, u32[]{:S(2)}, u32[]{:S(2)}) collective-permute-start(bf16[96,2816]{1,0:T(8,128)(2,1)S(1)} %collective-permute-done.23.refs_19_.refs_3_), channel_id=1, source_target_pairs={{1,0},{3,1},{5,3},{7,5},{6,7},{4,6},{2,4},{0,2},{9,8},{11,9},{13,1... | collective-permute-start | bytes 1622024 | tf_op jit(solution)/shard_map/ppermute | solution.py:486
  60.0 22.1 %collective-permute-start.12 = (bf16[96,2560]{1,0:T(8,128)(2,1)S(1)}, bf16[96,2560]{1,0:T(8,128)(2,1)S(1)}, u32[]{:S(2)}, u32[]{:S(2)}) collective-permute-start(bf16[96,2560]{1,0:T(8,128)(2,1)S(1)} %collective-permute-done.11.refs_1_), channel_id=1, source_target_pairs={{1,3},{3,5},{5,7},{7,6},{6,4},{4,2},{2,0},{0,1},{9,11},{11,13},{13... | collective-permute-start | bytes 1474568 | tf_op jit(solution)/shard_map/ppermute | solution.py:486
  61.5 22.1 %collective-permute-start.3 = (bf16[96,2560]{1,0:T(8,128)(2,1)S(1)}, bf16[96,2560]{1,0:T(8,128)(2,1)S(1)}, u32[]{:S(2)}, u32[]{:S(2)}) collective-permute-start(bf16[96,2560]{1,0:T(8,128)(2,1)S(1)} %collective-permute-done.2.refs_1_), channel_id=1, source_target_pairs={{1,0},{3,1},{5,3},{7,5},{6,7},{4,6},{2,4},{0,2},{9,8},{11,9},{13,1... | collective-permute-start | bytes 1474568 | tf_op jit(solution)/shard_map/ppermute | solution.py:486
  71.6 22.1 %collective-permute-start.20 = (bf16[96,2816]{1,0:T(8,128)(2,1)S(1)}, bf16[96,2816]{1,0:T(8,128)(2,1)S(1)}, u32[]{:S(2)}, u32[]{:S(2)}) collective-permute-start(bf16[96,2816]{1,0:T(8,128)(2,1)S(1)} %collective-permute-done.19.refs_4_.refs_12_), channel_id=1, source_target_pairs={{1,3},{3,5},{5,7},{7,6},{6,4},{4,2},{2,0},{0,1},{9,11},{11,13},{13... | collective-permute-start | bytes 1622024 | tf_op jit(solution)/shard_map/ppermute | solution.py:486
  73.1 22.1 %collective-permute-start.25 = (bf16[96,2816]{1,0:T(8,128)(2,1)S(1)}, bf16[96,2816]{1,0:T(8,128)(2,1)S(1)}, u32[]{:S(2)}, u32[]{:S(2)}) collective-permute-start(bf16[96,2816]{1,0:T(8,128)(2,1)S(1)} %collective-permute-done.24.refs_20_.refs_4_), channel_id=1, source_target_pairs={{1,0},{3,1},{5,3},{7,5},{6,7},{4,6},{2,4},{0,2},{9,8},{11,9},{13,1... | collective-permute-start | bytes 1622024 | tf_op jit(solution)/shard_map/ppermute | solution.py:486
  82.1 22.1 %collective-permute-start.13 = (bf16[96,2560]{1,0:T(8,128)(2,1)S(1)}, bf16[96,2560]{1,0:T(8,128)(2,1)S(1)}, u32[]{:S(2)}, u32[]{:S(2)}) collective-permute-start(bf16[96,2560]{1,0:T(8,128)(2,1)S(1)} %collective-permute-done.12.refs_2_), channel_id=1, source_target_pairs={{1,3},{3,5},{5,7},{7,6},{6,4},{4,2},{2,0},{0,1},{9,11},{11,13},{13... | collective-permute-start | bytes 1474568 | tf_op jit(solution)/shard_map/ppermute | solution.py:486
  83.7 22.1 %collective-permute-start.4 = (bf16[96,2560]{1,0:T(8,128)(2,1)S(1)}, bf16[96,2560]{1,0:T(8,128)(2,1)S(1)}, u32[]{:S(2)}, u32[]{:S(2)}) collective-permute-start(bf16[96,2560]{1,0:T(8,128)(2,1)S(1)} %collective-permute-done.3.refs_2_), channel_id=1, source_target_pairs={{1,0},{3,1},{5,3},{7,5},{6,7},{4,6},{2,4},{0,2},{9,8},{11,9},{13,1... | collective-permute-start | bytes 1474568 | tf_op jit(solution)/shard_map/ppermute | solution.py:486
  93.7 22.1 %collective-permute-start.21 = (bf16[96,2816]{1,0:T(8,128)(2,1)S(1)}, bf16[96,2816]{1,0:T(8,128)(2,1)S(1)}, u32[]{:S(2)}, u32[]{:S(2)}) collective-permute-start(bf16[96,2816]{1,0:T(8,128)(2,1)S(1)} %collective-permute-done.20.refs_5_.refs_13_), channel_id=1, source_target_pairs={{1,3},{3,5},{5,7},{7,6},{6,4},{4,2},{2,0},{0,1},{9,11},{11,13},{13... | collective-permute-start | bytes 1622024 | tf_op jit(solution)/shard_map/ppermute | solution.py:486
  95.3 22.1 %collective-permute-start.26 = (bf16[96,2816]{1,0:T(8,128)(2,1)S(1)}, bf16[96,2816]{1,0:T(8,128)(2,1)S(1)}, u32[]{:S(2)}, u32[]{:S(2)}) collective-permute-start(bf16[96,2816]{1,0:T(8,128)(2,1)S(1)} %collective-permute-done.25.refs_21_.refs_5_), channel_id=1, source_target_pairs={{1,0},{3,1},{5,3},{7,5},{6,7},{4,6},{2,4},{0,2},{9,8},{11,9},{13,1... | collective-permute-start | bytes 1622024 | tf_op jit(solution)/shard_map/ppermute | solution.py:486
  104.2 22.1 %collective-permute-start.14 = (bf16[96,2560]{1,0:T(8,128)(2,1)S(1)}, bf16[96,2560]{1,0:T(8,128)(2,1)S(1)}, u32[]{:S(2)}, u32[]{:S(2)}) collective-permute-start(bf16[96,2560]{1,0:T(8,128)(2,1)S(1)} %collective-permute-done.13.refs_3_), channel_id=1, source_target_pairs={{1,3},{3,5},{5,7},{7,6},{6,4},{4,2},{2,0},{0,1},{9,11},{11,13},{13... | collective-permute-start | bytes 1474568 | tf_op jit(solution)/shard_map/ppermute | solution.py:486
  105.8 22.1 %collective-permute-start.5 = (bf16[96,2560]{1,0:T(8,128)(2,1)S(1)}, bf16[96,2560]{1,0:T(8,128)(2,1)S(1)}, u32[]{:S(2)}, u32[]{:S(2)}) collective-permute-start(bf16[96,2560]{1,0:T(8,128)(2,1)S(1)} %collective-permute-done.4.refs_3_), channel_id=1, source_target_pairs={{1,0},{3,1},{5,3},{7,5},{6,7},{4,6},{2,4},{0,2},{9,8},{11,9},{13,1... | collective-permute-start | bytes 1474568 | tf_op jit(solution)/shard_map/ppermute | solution.py:486
  115.8 31.9 %collective-permute-start.22 = (bf16[96,2816]{1,0:T(8,128)(2,1)S(1)}, bf16[96,2816]{1,0:T(8,128)(2,1)S(1)}, u32[]{:S(2)}, u32[]{:S(2)}) collective-permute-start(bf16[96,2816]{1,0:T(8,128)(2,1)S(1)} %collective-permute-done.21.refs_6_.refs_14_), channel_id=1, source_target_pairs={{1,3},{3,5},{5,7},{7,6},{6,4},{4,2},{2,0},{0,1},{9,11},{11,13},{13... | collective-permute-start | bytes 1622024 | tf_op jit(solution)/shard_map/ppermute | solution.py:486
  117.4 30.3 %collective-permute-start.27 = (bf16[96,2816]{1,0:T(8,128)(2,1)S(1)}, bf16[96,2816]{1,0:T(8,128)(2,1)S(1)}, u32[]{:S(2)}, u32[]{:S(2)}) collective-permute-start(bf16[96,2816]{1,0:T(8,128)(2,1)S(1)} %collective-permute-done.26.refs_22_.refs_6_), channel_id=1, source_target_pairs={{1,0},{3,1},{5,3},{7,5},{6,7},{4,6},{2,4},{0,2},{9,8},{11,9},{13,1... | collective-permute-start | bytes 1622024 | tf_op jit(solution)/shard_map/ppermute | solution.py:486
  126.3 19.3 %collective-permute-start.15 = (bf16[96,2560]{1,0:T(8,128)(2,1)S(1)}, bf16[96,2560]{1,0:T(8,128)(2,1)S(1)}, u32[]{:S(2)}, u32[]{:S(2)}) collective-permute-start(bf16[96,2560]{1,0:T(8,128)(2,1)S(1)} %collective-permute-done.14.refs_4_), channel_id=1, source_target_pairs={{1,3},{3,5},{5,7},{7,6},{6,4},{4,2},{2,0},{0,1},{9,11},{11,13},{13... | collective-permute-start | bytes 1474568 | tf_op jit(solution)/shard_map/ppermute | solution.py:486
  127.9 19.3 %collective-permute-start.6 = (bf16[96,2560]{1,0:T(8,128)(2,1)S(1)}, bf16[96,2560]{1,0:T(8,128)(2,1)S(1)}, u32[]{:S(2)}, u32[]{:S(2)}) collective-permute-start(bf16[96,2560]{1,0:T(8,128)(2,1)S(1)} %collective-permute-done.5.refs_4_), channel_id=1, source_target_pairs={{1,0},{3,1},{5,3},{7,5},{6,7},{4,6},{2,4},{0,2},{9,8},{11,9},{13,1... | collective-permute-start | bytes 1474568 | tf_op jit(solution)/shard_map/ppermute | solution.py:486
  145.7 12.3 %collective-permute-start.16 = (bf16[96,2560]{1,0:T(8,128)(2,1)S(1)}, bf16[96,2560]{1,0:T(8,128)(2,1)S(1)}, u32[]{:S(2)}, u32[]{:S(2)}) collective-permute-start(bf16[96,2560]{1,0:T(8,128)(2,1)S(1)} %collective-permute-done.15.refs_5_), channel_id=1, source_target_pairs={{1,3},{3,5},{5,7},{7,6},{6,4},{4,2},{2,0},{0,1},{9,11},{11,13},{13... | collective-permute-start | bytes 1474568 | tf_op jit(solution)/shard_map/ppermute | solution.py:486
  147.3 10.7 %collective-permute-start.7 = (bf16[96,2560]{1,0:T(8,128)(2,1)S(1)}, bf16[96,2560]{1,0:T(8,128)(2,1)S(1)}, u32[]{:S(2)}, u32[]{:S(2)}) collective-permute-start(bf16[96,2560]{1,0:T(8,128)(2,1)S(1)} %collective-permute-done.6.refs_5_), channel_id=1, source_target_pairs={{1,0},{3,1},{5,3},{7,5},{6,7},{4,6},{2,4},{0,2},{9,8},{11,9},{13,1... | collective-permute-start | bytes 1474568 | tf_op jit(solution)/shard_map/ppermute | solution.py:486
  147.7 1.0 copy-start
  148.8 1.0 copy-start.2
  149.8 10.3 %copy-start.1 = (bf16[96,2816]{1,0:T(8,128)(2,1)S(1)}, bf16[96,2816]{1,0:T(8,128)(2,1)}, u32[]{:S(2)}) copy-start(bf16[96,2816]{1,0:T(8,128)(2,1)} %get-tuple-element.85.refs_16_.refs_0_) | copy-start | bytes 1622020
  158.0 10.8 %collective-permute-start.17 = (bf16[96,2560]{1,0:T(8,128)(2,1)S(1)}, bf16[96,2560]{1,0:T(8,128)(2,1)S(1)}, u32[]{:S(2)}, u32[]{:S(2)}) collective-permute-start(bf16[96,2560]{1,0:T(8,128)(2,1)S(1)} %collective-permute-done.16.refs_6_), channel_id=1, source_target_pairs={{1,3},{3,5},{5,7},{7,6},{6,4},{4,2},{2,0},{0,1},{9,11},{11,13},{13... | collective-permute-start | bytes 1474568 | tf_op jit(solution)/shard_map/ppermute | solution.py:486
  159.6 14.4 %collective-permute-start.8 = (bf16[96,2560]{1,0:T(8,128)(2,1)S(1)}, bf16[96,2560]{1,0:T(8,128)(2,1)S(1)}, u32[]{:S(2)}, u32[]{:S(2)}) collective-permute-start(bf16[96,2560]{1,0:T(8,128)(2,1)S(1)} %collective-permute-done.7.refs_6_), channel_id=1, source_target_pairs={{1,0},{3,1},{5,3},{7,5},{6,7},{4,6},{2,4},{0,2},{9,8},{11,9},{13,1... | collective-permute-start | bytes 1474568 | tf_op jit(solution)/shard_map/ppermute | solution.py:486
  160.1 8.8 %copy-start.4 = (bf16[96,2560]{1,0:T(8,128)(2,1)S(1)}, bf16[96,2560]{1,0:T(8,128)(2,1)}, u32[]{:S(2)}) copy-start(bf16[96,2560]{1,0:T(8,128)(2,1)} %get-tuple-element.65.refs_0_) | copy-start | bytes 1474564
  168.9 5.2 %copy-start.3 = (bf16[96,2560]{1,0:T(8,128)(2,1)S(1)}, bf16[96,2560]{1,0:T(8,128)(2,1)}, u32[]{:S(2)}) copy-start(bf16[96,2560]{1,0:T(8,128)(2,1)} %get-tuple-element.62.refs_0_) | copy-start | bytes 1474564
  179.5 5.3 %collective-permute-start.28 = (bf16[6,256,256]{2,1,0:T(8,128)(2,1)S(1)}, bf16[6,256,256]{2,1,0:T(8,128)(2,1)S(1)}, u32[]{:S(2)}, u32[]{:S(2)}) collective-permute-start(bf16[6,256,256]{2,1,0:T(8,128)(2,1)S(1)} %fold.1), channel_id=1, source_target_pairs={{24,16},{25,17},{26,18},{27,19},{28,20},{29,21},{30,22},{31,23}} | collective-permute-start | bytes 2359304 | tf_op jit(solution)/shard_map/ppermute | solution.py:519
  186.6 0.9 collective-permute-start.29
  189.4 15.2 %collective-permute-start.30 = (bf16[6,256,256]{2,1,0:T(8,128)(2,1)S(1)}, bf16[6,256,256]{2,1,0:T(8,128)(2,1)S(1)}, u32[]{:S(2)}, u32[]{:S(2)}) collective-permute-start(bf16[6,256,256]{2,1,0:T(8,128)(2,1)S(1)} %hop.3), channel_id=1, source_target_pairs={{8,0},{9,1},{10,2},{11,3},{12,4},{13,5},{14,6},{15,7}} | collective-permute-start | bytes 2359304 | tf_op jit(solution)/shard_map/ppermute | solution.py:519

commit v10 on v9

--- a/solution.py
+++ b/solution.py
@@ -18,67 +18,86 @@
 CLAIM = 60 * MIB
 
 
-def half_width(rows, count):
-    used = (count // 2 + 1) * rows
-    return used, -(-used // LANES) * LANES
-
-
 def nt(left, right):
     return lax.dot_general(left, right, (((1,), (1,)), ((), ())), preferred_element_type=F32)
 
 
 def packed_half(increment, place, count):
     rows, width = increment.shape
-    used, half = half_width(rows, count)
-    turned = pltpu.roll(increment, lax.rem(width - place * rows, width), 1)[:, :half]
-    column = lax.broadcasted_iota(jnp.int32, turned.shape, 1)
-    halved = (column < rows) | (column >= used - rows)
-    weight = jnp.where(column < used, jnp.where(halved, 0.5, 1.0), 0.0)
-    return (turned * weight).astype(BF16)
-
-
-def unpacked_half(piece, start, width):
-    piece = piece.astype(F32)
-    rest = width - piece.shape[1]
-    wide = jnp.concatenate([piece, jnp.zeros((piece.shape[0], rest), F32)], axis=1) if rest else piece
-    return pltpu.roll(wide, start, 1) if start else wide
-
-
-def pack_kernel(count, ranges, place_ref, gain_ref, increment_ref, terminal_ref, *packed_refs):
-    width = gain_ref.shape[2]
-    half = half_width(gain_ref.shape[1], count)[1]
-    stride = width + half
+    turned = pltpu.roll(increment, lax.rem(width - place * rows, width), 1)
+    column = lax.broadcasted_iota(jnp.int32, (rows, width // 2), 1)
+    main = turned[:, :width // 2] * jnp.where(column < rows, 0.5, 1.0)
+    opposite = turned[:, width // 2:width // 2 + LANES]
+    lower = opposite[rows // 2:]
+    side = jnp.concatenate([lower, pltpu.roll(lower, LANES - rows // 2, 1)], axis=0)
+    return main.astype(BF16), jnp.where(place < count // 2, opposite, side)
+
+
+def unpacked_half(main, extra, block, count):
+    rows = main.shape[0]
+    width = rows * count
+    column = lax.broadcasted_iota(jnp.int32, extra.shape, 1)
+    extra = jnp.where(column < rows // 2, extra, 0.0)
+    if block >= count // 2:
+        lower = extra[:rows // 2] + pltpu.roll(extra[rows // 2:], rows // 2, 1)
+        extra = jnp.concatenate([jnp.zeros_like(lower), lower], axis=0)
+    rest = jnp.zeros((rows, width // 2 - LANES), F32)
+    wide = jnp.concatenate([main.astype(F32), extra, rest], axis=1)
+    return pltpu.roll(wide, block * rows, 1) if block else wide
+
+
+def pack_kernel(count, ranges, place_ref, gain_ref, increment_ref, *refs):
+    outs = refs[-len(ranges):]
+    rows, width = gain_ref.shape[1:]
+    stride = width + width // 2
     place = place_ref[0]
-    for (low, high), packed_ref in zip(ranges, packed_refs):
-        for step in range(low, high):
-            base = (step - low) * stride
-            packed_ref[:, base:base + width] = gain_ref[step]
-            packed_ref[:, base + width:base + stride] = packed_half(increment_ref[step], place, count)
-    end = packed_half(terminal_ref[...], place, count)
-    for turn in range(2):
-        base = (ranges[turn][1] - ranges[turn][0]) * stride
-        packed_refs[turn][:, base:] = end[:, turn * half // 2:(turn + 1) * half // 2]
+    base = min(low for low, _ in ranges)
+    column = lax.broadcasted_iota(jnp.int32, (rows, LANES), 1)
+    for (low, high), packed_ref in zip(ranges, outs):
+        extras = jnp.zeros((rows, LANES), F32)
+        for step in range(high - low):
+            at = step * stride
+            main, extra = packed_half(increment_ref[low - base + step], place, count)
+            packed_ref[:, at:at + width] = gain_ref[low - base + step]
+            packed_ref[:, at + width:at + stride] = main
+            shift = step * rows // 2
+            here = (column >= shift) & (column < shift + rows // 2)
+            extras = jnp.where(here, pltpu.roll(extra, shift, 1) if shift else extra, extras)
+        packed_ref[:, (high - low) * stride:(high - low) * stride + LANES] = extras.astype(BF16)
+    if len(refs) > len(ranges):
+        main, extra = packed_half(refs[0][...], place, count)
+        at = (ranges[0][1] - ranges[0][0]) * stride + LANES
+        outs[0][:, at:] = main[:, :2 * LANES]
+        outs[1][:, at:at + LANES] = main[:, 2 * LANES:]
+        outs[1][:, at + LANES:] = extra.astype(BF16)
 
 
 def pack(place, gains, increments, terminal, count, ranges):
     rows, width = gains.shape[1:]
-    half = half_width(rows, count)[1]
-    lanes = [(high - low) * (width + half) + half // 2 * (n < 2) for n, (low, high) in enumerate(ranges)]
-    vmem = pl.BlockSpec(memory_space=pltpu.VMEM)
+    first, size = ranges[1][0], ranges[0][1] - ranges[1][0]
+    ends = [] if terminal is None else [terminal]
+    lanes = [(high - low) * (width + width // 2) + LANES * (1 + 2 * len(ends)) for low, high in ranges]
+    some = pl.BlockSpec((size, rows, width), lambda i, p: (first // size, 0, 0))
     return pl.pallas_call(
         functools.partial(pack_kernel, count, ranges),
-        in_specs=[pl.BlockSpec(memory_space=pltpu.SMEM), vmem, vmem, vmem],
-        out_specs=[vmem] * len(lanes),
-        out_shape=[jax.ShapeDtypeStruct((rows, size), BF16) for size in lanes],
-        compiler_params=pltpu.CompilerParams(vmem_limit_bytes=CLAIM),
+        grid_spec=pltpu.PrefetchScalarGridSpec(
+            num_scalar_prefetch=1,
+            grid=(1,),
+            in_specs=[some, some] + [pl.BlockSpec((rows, width), lambda i, p: (0, 0))] * len(ends),
+            out_specs=[pl.BlockSpec((rows, n), lambda i, p: (0, 0)) for n in lanes],
+        ),
+        out_shape=[jax.ShapeDtypeStruct((rows, n), BF16) for n in lanes],
+        compiler_params=pltpu.CompilerParams(vmem_limit_bytes=CLAIM if ends else 14 * MIB),
         name="pack",
-    )(place, gains, increments, terminal)
-
-
-def unpack(raw, half):
+    )(place, gains, increments, *ends)
+
+
+def unpack(raw, extras, step, half):
     count, rows, _ = raw.shape
+    shift = lax.rem(LANES - step * (rows // 2), LANES)
     for n in range(count):
-        half[n * rows:(n + 1) * rows, :] = unpacked_half(raw[n], n * rows, half.shape[1]).astype(BF16)
+        extra = pltpu.roll(extras[n].astype(F32), shift, 1)
+        half[n * rows:(n + 1) * rows, :] = unpacked_half(raw[n], extra, n, count).astype(BF16)
 
 
 def origins(place, cycle, way):
@@ -91,13 +110,14 @@
     return [look(cycle, lax.rem(spot - way * n + count, count)) for n in range(count)]
 
 
-def assemble(places, blocks, gain, fresh, raw):
+def assemble(places, blocks, sides, step, gain, fresh, raw, extras):
     rows = blocks[0].shape[0]
     width = gain.shape[0]
-    for place, block in zip(places, blocks):
+    for place, block, side in zip(places, blocks, sides):
         gain[pl.ds(pl.multiple_of(place * rows, 16), rows), :] = block[:, :width]
         raw[place] = block[:, width:]
-    unpack(raw, fresh)
+        extras[place] = side[...]
+    unpack(raw, extras, step, fresh)
 
 
 def advance(gain, half, fresh, middle):
@@ -127,28 +147,31 @@
 def compose_kernel(cycle, way, first, last_ref, place_ref, *refs):
     count = len(cycle)
     places = origins(place_ref[0], cycle, way)
-    blocks, refs = refs[:count], refs[count:]
+    blocks, sides, refs = refs[:count], refs[count:2 * count], refs[2 * count:]
     if first:
-        ends, refs = refs[:2 * count], refs[2 * count:]
+        ends, refs = refs[:4 * count], refs[4 * count:]
     else:
         half_in, factor_in, refs = refs[0], refs[1], refs[4:]
-    factor_out, own_out, mine_out, half, gain, factor, fresh, middle, raw = refs
+    factor_out, own_out, mine_out, half, gain, factor, fresh, middle, raw, extras = refs
     rows = blocks[0].shape[0]
 
     @pl.when(pl.program_id(0) == 0)
     def _():
         if first:
             scale = jnp.where(last_ref[0] == 1, 1.0, 0.0).astype(BF16)
-            cut = ends[0].shape[1]
-            for n, end in enumerate(ends):
-                spots = places if n < count else origins(place_ref[0], cycle, -way)
-                raw[spots[n % count], :, n // count * cut:(n // count + 1) * cut] = end[...] * scale
-            unpack(raw, half)
+            back = origins(place_ref[0], cycle, -way)
+            for n in range(count):
+                raw[places[n], :, :LANES] = ends[n][...] * scale
+                raw[places[n], :, LANES:2 * LANES] = ends[count + n][...] * scale
+                raw[back[n], :, 2 * LANES:] = ends[2 * count + n][...] * scale
+                extras[back[n]] = ends[3 * count + n][...] * scale
+            unpack(raw, extras, 0, half)
         else:
             factor[...] = factor_in[0]
             half[...] = half_in[...]
 
-    assemble(places, blocks, gain, fresh, raw)
+    step = pl.num_programs(0) - 1 - pl.program_id(0)
+    assemble(places, blocks, sides, step, gain, fresh, raw, extras)
     if first:
 
         @pl.when(pl.program_id(0) == 0)
@@ -171,27 +194,42 @@
     return pl.BlockSpec((1, width, width), lambda i, *p: (place(i), 0, 0))
 
 
+def row_specs(blocks, turns):
+    rows = blocks[0].shape[0]
+    stride = rows * len(blocks) * 3 // 2
+    step = pl.BlockSpec((rows, stride), lambda i, *p: (0, turns - 1 - i))
+    side = pl.BlockSpec((rows, LANES), lambda i, *p: (0, turns * stride // LANES), pipeline_mode=pl.Buffered(1))
+    return [step] * len(blocks) + [side] * len(blocks)
+
+
+def row_scratch(count, rows):
+    width = count * rows
+    return [pltpu.VMEM((width, width), BF16)] * 4 + [
+        pltpu.VMEM((count, rows, width // 2), BF16),
+        pltpu.VMEM((count, rows, LANES), BF16),
+    ]
+
+
 def compose(last, place, cycle, way, blocks, ends, state, half, low, turns, steps):
     count = len(blocks)
     rows = blocks[0].shape[0]
     width = rows * count
-    lanes = half_width(rows, count)[1]
-    stride = width + lanes
     first = state is None
     anywhere = pl.BlockSpec(memory_space=pl.ANY)
-    in_specs = [pl.BlockSpec((rows, stride), lambda i, *p: (0, turns - 1 - i))] * count
+    in_specs = row_specs(blocks, turns)
     if first:
-        at = turns * stride // (lanes // 2)
-        in_specs += [
-            pl.BlockSpec((rows, lanes // 2), lambda i, *p: (0, at), pipeline_mode=pl.Buffered(1))
-        ] * len(ends)
-        args = ends
+        at = turns * width * 3 // 2 // LANES + 1
+        for n in (at, at + 1):
+            tile = pl.BlockSpec((rows, LANES), lambda i, *p, n=n: (0, n), pipeline_mode=pl.Buffered(1))
+            in_specs += [tile] * count
+        in_specs += in_specs[-2 * count:]
+        args = ends[:count] * 2 + ends[count:] * 2
     else:
         after = pl.BlockSpec((1, width, width), lambda i, *p: (low + turns, 0, 0), pipeline_mode=pl.Buffered(1))
         in_specs += [square(width), after, anywhere, anywhere]
         args = [half, *state]
     band = pl.BlockSpec((1, rows, width), lambda i, *p: (low + turns - 1 - i, 0, 0))
-    base = 2 + count + 1
+    base = 2 + 2 * count + 1
     return pl.pallas_call(
         functools.partial(compose_kernel, cycle, way, first),
         grid_spec=pltpu.PrefetchScalarGridSpec(
@@ -199,7 +237,7 @@
             grid=(turns,),
             in_specs=in_specs,
             out_specs=[square(width, lambda i: low + turns - 1 - i), band, band, square(width)],
-            scratch_shapes=[pltpu.VMEM((width, width), BF16)] * 4 + [pltpu.VMEM((count, rows, lanes), BF16)],
+            scratch_shapes=row_scratch(count, rows),
         ),
         out_shape=[
             jax.ShapeDtypeStruct((steps, width, width), BF16),
@@ -213,21 +251,22 @@
             flops=6 * turns * width**3, bytes_accessed=8 * turns * width * width, transcendentals=0
         ),
         name="compose",
-    )(last, place, *blocks, *args)
+    )(last, place, *blocks, *blocks, *args)
 
 
 def chain_kernel(cycle, way, place_ref, *refs):
     count = len(cycle)
     places = origins(place_ref[0], cycle, way)
-    blocks, refs = refs[:count], refs[count:]
-    half_in, refs = refs[0], refs[-7:]
-    gain_out, half_out, gain, half, fresh, middle, raw = refs
+    blocks, sides, refs = refs[:count], refs[count:2 * count], refs[2 * count:]
+    half_in, refs = refs[0], refs[-8:]
+    gain_out, half_out, gain, half, fresh, middle, raw, extras = refs
 
     @pl.when(pl.program_id(0) == 0)
     def _():
         half[...] = half_in[...].reshape(half.shape)
 
-    assemble(places, blocks, gain, fresh, raw)
+    step = pl.num_programs(0) - 1 - pl.program_id(0)
+    assemble(places, blocks, sides, step, gain, fresh, raw, extras)
     gain_out[0] = gain[...]
     advance(gain, half, fresh, middle)
     half_out[0] = half[...]
@@ -237,9 +276,8 @@
     count = len(blocks)
     rows = blocks[0].shape[0]
     width = rows * count
-    lanes = half_width(rows, count)[1]
     anywhere = pl.BlockSpec(memory_space=pl.ANY)
-    in_specs = [pl.BlockSpec((rows, width + lanes), lambda i, *p: (0, turns - 1 - i))] * count
+    in_specs = row_specs(blocks, turns)
     if state is None:
         in_specs += [square(width)]
         args = [half]
@@ -257,16 +295,16 @@
             grid=(turns,),
             in_specs=in_specs,
             out_specs=[whole, whole],
-            scratch_shapes=[pltpu.VMEM((width, width), BF16)] * 4 + [pltpu.VMEM((count, rows, lanes), BF16)],
+            scratch_shapes=row_scratch(count, rows),
         ),
         out_shape=[jax.ShapeDtypeStruct((steps, width, width), BF16)] * 2,
-        input_output_aliases={} if state is None else {1 + count + 1: 0, 1 + count: 1},
+        input_output_aliases={} if state is None else {1 + 2 * count + 1: 0, 1 + 2 * count: 1},
         compiler_params=pltpu.CompilerParams(vmem_limit_bytes=18 * MIB),
         cost_estimate=pl.CostEstimate(
             flops=4 * turns * width**3, bytes_accessed=8 * turns * width * width, transcendentals=0
         ),
         name="chain",
-    )(place, *blocks, *args)
+    )(place, *blocks, *blocks, *args)
 
 
 def factors_kernel(place_ref, gain_ref, factor_in, mine_ref, factor_out, mine_out, factor):
@@ -486,8 +524,9 @@
         return lax.ppermute(array, "tile", [(cycle[n], cycle[(n + way) % count]) for n in range(count)])
 
     ranges = pieces(steps)
-    own = pack(place, gains, increments, terminal, count, ranges)
-    own, last = lax.optimization_barrier((own, last))
+    own = list(pack(place, gains, increments, terminal, count, ranges[:2]))
+    own += pack(place, gains, increments, None, count, ranges[2:])
+    own[:2], last = lax.optimization_barrier((own[:2], last))
     arrived = []
     for turn, array in enumerate(own):
         way = 1 if turn % 2 == 0 else -1

time: 212 us -> 206 us (0.972)
  waiting for transfers between devices: 128 us -> 121 us
  Pallas kernels: 48.8 us -> 51.8 us
    ppermute x28, waiting for transfers between devices: 116 us -> 109 us  [passed(): lax.ppermute(array, 'tile', [(cycle[n], cycle[(n + way) % count]) for n i...]
    pallas_call x1 -> x2, Pallas kernels: 4.16 us -> 4.27 us  [pack(): pl.pallas_call(functools.partial(pack_kernel, count, ranges), grid_spec=p...]
  transfers between devices with their start and end apart: 31 -> 31, of which waited for: 13 -> 13; matrix products, arithmetic and copies ran while one was open for 0% -> 0% of each run, Pallas kernels for 14% -> 15%
where the time goes in v10:
time: 206 us
  waiting for transfers between devices  121 us (59%)
  Pallas kernels  51.8 us (25%)
  starting transfers between devices  32.4 us (16%)
    ppermute x28, waiting for transfers between devices, passed(): lax.ppermute(array, 'tile', [(cycle[n], cycle[(n + way) % count]) for n i...  109 us
    ppermute x28, starting transfers between devices, passed(): lax.ppermute(array, 'tile', [(cycle[n], cycle[(n + way) % count]) for n i...  29.5 us
    pallas_call x2, Pallas kernels, compose(): pl.pallas_call(functools.partial(compose_kernel, cycle, way, first), grid...  18.5 us
    ppermute x3, waiting for transfers between devices, local(): lax.ppermute(hop(factors, early[1], packed), 'tm', [(turn, turn - 1)])  12.1 us
    pallas_call x2, Pallas kernels, chain(): pl.pallas_call(functools.partial(chain_kernel, cycle, way), grid_spec=plt...  11.7 us
    pallas_call x1, Pallas kernels, finish(): pl.pallas_call(functools.partial(finish_kernel, len(packed)), grid=(steps...  6.8 us
    pallas_call x1, Pallas kernels, extend_factors(): pl.pallas_call(factors_kernel, grid_spec=pltpu.PrefetchScalarGridSpec(num...  4.55 us
    pallas_call x2, Pallas kernels, pack(): pl.pallas_call(functools.partial(pack_kernel, count, ranges), grid_spec=p...  4.27 us
  transfers between devices with their start and end apart: 31, of which 13 were waited for; matrix products, arithmetic and copies ran while one was open for 0% of the time, Pallas kernels for 15%

profile of v10, /device:TPU:0, one launch (start us, length us, event | category | flops | bytes accessed | tf_op | source)
XLA Modules:
  0.0 205.6 jit_solution(6663439555971051232)
XLA Ops:
  0.0 3.5 %pack.3 = (bf16[96,2688]{1,0:T(8,128)(2,1)}, bf16[96,2688]{1,0:T(8,128)(2,1)}) custom-call(s32[1]{0:T(128)} %bitcast.place_ref, bf16[8,96,768]{2,1,0:T(8,128)(2,1)} %gain_ref.3, f32[8,96,768]{2,1,0:T(8,128)} %increment_ref.3, f32[96,768]{1,0:T(8,128)} %refs_0_.1), custom_call_target="tpu_custom_call" | custom-call | tf_op jit(solution)/shard_map/pack/pallas_call | solution.py:81
  3.6 3.0 %collective-permute-start.9 = (bf16[96,2688]{1,0:T(8,128)(2,1)}, bf16[96,2688]{1,0:T(8,128)(2,1)S(1)}, u32[]{:S(2)}, u32[]{:S(2)}) collective-permute-start(bf16[96,2688]{1,0:T(8,128)(2,1)} %get-tuple-element.65.refs_0_.refs_8_.refs_16_.refs_24_), channel_id=1, source_target_pairs={{1,3},{3,5},{5,7},{7,6},{6,4},{4,2},{2,0},{0,1},{9,11},{11,13},{13... | collective-permute-start | bytes 1548296 | tf_op jit(solution)/shard_map/ppermute | solution.py:524
  6.6 12.0 %collective-permute-done.9.refs_1_.refs_9_.refs_17_.refs_25_ = bf16[96,2688]{1,0:T(8,128)(2,1)S(1)} collective-permute-done((bf16[96,2688]{1,0:T(8,128)(2,1)}, bf16[96,2688]{1,0:T(8,128)(2,1)S(1)}, u32[]{:S(2)}, u32[]{:S(2)}) %collective-permute-start.9) | collective-permute-done | bytes 516128 | tf_op jit(solution)/shard_map/ppermute | solution.py:524
  18.6 1.6 collective-permute-start.10
  20.6 0.7 pack.2
  21.4 10.2 %collective-permute-done.10.refs_2_.refs_10_.refs_18_.refs_26_ = bf16[96,2688]{1,0:T(8,128)(2,1)S(1)} collective-permute-done((bf16[96,2688]{1,0:T(8,128)(2,1)S(1)}, bf16[96,2688]{1,0:T(8,128)(2,1)S(1)}, u32[]{:S(2)}, u32[]{:S(2)}) %collective-permute-start.10) | collective-permute-done | bytes 516128 | tf_op jit(solution)/shard_map/ppermute | solution.py:524
  31.5 1.0 collective-permute-done.1.refs_34_.refs_42_.refs_2_.refs_10_
  32.6 1.6 collective-permute-start.18
  34.6 1.6 collective-permute-start.11
  36.6 10.6 %collective-permute-done.18.refs_3_.refs_11_.refs_19_.refs_27_ = bf16[96,2688]{1,0:T(8,128)(2,1)S(1)} collective-permute-done((bf16[96,2688]{1,0:T(8,128)(2,1)S(1)}, bf16[96,2688]{1,0:T(8,128)(2,1)S(1)}, u32[]{:S(2)}, u32[]{:S(2)}) %collective-permute-start.18) | collective-permute-done | bytes 516128 | tf_op jit(solution)/shard_map/ppermute | solution.py:524
  47.2 1.6 collective-permute-start.19
  48.8 0.5 collective-permute-start.24
  49.3 8.0 %collective-permute-done.11.refs_1_.refs_9_ = bf16[96,2432]{1,0:T(8,128)(2,1)S(1)} collective-permute-done((bf16[96,2432]{1,0:T(8,128)(2,1)S(1)}, bf16[96,2432]{1,0:T(8,128)(2,1)S(1)}, u32[]{:S(2)}, u32[]{:S(2)}) %collective-permute-start.11) | collective-permute-done | bytes 466976 | tf_op jit(solution)/shard_map/ppermute | solution.py:524
  57.3 1.6 collective-permute-start.12
  58.8 0.5 collective-permute-start.3
  59.3 9.0 %collective-permute-done.19.refs_4_.refs_12_.refs_20_.refs_28_ = bf16[96,2688]{1,0:T(8,128)(2,1)S(1)} collective-permute-done((bf16[96,2688]{1,0:T(8,128)(2,1)S(1)}, bf16[96,2688]{1,0:T(8,128)(2,1)S(1)}, u32[]{:S(2)}, u32[]{:S(2)}) %collective-permute-start.19) | collective-permute-done | bytes 516128 | tf_op jit(solution)/shard_map/ppermute | solution.py:524
  68.3 1.6 collective-permute-start.20
  69.9 0.5 collective-permute-start.25
  70.3 8.0 %collective-permute-done.12.refs_2_.refs_10_ = bf16[96,2432]{1,0:T(8,128)(2,1)S(1)} collective-permute-done((bf16[96,2432]{1,0:T(8,128)(2,1)S(1)}, bf16[96,2432]{1,0:T(8,128)(2,1)S(1)}, u32[]{:S(2)}, u32[]{:S(2)}) %collective-permute-start.12) | collective-permute-done | bytes 466976 | tf_op jit(solution)/shard_map/ppermute | solution.py:524
  78.3 1.6 collective-permute-start.13
  79.9 0.5 collective-permute-start.4
  80.3 9.0 %collective-permute-done.20.refs_5_.refs_13_.refs_21_.refs_29_ = bf16[96,2688]{1,0:T(8,128)(2,1)S(1)} collective-permute-done((bf16[96,2688]{1,0:T(8,128)(2,1)S(1)}, bf16[96,2688]{1,0:T(8,128)(2,1)S(1)}, u32[]{:S(2)}, u32[]{:S(2)}) %collective-permute-start.20) | collective-permute-done | bytes 516128 | tf_op jit(solution)/shard_map/ppermute | solution.py:524
  89.4 1.6 collective-permute-start.21
  91.0 0.5 collective-permute-start.26
  91.4 8.0 %collective-permute-done.13.refs_3_.refs_11_ = bf16[96,2432]{1,0:T(8,128)(2,1)S(1)} collective-permute-done((bf16[96,2432]{1,0:T(8,128)(2,1)S(1)}, bf16[96,2432]{1,0:T(8,128)(2,1)S(1)}, u32[]{:S(2)}, u32[]{:S(2)}) %collective-permute-start.13) | collective-permute-done | bytes 466976 | tf_op jit(solution)/shard_map/ppermute | solution.py:524
  99.4 1.6 collective-permute-start.14
  101.0 0.5 collective-permute-start.5
  101.4 9.0 %collective-permute-done.21.refs_6_.refs_14_.refs_22_.refs_30_ = bf16[96,2688]{1,0:T(8,128)(2,1)S(1)} collective-permute-done((bf16[96,2688]{1,0:T(8,128)(2,1)S(1)}, bf16[96,2688]{1,0:T(8,128)(2,1)S(1)}, u32[]{:S(2)}, u32[]{:S(2)}) %collective-permute-start.21) | collective-permute-done | bytes 516128 | tf_op jit(solution)/shard_map/ppermute | solution.py:524
  110.4 1.6 collective-permute-start.22
  112.5 8.0 %collective-permute-done.14.refs_4_.refs_12_ = bf16[96,2432]{1,0:T(8,128)(2,1)S(1)} collective-permute-done((bf16[96,2432]{1,0:T(8,128)(2,1)S(1)}, bf16[96,2432]{1,0:T(8,128)(2,1)S(1)}, u32[]{:S(2)}, u32[]{:S(2)}) %collective-permute-start.14) | collective-permute-done | bytes 466976 | tf_op jit(solution)/shard_map/ppermute | solution.py:524
  120.5 1.6 collective-permute-start.15
  122.5 16.3 %collective-permute-done.15.refs_5_.refs_13_ = bf16[96,2432]{1,0:T(8,128)(2,1)S(1)} collective-permute-done((bf16[96,2432]{1,0:T(8,128)(2,1)S(1)}, bf16[96,2432]{1,0:T(8,128)(2,1)S(1)}, u32[]{:S(2)}, u32[]{:S(2)}) %collective-permute-start.15) | collective-permute-done | bytes 466976 | tf_op jit(solution)/shard_map/ppermute | solution.py:524
  138.7 1.6 collective-permute-start.16
  140.8 9.6 %compose.2 = (bf16[8,768,768]{2,1,0:T(8,128)(2,1)S(1)}, f32[8,96,768]{2,1,0:T(8,128)S(1)}, bf16[8,96,768]{2,1,0:T(8,128)(2,1)S(1)}, bf16[768,768]{1,0:T(8,128)(2,1)S(1)}) custom-call(s32[1]{0:T(128)} %bitcast.1.last_ref, s32[1]{0:T(128)} %bitcast.place_ref, bf16[96,2688]{1,0:T(8,128)(2,1)S(1)} %copy-done.1, ...), custom_call_target="tpu_custom_call" | custom-call | flops 5435817984 | bytes 9437184 | tf_op jit(solution)/shard_map/compose/pallas_call | solution.py:233
  150.4 1.6 collective-permute-start.17
  152.0 0.5 collective-permute-start.8
  152.5 8.9 %compose.3 = (bf16[8,768,768]{2,1,0:T(8,128)(2,1)S(1)}, f32[8,96,768]{2,1,0:T(8,128)S(1)}, bf16[8,96,768]{2,1,0:T(8,128)(2,1)S(1)}, bf16[768,768]{1,0:T(8,128)(2,1)S(1)}) custom-call(s32[1]{0:T(128)} %bitcast.1.last_ref, s32[1]{0:T(128)} %bitcast.place_ref, ...), custom_call_target="tpu_custom_call", output_to_operand_aliasing={{0}: (19, {}), {1}: (20, {}), {2}: (21, {})} | custom-call | flops 5435817984 | bytes 9437184 | tf_op jit(solution)/shard_map/compose/pallas_call | solution.py:233
  161.4 5.9 %chain.2 = (bf16[4,768,768]{2,1,0:T(8,128)(2,1)S(1)}, bf16[4,768,768]{2,1,0:T(8,128)(2,1)S(1)}) custom-call(s32[1]{0:T(128)} %bitcast.place_ref, bf16[96,2432]{1,0:T(8,128)(2,1)S(1)} %get-tuple-element.61.refs_0_.refs_8_, bf16[96,2432]{1,0:T(8,128)(2,1)S(1)} %collective-permute-done.11.refs_1_.refs_9_, ...), custom_call_target="tpu_custom_call" | custom-call | flops 3623878656 | bytes 9437184 | tf_op jit(solution)/shard_map/chain/pallas_call | solution.py:291
  167.3 5.9 %chain.3 = (bf16[4,768,768]{2,1,0:T(8,128)(2,1)S(1)}, bf16[4,768,768]{2,1,0:T(8,128)(2,1)S(1)}) custom-call(s32[1]{0:T(128)} %bitcast.place_ref, bf16[96,2432]{1,0:T(8,128)(2,1)S(1)} %get-tuple-element.58.refs_0_.refs_8_, bf16[96,2432]{1,0:T(8,128)(2,1)S(1)} %collective-permute-done.2.refs_1_.refs_9_, ...), custom_call_target="tpu_custom_call", output_to_operand_aliasing={{0}: (18, {}), {1}: (17, {})} | custom-call | flops 3623878656 | bytes 9437184 | tf_op jit(solution)/shard_map/chain/pallas_call | solution.py:291
  173.4 0.9 collective-permute-start.28
  174.4 4.5 %extend_factors.1 = (bf16[8,768,768]{2,1,0:T(8,128)(2,1)S(1)}, bf16[8,96,768]{2,1,0:T(8,128)(2,1)S(1)}) custom-call(s32[1]{0:T(128)} %bitcast.place_ref, bf16[4,768,768]{2,1,0:T(8,128)(2,1)S(1)} %get-tuple-element.96.gain_ref, bf16[8,768,768]{2,1,0:T(8,128)(2,1)S(1)} %get-tuple-element.97.factor_in, ...), custom_call_target="tpu_custom_call", output_to_operand_aliasing={{0}: (2, {}), {1}: (3, {})} | custom-call | flops 3623878656 | bytes 9437184 | tf_op jit(solution)/shard_map/extend_factors/pallas_call | solution.py:327
  179.0 1.8 hop.2
  180.8 0.7 collective-permute-start.29
  181.5 1.8 hop.3
  183.3 1.3 collective-permute-start.30
  184.6 2.1 %own_rows.1.own_ref = f32[8,96,768]{2,1,0:T(8,128)S(1)} custom-call(s32[1]{0:T(128)} %bitcast.place_ref, bf16[4,768,768]{2,1,0:T(8,128)(2,1)S(1)} %get-tuple-element.100.half_ref, f32[8,96,768]{2,1,0:T(8,128)S(1)} %get-tuple-element.101.own_ref), custom_call_target="tpu_custom_call", output_to_operand_aliasing={{}: (2, {})} | custom-call | flops 452984832 | bytes 4718592 | tf_op jit(solution)/shard_map/own_rows/pallas_call | solution.py:361
  186.7 12.1 %collective-permute-done.30.refs_2_ = bf16[6,256,256]{2,1,0:T(8,128)(2,1)S(1)} collective-permute-done((bf16[6,256,256]{2,1,0:T(8,128)(2,1)S(1)}, bf16[6,256,256]{2,1,0:T(8,128)(2,1)S(1)}, u32[]{:S(2)}, u32[]{:S(2)}) %collective-permute-start.30) | collective-permute-done | bytes 786464 | tf_op jit(solution)/shard_map/ppermute | solution.py:558
  198.8 6.8 %finish.1 = f32[8,96,768]{2,1,0:T(8,128)} custom-call(bf16[8,768,768]{2,1,0:T(8,128)(2,1)S(1)} %get-tuple-element.99.factor_ref, f32[8,96,768]{2,1,0:T(8,128)S(1)} %own_rows.1.own_ref, bf16[8,96,768]{2,1,0:T(8,128)(2,1)S(1)} %get-tuple-element.102.mine_ref, bf16[6,256,256]{2,1,0:T(8,128)(2,1)S(1)} %collective-permute-done.28.refs_0_, ...), custom_call_target="tpu_custom_call" | custom-call | tf_op jit(solution)/shard_map/finish/pallas_call | solution.py:483
  (34 shorter events, 3.1 us)
Async XLA Ops:
  0.0 20.6 %copy-start.3 = (bf16[8,96,768]{2,1,0:T(8,128)(2,1)S(1)}, bf16[8,96,768]{2,1,0:T(8,128)(2,1)}, u32[]{:S(2)}) copy-start(bf16[8,96,768]{2,1,0:T(8,128)(2,1)} %gain_ref.3) | copy-start | bytes 3538948
  0.0 20.6 %copy-start = (f32[8,96,768]{2,1,0:T(8,128)S(1)}, f32[8,96,768]{2,1,0:T(8,128)}, u32[]{:S(2)}) copy-start(f32[8,96,768]{2,1,0:T(8,128)} %increment_ref.3) | copy-start | bytes 7077892
  3.5 137.2 %copy-start.1 = (bf16[96,2688]{1,0:T(8,128)(2,1)S(1)}, bf16[96,2688]{1,0:T(8,128)(2,1)}, u32[]{:S(2)}) copy-start(bf16[96,2688]{1,0:T(8,128)(2,1)} %get-tuple-element.65.refs_0_.refs_8_.refs_16_.refs_24_) | copy-start | bytes 1548292
  3.6 137.2 %copy-start.2 = (bf16[96,2688]{1,0:T(8,128)(2,1)S(1)}, bf16[96,2688]{1,0:T(8,128)(2,1)}, u32[]{:S(2)}) copy-start(bf16[96,2688]{1,0:T(8,128)(2,1)} %get-tuple-element.81.refs_32_.refs_40_.refs_0_.refs_8_) | copy-start | bytes 1548292
  3.6 15.0 %collective-permute-start.9 = (bf16[96,2688]{1,0:T(8,128)(2,1)}, bf16[96,2688]{1,0:T(8,128)(2,1)S(1)}, u32[]{:S(2)}, u32[]{:S(2)}) collective-permute-start(bf16[96,2688]{1,0:T(8,128)(2,1)} %get-tuple-element.65.refs_0_.refs_8_.refs_16_.refs_24_), channel_id=1, source_target_pairs={{1,3},{3,5},{5,7},{7,6},{6,4},{4,2},{2,0},{0,1},{9,11},{11,13},{13... | collective-permute-start | bytes 1548296 | tf_op jit(solution)/shard_map/ppermute | solution.py:524
  6.5 13.7 %collective-permute-start = (bf16[96,2688]{1,0:T(8,128)(2,1)}, bf16[96,2688]{1,0:T(8,128)(2,1)S(1)}, u32[]{:S(2)}, u32[]{:S(2)}) collective-permute-start(bf16[96,2688]{1,0:T(8,128)(2,1)} %get-tuple-element.81.refs_32_.refs_40_.refs_0_.refs_8_), channel_id=1, source_target_pairs={{1,0},{3,1},{5,3},{7,5},{6,7},{4,6},{2,4},{0,2},{9,8},{11,9},{13,1... | collective-permute-start | bytes 1548296 | tf_op jit(solution)/shard_map/ppermute | solution.py:524
  18.6 12.9 %collective-permute-start.10 = (bf16[96,2688]{1,0:T(8,128)(2,1)S(1)}, bf16[96,2688]{1,0:T(8,128)(2,1)S(1)}, u32[]{:S(2)}, u32[]{:S(2)}) collective-permute-start(bf16[96,2688]{1,0:T(8,128)(2,1)S(1)} %collective-permute-done.9.refs_1_.refs_9_.refs_17_.refs_25_), channel_id=1, source_target_pairs={{1,3},{3,5},{5,7},{7,6},{6,4},{4,2},{2,0},{0,1},{9,11},{11,13},{13... | collective-permute-start | bytes 1548296 | tf_op jit(solution)/shard_map/ppermute | solution.py:524
  20.2 12.3 %collective-permute-start.1 = (bf16[96,2688]{1,0:T(8,128)(2,1)S(1)}, bf16[96,2688]{1,0:T(8,128)(2,1)S(1)}, u32[]{:S(2)}, u32[]{:S(2)}) collective-permute-start(bf16[96,2688]{1,0:T(8,128)(2,1)S(1)} %collective-permute-done.refs_33_.refs_41_.refs_1_.refs_9_), channel_id=1, source_target_pairs={{1,0},{3,1},{5,3},{7,5},{6,7},{4,6},{2,4},{0,2},{9,8},{11,9},{13,1... | collective-permute-start | bytes 1548296 | tf_op jit(solution)/shard_map/ppermute | solution.py:524
  32.6 14.7 %collective-permute-start.18 = (bf16[96,2688]{1,0:T(8,128)(2,1)S(1)}, bf16[96,2688]{1,0:T(8,128)(2,1)S(1)}, u32[]{:S(2)}, u32[]{:S(2)}) collective-permute-start(bf16[96,2688]{1,0:T(8,128)(2,1)S(1)} %collective-permute-done.10.refs_2_.refs_10_.refs_18_.refs_26_), channel_id=1, source_target_pairs={{1,3},{3,5},{5,7},{7,6},{6,4},{4,2},{2,0},{0,1},{9,11},{11,13},{13... | collective-permute-start | bytes 1548296 | tf_op jit(solution)/shard_map/ppermute | solution.py:524
  34.1 14.7 %collective-permute-start.23 = (bf16[96,2688]{1,0:T(8,128)(2,1)S(1)}, bf16[96,2688]{1,0:T(8,128)(2,1)S(1)}, u32[]{:S(2)}, u32[]{:S(2)}) collective-permute-start(bf16[96,2688]{1,0:T(8,128)(2,1)S(1)} %collective-permute-done.1.refs_34_.refs_42_.refs_2_.refs_10_), channel_id=1, source_target_pairs={{1,0},{3,1},{5,3},{7,5},{6,7},{4,6},{2,4},{0,2},{9,8},{11,9},{13,1... | collective-permute-start | bytes 1548296 | tf_op jit(solution)/shard_map/ppermute | solution.py:524
  34.6 22.7 %collective-permute-start.11 = (bf16[96,2432]{1,0:T(8,128)(2,1)S(1)}, bf16[96,2432]{1,0:T(8,128)(2,1)S(1)}, u32[]{:S(2)}, u32[]{:S(2)}) collective-permute-start(bf16[96,2432]{1,0:T(8,128)(2,1)S(1)} %get-tuple-element.61.refs_0_.refs_8_), channel_id=1, source_target_pairs={{1,3},{3,5},{5,7},{7,6},{6,4},{4,2},{2,0},{0,1},{9,11},{11,13},{13... | collective-permute-start | bytes 1400840 | tf_op jit(solution)/shard_map/ppermute | solution.py:524
  36.2 22.7 %collective-permute-start.2 = (bf16[96,2432]{1,0:T(8,128)(2,1)S(1)}, bf16[96,2432]{1,0:T(8,128)(2,1)S(1)}, u32[]{:S(2)}, u32[]{:S(2)}) collective-permute-start(bf16[96,2432]{1,0:T(8,128)(2,1)S(1)} %get-tuple-element.58.refs_0_.refs_8_), channel_id=1, source_target_pairs={{1,0},{3,1},{5,3},{7,5},{6,7},{4,6},{2,4},{0,2},{9,8},{11,9},{13,1... | collective-permute-start | bytes 1400840 | tf_op jit(solution)/shard_map/ppermute | solution.py:524
  47.2 21.1 %collective-permute-start.19 = (bf16[96,2688]{1,0:T(8,128)(2,1)S(1)}, bf16[96,2688]{1,0:T(8,128)(2,1)S(1)}, u32[]{:S(2)}, u32[]{:S(2)}) collective-permute-start(bf16[96,2688]{1,0:T(8,128)(2,1)S(1)} %collective-permute-done.18.refs_3_.refs_11_.refs_19_.refs_27_), channel_id=1, source_target_pairs={{1,3},{3,5},{5,7},{7,6},{6,4},{4,2},{2,0},{0,1},{9,11},{11,13},{13... | collective-permute-start | bytes 1548296 | tf_op jit(solution)/shard_map/ppermute | solution.py:524
  48.8 21.1 %collective-permute-start.24 = (bf16[96,2688]{1,0:T(8,128)(2,1)S(1)}, bf16[96,2688]{1,0:T(8,128)(2,1)S(1)}, u32[]{:S(2)}, u32[]{:S(2)}) collective-permute-start(bf16[96,2688]{1,0:T(8,128)(2,1)S(1)} %collective-permute-done.23.refs_35_.refs_43_.refs_3_.refs_11_), channel_id=1, source_target_pairs={{1,0},{3,1},{5,3},{7,5},{6,7},{4,6},{2,4},{0,2},{9,8},{11,9},{13,1... | collective-permute-start | bytes 1548296 | tf_op jit(solution)/shard_map/ppermute | solution.py:524
  57.3 21.1 %collective-permute-start.12 = (bf16[96,2432]{1,0:T(8,128)(2,1)S(1)}, bf16[96,2432]{1,0:T(8,128)(2,1)S(1)}, u32[]{:S(2)}, u32[]{:S(2)}) collective-permute-start(bf16[96,2432]{1,0:T(8,128)(2,1)S(1)} %collective-permute-done.11.refs_1_.refs_9_), channel_id=1, source_target_pairs={{1,3},{3,5},{5,7},{7,6},{6,4},{4,2},{2,0},{0,1},{9,11},{11,13},{13... | collective-permute-start | bytes 1400840 | tf_op jit(solution)/shard_map/ppermute | solution.py:524
  58.8 21.1 %collective-permute-start.3 = (bf16[96,2432]{1,0:T(8,128)(2,1)S(1)}, bf16[96,2432]{1,0:T(8,128)(2,1)S(1)}, u32[]{:S(2)}, u32[]{:S(2)}) collective-permute-start(bf16[96,2432]{1,0:T(8,128)(2,1)S(1)} %collective-permute-done.2.refs_1_.refs_9_), channel_id=1, source_target_pairs={{1,0},{3,1},{5,3},{7,5},{6,7},{4,6},{2,4},{0,2},{9,8},{11,9},{13,1... | collective-permute-start | bytes 1400840 | tf_op jit(solution)/shard_map/ppermute | solution.py:524
  68.3 21.1 %collective-permute-start.20 = (bf16[96,2688]{1,0:T(8,128)(2,1)S(1)}, bf16[96,2688]{1,0:T(8,128)(2,1)S(1)}, u32[]{:S(2)}, u32[]{:S(2)}) collective-permute-start(bf16[96,2688]{1,0:T(8,128)(2,1)S(1)} %collective-permute-done.19.refs_4_.refs_12_.refs_20_.refs_28_), channel_id=1, source_target_pairs={{1,3},{3,5},{5,7},{7,6},{6,4},{4,2},{2,0},{0,1},{9,11},{11,13},{13... | collective-permute-start | bytes 1548296 | tf_op jit(solution)/shard_map/ppermute | solution.py:524
  69.9 21.1 %collective-permute-start.25 = (bf16[96,2688]{1,0:T(8,128)(2,1)S(1)}, bf16[96,2688]{1,0:T(8,128)(2,1)S(1)}, u32[]{:S(2)}, u32[]{:S(2)}) collective-permute-start(bf16[96,2688]{1,0:T(8,128)(2,1)S(1)} %collective-permute-done.24.refs_36_.refs_44_.refs_4_.refs_12_), channel_id=1, source_target_pairs={{1,0},{3,1},{5,3},{7,5},{6,7},{4,6},{2,4},{0,2},{9,8},{11,9},{13,1... | collective-permute-start | bytes 1548296 | tf_op jit(solution)/shard_map/ppermute | solution.py:524
  78.3 21.1 %collective-permute-start.13 = (bf16[96,2432]{1,0:T(8,128)(2,1)S(1)}, bf16[96,2432]{1,0:T(8,128)(2,1)S(1)}, u32[]{:S(2)}, u32[]{:S(2)}) collective-permute-start(bf16[96,2432]{1,0:T(8,128)(2,1)S(1)} %collective-permute-done.12.refs_2_.refs_10_), channel_id=1, source_target_pairs={{1,3},{3,5},{5,7},{7,6},{6,4},{4,2},{2,0},{0,1},{9,11},{11,13},{13... | collective-permute-start | bytes 1400840 | tf_op jit(solution)/shard_map/ppermute | solution.py:524
  79.9 21.1 %collective-permute-start.4 = (bf16[96,2432]{1,0:T(8,128)(2,1)S(1)}, bf16[96,2432]{1,0:T(8,128)(2,1)S(1)}, u32[]{:S(2)}, u32[]{:S(2)}) collective-permute-start(bf16[96,2432]{1,0:T(8,128)(2,1)S(1)} %collective-permute-done.3.refs_2_.refs_10_), channel_id=1, source_target_pairs={{1,0},{3,1},{5,3},{7,5},{6,7},{4,6},{2,4},{0,2},{9,8},{11,9},{13,1... | collective-permute-start | bytes 1400840 | tf_op jit(solution)/shard_map/ppermute | solution.py:524
  89.4 21.1 %collective-permute-start.21 = (bf16[96,2688]{1,0:T(8,128)(2,1)S(1)}, bf16[96,2688]{1,0:T(8,128)(2,1)S(1)}, u32[]{:S(2)}, u32[]{:S(2)}) collective-permute-start(bf16[96,2688]{1,0:T(8,128)(2,1)S(1)} %collective-permute-done.20.refs_5_.refs_13_.refs_21_.refs_29_), channel_id=1, source_target_pairs={{1,3},{3,5},{5,7},{7,6},{6,4},{4,2},{2,0},{0,1},{9,11},{11,13},{13... | collective-permute-start | bytes 1548296 | tf_op jit(solution)/shard_map/ppermute | solution.py:524
  91.0 21.1 %collective-permute-start.26 = (bf16[96,2688]{1,0:T(8,128)(2,1)S(1)}, bf16[96,2688]{1,0:T(8,128)(2,1)S(1)}, u32[]{:S(2)}, u32[]{:S(2)}) collective-permute-start(bf16[96,2688]{1,0:T(8,128)(2,1)S(1)} %collective-permute-done.25.refs_37_.refs_45_.refs_5_.refs_13_), channel_id=1, source_target_pairs={{1,0},{3,1},{5,3},{7,5},{6,7},{4,6},{2,4},{0,2},{9,8},{11,9},{13,1... | collective-permute-start | bytes 1548296 | tf_op jit(solution)/shard_map/ppermute | solution.py:524
  99.4 21.1 %collective-permute-start.14 = (bf16[96,2432]{1,0:T(8,128)(2,1)S(1)}, bf16[96,2432]{1,0:T(8,128)(2,1)S(1)}, u32[]{:S(2)}, u32[]{:S(2)}) collective-permute-start(bf16[96,2432]{1,0:T(8,128)(2,1)S(1)} %collective-permute-done.13.refs_3_.refs_11_), channel_id=1, source_target_pairs={{1,3},{3,5},{5,7},{7,6},{6,4},{4,2},{2,0},{0,1},{9,11},{11,13},{13... | collective-permute-start | bytes 1400840 | tf_op jit(solution)/shard_map/ppermute | solution.py:524
  101.0 21.1 %collective-permute-start.5 = (bf16[96,2432]{1,0:T(8,128)(2,1)S(1)}, bf16[96,2432]{1,0:T(8,128)(2,1)S(1)}, u32[]{:S(2)}, u32[]{:S(2)}) collective-permute-start(bf16[96,2432]{1,0:T(8,128)(2,1)S(1)} %collective-permute-done.4.refs_3_.refs_11_), channel_id=1, source_target_pairs={{1,0},{3,1},{5,3},{7,5},{6,7},{4,6},{2,4},{0,2},{9,8},{11,9},{13,1... | collective-permute-start | bytes 1400840 | tf_op jit(solution)/shard_map/ppermute | solution.py:524
  110.4 30.3 %collective-permute-start.22 = (bf16[96,2688]{1,0:T(8,128)(2,1)S(1)}, bf16[96,2688]{1,0:T(8,128)(2,1)S(1)}, u32[]{:S(2)}, u32[]{:S(2)}) collective-permute-start(bf16[96,2688]{1,0:T(8,128)(2,1)S(1)} %collective-permute-done.21.refs_6_.refs_14_.refs_22_.refs_30_), channel_id=1, source_target_pairs={{1,3},{3,5},{5,7},{7,6},{6,4},{4,2},{2,0},{0,1},{9,11},{11,13},{13... | collective-permute-start | bytes 1548296 | tf_op jit(solution)/shard_map/ppermute | solution.py:524
  112.0 28.8 %collective-permute-start.27 = (bf16[96,2688]{1,0:T(8,128)(2,1)S(1)}, bf16[96,2688]{1,0:T(8,128)(2,1)S(1)}, u32[]{:S(2)}, u32[]{:S(2)}) collective-permute-start(bf16[96,2688]{1,0:T(8,128)(2,1)S(1)} %collective-permute-done.26.refs_38_.refs_46_.refs_6_.refs_14_), channel_id=1, source_target_pairs={{1,0},{3,1},{5,3},{7,5},{6,7},{4,6},{2,4},{0,2},{9,8},{11,9},{13,1... | collective-permute-start | bytes 1548296 | tf_op jit(solution)/shard_map/ppermute | solution.py:524
  120.5 18.3 %collective-permute-start.15 = (bf16[96,2432]{1,0:T(8,128)(2,1)S(1)}, bf16[96,2432]{1,0:T(8,128)(2,1)S(1)}, u32[]{:S(2)}, u32[]{:S(2)}) collective-permute-start(bf16[96,2432]{1,0:T(8,128)(2,1)S(1)} %collective-permute-done.14.refs_4_.refs_12_), channel_id=1, source_target_pairs={{1,3},{3,5},{5,7},{7,6},{6,4},{4,2},{2,0},{0,1},{9,11},{11,13},{13... | collective-permute-start | bytes 1400840 | tf_op jit(solution)/shard_map/ppermute | solution.py:524
  122.0 18.3 %collective-permute-start.6 = (bf16[96,2432]{1,0:T(8,128)(2,1)S(1)}, bf16[96,2432]{1,0:T(8,128)(2,1)S(1)}, u32[]{:S(2)}, u32[]{:S(2)}) collective-permute-start(bf16[96,2432]{1,0:T(8,128)(2,1)S(1)} %collective-permute-done.5.refs_4_.refs_12_), channel_id=1, source_target_pairs={{1,0},{3,1},{5,3},{7,5},{6,7},{4,6},{2,4},{0,2},{9,8},{11,9},{13,1... | collective-permute-start | bytes 1400840 | tf_op jit(solution)/shard_map/ppermute | solution.py:524
  138.7 11.6 %collective-permute-start.16 = (bf16[96,2432]{1,0:T(8,128)(2,1)S(1)}, bf16[96,2432]{1,0:T(8,128)(2,1)S(1)}, u32[]{:S(2)}, u32[]{:S(2)}) collective-permute-start(bf16[96,2432]{1,0:T(8,128)(2,1)S(1)} %collective-permute-done.15.refs_5_.refs_13_), channel_id=1, source_target_pairs={{1,3},{3,5},{5,7},{7,6},{6,4},{4,2},{2,0},{0,1},{9,11},{11,13},{13... | collective-permute-start | bytes 1400840 | tf_op jit(solution)/shard_map/ppermute | solution.py:524
  140.3 10.1 %collective-permute-start.7 = (bf16[96,2432]{1,0:T(8,128)(2,1)S(1)}, bf16[96,2432]{1,0:T(8,128)(2,1)S(1)}, u32[]{:S(2)}, u32[]{:S(2)}) collective-permute-start(bf16[96,2432]{1,0:T(8,128)(2,1)S(1)} %collective-permute-done.6.refs_5_.refs_13_), channel_id=1, source_target_pairs={{1,0},{3,1},{5,3},{7,5},{6,7},{4,6},{2,4},{0,2},{9,8},{11,9},{13,1... | collective-permute-start | bytes 1400840 | tf_op jit(solution)/shard_map/ppermute | solution.py:524
  150.4 11.0 %collective-permute-start.17 = (bf16[96,2432]{1,0:T(8,128)(2,1)S(1)}, bf16[96,2432]{1,0:T(8,128)(2,1)S(1)}, u32[]{:S(2)}, u32[]{:S(2)}) collective-permute-start(bf16[96,2432]{1,0:T(8,128)(2,1)S(1)} %collective-permute-done.16.refs_6_.refs_14_), channel_id=1, source_target_pairs={{1,3},{3,5},{5,7},{7,6},{6,4},{4,2},{2,0},{0,1},{9,11},{11,13},{13... | collective-permute-start | bytes 1400840 | tf_op jit(solution)/shard_map/ppermute | solution.py:524
  152.0 15.2 %collective-permute-start.8 = (bf16[96,2432]{1,0:T(8,128)(2,1)S(1)}, bf16[96,2432]{1,0:T(8,128)(2,1)S(1)}, u32[]{:S(2)}, u32[]{:S(2)}) collective-permute-start(bf16[96,2432]{1,0:T(8,128)(2,1)S(1)} %collective-permute-done.7.refs_6_.refs_14_), channel_id=1, source_target_pairs={{1,0},{3,1},{5,3},{7,5},{6,7},{4,6},{2,4},{0,2},{9,8},{11,9},{13,1... | collective-permute-start | bytes 1400840 | tf_op jit(solution)/shard_map/ppermute | solution.py:524
  173.4 5.5 %collective-permute-start.28 = (bf16[6,256,256]{2,1,0:T(8,128)(2,1)S(1)}, bf16[6,256,256]{2,1,0:T(8,128)(2,1)S(1)}, u32[]{:S(2)}, u32[]{:S(2)}) collective-permute-start(bf16[6,256,256]{2,1,0:T(8,128)(2,1)S(1)} %fold.1), channel_id=1, source_target_pairs={{24,16},{25,17},{26,18},{27,19},{28,20},{29,21},{30,22},{31,23}} | collective-permute-start | bytes 2359304 | tf_op jit(solution)/shard_map/ppermute | solution.py:558
  180.8 0.7 collective-permute-start.29
  183.3 15.5 %collective-permute-start.30 = (bf16[6,256,256]{2,1,0:T(8,128)(2,1)S(1)}, bf16[6,256,256]{2,1,0:T(8,128)(2,1)S(1)}, u32[]{:S(2)}, u32[]{:S(2)}) collective-permute-start(bf16[6,256,256]{2,1,0:T(8,128)(2,1)S(1)} %hop.3), channel_id=1, source_target_pairs={{8,0},{9,1},{10,2},{11,3},{12,4},{13,5},{14,6},{15,7}} | collective-permute-start | bytes 2359304 | tf_op jit(solution)/shard_map/ppermute | solution.py:558

commit v11 on v10

--- a/solution.py
+++ b/solution.py
@@ -254,22 +254,36 @@
     )(last, place, *blocks, *blocks, *args)
 
 
-def chain_kernel(cycle, way, place_ref, *refs):
+def chain_kernel(cycle, way, turns, place_ref, *refs):
     count = len(cycle)
     places = origins(place_ref[0], cycle, way)
-    blocks, sides, refs = refs[:count], refs[count:2 * count], refs[2 * count:]
-    half_in, refs = refs[0], refs[-8:]
-    gain_out, half_out, gain, half, fresh, middle, raw, extras = refs
-
-    @pl.when(pl.program_id(0) == 0)
-    def _():
-        half[...] = half_in[...].reshape(half.shape)
-
-    step = pl.num_programs(0) - 1 - pl.program_id(0)
-    assemble(places, blocks, sides, step, gain, fresh, raw, extras)
-    gain_out[0] = gain[...]
-    advance(gain, half, fresh, middle)
-    half_out[0] = half[...]
+    blocks, refs = refs[:count], refs[count:]
+    half_in, refs = refs[0], refs[-9:]
+    gain_out, half_out, half, middle, raw, extras, gain, fresh, spare = refs
+    gains, freshes = (gain, spare.at[0]), (fresh, spare.at[1])
+    rows, width = blocks[0].shape[0], half.shape[0]
+    stride = width * 3 // 2
+    side = slice(turns * stride, turns * stride + LANES)
+
+    def prepare(turn):
+        step = turns - 1 - turn
+        lanes = slice(step * stride, (step + 1) * stride)
+        parts = [block.at[:, lanes] for block in blocks]
+        sides = [block.at[:, side] for block in blocks]
+        assemble(places, parts, sides, step, gains[turn % 2], freshes[turn % 2], raw, extras)
+
+    for turn in range(turns):
+
+        @pl.when(pl.program_id(0) == turn)
+        def _():
+            if turn == 0:
+                half[...] = half_in[...].reshape(half.shape)
+                prepare(0)
+            gain_out[0] = gains[turn % 2][...]
+            if turn + 1 < turns:
+                prepare(turn + 1)
+            advance(gains[turn % 2], half, freshes[turn % 2], middle)
+            half_out[0] = half[...]
 
 
 def chain(place, cycle, way, blocks, half, state, low, turns, steps):
@@ -277,7 +291,7 @@
     rows = blocks[0].shape[0]
     width = rows * count
     anywhere = pl.BlockSpec(memory_space=pl.ANY)
-    in_specs = row_specs(blocks, turns)
+    in_specs = [pl.BlockSpec(blocks[0].shape, lambda i, *p: (0, 0), pipeline_mode=pl.Buffered(1))] * count
     if state is None:
         in_specs += [square(width)]
         args = [half]
@@ -289,22 +303,30 @@
         args = [state[1], state[0]]
     whole = square(width, lambda i: low + turns - 1 - i)
     return pl.pallas_call(
-        functools.partial(chain_kernel, cycle, way),
+        functools.partial(chain_kernel, cycle, way, turns),
         grid_spec=pltpu.PrefetchScalarGridSpec(
             num_scalar_prefetch=1,
             grid=(turns,),
             in_specs=in_specs,
             out_specs=[whole, whole],
-            scratch_shapes=row_scratch(count, rows),
+            scratch_shapes=[
+                pltpu.VMEM((width, width), BF16),
+                pltpu.VMEM((width, width), BF16),
+                pltpu.VMEM((count, rows, width // 2), BF16),
+                pltpu.VMEM((count, rows, LANES), BF16),
+                pltpu.VMEM((width, width), BF16),
+                pltpu.VMEM((width, width), BF16),
+                pltpu.VMEM((2, width, width), BF16),
+            ],
         ),
         out_shape=[jax.ShapeDtypeStruct((steps, width, width), BF16)] * 2,
-        input_output_aliases={} if state is None else {1 + 2 * count + 1: 0, 1 + 2 * count: 1},
+        input_output_aliases={} if state is None else {1 + count + 1: 0, 1 + count: 1},
         compiler_params=pltpu.CompilerParams(vmem_limit_bytes=18 * MIB),
         cost_estimate=pl.CostEstimate(
             flops=4 * turns * width**3, bytes_accessed=8 * turns * width * width, transcendentals=0
         ),
         name="chain",
-    )(place, *blocks, *blocks, *args)
+    )(place, *blocks, *args)
 
 
 def factors_kernel(place_ref, gain_ref, factor_in, mine_ref, factor_out, mine_out, factor):
@@ -473,26 +495,30 @@
             cols = slice(j, j + TILE)
             middle[:, cols] = jnp.dot(mine, covariance[:, cols], preferred_element_type=F32).astype(BF16)
 
-    left = middle[pl.ds(pl.multiple_of(turn * rows, 16), rows), :]
-    out_ref[0] = nt(left, factor_ref[0]) + own_ref[0]
+    for n in range(out_ref.shape[0]):
+        at = (turn * out_ref.shape[0] + n) * rows
+        left = middle[pl.ds(pl.multiple_of(at, 16), rows), :]
+        out_ref[n] = nt(left, factor_ref[n]) + own_ref[n]
 
 
 def finish(factors, own, mine, packed):
     steps, rows, width = own.shape
+    some = 2 if steps % 2 == 0 else 1
     whole = pl.BlockSpec(packed[0].shape, lambda i: (0, 0, 0), pipeline_mode=pl.Buffered(1))
+    band = pl.BlockSpec((some, rows, width), lambda i: (i, 0, 0))
     return pl.pallas_call(
         functools.partial(finish_kernel, len(packed)),
-        grid=(steps,),
+        grid=(steps // some,),
         in_specs=[
-            pl.BlockSpec((1, width, width), lambda i: (i, 0, 0)),
-            pl.BlockSpec((1, rows, width), lambda i: (i, 0, 0)),
+            pl.BlockSpec((some, width, width), lambda i: (i, 0, 0)),
+            band,
             pl.BlockSpec(mine.shape, lambda i: (0, 0, 0), pipeline_mode=pl.Buffered(1)),
         ]
         + [whole] * len(packed),
-        out_specs=pl.BlockSpec((1, rows, width), lambda i: (i, 0, 0)),
+        out_specs=band,
         scratch_shapes=[pltpu.VMEM((width, width), BF16), pltpu.VMEM((steps * rows, width), BF16)],
         out_shape=jax.ShapeDtypeStruct((steps, rows, width), F32),
-        compiler_params=pltpu.CompilerParams(vmem_limit_bytes=20 * MIB),
+        compiler_params=pltpu.CompilerParams(vmem_limit_bytes=24 * MIB),
         name="finish",
     )(factors, own, mine, *packed)
 

time: 206 us -> 203 us (0.985)
  Pallas kernels: 51.8 us -> 48.9 us
where the time goes in v11:
time: 203 us
  waiting for transfers between devices  121 us (60%)
  Pallas kernels  48.9 us (24%)
  starting transfers between devices  32.4 us (16%)
    ppermute x28, waiting for transfers between devices, passed(): lax.ppermute(array, 'tile', [(cycle[n], cycle[(n + way) % count]) for n i...  109 us
    ppermute x28, starting transfers between devices, passed(): lax.ppermute(array, 'tile', [(cycle[n], cycle[(n + way) % count]) for n i...  29.5 us
    pallas_call x2, Pallas kernels, compose(): pl.pallas_call(functools.partial(compose_kernel, cycle, way, first), grid...  18.4 us
    ppermute x3, waiting for transfers between devices, local(): lax.ppermute(hop(factors, early[1], packed), 'tm', [(turn, turn - 1)])  12.1 us
    pallas_call x2, Pallas kernels, chain(): pl.pallas_call(functools.partial(chain_kernel, cycle, way, turns), grid_s...  10 us
    pallas_call x1, Pallas kernels, finish(): pl.pallas_call(functools.partial(finish_kernel, len(packed)), grid=(steps...  5.58 us
    pallas_call x1, Pallas kernels, extend_factors(): pl.pallas_call(factors_kernel, grid_spec=pltpu.PrefetchScalarGridSpec(num...  4.55 us
    pallas_call x2, Pallas kernels, pack(): pl.pallas_call(functools.partial(pack_kernel, count, ranges), grid_spec=p...  4.27 us
  transfers between devices with their start and end apart: 31, of which 13 were waited for; matrix products, arithmetic and copies ran while one was open for 0% of the time, Pallas kernels for 15%

profile of v11, /device:TPU:0, one launch (start us, length us, event | category | flops | bytes accessed | tf_op | source)
XLA Modules:
  0.0 202.7 jit_solution(3078740502783080186)
XLA Ops:
  0.0 3.5 %pack.3 = (bf16[96,2688]{1,0:T(8,128)(2,1)}, bf16[96,2688]{1,0:T(8,128)(2,1)}) custom-call(s32[1]{0:T(128)} %bitcast.place_ref, bf16[8,96,768]{2,1,0:T(8,128)(2,1)} %gain_ref.3, f32[8,96,768]{2,1,0:T(8,128)} %increment_ref.3, f32[96,768]{1,0:T(8,128)} %refs_0_.1), custom_call_target="tpu_custom_call" | custom-call | tf_op jit(solution)/shard_map/pack/pallas_call | solution.py:81
  3.6 3.0 %collective-permute-start.9 = (bf16[96,2688]{1,0:T(8,128)(2,1)}, bf16[96,2688]{1,0:T(8,128)(2,1)S(1)}, u32[]{:S(2)}, u32[]{:S(2)}) collective-permute-start(bf16[96,2688]{1,0:T(8,128)(2,1)} %get-tuple-element.65.refs_0_.refs_8_.refs_16_.refs_24_), channel_id=1, source_target_pairs={{1,3},{3,5},{5,7},{7,6},{6,4},{4,2},{2,0},{0,1},{9,11},{11,13},{13... | collective-permute-start | bytes 1548296 | tf_op jit(solution)/shard_map/ppermute | solution.py:550
  6.6 12.0 %collective-permute-done.9.refs_1_.refs_9_.refs_17_.refs_25_ = bf16[96,2688]{1,0:T(8,128)(2,1)S(1)} collective-permute-done((bf16[96,2688]{1,0:T(8,128)(2,1)}, bf16[96,2688]{1,0:T(8,128)(2,1)S(1)}, u32[]{:S(2)}, u32[]{:S(2)}) %collective-permute-start.9) | collective-permute-done | bytes 516128 | tf_op jit(solution)/shard_map/ppermute | solution.py:550
  18.6 1.6 collective-permute-start.10
  20.6 0.7 pack.2
  21.4 10.2 %collective-permute-done.10.refs_2_.refs_10_.refs_18_.refs_26_ = bf16[96,2688]{1,0:T(8,128)(2,1)S(1)} collective-permute-done((bf16[96,2688]{1,0:T(8,128)(2,1)S(1)}, bf16[96,2688]{1,0:T(8,128)(2,1)S(1)}, u32[]{:S(2)}, u32[]{:S(2)}) %collective-permute-start.10) | collective-permute-done | bytes 516128 | tf_op jit(solution)/shard_map/ppermute | solution.py:550
  31.5 1.0 collective-permute-done.1.refs_34_.refs_42_.refs_2_.refs_10_
  32.6 1.6 collective-permute-start.18
  34.6 1.6 collective-permute-start.11
  36.6 10.6 %collective-permute-done.18.refs_3_.refs_11_.refs_19_.refs_27_ = bf16[96,2688]{1,0:T(8,128)(2,1)S(1)} collective-permute-done((bf16[96,2688]{1,0:T(8,128)(2,1)S(1)}, bf16[96,2688]{1,0:T(8,128)(2,1)S(1)}, u32[]{:S(2)}, u32[]{:S(2)}) %collective-permute-start.18) | collective-permute-done | bytes 516128 | tf_op jit(solution)/shard_map/ppermute | solution.py:550
  47.2 1.6 collective-permute-start.19
  48.8 0.5 collective-permute-start.24
  49.3 8.0 %collective-permute-done.11.refs_1_ = bf16[96,2432]{1,0:T(8,128)(2,1)S(1)} collective-permute-done((bf16[96,2432]{1,0:T(8,128)(2,1)S(1)}, bf16[96,2432]{1,0:T(8,128)(2,1)S(1)}, u32[]{:S(2)}, u32[]{:S(2)}) %collective-permute-start.11) | collective-permute-done | bytes 466976 | tf_op jit(solution)/shard_map/ppermute | solution.py:550
  57.3 1.6 collective-permute-start.12
  58.8 0.5 collective-permute-start.3
  59.3 9.0 %collective-permute-done.19.refs_4_.refs_12_.refs_20_.refs_28_ = bf16[96,2688]{1,0:T(8,128)(2,1)S(1)} collective-permute-done((bf16[96,2688]{1,0:T(8,128)(2,1)S(1)}, bf16[96,2688]{1,0:T(8,128)(2,1)S(1)}, u32[]{:S(2)}, u32[]{:S(2)}) %collective-permute-start.19) | collective-permute-done | bytes 516128 | tf_op jit(solution)/shard_map/ppermute | solution.py:550
  68.3 1.6 collective-permute-start.20
  69.9 0.5 collective-permute-start.25
  70.3 8.0 %collective-permute-done.12.refs_2_ = bf16[96,2432]{1,0:T(8,128)(2,1)S(1)} collective-permute-done((bf16[96,2432]{1,0:T(8,128)(2,1)S(1)}, bf16[96,2432]{1,0:T(8,128)(2,1)S(1)}, u32[]{:S(2)}, u32[]{:S(2)}) %collective-permute-start.12) | collective-permute-done | bytes 466976 | tf_op jit(solution)/shard_map/ppermute | solution.py:550
  78.3 1.6 collective-permute-start.13
  79.9 0.5 collective-permute-start.4
  80.3 9.0 %collective-permute-done.20.refs_5_.refs_13_.refs_21_.refs_29_ = bf16[96,2688]{1,0:T(8,128)(2,1)S(1)} collective-permute-done((bf16[96,2688]{1,0:T(8,128)(2,1)S(1)}, bf16[96,2688]{1,0:T(8,128)(2,1)S(1)}, u32[]{:S(2)}, u32[]{:S(2)}) %collective-permute-start.20) | collective-permute-done | bytes 516128 | tf_op jit(solution)/shard_map/ppermute | solution.py:550
  89.4 1.6 collective-permute-start.21
  91.0 0.5 collective-permute-start.26
  91.4 8.0 %collective-permute-done.13.refs_3_ = bf16[96,2432]{1,0:T(8,128)(2,1)S(1)} collective-permute-done((bf16[96,2432]{1,0:T(8,128)(2,1)S(1)}, bf16[96,2432]{1,0:T(8,128)(2,1)S(1)}, u32[]{:S(2)}, u32[]{:S(2)}) %collective-permute-start.13) | collective-permute-done | bytes 466976 | tf_op jit(solution)/shard_map/ppermute | solution.py:550
  99.4 1.6 collective-permute-start.14
  101.0 0.5 collective-permute-start.5
  101.4 9.0 %collective-permute-done.21.refs_6_.refs_14_.refs_22_.refs_30_ = bf16[96,2688]{1,0:T(8,128)(2,1)S(1)} collective-permute-done((bf16[96,2688]{1,0:T(8,128)(2,1)S(1)}, bf16[96,2688]{1,0:T(8,128)(2,1)S(1)}, u32[]{:S(2)}, u32[]{:S(2)}) %collective-permute-start.21) | collective-permute-done | bytes 516128 | tf_op jit(solution)/shard_map/ppermute | solution.py:550
  110.4 1.6 collective-permute-start.22
  112.0 0.5 collective-permute-start.27
  112.5 8.0 %collective-permute-done.14.refs_4_ = bf16[96,2432]{1,0:T(8,128)(2,1)S(1)} collective-permute-done((bf16[96,2432]{1,0:T(8,128)(2,1)S(1)}, bf16[96,2432]{1,0:T(8,128)(2,1)S(1)}, u32[]{:S(2)}, u32[]{:S(2)}) %collective-permute-start.14) | collective-permute-done | bytes 466976 | tf_op jit(solution)/shard_map/ppermute | solution.py:550
  120.5 1.6 collective-permute-start.15
  122.5 16.3 %collective-permute-done.15.refs_5_ = bf16[96,2432]{1,0:T(8,128)(2,1)S(1)} collective-permute-done((bf16[96,2432]{1,0:T(8,128)(2,1)S(1)}, bf16[96,2432]{1,0:T(8,128)(2,1)S(1)}, u32[]{:S(2)}, u32[]{:S(2)}) %collective-permute-start.15) | collective-permute-done | bytes 466976 | tf_op jit(solution)/shard_map/ppermute | solution.py:550
  138.7 1.6 collective-permute-start.16
  140.8 9.5 %compose.2 = (bf16[8,768,768]{2,1,0:T(8,128)(2,1)S(1)}, f32[8,96,768]{2,1,0:T(8,128)S(1)}, bf16[8,96,768]{2,1,0:T(8,128)(2,1)S(1)}, bf16[768,768]{1,0:T(8,128)(2,1)S(1)}) custom-call(s32[1]{0:T(128)} %bitcast.1.last_ref, s32[1]{0:T(128)} %bitcast.place_ref, bf16[96,2688]{1,0:T(8,128)(2,1)S(1)} %copy-done.1, ...), custom_call_target="tpu_custom_call" | custom-call | flops 5435817984 | bytes 9437184 | tf_op jit(solution)/shard_map/compose/pallas_call | solution.py:233
  150.4 1.6 collective-permute-start.17
  152.4 8.9 %compose.3 = (bf16[8,768,768]{2,1,0:T(8,128)(2,1)S(1)}, f32[8,96,768]{2,1,0:T(8,128)S(1)}, bf16[8,96,768]{2,1,0:T(8,128)(2,1)S(1)}, bf16[768,768]{1,0:T(8,128)(2,1)S(1)}) custom-call(s32[1]{0:T(128)} %bitcast.1.last_ref, s32[1]{0:T(128)} %bitcast.place_ref, ...), custom_call_target="tpu_custom_call", output_to_operand_aliasing={{0}: (19, {}), {1}: (20, {}), {2}: (21, {})} | custom-call | flops 5435817984 | bytes 9437184 | tf_op jit(solution)/shard_map/compose/pallas_call | solution.py:233
  161.4 5.0 %chain.2 = (bf16[4,768,768]{2,1,0:T(8,128)(2,1)S(1)}, bf16[4,768,768]{2,1,0:T(8,128)(2,1)S(1)}) custom-call(s32[1]{0:T(128)} %bitcast.place_ref, bf16[96,2432]{1,0:T(8,128)(2,1)S(1)} %get-tuple-element.61.refs_0_, bf16[96,2432]{1,0:T(8,128)(2,1)S(1)} %collective-permute-done.11.refs_1_, bf16[96,2432]{1,0:T(8,128)(2,1)S(1)} %collective-permute-done.12.refs_2_, ...), custom_call_target="tpu_custom_call" | custom-call | flops 3623878656 | bytes 9437184 | tf_op jit(solution)/shard_map/chain/pallas_call | solution.py:305
  166.4 5.0 %chain.3 = (bf16[4,768,768]{2,1,0:T(8,128)(2,1)S(1)}, bf16[4,768,768]{2,1,0:T(8,128)(2,1)S(1)}) custom-call(s32[1]{0:T(128)} %bitcast.place_ref, bf16[96,2432]{1,0:T(8,128)(2,1)S(1)} %get-tuple-element.58.refs_0_, bf16[96,2432]{1,0:T(8,128)(2,1)S(1)} %collective-permute-done.2.refs_1_, ...), custom_call_target="tpu_custom_call", output_to_operand_aliasing={{0}: (10, {}), {1}: (9, {})} | custom-call | flops 3623878656 | bytes 9437184 | tf_op jit(solution)/shard_map/chain/pallas_call | solution.py:305
  171.7 0.9 collective-permute-start.28
  172.7 4.5 %extend_factors.1 = (bf16[8,768,768]{2,1,0:T(8,128)(2,1)S(1)}, bf16[8,96,768]{2,1,0:T(8,128)(2,1)S(1)}) custom-call(s32[1]{0:T(128)} %bitcast.place_ref, bf16[4,768,768]{2,1,0:T(8,128)(2,1)S(1)} %get-tuple-element.96.gain_ref, bf16[8,768,768]{2,1,0:T(8,128)(2,1)S(1)} %get-tuple-element.97.factor_in, ...), custom_call_target="tpu_custom_call", output_to_operand_aliasing={{0}: (2, {}), {1}: (3, {})} | custom-call | flops 3623878656 | bytes 9437184 | tf_op jit(solution)/shard_map/extend_factors/pallas_call | solution.py:349
  177.2 1.8 hop.2
  179.1 0.7 collective-permute-start.29
  179.8 1.8 hop.3
  181.6 1.3 collective-permute-start.30
  182.9 2.1 %own_rows.1.own_ref = f32[8,96,768]{2,1,0:T(8,128)S(1)} custom-call(s32[1]{0:T(128)} %bitcast.place_ref, bf16[4,768,768]{2,1,0:T(8,128)(2,1)S(1)} %get-tuple-element.100.half_ref, f32[8,96,768]{2,1,0:T(8,128)S(1)} %get-tuple-element.101.own_ref), custom_call_target="tpu_custom_call", output_to_operand_aliasing={{}: (2, {})} | custom-call | flops 452984832 | bytes 4718592 | tf_op jit(solution)/shard_map/own_rows/pallas_call | solution.py:383
  185.0 12.1 %collective-permute-done.30.refs_2_ = bf16[6,256,256]{2,1,0:T(8,128)(2,1)S(1)} collective-permute-done((bf16[6,256,256]{2,1,0:T(8,128)(2,1)S(1)}, bf16[6,256,256]{2,1,0:T(8,128)(2,1)S(1)}, u32[]{:S(2)}, u32[]{:S(2)}) %collective-permute-start.30) | collective-permute-done | bytes 786464 | tf_op jit(solution)/shard_map/ppermute | solution.py:584
  197.1 5.6 %finish.1 = f32[8,96,768]{2,1,0:T(8,128)} custom-call(bf16[8,768,768]{2,1,0:T(8,128)(2,1)S(1)} %get-tuple-element.99.factor_ref, f32[8,96,768]{2,1,0:T(8,128)S(1)} %own_rows.1.own_ref, bf16[8,96,768]{2,1,0:T(8,128)(2,1)S(1)} %get-tuple-element.102.mine_ref, bf16[6,256,256]{2,1,0:T(8,128)(2,1)S(1)} %collective-permute-done.28.refs_0_, ...), custom_call_target="tpu_custom_call" | custom-call | tf_op jit(solution)/shard_map/finish/pallas_call | solution.py:509
  (34 shorter events, 3.1 us)
Async XLA Ops:
  0.0 20.6 %copy-start.3 = (bf16[8,96,768]{2,1,0:T(8,128)(2,1)S(1)}, bf16[8,96,768]{2,1,0:T(8,128)(2,1)}, u32[]{:S(2)}) copy-start(bf16[8,96,768]{2,1,0:T(8,128)(2,1)} %gain_ref.3) | copy-start | bytes 3538948
  0.0 20.6 %copy-start = (f32[8,96,768]{2,1,0:T(8,128)S(1)}, f32[8,96,768]{2,1,0:T(8,128)}, u32[]{:S(2)}) copy-start(f32[8,96,768]{2,1,0:T(8,128)} %increment_ref.3) | copy-start | bytes 7077892
  3.5 137.2 %copy-start.1 = (bf16[96,2688]{1,0:T(8,128)(2,1)S(1)}, bf16[96,2688]{1,0:T(8,128)(2,1)}, u32[]{:S(2)}) copy-start(bf16[96,2688]{1,0:T(8,128)(2,1)} %get-tuple-element.65.refs_0_.refs_8_.refs_16_.refs_24_) | copy-start | bytes 1548292
  3.6 137.2 %copy-start.2 = (bf16[96,2688]{1,0:T(8,128)(2,1)S(1)}, bf16[96,2688]{1,0:T(8,128)(2,1)}, u32[]{:S(2)}) copy-start(bf16[96,2688]{1,0:T(8,128)(2,1)} %get-tuple-element.81.refs_32_.refs_40_.refs_0_.refs_8_) | copy-start | bytes 1548292
  3.6 15.0 %collective-permute-start.9 = (bf16[96,2688]{1,0:T(8,128)(2,1)}, bf16[96,2688]{1,0:T(8,128)(2,1)S(1)}, u32[]{:S(2)}, u32[]{:S(2)}) collective-permute-start(bf16[96,2688]{1,0:T(8,128)(2,1)} %get-tuple-element.65.refs_0_.refs_8_.refs_16_.refs_24_), channel_id=1, source_target_pairs={{1,3},{3,5},{5,7},{7,6},{6,4},{4,2},{2,0},{0,1},{9,11},{11,13},{13... | collective-permute-start | bytes 1548296 | tf_op jit(solution)/shard_map/ppermute | solution.py:550
  6.5 13.7 %collective-permute-start = (bf16[96,2688]{1,0:T(8,128)(2,1)}, bf16[96,2688]{1,0:T(8,128)(2,1)S(1)}, u32[]{:S(2)}, u32[]{:S(2)}) collective-permute-start(bf16[96,2688]{1,0:T(8,128)(2,1)} %get-tuple-element.81.refs_32_.refs_40_.refs_0_.refs_8_), channel_id=1, source_target_pairs={{1,0},{3,1},{5,3},{7,5},{6,7},{4,6},{2,4},{0,2},{9,8},{11,9},{13,1... | collective-permute-start | bytes 1548296 | tf_op jit(solution)/shard_map/ppermute | solution.py:550
  18.6 12.9 %collective-permute-start.10 = (bf16[96,2688]{1,0:T(8,128)(2,1)S(1)}, bf16[96,2688]{1,0:T(8,128)(2,1)S(1)}, u32[]{:S(2)}, u32[]{:S(2)}) collective-permute-start(bf16[96,2688]{1,0:T(8,128)(2,1)S(1)} %collective-permute-done.9.refs_1_.refs_9_.refs_17_.refs_25_), channel_id=1, source_target_pairs={{1,3},{3,5},{5,7},{7,6},{6,4},{4,2},{2,0},{0,1},{9,11},{11,13},{13... | collective-permute-start | bytes 1548296 | tf_op jit(solution)/shard_map/ppermute | solution.py:550
  20.2 12.3 %collective-permute-start.1 = (bf16[96,2688]{1,0:T(8,128)(2,1)S(1)}, bf16[96,2688]{1,0:T(8,128)(2,1)S(1)}, u32[]{:S(2)}, u32[]{:S(2)}) collective-permute-start(bf16[96,2688]{1,0:T(8,128)(2,1)S(1)} %collective-permute-done.refs_33_.refs_41_.refs_1_.refs_9_), channel_id=1, source_target_pairs={{1,0},{3,1},{5,3},{7,5},{6,7},{4,6},{2,4},{0,2},{9,8},{11,9},{13,1... | collective-permute-start | bytes 1548296 | tf_op jit(solution)/shard_map/ppermute | solution.py:550
  32.6 14.7 %collective-permute-start.18 = (bf16[96,2688]{1,0:T(8,128)(2,1)S(1)}, bf16[96,2688]{1,0:T(8,128)(2,1)S(1)}, u32[]{:S(2)}, u32[]{:S(2)}) collective-permute-start(bf16[96,2688]{1,0:T(8,128)(2,1)S(1)} %collective-permute-done.10.refs_2_.refs_10_.refs_18_.refs_26_), channel_id=1, source_target_pairs={{1,3},{3,5},{5,7},{7,6},{6,4},{4,2},{2,0},{0,1},{9,11},{11,13},{13... | collective-permute-start | bytes 1548296 | tf_op jit(solution)/shard_map/ppermute | solution.py:550
  34.1 14.7 %collective-permute-start.23 = (bf16[96,2688]{1,0:T(8,128)(2,1)S(1)}, bf16[96,2688]{1,0:T(8,128)(2,1)S(1)}, u32[]{:S(2)}, u32[]{:S(2)}) collective-permute-start(bf16[96,2688]{1,0:T(8,128)(2,1)S(1)} %collective-permute-done.1.refs_34_.refs_42_.refs_2_.refs_10_), channel_id=1, source_target_pairs={{1,0},{3,1},{5,3},{7,5},{6,7},{4,6},{2,4},{0,2},{9,8},{11,9},{13,1... | collective-permute-start | bytes 1548296 | tf_op jit(solution)/shard_map/ppermute | solution.py:550
  34.6 22.7 %collective-permute-start.11 = (bf16[96,2432]{1,0:T(8,128)(2,1)S(1)}, bf16[96,2432]{1,0:T(8,128)(2,1)S(1)}, u32[]{:S(2)}, u32[]{:S(2)}) collective-permute-start(bf16[96,2432]{1,0:T(8,128)(2,1)S(1)} %get-tuple-element.61.refs_0_), channel_id=1, source_target_pairs={{1,3},{3,5},{5,7},{7,6},{6,4},{4,2},{2,0},{0,1},{9,11},{11,13},{13... | collective-permute-start | bytes 1400840 | tf_op jit(solution)/shard_map/ppermute | solution.py:550
  36.2 22.7 %collective-permute-start.2 = (bf16[96,2432]{1,0:T(8,128)(2,1)S(1)}, bf16[96,2432]{1,0:T(8,128)(2,1)S(1)}, u32[]{:S(2)}, u32[]{:S(2)}) collective-permute-start(bf16[96,2432]{1,0:T(8,128)(2,1)S(1)} %get-tuple-element.58.refs_0_), channel_id=1, source_target_pairs={{1,0},{3,1},{5,3},{7,5},{6,7},{4,6},{2,4},{0,2},{9,8},{11,9},{13,1... | collective-permute-start | bytes 1400840 | tf_op jit(solution)/shard_map/ppermute | solution.py:550
  47.2 21.1 %collective-permute-start.19 = (bf16[96,2688]{1,0:T(8,128)(2,1)S(1)}, bf16[96,2688]{1,0:T(8,128)(2,1)S(1)}, u32[]{:S(2)}, u32[]{:S(2)}) collective-permute-start(bf16[96,2688]{1,0:T(8,128)(2,1)S(1)} %collective-permute-done.18.refs_3_.refs_11_.refs_19_.refs_27_), channel_id=1, source_target_pairs={{1,3},{3,5},{5,7},{7,6},{6,4},{4,2},{2,0},{0,1},{9,11},{11,13},{13... | collective-permute-start | bytes 1548296 | tf_op jit(solution)/shard_map/ppermute | solution.py:550
  48.8 21.1 %collective-permute-start.24 = (bf16[96,2688]{1,0:T(8,128)(2,1)S(1)}, bf16[96,2688]{1,0:T(8,128)(2,1)S(1)}, u32[]{:S(2)}, u32[]{:S(2)}) collective-permute-start(bf16[96,2688]{1,0:T(8,128)(2,1)S(1)} %collective-permute-done.23.refs_35_.refs_43_.refs_3_.refs_11_), channel_id=1, source_target_pairs={{1,0},{3,1},{5,3},{7,5},{6,7},{4,6},{2,4},{0,2},{9,8},{11,9},{13,1... | collective-permute-start | bytes 1548296 | tf_op jit(solution)/shard_map/ppermute | solution.py:550
  57.3 21.1 %collective-permute-start.12 = (bf16[96,2432]{1,0:T(8,128)(2,1)S(1)}, bf16[96,2432]{1,0:T(8,128)(2,1)S(1)}, u32[]{:S(2)}, u32[]{:S(2)}) collective-permute-start(bf16[96,2432]{1,0:T(8,128)(2,1)S(1)} %collective-permute-done.11.refs_1_), channel_id=1, source_target_pairs={{1,3},{3,5},{5,7},{7,6},{6,4},{4,2},{2,0},{0,1},{9,11},{11,13},{13... | collective-permute-start | bytes 1400840 | tf_op jit(solution)/shard_map/ppermute | solution.py:550
  58.8 21.1 %collective-permute-start.3 = (bf16[96,2432]{1,0:T(8,128)(2,1)S(1)}, bf16[96,2432]{1,0:T(8,128)(2,1)S(1)}, u32[]{:S(2)}, u32[]{:S(2)}) collective-permute-start(bf16[96,2432]{1,0:T(8,128)(2,1)S(1)} %collective-permute-done.2.refs_1_), channel_id=1, source_target_pairs={{1,0},{3,1},{5,3},{7,5},{6,7},{4,6},{2,4},{0,2},{9,8},{11,9},{13,1... | collective-permute-start | bytes 1400840 | tf_op jit(solution)/shard_map/ppermute | solution.py:550
  68.3 21.1 %collective-permute-start.20 = (bf16[96,2688]{1,0:T(8,128)(2,1)S(1)}, bf16[96,2688]{1,0:T(8,128)(2,1)S(1)}, u32[]{:S(2)}, u32[]{:S(2)}) collective-permute-start(bf16[96,2688]{1,0:T(8,128)(2,1)S(1)} %collective-permute-done.19.refs_4_.refs_12_.refs_20_.refs_28_), channel_id=1, source_target_pairs={{1,3},{3,5},{5,7},{7,6},{6,4},{4,2},{2,0},{0,1},{9,11},{11,13},{13... | collective-permute-start | bytes 1548296 | tf_op jit(solution)/shard_map/ppermute | solution.py:550
  69.9 21.1 %collective-permute-start.25 = (bf16[96,2688]{1,0:T(8,128)(2,1)S(1)}, bf16[96,2688]{1,0:T(8,128)(2,1)S(1)}, u32[]{:S(2)}, u32[]{:S(2)}) collective-permute-start(bf16[96,2688]{1,0:T(8,128)(2,1)S(1)} %collective-permute-done.24.refs_36_.refs_44_.refs_4_.refs_12_), channel_id=1, source_target_pairs={{1,0},{3,1},{5,3},{7,5},{6,7},{4,6},{2,4},{0,2},{9,8},{11,9},{13,1... | collective-permute-start | bytes 1548296 | tf_op jit(solution)/shard_map/ppermute | solution.py:550
  78.3 21.1 %collective-permute-start.13 = (bf16[96,2432]{1,0:T(8,128)(2,1)S(1)}, bf16[96,2432]{1,0:T(8,128)(2,1)S(1)}, u32[]{:S(2)}, u32[]{:S(2)}) collective-permute-start(bf16[96,2432]{1,0:T(8,128)(2,1)S(1)} %collective-permute-done.12.refs_2_), channel_id=1, source_target_pairs={{1,3},{3,5},{5,7},{7,6},{6,4},{4,2},{2,0},{0,1},{9,11},{11,13},{13... | collective-permute-start | bytes 1400840 | tf_op jit(solution)/shard_map/ppermute | solution.py:550
  79.9 21.1 %collective-permute-start.4 = (bf16[96,2432]{1,0:T(8,128)(2,1)S(1)}, bf16[96,2432]{1,0:T(8,128)(2,1)S(1)}, u32[]{:S(2)}, u32[]{:S(2)}) collective-permute-start(bf16[96,2432]{1,0:T(8,128)(2,1)S(1)} %collective-permute-done.3.refs_2_), channel_id=1, source_target_pairs={{1,0},{3,1},{5,3},{7,5},{6,7},{4,6},{2,4},{0,2},{9,8},{11,9},{13,1... | collective-permute-start | bytes 1400840 | tf_op jit(solution)/shard_map/ppermute | solution.py:550
  89.4 21.1 %collective-permute-start.21 = (bf16[96,2688]{1,0:T(8,128)(2,1)S(1)}, bf16[96,2688]{1,0:T(8,128)(2,1)S(1)}, u32[]{:S(2)}, u32[]{:S(2)}) collective-permute-start(bf16[96,2688]{1,0:T(8,128)(2,1)S(1)} %collective-permute-done.20.refs_5_.refs_13_.refs_21_.refs_29_), channel_id=1, source_target_pairs={{1,3},{3,5},{5,7},{7,6},{6,4},{4,2},{2,0},{0,1},{9,11},{11,13},{13... | collective-permute-start | bytes 1548296 | tf_op jit(solution)/shard_map/ppermute | solution.py:550
  91.0 21.1 %collective-permute-start.26 = (bf16[96,2688]{1,0:T(8,128)(2,1)S(1)}, bf16[96,2688]{1,0:T(8,128)(2,1)S(1)}, u32[]{:S(2)}, u32[]{:S(2)}) collective-permute-start(bf16[96,2688]{1,0:T(8,128)(2,1)S(1)} %collective-permute-done.25.refs_37_.refs_45_.refs_5_.refs_13_), channel_id=1, source_target_pairs={{1,0},{3,1},{5,3},{7,5},{6,7},{4,6},{2,4},{0,2},{9,8},{11,9},{13,1... | collective-permute-start | bytes 1548296 | tf_op jit(solution)/shard_map/ppermute | solution.py:550
  99.4 21.1 %collective-permute-start.14 = (bf16[96,2432]{1,0:T(8,128)(2,1)S(1)}, bf16[96,2432]{1,0:T(8,128)(2,1)S(1)}, u32[]{:S(2)}, u32[]{:S(2)}) collective-permute-start(bf16[96,2432]{1,0:T(8,128)(2,1)S(1)} %collective-permute-done.13.refs_3_), channel_id=1, source_target_pairs={{1,3},{3,5},{5,7},{7,6},{6,4},{4,2},{2,0},{0,1},{9,11},{11,13},{13... | collective-permute-start | bytes 1400840 | tf_op jit(solution)/shard_map/ppermute | solution.py:550
  101.0 21.1 %collective-permute-start.5 = (bf16[96,2432]{1,0:T(8,128)(2,1)S(1)}, bf16[96,2432]{1,0:T(8,128)(2,1)S(1)}, u32[]{:S(2)}, u32[]{:S(2)}) collective-permute-start(bf16[96,2432]{1,0:T(8,128)(2,1)S(1)} %collective-permute-done.4.refs_3_), channel_id=1, source_target_pairs={{1,0},{3,1},{5,3},{7,5},{6,7},{4,6},{2,4},{0,2},{9,8},{11,9},{13,1... | collective-permute-start | bytes 1400840 | tf_op jit(solution)/shard_map/ppermute | solution.py:550
  110.4 30.3 %collective-permute-start.22 = (bf16[96,2688]{1,0:T(8,128)(2,1)S(1)}, bf16[96,2688]{1,0:T(8,128)(2,1)S(1)}, u32[]{:S(2)}, u32[]{:S(2)}) collective-permute-start(bf16[96,2688]{1,0:T(8,128)(2,1)S(1)} %collective-permute-done.21.refs_6_.refs_14_.refs_22_.refs_30_), channel_id=1, source_target_pairs={{1,3},{3,5},{5,7},{7,6},{6,4},{4,2},{2,0},{0,1},{9,11},{11,13},{13... | collective-permute-start | bytes 1548296 | tf_op jit(solution)/shard_map/ppermute | solution.py:550
  112.0 28.8 %collective-permute-start.27 = (bf16[96,2688]{1,0:T(8,128)(2,1)S(1)}, bf16[96,2688]{1,0:T(8,128)(2,1)S(1)}, u32[]{:S(2)}, u32[]{:S(2)}) collective-permute-start(bf16[96,2688]{1,0:T(8,128)(2,1)S(1)} %collective-permute-done.26.refs_38_.refs_46_.refs_6_.refs_14_), channel_id=1, source_target_pairs={{1,0},{3,1},{5,3},{7,5},{6,7},{4,6},{2,4},{0,2},{9,8},{11,9},{13,1... | collective-permute-start | bytes 1548296 | tf_op jit(solution)/shard_map/ppermute | solution.py:550
  120.5 18.3 %collective-permute-start.15 = (bf16[96,2432]{1,0:T(8,128)(2,1)S(1)}, bf16[96,2432]{1,0:T(8,128)(2,1)S(1)}, u32[]{:S(2)}, u32[]{:S(2)}) collective-permute-start(bf16[96,2432]{1,0:T(8,128)(2,1)S(1)} %collective-permute-done.14.refs_4_), channel_id=1, source_target_pairs={{1,3},{3,5},{5,7},{7,6},{6,4},{4,2},{2,0},{0,1},{9,11},{11,13},{13... | collective-permute-start | bytes 1400840 | tf_op jit(solution)/shard_map/ppermute | solution.py:550
  122.0 18.3 %collective-permute-start.6 = (bf16[96,2432]{1,0:T(8,128)(2,1)S(1)}, bf16[96,2432]{1,0:T(8,128)(2,1)S(1)}, u32[]{:S(2)}, u32[]{:S(2)}) collective-permute-start(bf16[96,2432]{1,0:T(8,128)(2,1)S(1)} %collective-permute-done.5.refs_4_), channel_id=1, source_target_pairs={{1,0},{3,1},{5,3},{7,5},{6,7},{4,6},{2,4},{0,2},{9,8},{11,9},{13,1... | collective-permute-start | bytes 1400840 | tf_op jit(solution)/shard_map/ppermute | solution.py:550
  138.7 11.6 %collective-permute-start.16 = (bf16[96,2432]{1,0:T(8,128)(2,1)S(1)}, bf16[96,2432]{1,0:T(8,128)(2,1)S(1)}, u32[]{:S(2)}, u32[]{:S(2)}) collective-permute-start(bf16[96,2432]{1,0:T(8,128)(2,1)S(1)} %collective-permute-done.15.refs_5_), channel_id=1, source_target_pairs={{1,3},{3,5},{5,7},{7,6},{6,4},{4,2},{2,0},{0,1},{9,11},{11,13},{13... | collective-permute-start | bytes 1400840 | tf_op jit(solution)/shard_map/ppermute | solution.py:550
  140.3 10.0 %collective-permute-start.7 = (bf16[96,2432]{1,0:T(8,128)(2,1)S(1)}, bf16[96,2432]{1,0:T(8,128)(2,1)S(1)}, u32[]{:S(2)}, u32[]{:S(2)}) collective-permute-start(bf16[96,2432]{1,0:T(8,128)(2,1)S(1)} %collective-permute-done.6.refs_5_), channel_id=1, source_target_pairs={{1,0},{3,1},{5,3},{7,5},{6,7},{4,6},{2,4},{0,2},{9,8},{11,9},{13,1... | collective-permute-start | bytes 1400840 | tf_op jit(solution)/shard_map/ppermute | solution.py:550
  150.4 11.0 %collective-permute-start.17 = (bf16[96,2432]{1,0:T(8,128)(2,1)S(1)}, bf16[96,2432]{1,0:T(8,128)(2,1)S(1)}, u32[]{:S(2)}, u32[]{:S(2)}) collective-permute-start(bf16[96,2432]{1,0:T(8,128)(2,1)S(1)} %collective-permute-done.16.refs_6_), channel_id=1, source_target_pairs={{1,3},{3,5},{5,7},{7,6},{6,4},{4,2},{2,0},{0,1},{9,11},{11,13},{13... | collective-permute-start | bytes 1400840 | tf_op jit(solution)/shard_map/ppermute | solution.py:550
  152.0 14.4 %collective-permute-start.8 = (bf16[96,2432]{1,0:T(8,128)(2,1)S(1)}, bf16[96,2432]{1,0:T(8,128)(2,1)S(1)}, u32[]{:S(2)}, u32[]{:S(2)}) collective-permute-start(bf16[96,2432]{1,0:T(8,128)(2,1)S(1)} %collective-permute-done.7.refs_6_), channel_id=1, source_target_pairs={{1,0},{3,1},{5,3},{7,5},{6,7},{4,6},{2,4},{0,2},{9,8},{11,9},{13,1... | collective-permute-start | bytes 1400840 | tf_op jit(solution)/shard_map/ppermute | solution.py:550
  171.7 5.5 %collective-permute-start.28 = (bf16[6,256,256]{2,1,0:T(8,128)(2,1)S(1)}, bf16[6,256,256]{2,1,0:T(8,128)(2,1)S(1)}, u32[]{:S(2)}, u32[]{:S(2)}) collective-permute-start(bf16[6,256,256]{2,1,0:T(8,128)(2,1)S(1)} %fold.1), channel_id=1, source_target_pairs={{24,16},{25,17},{26,18},{27,19},{28,20},{29,21},{30,22},{31,23}} | collective-permute-start | bytes 2359304 | tf_op jit(solution)/shard_map/ppermute | solution.py:584
  179.1 0.7 collective-permute-start.29
  181.6 15.5 %collective-permute-start.30 = (bf16[6,256,256]{2,1,0:T(8,128)(2,1)S(1)}, bf16[6,256,256]{2,1,0:T(8,128)(2,1)S(1)}, u32[]{:S(2)}, u32[]{:S(2)}) collective-permute-start(bf16[6,256,256]{2,1,0:T(8,128)(2,1)S(1)} %hop.3), channel_id=1, source_target_pairs={{8,0},{9,1},{10,2},{11,3},{12,4},{13,5},{14,6},{15,7}} | collective-permute-start | bytes 2359304 | tf_op jit(solution)/shard_map/ppermute | solution.py:584

commit v12 on v11

--- a/solution.py
+++ b/solution.py
@@ -13,7 +13,6 @@
 LANES = 128
 TILE = 256
 LINE = 4
-GATE = 2
 MIB = 1024 * 1024
 CLAIM = 60 * MIB
 
@@ -67,16 +66,16 @@
     if len(refs) > len(ranges):
         main, extra = packed_half(refs[0][...], place, count)
         at = (ranges[0][1] - ranges[0][0]) * stride + LANES
-        outs[0][:, at:] = main[:, :2 * LANES]
-        outs[1][:, at:at + LANES] = main[:, 2 * LANES:]
-        outs[1][:, at + LANES:] = extra.astype(BF16)
+        outs[0][:, at:at + width // 2] = main
+        outs[0][:, at + width // 2:] = extra.astype(BF16)
 
 
 def pack(place, gains, increments, terminal, count, ranges):
     rows, width = gains.shape[1:]
     first, size = ranges[1][0], ranges[0][1] - ranges[1][0]
     ends = [] if terminal is None else [terminal]
-    lanes = [(high - low) * (width + width // 2) + LANES * (1 + 2 * len(ends)) for low, high in ranges]
+    lanes = [(high - low) * (width + width // 2) + LANES for low, high in ranges]
+    lanes[0] += (width // 2 + LANES) * len(ends)
     some = pl.BlockSpec((size, rows, width), lambda i, p: (first // size, 0, 0))
     return pl.pallas_call(
         functools.partial(pack_kernel, count, ranges),
@@ -100,14 +99,15 @@
         half[n * rows:(n + 1) * rows, :] = unpacked_half(raw[n], extra, n, count).astype(BF16)
 
 
-def origins(place, cycle, way):
+def origins(place, cycle, right):
     count = len(cycle)
 
     def look(table, at):
         return sum(jnp.where(at == n, value, 0) for n, value in enumerate(table))
 
     spot = look([cycle.index(d) for d in range(count)], place)
-    return [look(cycle, lax.rem(spot - way * n + count, count)) for n in range(count)]
+    hops = [0] + [-n for n in range(1, right + 1)] + list(range(1, count - right))
+    return [look(cycle, lax.rem(spot + n + count, count)) for n in hops]
 
 
 def assemble(places, blocks, sides, step, gain, fresh, raw, extras):
@@ -144,12 +144,13 @@
     return own + nt(jnp.where(picked, 1.0, 0.0).astype(BF16), half[...])
 
 
-def compose_kernel(cycle, way, first, last_ref, place_ref, *refs):
+def compose_kernel(cycle, right, first, last_ref, place_ref, *refs):
     count = len(cycle)
-    places = origins(place_ref[0], cycle, way)
+    places = origins(place_ref[0], cycle, right)
     blocks, sides, refs = refs[:count], refs[count:2 * count], refs[2 * count:]
+    tiles = blocks[0].shape[1] // 3 // LANES
     if first:
-        ends, refs = refs[:4 * count], refs[4 * count:]
+        ends, refs = refs[:(tiles + 1) * count], refs[(tiles + 1) * count:]
     else:
         half_in, factor_in, refs = refs[0], refs[1], refs[4:]
     factor_out, own_out, mine_out, half, gain, factor, fresh, middle, raw, extras = refs
@@ -159,12 +160,11 @@
     def _():
         if first:
             scale = jnp.where(last_ref[0] == 1, 1.0, 0.0).astype(BF16)
-            back = origins(place_ref[0], cycle, -way)
             for n in range(count):
-                raw[places[n], :, :LANES] = ends[n][...] * scale
-                raw[places[n], :, LANES:2 * LANES] = ends[count + n][...] * scale
-                raw[back[n], :, 2 * LANES:] = ends[2 * count + n][...] * scale
-                extras[back[n]] = ends[3 * count + n][...] * scale
+                for tile in range(tiles):
+                    lanes = slice(tile * LANES, (tile + 1) * LANES)
+                    raw[places[n], :, lanes] = ends[tile * count + n][...] * scale
+                extras[places[n]] = ends[tiles * count + n][...] * scale
             unpack(raw, extras, 0, half)
         else:
             factor[...] = factor_in[0]
@@ -210,7 +210,7 @@
     ]
 
 
-def compose(last, place, cycle, way, blocks, ends, state, half, low, turns, steps):
+def compose(last, place, cycle, right, blocks, state, half, low, turns, steps):
     count = len(blocks)
     rows = blocks[0].shape[0]
     width = rows * count
@@ -219,11 +219,11 @@
     in_specs = row_specs(blocks, turns)
     if first:
         at = turns * width * 3 // 2 // LANES + 1
-        for n in (at, at + 1):
+        tiles = width // 2 // LANES + 1
+        for n in range(at, at + tiles):
             tile = pl.BlockSpec((rows, LANES), lambda i, *p, n=n: (0, n), pipeline_mode=pl.Buffered(1))
             in_specs += [tile] * count
-        in_specs += in_specs[-2 * count:]
-        args = ends[:count] * 2 + ends[count:] * 2
+        args = list(blocks) * tiles
     else:
         after = pl.BlockSpec((1, width, width), lambda i, *p: (low + turns, 0, 0), pipeline_mode=pl.Buffered(1))
         in_specs += [square(width), after, anywhere, anywhere]
@@ -231,7 +231,7 @@
     band = pl.BlockSpec((1, rows, width), lambda i, *p: (low + turns - 1 - i, 0, 0))
     base = 2 + 2 * count + 1
     return pl.pallas_call(
-        functools.partial(compose_kernel, cycle, way, first),
+        functools.partial(compose_kernel, cycle, right, first),
         grid_spec=pltpu.PrefetchScalarGridSpec(
             num_scalar_prefetch=2,
             grid=(turns,),
@@ -254,9 +254,9 @@
     )(last, place, *blocks, *blocks, *args)
 
 
-def chain_kernel(cycle, way, turns, place_ref, *refs):
+def chain_kernel(cycle, right, turns, place_ref, *refs):
     count = len(cycle)
-    places = origins(place_ref[0], cycle, way)
+    places = origins(place_ref[0], cycle, right)
     blocks, refs = refs[:count], refs[count:]
     half_in, refs = refs[0], refs[-9:]
     gain_out, half_out, half, middle, raw, extras, gain, fresh, spare = refs
@@ -277,7 +277,7 @@
         @pl.when(pl.program_id(0) == turn)
         def _():
             if turn == 0:
-                half[...] = half_in[...].reshape(half.shape)
+                half[...] = half_in[...]
                 prepare(0)
             gain_out[0] = gains[turn % 2][...]
             if turn + 1 < turns:
@@ -286,28 +286,18 @@
             half_out[0] = half[...]
 
 
-def chain(place, cycle, way, blocks, half, state, low, turns, steps):
+def chain(place, cycle, right, blocks, half, turns):
     count = len(blocks)
     rows = blocks[0].shape[0]
     width = rows * count
-    anywhere = pl.BlockSpec(memory_space=pl.ANY)
     in_specs = [pl.BlockSpec(blocks[0].shape, lambda i, *p: (0, 0), pipeline_mode=pl.Buffered(1))] * count
-    if state is None:
-        in_specs += [square(width)]
-        args = [half]
-    else:
-        in_specs += [
-            pl.BlockSpec((1, width, width), lambda i, *p: (low + turns, 0, 0), pipeline_mode=pl.Buffered(1)),
-            anywhere,
-        ]
-        args = [state[1], state[0]]
-    whole = square(width, lambda i: low + turns - 1 - i)
-    return pl.pallas_call(
-        functools.partial(chain_kernel, cycle, way, turns),
+    whole = square(width, lambda i: turns - 1 - i)
+    return pl.pallas_call(
+        functools.partial(chain_kernel, cycle, right, turns),
         grid_spec=pltpu.PrefetchScalarGridSpec(
             num_scalar_prefetch=1,
             grid=(turns,),
-            in_specs=in_specs,
+            in_specs=in_specs + [square(width)],
             out_specs=[whole, whole],
             scratch_shapes=[
                 pltpu.VMEM((width, width), BF16),
@@ -319,14 +309,13 @@
                 pltpu.VMEM((2, width, width), BF16),
             ],
         ),
-        out_shape=[jax.ShapeDtypeStruct((steps, width, width), BF16)] * 2,
-        input_output_aliases={} if state is None else {1 + count + 1: 0, 1 + count: 1},
+        out_shape=[jax.ShapeDtypeStruct((turns, width, width), BF16)] * 2,
         compiler_params=pltpu.CompilerParams(vmem_limit_bytes=18 * MIB),
         cost_estimate=pl.CostEstimate(
             flops=4 * turns * width**3, bytes_accessed=8 * turns * width * width, transcendentals=0
         ),
         name="chain",
-    )(place, *blocks, *args)
+    )(place, *blocks, half)
 
 
 def factors_kernel(place_ref, gain_ref, factor_in, mine_ref, factor_out, mine_out, factor):
@@ -532,9 +521,8 @@
 
 
 def pieces(steps):
-    small = max(steps // 8, 1)
-    cuts = [0, 2 * small, 4 * small, 6 * small, steps]
-    return list(zip(cuts, cuts[1:]))[::-1]
+    size = steps // 4
+    return [(low, low + size) for low in reversed(range(0, steps, size))]
 
 
 def local(gains, increments, terminal):
@@ -553,30 +541,35 @@
     own = list(pack(place, gains, increments, terminal, count, ranges[:2]))
     own += pack(place, gains, increments, None, count, ranges[2:])
     own[:2], last = lax.optimization_barrier((own[:2], last))
-    arrived = []
+    rights = [count // 2 - turn % 2 for turn in range(len(own))]
+    found = []
     for turn, array in enumerate(own):
-        way = 1 if turn % 2 == 0 else -1
-        if turn >= 2:
-            before = arrived[turn - 2]
-            array, before[GATE] = lax.optimization_barrier((array, before[GATE]))
-            for hop_count in range(GATE + 1, count):
-                before[hop_count] = passed(before[hop_count - 1], way)
-        found = [array]
-        for hop_count in range(1, count):
-            found.append(passed(found[-1], way))
-        arrived.append(found)
+        found.append({})
+        for way, hops in ((1, rights[turn]), (-1, count - 1 - rights[turn])):
+            source = array
+            if turn:
+                before = found[turn - 1][way]
+                gate = len(before) - 3
+                source, before[gate] = lax.optimization_barrier((source, before[gate]))
+                for n in range(gate + 1, len(before)):
+                    before[n] = passed(before[n - 1], way)
+            found[turn][way] = [source]
+            for _ in range(hops):
+                found[turn][way].append(passed(found[turn][way][-1], way))
+    ties = [
+        [found[1][1][2], found[2][1][1], found[1][-1][3], found[2][-1][1]],
+        [found[2][1][2], found[2][-1][2], found[3][-1][1]],
+        [found[3][1][-2], found[3][-1][-2]],
+    ]
     state, half = None, None
-    for turn in range(2):
-        reached = count - 3 + turn
-        arrived[:2], _ = lax.optimization_barrier((arrived[:2], (arrived[2][reached], arrived[3][reached])))
-        ends = [] if turn else arrived[0] + arrived[1]
-        low, high = ranges[turn]
-        *state, half = compose(last, place, cycle, 1 - 2 * turn, arrived[turn], ends, state, half, low, high - low, steps)
+    for turn, (low, high) in enumerate(ranges):
+        parts = [own[turn]] + found[turn][1][1:] + found[turn][-1][1:]
+        if turn < len(ties):
+            parts, _ = lax.optimization_barrier((parts, ties[turn]))
+            *state, half = compose(last, place, cycle, rights[turn], parts, state, half, low, high - low, steps)
+        else:
+            early = chain(place, cycle, rights[turn], parts, half, high)
     factors, own, mine = state
-    early = None
-    for turn in range(2, 4):
-        low, high = ranges[turn]
-        early = chain(place, cycle, 5 - 2 * turn, arrived[turn], half, early, low, high - low, ranges[2][1])
     factors, mine = extend_factors(place, early[0], factors, mine)
     own = own_rows(place, early[1], own)
     packed = []

time: 203 us -> 194 us (0.956)
  waiting for transfers between devices: 121 us -> 111 us
    ppermute x28, waiting for transfers between devices: 109 us -> 98.1 us  [passed(): lax.ppermute(array, 'tile', [(cycle[n], cycle[(n + way) % count]) for n i...]
    pallas_call x4, Pallas kernels: 28.5 us -> 32.1 us  [the longest x3 27.1 us: compose(): pl.pallas_call(functools.partial(compose_kernel, cycle, right, first), gr...]
    pallas_call x1, Pallas kernels: 4.55 us -> 2.32 us  [extend_factors(): pl.pallas_call(factors_kernel, grid_spec=pltpu.PrefetchScalarGridSpec(num...]
  transfers between devices with their start and end apart: 31 -> 31, of which waited for: 13 -> 14; matrix products, arithmetic and copies ran while one was open for 0% -> 0% of each run, Pallas kernels for 15% -> 16%
where the time goes in v12:
time: 194 us
  waiting for transfers between devices  111 us (57%)
  Pallas kernels  49.3 us (25%)
  starting transfers between devices  33.2 us (17%)
    ppermute x28, waiting for transfers between devices, passed(): lax.ppermute(array, 'tile', [(cycle[n], cycle[(n + way) % count]) for n i...  98.1 us
    ppermute x28, starting transfers between devices, passed(): lax.ppermute(array, 'tile', [(cycle[n], cycle[(n + way) % count]) for n i...  30.3 us
    pallas_call x3, Pallas kernels, compose(): pl.pallas_call(functools.partial(compose_kernel, cycle, right, first), gr...  27.1 us
    ppermute x3, waiting for transfers between devices, local(): lax.ppermute(hop(factors, early[1], packed), 'tm', [(turn, turn - 1)])  13.4 us
    pallas_call x1, Pallas kernels, finish(): pl.pallas_call(functools.partial(finish_kernel, len(packed)), grid=(steps...  5.6 us
    pallas_call x1, Pallas kernels, chain(): pl.pallas_call(functools.partial(chain_kernel, cycle, right, turns), grid...  5.03 us
    pallas_call x2, Pallas kernels, pack(): pl.pallas_call(functools.partial(pack_kernel, count, ranges), grid_spec=p...  4.27 us
  transfers between devices with their start and end apart: 31, of which 14 were waited for; matrix products, arithmetic and copies ran while one was open for 0% of the time, Pallas kernels for 16%

profile of v12, /device:TPU:0, one launch (start us, length us, event | category | flops | bytes accessed | tf_op | source)
XLA Modules:
  0.0 194.2 jit_solution(3324788445764833333)
XLA Ops:
  0.0 3.6 %pack.3 = (bf16[96,2944]{1,0:T(8,128)(2,1)}, bf16[96,2432]{1,0:T(8,128)(2,1)}) custom-call(s32[1]{0:T(128)} %bitcast.place_ref, bf16[8,96,768]{2,1,0:T(8,128)(2,1)} %gain_ref.3, f32[8,96,768]{2,1,0:T(8,128)} %increment_ref.3, f32[96,768]{1,0:T(8,128)} %refs_0_.1), custom_call_target="tpu_custom_call" | custom-call | tf_op jit(solution)/shard_map/pack/pallas_call | solution.py:80
  3.6 3.0 %collective-permute-start = (bf16[96,2944]{1,0:T(8,128)(2,1)}, bf16[96,2944]{1,0:T(8,128)(2,1)S(1)}, u32[]{:S(2)}, u32[]{:S(2)}) collective-permute-start(bf16[96,2944]{1,0:T(8,128)(2,1)} %get-tuple-element.99.refs_0_.refs_8_.refs_16_.refs_24_.refs_32_.refs_40_), channel_id=1, source_target_pairs={{1,3},{3,5},{5,7},{7,6},{6,4},{4,2},{2,0},{0,1},{9,11},{11,13},{13... | collective-permute-start | bytes 1695752 | tf_op jit(solution)/shard_map/ppermute | solution.py:538
  6.6 13.0 %collective-permute-done.refs_1_.refs_9_.refs_17_.refs_25_.refs_33_.refs_41_ = bf16[96,2944]{1,0:T(8,128)(2,1)S(1)} collective-permute-done((bf16[96,2944]{1,0:T(8,128)(2,1)}, bf16[96,2944]{1,0:T(8,128)(2,1)S(1)}, u32[]{:S(2)}, u32[]{:S(2)}) %collective-permute-start) | collective-permute-done | bytes 565280 | tf_op jit(solution)/shard_map/ppermute | solution.py:538
  19.7 1.6 collective-permute-start.1
  21.3 0.4 collective-permute-start.9
  21.7 1.7 collective-permute-start.26
  23.4 11.8 %collective-permute-done.9.refs_4_.refs_12_ = bf16[96,2432]{1,0:T(8,128)(2,1)S(1)} collective-permute-done((bf16[96,2432]{1,0:T(8,128)(2,1)}, bf16[96,2432]{1,0:T(8,128)(2,1)S(1)}, u32[]{:S(2)}, u32[]{:S(2)}) %collective-permute-start.9) | collective-permute-done | bytes 466976 | tf_op jit(solution)/shard_map/ppermute | solution.py:538
  35.5 1.6 collective-permute-start.2
  37.2 1.6 collective-permute-start.24
  38.7 8.5 %collective-permute-done.26.refs_6_.refs_14_.refs_22_.refs_30_.refs_38_.refs_46_ = bf16[96,2944]{1,0:T(8,128)(2,1)S(1)} collective-permute-done((bf16[96,2944]{1,0:T(8,128)(2,1)S(1)}, bf16[96,2944]{1,0:T(8,128)(2,1)S(1)}, u32[]{:S(2)}, u32[]{:S(2)}) %collective-permute-start.26) | collective-permute-done | bytes 565280 | tf_op jit(solution)/shard_map/ppermute | solution.py:538
  47.7 0.7 pack.2
  48.4 8.9 %collective-permute-done.10.refs_5_.refs_13_ = bf16[96,2432]{1,0:T(8,128)(2,1)S(1)} collective-permute-done((bf16[96,2432]{1,0:T(8,128)(2,1)S(1)}, bf16[96,2432]{1,0:T(8,128)(2,1)S(1)}, u32[]{:S(2)}, u32[]{:S(2)}) %collective-permute-start.10) | collective-permute-done | bytes 466976 | tf_op jit(solution)/shard_map/ppermute | solution.py:538
  57.7 1.6 collective-permute-start.3
  59.7 1.6 collective-permute-start.25
  61.3 18.1 %collective-permute-done.11.refs_5_.refs_13_ = bf16[96,2432]{1,0:T(8,128)(2,1)S(1)} collective-permute-done((bf16[96,2432]{1,0:T(8,128)(2,1)S(1)}, bf16[96,2432]{1,0:T(8,128)(2,1)S(1)}, u32[]{:S(2)}, u32[]{:S(2)}) %collective-permute-start.11) | collective-permute-done | bytes 466976 | tf_op jit(solution)/shard_map/ppermute | solution.py:538
  79.4 1.6 collective-permute-start.20
  80.9 0.5 collective-permute-start.12
  81.4 1.6 collective-permute-start.4
  83.0 6.4 %collective-permute-done.22.refs_6_.refs_14_ = bf16[96,2432]{1,0:T(8,128)(2,1)S(1)} collective-permute-done((bf16[96,2432]{1,0:T(8,128)(2,1)S(1)}, bf16[96,2432]{1,0:T(8,128)(2,1)S(1)}, u32[]{:S(2)}, u32[]{:S(2)}) %collective-permute-start.22) | collective-permute-done | bytes 466976 | tf_op jit(solution)/shard_map/ppermute | solution.py:538
  89.8 3.2 %collective-permute-done.20.refs_2_.refs_10_ = bf16[96,2432]{1,0:T(8,128)(2,1)S(1)} collective-permute-done((bf16[96,2432]{1,0:T(8,128)(2,1)S(1)}, bf16[96,2432]{1,0:T(8,128)(2,1)S(1)}, u32[]{:S(2)}, u32[]{:S(2)}) %collective-permute-start.20) | collective-permute-done | bytes 466976 | tf_op jit(solution)/shard_map/ppermute | solution.py:538
  93.0 0.4 collective-permute-start.23
  93.4 1.6 collective-permute-start.21
  95.0 4.4 %collective-permute-done.12.refs_4_ = bf16[96,2432]{1,0:T(8,128)(2,1)S(1)} collective-permute-done((bf16[96,2432]{1,0:T(8,128)(2,1)S(1)}, bf16[96,2432]{1,0:T(8,128)(2,1)S(1)}, u32[]{:S(2)}, u32[]{:S(2)}) %collective-permute-start.12) | collective-permute-done | bytes 466976 | tf_op jit(solution)/shard_map/ppermute | solution.py:538
  99.8 3.2 %collective-permute-done.4.refs_2_.refs_10_ = bf16[96,2432]{1,0:T(8,128)(2,1)S(1)} collective-permute-done((bf16[96,2432]{1,0:T(8,128)(2,1)S(1)}, bf16[96,2432]{1,0:T(8,128)(2,1)S(1)}, u32[]{:S(2)}, u32[]{:S(2)}) %collective-permute-start.4) | collective-permute-done | bytes 466976 | tf_op jit(solution)/shard_map/ppermute | solution.py:538
  103.0 1.6 collective-permute-start.16
  104.6 4.8 %collective-permute-done.18.refs_6_.refs_14_ = bf16[96,2432]{1,0:T(8,128)(2,1)S(1)} collective-permute-done((bf16[96,2432]{1,0:T(8,128)(2,1)S(1)}, bf16[96,2432]{1,0:T(8,128)(2,1)S(1)}, u32[]{:S(2)}, u32[]{:S(2)}) %collective-permute-start.18) | collective-permute-done | bytes 466976 | tf_op jit(solution)/shard_map/ppermute | solution.py:538
  109.4 1.6 collective-permute-start.5
  111.0 9.3 %compose.3 = (bf16[8,768,768]{2,1,0:T(8,128)(2,1)S(1)}, f32[8,96,768]{2,1,0:T(8,128)S(1)}, bf16[8,96,768]{2,1,0:T(8,128)(2,1)S(1)}, bf16[768,768]{1,0:T(8,128)(2,1)S(1)}) custom-call(s32[1]{0:T(128)} %bitcast.1.last_ref, s32[1]{0:T(128)} %bitcast.place_ref, bf16[96,2944]{1,0:T(8,128)(2,1)S(1)} %copy-done, ...), custom_call_target="tpu_custom_call" | custom-call | flops 5435817984 | bytes 9437184 | tf_op jit(solution)/shard_map/compose/pallas_call | solution.py:233
  120.3 0.5 collective-permute-start.19
  120.8 8.6 %collective-permute-done.13.refs_5_ = bf16[96,2432]{1,0:T(8,128)(2,1)S(1)} collective-permute-done((bf16[96,2432]{1,0:T(8,128)(2,1)S(1)}, bf16[96,2432]{1,0:T(8,128)(2,1)S(1)}, u32[]{:S(2)}, u32[]{:S(2)}) %collective-permute-start.13) | collective-permute-done | bytes 466976 | tf_op jit(solution)/shard_map/ppermute | solution.py:538
  129.8 1.6 collective-permute-start.17
  131.4 1.6 collective-permute-start.6
  133.0 8.9 %compose.4 = (bf16[8,768,768]{2,1,0:T(8,128)(2,1)S(1)}, f32[8,96,768]{2,1,0:T(8,128)S(1)}, bf16[8,96,768]{2,1,0:T(8,128)(2,1)S(1)}, bf16[768,768]{1,0:T(8,128)(2,1)S(1)}) custom-call(s32[1]{0:T(128)} %bitcast.1.last_ref, s32[1]{0:T(128)} %bitcast.place_ref, ...), custom_call_target="tpu_custom_call", output_to_operand_aliasing={{0}: (19, {}), {1}: (20, {}), {2}: (21, {})} | custom-call | flops 5435817984 | bytes 9437184 | tf_op jit(solution)/shard_map/compose/pallas_call | solution.py:233
  141.9 5.2 %collective-permute-done.14.refs_6_ = bf16[96,2432]{1,0:T(8,128)(2,1)S(1)} collective-permute-done((bf16[96,2432]{1,0:T(8,128)(2,1)S(1)}, bf16[96,2432]{1,0:T(8,128)(2,1)S(1)}, u32[]{:S(2)}, u32[]{:S(2)}) %collective-permute-start.14) | collective-permute-done | bytes 466976 | tf_op jit(solution)/shard_map/ppermute | solution.py:538
  147.1 0.7 collective-permute-start.15
  147.8 2.1 %collective-permute-done.6.refs_2_ = bf16[96,2432]{1,0:T(8,128)(2,1)S(1)} collective-permute-done((bf16[96,2432]{1,0:T(8,128)(2,1)S(1)}, bf16[96,2432]{1,0:T(8,128)(2,1)S(1)}, u32[]{:S(2)}, u32[]{:S(2)}) %collective-permute-start.6) | collective-permute-done | bytes 466976 | tf_op jit(solution)/shard_map/ppermute | solution.py:538
  149.9 1.0 collective-permute-start.7
  150.9 8.9 %compose.5 = (bf16[8,768,768]{2,1,0:T(8,128)(2,1)S(1)}, f32[8,96,768]{2,1,0:T(8,128)S(1)}, bf16[8,96,768]{2,1,0:T(8,128)(2,1)S(1)}, bf16[768,768]{1,0:T(8,128)(2,1)S(1)}) custom-call(s32[1]{0:T(128)} %bitcast.1.last_ref, s32[1]{0:T(128)} %bitcast.place_ref, ...), custom_call_target="tpu_custom_call", output_to_operand_aliasing={{0}: (19, {}), {1}: (20, {}), {2}: (21, {})} | custom-call | flops 5435817984 | bytes 9437184 | tf_op jit(solution)/shard_map/compose/pallas_call | solution.py:233
  159.8 5.0 %chain.1 = (bf16[2,768,768]{2,1,0:T(8,128)(2,1)S(1)}, bf16[2,768,768]{2,1,0:T(8,128)(2,1)S(1)}) custom-call(s32[1]{0:T(128)} %bitcast.place_ref, bf16[96,2432]{1,0:T(8,128)(2,1)S(1)} %get-tuple-element.75.refs_0_, bf16[96,2432]{1,0:T(8,128)(2,1)S(1)} %collective-permute-done.5.refs_1_, bf16[96,2432]{1,0:T(8,128)(2,1)S(1)} %collective-permute-done.6.refs_2_, ...), custom_call_target="tpu_custom_call" | custom-call | flops 3623878656 | bytes 9437184 | tf_op jit(solution)/shard_map/chain/pallas_call | solution.py:295
  165.1 0.9 collective-permute-start.28
  166.1 2.3 %extend_factors.1 = (bf16[8,768,768]{2,1,0:T(8,128)(2,1)S(1)}, bf16[8,96,768]{2,1,0:T(8,128)(2,1)S(1)}) custom-call(s32[1]{0:T(128)} %bitcast.place_ref, bf16[2,768,768]{2,1,0:T(8,128)(2,1)S(1)} %get-tuple-element.116.gain_ref, bf16[8,768,768]{2,1,0:T(8,128)(2,1)S(1)} %get-tuple-element.117.factor_in, ...), custom_call_target="tpu_custom_call", output_to_operand_aliasing={{0}: (2, {}), {1}: (3, {})} | custom-call | flops 1811939328 | bytes 4718592 | tf_op jit(solution)/shard_map/extend_factors/pallas_call | solution.py:338
  168.4 1.8 hop.2
  170.2 0.7 collective-permute-start.29
  171.0 1.8 hop.3
  172.8 1.3 collective-permute-start.30
  174.1 1.1 own_rows.1.own_ref
  175.2 13.4 %collective-permute-done.30.refs_2_ = bf16[6,256,256]{2,1,0:T(8,128)(2,1)S(1)} collective-permute-done((bf16[6,256,256]{2,1,0:T(8,128)(2,1)S(1)}, bf16[6,256,256]{2,1,0:T(8,128)(2,1)S(1)}, u32[]{:S(2)}, u32[]{:S(2)}) %collective-permute-start.30) | collective-permute-done | bytes 786464 | tf_op jit(solution)/shard_map/ppermute | solution.py:577
  188.6 5.6 %finish.1 = f32[8,96,768]{2,1,0:T(8,128)} custom-call(bf16[8,768,768]{2,1,0:T(8,128)(2,1)S(1)} %get-tuple-element.119.factor_ref, f32[8,96,768]{2,1,0:T(8,128)S(1)} %own_rows.1.own_ref, bf16[8,96,768]{2,1,0:T(8,128)(2,1)S(1)} %get-tuple-element.122.mine_ref, bf16[6,256,256]{2,1,0:T(8,128)(2,1)S(1)} %collective-permute-done.28.refs_0_, ...), custom_call_target="tpu_custom_call" | custom-call | tf_op jit(solution)/shard_map/finish/pallas_call | solution.py:498
  (34 shorter events, 3.3 us)
Async XLA Ops:
  0.0 47.7 %copy-start.2 = (bf16[8,96,768]{2,1,0:T(8,128)(2,1)S(1)}, bf16[8,96,768]{2,1,0:T(8,128)(2,1)}, u32[]{:S(2)}) copy-start(bf16[8,96,768]{2,1,0:T(8,128)(2,1)} %gain_ref.3) | copy-start | bytes 3538948
  0.0 47.7 %copy-start.1 = (f32[8,96,768]{2,1,0:T(8,128)S(1)}, f32[8,96,768]{2,1,0:T(8,128)}, u32[]{:S(2)}) copy-start(f32[8,96,768]{2,1,0:T(8,128)} %increment_ref.3) | copy-start | bytes 7077892
  3.6 107.4 %copy-start = (bf16[96,2944]{1,0:T(8,128)(2,1)S(1)}, bf16[96,2944]{1,0:T(8,128)(2,1)}, u32[]{:S(2)}) copy-start(bf16[96,2944]{1,0:T(8,128)(2,1)} %get-tuple-element.99.refs_0_.refs_8_.refs_16_.refs_24_.refs_32_.refs_40_) | copy-start | bytes 1695748
  3.6 16.1 %collective-permute-start = (bf16[96,2944]{1,0:T(8,128)(2,1)}, bf16[96,2944]{1,0:T(8,128)(2,1)S(1)}, u32[]{:S(2)}, u32[]{:S(2)}) collective-permute-start(bf16[96,2944]{1,0:T(8,128)(2,1)} %get-tuple-element.99.refs_0_.refs_8_.refs_16_.refs_24_.refs_32_.refs_40_), channel_id=1, source_target_pairs={{1,3},{3,5},{5,7},{7,6},{6,4},{4,2},{2,0},{0,1},{9,11},{11,13},{13... | collective-permute-start | bytes 1695752 | tf_op jit(solution)/shard_map/ppermute | solution.py:538
  6.5 14.8 %collective-permute-start.8 = (bf16[96,2944]{1,0:T(8,128)(2,1)}, bf16[96,2944]{1,0:T(8,128)(2,1)S(1)}, u32[]{:S(2)}, u32[]{:S(2)}) collective-permute-start(bf16[96,2944]{1,0:T(8,128)(2,1)} %get-tuple-element.99.refs_0_.refs_8_.refs_16_.refs_24_.refs_32_.refs_40_), channel_id=1, source_target_pairs={{1,0},{3,1},{5,3},{7,5},{6,7},{4,6},{2,4},{0,2},{9,8},{11,9},{13,1... | collective-permute-start | bytes 1695752 | tf_op jit(solution)/shard_map/ppermute | solution.py:538
  19.7 15.9 %collective-permute-start.1 = (bf16[96,2944]{1,0:T(8,128)(2,1)S(1)}, bf16[96,2944]{1,0:T(8,128)(2,1)S(1)}, u32[]{:S(2)}, u32[]{:S(2)}) collective-permute-start(bf16[96,2944]{1,0:T(8,128)(2,1)S(1)} %collective-permute-done.refs_1_.refs_9_.refs_17_.refs_25_.refs_33_.refs_41_), channel_id=1, source_target_pairs={{1,3},{3,5},{5,7},{7,6},{6,4},{4,2},{2,0},{0,1},{9,11},{11,13},{13... | collective-permute-start | bytes 1695752 | tf_op jit(solution)/shard_map/ppermute | solution.py:538
  21.3 13.8 %collective-permute-start.9 = (bf16[96,2432]{1,0:T(8,128)(2,1)}, bf16[96,2432]{1,0:T(8,128)(2,1)S(1)}, u32[]{:S(2)}, u32[]{:S(2)}) collective-permute-start(bf16[96,2432]{1,0:T(8,128)(2,1)} %get-tuple-element.89.refs_0_.refs_8_), channel_id=1, source_target_pairs={{1,0},{3,1},{5,3},{7,5},{6,7},{4,6},{2,4},{0,2},{9,8},{11,9},{13,1... | collective-permute-start | bytes 1400840 | tf_op jit(solution)/shard_map/ppermute | solution.py:538
  21.7 25.5 %collective-permute-start.26 = (bf16[96,2944]{1,0:T(8,128)(2,1)S(1)}, bf16[96,2944]{1,0:T(8,128)(2,1)S(1)}, u32[]{:S(2)}, u32[]{:S(2)}) collective-permute-start(bf16[96,2944]{1,0:T(8,128)(2,1)S(1)} %collective-permute-done.8.refs_5_.refs_13_.refs_21_.refs_29_.refs_37_.refs_45_), channel_id=1, source_target_pairs={{1,0},{3,1},{5,3},{7,5},{6,7},{4,6},{2,4},{0,2},{9,8},{11,9},{13,1... | collective-permute-start | bytes 1695752 | tf_op jit(solution)/shard_map/ppermute | solution.py:538
  35.1 22.1 %collective-permute-start.10 = (bf16[96,2432]{1,0:T(8,128)(2,1)S(1)}, bf16[96,2432]{1,0:T(8,128)(2,1)S(1)}, u32[]{:S(2)}, u32[]{:S(2)}) collective-permute-start(bf16[96,2432]{1,0:T(8,128)(2,1)S(1)} %collective-permute-done.9.refs_4_.refs_12_), channel_id=1, source_target_pairs={{1,0},{3,1},{5,3},{7,5},{6,7},{4,6},{2,4},{0,2},{9,8},{11,9},{13,1... | collective-permute-start | bytes 1400840 | tf_op jit(solution)/shard_map/ppermute | solution.py:538
  35.5 22.1 %collective-permute-start.2 = (bf16[96,2432]{1,0:T(8,128)(2,1)}, bf16[96,2432]{1,0:T(8,128)(2,1)S(1)}, u32[]{:S(2)}, u32[]{:S(2)}) collective-permute-start(bf16[96,2432]{1,0:T(8,128)(2,1)} %get-tuple-element.89.refs_0_.refs_8_), channel_id=1, source_target_pairs={{1,3},{3,5},{5,7},{7,6},{6,4},{4,2},{2,0},{0,1},{9,11},{11,13},{13... | collective-permute-start | bytes 1400840 | tf_op jit(solution)/shard_map/ppermute | solution.py:538
  37.2 22.5 %collective-permute-start.24 = (bf16[96,2944]{1,0:T(8,128)(2,1)S(1)}, bf16[96,2944]{1,0:T(8,128)(2,1)S(1)}, u32[]{:S(2)}, u32[]{:S(2)}) collective-permute-start(bf16[96,2944]{1,0:T(8,128)(2,1)S(1)} %collective-permute-done.1.refs_2_.refs_10_.refs_18_.refs_26_.refs_34_.refs_42_), channel_id=1, source_target_pairs={{1,3},{3,5},{5,7},{7,6},{6,4},{4,2},{2,0},{0,1},{9,11},{11,13},{13... | collective-permute-start | bytes 1695752 | tf_op jit(solution)/shard_map/ppermute | solution.py:538
  47.2 33.7 %collective-permute-start.27 = (bf16[96,2944]{1,0:T(8,128)(2,1)S(1)}, bf16[96,2944]{1,0:T(8,128)(2,1)S(1)}, u32[]{:S(2)}, u32[]{:S(2)}) collective-permute-start(bf16[96,2944]{1,0:T(8,128)(2,1)S(1)} %collective-permute-done.26.refs_6_.refs_14_.refs_22_.refs_30_.refs_38_.refs_46_), channel_id=1, source_target_pairs={{1,0},{3,1},{5,3},{7,5},{6,7},{4,6},{2,4},{0,2},{9,8},{11,9},{13,1... | collective-permute-start | bytes 1695752 | tf_op jit(solution)/shard_map/ppermute | solution.py:538
  57.2 22.1 %collective-permute-start.11 = (bf16[96,2432]{1,0:T(8,128)(2,1)S(1)}, bf16[96,2432]{1,0:T(8,128)(2,1)S(1)}, u32[]{:S(2)}, u32[]{:S(2)}) collective-permute-start(bf16[96,2432]{1,0:T(8,128)(2,1)S(1)} %get-tuple-element.79.refs_0_.refs_8_), channel_id=1, source_target_pairs={{1,0},{3,1},{5,3},{7,5},{6,7},{4,6},{2,4},{0,2},{9,8},{11,9},{13,1... | collective-permute-start | bytes 1400840 | tf_op jit(solution)/shard_map/ppermute | solution.py:538
  57.7 23.7 %collective-permute-start.3 = (bf16[96,2432]{1,0:T(8,128)(2,1)S(1)}, bf16[96,2432]{1,0:T(8,128)(2,1)S(1)}, u32[]{:S(2)}, u32[]{:S(2)}) collective-permute-start(bf16[96,2432]{1,0:T(8,128)(2,1)S(1)} %get-tuple-element.79.refs_0_.refs_8_), channel_id=1, source_target_pairs={{1,3},{3,5},{5,7},{7,6},{6,4},{4,2},{2,0},{0,1},{9,11},{11,13},{13... | collective-permute-start | bytes 1400840 | tf_op jit(solution)/shard_map/ppermute | solution.py:538
  59.3 30.1 %collective-permute-start.22 = (bf16[96,2432]{1,0:T(8,128)(2,1)S(1)}, bf16[96,2432]{1,0:T(8,128)(2,1)S(1)}, u32[]{:S(2)}, u32[]{:S(2)}) collective-permute-start(bf16[96,2432]{1,0:T(8,128)(2,1)S(1)} %collective-permute-done.10.refs_5_.refs_13_), channel_id=1, source_target_pairs={{1,0},{3,1},{5,3},{7,5},{6,7},{4,6},{2,4},{0,2},{9,8},{11,9},{13,1... | collective-permute-start | bytes 1400840 | tf_op jit(solution)/shard_map/ppermute | solution.py:538
  59.7 33.7 %collective-permute-start.25 = (bf16[96,2944]{1,0:T(8,128)(2,1)S(1)}, bf16[96,2944]{1,0:T(8,128)(2,1)S(1)}, u32[]{:S(2)}, u32[]{:S(2)}) collective-permute-start(bf16[96,2944]{1,0:T(8,128)(2,1)S(1)} %collective-permute-done.24.refs_3_.refs_11_.refs_19_.refs_27_.refs_35_.refs_43_), channel_id=1, source_target_pairs={{1,3},{3,5},{5,7},{7,6},{6,4},{4,2},{2,0},{0,1},{9,11},{11,13},{13... | collective-permute-start | bytes 1695752 | tf_op jit(solution)/shard_map/ppermute | solution.py:538
  79.4 13.6 %collective-permute-start.20 = (bf16[96,2432]{1,0:T(8,128)(2,1)S(1)}, bf16[96,2432]{1,0:T(8,128)(2,1)S(1)}, u32[]{:S(2)}, u32[]{:S(2)}) collective-permute-start(bf16[96,2432]{1,0:T(8,128)(2,1)S(1)} %collective-permute-done.2.refs_1_.refs_9_), channel_id=1, source_target_pairs={{1,3},{3,5},{5,7},{7,6},{6,4},{4,2},{2,0},{0,1},{9,11},{11,13},{13... | collective-permute-start | bytes 1400840 | tf_op jit(solution)/shard_map/ppermute | solution.py:538
  80.9 52.1 %copy-start.3 = (bf16[96,2432]{1,0:T(8,128)(2,1)S(1)}, bf16[96,2432]{1,0:T(8,128)(2,1)}, u32[]{:S(2)}) copy-start(bf16[96,2432]{1,0:T(8,128)(2,1)} %get-tuple-element.89.refs_0_.refs_8_) | copy-start | bytes 1400836
  80.9 18.4 %collective-permute-start.12 = (bf16[96,2432]{1,0:T(8,128)(2,1)S(1)}, bf16[96,2432]{1,0:T(8,128)(2,1)S(1)}, u32[]{:S(2)}, u32[]{:S(2)}) collective-permute-start(bf16[96,2432]{1,0:T(8,128)(2,1)S(1)} %get-tuple-element.75.refs_0_), channel_id=1, source_target_pairs={{1,0},{3,1},{5,3},{7,5},{6,7},{4,6},{2,4},{0,2},{9,8},{11,9},{13,1... | collective-permute-start | bytes 1400840 | tf_op jit(solution)/shard_map/ppermute | solution.py:538
  81.4 21.6 %collective-permute-start.4 = (bf16[96,2432]{1,0:T(8,128)(2,1)S(1)}, bf16[96,2432]{1,0:T(8,128)(2,1)S(1)}, u32[]{:S(2)}, u32[]{:S(2)}) collective-permute-start(bf16[96,2432]{1,0:T(8,128)(2,1)S(1)} %collective-permute-done.3.refs_1_.refs_9_), channel_id=1, source_target_pairs={{1,3},{3,5},{5,7},{7,6},{6,4},{4,2},{2,0},{0,1},{9,11},{11,13},{13... | collective-permute-start | bytes 1400840 | tf_op jit(solution)/shard_map/ppermute | solution.py:538
  89.4 20.0 %collective-permute-start.18 = (bf16[96,2432]{1,0:T(8,128)(2,1)S(1)}, bf16[96,2432]{1,0:T(8,128)(2,1)S(1)}, u32[]{:S(2)}, u32[]{:S(2)}) collective-permute-start(bf16[96,2432]{1,0:T(8,128)(2,1)S(1)} %collective-permute-done.11.refs_5_.refs_13_), channel_id=1, source_target_pairs={{1,0},{3,1},{5,3},{7,5},{6,7},{4,6},{2,4},{0,2},{9,8},{11,9},{13,1... | collective-permute-start | bytes 1400840 | tf_op jit(solution)/shard_map/ppermute | solution.py:538
  93.0 27.3 %collective-permute-start.23 = (bf16[96,2432]{1,0:T(8,128)(2,1)S(1)}, bf16[96,2432]{1,0:T(8,128)(2,1)S(1)}, u32[]{:S(2)}, u32[]{:S(2)}) collective-permute-start(bf16[96,2432]{1,0:T(8,128)(2,1)S(1)} %collective-permute-done.22.refs_6_.refs_14_), channel_id=1, source_target_pairs={{1,0},{3,1},{5,3},{7,5},{6,7},{4,6},{2,4},{0,2},{9,8},{11,9},{13,1... | collective-permute-start | bytes 1400840 | tf_op jit(solution)/shard_map/ppermute | solution.py:538
  93.4 27.4 %collective-permute-start.21 = (bf16[96,2432]{1,0:T(8,128)(2,1)S(1)}, bf16[96,2432]{1,0:T(8,128)(2,1)S(1)}, u32[]{:S(2)}, u32[]{:S(2)}) collective-permute-start(bf16[96,2432]{1,0:T(8,128)(2,1)S(1)} %collective-permute-done.20.refs_2_.refs_10_), channel_id=1, source_target_pairs={{1,3},{3,5},{5,7},{7,6},{6,4},{4,2},{2,0},{0,1},{9,11},{11,13},{13... | collective-permute-start | bytes 1400840 | tf_op jit(solution)/shard_map/ppermute | solution.py:538
  99.4 30.0 %collective-permute-start.13 = (bf16[96,2432]{1,0:T(8,128)(2,1)S(1)}, bf16[96,2432]{1,0:T(8,128)(2,1)S(1)}, u32[]{:S(2)}, u32[]{:S(2)}) collective-permute-start(bf16[96,2432]{1,0:T(8,128)(2,1)S(1)} %collective-permute-done.12.refs_4_), channel_id=1, source_target_pairs={{1,0},{3,1},{5,3},{7,5},{6,7},{4,6},{2,4},{0,2},{9,8},{11,9},{13,1... | collective-permute-start | bytes 1400840 | tf_op jit(solution)/shard_map/ppermute | solution.py:538
  103.0 26.8 %collective-permute-start.16 = (bf16[96,2432]{1,0:T(8,128)(2,1)S(1)}, bf16[96,2432]{1,0:T(8,128)(2,1)S(1)}, u32[]{:S(2)}, u32[]{:S(2)}) collective-permute-start(bf16[96,2432]{1,0:T(8,128)(2,1)S(1)} %collective-permute-done.4.refs_2_.refs_10_), channel_id=1, source_target_pairs={{1,3},{3,5},{5,7},{7,6},{6,4},{4,2},{2,0},{0,1},{9,11},{11,13},{13... | collective-permute-start | bytes 1400840 | tf_op jit(solution)/shard_map/ppermute | solution.py:538
  109.4 22.0 %collective-permute-start.5 = (bf16[96,2432]{1,0:T(8,128)(2,1)S(1)}, bf16[96,2432]{1,0:T(8,128)(2,1)S(1)}, u32[]{:S(2)}, u32[]{:S(2)}) collective-permute-start(bf16[96,2432]{1,0:T(8,128)(2,1)S(1)} %get-tuple-element.75.refs_0_), channel_id=1, source_target_pairs={{1,3},{3,5},{5,7},{7,6},{6,4},{4,2},{2,0},{0,1},{9,11},{11,13},{13... | collective-permute-start | bytes 1400840 | tf_op jit(solution)/shard_map/ppermute | solution.py:538
  120.3 27.5 %collective-permute-start.19 = (bf16[96,2432]{1,0:T(8,128)(2,1)S(1)}, bf16[96,2432]{1,0:T(8,128)(2,1)S(1)}, u32[]{:S(2)}, u32[]{:S(2)}) collective-permute-start(bf16[96,2432]{1,0:T(8,128)(2,1)S(1)} %collective-permute-done.18.refs_6_.refs_14_), channel_id=1, source_target_pairs={{1,0},{3,1},{5,3},{7,5},{6,7},{4,6},{2,4},{0,2},{9,8},{11,9},{13,1... | collective-permute-start | bytes 1400840 | tf_op jit(solution)/shard_map/ppermute | solution.py:538
  129.4 17.7 %collective-permute-start.14 = (bf16[96,2432]{1,0:T(8,128)(2,1)S(1)}, bf16[96,2432]{1,0:T(8,128)(2,1)S(1)}, u32[]{:S(2)}, u32[]{:S(2)}) collective-permute-start(bf16[96,2432]{1,0:T(8,128)(2,1)S(1)} %collective-permute-done.13.refs_5_), channel_id=1, source_target_pairs={{1,0},{3,1},{5,3},{7,5},{6,7},{4,6},{2,4},{0,2},{9,8},{11,9},{13,1... | collective-permute-start | bytes 1400840 | tf_op jit(solution)/shard_map/ppermute | solution.py:538
  129.8 18.0 %collective-permute-start.17 = (bf16[96,2432]{1,0:T(8,128)(2,1)S(1)}, bf16[96,2432]{1,0:T(8,128)(2,1)S(1)}, u32[]{:S(2)}, u32[]{:S(2)}) collective-permute-start(bf16[96,2432]{1,0:T(8,128)(2,1)S(1)} %collective-permute-done.16.refs_3_.refs_11_), channel_id=1, source_target_pairs={{1,3},{3,5},{5,7},{7,6},{6,4},{4,2},{2,0},{0,1},{9,11},{11,13},{13... | collective-permute-start | bytes 1400840 | tf_op jit(solution)/shard_map/ppermute | solution.py:538
  131.4 18.5 %collective-permute-start.6 = (bf16[96,2432]{1,0:T(8,128)(2,1)S(1)}, bf16[96,2432]{1,0:T(8,128)(2,1)S(1)}, u32[]{:S(2)}, u32[]{:S(2)}) collective-permute-start(bf16[96,2432]{1,0:T(8,128)(2,1)S(1)} %collective-permute-done.5.refs_1_), channel_id=1, source_target_pairs={{1,3},{3,5},{5,7},{7,6},{6,4},{4,2},{2,0},{0,1},{9,11},{11,13},{13... | collective-permute-start | bytes 1400840 | tf_op jit(solution)/shard_map/ppermute | solution.py:538
  147.1 12.7 %collective-permute-start.15 = (bf16[96,2432]{1,0:T(8,128)(2,1)S(1)}, bf16[96,2432]{1,0:T(8,128)(2,1)S(1)}, u32[]{:S(2)}, u32[]{:S(2)}) collective-permute-start(bf16[96,2432]{1,0:T(8,128)(2,1)S(1)} %collective-permute-done.14.refs_6_), channel_id=1, source_target_pairs={{1,0},{3,1},{5,3},{7,5},{6,7},{4,6},{2,4},{0,2},{9,8},{11,9},{13,1... | collective-permute-start | bytes 1400840 | tf_op jit(solution)/shard_map/ppermute | solution.py:538
  149.9 9.9 %collective-permute-start.7 = (bf16[96,2432]{1,0:T(8,128)(2,1)S(1)}, bf16[96,2432]{1,0:T(8,128)(2,1)S(1)}, u32[]{:S(2)}, u32[]{:S(2)}) collective-permute-start(bf16[96,2432]{1,0:T(8,128)(2,1)S(1)} %collective-permute-done.6.refs_2_), channel_id=1, source_target_pairs={{1,3},{3,5},{5,7},{7,6},{6,4},{4,2},{2,0},{0,1},{9,11},{11,13},{13... | collective-permute-start | bytes 1400840 | tf_op jit(solution)/shard_map/ppermute | solution.py:538
  165.1 3.3 %collective-permute-start.28 = (bf16[6,256,256]{2,1,0:T(8,128)(2,1)S(1)}, bf16[6,256,256]{2,1,0:T(8,128)(2,1)S(1)}, u32[]{:S(2)}, u32[]{:S(2)}) collective-permute-start(bf16[6,256,256]{2,1,0:T(8,128)(2,1)S(1)} %fold.1), channel_id=1, source_target_pairs={{24,16},{25,17},{26,18},{27,19},{28,20},{29,21},{30,22},{31,23}} | collective-permute-start | bytes 2359304 | tf_op jit(solution)/shard_map/ppermute | solution.py:577
  170.2 0.7 collective-permute-start.29
  172.8 15.8 %collective-permute-start.30 = (bf16[6,256,256]{2,1,0:T(8,128)(2,1)S(1)}, bf16[6,256,256]{2,1,0:T(8,128)(2,1)S(1)}, u32[]{:S(2)}, u32[]{:S(2)}) collective-permute-start(bf16[6,256,256]{2,1,0:T(8,128)(2,1)S(1)} %hop.3), channel_id=1, source_target_pairs={{8,0},{9,1},{10,2},{11,3},{12,4},{13,5},{14,6},{15,7}} | collective-permute-start | bytes 2359304 | tf_op jit(solution)/shard_map/ppermute | solution.py:577

commit v13 on v12

--- a/solution.py
+++ b/solution.py
@@ -45,7 +45,7 @@
     return pltpu.roll(wide, block * rows, 1) if block else wide
 
 
-def pack_kernel(count, ranges, place_ref, gain_ref, increment_ref, *refs):
+def pack_kernel(count, ranges, place_ref, block_ref, gain_ref, increment_ref, *refs):
     outs = refs[-len(ranges):]
     rows, width = gain_ref.shape[1:]
     stride = width + width // 2
@@ -66,29 +66,52 @@
     if len(refs) > len(ranges):
         main, extra = packed_half(refs[0][...], place, count)
         at = (ranges[0][1] - ranges[0][0]) * stride + LANES
-        outs[0][:, at:at + width // 2] = main
-        outs[0][:, at + width // 2:] = extra.astype(BF16)
-
-
-def pack(place, gains, increments, terminal, count, ranges):
+        tiles = [main[:, n:n + LANES].astype(F32) for n in range(0, width // 2, LANES)] + [extra]
+        outs[0][:, at:] = sum(jnp.where(block_ref[0] == n, tile, 0.0) for n, tile in enumerate(tiles)).astype(BF16)
+
+
+def pack(place, block, gains, increments, terminal, count, ranges):
     rows, width = gains.shape[1:]
     first, size = ranges[1][0], ranges[0][1] - ranges[1][0]
     ends = [] if terminal is None else [terminal]
     lanes = [(high - low) * (width + width // 2) + LANES for low, high in ranges]
-    lanes[0] += (width // 2 + LANES) * len(ends)
-    some = pl.BlockSpec((size, rows, width), lambda i, p: (first // size, 0, 0))
+    lanes[0] += LANES * len(ends)
+    some = pl.BlockSpec((size, rows, width), lambda i, *p: (first // size, 0, 0))
     return pl.pallas_call(
         functools.partial(pack_kernel, count, ranges),
+        grid_spec=pltpu.PrefetchScalarGridSpec(
+            num_scalar_prefetch=2,
+            grid=(1,),
+            in_specs=[some, some] + [pl.BlockSpec((rows, width), lambda i, *p: (0, 0))] * len(ends),
+            out_specs=[pl.BlockSpec((rows, n), lambda i, *p: (0, 0)) for n in lanes],
+        ),
+        out_shape=[jax.ShapeDtypeStruct((rows, n), BF16) for n in lanes],
+        compiler_params=pltpu.CompilerParams(vmem_limit_bytes=CLAIM if ends else 14 * MIB),
+        name="pack",
+    )(place, block, gains, increments, *ends)
+
+
+def collect_kernel(cycle, right, place_ref, *refs):
+    out_ref = refs[-1]
+    for place, tile in zip(origins(place_ref[0], cycle, right), refs):
+        out_ref[place] = tile[...]
+
+
+def collect(place, cycle, right, blocks):
+    rows, lanes = blocks[0].shape
+    tile = pl.BlockSpec((rows, LANES), lambda i, *p: (0, lanes // LANES - 1), pipeline_mode=pl.Buffered(1))
+    return pl.pallas_call(
+        functools.partial(collect_kernel, cycle, right),
         grid_spec=pltpu.PrefetchScalarGridSpec(
             num_scalar_prefetch=1,
             grid=(1,),
-            in_specs=[some, some] + [pl.BlockSpec((rows, width), lambda i, p: (0, 0))] * len(ends),
-            out_specs=[pl.BlockSpec((rows, n), lambda i, p: (0, 0)) for n in lanes],
-        ),
-        out_shape=[jax.ShapeDtypeStruct((rows, n), BF16) for n in lanes],
-        compiler_params=pltpu.CompilerParams(vmem_limit_bytes=CLAIM if ends else 14 * MIB),
-        name="pack",
-    )(place, gains, increments, *ends)
+            in_specs=[tile] * len(blocks),
+            out_specs=pl.BlockSpec((len(blocks), rows, LANES), lambda i, *p: (0, 0, 0)),
+        ),
+        out_shape=jax.ShapeDtypeStruct((len(blocks), rows, LANES), BF16),
+        compiler_params=pltpu.CompilerParams(vmem_limit_bytes=6 * MIB),
+        name="collect",
+    )(place, *blocks)
 
 
 def unpack(raw, extras, step, half):
@@ -148,9 +171,9 @@
     count = len(cycle)
     places = origins(place_ref[0], cycle, right)
     blocks, sides, refs = refs[:count], refs[count:2 * count], refs[2 * count:]
-    tiles = blocks[0].shape[1] // 3 // LANES
     if first:
-        ends, refs = refs[:(tiles + 1) * count], refs[(tiles + 1) * count:]
+        tiles = blocks[0].shape[1] // 3 // LANES + 1
+        ends, refs = refs[:tiles], refs[tiles:]
     else:
         half_in, factor_in, refs = refs[0], refs[1], refs[4:]
     factor_out, own_out, mine_out, half, gain, factor, fresh, middle, raw, extras = refs
@@ -160,11 +183,9 @@
     def _():
         if first:
             scale = jnp.where(last_ref[0] == 1, 1.0, 0.0).astype(BF16)
-            for n in range(count):
-                for tile in range(tiles):
-                    lanes = slice(tile * LANES, (tile + 1) * LANES)
-                    raw[places[n], :, lanes] = ends[tile * count + n][...] * scale
-                extras[places[n]] = ends[tiles * count + n][...] * scale
+            for n, end in enumerate(ends[:-1]):
+                raw[:, :, n * LANES:(n + 1) * LANES] = end[...] * scale
+            extras[...] = ends[-1][...] * scale
             unpack(raw, extras, 0, half)
         else:
             factor[...] = factor_in[0]
@@ -210,7 +231,7 @@
     ]
 
 
-def compose(last, place, cycle, right, blocks, state, half, low, turns, steps):
+def compose(last, place, cycle, right, blocks, ends, state, half, low, turns, steps):
     count = len(blocks)
     rows = blocks[0].shape[0]
     width = rows * count
@@ -218,12 +239,8 @@
     anywhere = pl.BlockSpec(memory_space=pl.ANY)
     in_specs = row_specs(blocks, turns)
     if first:
-        at = turns * width * 3 // 2 // LANES + 1
-        tiles = width // 2 // LANES + 1
-        for n in range(at, at + tiles):
-            tile = pl.BlockSpec((rows, LANES), lambda i, *p, n=n: (0, n), pipeline_mode=pl.Buffered(1))
-            in_specs += [tile] * count
-        args = list(blocks) * tiles
+        in_specs += [pl.BlockSpec(end.shape, lambda i, *p: (0, 0, 0), pipeline_mode=pl.Buffered(1)) for end in ends]
+        args = ends
     else:
         after = pl.BlockSpec((1, width, width), lambda i, *p: (low + turns, 0, 0), pipeline_mode=pl.Buffered(1))
         in_specs += [square(width), after, anywhere, anywhere]
@@ -531,15 +548,16 @@
     line = math.gcd(count, LINE)
     steps = gains.shape[0]
     place = lax.axis_index("tile").astype(jnp.int32).reshape(1)
-    last = (lax.axis_index("tm") == blocks - 1).astype(jnp.int32).reshape(1)
+    block = lax.axis_index("tm").astype(jnp.int32).reshape(1)
+    last = (block == blocks - 1).astype(jnp.int32)
     cycle = ring_order(line, count // line)
 
     def passed(array, way):
         return lax.ppermute(array, "tile", [(cycle[n], cycle[(n + way) % count]) for n in range(count)])
 
     ranges = pieces(steps)
-    own = list(pack(place, gains, increments, terminal, count, ranges[:2]))
-    own += pack(place, gains, increments, None, count, ranges[2:])
+    own = list(pack(place, block, gains, increments, terminal, count, ranges[:2]))
+    own += pack(place, block, gains, increments, None, count, ranges[2:])
     own[:2], last = lax.optimization_barrier((own[:2], last))
     rights = [count // 2 - turn % 2 for turn in range(len(own))]
     found = []
@@ -547,9 +565,9 @@
         found.append({})
         for way, hops in ((1, rights[turn]), (-1, count - 1 - rights[turn])):
             source = array
-            if turn:
+            if turn > 1:
                 before = found[turn - 1][way]
-                gate = len(before) - 3
+                gate = count // 2 - 1 if turn == 2 else len(before) - 3
                 source, before[gate] = lax.optimization_barrier((source, before[gate]))
                 for n in range(gate + 1, len(before)):
                     before[n] = passed(before[n - 1], way)
@@ -557,16 +575,21 @@
             for _ in range(hops):
                 found[turn][way].append(passed(found[turn][way][-1], way))
     ties = [
-        [found[1][1][2], found[2][1][1], found[1][-1][3], found[2][-1][1]],
+        [found[2][1][1], found[2][-1][1], found[1][-1][-1]],
         [found[2][1][2], found[2][-1][2], found[3][-1][1]],
         [found[3][1][-2], found[3][-1][-2]],
+    ]
+    tile = collect(place, cycle, rights[0], [own[0]] + found[0][1][1:] + found[0][-1][1:])
+    ends = [
+        lax.ppermute(tile, "tm", [(n, blocks - 1)]) if n < blocks - 1 else tile
+        for n in range(gains.shape[2] // 2 // LANES + 1)
     ]
     state, half = None, None
     for turn, (low, high) in enumerate(ranges):
         parts = [own[turn]] + found[turn][1][1:] + found[turn][-1][1:]
         if turn < len(ties):
             parts, _ = lax.optimization_barrier((parts, ties[turn]))
-            *state, half = compose(last, place, cycle, rights[turn], parts, state, half, low, high - low, steps)
+            *state, half = compose(last, place, cycle, rights[turn], parts, ends, state, half, low, high - low, steps)
         else:
             early = chain(place, cycle, rights[turn], parts, half, high)
     factors, own, mine = state

time: 194 us -> 189 us (0.974)
  waiting for transfers between devices: 111 us -> 97 us
  starting transfers between devices: 33.2 us -> 42.5 us
    ppermute x28, waiting for transfers between devices: 98.1 us -> 83.8 us  [passed(): lax.ppermute(array, 'tile', [(cycle[n], cycle[(n + way) % count]) for n i...]
    ppermute x28, starting transfers between devices: 30.3 us -> 36.8 us  [passed(): lax.ppermute(array, 'tile', [(cycle[n], cycle[(n + way) % count]) for n i...]
    ppermute x0 -> x3, starting transfers between devices: none -> 2.78 us  [local(): lax.ppermute(tile, 'tm', [(n, blocks - 1)])]
  transfers between devices with their start and end apart: 31 -> 34, of which waited for: 14 -> 18; matrix products, arithmetic and copies ran while one was open for 0% -> 0% of each run, Pallas kernels for 16% -> 16%
where the time goes in v13:
time: 189 us
  waiting for transfers between devices  97 us (51%)
  Pallas kernels  49 us (26%)
  starting transfers between devices  42.5 us (22%)
    ppermute x28, waiting for transfers between devices, passed(): lax.ppermute(array, 'tile', [(cycle[n], cycle[(n + way) % count]) for n i...  83.8 us
    ppermute x28, starting transfers between devices, passed(): lax.ppermute(array, 'tile', [(cycle[n], cycle[(n + way) % count]) for n i...  36.8 us
    pallas_call x3, Pallas kernels, compose(): pl.pallas_call(functools.partial(compose_kernel, cycle, right, first), gr...  26.7 us
    ppermute x3, waiting for transfers between devices, local(): lax.ppermute(hop(factors, early[1], packed), 'tm', [(turn, turn - 1)])  13.2 us
    pallas_call x1, Pallas kernels, finish(): pl.pallas_call(functools.partial(finish_kernel, len(packed)), grid=(steps...  5.6 us
    pallas_call x1, Pallas kernels, chain(): pl.pallas_call(functools.partial(chain_kernel, cycle, right, turns), grid...  5.03 us
    pallas_call x2, Pallas kernels, pack(): pl.pallas_call(functools.partial(pack_kernel, count, ranges), grid_spec=p...  4.25 us
  transfers between devices with their start and end apart: 34, of which 18 were waited for; matrix products, arithmetic and copies ran while one was open for 0% of the time, Pallas kernels for 16%

profile of v13, /device:TPU:0, one launch (start us, length us, event | category | flops | bytes accessed | tf_op | source)
XLA Modules:
  0.0 188.8 jit_solution(12518104489235499949)
XLA Ops:
  0.0 3.5 %pack.3 = (bf16[96,2560]{1,0:T(8,128)(2,1)}, bf16[96,2432]{1,0:T(8,128)(2,1)}) custom-call(s32[1]{0:T(128)} %bitcast.place_ref, s32[1]{0:T(128)} %bitcast.1.block_ref, bf16[8,96,768]{2,1,0:T(8,128)(2,1)} %gain_ref.3, f32[8,96,768]{2,1,0:T(8,128)} %increment_ref.3, f32[96,768]{1,0:T(8,128)} %refs_0_.1), custom_call_target="tpu_custom_call" | custom-call | tf_op jit(solution)/shard_map/pack/pallas_call | solution.py:80
  3.5 3.0 %collective-permute-start = (bf16[96,2432]{1,0:T(8,128)(2,1)}, bf16[96,2432]{1,0:T(8,128)(2,1)S(1)}, u32[]{:S(2)}, u32[]{:S(2)}) collective-permute-start(bf16[96,2432]{1,0:T(8,128)(2,1)} %get-tuple-element.82.refs_0_.refs_8_), channel_id=1, source_target_pairs={{1,3},{3,5},{5,7},{7,6},{6,4},{4,2},{2,0},{0,1},{9,11},{11,13},{13... | collective-permute-start | bytes 1400840 | tf_op jit(solution)/shard_map/ppermute | solution.py:556
  6.6 1.9 %collective-permute-start.21 = (bf16[96,2560]{1,0:T(8,128)(2,1)}, bf16[96,2560]{1,0:T(8,128)(2,1)S(1)}, u32[]{:S(2)}, u32[]{:S(2)}) collective-permute-start(bf16[96,2560]{1,0:T(8,128)(2,1)} %get-tuple-element.91.refs_0_.refs_8_), channel_id=1, source_target_pairs={{1,3},{3,5},{5,7},{7,6},{6,4},{4,2},{2,0},{0,1},{9,11},{11,13},{13... | collective-permute-start | bytes 1474568 | tf_op jit(solution)/shard_map/ppermute | solution.py:556
  8.5 9.8 %collective-permute-done.refs_1_.refs_9_ = bf16[96,2432]{1,0:T(8,128)(2,1)S(1)} collective-permute-done((bf16[96,2432]{1,0:T(8,128)(2,1)}, bf16[96,2432]{1,0:T(8,128)(2,1)S(1)}, u32[]{:S(2)}, u32[]{:S(2)}) %collective-permute-start) | collective-permute-done | bytes 466976 | tf_op jit(solution)/shard_map/ppermute | solution.py:556
  18.3 2.0 %collective-permute-start.1 = (bf16[96,2432]{1,0:T(8,128)(2,1)S(1)}, bf16[96,2432]{1,0:T(8,128)(2,1)S(1)}, u32[]{:S(2)}, u32[]{:S(2)}) collective-permute-start(bf16[96,2432]{1,0:T(8,128)(2,1)S(1)} %collective-permute-done.refs_1_.refs_9_), channel_id=1, source_target_pairs={{1,3},{3,5},{5,7},{7,6},{6,4},{4,2},{2,0},{0,1},{9,11},{11,13},{13... | collective-permute-start | bytes 1400840 | tf_op jit(solution)/shard_map/ppermute | solution.py:556
  20.4 2.0 %collective-permute-start.25 = (bf16[96,2560]{1,0:T(8,128)(2,1)}, bf16[96,2560]{1,0:T(8,128)(2,1)S(1)}, u32[]{:S(2)}, u32[]{:S(2)}) collective-permute-start(bf16[96,2560]{1,0:T(8,128)(2,1)} %get-tuple-element.91.refs_0_.refs_8_), channel_id=1, source_target_pairs={{1,0},{3,1},{5,3},{7,5},{6,7},{4,6},{2,4},{0,2},{9,8},{11,9},{13,1... | collective-permute-start | bytes 1474568 | tf_op jit(solution)/shard_map/ppermute | solution.py:556
  22.4 6.4 %collective-permute-done.21.refs_1_.refs_9_ = bf16[96,2560]{1,0:T(8,128)(2,1)S(1)} collective-permute-done((bf16[96,2560]{1,0:T(8,128)(2,1)}, bf16[96,2560]{1,0:T(8,128)(2,1)S(1)}, u32[]{:S(2)}, u32[]{:S(2)}) %collective-permute-start.21) | collective-permute-done | bytes 491552 | tf_op jit(solution)/shard_map/ppermute | solution.py:556
  28.8 2.0 %collective-permute-start.22 = (bf16[96,2560]{1,0:T(8,128)(2,1)S(1)}, bf16[96,2560]{1,0:T(8,128)(2,1)S(1)}, u32[]{:S(2)}, u32[]{:S(2)}) collective-permute-start(bf16[96,2560]{1,0:T(8,128)(2,1)S(1)} %collective-permute-done.21.refs_1_.refs_9_), channel_id=1, source_target_pairs={{1,3},{3,5},{5,7},{7,6},{6,4},{4,2},{2,0},{0,1},{9,11},{11,13},{13... | collective-permute-start | bytes 1474568 | tf_op jit(solution)/shard_map/ppermute | solution.py:556
  30.8 8.0 %collective-permute-done.1.refs_2_.refs_10_ = bf16[96,2432]{1,0:T(8,128)(2,1)S(1)} collective-permute-done((bf16[96,2432]{1,0:T(8,128)(2,1)S(1)}, bf16[96,2432]{1,0:T(8,128)(2,1)S(1)}, u32[]{:S(2)}, u32[]{:S(2)}) %collective-permute-start.1) | collective-permute-done | bytes 466976 | tf_op jit(solution)/shard_map/ppermute | solution.py:556
  38.8 2.0 %collective-permute-start.2 = (bf16[96,2432]{1,0:T(8,128)(2,1)S(1)}, bf16[96,2432]{1,0:T(8,128)(2,1)S(1)}, u32[]{:S(2)}, u32[]{:S(2)}) collective-permute-start(bf16[96,2432]{1,0:T(8,128)(2,1)S(1)} %collective-permute-done.1.refs_2_.refs_10_), channel_id=1, source_target_pairs={{1,3},{3,5},{5,7},{7,6},{6,4},{4,2},{2,0},{0,1},{9,11},{11,13},{13... | collective-permute-start | bytes 1400840 | tf_op jit(solution)/shard_map/ppermute | solution.py:556
  41.0 2.0 %collective-permute-start.26 = (bf16[96,2560]{1,0:T(8,128)(2,1)S(1)}, bf16[96,2560]{1,0:T(8,128)(2,1)S(1)}, u32[]{:S(2)}, u32[]{:S(2)}) collective-permute-start(bf16[96,2560]{1,0:T(8,128)(2,1)S(1)} %collective-permute-done.25.refs_5_.refs_13_), channel_id=1, source_target_pairs={{1,0},{3,1},{5,3},{7,5},{6,7},{4,6},{2,4},{0,2},{9,8},{11,9},{13,1... | collective-permute-start | bytes 1474568 | tf_op jit(solution)/shard_map/ppermute | solution.py:556
  42.9 6.4 %collective-permute-done.22.refs_2_.refs_10_ = bf16[96,2560]{1,0:T(8,128)(2,1)S(1)} collective-permute-done((bf16[96,2560]{1,0:T(8,128)(2,1)S(1)}, bf16[96,2560]{1,0:T(8,128)(2,1)S(1)}, u32[]{:S(2)}, u32[]{:S(2)}) %collective-permute-start.22) | collective-permute-done | bytes 491552 | tf_op jit(solution)/shard_map/ppermute | solution.py:556
  49.4 2.0 %collective-permute-start.23 = (bf16[96,2560]{1,0:T(8,128)(2,1)S(1)}, bf16[96,2560]{1,0:T(8,128)(2,1)S(1)}, u32[]{:S(2)}, u32[]{:S(2)}) collective-permute-start(bf16[96,2560]{1,0:T(8,128)(2,1)S(1)} %collective-permute-done.22.refs_2_.refs_10_), channel_id=1, source_target_pairs={{1,3},{3,5},{5,7},{7,6},{6,4},{4,2},{2,0},{0,1},{9,11},{11,13},{13... | collective-permute-start | bytes 1474568 | tf_op jit(solution)/shard_map/ppermute | solution.py:556
  51.4 0.7 pack.2
  52.1 7.3 %collective-permute-done.2.refs_3_.refs_11_ = bf16[96,2432]{1,0:T(8,128)(2,1)S(1)} collective-permute-done((bf16[96,2432]{1,0:T(8,128)(2,1)S(1)}, bf16[96,2432]{1,0:T(8,128)(2,1)S(1)}, u32[]{:S(2)}, u32[]{:S(2)}) %collective-permute-start.2) | collective-permute-done | bytes 466976 | tf_op jit(solution)/shard_map/ppermute | solution.py:556
  59.4 2.0 %collective-permute-start.3 = (bf16[96,2432]{1,0:T(8,128)(2,1)S(1)}, bf16[96,2432]{1,0:T(8,128)(2,1)S(1)}, u32[]{:S(2)}, u32[]{:S(2)}) collective-permute-start(bf16[96,2432]{1,0:T(8,128)(2,1)S(1)} %get-tuple-element.72.refs_0_.refs_8_), channel_id=1, source_target_pairs={{1,3},{3,5},{5,7},{7,6},{6,4},{4,2},{2,0},{0,1},{9,11},{11,13},{13... | collective-permute-start | bytes 1400840 | tf_op jit(solution)/shard_map/ppermute | solution.py:556
  61.5 2.0 %collective-permute-start.27 = (bf16[96,2560]{1,0:T(8,128)(2,1)S(1)}, bf16[96,2560]{1,0:T(8,128)(2,1)S(1)}, u32[]{:S(2)}, u32[]{:S(2)}) collective-permute-start(bf16[96,2560]{1,0:T(8,128)(2,1)S(1)} %collective-permute-done.26.refs_6_.refs_14_), channel_id=1, source_target_pairs={{1,0},{3,1},{5,3},{7,5},{6,7},{4,6},{2,4},{0,2},{9,8},{11,9},{13,1... | collective-permute-start | bytes 1474568 | tf_op jit(solution)/shard_map/ppermute | solution.py:556
  63.5 6.4 %collective-permute-done.23.refs_3_.refs_11_ = bf16[96,2560]{1,0:T(8,128)(2,1)S(1)} collective-permute-done((bf16[96,2560]{1,0:T(8,128)(2,1)S(1)}, bf16[96,2560]{1,0:T(8,128)(2,1)S(1)}, u32[]{:S(2)}, u32[]{:S(2)}) %collective-permute-start.23) | collective-permute-done | bytes 491552 | tf_op jit(solution)/shard_map/ppermute | solution.py:556
  69.9 2.0 %collective-permute-start.24 = (bf16[96,2560]{1,0:T(8,128)(2,1)S(1)}, bf16[96,2560]{1,0:T(8,128)(2,1)S(1)}, u32[]{:S(2)}, u32[]{:S(2)}) collective-permute-start(bf16[96,2560]{1,0:T(8,128)(2,1)S(1)} %collective-permute-done.23.refs_3_.refs_11_), channel_id=1, source_target_pairs={{1,3},{3,5},{5,7},{7,6},{6,4},{4,2},{2,0},{0,1},{9,11},{11,13},{13... | collective-permute-start | bytes 1474568 | tf_op jit(solution)/shard_map/ppermute | solution.py:556
  72.0 7.9 %collective-permute-done.3.refs_1_.refs_9_ = bf16[96,2432]{1,0:T(8,128)(2,1)S(1)} collective-permute-done((bf16[96,2432]{1,0:T(8,128)(2,1)S(1)}, bf16[96,2432]{1,0:T(8,128)(2,1)S(1)}, u32[]{:S(2)}, u32[]{:S(2)}) %collective-permute-start.3) | collective-permute-done | bytes 466976 | tf_op jit(solution)/shard_map/ppermute | solution.py:556
  79.9 2.0 %collective-permute-start.4 = (bf16[96,2432]{1,0:T(8,128)(2,1)S(1)}, bf16[96,2432]{1,0:T(8,128)(2,1)S(1)}, u32[]{:S(2)}, u32[]{:S(2)}) collective-permute-start(bf16[96,2432]{1,0:T(8,128)(2,1)S(1)} %collective-permute-done.3.refs_1_.refs_9_), channel_id=1, source_target_pairs={{1,3},{3,5},{5,7},{7,6},{6,4},{4,2},{2,0},{0,1},{9,11},{11,13},{13... | collective-permute-start | bytes 1400840 | tf_op jit(solution)/shard_map/ppermute | solution.py:556
  82.0 3.6 %collective-permute-done.27.refs_7_.refs_15_ = bf16[96,2560]{1,0:T(8,128)(2,1)S(1)} collective-permute-done((bf16[96,2560]{1,0:T(8,128)(2,1)S(1)}, bf16[96,2560]{1,0:T(8,128)(2,1)S(1)}, u32[]{:S(2)}, u32[]{:S(2)}) %collective-permute-start.27) | collective-permute-done | bytes 491552 | tf_op jit(solution)/shard_map/ppermute | solution.py:556
  85.5 4.9 %collective-permute-done.24.refs_4_.refs_12_ = bf16[96,2560]{1,0:T(8,128)(2,1)S(1)} collective-permute-done((bf16[96,2560]{1,0:T(8,128)(2,1)S(1)}, bf16[96,2560]{1,0:T(8,128)(2,1)S(1)}, u32[]{:S(2)}, u32[]{:S(2)}) %collective-permute-start.24) | collective-permute-done | bytes 491552 | tf_op jit(solution)/shard_map/ppermute | solution.py:556
  90.6 1.4 collective-permute-start.28
  92.7 2.8 %collective-permute-done.20.refs_7_.refs_15_ = bf16[96,2432]{1,0:T(8,128)(2,1)S(1)} collective-permute-done((bf16[96,2432]{1,0:T(8,128)(2,1)S(1)}, bf16[96,2432]{1,0:T(8,128)(2,1)S(1)}, u32[]{:S(2)}, u32[]{:S(2)}) %collective-permute-start.20) | collective-permute-done | bytes 466976 | tf_op jit(solution)/shard_map/ppermute | solution.py:556
  96.2 3.4 %collective-permute-done.4.refs_2_.refs_10_ = bf16[96,2432]{1,0:T(8,128)(2,1)S(1)} collective-permute-done((bf16[96,2432]{1,0:T(8,128)(2,1)S(1)}, bf16[96,2432]{1,0:T(8,128)(2,1)S(1)}, u32[]{:S(2)}, u32[]{:S(2)}) %collective-permute-start.4) | collective-permute-done | bytes 466976 | tf_op jit(solution)/shard_map/ppermute | solution.py:556
  99.6 1.7 collective-permute-start.18
  101.7 1.7 collective-permute-start.5
  103.7 8.9 %compose.3 = (bf16[8,768,768]{2,1,0:T(8,128)(2,1)S(1)}, f32[8,96,768]{2,1,0:T(8,128)S(1)}, bf16[8,96,768]{2,1,0:T(8,128)(2,1)S(1)}, bf16[768,768]{1,0:T(8,128)(2,1)S(1)}) custom-call(s32[1]{0:T(128)S(6)} %convert_element_type.3.last_ref, s32[1]{0:T(128)} %bitcast.place_ref, bf16[96,2560]{1,0:T(8,128)(2,1)S(1)} %copy-done.3, ...), custom_call_target="tpu_custom_call" | custom-call | flops 5435817984 | bytes 9437184 | tf_op jit(solution)/shard_map/compose/pallas_call | solution.py:250
  113.2 1.7 collective-permute-start.19
  115.0 8.3 %collective-permute-done.13.refs_5_ = bf16[96,2432]{1,0:T(8,128)(2,1)S(1)} collective-permute-done((bf16[96,2432]{1,0:T(8,128)(2,1)S(1)}, bf16[96,2432]{1,0:T(8,128)(2,1)S(1)}, u32[]{:S(2)}, u32[]{:S(2)}) %collective-permute-start.13) | collective-permute-done | bytes 466976 | tf_op jit(solution)/shard_map/ppermute | solution.py:556
  123.3 1.7 collective-permute-start.14
  125.3 1.7 collective-permute-start.6
  127.0 8.9 %compose.4 = (bf16[8,768,768]{2,1,0:T(8,128)(2,1)S(1)}, f32[8,96,768]{2,1,0:T(8,128)S(1)}, bf16[8,96,768]{2,1,0:T(8,128)(2,1)S(1)}, bf16[768,768]{1,0:T(8,128)(2,1)S(1)}) custom-call(s32[1]{0:T(128)S(6)} %convert_element_type.3.last_ref, s32[1]{0:T(128)} %bitcast.place_ref, ...), custom_call_target="tpu_custom_call", output_to_operand_aliasing={{0}: (19, {}), {1}: (20, {}), {2}: (21, {})} | custom-call | flops 5435817984 | bytes 9437184 | tf_op jit(solution)/shard_map/compose/pallas_call | solution.py:250
  135.9 6.2 %collective-permute-done.14.refs_6_ = bf16[96,2432]{1,0:T(8,128)(2,1)S(1)} collective-permute-done((bf16[96,2432]{1,0:T(8,128)(2,1)S(1)}, bf16[96,2432]{1,0:T(8,128)(2,1)S(1)}, u32[]{:S(2)}, u32[]{:S(2)}) %collective-permute-start.14) | collective-permute-done | bytes 466976 | tf_op jit(solution)/shard_map/ppermute | solution.py:556
  142.1 1.5 collective-permute-done.6.refs_2_
  143.6 1.3 collective-permute-start.15
  144.9 0.8 collective-permute-start.7
  145.6 8.9 %compose.5 = (bf16[8,768,768]{2,1,0:T(8,128)(2,1)S(1)}, f32[8,96,768]{2,1,0:T(8,128)S(1)}, bf16[8,96,768]{2,1,0:T(8,128)(2,1)S(1)}, bf16[768,768]{1,0:T(8,128)(2,1)S(1)}) custom-call(s32[1]{0:T(128)S(6)} %convert_element_type.3.last_ref, s32[1]{0:T(128)} %bitcast.place_ref, ...), custom_call_target="tpu_custom_call", output_to_operand_aliasing={{0}: (19, {}), {1}: (20, {}), {2}: (21, {})} | custom-call | flops 5435817984 | bytes 9437184 | tf_op jit(solution)/shard_map/compose/pallas_call | solution.py:250
  154.6 5.0 %chain.1 = (bf16[2,768,768]{2,1,0:T(8,128)(2,1)S(1)}, bf16[2,768,768]{2,1,0:T(8,128)(2,1)S(1)}) custom-call(s32[1]{0:T(128)} %bitcast.place_ref, bf16[96,2432]{1,0:T(8,128)(2,1)S(1)} %get-tuple-element.68.refs_0_, bf16[96,2432]{1,0:T(8,128)(2,1)S(1)} %collective-permute-done.5.refs_1_, bf16[96,2432]{1,0:T(8,128)(2,1)S(1)} %collective-permute-done.6.refs_2_, ...), custom_call_target="tpu_custom_call" | custom-call | flops 3623878656 | bytes 9437184 | tf_op jit(solution)/shard_map/chain/pallas_call | solution.py:312
  159.9 0.9 collective-permute-start.31
  160.9 2.3 %extend_factors.1 = (bf16[8,768,768]{2,1,0:T(8,128)(2,1)S(1)}, bf16[8,96,768]{2,1,0:T(8,128)(2,1)S(1)}) custom-call(s32[1]{0:T(128)} %bitcast.place_ref, bf16[2,768,768]{2,1,0:T(8,128)(2,1)S(1)} %get-tuple-element.108.gain_ref, bf16[8,768,768]{2,1,0:T(8,128)(2,1)S(1)} %get-tuple-element.109.factor_in, ...), custom_call_target="tpu_custom_call", output_to_operand_aliasing={{0}: (2, {}), {1}: (3, {})} | custom-call | flops 1811939328 | bytes 4718592 | tf_op jit(solution)/shard_map/extend_factors/pallas_call | solution.py:355
  163.2 1.8 hop.2
  165.7 1.8 hop.3
  167.6 1.3 collective-permute-start.33
  168.9 1.1 own_rows.1.own_ref
  169.9 13.2 %collective-permute-done.33.refs_2_ = bf16[6,256,256]{2,1,0:T(8,128)(2,1)S(1)} collective-permute-done((bf16[6,256,256]{2,1,0:T(8,128)(2,1)S(1)}, bf16[6,256,256]{2,1,0:T(8,128)(2,1)S(1)}, u32[]{:S(2)}, u32[]{:S(2)}) %collective-permute-start.33) | collective-permute-done | bytes 786464 | tf_op jit(solution)/shard_map/ppermute | solution.py:600
  183.2 5.6 %finish.1 = f32[8,96,768]{2,1,0:T(8,128)} custom-call(bf16[8,768,768]{2,1,0:T(8,128)(2,1)S(1)} %get-tuple-element.111.factor_ref, f32[8,96,768]{2,1,0:T(8,128)S(1)} %own_rows.1.own_ref, bf16[8,96,768]{2,1,0:T(8,128)(2,1)S(1)} %get-tuple-element.114.mine_ref, bf16[6,256,256]{2,1,0:T(8,128)(2,1)S(1)} %collective-permute-done.31.refs_0_, ...), custom_call_target="tpu_custom_call" | custom-call | tf_op jit(solution)/shard_map/finish/pallas_call | solution.py:515
  (41 shorter events, 4.6 us)
Async XLA Ops:
  0.0 51.4 %copy-start.1 = (bf16[8,96,768]{2,1,0:T(8,128)(2,1)S(1)}, bf16[8,96,768]{2,1,0:T(8,128)(2,1)}, u32[]{:S(2)}) copy-start(bf16[8,96,768]{2,1,0:T(8,128)(2,1)} %gain_ref.3) | copy-start | bytes 3538948
  0.0 51.4 %copy-start = (f32[8,96,768]{2,1,0:T(8,128)S(1)}, f32[8,96,768]{2,1,0:T(8,128)}, u32[]{:S(2)}) copy-start(f32[8,96,768]{2,1,0:T(8,128)} %increment_ref.3) | copy-start | bytes 7077892
  3.5 86.9 %copy-start.3 = (bf16[96,2560]{1,0:T(8,128)(2,1)S(1)}, bf16[96,2560]{1,0:T(8,128)(2,1)}, u32[]{:S(2)}) copy-start(bf16[96,2560]{1,0:T(8,128)(2,1)} %get-tuple-element.91.refs_0_.refs_8_) | copy-start | bytes 1474564
  3.5 14.8 %collective-permute-start = (bf16[96,2432]{1,0:T(8,128)(2,1)}, bf16[96,2432]{1,0:T(8,128)(2,1)S(1)}, u32[]{:S(2)}, u32[]{:S(2)}) collective-permute-start(bf16[96,2432]{1,0:T(8,128)(2,1)} %get-tuple-element.82.refs_0_.refs_8_), channel_id=1, source_target_pairs={{1,3},{3,5},{5,7},{7,6},{6,4},{4,2},{2,0},{0,1},{9,11},{11,13},{13... | collective-permute-start | bytes 1400840 | tf_op jit(solution)/shard_map/ppermute | solution.py:556
  6.5 13.8 %collective-permute-start.8 = (bf16[96,2432]{1,0:T(8,128)(2,1)}, bf16[96,2432]{1,0:T(8,128)(2,1)S(1)}, u32[]{:S(2)}, u32[]{:S(2)}) collective-permute-start(bf16[96,2432]{1,0:T(8,128)(2,1)} %get-tuple-element.82.refs_0_.refs_8_), channel_id=1, source_target_pairs={{1,0},{3,1},{5,3},{7,5},{6,7},{4,6},{2,4},{0,2},{9,8},{11,9},{13,1... | collective-permute-start | bytes 1400840 | tf_op jit(solution)/shard_map/ppermute | solution.py:556
  6.6 22.2 %collective-permute-start.21 = (bf16[96,2560]{1,0:T(8,128)(2,1)}, bf16[96,2560]{1,0:T(8,128)(2,1)S(1)}, u32[]{:S(2)}, u32[]{:S(2)}) collective-permute-start(bf16[96,2560]{1,0:T(8,128)(2,1)} %get-tuple-element.91.refs_0_.refs_8_), channel_id=1, source_target_pairs={{1,3},{3,5},{5,7},{7,6},{6,4},{4,2},{2,0},{0,1},{9,11},{11,13},{13... | collective-permute-start | bytes 1474568 | tf_op jit(solution)/shard_map/ppermute | solution.py:556
  18.3 20.5 %collective-permute-start.1 = (bf16[96,2432]{1,0:T(8,128)(2,1)S(1)}, bf16[96,2432]{1,0:T(8,128)(2,1)S(1)}, u32[]{:S(2)}, u32[]{:S(2)}) collective-permute-start(bf16[96,2432]{1,0:T(8,128)(2,1)S(1)} %collective-permute-done.refs_1_.refs_9_), channel_id=1, source_target_pairs={{1,3},{3,5},{5,7},{7,6},{6,4},{4,2},{2,0},{0,1},{9,11},{11,13},{13... | collective-permute-start | bytes 1400840 | tf_op jit(solution)/shard_map/ppermute | solution.py:556
  20.3 20.5 %collective-permute-start.9 = (bf16[96,2432]{1,0:T(8,128)(2,1)S(1)}, bf16[96,2432]{1,0:T(8,128)(2,1)S(1)}, u32[]{:S(2)}, u32[]{:S(2)}) collective-permute-start(bf16[96,2432]{1,0:T(8,128)(2,1)S(1)} %collective-permute-done.8.refs_4_.refs_12_), channel_id=1, source_target_pairs={{1,0},{3,1},{5,3},{7,5},{6,7},{4,6},{2,4},{0,2},{9,8},{11,9},{13,1... | collective-permute-start | bytes 1400840 | tf_op jit(solution)/shard_map/ppermute | solution.py:556
  20.4 20.6 %collective-permute-start.25 = (bf16[96,2560]{1,0:T(8,128)(2,1)}, bf16[96,2560]{1,0:T(8,128)(2,1)S(1)}, u32[]{:S(2)}, u32[]{:S(2)}) collective-permute-start(bf16[96,2560]{1,0:T(8,128)(2,1)} %get-tuple-element.91.refs_0_.refs_8_), channel_id=1, source_target_pairs={{1,0},{3,1},{5,3},{7,5},{6,7},{4,6},{2,4},{0,2},{9,8},{11,9},{13,1... | collective-permute-start | bytes 1474568 | tf_op jit(solution)/shard_map/ppermute | solution.py:556
  28.8 20.5 %collective-permute-start.22 = (bf16[96,2560]{1,0:T(8,128)(2,1)S(1)}, bf16[96,2560]{1,0:T(8,128)(2,1)S(1)}, u32[]{:S(2)}, u32[]{:S(2)}) collective-permute-start(bf16[96,2560]{1,0:T(8,128)(2,1)S(1)} %collective-permute-done.21.refs_1_.refs_9_), channel_id=1, source_target_pairs={{1,3},{3,5},{5,7},{7,6},{6,4},{4,2},{2,0},{0,1},{9,11},{11,13},{13... | collective-permute-start | bytes 1474568 | tf_op jit(solution)/shard_map/ppermute | solution.py:556
  38.8 20.5 %collective-permute-start.2 = (bf16[96,2432]{1,0:T(8,128)(2,1)S(1)}, bf16[96,2432]{1,0:T(8,128)(2,1)S(1)}, u32[]{:S(2)}, u32[]{:S(2)}) collective-permute-start(bf16[96,2432]{1,0:T(8,128)(2,1)S(1)} %collective-permute-done.1.refs_2_.refs_10_), channel_id=1, source_target_pairs={{1,3},{3,5},{5,7},{7,6},{6,4},{4,2},{2,0},{0,1},{9,11},{11,13},{13... | collective-permute-start | bytes 1400840 | tf_op jit(solution)/shard_map/ppermute | solution.py:556
  40.8 20.5 %collective-permute-start.10 = (bf16[96,2432]{1,0:T(8,128)(2,1)S(1)}, bf16[96,2432]{1,0:T(8,128)(2,1)S(1)}, u32[]{:S(2)}, u32[]{:S(2)}) collective-permute-start(bf16[96,2432]{1,0:T(8,128)(2,1)S(1)} %collective-permute-done.9.refs_5_.refs_13_), channel_id=1, source_target_pairs={{1,0},{3,1},{5,3},{7,5},{6,7},{4,6},{2,4},{0,2},{9,8},{11,9},{13,1... | collective-permute-start | bytes 1400840 | tf_op jit(solution)/shard_map/ppermute | solution.py:556
  41.0 20.5 %collective-permute-start.26 = (bf16[96,2560]{1,0:T(8,128)(2,1)S(1)}, bf16[96,2560]{1,0:T(8,128)(2,1)S(1)}, u32[]{:S(2)}, u32[]{:S(2)}) collective-permute-start(bf16[96,2560]{1,0:T(8,128)(2,1)S(1)} %collective-permute-done.25.refs_5_.refs_13_), channel_id=1, source_target_pairs={{1,0},{3,1},{5,3},{7,5},{6,7},{4,6},{2,4},{0,2},{9,8},{11,9},{13,1... | collective-permute-start | bytes 1474568 | tf_op jit(solution)/shard_map/ppermute | solution.py:556
  49.4 20.5 %collective-permute-start.23 = (bf16[96,2560]{1,0:T(8,128)(2,1)S(1)}, bf16[96,2560]{1,0:T(8,128)(2,1)S(1)}, u32[]{:S(2)}, u32[]{:S(2)}) collective-permute-start(bf16[96,2560]{1,0:T(8,128)(2,1)S(1)} %collective-permute-done.22.refs_2_.refs_10_), channel_id=1, source_target_pairs={{1,3},{3,5},{5,7},{7,6},{6,4},{4,2},{2,0},{0,1},{9,11},{11,13},{13... | collective-permute-start | bytes 1474568 | tf_op jit(solution)/shard_map/ppermute | solution.py:556
  59.4 20.5 %collective-permute-start.3 = (bf16[96,2432]{1,0:T(8,128)(2,1)S(1)}, bf16[96,2432]{1,0:T(8,128)(2,1)S(1)}, u32[]{:S(2)}, u32[]{:S(2)}) collective-permute-start(bf16[96,2432]{1,0:T(8,128)(2,1)S(1)} %get-tuple-element.72.refs_0_.refs_8_), channel_id=1, source_target_pairs={{1,3},{3,5},{5,7},{7,6},{6,4},{4,2},{2,0},{0,1},{9,11},{11,13},{13... | collective-permute-start | bytes 1400840 | tf_op jit(solution)/shard_map/ppermute | solution.py:556
  61.4 20.5 %collective-permute-start.11 = (bf16[96,2432]{1,0:T(8,128)(2,1)S(1)}, bf16[96,2432]{1,0:T(8,128)(2,1)S(1)}, u32[]{:S(2)}, u32[]{:S(2)}) collective-permute-start(bf16[96,2432]{1,0:T(8,128)(2,1)S(1)} %get-tuple-element.72.refs_0_.refs_8_), channel_id=1, source_target_pairs={{1,0},{3,1},{5,3},{7,5},{6,7},{4,6},{2,4},{0,2},{9,8},{11,9},{13,1... | collective-permute-start | bytes 1400840 | tf_op jit(solution)/shard_map/ppermute | solution.py:556
  61.5 24.0 %collective-permute-start.27 = (bf16[96,2560]{1,0:T(8,128)(2,1)S(1)}, bf16[96,2560]{1,0:T(8,128)(2,1)S(1)}, u32[]{:S(2)}, u32[]{:S(2)}) collective-permute-start(bf16[96,2560]{1,0:T(8,128)(2,1)S(1)} %collective-permute-done.26.refs_6_.refs_14_), channel_id=1, source_target_pairs={{1,0},{3,1},{5,3},{7,5},{6,7},{4,6},{2,4},{0,2},{9,8},{11,9},{13,1... | collective-permute-start | bytes 1474568 | tf_op jit(solution)/shard_map/ppermute | solution.py:556
  69.9 20.5 %collective-permute-start.24 = (bf16[96,2560]{1,0:T(8,128)(2,1)S(1)}, bf16[96,2560]{1,0:T(8,128)(2,1)S(1)}, u32[]{:S(2)}, u32[]{:S(2)}) collective-permute-start(bf16[96,2560]{1,0:T(8,128)(2,1)S(1)} %collective-permute-done.23.refs_3_.refs_11_), channel_id=1, source_target_pairs={{1,3},{3,5},{5,7},{7,6},{6,4},{4,2},{2,0},{0,1},{9,11},{11,13},{13... | collective-permute-start | bytes 1474568 | tf_op jit(solution)/shard_map/ppermute | solution.py:556
  71.9 23.6 %collective-permute-start.20 = (bf16[96,2432]{1,0:T(8,128)(2,1)S(1)}, bf16[96,2432]{1,0:T(8,128)(2,1)S(1)}, u32[]{:S(2)}, u32[]{:S(2)}) collective-permute-start(bf16[96,2432]{1,0:T(8,128)(2,1)S(1)} %collective-permute-done.10.refs_6_.refs_14_), channel_id=1, source_target_pairs={{1,0},{3,1},{5,3},{7,5},{6,7},{4,6},{2,4},{0,2},{9,8},{11,9},{13,1... | collective-permute-start | bytes 1400840 | tf_op jit(solution)/shard_map/ppermute | solution.py:556
  79.9 19.7 %collective-permute-start.4 = (bf16[96,2432]{1,0:T(8,128)(2,1)S(1)}, bf16[96,2432]{1,0:T(8,128)(2,1)S(1)}, u32[]{:S(2)}, u32[]{:S(2)}) collective-permute-start(bf16[96,2432]{1,0:T(8,128)(2,1)S(1)} %collective-permute-done.3.refs_1_.refs_9_), channel_id=1, source_target_pairs={{1,3},{3,5},{5,7},{7,6},{6,4},{4,2},{2,0},{0,1},{9,11},{11,13},{13... | collective-permute-start | bytes 1400840 | tf_op jit(solution)/shard_map/ppermute | solution.py:556
  81.9 21.4 %collective-permute-start.12 = (bf16[96,2432]{1,0:T(8,128)(2,1)S(1)}, bf16[96,2432]{1,0:T(8,128)(2,1)S(1)}, u32[]{:S(2)}, u32[]{:S(2)}) collective-permute-start(bf16[96,2432]{1,0:T(8,128)(2,1)S(1)} %get-tuple-element.68.refs_0_), channel_id=1, source_target_pairs={{1,0},{3,1},{5,3},{7,5},{6,7},{4,6},{2,4},{0,2},{9,8},{11,9},{13,1... | collective-permute-start | bytes 1400840 | tf_op jit(solution)/shard_map/ppermute | solution.py:556
  90.6 36.4 %copy-start.2 = (bf16[96,2432]{1,0:T(8,128)(2,1)S(1)}, bf16[96,2432]{1,0:T(8,128)(2,1)}, u32[]{:S(2)}) copy-start(bf16[96,2432]{1,0:T(8,128)(2,1)} %get-tuple-element.82.refs_0_.refs_8_) | copy-start | bytes 1400836
  90.6 10.8 %collective-permute-start.28 = (bf16[8,96,128]{2,1,0:T(8,128)(2,1)S(1)}, bf16[8,96,128]{2,1,0:T(8,128)(2,1)S(1)}, u32[]{:S(2)}, u32[]{:S(2)}) collective-permute-start(bf16[8,96,128]{2,1,0:T(8,128)(2,1)S(1)} %collect.1.refs_19_), channel_id=1, source_target_pairs={{0,24},{1,25},{2,26},{3,27},{4,28},{5,29},{6,30},{7,31}} | collective-permute-start | bytes 589832 | tf_op jit(solution)/shard_map/ppermute | solution.py:584
  92.0 9.6 %collective-permute-start.29 = (bf16[8,96,128]{2,1,0:T(8,128)(2,1)S(1)}, bf16[8,96,128]{2,1,0:T(8,128)(2,1)S(1)}, u32[]{:S(2)}, u32[]{:S(2)}) collective-permute-start(bf16[8,96,128]{2,1,0:T(8,128)(2,1)S(1)} %collect.1.refs_19_), channel_id=1, source_target_pairs={{8,24},{9,25},{10,26},{11,27},{12,28},{13,29},{14,30},{15,31}} | collective-permute-start | bytes 589832 | tf_op jit(solution)/shard_map/ppermute | solution.py:584
  95.5 8.1 %collective-permute-start.30 = (bf16[8,96,128]{2,1,0:T(8,128)(2,1)S(1)}, bf16[8,96,128]{2,1,0:T(8,128)(2,1)S(1)}, u32[]{:S(2)}, u32[]{:S(2)}) collective-permute-start(bf16[8,96,128]{2,1,0:T(8,128)(2,1)S(1)} %collect.1.refs_19_), channel_id=1, source_target_pairs={{16,24},{17,25},{18,26},{19,27},{20,28},{21,29},{22,30},{23,31}} | collective-permute-start | bytes 589832 | tf_op jit(solution)/shard_map/ppermute | solution.py:584
  99.6 13.6 %collective-permute-start.18 = (bf16[96,2432]{1,0:T(8,128)(2,1)S(1)}, bf16[96,2432]{1,0:T(8,128)(2,1)S(1)}, u32[]{:S(2)}, u32[]{:S(2)}) collective-permute-start(bf16[96,2432]{1,0:T(8,128)(2,1)S(1)} %collective-permute-done.11.refs_5_.refs_13_), channel_id=1, source_target_pairs={{1,0},{3,1},{5,3},{7,5},{6,7},{4,6},{2,4},{0,2},{9,8},{11,9},{13,1... | collective-permute-start | bytes 1400840 | tf_op jit(solution)/shard_map/ppermute | solution.py:556
  101.4 23.6 %collective-permute-start.16 = (bf16[96,2432]{1,0:T(8,128)(2,1)S(1)}, bf16[96,2432]{1,0:T(8,128)(2,1)S(1)}, u32[]{:S(2)}, u32[]{:S(2)}) collective-permute-start(bf16[96,2432]{1,0:T(8,128)(2,1)S(1)} %collective-permute-done.4.refs_2_.refs_10_), channel_id=1, source_target_pairs={{1,3},{3,5},{5,7},{7,6},{6,4},{4,2},{2,0},{0,1},{9,11},{11,13},{13... | collective-permute-start | bytes 1400840 | tf_op jit(solution)/shard_map/ppermute | solution.py:556
  101.7 23.6 %collective-permute-start.5 = (bf16[96,2432]{1,0:T(8,128)(2,1)S(1)}, bf16[96,2432]{1,0:T(8,128)(2,1)S(1)}, u32[]{:S(2)}, u32[]{:S(2)}) collective-permute-start(bf16[96,2432]{1,0:T(8,128)(2,1)S(1)} %get-tuple-element.68.refs_0_), channel_id=1, source_target_pairs={{1,3},{3,5},{5,7},{7,6},{6,4},{4,2},{2,0},{0,1},{9,11},{11,13},{13... | collective-permute-start | bytes 1400840 | tf_op jit(solution)/shard_map/ppermute | solution.py:556
  103.3 19.9 %collective-permute-start.13 = (bf16[96,2432]{1,0:T(8,128)(2,1)S(1)}, bf16[96,2432]{1,0:T(8,128)(2,1)S(1)}, u32[]{:S(2)}, u32[]{:S(2)}) collective-permute-start(bf16[96,2432]{1,0:T(8,128)(2,1)S(1)} %collective-permute-done.12.refs_4_), channel_id=1, source_target_pairs={{1,0},{3,1},{5,3},{7,5},{6,7},{4,6},{2,4},{0,2},{9,8},{11,9},{13,1... | collective-permute-start | bytes 1400840 | tf_op jit(solution)/shard_map/ppermute | solution.py:556
  113.2 22.6 %collective-permute-start.19 = (bf16[96,2432]{1,0:T(8,128)(2,1)S(1)}, bf16[96,2432]{1,0:T(8,128)(2,1)S(1)}, u32[]{:S(2)}, u32[]{:S(2)}) collective-permute-start(bf16[96,2432]{1,0:T(8,128)(2,1)S(1)} %collective-permute-done.18.refs_6_.refs_14_), channel_id=1, source_target_pairs={{1,0},{3,1},{5,3},{7,5},{6,7},{4,6},{2,4},{0,2},{9,8},{11,9},{13,1... | collective-permute-start | bytes 1400840 | tf_op jit(solution)/shard_map/ppermute | solution.py:556
  123.3 18.8 %collective-permute-start.14 = (bf16[96,2432]{1,0:T(8,128)(2,1)S(1)}, bf16[96,2432]{1,0:T(8,128)(2,1)S(1)}, u32[]{:S(2)}, u32[]{:S(2)}) collective-permute-start(bf16[96,2432]{1,0:T(8,128)(2,1)S(1)} %collective-permute-done.13.refs_5_), channel_id=1, source_target_pairs={{1,0},{3,1},{5,3},{7,5},{6,7},{4,6},{2,4},{0,2},{9,8},{11,9},{13,1... | collective-permute-start | bytes 1400840 | tf_op jit(solution)/shard_map/ppermute | solution.py:556
  125.0 17.1 %collective-permute-start.17 = (bf16[96,2432]{1,0:T(8,128)(2,1)S(1)}, bf16[96,2432]{1,0:T(8,128)(2,1)S(1)}, u32[]{:S(2)}, u32[]{:S(2)}) collective-permute-start(bf16[96,2432]{1,0:T(8,128)(2,1)S(1)} %collective-permute-done.16.refs_3_.refs_11_), channel_id=1, source_target_pairs={{1,3},{3,5},{5,7},{7,6},{6,4},{4,2},{2,0},{0,1},{9,11},{11,13},{13... | collective-permute-start | bytes 1400840 | tf_op jit(solution)/shard_map/ppermute | solution.py:556
  125.3 18.3 %collective-permute-start.6 = (bf16[96,2432]{1,0:T(8,128)(2,1)S(1)}, bf16[96,2432]{1,0:T(8,128)(2,1)S(1)}, u32[]{:S(2)}, u32[]{:S(2)}) collective-permute-start(bf16[96,2432]{1,0:T(8,128)(2,1)S(1)} %collective-permute-done.5.refs_1_), channel_id=1, source_target_pairs={{1,3},{3,5},{5,7},{7,6},{6,4},{4,2},{2,0},{0,1},{9,11},{11,13},{13... | collective-permute-start | bytes 1400840 | tf_op jit(solution)/shard_map/ppermute | solution.py:556
  143.6 10.9 %collective-permute-start.15 = (bf16[96,2432]{1,0:T(8,128)(2,1)S(1)}, bf16[96,2432]{1,0:T(8,128)(2,1)S(1)}, u32[]{:S(2)}, u32[]{:S(2)}) collective-permute-start(bf16[96,2432]{1,0:T(8,128)(2,1)S(1)} %collective-permute-done.14.refs_6_), channel_id=1, source_target_pairs={{1,0},{3,1},{5,3},{7,5},{6,7},{4,6},{2,4},{0,2},{9,8},{11,9},{13,1... | collective-permute-start | bytes 1400840 | tf_op jit(solution)/shard_map/ppermute | solution.py:556
  144.9 9.7 %collective-permute-start.7 = (bf16[96,2432]{1,0:T(8,128)(2,1)S(1)}, bf16[96,2432]{1,0:T(8,128)(2,1)S(1)}, u32[]{:S(2)}, u32[]{:S(2)}) collective-permute-start(bf16[96,2432]{1,0:T(8,128)(2,1)S(1)} %collective-permute-done.6.refs_2_), channel_id=1, source_target_pairs={{1,3},{3,5},{5,7},{7,6},{6,4},{4,2},{2,0},{0,1},{9,11},{11,13},{13... | collective-permute-start | bytes 1400840 | tf_op jit(solution)/shard_map/ppermute | solution.py:556
  159.9 3.3 %collective-permute-start.31 = (bf16[6,256,256]{2,1,0:T(8,128)(2,1)S(1)}, bf16[6,256,256]{2,1,0:T(8,128)(2,1)S(1)}, u32[]{:S(2)}, u32[]{:S(2)}) collective-permute-start(bf16[6,256,256]{2,1,0:T(8,128)(2,1)S(1)} %fold.1), channel_id=1, source_target_pairs={{24,16},{25,17},{26,18},{27,19},{28,20},{29,21},{30,22},{31,23}} | collective-permute-start | bytes 2359304 | tf_op jit(solution)/shard_map/ppermute | solution.py:600
  165.0 0.7 collective-permute-start.32
  167.6 15.6 %collective-permute-start.33 = (bf16[6,256,256]{2,1,0:T(8,128)(2,1)S(1)}, bf16[6,256,256]{2,1,0:T(8,128)(2,1)S(1)}, u32[]{:S(2)}, u32[]{:S(2)}) collective-permute-start(bf16[6,256,256]{2,1,0:T(8,128)(2,1)S(1)} %hop.3), channel_id=1, source_target_pairs={{8,0},{9,1},{10,2},{11,3},{12,4},{13,5},{14,6},{15,7}} | collective-permute-start | bytes 2359304 | tf_op jit(solution)/shard_map/ppermute | solution.py:600

commit v14 on v13

--- a/solution.py
+++ b/solution.py
@@ -566,7 +566,7 @@
         for way, hops in ((1, rights[turn]), (-1, count - 1 - rights[turn])):
             source = array
             if turn > 1:
-                before = found[turn - 1][way]
+                before = found[0 if turn == 2 else turn - 1][way]
                 gate = count // 2 - 1 if turn == 2 else len(before) - 3
                 source, before[gate] = lax.optimization_barrier((source, before[gate]))
                 for n in range(gate + 1, len(before)):
@@ -575,11 +575,17 @@
             for _ in range(hops):
                 found[turn][way].append(passed(found[turn][way][-1], way))
     ties = [
-        [found[2][1][1], found[2][-1][1], found[1][-1][-1]],
-        [found[2][1][2], found[2][-1][2], found[3][-1][1]],
+        [found[2][1][2], found[2][-1][2]],
+        [found[2][1][3], found[2][-1][3]],
         [found[3][1][-2], found[3][-1][-2]],
     ]
-    tile = collect(place, cycle, rights[0], [own[0]] + found[0][1][1:] + found[0][-1][1:])
+    parts, _ = lax.optimization_barrier(
+        (
+            [own[0]] + found[0][1][1:] + found[0][-1][1:],
+            [found[2][1][1], found[2][-1][1], found[1][1][-1], found[1][-1][-1]],
+        )
+    )
+    tile = collect(place, cycle, rights[0], parts)
     ends = [
         lax.ppermute(tile, "tm", [(n, blocks - 1)]) if n < blocks - 1 else tile
         for n in range(gains.shape[2] // 2 // LANES + 1)

time: 189 us -> 190 us (level)
  waiting for transfers between devices: 97 us -> 104 us
  starting transfers between devices: 42.5 us -> 36.6 us
    ppermute x28, waiting for transfers between devices: 83.8 us -> 90.2 us  [passed(): lax.ppermute(array, 'tile', [(cycle[n], cycle[(n + way) % count]) for n i...]
    ppermute x28, starting transfers between devices: 36.8 us -> 30.9 us  [passed(): lax.ppermute(array, 'tile', [(cycle[n], cycle[(n + way) % count]) for n i...]
  transfers between devices with their start and end apart: 34 -> 34, of which waited for: 18 -> 15; matrix products, arithmetic and copies ran while one was open for 0% -> 0% of each run, Pallas kernels for 16% -> 16%
where the time goes in v14:
time: 190 us
  waiting for transfers between devices  104 us (55%)
  Pallas kernels  49 us (26%)
  starting transfers between devices  36.6 us (19%)
    ppermute x28, waiting for transfers between devices, passed(): lax.ppermute(array, 'tile', [(cycle[n], cycle[(n + way) % count]) for n i...  90.2 us
    ppermute x28, starting transfers between devices, passed(): lax.ppermute(array, 'tile', [(cycle[n], cycle[(n + way) % count]) for n i...  30.9 us
    pallas_call x3, Pallas kernels, compose(): pl.pallas_call(functools.partial(compose_kernel, cycle, right, first), gr...  26.7 us
    ppermute x3, waiting for transfers between devices, local(): lax.ppermute(hop(factors, early[1], packed), 'tm', [(turn, turn - 1)])  13.9 us
    pallas_call x1, Pallas kernels, finish(): pl.pallas_call(functools.partial(finish_kernel, len(packed)), grid=(steps...  5.6 us
    pallas_call x1, Pallas kernels, chain(): pl.pallas_call(functools.partial(chain_kernel, cycle, right, turns), grid...  5.02 us
    pallas_call x2, Pallas kernels, pack(): pl.pallas_call(functools.partial(pack_kernel, count, ranges), grid_spec=p...  4.25 us
  transfers between devices with their start and end apart: 34, of which 15 were waited for; matrix products, arithmetic and copies ran while one was open for 0% of the time, Pallas kernels for 16%

profile of v14, /device:TPU:0, one launch (start us, length us, event | category | flops | bytes accessed | tf_op | source)
XLA Modules:
  0.0 189.9 jit_solution(2246318895730995253)
XLA Ops:
  0.0 3.5 %pack.3 = (bf16[96,2560]{1,0:T(8,128)(2,1)}, bf16[96,2432]{1,0:T(8,128)(2,1)}) custom-call(s32[1]{0:T(128)} %bitcast.place_ref, s32[1]{0:T(128)} %bitcast.1.block_ref, bf16[8,96,768]{2,1,0:T(8,128)(2,1)} %gain_ref.3, f32[8,96,768]{2,1,0:T(8,128)} %increment_ref.3, f32[96,768]{1,0:T(8,128)} %refs_0_.1), custom_call_target="tpu_custom_call" | custom-call | tf_op jit(solution)/shard_map/pack/pallas_call | solution.py:80
  3.5 3.0 %collective-permute-start = (bf16[96,2560]{1,0:T(8,128)(2,1)}, bf16[96,2560]{1,0:T(8,128)(2,1)S(1)}, u32[]{:S(2)}, u32[]{:S(2)}) collective-permute-start(bf16[96,2560]{1,0:T(8,128)(2,1)} %get-tuple-element.107.refs_0_.refs_8_), channel_id=1, source_target_pairs={{1,3},{3,5},{5,7},{7,6},{6,4},{4,2},{2,0},{0,1},{9,11},{11,13},{13... | collective-permute-start | bytes 1474568 | tf_op jit(solution)/shard_map/ppermute | solution.py:556
  6.6 11.4 %collective-permute-done.refs_1_.refs_9_ = bf16[96,2560]{1,0:T(8,128)(2,1)S(1)} collective-permute-done((bf16[96,2560]{1,0:T(8,128)(2,1)}, bf16[96,2560]{1,0:T(8,128)(2,1)S(1)}, u32[]{:S(2)}, u32[]{:S(2)}) %collective-permute-start) | collective-permute-done | bytes 491552 | tf_op jit(solution)/shard_map/ppermute | solution.py:556
  18.1 1.6 collective-permute-start.1
  20.1 1.7 collective-permute-start.9
  22.1 10.1 %collective-permute-done.1.refs_2_.refs_10_ = bf16[96,2560]{1,0:T(8,128)(2,1)S(1)} collective-permute-done((bf16[96,2560]{1,0:T(8,128)(2,1)S(1)}, bf16[96,2560]{1,0:T(8,128)(2,1)S(1)}, u32[]{:S(2)}, u32[]{:S(2)}) %collective-permute-start.1) | collective-permute-done | bytes 491552 | tf_op jit(solution)/shard_map/ppermute | solution.py:556
  32.2 1.6 collective-permute-start.2
  34.2 9.8 %collective-permute-done.9.refs_6_.refs_14_ = bf16[96,2560]{1,0:T(8,128)(2,1)S(1)} collective-permute-done((bf16[96,2560]{1,0:T(8,128)(2,1)S(1)}, bf16[96,2560]{1,0:T(8,128)(2,1)S(1)}, u32[]{:S(2)}, u32[]{:S(2)}) %collective-permute-start.9) | collective-permute-done | bytes 491552 | tf_op jit(solution)/shard_map/ppermute | solution.py:556
  44.5 1.6 collective-permute-start.21
  46.1 8.0 %collective-permute-done.24.refs_5_.refs_13_ = bf16[96,2432]{1,0:T(8,128)(2,1)S(1)} collective-permute-done((bf16[96,2432]{1,0:T(8,128)(2,1)S(1)}, bf16[96,2432]{1,0:T(8,128)(2,1)S(1)}, u32[]{:S(2)}, u32[]{:S(2)}) %collective-permute-start.24) | collective-permute-done | bytes 466976 | tf_op jit(solution)/shard_map/ppermute | solution.py:556
  54.5 0.7 pack.2
  55.2 1.7 collective-permute-start.3
  56.9 7.7 %collective-permute-done.10.refs_7_.refs_15_ = bf16[96,2560]{1,0:T(8,128)(2,1)S(1)} collective-permute-done((bf16[96,2560]{1,0:T(8,128)(2,1)S(1)}, bf16[96,2560]{1,0:T(8,128)(2,1)S(1)}, u32[]{:S(2)}, u32[]{:S(2)}) %collective-permute-start.10) | collective-permute-done | bytes 491552 | tf_op jit(solution)/shard_map/ppermute | solution.py:556
  65.0 1.6 collective-permute-start.22
  66.6 1.6 collective-permute-start.27
  68.2 6.4 %collective-permute-done.25.refs_6_.refs_14_ = bf16[96,2432]{1,0:T(8,128)(2,1)S(1)} collective-permute-done((bf16[96,2432]{1,0:T(8,128)(2,1)S(1)}, bf16[96,2432]{1,0:T(8,128)(2,1)S(1)}, u32[]{:S(2)}, u32[]{:S(2)}) %collective-permute-start.25) | collective-permute-done | bytes 466976 | tf_op jit(solution)/shard_map/ppermute | solution.py:556
  75.0 1.6 collective-permute-start.4
  76.6 8.0 %collective-permute-done.11.refs_5_.refs_13_ = bf16[96,2432]{1,0:T(8,128)(2,1)S(1)} collective-permute-done((bf16[96,2432]{1,0:T(8,128)(2,1)S(1)}, bf16[96,2432]{1,0:T(8,128)(2,1)S(1)}, u32[]{:S(2)}, u32[]{:S(2)}) %collective-permute-start.11) | collective-permute-done | bytes 466976 | tf_op jit(solution)/shard_map/ppermute | solution.py:556
  85.0 1.7 collective-permute-start.12
  86.7 7.9 %collective-permute-done.26.refs_7_.refs_15_ = bf16[96,2432]{1,0:T(8,128)(2,1)S(1)} collective-permute-done((bf16[96,2432]{1,0:T(8,128)(2,1)S(1)}, bf16[96,2432]{1,0:T(8,128)(2,1)S(1)}, u32[]{:S(2)}, u32[]{:S(2)}) %collective-permute-start.26) | collective-permute-done | bytes 466976 | tf_op jit(solution)/shard_map/ppermute | solution.py:556
  94.7 1.4 collective-permute-start.28
  96.2 0.7 collective-permute-start.29
  96.9 4.7 %collective-permute-done.4.refs_2_.refs_10_ = bf16[96,2432]{1,0:T(8,128)(2,1)S(1)} collective-permute-done((bf16[96,2432]{1,0:T(8,128)(2,1)S(1)}, bf16[96,2432]{1,0:T(8,128)(2,1)S(1)}, u32[]{:S(2)}, u32[]{:S(2)}) %collective-permute-start.4) | collective-permute-done | bytes 466976 | tf_op jit(solution)/shard_map/ppermute | solution.py:556
  101.6 0.7 collective-permute-start.30
  102.2 2.4 %collective-permute-done.18.refs_6_.refs_14_ = bf16[96,2432]{1,0:T(8,128)(2,1)S(1)} collective-permute-done((bf16[96,2432]{1,0:T(8,128)(2,1)S(1)}, bf16[96,2432]{1,0:T(8,128)(2,1)S(1)}, u32[]{:S(2)}, u32[]{:S(2)}) %collective-permute-start.18) | collective-permute-done | bytes 466976 | tf_op jit(solution)/shard_map/ppermute | solution.py:556
  104.6 1.6 collective-permute-start.16
  106.2 1.6 collective-permute-start.5
  108.2 6.4 %collective-permute-done.12.refs_4_ = bf16[96,2432]{1,0:T(8,128)(2,1)S(1)} collective-permute-done((bf16[96,2432]{1,0:T(8,128)(2,1)S(1)}, bf16[96,2432]{1,0:T(8,128)(2,1)S(1)}, u32[]{:S(2)}, u32[]{:S(2)}) %collective-permute-start.12) | collective-permute-done | bytes 466976 | tf_op jit(solution)/shard_map/ppermute | solution.py:556
  115.0 8.9 %compose.3 = (bf16[8,768,768]{2,1,0:T(8,128)(2,1)S(1)}, f32[8,96,768]{2,1,0:T(8,128)S(1)}, bf16[8,96,768]{2,1,0:T(8,128)(2,1)S(1)}, bf16[768,768]{1,0:T(8,128)(2,1)S(1)}) custom-call(s32[1]{0:T(128)S(6)} %convert_element_type.3.last_ref, s32[1]{0:T(128)} %bitcast.place_ref, bf16[96,2560]{1,0:T(8,128)(2,1)S(1)} %copy-done.3, ...), custom_call_target="tpu_custom_call" | custom-call | flops 5435817984 | bytes 9437184 | tf_op jit(solution)/shard_map/compose/pallas_call | solution.py:250
  124.6 1.6 collective-permute-start.17
  126.2 1.6 collective-permute-start.6
  127.8 4.5 %collective-permute-done.13.refs_5_ = bf16[96,2432]{1,0:T(8,128)(2,1)S(1)} collective-permute-done((bf16[96,2432]{1,0:T(8,128)(2,1)S(1)}, bf16[96,2432]{1,0:T(8,128)(2,1)S(1)}, u32[]{:S(2)}, u32[]{:S(2)}) %collective-permute-start.13) | collective-permute-done | bytes 466976 | tf_op jit(solution)/shard_map/ppermute | solution.py:556
  132.3 0.7 collective-permute-start.14
  133.0 8.9 %compose.4 = (bf16[8,768,768]{2,1,0:T(8,128)(2,1)S(1)}, f32[8,96,768]{2,1,0:T(8,128)S(1)}, bf16[8,96,768]{2,1,0:T(8,128)(2,1)S(1)}, bf16[768,768]{1,0:T(8,128)(2,1)S(1)}) custom-call(s32[1]{0:T(128)S(6)} %convert_element_type.3.last_ref, s32[1]{0:T(128)} %bitcast.place_ref, ...), custom_call_target="tpu_custom_call", output_to_operand_aliasing={{0}: (19, {}), {1}: (20, {}), {2}: (21, {})} | custom-call | flops 5435817984 | bytes 9437184 | tf_op jit(solution)/shard_map/compose/pallas_call | solution.py:250
  141.9 2.2 %collective-permute-done.6.refs_2_ = bf16[96,2432]{1,0:T(8,128)(2,1)S(1)} collective-permute-done((bf16[96,2432]{1,0:T(8,128)(2,1)S(1)}, bf16[96,2432]{1,0:T(8,128)(2,1)S(1)}, u32[]{:S(2)}, u32[]{:S(2)}) %collective-permute-start.6) | collective-permute-done | bytes 466976 | tf_op jit(solution)/shard_map/ppermute | solution.py:556
  144.1 0.7 collective-permute-start.7
  144.8 1.3 collective-permute-start.15
  146.1 8.9 %compose.5 = (bf16[8,768,768]{2,1,0:T(8,128)(2,1)S(1)}, f32[8,96,768]{2,1,0:T(8,128)S(1)}, bf16[8,96,768]{2,1,0:T(8,128)(2,1)S(1)}, bf16[768,768]{1,0:T(8,128)(2,1)S(1)}) custom-call(s32[1]{0:T(128)S(6)} %convert_element_type.3.last_ref, s32[1]{0:T(128)} %bitcast.place_ref, ...), custom_call_target="tpu_custom_call", output_to_operand_aliasing={{0}: (19, {}), {1}: (20, {}), {2}: (21, {})} | custom-call | flops 5435817984 | bytes 9437184 | tf_op jit(solution)/shard_map/compose/pallas_call | solution.py:250
  155.1 5.0 %chain.1 = (bf16[2,768,768]{2,1,0:T(8,128)(2,1)S(1)}, bf16[2,768,768]{2,1,0:T(8,128)(2,1)S(1)}) custom-call(s32[1]{0:T(128)} %bitcast.place_ref, bf16[96,2432]{1,0:T(8,128)(2,1)S(1)} %get-tuple-element.76.refs_0_, bf16[96,2432]{1,0:T(8,128)(2,1)S(1)} %collective-permute-done.5.refs_1_, bf16[96,2432]{1,0:T(8,128)(2,1)S(1)} %collective-permute-done.6.refs_2_, ...), custom_call_target="tpu_custom_call" | custom-call | flops 3623878656 | bytes 9437184 | tf_op jit(solution)/shard_map/chain/pallas_call | solution.py:312
  160.4 0.9 collective-permute-start.31
  161.3 2.3 %extend_factors.1 = (bf16[8,768,768]{2,1,0:T(8,128)(2,1)S(1)}, bf16[8,96,768]{2,1,0:T(8,128)(2,1)S(1)}) custom-call(s32[1]{0:T(128)} %bitcast.place_ref, bf16[2,768,768]{2,1,0:T(8,128)(2,1)S(1)} %get-tuple-element.124.gain_ref, bf16[8,768,768]{2,1,0:T(8,128)(2,1)S(1)} %get-tuple-element.125.factor_in, ...), custom_call_target="tpu_custom_call", output_to_operand_aliasing={{0}: (2, {}), {1}: (3, {})} | custom-call | flops 1811939328 | bytes 4718592 | tf_op jit(solution)/shard_map/extend_factors/pallas_call | solution.py:355
  163.7 1.8 hop.2
  165.5 0.7 collective-permute-start.32
  166.2 1.8 hop.3
  168.0 1.3 collective-permute-start.33
  169.3 1.1 own_rows.1.own_ref
  170.4 13.9 %collective-permute-done.33.refs_2_ = bf16[6,256,256]{2,1,0:T(8,128)(2,1)S(1)} collective-permute-done((bf16[6,256,256]{2,1,0:T(8,128)(2,1)S(1)}, bf16[6,256,256]{2,1,0:T(8,128)(2,1)S(1)}, u32[]{:S(2)}, u32[]{:S(2)}) %collective-permute-start.33) | collective-permute-done | bytes 786464 | tf_op jit(solution)/shard_map/ppermute | solution.py:606
  184.3 5.6 %finish.1 = f32[8,96,768]{2,1,0:T(8,128)} custom-call(bf16[8,768,768]{2,1,0:T(8,128)(2,1)S(1)} %get-tuple-element.127.factor_ref, f32[8,96,768]{2,1,0:T(8,128)S(1)} %own_rows.1.own_ref, bf16[8,96,768]{2,1,0:T(8,128)(2,1)S(1)} %get-tuple-element.130.mine_ref, bf16[6,256,256]{2,1,0:T(8,128)(2,1)S(1)} %collective-permute-done.31.refs_0_, ...), custom_call_target="tpu_custom_call" | custom-call | tf_op jit(solution)/shard_map/finish/pallas_call | solution.py:515
  (41 shorter events, 5.3 us)
Async XLA Ops:
  0.0 54.5 %copy-start.1 = (bf16[8,96,768]{2,1,0:T(8,128)(2,1)S(1)}, bf16[8,96,768]{2,1,0:T(8,128)(2,1)}, u32[]{:S(2)}) copy-start(bf16[8,96,768]{2,1,0:T(8,128)(2,1)} %gain_ref.3) | copy-start | bytes 3538948
  0.0 54.5 %copy-start = (f32[8,96,768]{2,1,0:T(8,128)S(1)}, f32[8,96,768]{2,1,0:T(8,128)}, u32[]{:S(2)}) copy-start(f32[8,96,768]{2,1,0:T(8,128)} %increment_ref.3) | copy-start | bytes 7077892
  3.5 91.1 %copy-start.3 = (bf16[96,2560]{1,0:T(8,128)(2,1)S(1)}, bf16[96,2560]{1,0:T(8,128)(2,1)}, u32[]{:S(2)}) copy-start(bf16[96,2560]{1,0:T(8,128)(2,1)} %get-tuple-element.107.refs_0_.refs_8_) | copy-start | bytes 1474564
  3.5 14.5 %collective-permute-start = (bf16[96,2560]{1,0:T(8,128)(2,1)}, bf16[96,2560]{1,0:T(8,128)(2,1)S(1)}, u32[]{:S(2)}, u32[]{:S(2)}) collective-permute-start(bf16[96,2560]{1,0:T(8,128)(2,1)} %get-tuple-element.107.refs_0_.refs_8_), channel_id=1, source_target_pairs={{1,3},{3,5},{5,7},{7,6},{6,4},{4,2},{2,0},{0,1},{9,11},{11,13},{13... | collective-permute-start | bytes 1474568 | tf_op jit(solution)/shard_map/ppermute | solution.py:556
  6.5 13.6 %collective-permute-start.8 = (bf16[96,2560]{1,0:T(8,128)(2,1)}, bf16[96,2560]{1,0:T(8,128)(2,1)S(1)}, u32[]{:S(2)}, u32[]{:S(2)}) collective-permute-start(bf16[96,2560]{1,0:T(8,128)(2,1)} %get-tuple-element.107.refs_0_.refs_8_), channel_id=1, source_target_pairs={{1,0},{3,1},{5,3},{7,5},{6,7},{4,6},{2,4},{0,2},{9,8},{11,9},{13,1... | collective-permute-start | bytes 1474568 | tf_op jit(solution)/shard_map/ppermute | solution.py:556
  18.1 14.2 %collective-permute-start.1 = (bf16[96,2560]{1,0:T(8,128)(2,1)S(1)}, bf16[96,2560]{1,0:T(8,128)(2,1)S(1)}, u32[]{:S(2)}, u32[]{:S(2)}) collective-permute-start(bf16[96,2560]{1,0:T(8,128)(2,1)S(1)} %collective-permute-done.refs_1_.refs_9_), channel_id=1, source_target_pairs={{1,3},{3,5},{5,7},{7,6},{6,4},{4,2},{2,0},{0,1},{9,11},{11,13},{13... | collective-permute-start | bytes 1474568 | tf_op jit(solution)/shard_map/ppermute | solution.py:556
  19.7 14.2 %collective-permute-start.23 = (bf16[96,2432]{1,0:T(8,128)(2,1)}, bf16[96,2432]{1,0:T(8,128)(2,1)S(1)}, u32[]{:S(2)}, u32[]{:S(2)}) collective-permute-start(bf16[96,2432]{1,0:T(8,128)(2,1)} %get-tuple-element.89.refs_0_.refs_8_), channel_id=1, source_target_pairs={{1,0},{3,1},{5,3},{7,5},{6,7},{4,6},{2,4},{0,2},{9,8},{11,9},{13,1... | collective-permute-start | bytes 1400840 | tf_op jit(solution)/shard_map/ppermute | solution.py:556
  20.1 24.0 %collective-permute-start.9 = (bf16[96,2560]{1,0:T(8,128)(2,1)S(1)}, bf16[96,2560]{1,0:T(8,128)(2,1)S(1)}, u32[]{:S(2)}, u32[]{:S(2)}) collective-permute-start(bf16[96,2560]{1,0:T(8,128)(2,1)S(1)} %collective-permute-done.8.refs_5_.refs_13_), channel_id=1, source_target_pairs={{1,0},{3,1},{5,3},{7,5},{6,7},{4,6},{2,4},{0,2},{9,8},{11,9},{13,1... | collective-permute-start | bytes 1474568 | tf_op jit(solution)/shard_map/ppermute | solution.py:556
  21.8 22.7 %collective-permute-start.20 = (bf16[96,2432]{1,0:T(8,128)(2,1)}, bf16[96,2432]{1,0:T(8,128)(2,1)S(1)}, u32[]{:S(2)}, u32[]{:S(2)}) collective-permute-start(bf16[96,2432]{1,0:T(8,128)(2,1)} %get-tuple-element.89.refs_0_.refs_8_), channel_id=1, source_target_pairs={{1,3},{3,5},{5,7},{7,6},{6,4},{4,2},{2,0},{0,1},{9,11},{11,13},{13... | collective-permute-start | bytes 1400840 | tf_op jit(solution)/shard_map/ppermute | solution.py:556
  32.2 23.0 %collective-permute-start.2 = (bf16[96,2560]{1,0:T(8,128)(2,1)S(1)}, bf16[96,2560]{1,0:T(8,128)(2,1)S(1)}, u32[]{:S(2)}, u32[]{:S(2)}) collective-permute-start(bf16[96,2560]{1,0:T(8,128)(2,1)S(1)} %collective-permute-done.1.refs_2_.refs_10_), channel_id=1, source_target_pairs={{1,3},{3,5},{5,7},{7,6},{6,4},{4,2},{2,0},{0,1},{9,11},{11,13},{13... | collective-permute-start | bytes 1474568 | tf_op jit(solution)/shard_map/ppermute | solution.py:556
  33.8 20.2 %collective-permute-start.24 = (bf16[96,2432]{1,0:T(8,128)(2,1)S(1)}, bf16[96,2432]{1,0:T(8,128)(2,1)S(1)}, u32[]{:S(2)}, u32[]{:S(2)}) collective-permute-start(bf16[96,2432]{1,0:T(8,128)(2,1)S(1)} %collective-permute-done.23.refs_4_.refs_12_), channel_id=1, source_target_pairs={{1,0},{3,1},{5,3},{7,5},{6,7},{4,6},{2,4},{0,2},{9,8},{11,9},{13,1... | collective-permute-start | bytes 1400840 | tf_op jit(solution)/shard_map/ppermute | solution.py:556
  44.0 20.5 %collective-permute-start.10 = (bf16[96,2560]{1,0:T(8,128)(2,1)S(1)}, bf16[96,2560]{1,0:T(8,128)(2,1)S(1)}, u32[]{:S(2)}, u32[]{:S(2)}) collective-permute-start(bf16[96,2560]{1,0:T(8,128)(2,1)S(1)} %collective-permute-done.9.refs_6_.refs_14_), channel_id=1, source_target_pairs={{1,0},{3,1},{5,3},{7,5},{6,7},{4,6},{2,4},{0,2},{9,8},{11,9},{13,1... | collective-permute-start | bytes 1474568 | tf_op jit(solution)/shard_map/ppermute | solution.py:556
  44.5 20.5 %collective-permute-start.21 = (bf16[96,2432]{1,0:T(8,128)(2,1)S(1)}, bf16[96,2432]{1,0:T(8,128)(2,1)S(1)}, u32[]{:S(2)}, u32[]{:S(2)}) collective-permute-start(bf16[96,2432]{1,0:T(8,128)(2,1)S(1)} %collective-permute-done.20.refs_1_.refs_9_), channel_id=1, source_target_pairs={{1,3},{3,5},{5,7},{7,6},{6,4},{4,2},{2,0},{0,1},{9,11},{11,13},{13... | collective-permute-start | bytes 1400840 | tf_op jit(solution)/shard_map/ppermute | solution.py:556
  54.1 20.5 %collective-permute-start.25 = (bf16[96,2432]{1,0:T(8,128)(2,1)S(1)}, bf16[96,2432]{1,0:T(8,128)(2,1)S(1)}, u32[]{:S(2)}, u32[]{:S(2)}) collective-permute-start(bf16[96,2432]{1,0:T(8,128)(2,1)S(1)} %collective-permute-done.24.refs_5_.refs_13_), channel_id=1, source_target_pairs={{1,0},{3,1},{5,3},{7,5},{6,7},{4,6},{2,4},{0,2},{9,8},{11,9},{13,1... | collective-permute-start | bytes 1400840 | tf_op jit(solution)/shard_map/ppermute | solution.py:556
  55.2 19.8 %collective-permute-start.3 = (bf16[96,2432]{1,0:T(8,128)(2,1)S(1)}, bf16[96,2432]{1,0:T(8,128)(2,1)S(1)}, u32[]{:S(2)}, u32[]{:S(2)}) collective-permute-start(bf16[96,2432]{1,0:T(8,128)(2,1)S(1)} %get-tuple-element.80.refs_0_.refs_8_), channel_id=1, source_target_pairs={{1,3},{3,5},{5,7},{7,6},{6,4},{4,2},{2,0},{0,1},{9,11},{11,13},{13... | collective-permute-start | bytes 1400840 | tf_op jit(solution)/shard_map/ppermute | solution.py:556
  64.6 20.0 %collective-permute-start.11 = (bf16[96,2432]{1,0:T(8,128)(2,1)S(1)}, bf16[96,2432]{1,0:T(8,128)(2,1)S(1)}, u32[]{:S(2)}, u32[]{:S(2)}) collective-permute-start(bf16[96,2432]{1,0:T(8,128)(2,1)S(1)} %get-tuple-element.80.refs_0_.refs_8_), channel_id=1, source_target_pairs={{1,0},{3,1},{5,3},{7,5},{6,7},{4,6},{2,4},{0,2},{9,8},{11,9},{13,1... | collective-permute-start | bytes 1400840 | tf_op jit(solution)/shard_map/ppermute | solution.py:556
  65.0 20.0 %collective-permute-start.22 = (bf16[96,2432]{1,0:T(8,128)(2,1)S(1)}, bf16[96,2432]{1,0:T(8,128)(2,1)S(1)}, u32[]{:S(2)}, u32[]{:S(2)}) collective-permute-start(bf16[96,2432]{1,0:T(8,128)(2,1)S(1)} %collective-permute-done.21.refs_2_.refs_10_), channel_id=1, source_target_pairs={{1,3},{3,5},{5,7},{7,6},{6,4},{4,2},{2,0},{0,1},{9,11},{11,13},{13... | collective-permute-start | bytes 1400840 | tf_op jit(solution)/shard_map/ppermute | solution.py:556
  66.6 28.0 %collective-permute-start.27 = (bf16[96,2560]{1,0:T(8,128)(2,1)S(1)}, bf16[96,2560]{1,0:T(8,128)(2,1)S(1)}, u32[]{:S(2)}, u32[]{:S(2)}) collective-permute-start(bf16[96,2560]{1,0:T(8,128)(2,1)S(1)} %collective-permute-done.2.refs_3_.refs_11_), channel_id=1, source_target_pairs={{1,3},{3,5},{5,7},{7,6},{6,4},{4,2},{2,0},{0,1},{9,11},{11,13},{13... | collective-permute-start | bytes 1474568 | tf_op jit(solution)/shard_map/ppermute | solution.py:556
  74.6 20.0 %collective-permute-start.26 = (bf16[96,2432]{1,0:T(8,128)(2,1)S(1)}, bf16[96,2432]{1,0:T(8,128)(2,1)S(1)}, u32[]{:S(2)}, u32[]{:S(2)}) collective-permute-start(bf16[96,2432]{1,0:T(8,128)(2,1)S(1)} %collective-permute-done.25.refs_6_.refs_14_), channel_id=1, source_target_pairs={{1,0},{3,1},{5,3},{7,5},{6,7},{4,6},{2,4},{0,2},{9,8},{11,9},{13,1... | collective-permute-start | bytes 1400840 | tf_op jit(solution)/shard_map/ppermute | solution.py:556
  75.0 26.6 %collective-permute-start.4 = (bf16[96,2432]{1,0:T(8,128)(2,1)S(1)}, bf16[96,2432]{1,0:T(8,128)(2,1)S(1)}, u32[]{:S(2)}, u32[]{:S(2)}) collective-permute-start(bf16[96,2432]{1,0:T(8,128)(2,1)S(1)} %collective-permute-done.3.refs_1_.refs_9_), channel_id=1, source_target_pairs={{1,3},{3,5},{5,7},{7,6},{6,4},{4,2},{2,0},{0,1},{9,11},{11,13},{13... | collective-permute-start | bytes 1400840 | tf_op jit(solution)/shard_map/ppermute | solution.py:556
  84.6 20.0 %collective-permute-start.18 = (bf16[96,2432]{1,0:T(8,128)(2,1)S(1)}, bf16[96,2432]{1,0:T(8,128)(2,1)S(1)}, u32[]{:S(2)}, u32[]{:S(2)}) collective-permute-start(bf16[96,2432]{1,0:T(8,128)(2,1)S(1)} %collective-permute-done.11.refs_5_.refs_13_), channel_id=1, source_target_pairs={{1,0},{3,1},{5,3},{7,5},{6,7},{4,6},{2,4},{0,2},{9,8},{11,9},{13,1... | collective-permute-start | bytes 1400840 | tf_op jit(solution)/shard_map/ppermute | solution.py:556
  85.0 29.6 %collective-permute-start.12 = (bf16[96,2432]{1,0:T(8,128)(2,1)S(1)}, bf16[96,2432]{1,0:T(8,128)(2,1)S(1)}, u32[]{:S(2)}, u32[]{:S(2)}) collective-permute-start(bf16[96,2432]{1,0:T(8,128)(2,1)S(1)} %get-tuple-element.76.refs_0_), channel_id=1, source_target_pairs={{1,0},{3,1},{5,3},{7,5},{6,7},{4,6},{2,4},{0,2},{9,8},{11,9},{13,1... | collective-permute-start | bytes 1400840 | tf_op jit(solution)/shard_map/ppermute | solution.py:556
  94.7 38.3 %copy-start.2 = (bf16[96,2432]{1,0:T(8,128)(2,1)S(1)}, bf16[96,2432]{1,0:T(8,128)(2,1)}, u32[]{:S(2)}) copy-start(bf16[96,2432]{1,0:T(8,128)(2,1)} %get-tuple-element.89.refs_0_.refs_8_) | copy-start | bytes 1400836
  94.7 11.4 %collective-permute-start.28 = (bf16[8,96,128]{2,1,0:T(8,128)(2,1)S(1)}, bf16[8,96,128]{2,1,0:T(8,128)(2,1)S(1)}, u32[]{:S(2)}, u32[]{:S(2)}) collective-permute-start(bf16[8,96,128]{2,1,0:T(8,128)(2,1)S(1)} %collect.1.refs_19_), channel_id=1, source_target_pairs={{0,24},{1,25},{2,26},{3,27},{4,28},{5,29},{6,30},{7,31}} | collective-permute-start | bytes 589832 | tf_op jit(solution)/shard_map/ppermute | solution.py:590
  96.2 11.6 %collective-permute-start.29 = (bf16[8,96,128]{2,1,0:T(8,128)(2,1)S(1)}, bf16[8,96,128]{2,1,0:T(8,128)(2,1)S(1)}, u32[]{:S(2)}, u32[]{:S(2)}) collective-permute-start(bf16[8,96,128]{2,1,0:T(8,128)(2,1)S(1)} %collect.1.refs_19_), channel_id=1, source_target_pairs={{8,24},{9,25},{10,26},{11,27},{12,28},{13,29},{14,30},{15,31}} | collective-permute-start | bytes 589832 | tf_op jit(solution)/shard_map/ppermute | solution.py:590
  101.6 13.5 %collective-permute-start.30 = (bf16[8,96,128]{2,1,0:T(8,128)(2,1)S(1)}, bf16[8,96,128]{2,1,0:T(8,128)(2,1)S(1)}, u32[]{:S(2)}, u32[]{:S(2)}) collective-permute-start(bf16[8,96,128]{2,1,0:T(8,128)(2,1)S(1)} %collect.1.refs_19_), channel_id=1, source_target_pairs={{16,24},{17,25},{18,26},{19,27},{20,28},{21,29},{22,30},{23,31}} | collective-permute-start | bytes 589832 | tf_op jit(solution)/shard_map/ppermute | solution.py:590
  104.6 19.4 %collective-permute-start.16 = (bf16[96,2432]{1,0:T(8,128)(2,1)S(1)}, bf16[96,2432]{1,0:T(8,128)(2,1)S(1)}, u32[]{:S(2)}, u32[]{:S(2)}) collective-permute-start(bf16[96,2432]{1,0:T(8,128)(2,1)S(1)} %collective-permute-done.4.refs_2_.refs_10_), channel_id=1, source_target_pairs={{1,3},{3,5},{5,7},{7,6},{6,4},{4,2},{2,0},{0,1},{9,11},{11,13},{13... | collective-permute-start | bytes 1400840 | tf_op jit(solution)/shard_map/ppermute | solution.py:556
  106.2 20.0 %collective-permute-start.5 = (bf16[96,2432]{1,0:T(8,128)(2,1)S(1)}, bf16[96,2432]{1,0:T(8,128)(2,1)S(1)}, u32[]{:S(2)}, u32[]{:S(2)}) collective-permute-start(bf16[96,2432]{1,0:T(8,128)(2,1)S(1)} %get-tuple-element.76.refs_0_), channel_id=1, source_target_pairs={{1,3},{3,5},{5,7},{7,6},{6,4},{4,2},{2,0},{0,1},{9,11},{11,13},{13... | collective-permute-start | bytes 1400840 | tf_op jit(solution)/shard_map/ppermute | solution.py:556
  107.8 16.9 %collective-permute-start.19 = (bf16[96,2432]{1,0:T(8,128)(2,1)S(1)}, bf16[96,2432]{1,0:T(8,128)(2,1)S(1)}, u32[]{:S(2)}, u32[]{:S(2)}) collective-permute-start(bf16[96,2432]{1,0:T(8,128)(2,1)S(1)} %collective-permute-done.18.refs_6_.refs_14_), channel_id=1, source_target_pairs={{1,0},{3,1},{5,3},{7,5},{6,7},{4,6},{2,4},{0,2},{9,8},{11,9},{13,1... | collective-permute-start | bytes 1400840 | tf_op jit(solution)/shard_map/ppermute | solution.py:556
  114.6 17.7 %collective-permute-start.13 = (bf16[96,2432]{1,0:T(8,128)(2,1)S(1)}, bf16[96,2432]{1,0:T(8,128)(2,1)S(1)}, u32[]{:S(2)}, u32[]{:S(2)}) collective-permute-start(bf16[96,2432]{1,0:T(8,128)(2,1)S(1)} %collective-permute-done.12.refs_4_), channel_id=1, source_target_pairs={{1,0},{3,1},{5,3},{7,5},{6,7},{4,6},{2,4},{0,2},{9,8},{11,9},{13,1... | collective-permute-start | bytes 1400840 | tf_op jit(solution)/shard_map/ppermute | solution.py:556
  124.6 17.3 %collective-permute-start.17 = (bf16[96,2432]{1,0:T(8,128)(2,1)S(1)}, bf16[96,2432]{1,0:T(8,128)(2,1)S(1)}, u32[]{:S(2)}, u32[]{:S(2)}) collective-permute-start(bf16[96,2432]{1,0:T(8,128)(2,1)S(1)} %collective-permute-done.16.refs_3_.refs_11_), channel_id=1, source_target_pairs={{1,3},{3,5},{5,7},{7,6},{6,4},{4,2},{2,0},{0,1},{9,11},{11,13},{13... | collective-permute-start | bytes 1400840 | tf_op jit(solution)/shard_map/ppermute | solution.py:556
  126.2 17.9 %collective-permute-start.6 = (bf16[96,2432]{1,0:T(8,128)(2,1)S(1)}, bf16[96,2432]{1,0:T(8,128)(2,1)S(1)}, u32[]{:S(2)}, u32[]{:S(2)}) collective-permute-start(bf16[96,2432]{1,0:T(8,128)(2,1)S(1)} %collective-permute-done.5.refs_1_), channel_id=1, source_target_pairs={{1,3},{3,5},{5,7},{7,6},{6,4},{4,2},{2,0},{0,1},{9,11},{11,13},{13... | collective-permute-start | bytes 1400840 | tf_op jit(solution)/shard_map/ppermute | solution.py:556
  132.3 11.8 %collective-permute-start.14 = (bf16[96,2432]{1,0:T(8,128)(2,1)S(1)}, bf16[96,2432]{1,0:T(8,128)(2,1)S(1)}, u32[]{:S(2)}, u32[]{:S(2)}) collective-permute-start(bf16[96,2432]{1,0:T(8,128)(2,1)S(1)} %collective-permute-done.13.refs_5_), channel_id=1, source_target_pairs={{1,0},{3,1},{5,3},{7,5},{6,7},{4,6},{2,4},{0,2},{9,8},{11,9},{13,1... | collective-permute-start | bytes 1400840 | tf_op jit(solution)/shard_map/ppermute | solution.py:556
  144.1 10.9 %collective-permute-start.7 = (bf16[96,2432]{1,0:T(8,128)(2,1)S(1)}, bf16[96,2432]{1,0:T(8,128)(2,1)S(1)}, u32[]{:S(2)}, u32[]{:S(2)}) collective-permute-start(bf16[96,2432]{1,0:T(8,128)(2,1)S(1)} %collective-permute-done.6.refs_2_), channel_id=1, source_target_pairs={{1,3},{3,5},{5,7},{7,6},{6,4},{4,2},{2,0},{0,1},{9,11},{11,13},{13... | collective-permute-start | bytes 1400840 | tf_op jit(solution)/shard_map/ppermute | solution.py:556
  144.8 10.3 %collective-permute-start.15 = (bf16[96,2432]{1,0:T(8,128)(2,1)S(1)}, bf16[96,2432]{1,0:T(8,128)(2,1)S(1)}, u32[]{:S(2)}, u32[]{:S(2)}) collective-permute-start(bf16[96,2432]{1,0:T(8,128)(2,1)S(1)} %collective-permute-done.14.refs_6_), channel_id=1, source_target_pairs={{1,0},{3,1},{5,3},{7,5},{6,7},{4,6},{2,4},{0,2},{9,8},{11,9},{13,1... | collective-permute-start | bytes 1400840 | tf_op jit(solution)/shard_map/ppermute | solution.py:556
  160.4 3.3 %collective-permute-start.31 = (bf16[6,256,256]{2,1,0:T(8,128)(2,1)S(1)}, bf16[6,256,256]{2,1,0:T(8,128)(2,1)S(1)}, u32[]{:S(2)}, u32[]{:S(2)}) collective-permute-start(bf16[6,256,256]{2,1,0:T(8,128)(2,1)S(1)} %fold.1), channel_id=1, source_target_pairs={{24,16},{25,17},{26,18},{27,19},{28,20},{29,21},{30,22},{31,23}} | collective-permute-start | bytes 2359304 | tf_op jit(solution)/shard_map/ppermute | solution.py:606
  165.5 0.7 collective-permute-start.32
  168.0 16.2 %collective-permute-start.33 = (bf16[6,256,256]{2,1,0:T(8,128)(2,1)S(1)}, bf16[6,256,256]{2,1,0:T(8,128)(2,1)S(1)}, u32[]{:S(2)}, u32[]{:S(2)}) collective-permute-start(bf16[6,256,256]{2,1,0:T(8,128)(2,1)S(1)} %hop.3), channel_id=1, source_target_pairs={{8,0},{9,1},{10,2},{11,3},{12,4},{13,5},{14,6},{15,7}} | collective-permute-start | bytes 2359304 | tf_op jit(solution)/shard_map/ppermute | solution.py:606

commit v15 on v14

--- a/solution.py
+++ b/solution.py
@@ -72,7 +72,7 @@
 
 def pack(place, block, gains, increments, terminal, count, ranges):
     rows, width = gains.shape[1:]
-    first, size = ranges[1][0], ranges[0][1] - ranges[1][0]
+    first, size = ranges[-1][0], ranges[0][1] - ranges[-1][0]
     ends = [] if terminal is None else [terminal]
     lanes = [(high - low) * (width + width // 2) + LANES for low, high in ranges]
     lanes[0] += LANES * len(ends)
@@ -86,7 +86,7 @@
             out_specs=[pl.BlockSpec((rows, n), lambda i, *p: (0, 0)) for n in lanes],
         ),
         out_shape=[jax.ShapeDtypeStruct((rows, n), BF16) for n in lanes],
-        compiler_params=pltpu.CompilerParams(vmem_limit_bytes=CLAIM if ends else 14 * MIB),
+        compiler_params=pltpu.CompilerParams(vmem_limit_bytes=CLAIM if len(ranges) == 1 else 14 * MIB),
         name="pack",
     )(place, block, gains, increments, *ends)
 
@@ -275,8 +275,8 @@
     count = len(cycle)
     places = origins(place_ref[0], cycle, right)
     blocks, refs = refs[:count], refs[count:]
-    half_in, refs = refs[0], refs[-9:]
-    gain_out, half_out, half, middle, raw, extras, gain, fresh, spare = refs
+    half_in, refs = refs[0], refs[-10:]
+    gain_out, half_out, packed_out, half, middle, raw, extras, gain, fresh, spare = refs
     gains, freshes = (gain, spare.at[0]), (fresh, spare.at[1])
     rows, width = blocks[0].shape[0], half.shape[0]
     stride = width * 3 // 2
@@ -301,6 +301,8 @@
                 prepare(turn + 1)
             advance(gains[turn % 2], half, freshes[turn % 2], middle)
             half_out[0] = half[...]
+            if turn == turns - 1:
+                fold(half, packed_out)
 
 
 def chain(place, cycle, right, blocks, half, turns):
@@ -315,7 +317,7 @@
             num_scalar_prefetch=1,
             grid=(turns,),
             in_specs=in_specs + [square(width)],
-            out_specs=[whole, whole],
+            out_specs=[whole, whole, pl.BlockSpec(blocks_shape(width), lambda i, *p: (0, 0, 0))],
             scratch_shapes=[
                 pltpu.VMEM((width, width), BF16),
                 pltpu.VMEM((width, width), BF16),
@@ -326,7 +328,8 @@
                 pltpu.VMEM((2, width, width), BF16),
             ],
         ),
-        out_shape=[jax.ShapeDtypeStruct((turns, width, width), BF16)] * 2,
+        out_shape=[jax.ShapeDtypeStruct((turns, width, width), BF16)] * 2
+        + [jax.ShapeDtypeStruct(blocks_shape(width), BF16)],
         compiler_params=pltpu.CompilerParams(vmem_limit_bytes=18 * MIB),
         cost_estimate=pl.CostEstimate(
             flops=4 * turns * width**3, bytes_accessed=8 * turns * width * width, transcendentals=0
@@ -408,6 +411,10 @@
     return [(a, b) for a in range(0, width, TILE) for b in range(a, width, TILE)]
 
 
+def blocks_shape(width):
+    return (len(upper_blocks(width)), TILE, TILE)
+
+
 def identity(size):
     row = lax.broadcasted_iota(jnp.int32, (size, size), 0)
     column = lax.broadcasted_iota(jnp.int32, (size, size), 1)
@@ -428,10 +435,6 @@
     for extra in refs[1:]:
         value = value + extra[n]
     return value
-
-
-def fold_kernel(half_ref, packed_ref):
-    fold(half_ref.at[0], packed_ref)
 
 
 def hop_kernel(arrived, factor_ref, half_ref, *refs):
@@ -452,19 +455,9 @@
 
 def hop(factors, halves, packed):
     width = halves.shape[1]
-    shape = (len(upper_blocks(width)), TILE, TILE)
+    shape = blocks_shape(width)
     blocks = pl.BlockSpec(shape, lambda i: (0, 0, 0), pipeline_mode=pl.Buffered(1))
     whole = pl.BlockSpec((1, width, width), lambda i: (0, 0, 0), pipeline_mode=pl.Buffered(1))
-    if not packed:
-        return pl.pallas_call(
-            fold_kernel,
-            grid=(1,),
-            in_specs=[whole],
-            out_specs=blocks,
-            out_shape=jax.ShapeDtypeStruct(shape, BF16),
-            compiler_params=pltpu.CompilerParams(vmem_limit_bytes=8 * MIB),
-            name="fold",
-        )(halves)
     return pl.pallas_call(
         functools.partial(hop_kernel, len(packed)),
         grid=(1,),
@@ -556,9 +549,12 @@
         return lax.ppermute(array, "tile", [(cycle[n], cycle[(n + way) % count]) for n in range(count)])
 
     ranges = pieces(steps)
-    own = list(pack(place, block, gains, increments, terminal, count, ranges[:2]))
-    own += pack(place, block, gains, increments, None, count, ranges[2:])
-    own[:2], last = lax.optimization_barrier((own[:2], last))
+    own = [
+        *pack(place, block, gains, increments, terminal, count, ranges[:1]),
+        *pack(place, block, gains, increments, None, count, ranges[1:2]),
+        *pack(place, block, gains, increments, None, count, ranges[2:]),
+    ]
+    own[1], last = lax.optimization_barrier((own[1], last))
     rights = [count // 2 - turn % 2 for turn in range(len(own))]
     found = []
     for turn, array in enumerate(own):
@@ -566,7 +562,7 @@
         for way, hops in ((1, rights[turn]), (-1, count - 1 - rights[turn])):
             source = array
             if turn > 1:
-                before = found[0 if turn == 2 else turn - 1][way]
+                before = found[turn - 1][way]
                 gate = count // 2 - 1 if turn == 2 else len(before) - 3
                 source, before[gate] = lax.optimization_barrier((source, before[gate]))
                 for n in range(gate + 1, len(before)):
@@ -603,7 +599,8 @@
     own = own_rows(place, early[1], own)
     packed = []
     for turn in range(blocks - 1, 0, -1):
-        packed.append(lax.ppermute(hop(factors, early[1], packed), "tm", [(turn, turn - 1)]))
+        before = hop(factors, early[1], packed) if packed else early[2]
+        packed.append(lax.ppermute(before, "tm", [(turn, turn - 1)]))
     return finish(factors, own, mine, packed)
 
 

time: 190 us -> 188 us (0.989)
  waiting for transfers between devices: 104 us -> 96.4 us
  starting transfers between devices: 36.6 us -> 41 us
    ppermute x28, waiting for transfers between devices: 90.2 us -> 81.3 us  [passed(): lax.ppermute(array, 'tile', [(cycle[n], cycle[(n + way) % count]) for n i...]
    ppermute x28, starting transfers between devices: 30.9 us -> 35.3 us  [passed(): lax.ppermute(array, 'tile', [(cycle[n], cycle[(n + way) % count]) for n i...]
    pallas_call x2 -> x3, Pallas kernels: 4.25 us -> 5.57 us  [pack(): pl.pallas_call(functools.partial(pack_kernel, count, ranges), grid_spec=p...]
  transfers between devices with their start and end apart: 34 -> 34, of which waited for: 15 -> 18; matrix products, arithmetic and copies ran while one was open for 0% -> 0% of each run, Pallas kernels for 16% -> 18%
where the time goes in v15:
time: 188 us
  waiting for transfers between devices  96.4 us (51%)
  Pallas kernels  50.2 us (27%)
  starting transfers between devices  41 us (22%)
    ppermute x28, waiting for transfers between devices, passed(): lax.ppermute(array, 'tile', [(cycle[n], cycle[(n + way) % count]) for n i...  81.3 us
    ppermute x28, starting transfers between devices, passed(): lax.ppermute(array, 'tile', [(cycle[n], cycle[(n + way) % count]) for n i...  35.3 us
    pallas_call x3, Pallas kernels, compose(): pl.pallas_call(functools.partial(compose_kernel, cycle, right, first), gr...  26.9 us
    ppermute x3, waiting for transfers between devices, local(): packed.append(lax.ppermute(before, 'tm', [(turn, turn - 1)]))  15.1 us
    pallas_call x3, Pallas kernels, pack(): pl.pallas_call(functools.partial(pack_kernel, count, ranges), grid_spec=p...  5.57 us
    pallas_call x1, Pallas kernels, finish(): pl.pallas_call(functools.partial(finish_kernel, len(packed)), grid=(steps...  5.57 us
    pallas_call x1, Pallas kernels, chain(): pl.pallas_call(functools.partial(chain_kernel, cycle, right, turns), grid...  5.07 us
  transfers between devices with their start and end apart: 34, of which 18 were waited for; matrix products, arithmetic and copies ran while one was open for 0% of the time, Pallas kernels for 18%

profile of v15, /device:TPU:0, one launch (start us, length us, event | category | flops | bytes accessed | tf_op | source)
XLA Modules:
  0.0 187.8 jit_solution(2958152577621592604)
XLA Ops:
  0.0 2.3 %pack.4.refs_0_.refs_8_ = bf16[96,2432]{1,0:T(8,128)(2,1)} custom-call(s32[1]{0:T(128)} %bitcast.place_ref, s32[1]{0:T(128)} %bitcast.1.block_ref, bf16[8,96,768]{2,1,0:T(8,128)(2,1)} %gain_ref.5, f32[8,96,768]{2,1,0:T(8,128)} %increment_ref.5), custom_call_target="tpu_custom_call" | custom-call | tf_op jit(solution)/shard_map/pack/pallas_call | solution.py:80
  2.3 3.0 %collective-permute-start = (bf16[96,2432]{1,0:T(8,128)(2,1)}, bf16[96,2432]{1,0:T(8,128)(2,1)S(1)}, u32[]{:S(2)}, u32[]{:S(2)}) collective-permute-start(bf16[96,2432]{1,0:T(8,128)(2,1)} %pack.4.refs_0_.refs_8_), channel_id=1, source_target_pairs={{1,3},{3,5},{5,7},{7,6},{6,4},{4,2},{2,0},{0,1},{9,11},{11,13},{13... | collective-permute-start | bytes 1400840 | tf_op jit(solution)/shard_map/ppermute | solution.py:549
  5.3 2.6 %pack.5.refs_0_.refs_8_ = bf16[96,2560]{1,0:T(8,128)(2,1)} custom-call(s32[1]{0:T(128)} %bitcast.place_ref, s32[1]{0:T(128)} %bitcast.1.block_ref, bf16[8,96,768]{2,1,0:T(8,128)(2,1)} %gain_ref.5, f32[8,96,768]{2,1,0:T(8,128)} %increment_ref.5, f32[96,768]{1,0:T(8,128)} %refs_0_.1), custom_call_target="tpu_custom_call" | custom-call | tf_op jit(solution)/shard_map/pack/pallas_call | solution.py:80
  7.9 1.9 %collective-permute-start.21 = (bf16[96,2560]{1,0:T(8,128)(2,1)}, bf16[96,2560]{1,0:T(8,128)(2,1)S(1)}, u32[]{:S(2)}, u32[]{:S(2)}) collective-permute-start(bf16[96,2560]{1,0:T(8,128)(2,1)} %pack.5.refs_0_.refs_8_), channel_id=1, source_target_pairs={{1,3},{3,5},{5,7},{7,6},{6,4},{4,2},{2,0},{0,1},{9,11},{11,13},{13... | collective-permute-start | bytes 1474568 | tf_op jit(solution)/shard_map/ppermute | solution.py:549
  9.9 7.2 %collective-permute-done.refs_1_.refs_9_ = bf16[96,2432]{1,0:T(8,128)(2,1)S(1)} collective-permute-done((bf16[96,2432]{1,0:T(8,128)(2,1)}, bf16[96,2432]{1,0:T(8,128)(2,1)S(1)}, u32[]{:S(2)}, u32[]{:S(2)}) %collective-permute-start) | collective-permute-done | bytes 466976 | tf_op jit(solution)/shard_map/ppermute | solution.py:549
  17.0 2.0 %collective-permute-start.1 = (bf16[96,2432]{1,0:T(8,128)(2,1)S(1)}, bf16[96,2432]{1,0:T(8,128)(2,1)S(1)}, u32[]{:S(2)}, u32[]{:S(2)}) collective-permute-start(bf16[96,2432]{1,0:T(8,128)(2,1)S(1)} %collective-permute-done.refs_1_.refs_9_), channel_id=1, source_target_pairs={{1,3},{3,5},{5,7},{7,6},{6,4},{4,2},{2,0},{0,1},{9,11},{11,13},{13... | collective-permute-start | bytes 1400840 | tf_op jit(solution)/shard_map/ppermute | solution.py:549
  19.1 2.0 %collective-permute-start.9 = (bf16[96,2432]{1,0:T(8,128)(2,1)}, bf16[96,2432]{1,0:T(8,128)(2,1)S(1)}, u32[]{:S(2)}, u32[]{:S(2)}) collective-permute-start(bf16[96,2432]{1,0:T(8,128)(2,1)} %collective-permute-done.8.refs_4_.refs_12_), channel_id=1, source_target_pairs={{1,0},{3,1},{5,3},{7,5},{6,7},{4,6},{2,4},{0,2},{9,8},{11,9},{13,1... | collective-permute-start | bytes 1400840 | tf_op jit(solution)/shard_map/ppermute | solution.py:549
  21.1 6.4 %collective-permute-done.21.refs_1_.refs_9_ = bf16[96,2560]{1,0:T(8,128)(2,1)S(1)} collective-permute-done((bf16[96,2560]{1,0:T(8,128)(2,1)}, bf16[96,2560]{1,0:T(8,128)(2,1)S(1)}, u32[]{:S(2)}, u32[]{:S(2)}) %collective-permute-start.21) | collective-permute-done | bytes 491552 | tf_op jit(solution)/shard_map/ppermute | solution.py:549
  27.6 2.0 %collective-permute-start.22 = (bf16[96,2560]{1,0:T(8,128)(2,1)S(1)}, bf16[96,2560]{1,0:T(8,128)(2,1)S(1)}, u32[]{:S(2)}, u32[]{:S(2)}) collective-permute-start(bf16[96,2560]{1,0:T(8,128)(2,1)S(1)} %collective-permute-done.21.refs_1_.refs_9_), channel_id=1, source_target_pairs={{1,3},{3,5},{5,7},{7,6},{6,4},{4,2},{2,0},{0,1},{9,11},{11,13},{13... | collective-permute-start | bytes 1474568 | tf_op jit(solution)/shard_map/ppermute | solution.py:549
  29.6 8.0 %collective-permute-done.1.refs_2_.refs_10_ = bf16[96,2432]{1,0:T(8,128)(2,1)S(1)} collective-permute-done((bf16[96,2432]{1,0:T(8,128)(2,1)S(1)}, bf16[96,2432]{1,0:T(8,128)(2,1)S(1)}, u32[]{:S(2)}, u32[]{:S(2)}) %collective-permute-start.1) | collective-permute-done | bytes 466976 | tf_op jit(solution)/shard_map/ppermute | solution.py:549
  37.6 2.0 %collective-permute-start.2 = (bf16[96,2432]{1,0:T(8,128)(2,1)S(1)}, bf16[96,2432]{1,0:T(8,128)(2,1)S(1)}, u32[]{:S(2)}, u32[]{:S(2)}) collective-permute-start(bf16[96,2432]{1,0:T(8,128)(2,1)S(1)} %collective-permute-done.1.refs_2_.refs_10_), channel_id=1, source_target_pairs={{1,3},{3,5},{5,7},{7,6},{6,4},{4,2},{2,0},{0,1},{9,11},{11,13},{13... | collective-permute-start | bytes 1400840 | tf_op jit(solution)/shard_map/ppermute | solution.py:549
  40.3 1.4 collective-permute-start.10
  41.7 6.4 %collective-permute-done.22.refs_2_.refs_10_ = bf16[96,2560]{1,0:T(8,128)(2,1)S(1)} collective-permute-done((bf16[96,2560]{1,0:T(8,128)(2,1)S(1)}, bf16[96,2560]{1,0:T(8,128)(2,1)S(1)}, u32[]{:S(2)}, u32[]{:S(2)}) %collective-permute-start.22) | collective-permute-done | bytes 491552 | tf_op jit(solution)/shard_map/ppermute | solution.py:549
  48.1 2.0 %collective-permute-start.23 = (bf16[96,2560]{1,0:T(8,128)(2,1)S(1)}, bf16[96,2560]{1,0:T(8,128)(2,1)S(1)}, u32[]{:S(2)}, u32[]{:S(2)}) collective-permute-start(bf16[96,2560]{1,0:T(8,128)(2,1)S(1)} %collective-permute-done.22.refs_2_.refs_10_), channel_id=1, source_target_pairs={{1,3},{3,5},{5,7},{7,6},{6,4},{4,2},{2,0},{0,1},{9,11},{11,13},{13... | collective-permute-start | bytes 1474568 | tf_op jit(solution)/shard_map/ppermute | solution.py:549
  50.1 0.7 pack.3
  50.8 7.3 %collective-permute-done.2.refs_3_.refs_11_ = bf16[96,2432]{1,0:T(8,128)(2,1)S(1)} collective-permute-done((bf16[96,2432]{1,0:T(8,128)(2,1)S(1)}, bf16[96,2432]{1,0:T(8,128)(2,1)S(1)}, u32[]{:S(2)}, u32[]{:S(2)}) %collective-permute-start.2) | collective-permute-done | bytes 466976 | tf_op jit(solution)/shard_map/ppermute | solution.py:549
  58.1 2.0 %collective-permute-start.3 = (bf16[96,2432]{1,0:T(8,128)(2,1)S(1)}, bf16[96,2432]{1,0:T(8,128)(2,1)S(1)}, u32[]{:S(2)}, u32[]{:S(2)}) collective-permute-start(bf16[96,2432]{1,0:T(8,128)(2,1)S(1)} %get-tuple-element.76.refs_0_.refs_8_), channel_id=1, source_target_pairs={{1,3},{3,5},{5,7},{7,6},{6,4},{4,2},{2,0},{0,1},{9,11},{11,13},{13... | collective-permute-start | bytes 1400840 | tf_op jit(solution)/shard_map/ppermute | solution.py:549
  60.8 1.4 collective-permute-start.11
  62.2 6.4 %collective-permute-done.23.refs_3_.refs_11_ = bf16[96,2560]{1,0:T(8,128)(2,1)S(1)} collective-permute-done((bf16[96,2560]{1,0:T(8,128)(2,1)S(1)}, bf16[96,2560]{1,0:T(8,128)(2,1)S(1)}, u32[]{:S(2)}, u32[]{:S(2)}) %collective-permute-start.23) | collective-permute-done | bytes 491552 | tf_op jit(solution)/shard_map/ppermute | solution.py:549
  68.6 2.0 %collective-permute-start.24 = (bf16[96,2560]{1,0:T(8,128)(2,1)S(1)}, bf16[96,2560]{1,0:T(8,128)(2,1)S(1)}, u32[]{:S(2)}, u32[]{:S(2)}) collective-permute-start(bf16[96,2560]{1,0:T(8,128)(2,1)S(1)} %collective-permute-done.23.refs_3_.refs_11_), channel_id=1, source_target_pairs={{1,3},{3,5},{5,7},{7,6},{6,4},{4,2},{2,0},{0,1},{9,11},{11,13},{13... | collective-permute-start | bytes 1474568 | tf_op jit(solution)/shard_map/ppermute | solution.py:549
  70.7 7.9 %collective-permute-done.3.refs_1_.refs_9_ = bf16[96,2432]{1,0:T(8,128)(2,1)S(1)} collective-permute-done((bf16[96,2432]{1,0:T(8,128)(2,1)S(1)}, bf16[96,2432]{1,0:T(8,128)(2,1)S(1)}, u32[]{:S(2)}, u32[]{:S(2)}) %collective-permute-start.3) | collective-permute-done | bytes 466976 | tf_op jit(solution)/shard_map/ppermute | solution.py:549
  78.6 2.0 %collective-permute-start.4 = (bf16[96,2432]{1,0:T(8,128)(2,1)S(1)}, bf16[96,2432]{1,0:T(8,128)(2,1)S(1)}, u32[]{:S(2)}, u32[]{:S(2)}) collective-permute-start(bf16[96,2432]{1,0:T(8,128)(2,1)S(1)} %collective-permute-done.3.refs_1_.refs_9_), channel_id=1, source_target_pairs={{1,3},{3,5},{5,7},{7,6},{6,4},{4,2},{2,0},{0,1},{9,11},{11,13},{13... | collective-permute-start | bytes 1400840 | tf_op jit(solution)/shard_map/ppermute | solution.py:549
  80.6 3.6 %collective-permute-done.11.refs_5_.refs_13_ = bf16[96,2432]{1,0:T(8,128)(2,1)S(1)} collective-permute-done((bf16[96,2432]{1,0:T(8,128)(2,1)S(1)}, bf16[96,2432]{1,0:T(8,128)(2,1)S(1)}, u32[]{:S(2)}, u32[]{:S(2)}) %collective-permute-start.11) | collective-permute-done | bytes 466976 | tf_op jit(solution)/shard_map/ppermute | solution.py:549
  84.3 2.0 %collective-permute-start.12 = (bf16[96,2432]{1,0:T(8,128)(2,1)S(1)}, bf16[96,2432]{1,0:T(8,128)(2,1)S(1)}, u32[]{:S(2)}, u32[]{:S(2)}) collective-permute-start(bf16[96,2432]{1,0:T(8,128)(2,1)S(1)} %get-tuple-element.72.refs_0_), channel_id=1, source_target_pairs={{1,0},{3,1},{5,3},{7,5},{6,7},{4,6},{2,4},{0,2},{9,8},{11,9},{13,1... | collective-permute-start | bytes 1400840 | tf_op jit(solution)/shard_map/ppermute | solution.py:549
  86.4 7.9 %collective-permute-done.20.refs_7_.refs_15_ = bf16[96,2432]{1,0:T(8,128)(2,1)S(1)} collective-permute-done((bf16[96,2432]{1,0:T(8,128)(2,1)S(1)}, bf16[96,2432]{1,0:T(8,128)(2,1)S(1)}, u32[]{:S(2)}, u32[]{:S(2)}) %collective-permute-start.20) | collective-permute-done | bytes 466976 | tf_op jit(solution)/shard_map/ppermute | solution.py:549
  94.4 1.4 collective-permute-start.28
  96.5 1.8 collective-permute-done.4.refs_2_.refs_10_
  99.0 5.3 %collective-permute-done.18.refs_6_.refs_14_ = bf16[96,2432]{1,0:T(8,128)(2,1)S(1)} collective-permute-done((bf16[96,2432]{1,0:T(8,128)(2,1)S(1)}, bf16[96,2432]{1,0:T(8,128)(2,1)S(1)}, u32[]{:S(2)}, u32[]{:S(2)}) %collective-permute-start.18) | collective-permute-done | bytes 466976 | tf_op jit(solution)/shard_map/ppermute | solution.py:549
  104.3 1.6 collective-permute-start.16
  105.9 1.6 collective-permute-start.5
  107.9 6.4 %collective-permute-done.12.refs_4_ = bf16[96,2432]{1,0:T(8,128)(2,1)S(1)} collective-permute-done((bf16[96,2432]{1,0:T(8,128)(2,1)S(1)}, bf16[96,2432]{1,0:T(8,128)(2,1)S(1)}, u32[]{:S(2)}, u32[]{:S(2)}) %collective-permute-start.12) | collective-permute-done | bytes 466976 | tf_op jit(solution)/shard_map/ppermute | solution.py:549
  114.4 8.9 %compose.3 = (bf16[8,768,768]{2,1,0:T(8,128)(2,1)S(1)}, f32[8,96,768]{2,1,0:T(8,128)S(1)}, bf16[8,96,768]{2,1,0:T(8,128)(2,1)S(1)}, bf16[768,768]{1,0:T(8,128)(2,1)S(1)}) custom-call(s32[1]{0:T(128)S(6)} %convert_element_type.3.last_ref, s32[1]{0:T(128)} %bitcast.place_ref, bf16[96,2560]{1,0:T(8,128)(2,1)S(1)} %copy-done.3, ...), custom_call_target="tpu_custom_call" | custom-call | flops 5435817984 | bytes 9437184 | tf_op jit(solution)/shard_map/compose/pallas_call | solution.py:250
  123.3 1.0 collective-permute-done.19.refs_7_.refs_15_
  124.3 1.6 collective-permute-start.17
  125.9 1.6 collective-permute-start.6
  127.5 4.1 %collective-permute-done.13.refs_5_ = bf16[96,2432]{1,0:T(8,128)(2,1)S(1)} collective-permute-done((bf16[96,2432]{1,0:T(8,128)(2,1)S(1)}, bf16[96,2432]{1,0:T(8,128)(2,1)S(1)}, u32[]{:S(2)}, u32[]{:S(2)}) %collective-permute-start.13) | collective-permute-done | bytes 466976 | tf_op jit(solution)/shard_map/ppermute | solution.py:549
  131.8 9.1 %compose.4 = (bf16[8,768,768]{2,1,0:T(8,128)(2,1)S(1)}, f32[8,96,768]{2,1,0:T(8,128)S(1)}, bf16[8,96,768]{2,1,0:T(8,128)(2,1)S(1)}, bf16[768,768]{1,0:T(8,128)(2,1)S(1)}) custom-call(s32[1]{0:T(128)S(6)} %convert_element_type.3.last_ref, s32[1]{0:T(128)} %bitcast.place_ref, ...), custom_call_target="tpu_custom_call", output_to_operand_aliasing={{0}: (19, {}), {1}: (20, {}), {2}: (21, {})} | custom-call | flops 5435817984 | bytes 9437184 | tf_op jit(solution)/shard_map/compose/pallas_call | solution.py:250
  141.1 1.9 %collective-permute-start.7 = (bf16[96,2432]{1,0:T(8,128)(2,1)S(1)}, bf16[96,2432]{1,0:T(8,128)(2,1)S(1)}, u32[]{:S(2)}, u32[]{:S(2)}) collective-permute-start(bf16[96,2432]{1,0:T(8,128)(2,1)S(1)} %collective-permute-done.6.refs_2_), channel_id=1, source_target_pairs={{1,3},{3,5},{5,7},{7,6},{6,4},{4,2},{2,0},{0,1},{9,11},{11,13},{13... | collective-permute-start | bytes 1400840 | tf_op jit(solution)/shard_map/ppermute | solution.py:549
  143.2 8.9 %compose.5 = (bf16[8,768,768]{2,1,0:T(8,128)(2,1)S(1)}, f32[8,96,768]{2,1,0:T(8,128)S(1)}, bf16[8,96,768]{2,1,0:T(8,128)(2,1)S(1)}, bf16[768,768]{1,0:T(8,128)(2,1)S(1)}) custom-call(s32[1]{0:T(128)S(6)} %convert_element_type.3.last_ref, s32[1]{0:T(128)} %bitcast.place_ref, ...), custom_call_target="tpu_custom_call", output_to_operand_aliasing={{0}: (19, {}), {1}: (20, {}), {2}: (21, {})} | custom-call | flops 5435817984 | bytes 9437184 | tf_op jit(solution)/shard_map/compose/pallas_call | solution.py:250
  152.1 5.1 %chain.1 = (bf16[2,768,768]{2,1,0:T(8,128)(2,1)S(1)}, bf16[2,768,768]{2,1,0:T(8,128)(2,1)S(1)}, bf16[6,256,256]{2,1,0:T(8,128)(2,1)S(1)}) custom-call(s32[1]{0:T(128)} %bitcast.place_ref, bf16[96,2432]{1,0:T(8,128)(2,1)S(1)} %get-tuple-element.72.refs_0_, bf16[96,2432]{1,0:T(8,128)(2,1)S(1)} %collective-permute-done.5.refs_1_, ...), custom_call_target="tpu_custom_call" | custom-call | flops 3623878656 | bytes 9437184 | tf_op jit(solution)/shard_map/chain/pallas_call | solution.py:314
  157.2 0.9 collective-permute-start.31
  158.1 2.3 %extend_factors.1 = (bf16[8,768,768]{2,1,0:T(8,128)(2,1)S(1)}, bf16[8,96,768]{2,1,0:T(8,128)(2,1)S(1)}) custom-call(s32[1]{0:T(128)} %bitcast.place_ref, bf16[2,768,768]{2,1,0:T(8,128)(2,1)S(1)} %get-tuple-element.119.gain_ref, bf16[8,768,768]{2,1,0:T(8,128)(2,1)S(1)} %get-tuple-element.120.factor_in, ...), custom_call_target="tpu_custom_call", output_to_operand_aliasing={{0}: (2, {}), {1}: (3, {})} | custom-call | flops 1811939328 | bytes 4718592 | tf_op jit(solution)/shard_map/extend_factors/pallas_call | solution.py:358
  160.4 1.8 hop.2
  163.0 1.8 hop.3
  164.8 1.3 collective-permute-start.33
  166.1 1.1 own_rows.1.own_ref
  167.2 15.1 %collective-permute-done.33.refs_2_ = bf16[6,256,256]{2,1,0:T(8,128)(2,1)S(1)} collective-permute-done((bf16[6,256,256]{2,1,0:T(8,128)(2,1)S(1)}, bf16[6,256,256]{2,1,0:T(8,128)(2,1)S(1)}, u32[]{:S(2)}, u32[]{:S(2)}) %collective-permute-start.33) | collective-permute-done | bytes 786464 | tf_op jit(solution)/shard_map/ppermute | solution.py:603
  182.2 5.6 %finish.1 = f32[8,96,768]{2,1,0:T(8,128)} custom-call(bf16[8,768,768]{2,1,0:T(8,128)(2,1)S(1)} %get-tuple-element.122.factor_ref, f32[8,96,768]{2,1,0:T(8,128)S(1)} %own_rows.1.own_ref, bf16[8,96,768]{2,1,0:T(8,128)(2,1)S(1)} %get-tuple-element.125.mine_ref, bf16[6,256,256]{2,1,0:T(8,128)(2,1)S(1)} %collective-permute-done.31.refs_0_, ...), custom_call_target="tpu_custom_call" | custom-call | tf_op jit(solution)/shard_map/finish/pallas_call | solution.py:508
  (41 shorter events, 5.0 us)
Async XLA Ops:
  2.3 47.8 %copy-start = (f32[8,96,768]{2,1,0:T(8,128)S(1)}, f32[8,96,768]{2,1,0:T(8,128)}, u32[]{:S(2)}) copy-start(f32[8,96,768]{2,1,0:T(8,128)} %increment_ref.5) | copy-start | bytes 7077892
  2.3 47.8 %copy-start.1 = (bf16[8,96,768]{2,1,0:T(8,128)(2,1)S(1)}, bf16[8,96,768]{2,1,0:T(8,128)(2,1)}, u32[]{:S(2)}) copy-start(bf16[8,96,768]{2,1,0:T(8,128)(2,1)} %gain_ref.5) | copy-start | bytes 3538948
  2.3 14.8 %collective-permute-start = (bf16[96,2432]{1,0:T(8,128)(2,1)}, bf16[96,2432]{1,0:T(8,128)(2,1)S(1)}, u32[]{:S(2)}, u32[]{:S(2)}) collective-permute-start(bf16[96,2432]{1,0:T(8,128)(2,1)} %pack.4.refs_0_.refs_8_), channel_id=1, source_target_pairs={{1,3},{3,5},{5,7},{7,6},{6,4},{4,2},{2,0},{0,1},{9,11},{11,13},{13... | collective-permute-start | bytes 1400840 | tf_op jit(solution)/shard_map/ppermute | solution.py:549
  5.2 13.9 %collective-permute-start.8 = (bf16[96,2432]{1,0:T(8,128)(2,1)}, bf16[96,2432]{1,0:T(8,128)(2,1)}, u32[]{:S(2)}, u32[]{:S(2)}) collective-permute-start(bf16[96,2432]{1,0:T(8,128)(2,1)} %pack.4.refs_0_.refs_8_), channel_id=1, source_target_pairs={{1,0},{3,1},{5,3},{7,5},{6,7},{4,6},{2,4},{0,2},{9,8},{11,9},{13,1... | collective-permute-start | bytes 1400840 | tf_op jit(solution)/shard_map/ppermute | solution.py:549
  7.9 86.3 %copy-start.3 = (bf16[96,2560]{1,0:T(8,128)(2,1)S(1)}, bf16[96,2560]{1,0:T(8,128)(2,1)}, u32[]{:S(2)}) copy-start(bf16[96,2560]{1,0:T(8,128)(2,1)} %pack.5.refs_0_.refs_8_) | copy-start | bytes 1474564
  7.9 19.6 %collective-permute-start.21 = (bf16[96,2560]{1,0:T(8,128)(2,1)}, bf16[96,2560]{1,0:T(8,128)(2,1)S(1)}, u32[]{:S(2)}, u32[]{:S(2)}) collective-permute-start(bf16[96,2560]{1,0:T(8,128)(2,1)} %pack.5.refs_0_.refs_8_), channel_id=1, source_target_pairs={{1,3},{3,5},{5,7},{7,6},{6,4},{4,2},{2,0},{0,1},{9,11},{11,13},{13... | collective-permute-start | bytes 1474568 | tf_op jit(solution)/shard_map/ppermute | solution.py:549
  17.0 20.5 %collective-permute-start.1 = (bf16[96,2432]{1,0:T(8,128)(2,1)S(1)}, bf16[96,2432]{1,0:T(8,128)(2,1)S(1)}, u32[]{:S(2)}, u32[]{:S(2)}) collective-permute-start(bf16[96,2432]{1,0:T(8,128)(2,1)S(1)} %collective-permute-done.refs_1_.refs_9_), channel_id=1, source_target_pairs={{1,3},{3,5},{5,7},{7,6},{6,4},{4,2},{2,0},{0,1},{9,11},{11,13},{13... | collective-permute-start | bytes 1400840 | tf_op jit(solution)/shard_map/ppermute | solution.py:549
  19.0 20.5 %collective-permute-start.25 = (bf16[96,2560]{1,0:T(8,128)(2,1)}, bf16[96,2560]{1,0:T(8,128)(2,1)S(1)}, u32[]{:S(2)}, u32[]{:S(2)}) collective-permute-start(bf16[96,2560]{1,0:T(8,128)(2,1)} %pack.5.refs_0_.refs_8_), channel_id=1, source_target_pairs={{1,0},{3,1},{5,3},{7,5},{6,7},{4,6},{2,4},{0,2},{9,8},{11,9},{13,1... | collective-permute-start | bytes 1474568 | tf_op jit(solution)/shard_map/ppermute | solution.py:549
  19.1 21.2 %collective-permute-start.9 = (bf16[96,2432]{1,0:T(8,128)(2,1)}, bf16[96,2432]{1,0:T(8,128)(2,1)S(1)}, u32[]{:S(2)}, u32[]{:S(2)}) collective-permute-start(bf16[96,2432]{1,0:T(8,128)(2,1)} %collective-permute-done.8.refs_4_.refs_12_), channel_id=1, source_target_pairs={{1,0},{3,1},{5,3},{7,5},{6,7},{4,6},{2,4},{0,2},{9,8},{11,9},{13,1... | collective-permute-start | bytes 1400840 | tf_op jit(solution)/shard_map/ppermute | solution.py:549
  27.6 20.5 %collective-permute-start.22 = (bf16[96,2560]{1,0:T(8,128)(2,1)S(1)}, bf16[96,2560]{1,0:T(8,128)(2,1)S(1)}, u32[]{:S(2)}, u32[]{:S(2)}) collective-permute-start(bf16[96,2560]{1,0:T(8,128)(2,1)S(1)} %collective-permute-done.21.refs_1_.refs_9_), channel_id=1, source_target_pairs={{1,3},{3,5},{5,7},{7,6},{6,4},{4,2},{2,0},{0,1},{9,11},{11,13},{13... | collective-permute-start | bytes 1474568 | tf_op jit(solution)/shard_map/ppermute | solution.py:549
  37.6 20.5 %collective-permute-start.2 = (bf16[96,2432]{1,0:T(8,128)(2,1)S(1)}, bf16[96,2432]{1,0:T(8,128)(2,1)S(1)}, u32[]{:S(2)}, u32[]{:S(2)}) collective-permute-start(bf16[96,2432]{1,0:T(8,128)(2,1)S(1)} %collective-permute-done.1.refs_2_.refs_10_), channel_id=1, source_target_pairs={{1,3},{3,5},{5,7},{7,6},{6,4},{4,2},{2,0},{0,1},{9,11},{11,13},{13... | collective-permute-start | bytes 1400840 | tf_op jit(solution)/shard_map/ppermute | solution.py:549
  39.6 20.5 %collective-permute-start.26 = (bf16[96,2560]{1,0:T(8,128)(2,1)S(1)}, bf16[96,2560]{1,0:T(8,128)(2,1)S(1)}, u32[]{:S(2)}, u32[]{:S(2)}) collective-permute-start(bf16[96,2560]{1,0:T(8,128)(2,1)S(1)} %collective-permute-done.25.refs_5_.refs_13_), channel_id=1, source_target_pairs={{1,0},{3,1},{5,3},{7,5},{6,7},{4,6},{2,4},{0,2},{9,8},{11,9},{13,1... | collective-permute-start | bytes 1474568 | tf_op jit(solution)/shard_map/ppermute | solution.py:549
  40.3 20.5 %collective-permute-start.10 = (bf16[96,2432]{1,0:T(8,128)(2,1)S(1)}, bf16[96,2432]{1,0:T(8,128)(2,1)S(1)}, u32[]{:S(2)}, u32[]{:S(2)}) collective-permute-start(bf16[96,2432]{1,0:T(8,128)(2,1)S(1)} %collective-permute-done.9.refs_5_.refs_13_), channel_id=1, source_target_pairs={{1,0},{3,1},{5,3},{7,5},{6,7},{4,6},{2,4},{0,2},{9,8},{11,9},{13,1... | collective-permute-start | bytes 1400840 | tf_op jit(solution)/shard_map/ppermute | solution.py:549
  48.1 20.5 %collective-permute-start.23 = (bf16[96,2560]{1,0:T(8,128)(2,1)S(1)}, bf16[96,2560]{1,0:T(8,128)(2,1)S(1)}, u32[]{:S(2)}, u32[]{:S(2)}) collective-permute-start(bf16[96,2560]{1,0:T(8,128)(2,1)S(1)} %collective-permute-done.22.refs_2_.refs_10_), channel_id=1, source_target_pairs={{1,3},{3,5},{5,7},{7,6},{6,4},{4,2},{2,0},{0,1},{9,11},{11,13},{13... | collective-permute-start | bytes 1474568 | tf_op jit(solution)/shard_map/ppermute | solution.py:549
  58.1 20.5 %collective-permute-start.3 = (bf16[96,2432]{1,0:T(8,128)(2,1)S(1)}, bf16[96,2432]{1,0:T(8,128)(2,1)S(1)}, u32[]{:S(2)}, u32[]{:S(2)}) collective-permute-start(bf16[96,2432]{1,0:T(8,128)(2,1)S(1)} %get-tuple-element.76.refs_0_.refs_8_), channel_id=1, source_target_pairs={{1,3},{3,5},{5,7},{7,6},{6,4},{4,2},{2,0},{0,1},{9,11},{11,13},{13... | collective-permute-start | bytes 1400840 | tf_op jit(solution)/shard_map/ppermute | solution.py:549
  60.1 24.2 %collective-permute-start.27 = (bf16[96,2560]{1,0:T(8,128)(2,1)S(1)}, bf16[96,2560]{1,0:T(8,128)(2,1)S(1)}, u32[]{:S(2)}, u32[]{:S(2)}) collective-permute-start(bf16[96,2560]{1,0:T(8,128)(2,1)S(1)} %collective-permute-done.26.refs_6_.refs_14_), channel_id=1, source_target_pairs={{1,0},{3,1},{5,3},{7,5},{6,7},{4,6},{2,4},{0,2},{9,8},{11,9},{13,1... | collective-permute-start | bytes 1474568 | tf_op jit(solution)/shard_map/ppermute | solution.py:549
  60.8 23.5 %collective-permute-start.11 = (bf16[96,2432]{1,0:T(8,128)(2,1)S(1)}, bf16[96,2432]{1,0:T(8,128)(2,1)S(1)}, u32[]{:S(2)}, u32[]{:S(2)}) collective-permute-start(bf16[96,2432]{1,0:T(8,128)(2,1)S(1)} %get-tuple-element.76.refs_0_.refs_8_), channel_id=1, source_target_pairs={{1,0},{3,1},{5,3},{7,5},{6,7},{4,6},{2,4},{0,2},{9,8},{11,9},{13,1... | collective-permute-start | bytes 1400840 | tf_op jit(solution)/shard_map/ppermute | solution.py:549
  68.6 25.6 %collective-permute-start.24 = (bf16[96,2560]{1,0:T(8,128)(2,1)S(1)}, bf16[96,2560]{1,0:T(8,128)(2,1)S(1)}, u32[]{:S(2)}, u32[]{:S(2)}) collective-permute-start(bf16[96,2560]{1,0:T(8,128)(2,1)S(1)} %collective-permute-done.23.refs_3_.refs_11_), channel_id=1, source_target_pairs={{1,3},{3,5},{5,7},{7,6},{6,4},{4,2},{2,0},{0,1},{9,11},{11,13},{13... | collective-permute-start | bytes 1474568 | tf_op jit(solution)/shard_map/ppermute | solution.py:549
  70.6 23.6 %collective-permute-start.20 = (bf16[96,2432]{1,0:T(8,128)(2,1)S(1)}, bf16[96,2432]{1,0:T(8,128)(2,1)S(1)}, u32[]{:S(2)}, u32[]{:S(2)}) collective-permute-start(bf16[96,2432]{1,0:T(8,128)(2,1)S(1)} %collective-permute-done.10.refs_6_.refs_14_), channel_id=1, source_target_pairs={{1,0},{3,1},{5,3},{7,5},{6,7},{4,6},{2,4},{0,2},{9,8},{11,9},{13,1... | collective-permute-start | bytes 1400840 | tf_op jit(solution)/shard_map/ppermute | solution.py:549
  78.6 19.7 %collective-permute-start.4 = (bf16[96,2432]{1,0:T(8,128)(2,1)S(1)}, bf16[96,2432]{1,0:T(8,128)(2,1)S(1)}, u32[]{:S(2)}, u32[]{:S(2)}) collective-permute-start(bf16[96,2432]{1,0:T(8,128)(2,1)S(1)} %collective-permute-done.3.refs_1_.refs_9_), channel_id=1, source_target_pairs={{1,3},{3,5},{5,7},{7,6},{6,4},{4,2},{2,0},{0,1},{9,11},{11,13},{13... | collective-permute-start | bytes 1400840 | tf_op jit(solution)/shard_map/ppermute | solution.py:549
  84.3 20.0 %collective-permute-start.18 = (bf16[96,2432]{1,0:T(8,128)(2,1)S(1)}, bf16[96,2432]{1,0:T(8,128)(2,1)S(1)}, u32[]{:S(2)}, u32[]{:S(2)}) collective-permute-start(bf16[96,2432]{1,0:T(8,128)(2,1)S(1)} %collective-permute-done.11.refs_5_.refs_13_), channel_id=1, source_target_pairs={{1,0},{3,1},{5,3},{7,5},{6,7},{4,6},{2,4},{0,2},{9,8},{11,9},{13,1... | collective-permute-start | bytes 1400840 | tf_op jit(solution)/shard_map/ppermute | solution.py:549
  84.3 29.9 %collective-permute-start.12 = (bf16[96,2432]{1,0:T(8,128)(2,1)S(1)}, bf16[96,2432]{1,0:T(8,128)(2,1)S(1)}, u32[]{:S(2)}, u32[]{:S(2)}) collective-permute-start(bf16[96,2432]{1,0:T(8,128)(2,1)S(1)} %get-tuple-element.72.refs_0_), channel_id=1, source_target_pairs={{1,0},{3,1},{5,3},{7,5},{6,7},{4,6},{2,4},{0,2},{9,8},{11,9},{13,1... | collective-permute-start | bytes 1400840 | tf_op jit(solution)/shard_map/ppermute | solution.py:549
  94.4 37.4 %copy-start.2 = (bf16[96,2432]{1,0:T(8,128)(2,1)S(1)}, bf16[96,2432]{1,0:T(8,128)(2,1)}, u32[]{:S(2)}) copy-start(bf16[96,2432]{1,0:T(8,128)(2,1)} %pack.4.refs_0_.refs_8_) | copy-start | bytes 1400836
  94.4 11.4 %collective-permute-start.28 = (bf16[8,96,128]{2,1,0:T(8,128)(2,1)S(1)}, bf16[8,96,128]{2,1,0:T(8,128)(2,1)S(1)}, u32[]{:S(2)}, u32[]{:S(2)}) collective-permute-start(bf16[8,96,128]{2,1,0:T(8,128)(2,1)S(1)} %collect.1.refs_19_), channel_id=1, source_target_pairs={{0,24},{1,25},{2,26},{3,27},{4,28},{5,29},{6,30},{7,31}} | collective-permute-start | bytes 589832 | tf_op jit(solution)/shard_map/ppermute | solution.py:586
  95.9 11.6 %collective-permute-start.29 = (bf16[8,96,128]{2,1,0:T(8,128)(2,1)S(1)}, bf16[8,96,128]{2,1,0:T(8,128)(2,1)S(1)}, u32[]{:S(2)}, u32[]{:S(2)}) collective-permute-start(bf16[8,96,128]{2,1,0:T(8,128)(2,1)S(1)} %collect.1.refs_19_), channel_id=1, source_target_pairs={{8,24},{9,25},{10,26},{11,27},{12,28},{13,29},{14,30},{15,31}} | collective-permute-start | bytes 589832 | tf_op jit(solution)/shard_map/ppermute | solution.py:586
  98.4 16.0 %collective-permute-start.30 = (bf16[8,96,128]{2,1,0:T(8,128)(2,1)S(1)}, bf16[8,96,128]{2,1,0:T(8,128)(2,1)S(1)}, u32[]{:S(2)}, u32[]{:S(2)}) collective-permute-start(bf16[8,96,128]{2,1,0:T(8,128)(2,1)S(1)} %collect.1.refs_19_), channel_id=1, source_target_pairs={{16,24},{17,25},{18,26},{19,27},{20,28},{21,29},{22,30},{23,31}} | collective-permute-start | bytes 589832 | tf_op jit(solution)/shard_map/ppermute | solution.py:586
  104.3 19.0 %collective-permute-start.16 = (bf16[96,2432]{1,0:T(8,128)(2,1)S(1)}, bf16[96,2432]{1,0:T(8,128)(2,1)S(1)}, u32[]{:S(2)}, u32[]{:S(2)}) collective-permute-start(bf16[96,2432]{1,0:T(8,128)(2,1)S(1)} %collective-permute-done.4.refs_2_.refs_10_), channel_id=1, source_target_pairs={{1,3},{3,5},{5,7},{7,6},{6,4},{4,2},{2,0},{0,1},{9,11},{11,13},{13... | collective-permute-start | bytes 1400840 | tf_op jit(solution)/shard_map/ppermute | solution.py:549
  105.9 20.0 %collective-permute-start.5 = (bf16[96,2432]{1,0:T(8,128)(2,1)S(1)}, bf16[96,2432]{1,0:T(8,128)(2,1)S(1)}, u32[]{:S(2)}, u32[]{:S(2)}) collective-permute-start(bf16[96,2432]{1,0:T(8,128)(2,1)S(1)} %get-tuple-element.72.refs_0_), channel_id=1, source_target_pairs={{1,3},{3,5},{5,7},{7,6},{6,4},{4,2},{2,0},{0,1},{9,11},{11,13},{13... | collective-permute-start | bytes 1400840 | tf_op jit(solution)/shard_map/ppermute | solution.py:549
  107.4 16.9 %collective-permute-start.19 = (bf16[96,2432]{1,0:T(8,128)(2,1)S(1)}, bf16[96,2432]{1,0:T(8,128)(2,1)S(1)}, u32[]{:S(2)}, u32[]{:S(2)}) collective-permute-start(bf16[96,2432]{1,0:T(8,128)(2,1)S(1)} %collective-permute-done.18.refs_6_.refs_14_), channel_id=1, source_target_pairs={{1,0},{3,1},{5,3},{7,5},{6,7},{4,6},{2,4},{0,2},{9,8},{11,9},{13,1... | collective-permute-start | bytes 1400840 | tf_op jit(solution)/shard_map/ppermute | solution.py:549
  114.3 17.2 %collective-permute-start.13 = (bf16[96,2432]{1,0:T(8,128)(2,1)S(1)}, bf16[96,2432]{1,0:T(8,128)(2,1)S(1)}, u32[]{:S(2)}, u32[]{:S(2)}) collective-permute-start(bf16[96,2432]{1,0:T(8,128)(2,1)S(1)} %collective-permute-done.12.refs_4_), channel_id=1, source_target_pairs={{1,0},{3,1},{5,3},{7,5},{6,7},{4,6},{2,4},{0,2},{9,8},{11,9},{13,1... | collective-permute-start | bytes 1400840 | tf_op jit(solution)/shard_map/ppermute | solution.py:549
  124.3 16.6 %collective-permute-start.17 = (bf16[96,2432]{1,0:T(8,128)(2,1)S(1)}, bf16[96,2432]{1,0:T(8,128)(2,1)S(1)}, u32[]{:S(2)}, u32[]{:S(2)}) collective-permute-start(bf16[96,2432]{1,0:T(8,128)(2,1)S(1)} %collective-permute-done.16.refs_3_.refs_11_), channel_id=1, source_target_pairs={{1,3},{3,5},{5,7},{7,6},{6,4},{4,2},{2,0},{0,1},{9,11},{11,13},{13... | collective-permute-start | bytes 1400840 | tf_op jit(solution)/shard_map/ppermute | solution.py:549
  125.9 15.2 %collective-permute-start.6 = (bf16[96,2432]{1,0:T(8,128)(2,1)S(1)}, bf16[96,2432]{1,0:T(8,128)(2,1)S(1)}, u32[]{:S(2)}, u32[]{:S(2)}) collective-permute-start(bf16[96,2432]{1,0:T(8,128)(2,1)S(1)} %collective-permute-done.5.refs_1_), channel_id=1, source_target_pairs={{1,3},{3,5},{5,7},{7,6},{6,4},{4,2},{2,0},{0,1},{9,11},{11,13},{13... | collective-permute-start | bytes 1400840 | tf_op jit(solution)/shard_map/ppermute | solution.py:549
  131.5 9.6 %collective-permute-start.14 = (bf16[96,2432]{1,0:T(8,128)(2,1)S(1)}, bf16[96,2432]{1,0:T(8,128)(2,1)S(1)}, u32[]{:S(2)}, u32[]{:S(2)}) collective-permute-start(bf16[96,2432]{1,0:T(8,128)(2,1)S(1)} %collective-permute-done.13.refs_5_), channel_id=1, source_target_pairs={{1,0},{3,1},{5,3},{7,5},{6,7},{4,6},{2,4},{0,2},{9,8},{11,9},{13,1... | collective-permute-start | bytes 1400840 | tf_op jit(solution)/shard_map/ppermute | solution.py:549
  141.1 10.9 %collective-permute-start.7 = (bf16[96,2432]{1,0:T(8,128)(2,1)S(1)}, bf16[96,2432]{1,0:T(8,128)(2,1)S(1)}, u32[]{:S(2)}, u32[]{:S(2)}) collective-permute-start(bf16[96,2432]{1,0:T(8,128)(2,1)S(1)} %collective-permute-done.6.refs_2_), channel_id=1, source_target_pairs={{1,3},{3,5},{5,7},{7,6},{6,4},{4,2},{2,0},{0,1},{9,11},{11,13},{13... | collective-permute-start | bytes 1400840 | tf_op jit(solution)/shard_map/ppermute | solution.py:549
  143.1 9.0 %collective-permute-start.15 = (bf16[96,2432]{1,0:T(8,128)(2,1)S(1)}, bf16[96,2432]{1,0:T(8,128)(2,1)S(1)}, u32[]{:S(2)}, u32[]{:S(2)}) collective-permute-start(bf16[96,2432]{1,0:T(8,128)(2,1)S(1)} %collective-permute-done.14.refs_6_), channel_id=1, source_target_pairs={{1,0},{3,1},{5,3},{7,5},{6,7},{4,6},{2,4},{0,2},{9,8},{11,9},{13,1... | collective-permute-start | bytes 1400840 | tf_op jit(solution)/shard_map/ppermute | solution.py:549
  157.2 3.3 %collective-permute-start.31 = (bf16[6,256,256]{2,1,0:T(8,128)(2,1)S(1)}, bf16[6,256,256]{2,1,0:T(8,128)(2,1)S(1)}, u32[]{:S(2)}, u32[]{:S(2)}) collective-permute-start(bf16[6,256,256]{2,1,0:T(8,128)(2,1)S(1)} %get-tuple-element.126), channel_id=1, source_target_pairs={{24,16},{25,17},{26,18},{27,19},{28,20},{29,21},{30,22},{31,23}} | collective-permute-start | bytes 2359304 | tf_op jit(solution)/shard_map/ppermute | solution.py:603
  162.2 0.7 collective-permute-start.32
  164.8 17.4 %collective-permute-start.33 = (bf16[6,256,256]{2,1,0:T(8,128)(2,1)S(1)}, bf16[6,256,256]{2,1,0:T(8,128)(2,1)S(1)}, u32[]{:S(2)}, u32[]{:S(2)}) collective-permute-start(bf16[6,256,256]{2,1,0:T(8,128)(2,1)S(1)} %hop.3), channel_id=1, source_target_pairs={{8,0},{9,1},{10,2},{11,3},{12,4},{13,5},{14,6},{15,7}} | collective-permute-start | bytes 2359304 | tf_op jit(solution)/shard_map/ppermute | solution.py:603

commit v16 on v15

--- a/solution.py
+++ b/solution.py
@@ -167,46 +167,52 @@
     return own + nt(jnp.where(picked, 1.0, 0.0).astype(BF16), half[...])
 
 
-def compose_kernel(cycle, right, first, last_ref, place_ref, *refs):
+def prepare(places, blocks, step, turns, gain, fresh, raw, extras):
+    stride = gain.shape[0] * 3 // 2
+    lanes, side = slice(step * stride, (step + 1) * stride), slice(turns * stride, turns * stride + LANES)
+    parts, sides = [block.at[:, lanes] for block in blocks], [block.at[:, side] for block in blocks]
+    assemble(places, parts, sides, step, gain, fresh, raw, extras)
+
+
+def compose_kernel(cycle, right, turns, first, last_ref, place_ref, *refs):
     count = len(cycle)
     places = origins(place_ref[0], cycle, right)
-    blocks, sides, refs = refs[:count], refs[count:2 * count], refs[2 * count:]
+    blocks, refs = refs[:count], refs[count:]
     if first:
-        tiles = blocks[0].shape[1] // 3 // LANES + 1
+        tiles = blocks[0].shape[0] * count // 2 // LANES + 1
         ends, refs = refs[:tiles], refs[tiles:]
     else:
-        half_in, factor_in, refs = refs[0], refs[1], refs[4:]
-    factor_out, own_out, mine_out, half, gain, factor, fresh, middle, raw, extras = refs
+        half_in, factor_in, refs = refs[0], refs[1], refs[3:]
+    factor_out, mine_out, half_out, half, factor, middle, raw, extras, gain, fresh, spare = refs
+    gains, freshes = (gain, spare.at[0]), (fresh, spare.at[1])
     rows = blocks[0].shape[0]
-
-    @pl.when(pl.program_id(0) == 0)
-    def _():
-        if first:
-            scale = jnp.where(last_ref[0] == 1, 1.0, 0.0).astype(BF16)
-            for n, end in enumerate(ends[:-1]):
-                raw[:, :, n * LANES:(n + 1) * LANES] = end[...] * scale
-            extras[...] = ends[-1][...] * scale
-            unpack(raw, extras, 0, half)
-        else:
-            factor[...] = factor_in[0]
-            half[...] = half_in[...]
-
-    step = pl.num_programs(0) - 1 - pl.program_id(0)
-    assemble(places, blocks, sides, step, gain, fresh, raw, extras)
-    if first:
-
-        @pl.when(pl.program_id(0) == 0)
+    mine = pl.multiple_of(place_ref[0] * rows, 16)
+    for turn in range(turns):
+
+        @pl.when(pl.program_id(0) == turn)
         def _():
-            factor[...] = gain[...]
-
-        pl.when(pl.program_id(0) > 0)(lambda: extend(gain, factor))
-    else:
-        extend(gain, factor)
-    advance(gain, half, fresh, middle)
-    mine = pl.multiple_of(place_ref[0] * rows, 16)
-    own_out[0] = whole_rows(half, mine, rows)
-    mine_out[0] = factor[pl.ds(mine, rows), :]
-    factor_out[0] = factor[...]
+            now = turn % 2
+            if turn == 0 and first:
+                scale = jnp.where(last_ref[0] == 1, 1.0, 0.0).astype(BF16)
+                for n, end in enumerate(ends[:-1]):
+                    raw[:, :, n * LANES:(n + 1) * LANES] = end[...] * scale
+                extras[...] = ends[-1][...] * scale
+                unpack(raw, extras, 0, half)
+            elif turn == 0:
+                factor[...] = factor_in[0]
+                half[...] = half_in[...]
+            if turn == 0:
+                prepare(places, blocks, turns - 1, turns, gains[0], freshes[0], raw, extras)
+            if turn == 0 and first:
+                factor[...] = gains[0][...]
+            else:
+                extend(gains[now], factor)
+            if turn + 1 < turns:
+                prepare(places, blocks, turns - 2 - turn, turns, gains[1 - now], freshes[1 - now], raw, extras)
+            advance(gains[now], half, freshes[now], middle)
+            half_out[0] = half[...]
+            mine_out[0] = factor[pl.ds(mine, rows), :]
+            factor_out[0] = factor[...]
 
 
 def square(width, place=None):
@@ -215,19 +221,20 @@
     return pl.BlockSpec((1, width, width), lambda i, *p: (place(i), 0, 0))
 
 
-def row_specs(blocks, turns):
-    rows = blocks[0].shape[0]
-    stride = rows * len(blocks) * 3 // 2
-    step = pl.BlockSpec((rows, stride), lambda i, *p: (0, turns - 1 - i))
-    side = pl.BlockSpec((rows, LANES), lambda i, *p: (0, turns * stride // LANES), pipeline_mode=pl.Buffered(1))
-    return [step] * len(blocks) + [side] * len(blocks)
+def row_specs(blocks):
+    return [pl.BlockSpec(block.shape, lambda i, *p: (0, 0), pipeline_mode=pl.Buffered(1)) for block in blocks]
 
 
 def row_scratch(count, rows):
     width = count * rows
-    return [pltpu.VMEM((width, width), BF16)] * 4 + [
+    whole = pltpu.VMEM((width, width), BF16)
+    return [
+        whole,
         pltpu.VMEM((count, rows, width // 2), BF16),
         pltpu.VMEM((count, rows, LANES), BF16),
+        whole,
+        whole,
+        pltpu.VMEM((2, width, width), BF16),
     ]
 
 
@@ -237,69 +244,60 @@
     width = rows * count
     first = state is None
     anywhere = pl.BlockSpec(memory_space=pl.ANY)
-    in_specs = row_specs(blocks, turns)
+    in_specs = row_specs(blocks)
     if first:
         in_specs += [pl.BlockSpec(end.shape, lambda i, *p: (0, 0, 0), pipeline_mode=pl.Buffered(1)) for end in ends]
         args = ends
     else:
         after = pl.BlockSpec((1, width, width), lambda i, *p: (low + turns, 0, 0), pipeline_mode=pl.Buffered(1))
-        in_specs += [square(width), after, anywhere, anywhere]
+        in_specs += [square(width), after, anywhere]
         args = [half, *state]
+    whole = square(width, lambda i: low + turns - 1 - i)
     band = pl.BlockSpec((1, rows, width), lambda i, *p: (low + turns - 1 - i, 0, 0))
-    base = 2 + 2 * count + 1
-    return pl.pallas_call(
-        functools.partial(compose_kernel, cycle, right, first),
+    base = 2 + count + 1
+    return pl.pallas_call(
+        functools.partial(compose_kernel, cycle, right, turns, first),
         grid_spec=pltpu.PrefetchScalarGridSpec(
             num_scalar_prefetch=2,
             grid=(turns,),
             in_specs=in_specs,
-            out_specs=[square(width, lambda i: low + turns - 1 - i), band, band, square(width)],
-            scratch_shapes=row_scratch(count, rows),
+            out_specs=[whole, band, square(width, lambda i: turns - 1 - i), square(width)],
+            scratch_shapes=[pltpu.VMEM((width, width), BF16)] + row_scratch(count, rows),
         ),
         out_shape=[
             jax.ShapeDtypeStruct((steps, width, width), BF16),
-            jax.ShapeDtypeStruct((steps, rows, width), F32),
             jax.ShapeDtypeStruct((steps, rows, width), BF16),
+            jax.ShapeDtypeStruct((turns, width, width), BF16),
             jax.ShapeDtypeStruct((width, width), BF16),
         ],
-        input_output_aliases={} if first else {base: 0, base + 1: 1, base + 2: 2},
-        compiler_params=pltpu.CompilerParams(vmem_limit_bytes=18 * MIB),
+        input_output_aliases={} if first else {base: 0, base + 1: 1},
+        compiler_params=pltpu.CompilerParams(vmem_limit_bytes=22 * MIB),
         cost_estimate=pl.CostEstimate(
             flops=6 * turns * width**3, bytes_accessed=8 * turns * width * width, transcendentals=0
         ),
         name="compose",
-    )(last, place, *blocks, *blocks, *args)
+    )(last, place, *blocks, *args)
 
 
 def chain_kernel(cycle, right, turns, place_ref, *refs):
     count = len(cycle)
     places = origins(place_ref[0], cycle, right)
     blocks, refs = refs[:count], refs[count:]
-    half_in, refs = refs[0], refs[-10:]
+    half_in, refs = refs[0], refs[1:]
     gain_out, half_out, packed_out, half, middle, raw, extras, gain, fresh, spare = refs
     gains, freshes = (gain, spare.at[0]), (fresh, spare.at[1])
-    rows, width = blocks[0].shape[0], half.shape[0]
-    stride = width * 3 // 2
-    side = slice(turns * stride, turns * stride + LANES)
-
-    def prepare(turn):
-        step = turns - 1 - turn
-        lanes = slice(step * stride, (step + 1) * stride)
-        parts = [block.at[:, lanes] for block in blocks]
-        sides = [block.at[:, side] for block in blocks]
-        assemble(places, parts, sides, step, gains[turn % 2], freshes[turn % 2], raw, extras)
-
     for turn in range(turns):
 
         @pl.when(pl.program_id(0) == turn)
         def _():
+            now = turn % 2
             if turn == 0:
                 half[...] = half_in[...]
-                prepare(0)
-            gain_out[0] = gains[turn % 2][...]
+                prepare(places, blocks, turns - 1, turns, gains[0], freshes[0], raw, extras)
+            gain_out[0] = gains[now][...]
             if turn + 1 < turns:
-                prepare(turn + 1)
-            advance(gains[turn % 2], half, freshes[turn % 2], middle)
+                prepare(places, blocks, turns - 2 - turn, turns, gains[1 - now], freshes[1 - now], raw, extras)
+            advance(gains[now], half, freshes[now], middle)
             half_out[0] = half[...]
             if turn == turns - 1:
                 fold(half, packed_out)
@@ -309,27 +307,22 @@
     count = len(blocks)
     rows = blocks[0].shape[0]
     width = rows * count
-    in_specs = [pl.BlockSpec(blocks[0].shape, lambda i, *p: (0, 0), pipeline_mode=pl.Buffered(1))] * count
+    in_specs = row_specs(blocks) + [square(width)]
     whole = square(width, lambda i: turns - 1 - i)
     return pl.pallas_call(
         functools.partial(chain_kernel, cycle, right, turns),
         grid_spec=pltpu.PrefetchScalarGridSpec(
             num_scalar_prefetch=1,
             grid=(turns,),
-            in_specs=in_specs + [square(width)],
+            in_specs=in_specs,
             out_specs=[whole, whole, pl.BlockSpec(blocks_shape(width), lambda i, *p: (0, 0, 0))],
-            scratch_shapes=[
-                pltpu.VMEM((width, width), BF16),
-                pltpu.VMEM((width, width), BF16),
-                pltpu.VMEM((count, rows, width // 2), BF16),
-                pltpu.VMEM((count, rows, LANES), BF16),
-                pltpu.VMEM((width, width), BF16),
-                pltpu.VMEM((width, width), BF16),
-                pltpu.VMEM((2, width, width), BF16),
-            ],
-        ),
-        out_shape=[jax.ShapeDtypeStruct((turns, width, width), BF16)] * 2
-        + [jax.ShapeDtypeStruct(blocks_shape(width), BF16)],
+            scratch_shapes=[pltpu.VMEM((width, width), BF16)] + row_scratch(count, rows),
+        ),
+        out_shape=[
+            jax.ShapeDtypeStruct((turns, width, width), BF16),
+            jax.ShapeDtypeStruct((turns, width, width), BF16),
+            jax.ShapeDtypeStruct(blocks_shape(width), BF16),
+        ],
         compiler_params=pltpu.CompilerParams(vmem_limit_bytes=18 * MIB),
         cost_estimate=pl.CostEstimate(
             flops=4 * turns * width**3, bytes_accessed=8 * turns * width * width, transcendentals=0
@@ -380,31 +373,37 @@
     )(place, gains, factors, mine)
 
 
-def rows_kernel(place_ref, half_ref, own_ref, own_out):
-    del own_ref
+def rows_kernel(size, place_ref, *refs):
+    own_out = refs[-1]
     rows = own_out.shape[1]
-    own_out[0] = whole_rows(half_ref.at[0], pl.multiple_of(place_ref[0] * rows, 16), rows)
-
-
-def own_rows(place, halves, own):
-    turns, width, _ = halves.shape
-    steps, rows, _ = own.shape
-    return pl.pallas_call(
-        rows_kernel,
+    mine = pl.multiple_of(place_ref[0] * rows, 16)
+    for n, half_ref in enumerate(refs[:-1]):
+
+        @pl.when(pl.program_id(0) // size == n)
+        def _():
+            own_out[0] = whole_rows(half_ref.at[0], mine, rows)
+
+
+def own_rows(place, halves, rows):
+    size, width, _ = halves[0].shape
+    steps = size * len(halves)
+    return pl.pallas_call(
+        functools.partial(rows_kernel, size),
         grid_spec=pltpu.PrefetchScalarGridSpec(
             num_scalar_prefetch=1,
-            grid=(turns,),
-            in_specs=[square(width, lambda i: i), pl.BlockSpec(memory_space=pl.ANY)],
+            grid=(steps,),
+            in_specs=[
+                square(width, lambda i, n=n: jnp.clip(i - n * size, 0, size - 1)) for n in range(len(halves))
+            ],
             out_specs=pl.BlockSpec((1, rows, width), lambda i, *p: (i, 0, 0)),
         ),
         out_shape=jax.ShapeDtypeStruct((steps, rows, width), F32),
-        input_output_aliases={2: 0},
-        compiler_params=pltpu.CompilerParams(vmem_limit_bytes=8 * MIB),
+        compiler_params=pltpu.CompilerParams(vmem_limit_bytes=14 * MIB),
         cost_estimate=pl.CostEstimate(
-            flops=2 * turns * rows * width**2, bytes_accessed=2 * turns * width * width, transcendentals=0
+            flops=2 * steps * rows * width**2, bytes_accessed=2 * steps * width * width, transcendentals=0
         ),
         name="own_rows",
-    )(place, halves, own)
+    )(place, *halves)
 
 
 def upper_blocks(width):
@@ -587,19 +586,24 @@
         for n in range(gains.shape[2] // 2 // LANES + 1)
     ]
     state, half = None, None
+    halves = []
     for turn, (low, high) in enumerate(ranges):
         parts = [own[turn]] + found[turn][1][1:] + found[turn][-1][1:]
         if turn < len(ties):
             parts, _ = lax.optimization_barrier((parts, ties[turn]))
-            *state, half = compose(last, place, cycle, rights[turn], parts, ends, state, half, low, high - low, steps)
+            *state, kept, half = compose(
+                last, place, cycle, rights[turn], parts, ends, state, half, low, high - low, steps
+            )
         else:
-            early = chain(place, cycle, rights[turn], parts, half, high)
-    factors, own, mine = state
-    factors, mine = extend_factors(place, early[0], factors, mine)
-    own = own_rows(place, early[1], own)
+            late_gains, kept, folded = chain(place, cycle, rights[turn], parts, half, high)
+        halves.insert(0, kept)
+    factors, mine = extend_factors(place, late_gains, *state)
     packed = []
     for turn in range(blocks - 1, 0, -1):
-        before = hop(factors, early[1], packed) if packed else early[2]
+        if turn == 1:
+            own = own_rows(place, lax.optimization_barrier((halves, before))[0], gains.shape[1])
+            packed, own = lax.optimization_barrier((packed, own))
+        before = hop(factors, halves[0], packed) if packed else folded
         packed.append(lax.ppermute(before, "tm", [(turn, turn - 1)]))
     return finish(factors, own, mine, packed)
 

time: 188 us -> 187 us (level)
  Pallas kernels: 50.2 us -> 46.7 us
  waiting for transfers between devices: 96.4 us -> 99.1 us
    ppermute x28, waiting for transfers between devices: 81.3 us -> 87.8 us  [passed(): lax.ppermute(array, 'tile', [(cycle[n], cycle[(n + way) % count]) for n i...]
    ppermute x3, waiting for transfers between devices: 15.1 us -> 11.3 us  [local(): packed.append(lax.ppermute(before, 'tm', [(turn, turn - 1)]))]
    pallas_call x4, Pallas kernels: 28 us -> 24.6 us  [the longest x3 20.2 us: compose(): pl.pallas_call(functools.partial(compose_kernel, cycle, right, turns, fir...]
  transfers between devices with their start and end apart: 34 -> 34, of which waited for: 18 -> 20; matrix products, arithmetic and copies ran while one was open for 0% -> 0% of each run, Pallas kernels for 18% -> 16%
where the time goes in v16:
time: 187 us
  waiting for transfers between devices  99.1 us (53%)
  Pallas kernels  46.7 us (25%)
  starting transfers between devices  41 us (22%)
    ppermute x28, waiting for transfers between devices, passed(): lax.ppermute(array, 'tile', [(cycle[n], cycle[(n + way) % count]) for n i...  87.8 us
    ppermute x28, starting transfers between devices, passed(): lax.ppermute(array, 'tile', [(cycle[n], cycle[(n + way) % count]) for n i...  35.3 us
    pallas_call x3, Pallas kernels, compose(): pl.pallas_call(functools.partial(compose_kernel, cycle, right, turns, fir...  20.2 us
    ppermute x3, waiting for transfers between devices, local(): packed.append(lax.ppermute(before, 'tm', [(turn, turn - 1)]))  11.3 us
    pallas_call x3, Pallas kernels, pack(): pl.pallas_call(functools.partial(pack_kernel, count, ranges), grid_spec=p...  5.57 us
    pallas_call x1, Pallas kernels, finish(): pl.pallas_call(functools.partial(finish_kernel, len(packed)), grid=(steps...  5.56 us
    pallas_call x1, Pallas kernels, chain(): pl.pallas_call(functools.partial(chain_kernel, cycle, right, turns), grid...  4.95 us
    pallas_call x1, Pallas kernels, own_rows(): pl.pallas_call(functools.partial(rows_kernel, size), grid_spec=pltpu.Pref...  4.39 us
  transfers between devices with their start and end apart: 34, of which 20 were waited for; matrix products, arithmetic and copies ran while one was open for 0% of the time, Pallas kernels for 16%

profile of v16, /device:TPU:0, one launch (start us, length us, event | category | flops | bytes accessed | tf_op | source)
XLA Modules:
  0.0 187.0 jit_solution(25252585160227199)
XLA Ops:
  0.0 2.3 %pack.4.refs_0_ = bf16[96,2432]{1,0:T(8,128)(2,1)} custom-call(s32[1]{0:T(128)} %bitcast.place_ref, s32[1]{0:T(128)} %bitcast.1.block_ref, bf16[8,96,768]{2,1,0:T(8,128)(2,1)} %gain_ref.5, f32[8,96,768]{2,1,0:T(8,128)} %increment_ref.5), custom_call_target="tpu_custom_call" | custom-call | tf_op jit(solution)/shard_map/pack/pallas_call | solution.py:80
  2.3 3.0 %collective-permute-start = (bf16[96,2432]{1,0:T(8,128)(2,1)}, bf16[96,2432]{1,0:T(8,128)(2,1)S(1)}, u32[]{:S(2)}, u32[]{:S(2)}) collective-permute-start(bf16[96,2432]{1,0:T(8,128)(2,1)} %pack.4.refs_0_), channel_id=1, source_target_pairs={{1,3},{3,5},{5,7},{7,6},{6,4},{4,2},{2,0},{0,1},{9,11},{11,13},{13... | collective-permute-start | bytes 1400840 | tf_op jit(solution)/shard_map/ppermute | solution.py:548
  5.3 2.6 %pack.5.refs_0_ = bf16[96,2560]{1,0:T(8,128)(2,1)} custom-call(s32[1]{0:T(128)} %bitcast.place_ref, s32[1]{0:T(128)} %bitcast.1.block_ref, bf16[8,96,768]{2,1,0:T(8,128)(2,1)} %gain_ref.5, f32[8,96,768]{2,1,0:T(8,128)} %increment_ref.5, f32[96,768]{1,0:T(8,128)} %refs_0_.1), custom_call_target="tpu_custom_call" | custom-call | tf_op jit(solution)/shard_map/pack/pallas_call | solution.py:80
  7.9 1.9 %collective-permute-start.21 = (bf16[96,2560]{1,0:T(8,128)(2,1)}, bf16[96,2560]{1,0:T(8,128)(2,1)S(1)}, u32[]{:S(2)}, u32[]{:S(2)}) collective-permute-start(bf16[96,2560]{1,0:T(8,128)(2,1)} %pack.5.refs_0_), channel_id=1, source_target_pairs={{1,3},{3,5},{5,7},{7,6},{6,4},{4,2},{2,0},{0,1},{9,11},{11,13},{13... | collective-permute-start | bytes 1474568 | tf_op jit(solution)/shard_map/ppermute | solution.py:548
  9.9 7.2 %collective-permute-done.refs_1_ = bf16[96,2432]{1,0:T(8,128)(2,1)S(1)} collective-permute-done((bf16[96,2432]{1,0:T(8,128)(2,1)}, bf16[96,2432]{1,0:T(8,128)(2,1)S(1)}, u32[]{:S(2)}, u32[]{:S(2)}) %collective-permute-start) | collective-permute-done | bytes 466976 | tf_op jit(solution)/shard_map/ppermute | solution.py:548
  17.0 2.0 %collective-permute-start.1 = (bf16[96,2432]{1,0:T(8,128)(2,1)S(1)}, bf16[96,2432]{1,0:T(8,128)(2,1)S(1)}, u32[]{:S(2)}, u32[]{:S(2)}) collective-permute-start(bf16[96,2432]{1,0:T(8,128)(2,1)S(1)} %collective-permute-done.refs_1_), channel_id=1, source_target_pairs={{1,3},{3,5},{5,7},{7,6},{6,4},{4,2},{2,0},{0,1},{9,11},{11,13},{13... | collective-permute-start | bytes 1400840 | tf_op jit(solution)/shard_map/ppermute | solution.py:548
  19.1 2.0 %collective-permute-start.9 = (bf16[96,2432]{1,0:T(8,128)(2,1)}, bf16[96,2432]{1,0:T(8,128)(2,1)S(1)}, u32[]{:S(2)}, u32[]{:S(2)}) collective-permute-start(bf16[96,2432]{1,0:T(8,128)(2,1)} %collective-permute-done.8.refs_4_), channel_id=1, source_target_pairs={{1,0},{3,1},{5,3},{7,5},{6,7},{4,6},{2,4},{0,2},{9,8},{11,9},{13,1... | collective-permute-start | bytes 1400840 | tf_op jit(solution)/shard_map/ppermute | solution.py:548
  21.1 6.4 %collective-permute-done.21.refs_1_ = bf16[96,2560]{1,0:T(8,128)(2,1)S(1)} collective-permute-done((bf16[96,2560]{1,0:T(8,128)(2,1)}, bf16[96,2560]{1,0:T(8,128)(2,1)S(1)}, u32[]{:S(2)}, u32[]{:S(2)}) %collective-permute-start.21) | collective-permute-done | bytes 491552 | tf_op jit(solution)/shard_map/ppermute | solution.py:548
  27.6 2.0 %collective-permute-start.22 = (bf16[96,2560]{1,0:T(8,128)(2,1)S(1)}, bf16[96,2560]{1,0:T(8,128)(2,1)S(1)}, u32[]{:S(2)}, u32[]{:S(2)}) collective-permute-start(bf16[96,2560]{1,0:T(8,128)(2,1)S(1)} %collective-permute-done.21.refs_1_), channel_id=1, source_target_pairs={{1,3},{3,5},{5,7},{7,6},{6,4},{4,2},{2,0},{0,1},{9,11},{11,13},{13... | collective-permute-start | bytes 1474568 | tf_op jit(solution)/shard_map/ppermute | solution.py:548
  29.6 8.0 %collective-permute-done.1.refs_2_ = bf16[96,2432]{1,0:T(8,128)(2,1)S(1)} collective-permute-done((bf16[96,2432]{1,0:T(8,128)(2,1)S(1)}, bf16[96,2432]{1,0:T(8,128)(2,1)S(1)}, u32[]{:S(2)}, u32[]{:S(2)}) %collective-permute-start.1) | collective-permute-done | bytes 466976 | tf_op jit(solution)/shard_map/ppermute | solution.py:548
  37.6 2.0 %collective-permute-start.2 = (bf16[96,2432]{1,0:T(8,128)(2,1)S(1)}, bf16[96,2432]{1,0:T(8,128)(2,1)S(1)}, u32[]{:S(2)}, u32[]{:S(2)}) collective-permute-start(bf16[96,2432]{1,0:T(8,128)(2,1)S(1)} %collective-permute-done.1.refs_2_), channel_id=1, source_target_pairs={{1,3},{3,5},{5,7},{7,6},{6,4},{4,2},{2,0},{0,1},{9,11},{11,13},{13... | collective-permute-start | bytes 1400840 | tf_op jit(solution)/shard_map/ppermute | solution.py:548
  40.3 1.4 collective-permute-start.10
  41.7 6.4 %collective-permute-done.22.refs_2_ = bf16[96,2560]{1,0:T(8,128)(2,1)S(1)} collective-permute-done((bf16[96,2560]{1,0:T(8,128)(2,1)S(1)}, bf16[96,2560]{1,0:T(8,128)(2,1)S(1)}, u32[]{:S(2)}, u32[]{:S(2)}) %collective-permute-start.22) | collective-permute-done | bytes 491552 | tf_op jit(solution)/shard_map/ppermute | solution.py:548
  48.1 2.0 %collective-permute-start.23 = (bf16[96,2560]{1,0:T(8,128)(2,1)S(1)}, bf16[96,2560]{1,0:T(8,128)(2,1)S(1)}, u32[]{:S(2)}, u32[]{:S(2)}) collective-permute-start(bf16[96,2560]{1,0:T(8,128)(2,1)S(1)} %collective-permute-done.22.refs_2_), channel_id=1, source_target_pairs={{1,3},{3,5},{5,7},{7,6},{6,4},{4,2},{2,0},{0,1},{9,11},{11,13},{13... | collective-permute-start | bytes 1474568 | tf_op jit(solution)/shard_map/ppermute | solution.py:548
  50.8 7.3 %collective-permute-done.2.refs_3_ = bf16[96,2432]{1,0:T(8,128)(2,1)S(1)} collective-permute-done((bf16[96,2432]{1,0:T(8,128)(2,1)S(1)}, bf16[96,2432]{1,0:T(8,128)(2,1)S(1)}, u32[]{:S(2)}, u32[]{:S(2)}) %collective-permute-start.2) | collective-permute-done | bytes 466976 | tf_op jit(solution)/shard_map/ppermute | solution.py:548
  58.1 2.0 %collective-permute-start.3 = (bf16[96,2432]{1,0:T(8,128)(2,1)S(1)}, bf16[96,2432]{1,0:T(8,128)(2,1)S(1)}, u32[]{:S(2)}, u32[]{:S(2)}) collective-permute-start(bf16[96,2432]{1,0:T(8,128)(2,1)S(1)} %get-tuple-element.83.refs_0_), channel_id=1, source_target_pairs={{1,3},{3,5},{5,7},{7,6},{6,4},{4,2},{2,0},{0,1},{9,11},{11,13},{13... | collective-permute-start | bytes 1400840 | tf_op jit(solution)/shard_map/ppermute | solution.py:548
  60.8 1.4 collective-permute-start.11
  62.2 6.4 %collective-permute-done.23.refs_3_ = bf16[96,2560]{1,0:T(8,128)(2,1)S(1)} collective-permute-done((bf16[96,2560]{1,0:T(8,128)(2,1)S(1)}, bf16[96,2560]{1,0:T(8,128)(2,1)S(1)}, u32[]{:S(2)}, u32[]{:S(2)}) %collective-permute-start.23) | collective-permute-done | bytes 491552 | tf_op jit(solution)/shard_map/ppermute | solution.py:548
  68.6 2.0 %collective-permute-start.24 = (bf16[96,2560]{1,0:T(8,128)(2,1)S(1)}, bf16[96,2560]{1,0:T(8,128)(2,1)S(1)}, u32[]{:S(2)}, u32[]{:S(2)}) collective-permute-start(bf16[96,2560]{1,0:T(8,128)(2,1)S(1)} %collective-permute-done.23.refs_3_), channel_id=1, source_target_pairs={{1,3},{3,5},{5,7},{7,6},{6,4},{4,2},{2,0},{0,1},{9,11},{11,13},{13... | collective-permute-start | bytes 1474568 | tf_op jit(solution)/shard_map/ppermute | solution.py:548
  70.7 7.9 %collective-permute-done.3.refs_1_ = bf16[96,2432]{1,0:T(8,128)(2,1)S(1)} collective-permute-done((bf16[96,2432]{1,0:T(8,128)(2,1)S(1)}, bf16[96,2432]{1,0:T(8,128)(2,1)S(1)}, u32[]{:S(2)}, u32[]{:S(2)}) %collective-permute-start.3) | collective-permute-done | bytes 466976 | tf_op jit(solution)/shard_map/ppermute | solution.py:548
  78.6 2.0 %collective-permute-start.4 = (bf16[96,2432]{1,0:T(8,128)(2,1)S(1)}, bf16[96,2432]{1,0:T(8,128)(2,1)S(1)}, u32[]{:S(2)}, u32[]{:S(2)}) collective-permute-start(bf16[96,2432]{1,0:T(8,128)(2,1)S(1)} %collective-permute-done.3.refs_1_), channel_id=1, source_target_pairs={{1,3},{3,5},{5,7},{7,6},{6,4},{4,2},{2,0},{0,1},{9,11},{11,13},{13... | collective-permute-start | bytes 1400840 | tf_op jit(solution)/shard_map/ppermute | solution.py:548
  80.6 3.6 %collective-permute-done.11.refs_5_ = bf16[96,2432]{1,0:T(8,128)(2,1)S(1)} collective-permute-done((bf16[96,2432]{1,0:T(8,128)(2,1)S(1)}, bf16[96,2432]{1,0:T(8,128)(2,1)S(1)}, u32[]{:S(2)}, u32[]{:S(2)}) %collective-permute-start.11) | collective-permute-done | bytes 466976 | tf_op jit(solution)/shard_map/ppermute | solution.py:548
  84.3 2.0 %collective-permute-start.12 = (bf16[96,2432]{1,0:T(8,128)(2,1)S(1)}, bf16[96,2432]{1,0:T(8,128)(2,1)S(1)}, u32[]{:S(2)}, u32[]{:S(2)}) collective-permute-start(bf16[96,2432]{1,0:T(8,128)(2,1)S(1)} %get-tuple-element.79.refs_0_), channel_id=1, source_target_pairs={{1,0},{3,1},{5,3},{7,5},{6,7},{4,6},{2,4},{0,2},{9,8},{11,9},{13,1... | collective-permute-start | bytes 1400840 | tf_op jit(solution)/shard_map/ppermute | solution.py:548
  86.4 7.9 %collective-permute-done.20.refs_7_ = bf16[96,2432]{1,0:T(8,128)(2,1)S(1)} collective-permute-done((bf16[96,2432]{1,0:T(8,128)(2,1)S(1)}, bf16[96,2432]{1,0:T(8,128)(2,1)S(1)}, u32[]{:S(2)}, u32[]{:S(2)}) %collective-permute-start.20) | collective-permute-done | bytes 466976 | tf_op jit(solution)/shard_map/ppermute | solution.py:548
  94.4 1.4 collective-permute-start.28
  96.5 1.8 collective-permute-done.4.refs_2_
  99.0 5.3 %collective-permute-done.18.refs_6_ = bf16[96,2432]{1,0:T(8,128)(2,1)S(1)} collective-permute-done((bf16[96,2432]{1,0:T(8,128)(2,1)S(1)}, bf16[96,2432]{1,0:T(8,128)(2,1)S(1)}, u32[]{:S(2)}, u32[]{:S(2)}) %collective-permute-start.18) | collective-permute-done | bytes 466976 | tf_op jit(solution)/shard_map/ppermute | solution.py:548
  104.3 1.6 collective-permute-start.16
  105.9 1.6 collective-permute-start.5
  107.9 6.4 %collective-permute-done.12.refs_4_ = bf16[96,2432]{1,0:T(8,128)(2,1)S(1)} collective-permute-done((bf16[96,2432]{1,0:T(8,128)(2,1)S(1)}, bf16[96,2432]{1,0:T(8,128)(2,1)S(1)}, u32[]{:S(2)}, u32[]{:S(2)}) %collective-permute-start.12) | collective-permute-done | bytes 466976 | tf_op jit(solution)/shard_map/ppermute | solution.py:548
  114.4 6.0 %compose.3 = (bf16[8,768,768]{2,1,0:T(8,128)(2,1)S(1)}, bf16[8,96,768]{2,1,0:T(8,128)(2,1)S(1)}, bf16[2,768,768]{2,1,0:T(8,128)(2,1)S(1)}, bf16[768,768]{1,0:T(8,128)(2,1)S(1)}) custom-call(s32[1]{0:T(128)S(6)} %convert_element_type.3.last_ref, s32[1]{0:T(128)} %bitcast.place_ref, bf16[96,2560]{1,0:T(8,128)(2,1)S(1)} %copy-done.2, ...), custom_call_target="tpu_custom_call" | custom-call | flops 5435817984 | bytes 9437184 | tf_op jit(solution)/shard_map/compose/pallas_call | solution.py:258
  120.4 3.9 %collective-permute-done.19.refs_7_ = bf16[96,2432]{1,0:T(8,128)(2,1)S(1)} collective-permute-done((bf16[96,2432]{1,0:T(8,128)(2,1)S(1)}, bf16[96,2432]{1,0:T(8,128)(2,1)S(1)}, u32[]{:S(2)}, u32[]{:S(2)}) %collective-permute-start.19) | collective-permute-done | bytes 466976 | tf_op jit(solution)/shard_map/ppermute | solution.py:548
  124.3 1.6 collective-permute-start.17
  125.9 1.6 collective-permute-start.6
  127.5 4.1 %collective-permute-done.13.refs_5_ = bf16[96,2432]{1,0:T(8,128)(2,1)S(1)} collective-permute-done((bf16[96,2432]{1,0:T(8,128)(2,1)S(1)}, bf16[96,2432]{1,0:T(8,128)(2,1)S(1)}, u32[]{:S(2)}, u32[]{:S(2)}) %collective-permute-start.13) | collective-permute-done | bytes 466976 | tf_op jit(solution)/shard_map/ppermute | solution.py:548
  131.8 7.6 %compose.4 = (bf16[8,768,768]{2,1,0:T(8,128)(2,1)S(1)}, bf16[8,96,768]{2,1,0:T(8,128)(2,1)S(1)}, bf16[2,768,768]{2,1,0:T(8,128)(2,1)S(1)}, bf16[768,768]{1,0:T(8,128)(2,1)S(1)}) custom-call(s32[1]{0:T(128)S(6)} %convert_element_type.3.last_ref, s32[1]{0:T(128)} %bitcast.place_ref, ...), custom_call_target="tpu_custom_call", output_to_operand_aliasing={{0}: (11, {}), {1}: (12, {})} | custom-call | flops 5435817984 | bytes 9437184 | tf_op jit(solution)/shard_map/compose/pallas_call | solution.py:258
  139.4 2.7 %collective-permute-done.6.refs_2_ = bf16[96,2432]{1,0:T(8,128)(2,1)S(1)} collective-permute-done((bf16[96,2432]{1,0:T(8,128)(2,1)S(1)}, bf16[96,2432]{1,0:T(8,128)(2,1)S(1)}, u32[]{:S(2)}, u32[]{:S(2)}) %collective-permute-start.6) | collective-permute-done | bytes 466976 | tf_op jit(solution)/shard_map/ppermute | solution.py:548
  142.1 1.2 collective-permute-start.7
  144.1 6.6 %compose.5 = (bf16[8,768,768]{2,1,0:T(8,128)(2,1)S(1)}, bf16[8,96,768]{2,1,0:T(8,128)(2,1)S(1)}, bf16[2,768,768]{2,1,0:T(8,128)(2,1)S(1)}, bf16[768,768]{1,0:T(8,128)(2,1)S(1)}) custom-call(s32[1]{0:T(128)S(6)} %convert_element_type.3.last_ref, s32[1]{0:T(128)} %bitcast.place_ref, ...), custom_call_target="tpu_custom_call", output_to_operand_aliasing={{0}: (11, {}), {1}: (12, {})} | custom-call | flops 5435817984 | bytes 9437184 | tf_op jit(solution)/shard_map/compose/pallas_call | solution.py:258
  151.8 5.0 %chain.1 = (bf16[2,768,768]{2,1,0:T(8,128)(2,1)S(1)}, bf16[2,768,768]{2,1,0:T(8,128)(2,1)S(1)}, bf16[6,256,256]{2,1,0:T(8,128)(2,1)S(1)}) custom-call(s32[1]{0:T(128)} %bitcast.place_ref, bf16[96,2432]{1,0:T(8,128)(2,1)S(1)} %get-tuple-element.79.refs_0_, bf16[96,2432]{1,0:T(8,128)(2,1)S(1)} %collective-permute-done.5.refs_1_, ...), custom_call_target="tpu_custom_call" | custom-call | flops 3623878656 | bytes 9437184 | tf_op jit(solution)/shard_map/chain/pallas_call | solution.py:312
  156.8 1.0 collective-permute-start.31
  157.8 2.3 %extend_factors.1 = (bf16[8,768,768]{2,1,0:T(8,128)(2,1)S(1)}, bf16[8,96,768]{2,1,0:T(8,128)(2,1)S(1)}) custom-call(s32[1]{0:T(128)} %bitcast.place_ref, bf16[2,768,768]{2,1,0:T(8,128)(2,1)S(1)} %get-tuple-element.124.gain_ref, bf16[8,768,768]{2,1,0:T(8,128)(2,1)S(1)} %get-tuple-element.125.factor_in, ...), custom_call_target="tpu_custom_call", output_to_operand_aliasing={{0}: (2, {}), {1}: (3, {})} | custom-call | flops 1811939328 | bytes 4718592 | tf_op jit(solution)/shard_map/extend_factors/pallas_call | solution.py:351
  160.1 1.8 hop.2
  162.6 4.4 %own_rows.1.own_ref = f32[8,96,768]{2,1,0:T(8,128)S(1)} custom-call(s32[1]{0:T(128)} %bitcast.place_ref, bf16[2,768,768]{2,1,0:T(8,128)(2,1)S(1)} %get-tuple-element.133.half_ref.refs_0_, bf16[2,768,768]{2,1,0:T(8,128)(2,1)S(1)} %get-tuple-element.134.refs_1_, bf16[2,768,768]{2,1,0:T(8,128)(2,1)S(1)} %get-tuple-element.135.refs_2_, ...), custom_call_target="tpu_custom_call" | custom-call | flops 905969664 | bytes 9437184 | tf_op jit(solution)/shard_map/own_rows/pallas_call | solution.py:390
  167.0 1.8 hop.3
  168.9 1.3 collective-permute-start.33
  170.2 11.3 %collective-permute-done.33.refs_2_ = bf16[6,256,256]{2,1,0:T(8,128)(2,1)S(1)} collective-permute-done((bf16[6,256,256]{2,1,0:T(8,128)(2,1)S(1)}, bf16[6,256,256]{2,1,0:T(8,128)(2,1)S(1)}, u32[]{:S(2)}, u32[]{:S(2)}) %collective-permute-start.33) | collective-permute-done | bytes 786464 | tf_op jit(solution)/shard_map/ppermute | solution.py:607
  181.4 5.6 %finish.1 = f32[8,96,768]{2,1,0:T(8,128)} custom-call(bf16[8,768,768]{2,1,0:T(8,128)(2,1)S(1)} %get-tuple-element.127.factor_ref, f32[8,96,768]{2,1,0:T(8,128)S(1)} %own_rows.1.own_ref, bf16[8,96,768]{2,1,0:T(8,128)(2,1)S(1)} %get-tuple-element.138.mine_ref, bf16[6,256,256]{2,1,0:T(8,128)(2,1)S(1)} %collective-permute-done.31.refs_0_, ...), custom_call_target="tpu_custom_call" | custom-call | tf_op jit(solution)/shard_map/finish/pallas_call | solution.py:507
  (41 shorter events, 7.3 us)
Async XLA Ops:
  2.3 47.8 %copy-start = (f32[8,96,768]{2,1,0:T(8,128)S(1)}, f32[8,96,768]{2,1,0:T(8,128)}, u32[]{:S(2)}) copy-start(f32[8,96,768]{2,1,0:T(8,128)} %increment_ref.5) | copy-start | bytes 7077892
  2.3 47.8 %copy-start.1 = (bf16[8,96,768]{2,1,0:T(8,128)(2,1)S(1)}, bf16[8,96,768]{2,1,0:T(8,128)(2,1)}, u32[]{:S(2)}) copy-start(bf16[8,96,768]{2,1,0:T(8,128)(2,1)} %gain_ref.5) | copy-start | bytes 3538948
  2.3 14.8 %collective-permute-start = (bf16[96,2432]{1,0:T(8,128)(2,1)}, bf16[96,2432]{1,0:T(8,128)(2,1)S(1)}, u32[]{:S(2)}, u32[]{:S(2)}) collective-permute-start(bf16[96,2432]{1,0:T(8,128)(2,1)} %pack.4.refs_0_), channel_id=1, source_target_pairs={{1,3},{3,5},{5,7},{7,6},{6,4},{4,2},{2,0},{0,1},{9,11},{11,13},{13... | collective-permute-start | bytes 1400840 | tf_op jit(solution)/shard_map/ppermute | solution.py:548
  5.2 13.9 %collective-permute-start.8 = (bf16[96,2432]{1,0:T(8,128)(2,1)}, bf16[96,2432]{1,0:T(8,128)(2,1)}, u32[]{:S(2)}, u32[]{:S(2)}) collective-permute-start(bf16[96,2432]{1,0:T(8,128)(2,1)} %pack.4.refs_0_), channel_id=1, source_target_pairs={{1,0},{3,1},{5,3},{7,5},{6,7},{4,6},{2,4},{0,2},{9,8},{11,9},{13,1... | collective-permute-start | bytes 1400840 | tf_op jit(solution)/shard_map/ppermute | solution.py:548
  7.9 86.3 %copy-start.2 = (bf16[96,2560]{1,0:T(8,128)(2,1)S(1)}, bf16[96,2560]{1,0:T(8,128)(2,1)}, u32[]{:S(2)}) copy-start(bf16[96,2560]{1,0:T(8,128)(2,1)} %pack.5.refs_0_) | copy-start | bytes 1474564
  7.9 19.6 %collective-permute-start.21 = (bf16[96,2560]{1,0:T(8,128)(2,1)}, bf16[96,2560]{1,0:T(8,128)(2,1)S(1)}, u32[]{:S(2)}, u32[]{:S(2)}) collective-permute-start(bf16[96,2560]{1,0:T(8,128)(2,1)} %pack.5.refs_0_), channel_id=1, source_target_pairs={{1,3},{3,5},{5,7},{7,6},{6,4},{4,2},{2,0},{0,1},{9,11},{11,13},{13... | collective-permute-start | bytes 1474568 | tf_op jit(solution)/shard_map/ppermute | solution.py:548
  17.0 20.5 %collective-permute-start.1 = (bf16[96,2432]{1,0:T(8,128)(2,1)S(1)}, bf16[96,2432]{1,0:T(8,128)(2,1)S(1)}, u32[]{:S(2)}, u32[]{:S(2)}) collective-permute-start(bf16[96,2432]{1,0:T(8,128)(2,1)S(1)} %collective-permute-done.refs_1_), channel_id=1, source_target_pairs={{1,3},{3,5},{5,7},{7,6},{6,4},{4,2},{2,0},{0,1},{9,11},{11,13},{13... | collective-permute-start | bytes 1400840 | tf_op jit(solution)/shard_map/ppermute | solution.py:548
  19.0 20.5 %collective-permute-start.25 = (bf16[96,2560]{1,0:T(8,128)(2,1)}, bf16[96,2560]{1,0:T(8,128)(2,1)S(1)}, u32[]{:S(2)}, u32[]{:S(2)}) collective-permute-start(bf16[96,2560]{1,0:T(8,128)(2,1)} %pack.5.refs_0_), channel_id=1, source_target_pairs={{1,0},{3,1},{5,3},{7,5},{6,7},{4,6},{2,4},{0,2},{9,8},{11,9},{13,1... | collective-permute-start | bytes 1474568 | tf_op jit(solution)/shard_map/ppermute | solution.py:548
  19.1 21.2 %collective-permute-start.9 = (bf16[96,2432]{1,0:T(8,128)(2,1)}, bf16[96,2432]{1,0:T(8,128)(2,1)S(1)}, u32[]{:S(2)}, u32[]{:S(2)}) collective-permute-start(bf16[96,2432]{1,0:T(8,128)(2,1)} %collective-permute-done.8.refs_4_), channel_id=1, source_target_pairs={{1,0},{3,1},{5,3},{7,5},{6,7},{4,6},{2,4},{0,2},{9,8},{11,9},{13,1... | collective-permute-start | bytes 1400840 | tf_op jit(solution)/shard_map/ppermute | solution.py:548
  27.6 20.5 %collective-permute-start.22 = (bf16[96,2560]{1,0:T(8,128)(2,1)S(1)}, bf16[96,2560]{1,0:T(8,128)(2,1)S(1)}, u32[]{:S(2)}, u32[]{:S(2)}) collective-permute-start(bf16[96,2560]{1,0:T(8,128)(2,1)S(1)} %collective-permute-done.21.refs_1_), channel_id=1, source_target_pairs={{1,3},{3,5},{5,7},{7,6},{6,4},{4,2},{2,0},{0,1},{9,11},{11,13},{13... | collective-permute-start | bytes 1474568 | tf_op jit(solution)/shard_map/ppermute | solution.py:548
  37.6 20.5 %collective-permute-start.2 = (bf16[96,2432]{1,0:T(8,128)(2,1)S(1)}, bf16[96,2432]{1,0:T(8,128)(2,1)S(1)}, u32[]{:S(2)}, u32[]{:S(2)}) collective-permute-start(bf16[96,2432]{1,0:T(8,128)(2,1)S(1)} %collective-permute-done.1.refs_2_), channel_id=1, source_target_pairs={{1,3},{3,5},{5,7},{7,6},{6,4},{4,2},{2,0},{0,1},{9,11},{11,13},{13... | collective-permute-start | bytes 1400840 | tf_op jit(solution)/shard_map/ppermute | solution.py:548
  39.6 20.5 %collective-permute-start.26 = (bf16[96,2560]{1,0:T(8,128)(2,1)S(1)}, bf16[96,2560]{1,0:T(8,128)(2,1)S(1)}, u32[]{:S(2)}, u32[]{:S(2)}) collective-permute-start(bf16[96,2560]{1,0:T(8,128)(2,1)S(1)} %collective-permute-done.25.refs_5_), channel_id=1, source_target_pairs={{1,0},{3,1},{5,3},{7,5},{6,7},{4,6},{2,4},{0,2},{9,8},{11,9},{13,1... | collective-permute-start | bytes 1474568 | tf_op jit(solution)/shard_map/ppermute | solution.py:548
  40.3 20.5 %collective-permute-start.10 = (bf16[96,2432]{1,0:T(8,128)(2,1)S(1)}, bf16[96,2432]{1,0:T(8,128)(2,1)S(1)}, u32[]{:S(2)}, u32[]{:S(2)}) collective-permute-start(bf16[96,2432]{1,0:T(8,128)(2,1)S(1)} %collective-permute-done.9.refs_5_), channel_id=1, source_target_pairs={{1,0},{3,1},{5,3},{7,5},{6,7},{4,6},{2,4},{0,2},{9,8},{11,9},{13,1... | collective-permute-start | bytes 1400840 | tf_op jit(solution)/shard_map/ppermute | solution.py:548
  48.1 20.5 %collective-permute-start.23 = (bf16[96,2560]{1,0:T(8,128)(2,1)S(1)}, bf16[96,2560]{1,0:T(8,128)(2,1)S(1)}, u32[]{:S(2)}, u32[]{:S(2)}) collective-permute-start(bf16[96,2560]{1,0:T(8,128)(2,1)S(1)} %collective-permute-done.22.refs_2_), channel_id=1, source_target_pairs={{1,3},{3,5},{5,7},{7,6},{6,4},{4,2},{2,0},{0,1},{9,11},{11,13},{13... | collective-permute-start | bytes 1474568 | tf_op jit(solution)/shard_map/ppermute | solution.py:548
  58.1 20.5 %collective-permute-start.3 = (bf16[96,2432]{1,0:T(8,128)(2,1)S(1)}, bf16[96,2432]{1,0:T(8,128)(2,1)S(1)}, u32[]{:S(2)}, u32[]{:S(2)}) collective-permute-start(bf16[96,2432]{1,0:T(8,128)(2,1)S(1)} %get-tuple-element.83.refs_0_), channel_id=1, source_target_pairs={{1,3},{3,5},{5,7},{7,6},{6,4},{4,2},{2,0},{0,1},{9,11},{11,13},{13... | collective-permute-start | bytes 1400840 | tf_op jit(solution)/shard_map/ppermute | solution.py:548
  60.1 24.2 %collective-permute-start.27 = (bf16[96,2560]{1,0:T(8,128)(2,1)S(1)}, bf16[96,2560]{1,0:T(8,128)(2,1)S(1)}, u32[]{:S(2)}, u32[]{:S(2)}) collective-permute-start(bf16[96,2560]{1,0:T(8,128)(2,1)S(1)} %collective-permute-done.26.refs_6_), channel_id=1, source_target_pairs={{1,0},{3,1},{5,3},{7,5},{6,7},{4,6},{2,4},{0,2},{9,8},{11,9},{13,1... | collective-permute-start | bytes 1474568 | tf_op jit(solution)/shard_map/ppermute | solution.py:548
  60.8 23.5 %collective-permute-start.11 = (bf16[96,2432]{1,0:T(8,128)(2,1)S(1)}, bf16[96,2432]{1,0:T(8,128)(2,1)S(1)}, u32[]{:S(2)}, u32[]{:S(2)}) collective-permute-start(bf16[96,2432]{1,0:T(8,128)(2,1)S(1)} %get-tuple-element.83.refs_0_), channel_id=1, source_target_pairs={{1,0},{3,1},{5,3},{7,5},{6,7},{4,6},{2,4},{0,2},{9,8},{11,9},{13,1... | collective-permute-start | bytes 1400840 | tf_op jit(solution)/shard_map/ppermute | solution.py:548
  68.6 25.6 %collective-permute-start.24 = (bf16[96,2560]{1,0:T(8,128)(2,1)S(1)}, bf16[96,2560]{1,0:T(8,128)(2,1)S(1)}, u32[]{:S(2)}, u32[]{:S(2)}) collective-permute-start(bf16[96,2560]{1,0:T(8,128)(2,1)S(1)} %collective-permute-done.23.refs_3_), channel_id=1, source_target_pairs={{1,3},{3,5},{5,7},{7,6},{6,4},{4,2},{2,0},{0,1},{9,11},{11,13},{13... | collective-permute-start | bytes 1474568 | tf_op jit(solution)/shard_map/ppermute | solution.py:548
  70.6 23.6 %collective-permute-start.20 = (bf16[96,2432]{1,0:T(8,128)(2,1)S(1)}, bf16[96,2432]{1,0:T(8,128)(2,1)S(1)}, u32[]{:S(2)}, u32[]{:S(2)}) collective-permute-start(bf16[96,2432]{1,0:T(8,128)(2,1)S(1)} %collective-permute-done.10.refs_6_), channel_id=1, source_target_pairs={{1,0},{3,1},{5,3},{7,5},{6,7},{4,6},{2,4},{0,2},{9,8},{11,9},{13,1... | collective-permute-start | bytes 1400840 | tf_op jit(solution)/shard_map/ppermute | solution.py:548
  78.6 19.7 %collective-permute-start.4 = (bf16[96,2432]{1,0:T(8,128)(2,1)S(1)}, bf16[96,2432]{1,0:T(8,128)(2,1)S(1)}, u32[]{:S(2)}, u32[]{:S(2)}) collective-permute-start(bf16[96,2432]{1,0:T(8,128)(2,1)S(1)} %collective-permute-done.3.refs_1_), channel_id=1, source_target_pairs={{1,3},{3,5},{5,7},{7,6},{6,4},{4,2},{2,0},{0,1},{9,11},{11,13},{13... | collective-permute-start | bytes 1400840 | tf_op jit(solution)/shard_map/ppermute | solution.py:548
  84.3 20.0 %collective-permute-start.18 = (bf16[96,2432]{1,0:T(8,128)(2,1)S(1)}, bf16[96,2432]{1,0:T(8,128)(2,1)S(1)}, u32[]{:S(2)}, u32[]{:S(2)}) collective-permute-start(bf16[96,2432]{1,0:T(8,128)(2,1)S(1)} %collective-permute-done.11.refs_5_), channel_id=1, source_target_pairs={{1,0},{3,1},{5,3},{7,5},{6,7},{4,6},{2,4},{0,2},{9,8},{11,9},{13,1... | collective-permute-start | bytes 1400840 | tf_op jit(solution)/shard_map/ppermute | solution.py:548
  84.3 29.9 %collective-permute-start.12 = (bf16[96,2432]{1,0:T(8,128)(2,1)S(1)}, bf16[96,2432]{1,0:T(8,128)(2,1)S(1)}, u32[]{:S(2)}, u32[]{:S(2)}) collective-permute-start(bf16[96,2432]{1,0:T(8,128)(2,1)S(1)} %get-tuple-element.79.refs_0_), channel_id=1, source_target_pairs={{1,0},{3,1},{5,3},{7,5},{6,7},{4,6},{2,4},{0,2},{9,8},{11,9},{13,1... | collective-permute-start | bytes 1400840 | tf_op jit(solution)/shard_map/ppermute | solution.py:548
  94.4 37.4 %copy-start.3 = (bf16[96,2432]{1,0:T(8,128)(2,1)S(1)}, bf16[96,2432]{1,0:T(8,128)(2,1)}, u32[]{:S(2)}) copy-start(bf16[96,2432]{1,0:T(8,128)(2,1)} %pack.4.refs_0_) | copy-start | bytes 1400836
  94.4 11.4 %collective-permute-start.28 = (bf16[8,96,128]{2,1,0:T(8,128)(2,1)S(1)}, bf16[8,96,128]{2,1,0:T(8,128)(2,1)S(1)}, u32[]{:S(2)}, u32[]{:S(2)}) collective-permute-start(bf16[8,96,128]{2,1,0:T(8,128)(2,1)S(1)} %collect.1.refs_11_), channel_id=1, source_target_pairs={{0,24},{1,25},{2,26},{3,27},{4,28},{5,29},{6,30},{7,31}} | collective-permute-start | bytes 589832 | tf_op jit(solution)/shard_map/ppermute | solution.py:585
  95.9 11.6 %collective-permute-start.29 = (bf16[8,96,128]{2,1,0:T(8,128)(2,1)S(1)}, bf16[8,96,128]{2,1,0:T(8,128)(2,1)S(1)}, u32[]{:S(2)}, u32[]{:S(2)}) collective-permute-start(bf16[8,96,128]{2,1,0:T(8,128)(2,1)S(1)} %collect.1.refs_11_), channel_id=1, source_target_pairs={{8,24},{9,25},{10,26},{11,27},{12,28},{13,29},{14,30},{15,31}} | collective-permute-start | bytes 589832 | tf_op jit(solution)/shard_map/ppermute | solution.py:585
  98.4 16.0 %collective-permute-start.30 = (bf16[8,96,128]{2,1,0:T(8,128)(2,1)S(1)}, bf16[8,96,128]{2,1,0:T(8,128)(2,1)S(1)}, u32[]{:S(2)}, u32[]{:S(2)}) collective-permute-start(bf16[8,96,128]{2,1,0:T(8,128)(2,1)S(1)} %collect.1.refs_11_), channel_id=1, source_target_pairs={{16,24},{17,25},{18,26},{19,27},{20,28},{21,29},{22,30},{23,31}} | collective-permute-start | bytes 589832 | tf_op jit(solution)/shard_map/ppermute | solution.py:585
  104.3 16.1 %collective-permute-start.16 = (bf16[96,2432]{1,0:T(8,128)(2,1)S(1)}, bf16[96,2432]{1,0:T(8,128)(2,1)S(1)}, u32[]{:S(2)}, u32[]{:S(2)}) collective-permute-start(bf16[96,2432]{1,0:T(8,128)(2,1)S(1)} %collective-permute-done.4.refs_2_), channel_id=1, source_target_pairs={{1,3},{3,5},{5,7},{7,6},{6,4},{4,2},{2,0},{0,1},{9,11},{11,13},{13... | collective-permute-start | bytes 1400840 | tf_op jit(solution)/shard_map/ppermute | solution.py:548
  105.9 20.0 %collective-permute-start.5 = (bf16[96,2432]{1,0:T(8,128)(2,1)S(1)}, bf16[96,2432]{1,0:T(8,128)(2,1)S(1)}, u32[]{:S(2)}, u32[]{:S(2)}) collective-permute-start(bf16[96,2432]{1,0:T(8,128)(2,1)S(1)} %get-tuple-element.79.refs_0_), channel_id=1, source_target_pairs={{1,3},{3,5},{5,7},{7,6},{6,4},{4,2},{2,0},{0,1},{9,11},{11,13},{13... | collective-permute-start | bytes 1400840 | tf_op jit(solution)/shard_map/ppermute | solution.py:548
  107.4 16.9 %collective-permute-start.19 = (bf16[96,2432]{1,0:T(8,128)(2,1)S(1)}, bf16[96,2432]{1,0:T(8,128)(2,1)S(1)}, u32[]{:S(2)}, u32[]{:S(2)}) collective-permute-start(bf16[96,2432]{1,0:T(8,128)(2,1)S(1)} %collective-permute-done.18.refs_6_), channel_id=1, source_target_pairs={{1,0},{3,1},{5,3},{7,5},{6,7},{4,6},{2,4},{0,2},{9,8},{11,9},{13,1... | collective-permute-start | bytes 1400840 | tf_op jit(solution)/shard_map/ppermute | solution.py:548
  114.3 17.2 %collective-permute-start.13 = (bf16[96,2432]{1,0:T(8,128)(2,1)S(1)}, bf16[96,2432]{1,0:T(8,128)(2,1)S(1)}, u32[]{:S(2)}, u32[]{:S(2)}) collective-permute-start(bf16[96,2432]{1,0:T(8,128)(2,1)S(1)} %collective-permute-done.12.refs_4_), channel_id=1, source_target_pairs={{1,0},{3,1},{5,3},{7,5},{6,7},{4,6},{2,4},{0,2},{9,8},{11,9},{13,1... | collective-permute-start | bytes 1400840 | tf_op jit(solution)/shard_map/ppermute | solution.py:548
  124.3 15.1 %collective-permute-start.17 = (bf16[96,2432]{1,0:T(8,128)(2,1)S(1)}, bf16[96,2432]{1,0:T(8,128)(2,1)S(1)}, u32[]{:S(2)}, u32[]{:S(2)}) collective-permute-start(bf16[96,2432]{1,0:T(8,128)(2,1)S(1)} %collective-permute-done.16.refs_3_), channel_id=1, source_target_pairs={{1,3},{3,5},{5,7},{7,6},{6,4},{4,2},{2,0},{0,1},{9,11},{11,13},{13... | collective-permute-start | bytes 1400840 | tf_op jit(solution)/shard_map/ppermute | solution.py:548
  125.9 16.2 %collective-permute-start.6 = (bf16[96,2432]{1,0:T(8,128)(2,1)S(1)}, bf16[96,2432]{1,0:T(8,128)(2,1)S(1)}, u32[]{:S(2)}, u32[]{:S(2)}) collective-permute-start(bf16[96,2432]{1,0:T(8,128)(2,1)S(1)} %collective-permute-done.5.refs_1_), channel_id=1, source_target_pairs={{1,3},{3,5},{5,7},{7,6},{6,4},{4,2},{2,0},{0,1},{9,11},{11,13},{13... | collective-permute-start | bytes 1400840 | tf_op jit(solution)/shard_map/ppermute | solution.py:548
  131.5 10.6 %collective-permute-start.14 = (bf16[96,2432]{1,0:T(8,128)(2,1)S(1)}, bf16[96,2432]{1,0:T(8,128)(2,1)S(1)}, u32[]{:S(2)}, u32[]{:S(2)}) collective-permute-start(bf16[96,2432]{1,0:T(8,128)(2,1)S(1)} %collective-permute-done.13.refs_5_), channel_id=1, source_target_pairs={{1,0},{3,1},{5,3},{7,5},{6,7},{4,6},{2,4},{0,2},{9,8},{11,9},{13,1... | collective-permute-start | bytes 1400840 | tf_op jit(solution)/shard_map/ppermute | solution.py:548
  142.1 8.9 %collective-permute-start.7 = (bf16[96,2432]{1,0:T(8,128)(2,1)S(1)}, bf16[96,2432]{1,0:T(8,128)(2,1)S(1)}, u32[]{:S(2)}, u32[]{:S(2)}) collective-permute-start(bf16[96,2432]{1,0:T(8,128)(2,1)S(1)} %collective-permute-done.6.refs_2_), channel_id=1, source_target_pairs={{1,3},{3,5},{5,7},{7,6},{6,4},{4,2},{2,0},{0,1},{9,11},{11,13},{13... | collective-permute-start | bytes 1400840 | tf_op jit(solution)/shard_map/ppermute | solution.py:548
  143.3 8.6 %collective-permute-start.15 = (bf16[96,2432]{1,0:T(8,128)(2,1)S(1)}, bf16[96,2432]{1,0:T(8,128)(2,1)S(1)}, u32[]{:S(2)}, u32[]{:S(2)}) collective-permute-start(bf16[96,2432]{1,0:T(8,128)(2,1)S(1)} %collective-permute-done.14.refs_6_), channel_id=1, source_target_pairs={{1,0},{3,1},{5,3},{7,5},{6,7},{4,6},{2,4},{0,2},{9,8},{11,9},{13,1... | collective-permute-start | bytes 1400840 | tf_op jit(solution)/shard_map/ppermute | solution.py:548
  156.8 3.3 %collective-permute-start.31 = (bf16[6,256,256]{2,1,0:T(8,128)(2,1)S(1)}, bf16[6,256,256]{2,1,0:T(8,128)(2,1)S(1)}, u32[]{:S(2)}, u32[]{:S(2)}) collective-permute-start(bf16[6,256,256]{2,1,0:T(8,128)(2,1)S(1)} %get-tuple-element.128), channel_id=1, source_target_pairs={{24,16},{25,17},{26,18},{27,19},{28,20},{29,21},{30,22},{31,23}} | collective-permute-start | bytes 2359304 | tf_op jit(solution)/shard_map/ppermute | solution.py:607
  161.9 5.1 %collective-permute-start.32 = (bf16[6,256,256]{2,1,0:T(8,128)(2,1)S(1)}, bf16[6,256,256]{2,1,0:T(8,128)(2,1)S(1)}, u32[]{:S(2)}, u32[]{:S(2)}) collective-permute-start(bf16[6,256,256]{2,1,0:T(8,128)(2,1)S(1)} %hop.2), channel_id=1, source_target_pairs={{16,8},{17,9},{18,10},{19,11},{20,12},{21,13},{22,14},{23,15}} | collective-permute-start | bytes 2359304 | tf_op jit(solution)/shard_map/ppermute | solution.py:607
  168.9 12.6 %collective-permute-start.33 = (bf16[6,256,256]{2,1,0:T(8,128)(2,1)S(1)}, bf16[6,256,256]{2,1,0:T(8,128)(2,1)S(1)}, u32[]{:S(2)}, u32[]{:S(2)}) collective-permute-start(bf16[6,256,256]{2,1,0:T(8,128)(2,1)S(1)} %hop.3), channel_id=1, source_target_pairs={{8,0},{9,1},{10,2},{11,3},{12,4},{13,5},{14,6},{15,7}} | collective-permute-start | bytes 2359304 | tf_op jit(solution)/shard_map/ppermute | solution.py:607

commit v17 on v16

--- a/solution.py
+++ b/solution.py
@@ -143,14 +143,15 @@
     unpack(raw, extras, step, fresh)
 
 
-def advance(gain, half, fresh, middle):
+def advance(gain, half, fresh, middle, out=None):
+    out = half if out is None else out
     width = half.shape[0]
     for j in range(0, width, TILE):
         cols = slice(j, j + TILE)
         middle[:, cols] = jnp.dot(gain[...], half[:, cols], preferred_element_type=F32).astype(BF16)
     for j in range(0, width, TILE):
         cols = slice(j, j + TILE)
-        half[:, cols] = (nt(middle[...], gain[cols, :]) + fresh[:, cols].astype(F32)).astype(BF16)
+        out[:, cols] = (nt(middle[...], gain[cols, :]) + fresh[:, cols].astype(F32)).astype(BF16)
 
 
 def extend(gain, factor):
@@ -283,47 +284,38 @@
     count = len(cycle)
     places = origins(place_ref[0], cycle, right)
     blocks, refs = refs[:count], refs[count:]
-    half_in, refs = refs[0], refs[1:]
-    gain_out, half_out, packed_out, half, middle, raw, extras, gain, fresh, spare = refs
-    gains, freshes = (gain, spare.at[0]), (fresh, spare.at[1])
+    half, gain_out, half_out, packed_out, middle, raw, extras, fresh = refs
+    prepare(places, blocks, turns - 1, turns, gain_out.at[turns - 1], fresh.at[0], raw, extras)
     for turn in range(turns):
-
-        @pl.when(pl.program_id(0) == turn)
-        def _():
-            now = turn % 2
-            if turn == 0:
-                half[...] = half_in[...]
-                prepare(places, blocks, turns - 1, turns, gains[0], freshes[0], raw, extras)
-            gain_out[0] = gains[now][...]
-            if turn + 1 < turns:
-                prepare(places, blocks, turns - 2 - turn, turns, gains[1 - now], freshes[1 - now], raw, extras)
-            advance(gains[now], half, freshes[now], middle)
-            half_out[0] = half[...]
-            if turn == turns - 1:
-                fold(half, packed_out)
+        step = turns - 1 - turn
+        if step:
+            prepare(places, blocks, step - 1, turns, gain_out.at[step - 1], fresh.at[(turn + 1) % 2], raw, extras)
+        advance(gain_out.at[step], half, fresh.at[turn % 2], middle, half_out.at[step])
+        half = half_out.at[step]
+    fold(half, packed_out)
 
 
 def chain(place, cycle, right, blocks, half, turns):
     count = len(blocks)
     rows = blocks[0].shape[0]
     width = rows * count
-    in_specs = row_specs(blocks) + [square(width)]
-    whole = square(width, lambda i: turns - 1 - i)
+    vmem = pl.BlockSpec(memory_space=pltpu.VMEM)
     return pl.pallas_call(
         functools.partial(chain_kernel, cycle, right, turns),
-        grid_spec=pltpu.PrefetchScalarGridSpec(
-            num_scalar_prefetch=1,
-            grid=(turns,),
-            in_specs=in_specs,
-            out_specs=[whole, whole, pl.BlockSpec(blocks_shape(width), lambda i, *p: (0, 0, 0))],
-            scratch_shapes=[pltpu.VMEM((width, width), BF16)] + row_scratch(count, rows),
-        ),
+        in_specs=[pl.BlockSpec(memory_space=pltpu.SMEM)] + [vmem] * (count + 1),
+        out_specs=[vmem] * 3,
         out_shape=[
             jax.ShapeDtypeStruct((turns, width, width), BF16),
             jax.ShapeDtypeStruct((turns, width, width), BF16),
             jax.ShapeDtypeStruct(blocks_shape(width), BF16),
         ],
-        compiler_params=pltpu.CompilerParams(vmem_limit_bytes=18 * MIB),
+        scratch_shapes=[
+            pltpu.VMEM((width, width), BF16),
+            pltpu.VMEM((count, rows, width // 2), BF16),
+            pltpu.VMEM((count, rows, LANES), BF16),
+            pltpu.VMEM((2, width, width), BF16),
+        ],
+        compiler_params=pltpu.CompilerParams(vmem_limit_bytes=26 * MIB),
         cost_estimate=pl.CostEstimate(
             flops=4 * turns * width**3, bytes_accessed=8 * turns * width * width, transcendentals=0
         ),
@@ -454,17 +446,14 @@
 
 def hop(factors, halves, packed):
     width = halves.shape[1]
-    shape = blocks_shape(width)
-    blocks = pl.BlockSpec(shape, lambda i: (0, 0, 0), pipeline_mode=pl.Buffered(1))
-    whole = pl.BlockSpec((1, width, width), lambda i: (0, 0, 0), pipeline_mode=pl.Buffered(1))
+    vmem = pl.BlockSpec(memory_space=pltpu.VMEM)
     return pl.pallas_call(
         functools.partial(hop_kernel, len(packed)),
-        grid=(1,),
-        in_specs=[whole, whole] + [blocks] * len(packed),
-        out_specs=blocks,
-        out_shape=jax.ShapeDtypeStruct(shape, BF16),
+        in_specs=[vmem] * (2 + len(packed)),
+        out_specs=vmem,
+        out_shape=jax.ShapeDtypeStruct(blocks_shape(width), BF16),
         scratch_shapes=[pltpu.VMEM((width, width), BF16)] * 3,
-        compiler_params=pltpu.CompilerParams(vmem_limit_bytes=16 * MIB),
+        compiler_params=pltpu.CompilerParams(vmem_limit_bytes=24 * MIB),
         cost_estimate=pl.CostEstimate(flops=4 * width**3, bytes_accessed=10 * width * width, transcendentals=0),
         name="hop",
     )(factors, halves, *packed)

time: 187 us -> 187 us (level)
  no operation moved by 1% of the time
where the time goes in v17:
time: 187 us; the launch traced here: 186 us
  waiting for transfers between devices  99.1 us (53%)
  Pallas kernels  46.1 us (25%)
  starting transfers between devices  41 us (22%)
    ppermute x28, waiting for transfers between devices, passed(): lax.ppermute(array, 'tile', [(cycle[n], cycle[(n + way) % count]) for n i...  87.8 us
    ppermute x28, starting transfers between devices, passed(): lax.ppermute(array, 'tile', [(cycle[n], cycle[(n + way) % count]) for n i...  35.3 us
    pallas_call x3, Pallas kernels, compose(): pl.pallas_call(functools.partial(compose_kernel, cycle, right, turns, fir...  20.2 us
    ppermute x3, waiting for transfers between devices, local(): packed.append(lax.ppermute(before, 'tm', [(turn, turn - 1)]))  11.3 us
    pallas_call x3, Pallas kernels, pack(): pl.pallas_call(functools.partial(pack_kernel, count, ranges), grid_spec=p...  5.57 us
    pallas_call x1, Pallas kernels, finish(): pl.pallas_call(functools.partial(finish_kernel, len(packed)), grid=(steps...  5.56 us
    pallas_call x1, Pallas kernels, own_rows(): pl.pallas_call(functools.partial(rows_kernel, size), grid_spec=pltpu.Pref...  4.39 us
    pallas_call x1, Pallas kernels, chain(): pl.pallas_call(functools.partial(chain_kernel, cycle, right, turns), in_s...  4.35 us
  transfers between devices with their start and end apart: 34, of which 20 were waited for; matrix products, arithmetic and copies ran while one was open for 0% of the time, Pallas kernels for 16%

profile of v17, /device:TPU:0, one launch (start us, length us, event | category | flops | bytes accessed | tf_op | source)
XLA Modules:
  0.0 186.4 jit_solution(481252551675929304)
XLA Ops:
  0.0 2.3 %pack.4.refs_0_ = bf16[96,2432]{1,0:T(8,128)(2,1)} custom-call(s32[1]{0:T(128)} %bitcast.place_ref, s32[1]{0:T(128)} %bitcast.1.block_ref, bf16[8,96,768]{2,1,0:T(8,128)(2,1)} %gain_ref.5, f32[8,96,768]{2,1,0:T(8,128)} %increment_ref.5), custom_call_target="tpu_custom_call" | custom-call | tf_op jit(solution)/shard_map/pack/pallas_call | solution.py:80
  2.3 3.0 %collective-permute-start = (bf16[96,2432]{1,0:T(8,128)(2,1)}, bf16[96,2432]{1,0:T(8,128)(2,1)S(1)}, u32[]{:S(2)}, u32[]{:S(2)}) collective-permute-start(bf16[96,2432]{1,0:T(8,128)(2,1)} %pack.4.refs_0_), channel_id=1, source_target_pairs={{1,3},{3,5},{5,7},{7,6},{6,4},{4,2},{2,0},{0,1},{9,11},{11,13},{13... | collective-permute-start | bytes 1400840 | tf_op jit(solution)/shard_map/ppermute | solution.py:537
  5.3 2.6 %pack.5.refs_0_ = bf16[96,2560]{1,0:T(8,128)(2,1)} custom-call(s32[1]{0:T(128)} %bitcast.place_ref, s32[1]{0:T(128)} %bitcast.1.block_ref, bf16[8,96,768]{2,1,0:T(8,128)(2,1)} %gain_ref.5, f32[8,96,768]{2,1,0:T(8,128)} %increment_ref.5, f32[96,768]{1,0:T(8,128)} %refs_0_.1), custom_call_target="tpu_custom_call" | custom-call | tf_op jit(solution)/shard_map/pack/pallas_call | solution.py:80
  7.9 1.9 %collective-permute-start.21 = (bf16[96,2560]{1,0:T(8,128)(2,1)}, bf16[96,2560]{1,0:T(8,128)(2,1)S(1)}, u32[]{:S(2)}, u32[]{:S(2)}) collective-permute-start(bf16[96,2560]{1,0:T(8,128)(2,1)} %pack.5.refs_0_), channel_id=1, source_target_pairs={{1,3},{3,5},{5,7},{7,6},{6,4},{4,2},{2,0},{0,1},{9,11},{11,13},{13... | collective-permute-start | bytes 1474568 | tf_op jit(solution)/shard_map/ppermute | solution.py:537
  9.9 7.2 %collective-permute-done.refs_1_ = bf16[96,2432]{1,0:T(8,128)(2,1)S(1)} collective-permute-done((bf16[96,2432]{1,0:T(8,128)(2,1)}, bf16[96,2432]{1,0:T(8,128)(2,1)S(1)}, u32[]{:S(2)}, u32[]{:S(2)}) %collective-permute-start) | collective-permute-done | bytes 466976 | tf_op jit(solution)/shard_map/ppermute | solution.py:537
  17.0 2.0 %collective-permute-start.1 = (bf16[96,2432]{1,0:T(8,128)(2,1)S(1)}, bf16[96,2432]{1,0:T(8,128)(2,1)S(1)}, u32[]{:S(2)}, u32[]{:S(2)}) collective-permute-start(bf16[96,2432]{1,0:T(8,128)(2,1)S(1)} %collective-permute-done.refs_1_), channel_id=1, source_target_pairs={{1,3},{3,5},{5,7},{7,6},{6,4},{4,2},{2,0},{0,1},{9,11},{11,13},{13... | collective-permute-start | bytes 1400840 | tf_op jit(solution)/shard_map/ppermute | solution.py:537
  19.1 2.0 %collective-permute-start.9 = (bf16[96,2432]{1,0:T(8,128)(2,1)}, bf16[96,2432]{1,0:T(8,128)(2,1)S(1)}, u32[]{:S(2)}, u32[]{:S(2)}) collective-permute-start(bf16[96,2432]{1,0:T(8,128)(2,1)} %collective-permute-done.8.refs_4_), channel_id=1, source_target_pairs={{1,0},{3,1},{5,3},{7,5},{6,7},{4,6},{2,4},{0,2},{9,8},{11,9},{13,1... | collective-permute-start | bytes 1400840 | tf_op jit(solution)/shard_map/ppermute | solution.py:537
  21.1 6.4 %collective-permute-done.21.refs_1_ = bf16[96,2560]{1,0:T(8,128)(2,1)S(1)} collective-permute-done((bf16[96,2560]{1,0:T(8,128)(2,1)}, bf16[96,2560]{1,0:T(8,128)(2,1)S(1)}, u32[]{:S(2)}, u32[]{:S(2)}) %collective-permute-start.21) | collective-permute-done | bytes 491552 | tf_op jit(solution)/shard_map/ppermute | solution.py:537
  27.6 2.0 %collective-permute-start.22 = (bf16[96,2560]{1,0:T(8,128)(2,1)S(1)}, bf16[96,2560]{1,0:T(8,128)(2,1)S(1)}, u32[]{:S(2)}, u32[]{:S(2)}) collective-permute-start(bf16[96,2560]{1,0:T(8,128)(2,1)S(1)} %collective-permute-done.21.refs_1_), channel_id=1, source_target_pairs={{1,3},{3,5},{5,7},{7,6},{6,4},{4,2},{2,0},{0,1},{9,11},{11,13},{13... | collective-permute-start | bytes 1474568 | tf_op jit(solution)/shard_map/ppermute | solution.py:537
  29.6 8.0 %collective-permute-done.1.refs_2_ = bf16[96,2432]{1,0:T(8,128)(2,1)S(1)} collective-permute-done((bf16[96,2432]{1,0:T(8,128)(2,1)S(1)}, bf16[96,2432]{1,0:T(8,128)(2,1)S(1)}, u32[]{:S(2)}, u32[]{:S(2)}) %collective-permute-start.1) | collective-permute-done | bytes 466976 | tf_op jit(solution)/shard_map/ppermute | solution.py:537
  37.6 2.0 %collective-permute-start.2 = (bf16[96,2432]{1,0:T(8,128)(2,1)S(1)}, bf16[96,2432]{1,0:T(8,128)(2,1)S(1)}, u32[]{:S(2)}, u32[]{:S(2)}) collective-permute-start(bf16[96,2432]{1,0:T(8,128)(2,1)S(1)} %collective-permute-done.1.refs_2_), channel_id=1, source_target_pairs={{1,3},{3,5},{5,7},{7,6},{6,4},{4,2},{2,0},{0,1},{9,11},{11,13},{13... | collective-permute-start | bytes 1400840 | tf_op jit(solution)/shard_map/ppermute | solution.py:537
  40.3 1.4 collective-permute-start.10
  41.7 6.4 %collective-permute-done.22.refs_2_ = bf16[96,2560]{1,0:T(8,128)(2,1)S(1)} collective-permute-done((bf16[96,2560]{1,0:T(8,128)(2,1)S(1)}, bf16[96,2560]{1,0:T(8,128)(2,1)S(1)}, u32[]{:S(2)}, u32[]{:S(2)}) %collective-permute-start.22) | collective-permute-done | bytes 491552 | tf_op jit(solution)/shard_map/ppermute | solution.py:537
  48.1 2.0 %collective-permute-start.23 = (bf16[96,2560]{1,0:T(8,128)(2,1)S(1)}, bf16[96,2560]{1,0:T(8,128)(2,1)S(1)}, u32[]{:S(2)}, u32[]{:S(2)}) collective-permute-start(bf16[96,2560]{1,0:T(8,128)(2,1)S(1)} %collective-permute-done.22.refs_2_), channel_id=1, source_target_pairs={{1,3},{3,5},{5,7},{7,6},{6,4},{4,2},{2,0},{0,1},{9,11},{11,13},{13... | collective-permute-start | bytes 1474568 | tf_op jit(solution)/shard_map/ppermute | solution.py:537
  50.8 7.3 %collective-permute-done.2.refs_3_ = bf16[96,2432]{1,0:T(8,128)(2,1)S(1)} collective-permute-done((bf16[96,2432]{1,0:T(8,128)(2,1)S(1)}, bf16[96,2432]{1,0:T(8,128)(2,1)S(1)}, u32[]{:S(2)}, u32[]{:S(2)}) %collective-permute-start.2) | collective-permute-done | bytes 466976 | tf_op jit(solution)/shard_map/ppermute | solution.py:537
  58.1 2.0 %collective-permute-start.3 = (bf16[96,2432]{1,0:T(8,128)(2,1)S(1)}, bf16[96,2432]{1,0:T(8,128)(2,1)S(1)}, u32[]{:S(2)}, u32[]{:S(2)}) collective-permute-start(bf16[96,2432]{1,0:T(8,128)(2,1)S(1)} %get-tuple-element.83.refs_0_), channel_id=1, source_target_pairs={{1,3},{3,5},{5,7},{7,6},{6,4},{4,2},{2,0},{0,1},{9,11},{11,13},{13... | collective-permute-start | bytes 1400840 | tf_op jit(solution)/shard_map/ppermute | solution.py:537
  60.8 1.4 collective-permute-start.11
  62.2 6.4 %collective-permute-done.23.refs_3_ = bf16[96,2560]{1,0:T(8,128)(2,1)S(1)} collective-permute-done((bf16[96,2560]{1,0:T(8,128)(2,1)S(1)}, bf16[96,2560]{1,0:T(8,128)(2,1)S(1)}, u32[]{:S(2)}, u32[]{:S(2)}) %collective-permute-start.23) | collective-permute-done | bytes 491552 | tf_op jit(solution)/shard_map/ppermute | solution.py:537
  68.6 2.0 %collective-permute-start.24 = (bf16[96,2560]{1,0:T(8,128)(2,1)S(1)}, bf16[96,2560]{1,0:T(8,128)(2,1)S(1)}, u32[]{:S(2)}, u32[]{:S(2)}) collective-permute-start(bf16[96,2560]{1,0:T(8,128)(2,1)S(1)} %collective-permute-done.23.refs_3_), channel_id=1, source_target_pairs={{1,3},{3,5},{5,7},{7,6},{6,4},{4,2},{2,0},{0,1},{9,11},{11,13},{13... | collective-permute-start | bytes 1474568 | tf_op jit(solution)/shard_map/ppermute | solution.py:537
  70.7 7.9 %collective-permute-done.3.refs_1_ = bf16[96,2432]{1,0:T(8,128)(2,1)S(1)} collective-permute-done((bf16[96,2432]{1,0:T(8,128)(2,1)S(1)}, bf16[96,2432]{1,0:T(8,128)(2,1)S(1)}, u32[]{:S(2)}, u32[]{:S(2)}) %collective-permute-start.3) | collective-permute-done | bytes 466976 | tf_op jit(solution)/shard_map/ppermute | solution.py:537
  78.6 2.0 %collective-permute-start.4 = (bf16[96,2432]{1,0:T(8,128)(2,1)S(1)}, bf16[96,2432]{1,0:T(8,128)(2,1)S(1)}, u32[]{:S(2)}, u32[]{:S(2)}) collective-permute-start(bf16[96,2432]{1,0:T(8,128)(2,1)S(1)} %collective-permute-done.3.refs_1_), channel_id=1, source_target_pairs={{1,3},{3,5},{5,7},{7,6},{6,4},{4,2},{2,0},{0,1},{9,11},{11,13},{13... | collective-permute-start | bytes 1400840 | tf_op jit(solution)/shard_map/ppermute | solution.py:537
  80.6 3.6 %collective-permute-done.11.refs_5_ = bf16[96,2432]{1,0:T(8,128)(2,1)S(1)} collective-permute-done((bf16[96,2432]{1,0:T(8,128)(2,1)S(1)}, bf16[96,2432]{1,0:T(8,128)(2,1)S(1)}, u32[]{:S(2)}, u32[]{:S(2)}) %collective-permute-start.11) | collective-permute-done | bytes 466976 | tf_op jit(solution)/shard_map/ppermute | solution.py:537
  84.3 2.0 %collective-permute-start.12 = (bf16[96,2432]{1,0:T(8,128)(2,1)S(1)}, bf16[96,2432]{1,0:T(8,128)(2,1)S(1)}, u32[]{:S(2)}, u32[]{:S(2)}) collective-permute-start(bf16[96,2432]{1,0:T(8,128)(2,1)S(1)} %get-tuple-element.79.refs_0_), channel_id=1, source_target_pairs={{1,0},{3,1},{5,3},{7,5},{6,7},{4,6},{2,4},{0,2},{9,8},{11,9},{13,1... | collective-permute-start | bytes 1400840 | tf_op jit(solution)/shard_map/ppermute | solution.py:537
  86.4 7.9 %collective-permute-done.20.refs_7_ = bf16[96,2432]{1,0:T(8,128)(2,1)S(1)} collective-permute-done((bf16[96,2432]{1,0:T(8,128)(2,1)S(1)}, bf16[96,2432]{1,0:T(8,128)(2,1)S(1)}, u32[]{:S(2)}, u32[]{:S(2)}) %collective-permute-start.20) | collective-permute-done | bytes 466976 | tf_op jit(solution)/shard_map/ppermute | solution.py:537
  94.4 1.4 collective-permute-start.28
  96.5 1.8 collective-permute-done.4.refs_2_
  99.0 5.3 %collective-permute-done.18.refs_6_ = bf16[96,2432]{1,0:T(8,128)(2,1)S(1)} collective-permute-done((bf16[96,2432]{1,0:T(8,128)(2,1)S(1)}, bf16[96,2432]{1,0:T(8,128)(2,1)S(1)}, u32[]{:S(2)}, u32[]{:S(2)}) %collective-permute-start.18) | collective-permute-done | bytes 466976 | tf_op jit(solution)/shard_map/ppermute | solution.py:537
  104.3 1.6 collective-permute-start.16
  105.9 1.6 collective-permute-start.5
  107.9 6.4 %collective-permute-done.12.refs_4_ = bf16[96,2432]{1,0:T(8,128)(2,1)S(1)} collective-permute-done((bf16[96,2432]{1,0:T(8,128)(2,1)S(1)}, bf16[96,2432]{1,0:T(8,128)(2,1)S(1)}, u32[]{:S(2)}, u32[]{:S(2)}) %collective-permute-start.12) | collective-permute-done | bytes 466976 | tf_op jit(solution)/shard_map/ppermute | solution.py:537
  114.4 6.0 %compose.3 = (bf16[8,768,768]{2,1,0:T(8,128)(2,1)S(1)}, bf16[8,96,768]{2,1,0:T(8,128)(2,1)S(1)}, bf16[2,768,768]{2,1,0:T(8,128)(2,1)S(1)}, bf16[768,768]{1,0:T(8,128)(2,1)S(1)}) custom-call(s32[1]{0:T(128)S(6)} %convert_element_type.3.last_ref, s32[1]{0:T(128)} %bitcast.place_ref, bf16[96,2560]{1,0:T(8,128)(2,1)S(1)} %copy-done.2, ...), custom_call_target="tpu_custom_call" | custom-call | flops 5435817984 | bytes 9437184 | tf_op jit(solution)/shard_map/compose/pallas_call | solution.py:259
  120.4 3.9 %collective-permute-done.19.refs_7_ = bf16[96,2432]{1,0:T(8,128)(2,1)S(1)} collective-permute-done((bf16[96,2432]{1,0:T(8,128)(2,1)S(1)}, bf16[96,2432]{1,0:T(8,128)(2,1)S(1)}, u32[]{:S(2)}, u32[]{:S(2)}) %collective-permute-start.19) | collective-permute-done | bytes 466976 | tf_op jit(solution)/shard_map/ppermute | solution.py:537
  124.3 1.6 collective-permute-start.17
  125.9 1.6 collective-permute-start.6
  127.5 4.1 %collective-permute-done.13.refs_5_ = bf16[96,2432]{1,0:T(8,128)(2,1)S(1)} collective-permute-done((bf16[96,2432]{1,0:T(8,128)(2,1)S(1)}, bf16[96,2432]{1,0:T(8,128)(2,1)S(1)}, u32[]{:S(2)}, u32[]{:S(2)}) %collective-permute-start.13) | collective-permute-done | bytes 466976 | tf_op jit(solution)/shard_map/ppermute | solution.py:537
  131.8 7.6 %compose.4 = (bf16[8,768,768]{2,1,0:T(8,128)(2,1)S(1)}, bf16[8,96,768]{2,1,0:T(8,128)(2,1)S(1)}, bf16[2,768,768]{2,1,0:T(8,128)(2,1)S(1)}, bf16[768,768]{1,0:T(8,128)(2,1)S(1)}) custom-call(s32[1]{0:T(128)S(6)} %convert_element_type.3.last_ref, s32[1]{0:T(128)} %bitcast.place_ref, ...), custom_call_target="tpu_custom_call", output_to_operand_aliasing={{0}: (11, {}), {1}: (12, {})} | custom-call | flops 5435817984 | bytes 9437184 | tf_op jit(solution)/shard_map/compose/pallas_call | solution.py:259
  139.4 2.7 %collective-permute-done.6.refs_2_ = bf16[96,2432]{1,0:T(8,128)(2,1)S(1)} collective-permute-done((bf16[96,2432]{1,0:T(8,128)(2,1)S(1)}, bf16[96,2432]{1,0:T(8,128)(2,1)S(1)}, u32[]{:S(2)}, u32[]{:S(2)}) %collective-permute-start.6) | collective-permute-done | bytes 466976 | tf_op jit(solution)/shard_map/ppermute | solution.py:537
  142.1 1.2 collective-permute-start.7
  144.1 6.6 %compose.5 = (bf16[8,768,768]{2,1,0:T(8,128)(2,1)S(1)}, bf16[8,96,768]{2,1,0:T(8,128)(2,1)S(1)}, bf16[2,768,768]{2,1,0:T(8,128)(2,1)S(1)}, bf16[768,768]{1,0:T(8,128)(2,1)S(1)}) custom-call(s32[1]{0:T(128)S(6)} %convert_element_type.3.last_ref, s32[1]{0:T(128)} %bitcast.place_ref, ...), custom_call_target="tpu_custom_call", output_to_operand_aliasing={{0}: (11, {}), {1}: (12, {})} | custom-call | flops 5435817984 | bytes 9437184 | tf_op jit(solution)/shard_map/compose/pallas_call | solution.py:259
  151.8 4.3 %chain.1 = (bf16[2,768,768]{2,1,0:T(8,128)(2,1)S(1)}, bf16[2,768,768]{2,1,0:T(8,128)(2,1)S(1)}, bf16[6,256,256]{2,1,0:T(8,128)(2,1)S(1)}) custom-call(s32[1]{0:T(128)} %bitcast.place_ref, bf16[96,2432]{1,0:T(8,128)(2,1)S(1)} %get-tuple-element.79.refs_0_, bf16[96,2432]{1,0:T(8,128)(2,1)S(1)} %collective-permute-done.5.refs_1_, ...), custom_call_target="tpu_custom_call" | custom-call | flops 3623878656 | bytes 9437184 | tf_op jit(solution)/shard_map/chain/pallas_call | solution.py:303
  156.9 2.3 %extend_factors.1 = (bf16[8,768,768]{2,1,0:T(8,128)(2,1)S(1)}, bf16[8,96,768]{2,1,0:T(8,128)(2,1)S(1)}) custom-call(s32[1]{0:T(128)} %bitcast.place_ref, bf16[2,768,768]{2,1,0:T(8,128)(2,1)S(1)} %get-tuple-element.124.gain_ref, bf16[8,768,768]{2,1,0:T(8,128)(2,1)S(1)} %get-tuple-element.125.factor_in, ...), custom_call_target="tpu_custom_call", output_to_operand_aliasing={{0}: (2, {}), {1}: (3, {})} | custom-call | flops 1811939328 | bytes 4718592 | tf_op jit(solution)/shard_map/extend_factors/pallas_call | solution.py:343
  159.2 1.8 hop.2
  161.0 0.9 collective-permute-start.32
  162.0 4.4 %own_rows.1.own_ref = f32[8,96,768]{2,1,0:T(8,128)S(1)} custom-call(s32[1]{0:T(128)} %bitcast.place_ref, bf16[2,768,768]{2,1,0:T(8,128)(2,1)S(1)} %get-tuple-element.133.half_ref.refs_0_, bf16[2,768,768]{2,1,0:T(8,128)(2,1)S(1)} %get-tuple-element.134.refs_1_, bf16[2,768,768]{2,1,0:T(8,128)(2,1)S(1)} %get-tuple-element.135.refs_2_, ...), custom_call_target="tpu_custom_call" | custom-call | flops 905969664 | bytes 9437184 | tf_op jit(solution)/shard_map/own_rows/pallas_call | solution.py:382
  166.4 1.8 hop.3
  168.2 1.3 collective-permute-start.33
  169.5 11.3 %collective-permute-done.33.refs_2_ = bf16[6,256,256]{2,1,0:T(8,128)(2,1)S(1)} collective-permute-done((bf16[6,256,256]{2,1,0:T(8,128)(2,1)S(1)}, bf16[6,256,256]{2,1,0:T(8,128)(2,1)S(1)}, u32[]{:S(2)}, u32[]{:S(2)}) %collective-permute-start.33) | collective-permute-done | bytes 786464 | tf_op jit(solution)/shard_map/ppermute | solution.py:596
  180.8 5.6 %finish.1 = f32[8,96,768]{2,1,0:T(8,128)} custom-call(bf16[8,768,768]{2,1,0:T(8,128)(2,1)S(1)} %get-tuple-element.127.factor_ref, f32[8,96,768]{2,1,0:T(8,128)S(1)} %own_rows.1.own_ref, bf16[8,96,768]{2,1,0:T(8,128)(2,1)S(1)} %get-tuple-element.138.mine_ref, bf16[6,256,256]{2,1,0:T(8,128)(2,1)S(1)} %collective-permute-done.31.refs_0_, ...), custom_call_target="tpu_custom_call" | custom-call | tf_op jit(solution)/shard_map/finish/pallas_call | solution.py:496
  (41 shorter events, 7.3 us)
Async XLA Ops:
  2.3 47.8 %copy-start = (f32[8,96,768]{2,1,0:T(8,128)S(1)}, f32[8,96,768]{2,1,0:T(8,128)}, u32[]{:S(2)}) copy-start(f32[8,96,768]{2,1,0:T(8,128)} %increment_ref.5) | copy-start | bytes 7077892
  2.3 47.8 %copy-start.1 = (bf16[8,96,768]{2,1,0:T(8,128)(2,1)S(1)}, bf16[8,96,768]{2,1,0:T(8,128)(2,1)}, u32[]{:S(2)}) copy-start(bf16[8,96,768]{2,1,0:T(8,128)(2,1)} %gain_ref.5) | copy-start | bytes 3538948
  2.3 14.8 %collective-permute-start = (bf16[96,2432]{1,0:T(8,128)(2,1)}, bf16[96,2432]{1,0:T(8,128)(2,1)S(1)}, u32[]{:S(2)}, u32[]{:S(2)}) collective-permute-start(bf16[96,2432]{1,0:T(8,128)(2,1)} %pack.4.refs_0_), channel_id=1, source_target_pairs={{1,3},{3,5},{5,7},{7,6},{6,4},{4,2},{2,0},{0,1},{9,11},{11,13},{13... | collective-permute-start | bytes 1400840 | tf_op jit(solution)/shard_map/ppermute | solution.py:537
  5.2 13.9 %collective-permute-start.8 = (bf16[96,2432]{1,0:T(8,128)(2,1)}, bf16[96,2432]{1,0:T(8,128)(2,1)}, u32[]{:S(2)}, u32[]{:S(2)}) collective-permute-start(bf16[96,2432]{1,0:T(8,128)(2,1)} %pack.4.refs_0_), channel_id=1, source_target_pairs={{1,0},{3,1},{5,3},{7,5},{6,7},{4,6},{2,4},{0,2},{9,8},{11,9},{13,1... | collective-permute-start | bytes 1400840 | tf_op jit(solution)/shard_map/ppermute | solution.py:537
  7.9 86.3 %copy-start.2 = (bf16[96,2560]{1,0:T(8,128)(2,1)S(1)}, bf16[96,2560]{1,0:T(8,128)(2,1)}, u32[]{:S(2)}) copy-start(bf16[96,2560]{1,0:T(8,128)(2,1)} %pack.5.refs_0_) | copy-start | bytes 1474564
  7.9 19.6 %collective-permute-start.21 = (bf16[96,2560]{1,0:T(8,128)(2,1)}, bf16[96,2560]{1,0:T(8,128)(2,1)S(1)}, u32[]{:S(2)}, u32[]{:S(2)}) collective-permute-start(bf16[96,2560]{1,0:T(8,128)(2,1)} %pack.5.refs_0_), channel_id=1, source_target_pairs={{1,3},{3,5},{5,7},{7,6},{6,4},{4,2},{2,0},{0,1},{9,11},{11,13},{13... | collective-permute-start | bytes 1474568 | tf_op jit(solution)/shard_map/ppermute | solution.py:537
  17.0 20.5 %collective-permute-start.1 = (bf16[96,2432]{1,0:T(8,128)(2,1)S(1)}, bf16[96,2432]{1,0:T(8,128)(2,1)S(1)}, u32[]{:S(2)}, u32[]{:S(2)}) collective-permute-start(bf16[96,2432]{1,0:T(8,128)(2,1)S(1)} %collective-permute-done.refs_1_), channel_id=1, source_target_pairs={{1,3},{3,5},{5,7},{7,6},{6,4},{4,2},{2,0},{0,1},{9,11},{11,13},{13... | collective-permute-start | bytes 1400840 | tf_op jit(solution)/shard_map/ppermute | solution.py:537
  19.0 20.5 %collective-permute-start.25 = (bf16[96,2560]{1,0:T(8,128)(2,1)}, bf16[96,2560]{1,0:T(8,128)(2,1)S(1)}, u32[]{:S(2)}, u32[]{:S(2)}) collective-permute-start(bf16[96,2560]{1,0:T(8,128)(2,1)} %pack.5.refs_0_), channel_id=1, source_target_pairs={{1,0},{3,1},{5,3},{7,5},{6,7},{4,6},{2,4},{0,2},{9,8},{11,9},{13,1... | collective-permute-start | bytes 1474568 | tf_op jit(solution)/shard_map/ppermute | solution.py:537
  19.1 21.2 %collective-permute-start.9 = (bf16[96,2432]{1,0:T(8,128)(2,1)}, bf16[96,2432]{1,0:T(8,128)(2,1)S(1)}, u32[]{:S(2)}, u32[]{:S(2)}) collective-permute-start(bf16[96,2432]{1,0:T(8,128)(2,1)} %collective-permute-done.8.refs_4_), channel_id=1, source_target_pairs={{1,0},{3,1},{5,3},{7,5},{6,7},{4,6},{2,4},{0,2},{9,8},{11,9},{13,1... | collective-permute-start | bytes 1400840 | tf_op jit(solution)/shard_map/ppermute | solution.py:537
  27.6 20.5 %collective-permute-start.22 = (bf16[96,2560]{1,0:T(8,128)(2,1)S(1)}, bf16[96,2560]{1,0:T(8,128)(2,1)S(1)}, u32[]{:S(2)}, u32[]{:S(2)}) collective-permute-start(bf16[96,2560]{1,0:T(8,128)(2,1)S(1)} %collective-permute-done.21.refs_1_), channel_id=1, source_target_pairs={{1,3},{3,5},{5,7},{7,6},{6,4},{4,2},{2,0},{0,1},{9,11},{11,13},{13... | collective-permute-start | bytes 1474568 | tf_op jit(solution)/shard_map/ppermute | solution.py:537
  37.6 20.5 %collective-permute-start.2 = (bf16[96,2432]{1,0:T(8,128)(2,1)S(1)}, bf16[96,2432]{1,0:T(8,128)(2,1)S(1)}, u32[]{:S(2)}, u32[]{:S(2)}) collective-permute-start(bf16[96,2432]{1,0:T(8,128)(2,1)S(1)} %collective-permute-done.1.refs_2_), channel_id=1, source_target_pairs={{1,3},{3,5},{5,7},{7,6},{6,4},{4,2},{2,0},{0,1},{9,11},{11,13},{13... | collective-permute-start | bytes 1400840 | tf_op jit(solution)/shard_map/ppermute | solution.py:537
  39.6 20.5 %collective-permute-start.26 = (bf16[96,2560]{1,0:T(8,128)(2,1)S(1)}, bf16[96,2560]{1,0:T(8,128)(2,1)S(1)}, u32[]{:S(2)}, u32[]{:S(2)}) collective-permute-start(bf16[96,2560]{1,0:T(8,128)(2,1)S(1)} %collective-permute-done.25.refs_5_), channel_id=1, source_target_pairs={{1,0},{3,1},{5,3},{7,5},{6,7},{4,6},{2,4},{0,2},{9,8},{11,9},{13,1... | collective-permute-start | bytes 1474568 | tf_op jit(solution)/shard_map/ppermute | solution.py:537
  40.3 20.5 %collective-permute-start.10 = (bf16[96,2432]{1,0:T(8,128)(2,1)S(1)}, bf16[96,2432]{1,0:T(8,128)(2,1)S(1)}, u32[]{:S(2)}, u32[]{:S(2)}) collective-permute-start(bf16[96,2432]{1,0:T(8,128)(2,1)S(1)} %collective-permute-done.9.refs_5_), channel_id=1, source_target_pairs={{1,0},{3,1},{5,3},{7,5},{6,7},{4,6},{2,4},{0,2},{9,8},{11,9},{13,1... | collective-permute-start | bytes 1400840 | tf_op jit(solution)/shard_map/ppermute | solution.py:537
  48.1 20.5 %collective-permute-start.23 = (bf16[96,2560]{1,0:T(8,128)(2,1)S(1)}, bf16[96,2560]{1,0:T(8,128)(2,1)S(1)}, u32[]{:S(2)}, u32[]{:S(2)}) collective-permute-start(bf16[96,2560]{1,0:T(8,128)(2,1)S(1)} %collective-permute-done.22.refs_2_), channel_id=1, source_target_pairs={{1,3},{3,5},{5,7},{7,6},{6,4},{4,2},{2,0},{0,1},{9,11},{11,13},{13... | collective-permute-start | bytes 1474568 | tf_op jit(solution)/shard_map/ppermute | solution.py:537
  58.1 20.5 %collective-permute-start.3 = (bf16[96,2432]{1,0:T(8,128)(2,1)S(1)}, bf16[96,2432]{1,0:T(8,128)(2,1)S(1)}, u32[]{:S(2)}, u32[]{:S(2)}) collective-permute-start(bf16[96,2432]{1,0:T(8,128)(2,1)S(1)} %get-tuple-element.83.refs_0_), channel_id=1, source_target_pairs={{1,3},{3,5},{5,7},{7,6},{6,4},{4,2},{2,0},{0,1},{9,11},{11,13},{13... | collective-permute-start | bytes 1400840 | tf_op jit(solution)/shard_map/ppermute | solution.py:537
  60.1 24.2 %collective-permute-start.27 = (bf16[96,2560]{1,0:T(8,128)(2,1)S(1)}, bf16[96,2560]{1,0:T(8,128)(2,1)S(1)}, u32[]{:S(2)}, u32[]{:S(2)}) collective-permute-start(bf16[96,2560]{1,0:T(8,128)(2,1)S(1)} %collective-permute-done.26.refs_6_), channel_id=1, source_target_pairs={{1,0},{3,1},{5,3},{7,5},{6,7},{4,6},{2,4},{0,2},{9,8},{11,9},{13,1... | collective-permute-start | bytes 1474568 | tf_op jit(solution)/shard_map/ppermute | solution.py:537
  60.8 23.5 %collective-permute-start.11 = (bf16[96,2432]{1,0:T(8,128)(2,1)S(1)}, bf16[96,2432]{1,0:T(8,128)(2,1)S(1)}, u32[]{:S(2)}, u32[]{:S(2)}) collective-permute-start(bf16[96,2432]{1,0:T(8,128)(2,1)S(1)} %get-tuple-element.83.refs_0_), channel_id=1, source_target_pairs={{1,0},{3,1},{5,3},{7,5},{6,7},{4,6},{2,4},{0,2},{9,8},{11,9},{13,1... | collective-permute-start | bytes 1400840 | tf_op jit(solution)/shard_map/ppermute | solution.py:537
  68.6 25.6 %collective-permute-start.24 = (bf16[96,2560]{1,0:T(8,128)(2,1)S(1)}, bf16[96,2560]{1,0:T(8,128)(2,1)S(1)}, u32[]{:S(2)}, u32[]{:S(2)}) collective-permute-start(bf16[96,2560]{1,0:T(8,128)(2,1)S(1)} %collective-permute-done.23.refs_3_), channel_id=1, source_target_pairs={{1,3},{3,5},{5,7},{7,6},{6,4},{4,2},{2,0},{0,1},{9,11},{11,13},{13... | collective-permute-start | bytes 1474568 | tf_op jit(solution)/shard_map/ppermute | solution.py:537
  70.6 23.6 %collective-permute-start.20 = (bf16[96,2432]{1,0:T(8,128)(2,1)S(1)}, bf16[96,2432]{1,0:T(8,128)(2,1)S(1)}, u32[]{:S(2)}, u32[]{:S(2)}) collective-permute-start(bf16[96,2432]{1,0:T(8,128)(2,1)S(1)} %collective-permute-done.10.refs_6_), channel_id=1, source_target_pairs={{1,0},{3,1},{5,3},{7,5},{6,7},{4,6},{2,4},{0,2},{9,8},{11,9},{13,1... | collective-permute-start | bytes 1400840 | tf_op jit(solution)/shard_map/ppermute | solution.py:537
  78.6 19.7 %collective-permute-start.4 = (bf16[96,2432]{1,0:T(8,128)(2,1)S(1)}, bf16[96,2432]{1,0:T(8,128)(2,1)S(1)}, u32[]{:S(2)}, u32[]{:S(2)}) collective-permute-start(bf16[96,2432]{1,0:T(8,128)(2,1)S(1)} %collective-permute-done.3.refs_1_), channel_id=1, source_target_pairs={{1,3},{3,5},{5,7},{7,6},{6,4},{4,2},{2,0},{0,1},{9,11},{11,13},{13... | collective-permute-start | bytes 1400840 | tf_op jit(solution)/shard_map/ppermute | solution.py:537
  84.3 20.0 %collective-permute-start.18 = (bf16[96,2432]{1,0:T(8,128)(2,1)S(1)}, bf16[96,2432]{1,0:T(8,128)(2,1)S(1)}, u32[]{:S(2)}, u32[]{:S(2)}) collective-permute-start(bf16[96,2432]{1,0:T(8,128)(2,1)S(1)} %collective-permute-done.11.refs_5_), channel_id=1, source_target_pairs={{1,0},{3,1},{5,3},{7,5},{6,7},{4,6},{2,4},{0,2},{9,8},{11,9},{13,1... | collective-permute-start | bytes 1400840 | tf_op jit(solution)/shard_map/ppermute | solution.py:537
  84.3 29.9 %collective-permute-start.12 = (bf16[96,2432]{1,0:T(8,128)(2,1)S(1)}, bf16[96,2432]{1,0:T(8,128)(2,1)S(1)}, u32[]{:S(2)}, u32[]{:S(2)}) collective-permute-start(bf16[96,2432]{1,0:T(8,128)(2,1)S(1)} %get-tuple-element.79.refs_0_), channel_id=1, source_target_pairs={{1,0},{3,1},{5,3},{7,5},{6,7},{4,6},{2,4},{0,2},{9,8},{11,9},{13,1... | collective-permute-start | bytes 1400840 | tf_op jit(solution)/shard_map/ppermute | solution.py:537
  94.4 37.4 %copy-start.3 = (bf16[96,2432]{1,0:T(8,128)(2,1)S(1)}, bf16[96,2432]{1,0:T(8,128)(2,1)}, u32[]{:S(2)}) copy-start(bf16[96,2432]{1,0:T(8,128)(2,1)} %pack.4.refs_0_) | copy-start | bytes 1400836
  94.4 11.4 %collective-permute-start.28 = (bf16[8,96,128]{2,1,0:T(8,128)(2,1)S(1)}, bf16[8,96,128]{2,1,0:T(8,128)(2,1)S(1)}, u32[]{:S(2)}, u32[]{:S(2)}) collective-permute-start(bf16[8,96,128]{2,1,0:T(8,128)(2,1)S(1)} %collect.1.refs_11_), channel_id=1, source_target_pairs={{0,24},{1,25},{2,26},{3,27},{4,28},{5,29},{6,30},{7,31}} | collective-permute-start | bytes 589832 | tf_op jit(solution)/shard_map/ppermute | solution.py:574
  95.9 11.6 %collective-permute-start.29 = (bf16[8,96,128]{2,1,0:T(8,128)(2,1)S(1)}, bf16[8,96,128]{2,1,0:T(8,128)(2,1)S(1)}, u32[]{:S(2)}, u32[]{:S(2)}) collective-permute-start(bf16[8,96,128]{2,1,0:T(8,128)(2,1)S(1)} %collect.1.refs_11_), channel_id=1, source_target_pairs={{8,24},{9,25},{10,26},{11,27},{12,28},{13,29},{14,30},{15,31}} | collective-permute-start | bytes 589832 | tf_op jit(solution)/shard_map/ppermute | solution.py:574
  98.4 16.0 %collective-permute-start.30 = (bf16[8,96,128]{2,1,0:T(8,128)(2,1)S(1)}, bf16[8,96,128]{2,1,0:T(8,128)(2,1)S(1)}, u32[]{:S(2)}, u32[]{:S(2)}) collective-permute-start(bf16[8,96,128]{2,1,0:T(8,128)(2,1)S(1)} %collect.1.refs_11_), channel_id=1, source_target_pairs={{16,24},{17,25},{18,26},{19,27},{20,28},{21,29},{22,30},{23,31}} | collective-permute-start | bytes 589832 | tf_op jit(solution)/shard_map/ppermute | solution.py:574
  104.3 16.1 %collective-permute-start.16 = (bf16[96,2432]{1,0:T(8,128)(2,1)S(1)}, bf16[96,2432]{1,0:T(8,128)(2,1)S(1)}, u32[]{:S(2)}, u32[]{:S(2)}) collective-permute-start(bf16[96,2432]{1,0:T(8,128)(2,1)S(1)} %collective-permute-done.4.refs_2_), channel_id=1, source_target_pairs={{1,3},{3,5},{5,7},{7,6},{6,4},{4,2},{2,0},{0,1},{9,11},{11,13},{13... | collective-permute-start | bytes 1400840 | tf_op jit(solution)/shard_map/ppermute | solution.py:537
  105.9 20.0 %collective-permute-start.5 = (bf16[96,2432]{1,0:T(8,128)(2,1)S(1)}, bf16[96,2432]{1,0:T(8,128)(2,1)S(1)}, u32[]{:S(2)}, u32[]{:S(2)}) collective-permute-start(bf16[96,2432]{1,0:T(8,128)(2,1)S(1)} %get-tuple-element.79.refs_0_), channel_id=1, source_target_pairs={{1,3},{3,5},{5,7},{7,6},{6,4},{4,2},{2,0},{0,1},{9,11},{11,13},{13... | collective-permute-start | bytes 1400840 | tf_op jit(solution)/shard_map/ppermute | solution.py:537
  107.4 16.9 %collective-permute-start.19 = (bf16[96,2432]{1,0:T(8,128)(2,1)S(1)}, bf16[96,2432]{1,0:T(8,128)(2,1)S(1)}, u32[]{:S(2)}, u32[]{:S(2)}) collective-permute-start(bf16[96,2432]{1,0:T(8,128)(2,1)S(1)} %collective-permute-done.18.refs_6_), channel_id=1, source_target_pairs={{1,0},{3,1},{5,3},{7,5},{6,7},{4,6},{2,4},{0,2},{9,8},{11,9},{13,1... | collective-permute-start | bytes 1400840 | tf_op jit(solution)/shard_map/ppermute | solution.py:537
  114.3 17.2 %collective-permute-start.13 = (bf16[96,2432]{1,0:T(8,128)(2,1)S(1)}, bf16[96,2432]{1,0:T(8,128)(2,1)S(1)}, u32[]{:S(2)}, u32[]{:S(2)}) collective-permute-start(bf16[96,2432]{1,0:T(8,128)(2,1)S(1)} %collective-permute-done.12.refs_4_), channel_id=1, source_target_pairs={{1,0},{3,1},{5,3},{7,5},{6,7},{4,6},{2,4},{0,2},{9,8},{11,9},{13,1... | collective-permute-start | bytes 1400840 | tf_op jit(solution)/shard_map/ppermute | solution.py:537
  124.3 15.1 %collective-permute-start.17 = (bf16[96,2432]{1,0:T(8,128)(2,1)S(1)}, bf16[96,2432]{1,0:T(8,128)(2,1)S(1)}, u32[]{:S(2)}, u32[]{:S(2)}) collective-permute-start(bf16[96,2432]{1,0:T(8,128)(2,1)S(1)} %collective-permute-done.16.refs_3_), channel_id=1, source_target_pairs={{1,3},{3,5},{5,7},{7,6},{6,4},{4,2},{2,0},{0,1},{9,11},{11,13},{13... | collective-permute-start | bytes 1400840 | tf_op jit(solution)/shard_map/ppermute | solution.py:537
  125.9 16.2 %collective-permute-start.6 = (bf16[96,2432]{1,0:T(8,128)(2,1)S(1)}, bf16[96,2432]{1,0:T(8,128)(2,1)S(1)}, u32[]{:S(2)}, u32[]{:S(2)}) collective-permute-start(bf16[96,2432]{1,0:T(8,128)(2,1)S(1)} %collective-permute-done.5.refs_1_), channel_id=1, source_target_pairs={{1,3},{3,5},{5,7},{7,6},{6,4},{4,2},{2,0},{0,1},{9,11},{11,13},{13... | collective-permute-start | bytes 1400840 | tf_op jit(solution)/shard_map/ppermute | solution.py:537
  131.5 10.6 %collective-permute-start.14 = (bf16[96,2432]{1,0:T(8,128)(2,1)S(1)}, bf16[96,2432]{1,0:T(8,128)(2,1)S(1)}, u32[]{:S(2)}, u32[]{:S(2)}) collective-permute-start(bf16[96,2432]{1,0:T(8,128)(2,1)S(1)} %collective-permute-done.13.refs_5_), channel_id=1, source_target_pairs={{1,0},{3,1},{5,3},{7,5},{6,7},{4,6},{2,4},{0,2},{9,8},{11,9},{13,1... | collective-permute-start | bytes 1400840 | tf_op jit(solution)/shard_map/ppermute | solution.py:537
  142.1 8.9 %collective-permute-start.7 = (bf16[96,2432]{1,0:T(8,128)(2,1)S(1)}, bf16[96,2432]{1,0:T(8,128)(2,1)S(1)}, u32[]{:S(2)}, u32[]{:S(2)}) collective-permute-start(bf16[96,2432]{1,0:T(8,128)(2,1)S(1)} %collective-permute-done.6.refs_2_), channel_id=1, source_target_pairs={{1,3},{3,5},{5,7},{7,6},{6,4},{4,2},{2,0},{0,1},{9,11},{11,13},{13... | collective-permute-start | bytes 1400840 | tf_op jit(solution)/shard_map/ppermute | solution.py:537
  143.3 8.6 %collective-permute-start.15 = (bf16[96,2432]{1,0:T(8,128)(2,1)S(1)}, bf16[96,2432]{1,0:T(8,128)(2,1)S(1)}, u32[]{:S(2)}, u32[]{:S(2)}) collective-permute-start(bf16[96,2432]{1,0:T(8,128)(2,1)S(1)} %collective-permute-done.14.refs_6_), channel_id=1, source_target_pairs={{1,0},{3,1},{5,3},{7,5},{6,7},{4,6},{2,4},{0,2},{9,8},{11,9},{13,1... | collective-permute-start | bytes 1400840 | tf_op jit(solution)/shard_map/ppermute | solution.py:537
  156.2 3.0 %collective-permute-start.31 = (bf16[6,256,256]{2,1,0:T(8,128)(2,1)S(1)}, bf16[6,256,256]{2,1,0:T(8,128)(2,1)S(1)}, u32[]{:S(2)}, u32[]{:S(2)}) collective-permute-start(bf16[6,256,256]{2,1,0:T(8,128)(2,1)S(1)} %get-tuple-element.128), channel_id=1, source_target_pairs={{24,16},{25,17},{26,18},{27,19},{28,20},{29,21},{30,22},{31,23}} | collective-permute-start | bytes 2359304 | tf_op jit(solution)/shard_map/ppermute | solution.py:596
  161.0 5.3 %collective-permute-start.32 = (bf16[6,256,256]{2,1,0:T(8,128)(2,1)S(1)}, bf16[6,256,256]{2,1,0:T(8,128)(2,1)S(1)}, u32[]{:S(2)}, u32[]{:S(2)}) collective-permute-start(bf16[6,256,256]{2,1,0:T(8,128)(2,1)S(1)} %hop.2), channel_id=1, source_target_pairs={{16,8},{17,9},{18,10},{19,11},{20,12},{21,13},{22,14},{23,15}} | collective-permute-start | bytes 2359304 | tf_op jit(solution)/shard_map/ppermute | solution.py:596
  168.2 12.6 %collective-permute-start.33 = (bf16[6,256,256]{2,1,0:T(8,128)(2,1)S(1)}, bf16[6,256,256]{2,1,0:T(8,128)(2,1)S(1)}, u32[]{:S(2)}, u32[]{:S(2)}) collective-permute-start(bf16[6,256,256]{2,1,0:T(8,128)(2,1)S(1)} %hop.3), channel_id=1, source_target_pairs={{8,0},{9,1},{10,2},{11,3},{12,4},{13,5},{14,6},{15,7}} | collective-permute-start | bytes 2359304 | tf_op jit(solution)/shard_map/ppermute | solution.py:596

commit v18 on v17

--- a/solution.py
+++ b/solution.py
@@ -460,52 +460,45 @@
 
 
 def finish_kernel(arrived, factor_ref, own_ref, mine_ref, *refs):
-    out_ref, covariance, middle = refs[arrived:]
-    turn = pl.program_id(0)
-    rows = own_ref.shape[1]
-    steps = mine_ref.shape[0]
-    width = covariance.shape[0]
-
-    @pl.when(turn == 0)
-    def _():
-        one = identity(TILE)
-        for n, (a, b) in enumerate(upper_blocks(width)):
-            block = arrived_sum(refs[:arrived], n)
-            turned = nt(one, block)
-            if a == b:
-                covariance[a:a + TILE, b:b + TILE] = (block.astype(F32) + turned).astype(BF16)
-            else:
-                covariance[a:a + TILE, b:b + TILE] = block
-                covariance[b:b + TILE, a:a + TILE] = turned.astype(BF16)
-        mine = mine_ref[...].reshape(steps * rows, width)
-        for j in range(0, width, TILE):
-            cols = slice(j, j + TILE)
-            middle[:, cols] = jnp.dot(mine, covariance[:, cols], preferred_element_type=F32).astype(BF16)
-
-    for n in range(out_ref.shape[0]):
-        at = (turn * out_ref.shape[0] + n) * rows
-        left = middle[pl.ds(pl.multiple_of(at, 16), rows), :]
-        out_ref[n] = nt(left, factor_ref[n]) + own_ref[n]
+    out_ref, covariance, middle, rows_out, copied = refs[arrived:]
+    steps, rows, width = own_ref.shape
+    one = identity(TILE)
+    for n, (a, b) in enumerate(upper_blocks(width)):
+        block = arrived_sum(refs[:arrived], n)
+        turned = nt(one, block)
+        if a == b:
+            covariance[a:a + TILE, b:b + TILE] = (block.astype(F32) + turned).astype(BF16)
+        else:
+            covariance[a:a + TILE, b:b + TILE] = block
+            covariance[b:b + TILE, a:a + TILE] = turned.astype(BF16)
+    mine = mine_ref[...].reshape(steps * rows, width)
+    for j in range(0, width, TILE):
+        cols = slice(j, j + TILE)
+        middle[:, cols] = jnp.dot(mine, covariance[:, cols], preferred_element_type=F32).astype(BF16)
+    copies = []
+    for n in range(steps):
+        rows_out[n] = nt(middle[n * rows:(n + 1) * rows, :], factor_ref[n]) + own_ref[n]
+        copies.append(pltpu.make_async_copy(rows_out.at[n], out_ref.at[n], copied.at[n]))
+        copies[-1].start()
+    for copy in copies:
+        copy.wait()
 
 
 def finish(factors, own, mine, packed):
     steps, rows, width = own.shape
-    some = 2 if steps % 2 == 0 else 1
-    whole = pl.BlockSpec(packed[0].shape, lambda i: (0, 0, 0), pipeline_mode=pl.Buffered(1))
-    band = pl.BlockSpec((some, rows, width), lambda i: (i, 0, 0))
+    vmem = pl.BlockSpec(memory_space=pltpu.VMEM)
     return pl.pallas_call(
         functools.partial(finish_kernel, len(packed)),
-        grid=(steps // some,),
-        in_specs=[
-            pl.BlockSpec((some, width, width), lambda i: (i, 0, 0)),
-            band,
-            pl.BlockSpec(mine.shape, lambda i: (0, 0, 0), pipeline_mode=pl.Buffered(1)),
-        ]
-        + [whole] * len(packed),
-        out_specs=band,
-        scratch_shapes=[pltpu.VMEM((width, width), BF16), pltpu.VMEM((steps * rows, width), BF16)],
+        in_specs=[vmem] * (3 + len(packed)),
+        out_specs=pl.BlockSpec(memory_space=pl.ANY),
+        scratch_shapes=[
+            pltpu.VMEM((width, width), BF16),
+            pltpu.VMEM((steps * rows, width), BF16),
+            pltpu.VMEM((steps, rows, width), F32),
+            pltpu.SemaphoreType.DMA((steps,)),
+        ],
         out_shape=jax.ShapeDtypeStruct((steps, rows, width), F32),
-        compiler_params=pltpu.CompilerParams(vmem_limit_bytes=24 * MIB),
+        compiler_params=pltpu.CompilerParams(vmem_limit_bytes=26 * MIB),
         name="finish",
     )(factors, own, mine, *packed)
 

time: 187 us -> 186 us (level)
  no operation moved by 1% of the time
where the time goes in v18:
time: 186 us
  waiting for transfers between devices  99.1 us (53%)
  Pallas kernels  45.4 us (24%)
  starting transfers between devices  41 us (22%)
    ppermute x28, waiting for transfers between devices, passed(): lax.ppermute(array, 'tile', [(cycle[n], cycle[(n + way) % count]) for n i...  87.8 us
    ppermute x28, starting transfers between devices, passed(): lax.ppermute(array, 'tile', [(cycle[n], cycle[(n + way) % count]) for n i...  35.3 us
    pallas_call x3, Pallas kernels, compose(): pl.pallas_call(functools.partial(compose_kernel, cycle, right, turns, fir...  20.2 us
    ppermute x3, waiting for transfers between devices, local(): packed.append(lax.ppermute(before, 'tm', [(turn, turn - 1)]))  11.3 us
    pallas_call x3, Pallas kernels, pack(): pl.pallas_call(functools.partial(pack_kernel, count, ranges), grid_spec=p...  5.57 us
    pallas_call x1, Pallas kernels, finish(): pl.pallas_call(functools.partial(finish_kernel, len(packed)), in_specs=[v...  4.85 us
    pallas_call x1, Pallas kernels, own_rows(): pl.pallas_call(functools.partial(rows_kernel, size), grid_spec=pltpu.Pref...  4.39 us
    pallas_call x1, Pallas kernels, chain(): pl.pallas_call(functools.partial(chain_kernel, cycle, right, turns), in_s...  4.34 us
  transfers between devices with their start and end apart: 34, of which 20 were waited for; matrix products, arithmetic and copies ran while one was open for 0% of the time, Pallas kernels for 16%

profile of v18, /device:TPU:0, one launch (start us, length us, event | category | flops | bytes accessed | tf_op | source)
XLA Modules:
  0.0 185.9 jit_solution(242718478301379417)
XLA Ops:
  0.0 2.3 %pack.4.refs_0_ = bf16[96,2432]{1,0:T(8,128)(2,1)} custom-call(s32[1]{0:T(128)} %bitcast.place_ref, s32[1]{0:T(128)} %bitcast.1.block_ref, bf16[8,96,768]{2,1,0:T(8,128)(2,1)} %gain_ref.5, f32[8,96,768]{2,1,0:T(8,128)} %increment_ref.5), custom_call_target="tpu_custom_call" | custom-call | tf_op jit(solution)/shard_map/pack/pallas_call | solution.py:80
  2.3 3.0 %collective-permute-start = (bf16[96,2432]{1,0:T(8,128)(2,1)}, bf16[96,2432]{1,0:T(8,128)(2,1)S(1)}, u32[]{:S(2)}, u32[]{:S(2)}) collective-permute-start(bf16[96,2432]{1,0:T(8,128)(2,1)} %pack.4.refs_0_), channel_id=1, source_target_pairs={{1,3},{3,5},{5,7},{7,6},{6,4},{4,2},{2,0},{0,1},{9,11},{11,13},{13... | collective-permute-start | bytes 1400840 | tf_op jit(solution)/shard_map/ppermute | solution.py:530
  5.3 2.6 %pack.5.refs_0_ = bf16[96,2560]{1,0:T(8,128)(2,1)} custom-call(s32[1]{0:T(128)} %bitcast.place_ref, s32[1]{0:T(128)} %bitcast.1.block_ref, bf16[8,96,768]{2,1,0:T(8,128)(2,1)} %gain_ref.5, f32[8,96,768]{2,1,0:T(8,128)} %increment_ref.5, f32[96,768]{1,0:T(8,128)} %refs_0_.1), custom_call_target="tpu_custom_call" | custom-call | tf_op jit(solution)/shard_map/pack/pallas_call | solution.py:80
  7.9 1.9 %collective-permute-start.21 = (bf16[96,2560]{1,0:T(8,128)(2,1)}, bf16[96,2560]{1,0:T(8,128)(2,1)S(1)}, u32[]{:S(2)}, u32[]{:S(2)}) collective-permute-start(bf16[96,2560]{1,0:T(8,128)(2,1)} %pack.5.refs_0_), channel_id=1, source_target_pairs={{1,3},{3,5},{5,7},{7,6},{6,4},{4,2},{2,0},{0,1},{9,11},{11,13},{13... | collective-permute-start | bytes 1474568 | tf_op jit(solution)/shard_map/ppermute | solution.py:530
  9.9 7.2 %collective-permute-done.refs_1_ = bf16[96,2432]{1,0:T(8,128)(2,1)S(1)} collective-permute-done((bf16[96,2432]{1,0:T(8,128)(2,1)}, bf16[96,2432]{1,0:T(8,128)(2,1)S(1)}, u32[]{:S(2)}, u32[]{:S(2)}) %collective-permute-start) | collective-permute-done | bytes 466976 | tf_op jit(solution)/shard_map/ppermute | solution.py:530
  17.0 2.0 %collective-permute-start.1 = (bf16[96,2432]{1,0:T(8,128)(2,1)S(1)}, bf16[96,2432]{1,0:T(8,128)(2,1)S(1)}, u32[]{:S(2)}, u32[]{:S(2)}) collective-permute-start(bf16[96,2432]{1,0:T(8,128)(2,1)S(1)} %collective-permute-done.refs_1_), channel_id=1, source_target_pairs={{1,3},{3,5},{5,7},{7,6},{6,4},{4,2},{2,0},{0,1},{9,11},{11,13},{13... | collective-permute-start | bytes 1400840 | tf_op jit(solution)/shard_map/ppermute | solution.py:530
  19.1 2.0 %collective-permute-start.9 = (bf16[96,2432]{1,0:T(8,128)(2,1)}, bf16[96,2432]{1,0:T(8,128)(2,1)S(1)}, u32[]{:S(2)}, u32[]{:S(2)}) collective-permute-start(bf16[96,2432]{1,0:T(8,128)(2,1)} %collective-permute-done.8.refs_4_), channel_id=1, source_target_pairs={{1,0},{3,1},{5,3},{7,5},{6,7},{4,6},{2,4},{0,2},{9,8},{11,9},{13,1... | collective-permute-start | bytes 1400840 | tf_op jit(solution)/shard_map/ppermute | solution.py:530
  21.1 6.4 %collective-permute-done.21.refs_1_ = bf16[96,2560]{1,0:T(8,128)(2,1)S(1)} collective-permute-done((bf16[96,2560]{1,0:T(8,128)(2,1)}, bf16[96,2560]{1,0:T(8,128)(2,1)S(1)}, u32[]{:S(2)}, u32[]{:S(2)}) %collective-permute-start.21) | collective-permute-done | bytes 491552 | tf_op jit(solution)/shard_map/ppermute | solution.py:530
  27.6 2.0 %collective-permute-start.22 = (bf16[96,2560]{1,0:T(8,128)(2,1)S(1)}, bf16[96,2560]{1,0:T(8,128)(2,1)S(1)}, u32[]{:S(2)}, u32[]{:S(2)}) collective-permute-start(bf16[96,2560]{1,0:T(8,128)(2,1)S(1)} %collective-permute-done.21.refs_1_), channel_id=1, source_target_pairs={{1,3},{3,5},{5,7},{7,6},{6,4},{4,2},{2,0},{0,1},{9,11},{11,13},{13... | collective-permute-start | bytes 1474568 | tf_op jit(solution)/shard_map/ppermute | solution.py:530
  29.6 8.0 %collective-permute-done.1.refs_2_ = bf16[96,2432]{1,0:T(8,128)(2,1)S(1)} collective-permute-done((bf16[96,2432]{1,0:T(8,128)(2,1)S(1)}, bf16[96,2432]{1,0:T(8,128)(2,1)S(1)}, u32[]{:S(2)}, u32[]{:S(2)}) %collective-permute-start.1) | collective-permute-done | bytes 466976 | tf_op jit(solution)/shard_map/ppermute | solution.py:530
  37.6 2.0 %collective-permute-start.2 = (bf16[96,2432]{1,0:T(8,128)(2,1)S(1)}, bf16[96,2432]{1,0:T(8,128)(2,1)S(1)}, u32[]{:S(2)}, u32[]{:S(2)}) collective-permute-start(bf16[96,2432]{1,0:T(8,128)(2,1)S(1)} %collective-permute-done.1.refs_2_), channel_id=1, source_target_pairs={{1,3},{3,5},{5,7},{7,6},{6,4},{4,2},{2,0},{0,1},{9,11},{11,13},{13... | collective-permute-start | bytes 1400840 | tf_op jit(solution)/shard_map/ppermute | solution.py:530
  40.3 1.4 collective-permute-start.10
  41.7 6.4 %collective-permute-done.22.refs_2_ = bf16[96,2560]{1,0:T(8,128)(2,1)S(1)} collective-permute-done((bf16[96,2560]{1,0:T(8,128)(2,1)S(1)}, bf16[96,2560]{1,0:T(8,128)(2,1)S(1)}, u32[]{:S(2)}, u32[]{:S(2)}) %collective-permute-start.22) | collective-permute-done | bytes 491552 | tf_op jit(solution)/shard_map/ppermute | solution.py:530
  48.1 2.0 %collective-permute-start.23 = (bf16[96,2560]{1,0:T(8,128)(2,1)S(1)}, bf16[96,2560]{1,0:T(8,128)(2,1)S(1)}, u32[]{:S(2)}, u32[]{:S(2)}) collective-permute-start(bf16[96,2560]{1,0:T(8,128)(2,1)S(1)} %collective-permute-done.22.refs_2_), channel_id=1, source_target_pairs={{1,3},{3,5},{5,7},{7,6},{6,4},{4,2},{2,0},{0,1},{9,11},{11,13},{13... | collective-permute-start | bytes 1474568 | tf_op jit(solution)/shard_map/ppermute | solution.py:530
  50.8 7.3 %collective-permute-done.2.refs_3_ = bf16[96,2432]{1,0:T(8,128)(2,1)S(1)} collective-permute-done((bf16[96,2432]{1,0:T(8,128)(2,1)S(1)}, bf16[96,2432]{1,0:T(8,128)(2,1)S(1)}, u32[]{:S(2)}, u32[]{:S(2)}) %collective-permute-start.2) | collective-permute-done | bytes 466976 | tf_op jit(solution)/shard_map/ppermute | solution.py:530
  58.1 2.0 %collective-permute-start.3 = (bf16[96,2432]{1,0:T(8,128)(2,1)S(1)}, bf16[96,2432]{1,0:T(8,128)(2,1)S(1)}, u32[]{:S(2)}, u32[]{:S(2)}) collective-permute-start(bf16[96,2432]{1,0:T(8,128)(2,1)S(1)} %get-tuple-element.83.refs_0_), channel_id=1, source_target_pairs={{1,3},{3,5},{5,7},{7,6},{6,4},{4,2},{2,0},{0,1},{9,11},{11,13},{13... | collective-permute-start | bytes 1400840 | tf_op jit(solution)/shard_map/ppermute | solution.py:530
  60.8 1.4 collective-permute-start.11
  62.2 6.4 %collective-permute-done.23.refs_3_ = bf16[96,2560]{1,0:T(8,128)(2,1)S(1)} collective-permute-done((bf16[96,2560]{1,0:T(8,128)(2,1)S(1)}, bf16[96,2560]{1,0:T(8,128)(2,1)S(1)}, u32[]{:S(2)}, u32[]{:S(2)}) %collective-permute-start.23) | collective-permute-done | bytes 491552 | tf_op jit(solution)/shard_map/ppermute | solution.py:530
  68.6 2.0 %collective-permute-start.24 = (bf16[96,2560]{1,0:T(8,128)(2,1)S(1)}, bf16[96,2560]{1,0:T(8,128)(2,1)S(1)}, u32[]{:S(2)}, u32[]{:S(2)}) collective-permute-start(bf16[96,2560]{1,0:T(8,128)(2,1)S(1)} %collective-permute-done.23.refs_3_), channel_id=1, source_target_pairs={{1,3},{3,5},{5,7},{7,6},{6,4},{4,2},{2,0},{0,1},{9,11},{11,13},{13... | collective-permute-start | bytes 1474568 | tf_op jit(solution)/shard_map/ppermute | solution.py:530
  70.7 7.9 %collective-permute-done.3.refs_1_ = bf16[96,2432]{1,0:T(8,128)(2,1)S(1)} collective-permute-done((bf16[96,2432]{1,0:T(8,128)(2,1)S(1)}, bf16[96,2432]{1,0:T(8,128)(2,1)S(1)}, u32[]{:S(2)}, u32[]{:S(2)}) %collective-permute-start.3) | collective-permute-done | bytes 466976 | tf_op jit(solution)/shard_map/ppermute | solution.py:530
  78.6 2.0 %collective-permute-start.4 = (bf16[96,2432]{1,0:T(8,128)(2,1)S(1)}, bf16[96,2432]{1,0:T(8,128)(2,1)S(1)}, u32[]{:S(2)}, u32[]{:S(2)}) collective-permute-start(bf16[96,2432]{1,0:T(8,128)(2,1)S(1)} %collective-permute-done.3.refs_1_), channel_id=1, source_target_pairs={{1,3},{3,5},{5,7},{7,6},{6,4},{4,2},{2,0},{0,1},{9,11},{11,13},{13... | collective-permute-start | bytes 1400840 | tf_op jit(solution)/shard_map/ppermute | solution.py:530
  80.6 3.6 %collective-permute-done.11.refs_5_ = bf16[96,2432]{1,0:T(8,128)(2,1)S(1)} collective-permute-done((bf16[96,2432]{1,0:T(8,128)(2,1)S(1)}, bf16[96,2432]{1,0:T(8,128)(2,1)S(1)}, u32[]{:S(2)}, u32[]{:S(2)}) %collective-permute-start.11) | collective-permute-done | bytes 466976 | tf_op jit(solution)/shard_map/ppermute | solution.py:530
  84.3 2.0 %collective-permute-start.12 = (bf16[96,2432]{1,0:T(8,128)(2,1)S(1)}, bf16[96,2432]{1,0:T(8,128)(2,1)S(1)}, u32[]{:S(2)}, u32[]{:S(2)}) collective-permute-start(bf16[96,2432]{1,0:T(8,128)(2,1)S(1)} %get-tuple-element.79.refs_0_), channel_id=1, source_target_pairs={{1,0},{3,1},{5,3},{7,5},{6,7},{4,6},{2,4},{0,2},{9,8},{11,9},{13,1... | collective-permute-start | bytes 1400840 | tf_op jit(solution)/shard_map/ppermute | solution.py:530
  86.4 7.9 %collective-permute-done.20.refs_7_ = bf16[96,2432]{1,0:T(8,128)(2,1)S(1)} collective-permute-done((bf16[96,2432]{1,0:T(8,128)(2,1)S(1)}, bf16[96,2432]{1,0:T(8,128)(2,1)S(1)}, u32[]{:S(2)}, u32[]{:S(2)}) %collective-permute-start.20) | collective-permute-done | bytes 466976 | tf_op jit(solution)/shard_map/ppermute | solution.py:530
  94.4 1.4 collective-permute-start.28
  96.5 1.8 collective-permute-done.4.refs_2_
  99.0 5.3 %collective-permute-done.18.refs_6_ = bf16[96,2432]{1,0:T(8,128)(2,1)S(1)} collective-permute-done((bf16[96,2432]{1,0:T(8,128)(2,1)S(1)}, bf16[96,2432]{1,0:T(8,128)(2,1)S(1)}, u32[]{:S(2)}, u32[]{:S(2)}) %collective-permute-start.18) | collective-permute-done | bytes 466976 | tf_op jit(solution)/shard_map/ppermute | solution.py:530
  104.3 1.6 collective-permute-start.16
  105.9 1.6 collective-permute-start.5
  107.9 6.4 %collective-permute-done.12.refs_4_ = bf16[96,2432]{1,0:T(8,128)(2,1)S(1)} collective-permute-done((bf16[96,2432]{1,0:T(8,128)(2,1)S(1)}, bf16[96,2432]{1,0:T(8,128)(2,1)S(1)}, u32[]{:S(2)}, u32[]{:S(2)}) %collective-permute-start.12) | collective-permute-done | bytes 466976 | tf_op jit(solution)/shard_map/ppermute | solution.py:530
  114.4 6.0 %compose.3 = (bf16[8,768,768]{2,1,0:T(8,128)(2,1)S(1)}, bf16[8,96,768]{2,1,0:T(8,128)(2,1)S(1)}, bf16[2,768,768]{2,1,0:T(8,128)(2,1)S(1)}, bf16[768,768]{1,0:T(8,128)(2,1)S(1)}) custom-call(s32[1]{0:T(128)S(6)} %convert_element_type.3.last_ref, s32[1]{0:T(128)} %bitcast.place_ref, bf16[96,2560]{1,0:T(8,128)(2,1)S(1)} %copy-done.2, ...), custom_call_target="tpu_custom_call" | custom-call | flops 5435817984 | bytes 9437184 | tf_op jit(solution)/shard_map/compose/pallas_call | solution.py:259
  120.4 3.9 %collective-permute-done.19.refs_7_ = bf16[96,2432]{1,0:T(8,128)(2,1)S(1)} collective-permute-done((bf16[96,2432]{1,0:T(8,128)(2,1)S(1)}, bf16[96,2432]{1,0:T(8,128)(2,1)S(1)}, u32[]{:S(2)}, u32[]{:S(2)}) %collective-permute-start.19) | collective-permute-done | bytes 466976 | tf_op jit(solution)/shard_map/ppermute | solution.py:530
  124.3 1.6 collective-permute-start.17
  125.9 1.6 collective-permute-start.6
  127.5 4.1 %collective-permute-done.13.refs_5_ = bf16[96,2432]{1,0:T(8,128)(2,1)S(1)} collective-permute-done((bf16[96,2432]{1,0:T(8,128)(2,1)S(1)}, bf16[96,2432]{1,0:T(8,128)(2,1)S(1)}, u32[]{:S(2)}, u32[]{:S(2)}) %collective-permute-start.13) | collective-permute-done | bytes 466976 | tf_op jit(solution)/shard_map/ppermute | solution.py:530
  131.8 7.6 %compose.4 = (bf16[8,768,768]{2,1,0:T(8,128)(2,1)S(1)}, bf16[8,96,768]{2,1,0:T(8,128)(2,1)S(1)}, bf16[2,768,768]{2,1,0:T(8,128)(2,1)S(1)}, bf16[768,768]{1,0:T(8,128)(2,1)S(1)}) custom-call(s32[1]{0:T(128)S(6)} %convert_element_type.3.last_ref, s32[1]{0:T(128)} %bitcast.place_ref, ...), custom_call_target="tpu_custom_call", output_to_operand_aliasing={{0}: (11, {}), {1}: (12, {})} | custom-call | flops 5435817984 | bytes 9437184 | tf_op jit(solution)/shard_map/compose/pallas_call | solution.py:259
  139.4 2.7 %collective-permute-done.6.refs_2_ = bf16[96,2432]{1,0:T(8,128)(2,1)S(1)} collective-permute-done((bf16[96,2432]{1,0:T(8,128)(2,1)S(1)}, bf16[96,2432]{1,0:T(8,128)(2,1)S(1)}, u32[]{:S(2)}, u32[]{:S(2)}) %collective-permute-start.6) | collective-permute-done | bytes 466976 | tf_op jit(solution)/shard_map/ppermute | solution.py:530
  142.1 1.2 collective-permute-start.7
  144.1 6.6 %compose.5 = (bf16[8,768,768]{2,1,0:T(8,128)(2,1)S(1)}, bf16[8,96,768]{2,1,0:T(8,128)(2,1)S(1)}, bf16[2,768,768]{2,1,0:T(8,128)(2,1)S(1)}, bf16[768,768]{1,0:T(8,128)(2,1)S(1)}) custom-call(s32[1]{0:T(128)S(6)} %convert_element_type.3.last_ref, s32[1]{0:T(128)} %bitcast.place_ref, ...), custom_call_target="tpu_custom_call", output_to_operand_aliasing={{0}: (11, {}), {1}: (12, {})} | custom-call | flops 5435817984 | bytes 9437184 | tf_op jit(solution)/shard_map/compose/pallas_call | solution.py:259
  151.8 4.3 %chain.1 = (bf16[2,768,768]{2,1,0:T(8,128)(2,1)S(1)}, bf16[2,768,768]{2,1,0:T(8,128)(2,1)S(1)}, bf16[6,256,256]{2,1,0:T(8,128)(2,1)S(1)}) custom-call(s32[1]{0:T(128)} %bitcast.place_ref, bf16[96,2432]{1,0:T(8,128)(2,1)S(1)} %get-tuple-element.79.refs_0_, bf16[96,2432]{1,0:T(8,128)(2,1)S(1)} %collective-permute-done.5.refs_1_, ...), custom_call_target="tpu_custom_call" | custom-call | flops 3623878656 | bytes 9437184 | tf_op jit(solution)/shard_map/chain/pallas_call | solution.py:303
  156.9 2.3 %extend_factors.1 = (bf16[8,768,768]{2,1,0:T(8,128)(2,1)S(1)}, bf16[8,96,768]{2,1,0:T(8,128)(2,1)S(1)}) custom-call(s32[1]{0:T(128)} %bitcast.place_ref, bf16[2,768,768]{2,1,0:T(8,128)(2,1)S(1)} %get-tuple-element.124.gain_ref, bf16[8,768,768]{2,1,0:T(8,128)(2,1)S(1)} %get-tuple-element.125.factor_in, ...), custom_call_target="tpu_custom_call", output_to_operand_aliasing={{0}: (2, {}), {1}: (3, {})} | custom-call | flops 1811939328 | bytes 4718592 | tf_op jit(solution)/shard_map/extend_factors/pallas_call | solution.py:343
  159.2 1.8 hop.2
  161.0 0.9 collective-permute-start.32
  162.0 4.4 %own_rows.1.own_ref = f32[8,96,768]{2,1,0:T(8,128)S(1)} custom-call(s32[1]{0:T(128)} %bitcast.place_ref, bf16[2,768,768]{2,1,0:T(8,128)(2,1)S(1)} %get-tuple-element.133.half_ref.refs_0_, bf16[2,768,768]{2,1,0:T(8,128)(2,1)S(1)} %get-tuple-element.134.refs_1_, bf16[2,768,768]{2,1,0:T(8,128)(2,1)S(1)} %get-tuple-element.135.refs_2_, ...), custom_call_target="tpu_custom_call" | custom-call | flops 905969664 | bytes 9437184 | tf_op jit(solution)/shard_map/own_rows/pallas_call | solution.py:382
  166.4 1.8 hop.3
  168.2 1.3 collective-permute-start.33
  169.5 11.3 %collective-permute-done.33.refs_2_ = bf16[6,256,256]{2,1,0:T(8,128)(2,1)S(1)} collective-permute-done((bf16[6,256,256]{2,1,0:T(8,128)(2,1)S(1)}, bf16[6,256,256]{2,1,0:T(8,128)(2,1)S(1)}, u32[]{:S(2)}, u32[]{:S(2)}) %collective-permute-start.33) | collective-permute-done | bytes 786464 | tf_op jit(solution)/shard_map/ppermute | solution.py:589
  180.8 4.9 %finish.1 = f32[8,96,768]{2,1,0:T(8,128)} custom-call(bf16[8,768,768]{2,1,0:T(8,128)(2,1)S(1)} %get-tuple-element.127.factor_ref, f32[8,96,768]{2,1,0:T(8,128)S(1)} %own_rows.1.own_ref, bf16[8,96,768]{2,1,0:T(8,128)(2,1)S(1)} %get-tuple-element.138.mine_ref, bf16[6,256,256]{2,1,0:T(8,128)(2,1)S(1)} %collective-permute-done.31.refs_0_, ...), custom_call_target="tpu_custom_call" | custom-call | tf_op jit(solution)/shard_map/finish/pallas_call | solution.py:490
  (41 shorter events, 7.3 us)
Async XLA Ops:
  2.3 47.8 %copy-start = (f32[8,96,768]{2,1,0:T(8,128)S(1)}, f32[8,96,768]{2,1,0:T(8,128)}, u32[]{:S(2)}) copy-start(f32[8,96,768]{2,1,0:T(8,128)} %increment_ref.5) | copy-start | bytes 7077892
  2.3 47.8 %copy-start.1 = (bf16[8,96,768]{2,1,0:T(8,128)(2,1)S(1)}, bf16[8,96,768]{2,1,0:T(8,128)(2,1)}, u32[]{:S(2)}) copy-start(bf16[8,96,768]{2,1,0:T(8,128)(2,1)} %gain_ref.5) | copy-start | bytes 3538948
  2.3 14.8 %collective-permute-start = (bf16[96,2432]{1,0:T(8,128)(2,1)}, bf16[96,2432]{1,0:T(8,128)(2,1)S(1)}, u32[]{:S(2)}, u32[]{:S(2)}) collective-permute-start(bf16[96,2432]{1,0:T(8,128)(2,1)} %pack.4.refs_0_), channel_id=1, source_target_pairs={{1,3},{3,5},{5,7},{7,6},{6,4},{4,2},{2,0},{0,1},{9,11},{11,13},{13... | collective-permute-start | bytes 1400840 | tf_op jit(solution)/shard_map/ppermute | solution.py:530
  5.2 13.9 %collective-permute-start.8 = (bf16[96,2432]{1,0:T(8,128)(2,1)}, bf16[96,2432]{1,0:T(8,128)(2,1)}, u32[]{:S(2)}, u32[]{:S(2)}) collective-permute-start(bf16[96,2432]{1,0:T(8,128)(2,1)} %pack.4.refs_0_), channel_id=1, source_target_pairs={{1,0},{3,1},{5,3},{7,5},{6,7},{4,6},{2,4},{0,2},{9,8},{11,9},{13,1... | collective-permute-start | bytes 1400840 | tf_op jit(solution)/shard_map/ppermute | solution.py:530
  7.9 86.3 %copy-start.2 = (bf16[96,2560]{1,0:T(8,128)(2,1)S(1)}, bf16[96,2560]{1,0:T(8,128)(2,1)}, u32[]{:S(2)}) copy-start(bf16[96,2560]{1,0:T(8,128)(2,1)} %pack.5.refs_0_) | copy-start | bytes 1474564
  7.9 19.6 %collective-permute-start.21 = (bf16[96,2560]{1,0:T(8,128)(2,1)}, bf16[96,2560]{1,0:T(8,128)(2,1)S(1)}, u32[]{:S(2)}, u32[]{:S(2)}) collective-permute-start(bf16[96,2560]{1,0:T(8,128)(2,1)} %pack.5.refs_0_), channel_id=1, source_target_pairs={{1,3},{3,5},{5,7},{7,6},{6,4},{4,2},{2,0},{0,1},{9,11},{11,13},{13... | collective-permute-start | bytes 1474568 | tf_op jit(solution)/shard_map/ppermute | solution.py:530
  17.0 20.5 %collective-permute-start.1 = (bf16[96,2432]{1,0:T(8,128)(2,1)S(1)}, bf16[96,2432]{1,0:T(8,128)(2,1)S(1)}, u32[]{:S(2)}, u32[]{:S(2)}) collective-permute-start(bf16[96,2432]{1,0:T(8,128)(2,1)S(1)} %collective-permute-done.refs_1_), channel_id=1, source_target_pairs={{1,3},{3,5},{5,7},{7,6},{6,4},{4,2},{2,0},{0,1},{9,11},{11,13},{13... | collective-permute-start | bytes 1400840 | tf_op jit(solution)/shard_map/ppermute | solution.py:530
  19.0 20.5 %collective-permute-start.25 = (bf16[96,2560]{1,0:T(8,128)(2,1)}, bf16[96,2560]{1,0:T(8,128)(2,1)S(1)}, u32[]{:S(2)}, u32[]{:S(2)}) collective-permute-start(bf16[96,2560]{1,0:T(8,128)(2,1)} %pack.5.refs_0_), channel_id=1, source_target_pairs={{1,0},{3,1},{5,3},{7,5},{6,7},{4,6},{2,4},{0,2},{9,8},{11,9},{13,1... | collective-permute-start | bytes 1474568 | tf_op jit(solution)/shard_map/ppermute | solution.py:530
  19.1 21.2 %collective-permute-start.9 = (bf16[96,2432]{1,0:T(8,128)(2,1)}, bf16[96,2432]{1,0:T(8,128)(2,1)S(1)}, u32[]{:S(2)}, u32[]{:S(2)}) collective-permute-start(bf16[96,2432]{1,0:T(8,128)(2,1)} %collective-permute-done.8.refs_4_), channel_id=1, source_target_pairs={{1,0},{3,1},{5,3},{7,5},{6,7},{4,6},{2,4},{0,2},{9,8},{11,9},{13,1... | collective-permute-start | bytes 1400840 | tf_op jit(solution)/shard_map/ppermute | solution.py:530
  27.6 20.5 %collective-permute-start.22 = (bf16[96,2560]{1,0:T(8,128)(2,1)S(1)}, bf16[96,2560]{1,0:T(8,128)(2,1)S(1)}, u32[]{:S(2)}, u32[]{:S(2)}) collective-permute-start(bf16[96,2560]{1,0:T(8,128)(2,1)S(1)} %collective-permute-done.21.refs_1_), channel_id=1, source_target_pairs={{1,3},{3,5},{5,7},{7,6},{6,4},{4,2},{2,0},{0,1},{9,11},{11,13},{13... | collective-permute-start | bytes 1474568 | tf_op jit(solution)/shard_map/ppermute | solution.py:530
  37.6 20.5 %collective-permute-start.2 = (bf16[96,2432]{1,0:T(8,128)(2,1)S(1)}, bf16[96,2432]{1,0:T(8,128)(2,1)S(1)}, u32[]{:S(2)}, u32[]{:S(2)}) collective-permute-start(bf16[96,2432]{1,0:T(8,128)(2,1)S(1)} %collective-permute-done.1.refs_2_), channel_id=1, source_target_pairs={{1,3},{3,5},{5,7},{7,6},{6,4},{4,2},{2,0},{0,1},{9,11},{11,13},{13... | collective-permute-start | bytes 1400840 | tf_op jit(solution)/shard_map/ppermute | solution.py:530
  39.6 20.5 %collective-permute-start.26 = (bf16[96,2560]{1,0:T(8,128)(2,1)S(1)}, bf16[96,2560]{1,0:T(8,128)(2,1)S(1)}, u32[]{:S(2)}, u32[]{:S(2)}) collective-permute-start(bf16[96,2560]{1,0:T(8,128)(2,1)S(1)} %collective-permute-done.25.refs_5_), channel_id=1, source_target_pairs={{1,0},{3,1},{5,3},{7,5},{6,7},{4,6},{2,4},{0,2},{9,8},{11,9},{13,1... | collective-permute-start | bytes 1474568 | tf_op jit(solution)/shard_map/ppermute | solution.py:530
  40.3 20.5 %collective-permute-start.10 = (bf16[96,2432]{1,0:T(8,128)(2,1)S(1)}, bf16[96,2432]{1,0:T(8,128)(2,1)S(1)}, u32[]{:S(2)}, u32[]{:S(2)}) collective-permute-start(bf16[96,2432]{1,0:T(8,128)(2,1)S(1)} %collective-permute-done.9.refs_5_), channel_id=1, source_target_pairs={{1,0},{3,1},{5,3},{7,5},{6,7},{4,6},{2,4},{0,2},{9,8},{11,9},{13,1... | collective-permute-start | bytes 1400840 | tf_op jit(solution)/shard_map/ppermute | solution.py:530
  48.1 20.5 %collective-permute-start.23 = (bf16[96,2560]{1,0:T(8,128)(2,1)S(1)}, bf16[96,2560]{1,0:T(8,128)(2,1)S(1)}, u32[]{:S(2)}, u32[]{:S(2)}) collective-permute-start(bf16[96,2560]{1,0:T(8,128)(2,1)S(1)} %collective-permute-done.22.refs_2_), channel_id=1, source_target_pairs={{1,3},{3,5},{5,7},{7,6},{6,4},{4,2},{2,0},{0,1},{9,11},{11,13},{13... | collective-permute-start | bytes 1474568 | tf_op jit(solution)/shard_map/ppermute | solution.py:530
  58.1 20.5 %collective-permute-start.3 = (bf16[96,2432]{1,0:T(8,128)(2,1)S(1)}, bf16[96,2432]{1,0:T(8,128)(2,1)S(1)}, u32[]{:S(2)}, u32[]{:S(2)}) collective-permute-start(bf16[96,2432]{1,0:T(8,128)(2,1)S(1)} %get-tuple-element.83.refs_0_), channel_id=1, source_target_pairs={{1,3},{3,5},{5,7},{7,6},{6,4},{4,2},{2,0},{0,1},{9,11},{11,13},{13... | collective-permute-start | bytes 1400840 | tf_op jit(solution)/shard_map/ppermute | solution.py:530
  60.1 24.2 %collective-permute-start.27 = (bf16[96,2560]{1,0:T(8,128)(2,1)S(1)}, bf16[96,2560]{1,0:T(8,128)(2,1)S(1)}, u32[]{:S(2)}, u32[]{:S(2)}) collective-permute-start(bf16[96,2560]{1,0:T(8,128)(2,1)S(1)} %collective-permute-done.26.refs_6_), channel_id=1, source_target_pairs={{1,0},{3,1},{5,3},{7,5},{6,7},{4,6},{2,4},{0,2},{9,8},{11,9},{13,1... | collective-permute-start | bytes 1474568 | tf_op jit(solution)/shard_map/ppermute | solution.py:530
  60.8 23.5 %collective-permute-start.11 = (bf16[96,2432]{1,0:T(8,128)(2,1)S(1)}, bf16[96,2432]{1,0:T(8,128)(2,1)S(1)}, u32[]{:S(2)}, u32[]{:S(2)}) collective-permute-start(bf16[96,2432]{1,0:T(8,128)(2,1)S(1)} %get-tuple-element.83.refs_0_), channel_id=1, source_target_pairs={{1,0},{3,1},{5,3},{7,5},{6,7},{4,6},{2,4},{0,2},{9,8},{11,9},{13,1... | collective-permute-start | bytes 1400840 | tf_op jit(solution)/shard_map/ppermute | solution.py:530
  68.6 25.6 %collective-permute-start.24 = (bf16[96,2560]{1,0:T(8,128)(2,1)S(1)}, bf16[96,2560]{1,0:T(8,128)(2,1)S(1)}, u32[]{:S(2)}, u32[]{:S(2)}) collective-permute-start(bf16[96,2560]{1,0:T(8,128)(2,1)S(1)} %collective-permute-done.23.refs_3_), channel_id=1, source_target_pairs={{1,3},{3,5},{5,7},{7,6},{6,4},{4,2},{2,0},{0,1},{9,11},{11,13},{13... | collective-permute-start | bytes 1474568 | tf_op jit(solution)/shard_map/ppermute | solution.py:530
  70.6 23.6 %collective-permute-start.20 = (bf16[96,2432]{1,0:T(8,128)(2,1)S(1)}, bf16[96,2432]{1,0:T(8,128)(2,1)S(1)}, u32[]{:S(2)}, u32[]{:S(2)}) collective-permute-start(bf16[96,2432]{1,0:T(8,128)(2,1)S(1)} %collective-permute-done.10.refs_6_), channel_id=1, source_target_pairs={{1,0},{3,1},{5,3},{7,5},{6,7},{4,6},{2,4},{0,2},{9,8},{11,9},{13,1... | collective-permute-start | bytes 1400840 | tf_op jit(solution)/shard_map/ppermute | solution.py:530
  78.6 19.7 %collective-permute-start.4 = (bf16[96,2432]{1,0:T(8,128)(2,1)S(1)}, bf16[96,2432]{1,0:T(8,128)(2,1)S(1)}, u32[]{:S(2)}, u32[]{:S(2)}) collective-permute-start(bf16[96,2432]{1,0:T(8,128)(2,1)S(1)} %collective-permute-done.3.refs_1_), channel_id=1, source_target_pairs={{1,3},{3,5},{5,7},{7,6},{6,4},{4,2},{2,0},{0,1},{9,11},{11,13},{13... | collective-permute-start | bytes 1400840 | tf_op jit(solution)/shard_map/ppermute | solution.py:530
  84.3 20.0 %collective-permute-start.18 = (bf16[96,2432]{1,0:T(8,128)(2,1)S(1)}, bf16[96,2432]{1,0:T(8,128)(2,1)S(1)}, u32[]{:S(2)}, u32[]{:S(2)}) collective-permute-start(bf16[96,2432]{1,0:T(8,128)(2,1)S(1)} %collective-permute-done.11.refs_5_), channel_id=1, source_target_pairs={{1,0},{3,1},{5,3},{7,5},{6,7},{4,6},{2,4},{0,2},{9,8},{11,9},{13,1... | collective-permute-start | bytes 1400840 | tf_op jit(solution)/shard_map/ppermute | solution.py:530
  84.3 29.9 %collective-permute-start.12 = (bf16[96,2432]{1,0:T(8,128)(2,1)S(1)}, bf16[96,2432]{1,0:T(8,128)(2,1)S(1)}, u32[]{:S(2)}, u32[]{:S(2)}) collective-permute-start(bf16[96,2432]{1,0:T(8,128)(2,1)S(1)} %get-tuple-element.79.refs_0_), channel_id=1, source_target_pairs={{1,0},{3,1},{5,3},{7,5},{6,7},{4,6},{2,4},{0,2},{9,8},{11,9},{13,1... | collective-permute-start | bytes 1400840 | tf_op jit(solution)/shard_map/ppermute | solution.py:530
  94.4 37.4 %copy-start.3 = (bf16[96,2432]{1,0:T(8,128)(2,1)S(1)}, bf16[96,2432]{1,0:T(8,128)(2,1)}, u32[]{:S(2)}) copy-start(bf16[96,2432]{1,0:T(8,128)(2,1)} %pack.4.refs_0_) | copy-start | bytes 1400836
  94.4 11.4 %collective-permute-start.28 = (bf16[8,96,128]{2,1,0:T(8,128)(2,1)S(1)}, bf16[8,96,128]{2,1,0:T(8,128)(2,1)S(1)}, u32[]{:S(2)}, u32[]{:S(2)}) collective-permute-start(bf16[8,96,128]{2,1,0:T(8,128)(2,1)S(1)} %collect.1.refs_11_), channel_id=1, source_target_pairs={{0,24},{1,25},{2,26},{3,27},{4,28},{5,29},{6,30},{7,31}} | collective-permute-start | bytes 589832 | tf_op jit(solution)/shard_map/ppermute | solution.py:567
  95.9 11.6 %collective-permute-start.29 = (bf16[8,96,128]{2,1,0:T(8,128)(2,1)S(1)}, bf16[8,96,128]{2,1,0:T(8,128)(2,1)S(1)}, u32[]{:S(2)}, u32[]{:S(2)}) collective-permute-start(bf16[8,96,128]{2,1,0:T(8,128)(2,1)S(1)} %collect.1.refs_11_), channel_id=1, source_target_pairs={{8,24},{9,25},{10,26},{11,27},{12,28},{13,29},{14,30},{15,31}} | collective-permute-start | bytes 589832 | tf_op jit(solution)/shard_map/ppermute | solution.py:567
  98.4 16.0 %collective-permute-start.30 = (bf16[8,96,128]{2,1,0:T(8,128)(2,1)S(1)}, bf16[8,96,128]{2,1,0:T(8,128)(2,1)S(1)}, u32[]{:S(2)}, u32[]{:S(2)}) collective-permute-start(bf16[8,96,128]{2,1,0:T(8,128)(2,1)S(1)} %collect.1.refs_11_), channel_id=1, source_target_pairs={{16,24},{17,25},{18,26},{19,27},{20,28},{21,29},{22,30},{23,31}} | collective-permute-start | bytes 589832 | tf_op jit(solution)/shard_map/ppermute | solution.py:567
  104.3 16.1 %collective-permute-start.16 = (bf16[96,2432]{1,0:T(8,128)(2,1)S(1)}, bf16[96,2432]{1,0:T(8,128)(2,1)S(1)}, u32[]{:S(2)}, u32[]{:S(2)}) collective-permute-start(bf16[96,2432]{1,0:T(8,128)(2,1)S(1)} %collective-permute-done.4.refs_2_), channel_id=1, source_target_pairs={{1,3},{3,5},{5,7},{7,6},{6,4},{4,2},{2,0},{0,1},{9,11},{11,13},{13... | collective-permute-start | bytes 1400840 | tf_op jit(solution)/shard_map/ppermute | solution.py:530
  105.9 20.0 %collective-permute-start.5 = (bf16[96,2432]{1,0:T(8,128)(2,1)S(1)}, bf16[96,2432]{1,0:T(8,128)(2,1)S(1)}, u32[]{:S(2)}, u32[]{:S(2)}) collective-permute-start(bf16[96,2432]{1,0:T(8,128)(2,1)S(1)} %get-tuple-element.79.refs_0_), channel_id=1, source_target_pairs={{1,3},{3,5},{5,7},{7,6},{6,4},{4,2},{2,0},{0,1},{9,11},{11,13},{13... | collective-permute-start | bytes 1400840 | tf_op jit(solution)/shard_map/ppermute | solution.py:530
  107.4 16.9 %collective-permute-start.19 = (bf16[96,2432]{1,0:T(8,128)(2,1)S(1)}, bf16[96,2432]{1,0:T(8,128)(2,1)S(1)}, u32[]{:S(2)}, u32[]{:S(2)}) collective-permute-start(bf16[96,2432]{1,0:T(8,128)(2,1)S(1)} %collective-permute-done.18.refs_6_), channel_id=1, source_target_pairs={{1,0},{3,1},{5,3},{7,5},{6,7},{4,6},{2,4},{0,2},{9,8},{11,9},{13,1... | collective-permute-start | bytes 1400840 | tf_op jit(solution)/shard_map/ppermute | solution.py:530
  114.3 17.2 %collective-permute-start.13 = (bf16[96,2432]{1,0:T(8,128)(2,1)S(1)}, bf16[96,2432]{1,0:T(8,128)(2,1)S(1)}, u32[]{:S(2)}, u32[]{:S(2)}) collective-permute-start(bf16[96,2432]{1,0:T(8,128)(2,1)S(1)} %collective-permute-done.12.refs_4_), channel_id=1, source_target_pairs={{1,0},{3,1},{5,3},{7,5},{6,7},{4,6},{2,4},{0,2},{9,8},{11,9},{13,1... | collective-permute-start | bytes 1400840 | tf_op jit(solution)/shard_map/ppermute | solution.py:530
  124.3 15.1 %collective-permute-start.17 = (bf16[96,2432]{1,0:T(8,128)(2,1)S(1)}, bf16[96,2432]{1,0:T(8,128)(2,1)S(1)}, u32[]{:S(2)}, u32[]{:S(2)}) collective-permute-start(bf16[96,2432]{1,0:T(8,128)(2,1)S(1)} %collective-permute-done.16.refs_3_), channel_id=1, source_target_pairs={{1,3},{3,5},{5,7},{7,6},{6,4},{4,2},{2,0},{0,1},{9,11},{11,13},{13... | collective-permute-start | bytes 1400840 | tf_op jit(solution)/shard_map/ppermute | solution.py:530
  125.9 16.2 %collective-permute-start.6 = (bf16[96,2432]{1,0:T(8,128)(2,1)S(1)}, bf16[96,2432]{1,0:T(8,128)(2,1)S(1)}, u32[]{:S(2)}, u32[]{:S(2)}) collective-permute-start(bf16[96,2432]{1,0:T(8,128)(2,1)S(1)} %collective-permute-done.5.refs_1_), channel_id=1, source_target_pairs={{1,3},{3,5},{5,7},{7,6},{6,4},{4,2},{2,0},{0,1},{9,11},{11,13},{13... | collective-permute-start | bytes 1400840 | tf_op jit(solution)/shard_map/ppermute | solution.py:530
  131.5 10.6 %collective-permute-start.14 = (bf16[96,2432]{1,0:T(8,128)(2,1)S(1)}, bf16[96,2432]{1,0:T(8,128)(2,1)S(1)}, u32[]{:S(2)}, u32[]{:S(2)}) collective-permute-start(bf16[96,2432]{1,0:T(8,128)(2,1)S(1)} %collective-permute-done.13.refs_5_), channel_id=1, source_target_pairs={{1,0},{3,1},{5,3},{7,5},{6,7},{4,6},{2,4},{0,2},{9,8},{11,9},{13,1... | collective-permute-start | bytes 1400840 | tf_op jit(solution)/shard_map/ppermute | solution.py:530
  142.1 8.9 %collective-permute-start.7 = (bf16[96,2432]{1,0:T(8,128)(2,1)S(1)}, bf16[96,2432]{1,0:T(8,128)(2,1)S(1)}, u32[]{:S(2)}, u32[]{:S(2)}) collective-permute-start(bf16[96,2432]{1,0:T(8,128)(2,1)S(1)} %collective-permute-done.6.refs_2_), channel_id=1, source_target_pairs={{1,3},{3,5},{5,7},{7,6},{6,4},{4,2},{2,0},{0,1},{9,11},{11,13},{13... | collective-permute-start | bytes 1400840 | tf_op jit(solution)/shard_map/ppermute | solution.py:530
  143.3 8.6 %collective-permute-start.15 = (bf16[96,2432]{1,0:T(8,128)(2,1)S(1)}, bf16[96,2432]{1,0:T(8,128)(2,1)S(1)}, u32[]{:S(2)}, u32[]{:S(2)}) collective-permute-start(bf16[96,2432]{1,0:T(8,128)(2,1)S(1)} %collective-permute-done.14.refs_6_), channel_id=1, source_target_pairs={{1,0},{3,1},{5,3},{7,5},{6,7},{4,6},{2,4},{0,2},{9,8},{11,9},{13,1... | collective-permute-start | bytes 1400840 | tf_op jit(solution)/shard_map/ppermute | solution.py:530
  156.2 3.0 %collective-permute-start.31 = (bf16[6,256,256]{2,1,0:T(8,128)(2,1)S(1)}, bf16[6,256,256]{2,1,0:T(8,128)(2,1)S(1)}, u32[]{:S(2)}, u32[]{:S(2)}) collective-permute-start(bf16[6,256,256]{2,1,0:T(8,128)(2,1)S(1)} %get-tuple-element.128), channel_id=1, source_target_pairs={{24,16},{25,17},{26,18},{27,19},{28,20},{29,21},{30,22},{31,23}} | collective-permute-start | bytes 2359304 | tf_op jit(solution)/shard_map/ppermute | solution.py:589
  161.0 5.3 %collective-permute-start.32 = (bf16[6,256,256]{2,1,0:T(8,128)(2,1)S(1)}, bf16[6,256,256]{2,1,0:T(8,128)(2,1)S(1)}, u32[]{:S(2)}, u32[]{:S(2)}) collective-permute-start(bf16[6,256,256]{2,1,0:T(8,128)(2,1)S(1)} %hop.2), channel_id=1, source_target_pairs={{16,8},{17,9},{18,10},{19,11},{20,12},{21,13},{22,14},{23,15}} | collective-permute-start | bytes 2359304 | tf_op jit(solution)/shard_map/ppermute | solution.py:589
  168.2 12.6 %collective-permute-start.33 = (bf16[6,256,256]{2,1,0:T(8,128)(2,1)S(1)}, bf16[6,256,256]{2,1,0:T(8,128)(2,1)S(1)}, u32[]{:S(2)}, u32[]{:S(2)}) collective-permute-start(bf16[6,256,256]{2,1,0:T(8,128)(2,1)S(1)} %hop.3), channel_id=1, source_target_pairs={{8,0},{9,1},{10,2},{11,3},{12,4},{13,5},{14,6},{15,7}} | collective-permute-start | bytes 2359304 | tf_op jit(solution)/shard_map/ppermute | solution.py:589

commit v19 on v18

--- a/solution.py
+++ b/solution.py
@@ -399,11 +399,11 @@
 
 
 def upper_blocks(width):
-    return [(a, b) for a in range(0, width, TILE) for b in range(a, width, TILE)]
+    return [(a, b) for a in range(0, width, LANES) for b in range(a, width, LANES)]
 
 
 def blocks_shape(width):
-    return (len(upper_blocks(width)), TILE, TILE)
+    return (len(upper_blocks(width)), LANES, LANES)
 
 
 def identity(size):
@@ -413,11 +413,11 @@
 
 
 def fold(half_ref, packed_ref):
-    one = identity(TILE)
+    one = identity(LANES)
     for n, (a, b) in enumerate(upper_blocks(half_ref.shape[0])):
-        block = half_ref[a:a + TILE, b:b + TILE]
+        block = half_ref[a:a + LANES, b:b + LANES]
         if a != b:
-            block = block.astype(F32) + nt(one, half_ref[b:b + TILE, a:a + TILE])
+            block = block.astype(F32) + nt(one, half_ref[b:b + LANES, a:a + LANES])
         packed_ref[n] = block.astype(BF16)
 
 
@@ -432,7 +432,9 @@
     out_ref, covariance, middle, ahead = refs[arrived:]
     width = factor_ref.shape[1]
     for n, (a, b) in enumerate(upper_blocks(width)):
-        covariance[a:a + TILE, b:b + TILE] = arrived_sum(refs[:arrived], n)
+        covariance[a:a + LANES, b:b + LANES] = arrived_sum(refs[:arrived], n)
+    for a in range(0, width, TILE):
+        covariance[a + LANES:a + TILE, a:a + LANES] = jnp.zeros((LANES, LANES), BF16)
     for j in range(0, width, TILE):
         cols = slice(j, j + TILE)
         middle[:, cols] = jnp.dot(
@@ -462,15 +464,15 @@
 def finish_kernel(arrived, factor_ref, own_ref, mine_ref, *refs):
     out_ref, covariance, middle, rows_out, copied = refs[arrived:]
     steps, rows, width = own_ref.shape
-    one = identity(TILE)
+    one = identity(LANES)
     for n, (a, b) in enumerate(upper_blocks(width)):
         block = arrived_sum(refs[:arrived], n)
         turned = nt(one, block)
         if a == b:
-            covariance[a:a + TILE, b:b + TILE] = (block.astype(F32) + turned).astype(BF16)
+            covariance[a:a + LANES, b:b + LANES] = (block.astype(F32) + turned).astype(BF16)
         else:
-            covariance[a:a + TILE, b:b + TILE] = block
-            covariance[b:b + TILE, a:a + TILE] = turned.astype(BF16)
+            covariance[a:a + LANES, b:b + LANES] = block
+            covariance[b:b + LANES, a:a + LANES] = turned.astype(BF16)
     mine = mine_ref[...].reshape(steps * rows, width)
     for j in range(0, width, TILE):
         cols = slice(j, j + TILE)

time: 186 us -> 186 us (level)
  no operation moved by 1% of the time
where the time goes in v19:
time: 186 us
  waiting for transfers between devices  97.8 us (53%)
  Pallas kernels  46.7 us (25%)
  starting transfers between devices  41 us (22%)
    ppermute x28, waiting for transfers between devices, passed(): lax.ppermute(array, 'tile', [(cycle[n], cycle[(n + way) % count]) for n i...  87.8 us
    ppermute x28, starting transfers between devices, passed(): lax.ppermute(array, 'tile', [(cycle[n], cycle[(n + way) % count]) for n i...  35.3 us
    pallas_call x3, Pallas kernels, compose(): pl.pallas_call(functools.partial(compose_kernel, cycle, right, turns, fir...  20.2 us
    ppermute x3, waiting for transfers between devices, local(): packed.append(lax.ppermute(before, 'tm', [(turn, turn - 1)]))  10 us
    pallas_call x3, Pallas kernels, pack(): pl.pallas_call(functools.partial(pack_kernel, count, ranges), grid_spec=p...  5.57 us
    pallas_call x1, Pallas kernels, finish(): pl.pallas_call(functools.partial(finish_kernel, len(packed)), in_specs=[v...  5.07 us
    pallas_call x1, Pallas kernels, chain(): pl.pallas_call(functools.partial(chain_kernel, cycle, right, turns), in_s...  4.63 us
    pallas_call x2, Pallas kernels, hop(): pl.pallas_call(functools.partial(hop_kernel, len(packed)), in_specs=[vmem...  4.39 us
  transfers between devices with their start and end apart: 34, of which 20 were waited for; matrix products, arithmetic and copies ran while one was open for 0% of the time, Pallas kernels for 16%

profile of v19, /device:TPU:0, one launch (start us, length us, event | category | flops | bytes accessed | tf_op | source)
XLA Modules:
  0.0 185.8 jit_solution(6144950075851318858)
XLA Ops:
  0.0 2.3 %pack.4.refs_0_ = bf16[96,2432]{1,0:T(8,128)(2,1)} custom-call(s32[1]{0:T(128)} %bitcast.place_ref, s32[1]{0:T(128)} %bitcast.1.block_ref, bf16[8,96,768]{2,1,0:T(8,128)(2,1)} %gain_ref.5, f32[8,96,768]{2,1,0:T(8,128)} %increment_ref.5), custom_call_target="tpu_custom_call" | custom-call | tf_op jit(solution)/shard_map/pack/pallas_call | solution.py:80
  2.3 3.0 %collective-permute-start = (bf16[96,2432]{1,0:T(8,128)(2,1)}, bf16[96,2432]{1,0:T(8,128)(2,1)S(1)}, u32[]{:S(2)}, u32[]{:S(2)}) collective-permute-start(bf16[96,2432]{1,0:T(8,128)(2,1)} %pack.4.refs_0_), channel_id=1, source_target_pairs={{1,3},{3,5},{5,7},{7,6},{6,4},{4,2},{2,0},{0,1},{9,11},{11,13},{13... | collective-permute-start | bytes 1400840 | tf_op jit(solution)/shard_map/ppermute | solution.py:532
  5.3 2.6 %pack.5.refs_0_ = bf16[96,2560]{1,0:T(8,128)(2,1)} custom-call(s32[1]{0:T(128)} %bitcast.place_ref, s32[1]{0:T(128)} %bitcast.1.block_ref, bf16[8,96,768]{2,1,0:T(8,128)(2,1)} %gain_ref.5, f32[8,96,768]{2,1,0:T(8,128)} %increment_ref.5, f32[96,768]{1,0:T(8,128)} %refs_0_.1), custom_call_target="tpu_custom_call" | custom-call | tf_op jit(solution)/shard_map/pack/pallas_call | solution.py:80
  7.9 1.9 %collective-permute-start.21 = (bf16[96,2560]{1,0:T(8,128)(2,1)}, bf16[96,2560]{1,0:T(8,128)(2,1)S(1)}, u32[]{:S(2)}, u32[]{:S(2)}) collective-permute-start(bf16[96,2560]{1,0:T(8,128)(2,1)} %pack.5.refs_0_), channel_id=1, source_target_pairs={{1,3},{3,5},{5,7},{7,6},{6,4},{4,2},{2,0},{0,1},{9,11},{11,13},{13... | collective-permute-start | bytes 1474568 | tf_op jit(solution)/shard_map/ppermute | solution.py:532
  9.9 7.2 %collective-permute-done.refs_1_ = bf16[96,2432]{1,0:T(8,128)(2,1)S(1)} collective-permute-done((bf16[96,2432]{1,0:T(8,128)(2,1)}, bf16[96,2432]{1,0:T(8,128)(2,1)S(1)}, u32[]{:S(2)}, u32[]{:S(2)}) %collective-permute-start) | collective-permute-done | bytes 466976 | tf_op jit(solution)/shard_map/ppermute | solution.py:532
  17.0 2.0 %collective-permute-start.1 = (bf16[96,2432]{1,0:T(8,128)(2,1)S(1)}, bf16[96,2432]{1,0:T(8,128)(2,1)S(1)}, u32[]{:S(2)}, u32[]{:S(2)}) collective-permute-start(bf16[96,2432]{1,0:T(8,128)(2,1)S(1)} %collective-permute-done.refs_1_), channel_id=1, source_target_pairs={{1,3},{3,5},{5,7},{7,6},{6,4},{4,2},{2,0},{0,1},{9,11},{11,13},{13... | collective-permute-start | bytes 1400840 | tf_op jit(solution)/shard_map/ppermute | solution.py:532
  19.1 2.0 %collective-permute-start.9 = (bf16[96,2432]{1,0:T(8,128)(2,1)}, bf16[96,2432]{1,0:T(8,128)(2,1)S(1)}, u32[]{:S(2)}, u32[]{:S(2)}) collective-permute-start(bf16[96,2432]{1,0:T(8,128)(2,1)} %collective-permute-done.8.refs_4_), channel_id=1, source_target_pairs={{1,0},{3,1},{5,3},{7,5},{6,7},{4,6},{2,4},{0,2},{9,8},{11,9},{13,1... | collective-permute-start | bytes 1400840 | tf_op jit(solution)/shard_map/ppermute | solution.py:532
  21.1 6.4 %collective-permute-done.21.refs_1_ = bf16[96,2560]{1,0:T(8,128)(2,1)S(1)} collective-permute-done((bf16[96,2560]{1,0:T(8,128)(2,1)}, bf16[96,2560]{1,0:T(8,128)(2,1)S(1)}, u32[]{:S(2)}, u32[]{:S(2)}) %collective-permute-start.21) | collective-permute-done | bytes 491552 | tf_op jit(solution)/shard_map/ppermute | solution.py:532
  27.6 2.0 %collective-permute-start.22 = (bf16[96,2560]{1,0:T(8,128)(2,1)S(1)}, bf16[96,2560]{1,0:T(8,128)(2,1)S(1)}, u32[]{:S(2)}, u32[]{:S(2)}) collective-permute-start(bf16[96,2560]{1,0:T(8,128)(2,1)S(1)} %collective-permute-done.21.refs_1_), channel_id=1, source_target_pairs={{1,3},{3,5},{5,7},{7,6},{6,4},{4,2},{2,0},{0,1},{9,11},{11,13},{13... | collective-permute-start | bytes 1474568 | tf_op jit(solution)/shard_map/ppermute | solution.py:532
  29.6 8.0 %collective-permute-done.1.refs_2_ = bf16[96,2432]{1,0:T(8,128)(2,1)S(1)} collective-permute-done((bf16[96,2432]{1,0:T(8,128)(2,1)S(1)}, bf16[96,2432]{1,0:T(8,128)(2,1)S(1)}, u32[]{:S(2)}, u32[]{:S(2)}) %collective-permute-start.1) | collective-permute-done | bytes 466976 | tf_op jit(solution)/shard_map/ppermute | solution.py:532
  37.6 2.0 %collective-permute-start.2 = (bf16[96,2432]{1,0:T(8,128)(2,1)S(1)}, bf16[96,2432]{1,0:T(8,128)(2,1)S(1)}, u32[]{:S(2)}, u32[]{:S(2)}) collective-permute-start(bf16[96,2432]{1,0:T(8,128)(2,1)S(1)} %collective-permute-done.1.refs_2_), channel_id=1, source_target_pairs={{1,3},{3,5},{5,7},{7,6},{6,4},{4,2},{2,0},{0,1},{9,11},{11,13},{13... | collective-permute-start | bytes 1400840 | tf_op jit(solution)/shard_map/ppermute | solution.py:532
  40.3 1.4 collective-permute-start.10
  41.7 6.4 %collective-permute-done.22.refs_2_ = bf16[96,2560]{1,0:T(8,128)(2,1)S(1)} collective-permute-done((bf16[96,2560]{1,0:T(8,128)(2,1)S(1)}, bf16[96,2560]{1,0:T(8,128)(2,1)S(1)}, u32[]{:S(2)}, u32[]{:S(2)}) %collective-permute-start.22) | collective-permute-done | bytes 491552 | tf_op jit(solution)/shard_map/ppermute | solution.py:532
  48.1 2.0 %collective-permute-start.23 = (bf16[96,2560]{1,0:T(8,128)(2,1)S(1)}, bf16[96,2560]{1,0:T(8,128)(2,1)S(1)}, u32[]{:S(2)}, u32[]{:S(2)}) collective-permute-start(bf16[96,2560]{1,0:T(8,128)(2,1)S(1)} %collective-permute-done.22.refs_2_), channel_id=1, source_target_pairs={{1,3},{3,5},{5,7},{7,6},{6,4},{4,2},{2,0},{0,1},{9,11},{11,13},{13... | collective-permute-start | bytes 1474568 | tf_op jit(solution)/shard_map/ppermute | solution.py:532
  50.8 7.3 %collective-permute-done.2.refs_3_ = bf16[96,2432]{1,0:T(8,128)(2,1)S(1)} collective-permute-done((bf16[96,2432]{1,0:T(8,128)(2,1)S(1)}, bf16[96,2432]{1,0:T(8,128)(2,1)S(1)}, u32[]{:S(2)}, u32[]{:S(2)}) %collective-permute-start.2) | collective-permute-done | bytes 466976 | tf_op jit(solution)/shard_map/ppermute | solution.py:532
  58.1 2.0 %collective-permute-start.3 = (bf16[96,2432]{1,0:T(8,128)(2,1)S(1)}, bf16[96,2432]{1,0:T(8,128)(2,1)S(1)}, u32[]{:S(2)}, u32[]{:S(2)}) collective-permute-start(bf16[96,2432]{1,0:T(8,128)(2,1)S(1)} %get-tuple-element.83.refs_0_), channel_id=1, source_target_pairs={{1,3},{3,5},{5,7},{7,6},{6,4},{4,2},{2,0},{0,1},{9,11},{11,13},{13... | collective-permute-start | bytes 1400840 | tf_op jit(solution)/shard_map/ppermute | solution.py:532
  60.8 1.4 collective-permute-start.11
  62.2 6.4 %collective-permute-done.23.refs_3_ = bf16[96,2560]{1,0:T(8,128)(2,1)S(1)} collective-permute-done((bf16[96,2560]{1,0:T(8,128)(2,1)S(1)}, bf16[96,2560]{1,0:T(8,128)(2,1)S(1)}, u32[]{:S(2)}, u32[]{:S(2)}) %collective-permute-start.23) | collective-permute-done | bytes 491552 | tf_op jit(solution)/shard_map/ppermute | solution.py:532
  68.6 2.0 %collective-permute-start.24 = (bf16[96,2560]{1,0:T(8,128)(2,1)S(1)}, bf16[96,2560]{1,0:T(8,128)(2,1)S(1)}, u32[]{:S(2)}, u32[]{:S(2)}) collective-permute-start(bf16[96,2560]{1,0:T(8,128)(2,1)S(1)} %collective-permute-done.23.refs_3_), channel_id=1, source_target_pairs={{1,3},{3,5},{5,7},{7,6},{6,4},{4,2},{2,0},{0,1},{9,11},{11,13},{13... | collective-permute-start | bytes 1474568 | tf_op jit(solution)/shard_map/ppermute | solution.py:532
  70.7 7.9 %collective-permute-done.3.refs_1_ = bf16[96,2432]{1,0:T(8,128)(2,1)S(1)} collective-permute-done((bf16[96,2432]{1,0:T(8,128)(2,1)S(1)}, bf16[96,2432]{1,0:T(8,128)(2,1)S(1)}, u32[]{:S(2)}, u32[]{:S(2)}) %collective-permute-start.3) | collective-permute-done | bytes 466976 | tf_op jit(solution)/shard_map/ppermute | solution.py:532
  78.6 2.0 %collective-permute-start.4 = (bf16[96,2432]{1,0:T(8,128)(2,1)S(1)}, bf16[96,2432]{1,0:T(8,128)(2,1)S(1)}, u32[]{:S(2)}, u32[]{:S(2)}) collective-permute-start(bf16[96,2432]{1,0:T(8,128)(2,1)S(1)} %collective-permute-done.3.refs_1_), channel_id=1, source_target_pairs={{1,3},{3,5},{5,7},{7,6},{6,4},{4,2},{2,0},{0,1},{9,11},{11,13},{13... | collective-permute-start | bytes 1400840 | tf_op jit(solution)/shard_map/ppermute | solution.py:532
  80.6 3.6 %collective-permute-done.11.refs_5_ = bf16[96,2432]{1,0:T(8,128)(2,1)S(1)} collective-permute-done((bf16[96,2432]{1,0:T(8,128)(2,1)S(1)}, bf16[96,2432]{1,0:T(8,128)(2,1)S(1)}, u32[]{:S(2)}, u32[]{:S(2)}) %collective-permute-start.11) | collective-permute-done | bytes 466976 | tf_op jit(solution)/shard_map/ppermute | solution.py:532
  84.3 2.0 %collective-permute-start.12 = (bf16[96,2432]{1,0:T(8,128)(2,1)S(1)}, bf16[96,2432]{1,0:T(8,128)(2,1)S(1)}, u32[]{:S(2)}, u32[]{:S(2)}) collective-permute-start(bf16[96,2432]{1,0:T(8,128)(2,1)S(1)} %get-tuple-element.79.refs_0_), channel_id=1, source_target_pairs={{1,0},{3,1},{5,3},{7,5},{6,7},{4,6},{2,4},{0,2},{9,8},{11,9},{13,1... | collective-permute-start | bytes 1400840 | tf_op jit(solution)/shard_map/ppermute | solution.py:532
  86.4 7.9 %collective-permute-done.20.refs_7_ = bf16[96,2432]{1,0:T(8,128)(2,1)S(1)} collective-permute-done((bf16[96,2432]{1,0:T(8,128)(2,1)S(1)}, bf16[96,2432]{1,0:T(8,128)(2,1)S(1)}, u32[]{:S(2)}, u32[]{:S(2)}) %collective-permute-start.20) | collective-permute-done | bytes 466976 | tf_op jit(solution)/shard_map/ppermute | solution.py:532
  94.4 1.4 collective-permute-start.28
  96.5 1.8 collective-permute-done.4.refs_2_
  99.0 5.3 %collective-permute-done.18.refs_6_ = bf16[96,2432]{1,0:T(8,128)(2,1)S(1)} collective-permute-done((bf16[96,2432]{1,0:T(8,128)(2,1)S(1)}, bf16[96,2432]{1,0:T(8,128)(2,1)S(1)}, u32[]{:S(2)}, u32[]{:S(2)}) %collective-permute-start.18) | collective-permute-done | bytes 466976 | tf_op jit(solution)/shard_map/ppermute | solution.py:532
  104.3 1.6 collective-permute-start.16
  105.9 1.6 collective-permute-start.5
  107.9 6.4 %collective-permute-done.12.refs_4_ = bf16[96,2432]{1,0:T(8,128)(2,1)S(1)} collective-permute-done((bf16[96,2432]{1,0:T(8,128)(2,1)S(1)}, bf16[96,2432]{1,0:T(8,128)(2,1)S(1)}, u32[]{:S(2)}, u32[]{:S(2)}) %collective-permute-start.12) | collective-permute-done | bytes 466976 | tf_op jit(solution)/shard_map/ppermute | solution.py:532
  114.4 6.0 %compose.3 = (bf16[8,768,768]{2,1,0:T(8,128)(2,1)S(1)}, bf16[8,96,768]{2,1,0:T(8,128)(2,1)S(1)}, bf16[2,768,768]{2,1,0:T(8,128)(2,1)S(1)}, bf16[768,768]{1,0:T(8,128)(2,1)S(1)}) custom-call(s32[1]{0:T(128)S(6)} %convert_element_type.3.last_ref, s32[1]{0:T(128)} %bitcast.place_ref, bf16[96,2560]{1,0:T(8,128)(2,1)S(1)} %copy-done.2, ...), custom_call_target="tpu_custom_call" | custom-call | flops 5435817984 | bytes 9437184 | tf_op jit(solution)/shard_map/compose/pallas_call | solution.py:259
  120.4 3.9 %collective-permute-done.19.refs_7_ = bf16[96,2432]{1,0:T(8,128)(2,1)S(1)} collective-permute-done((bf16[96,2432]{1,0:T(8,128)(2,1)S(1)}, bf16[96,2432]{1,0:T(8,128)(2,1)S(1)}, u32[]{:S(2)}, u32[]{:S(2)}) %collective-permute-start.19) | collective-permute-done | bytes 466976 | tf_op jit(solution)/shard_map/ppermute | solution.py:532
  124.3 1.6 collective-permute-start.17
  125.9 1.6 collective-permute-start.6
  127.5 4.1 %collective-permute-done.13.refs_5_ = bf16[96,2432]{1,0:T(8,128)(2,1)S(1)} collective-permute-done((bf16[96,2432]{1,0:T(8,128)(2,1)S(1)}, bf16[96,2432]{1,0:T(8,128)(2,1)S(1)}, u32[]{:S(2)}, u32[]{:S(2)}) %collective-permute-start.13) | collective-permute-done | bytes 466976 | tf_op jit(solution)/shard_map/ppermute | solution.py:532
  131.8 7.6 %compose.4 = (bf16[8,768,768]{2,1,0:T(8,128)(2,1)S(1)}, bf16[8,96,768]{2,1,0:T(8,128)(2,1)S(1)}, bf16[2,768,768]{2,1,0:T(8,128)(2,1)S(1)}, bf16[768,768]{1,0:T(8,128)(2,1)S(1)}) custom-call(s32[1]{0:T(128)S(6)} %convert_element_type.3.last_ref, s32[1]{0:T(128)} %bitcast.place_ref, ...), custom_call_target="tpu_custom_call", output_to_operand_aliasing={{0}: (11, {}), {1}: (12, {})} | custom-call | flops 5435817984 | bytes 9437184 | tf_op jit(solution)/shard_map/compose/pallas_call | solution.py:259
  139.4 2.7 %collective-permute-done.6.refs_2_ = bf16[96,2432]{1,0:T(8,128)(2,1)S(1)} collective-permute-done((bf16[96,2432]{1,0:T(8,128)(2,1)S(1)}, bf16[96,2432]{1,0:T(8,128)(2,1)S(1)}, u32[]{:S(2)}, u32[]{:S(2)}) %collective-permute-start.6) | collective-permute-done | bytes 466976 | tf_op jit(solution)/shard_map/ppermute | solution.py:532
  142.1 1.2 collective-permute-start.7
  144.1 6.6 %compose.5 = (bf16[8,768,768]{2,1,0:T(8,128)(2,1)S(1)}, bf16[8,96,768]{2,1,0:T(8,128)(2,1)S(1)}, bf16[2,768,768]{2,1,0:T(8,128)(2,1)S(1)}, bf16[768,768]{1,0:T(8,128)(2,1)S(1)}) custom-call(s32[1]{0:T(128)S(6)} %convert_element_type.3.last_ref, s32[1]{0:T(128)} %bitcast.place_ref, ...), custom_call_target="tpu_custom_call", output_to_operand_aliasing={{0}: (11, {}), {1}: (12, {})} | custom-call | flops 5435817984 | bytes 9437184 | tf_op jit(solution)/shard_map/compose/pallas_call | solution.py:259
  151.8 4.6 %chain.1 = (bf16[2,768,768]{2,1,0:T(8,128)(2,1)S(1)}, bf16[2,768,768]{2,1,0:T(8,128)(2,1)S(1)}, bf16[21,128,128]{2,1,0:T(8,128)(2,1)S(1)}) custom-call(s32[1]{0:T(128)} %bitcast.place_ref, bf16[96,2432]{1,0:T(8,128)(2,1)S(1)} %get-tuple-element.79.refs_0_, bf16[96,2432]{1,0:T(8,128)(2,1)S(1)} %collective-permute-done.5.refs_1_, ...), custom_call_target="tpu_custom_call" | custom-call | flops 3623878656 | bytes 9437184 | tf_op jit(solution)/shard_map/chain/pallas_call | solution.py:303
  157.2 2.3 %extend_factors.1 = (bf16[8,768,768]{2,1,0:T(8,128)(2,1)S(1)}, bf16[8,96,768]{2,1,0:T(8,128)(2,1)S(1)}) custom-call(s32[1]{0:T(128)} %bitcast.place_ref, bf16[2,768,768]{2,1,0:T(8,128)(2,1)S(1)} %get-tuple-element.124.gain_ref, bf16[8,768,768]{2,1,0:T(8,128)(2,1)S(1)} %get-tuple-element.125.factor_in, ...), custom_call_target="tpu_custom_call", output_to_operand_aliasing={{0}: (2, {}), {1}: (3, {})} | custom-call | flops 1811939328 | bytes 4718592 | tf_op jit(solution)/shard_map/extend_factors/pallas_call | solution.py:343
  159.5 2.2 %hop.2 = bf16[21,128,128]{2,1,0:T(8,128)(2,1)S(1)} custom-call(bf16[8,768,768]{2,1,0:T(8,128)(2,1)S(1)} %get-tuple-element.127.factor_ref, bf16[2,768,768]{2,1,0:T(8,128)(2,1)S(1)} %get-tuple-element.133.half_ref.refs_0_, bf16[21,128,128]{2,1,0:T(8,128)(2,1)S(1)} %collective-permute-done.31.refs_0_), custom_call_target="tpu_custom_call" | custom-call | flops 1811939328 | bytes 5898240 | tf_op jit(solution)/shard_map/hop/pallas_call | solution.py:452
  161.7 0.9 collective-permute-start.32
  162.6 4.4 %own_rows.1.own_ref = f32[8,96,768]{2,1,0:T(8,128)S(1)} custom-call(s32[1]{0:T(128)} %bitcast.place_ref, bf16[2,768,768]{2,1,0:T(8,128)(2,1)S(1)} %get-tuple-element.133.half_ref.refs_0_, bf16[2,768,768]{2,1,0:T(8,128)(2,1)S(1)} %get-tuple-element.134.refs_1_, bf16[2,768,768]{2,1,0:T(8,128)(2,1)S(1)} %get-tuple-element.135.refs_2_, ...), custom_call_target="tpu_custom_call" | custom-call | flops 905969664 | bytes 9437184 | tf_op jit(solution)/shard_map/own_rows/pallas_call | solution.py:382
  167.0 2.2 %hop.3 = bf16[21,128,128]{2,1,0:T(8,128)(2,1)S(1)} custom-call(bf16[8,768,768]{2,1,0:T(8,128)(2,1)S(1)} %get-tuple-element.127.factor_ref, bf16[2,768,768]{2,1,0:T(8,128)(2,1)S(1)} %get-tuple-element.133.half_ref.refs_0_, bf16[21,128,128]{2,1,0:T(8,128)(2,1)S(1)} %collective-permute-done.31.refs_0_, bf16[21,128,128]{2,1,0:T(8,128)(2,1)S(1)} %collective-permute-done.32.refs_1_), custom_call_target="tpu_custom_call" | custom-call | flops 1811939328 | bytes 5898240 | tf_op jit(solution)/shard_map/hop/pallas_call | solution.py:452
  169.3 1.3 collective-permute-start.33
  170.6 10.0 %collective-permute-done.33.refs_2_ = bf16[21,128,128]{2,1,0:T(8,128)(2,1)S(1)} collective-permute-done((bf16[21,128,128]{2,1,0:T(8,128)(2,1)S(1)}, bf16[21,128,128]{2,1,0:T(8,128)(2,1)S(1)}, u32[]{:S(2)}, u32[]{:S(2)}) %collective-permute-start.33) | collective-permute-done | bytes 688160 | tf_op jit(solution)/shard_map/ppermute | solution.py:591
  180.6 5.1 %finish.1 = f32[8,96,768]{2,1,0:T(8,128)} custom-call(bf16[8,768,768]{2,1,0:T(8,128)(2,1)S(1)} %get-tuple-element.127.factor_ref, f32[8,96,768]{2,1,0:T(8,128)S(1)} %own_rows.1.own_ref, bf16[8,96,768]{2,1,0:T(8,128)(2,1)S(1)} %get-tuple-element.138.mine_ref, bf16[21,128,128]{2,1,0:T(8,128)(2,1)S(1)} %collective-permute-done.31.refs_0_, ...), custom_call_target="tpu_custom_call" | custom-call | tf_op jit(solution)/shard_map/finish/pallas_call | solution.py:492
  (41 shorter events, 7.3 us)
Async XLA Ops:
  2.3 47.8 %copy-start = (f32[8,96,768]{2,1,0:T(8,128)S(1)}, f32[8,96,768]{2,1,0:T(8,128)}, u32[]{:S(2)}) copy-start(f32[8,96,768]{2,1,0:T(8,128)} %increment_ref.5) | copy-start | bytes 7077892
  2.3 47.8 %copy-start.1 = (bf16[8,96,768]{2,1,0:T(8,128)(2,1)S(1)}, bf16[8,96,768]{2,1,0:T(8,128)(2,1)}, u32[]{:S(2)}) copy-start(bf16[8,96,768]{2,1,0:T(8,128)(2,1)} %gain_ref.5) | copy-start | bytes 3538948
  2.3 14.8 %collective-permute-start = (bf16[96,2432]{1,0:T(8,128)(2,1)}, bf16[96,2432]{1,0:T(8,128)(2,1)S(1)}, u32[]{:S(2)}, u32[]{:S(2)}) collective-permute-start(bf16[96,2432]{1,0:T(8,128)(2,1)} %pack.4.refs_0_), channel_id=1, source_target_pairs={{1,3},{3,5},{5,7},{7,6},{6,4},{4,2},{2,0},{0,1},{9,11},{11,13},{13... | collective-permute-start | bytes 1400840 | tf_op jit(solution)/shard_map/ppermute | solution.py:532
  5.2 13.9 %collective-permute-start.8 = (bf16[96,2432]{1,0:T(8,128)(2,1)}, bf16[96,2432]{1,0:T(8,128)(2,1)}, u32[]{:S(2)}, u32[]{:S(2)}) collective-permute-start(bf16[96,2432]{1,0:T(8,128)(2,1)} %pack.4.refs_0_), channel_id=1, source_target_pairs={{1,0},{3,1},{5,3},{7,5},{6,7},{4,6},{2,4},{0,2},{9,8},{11,9},{13,1... | collective-permute-start | bytes 1400840 | tf_op jit(solution)/shard_map/ppermute | solution.py:532
  7.9 86.3 %copy-start.2 = (bf16[96,2560]{1,0:T(8,128)(2,1)S(1)}, bf16[96,2560]{1,0:T(8,128)(2,1)}, u32[]{:S(2)}) copy-start(bf16[96,2560]{1,0:T(8,128)(2,1)} %pack.5.refs_0_) | copy-start | bytes 1474564
  7.9 19.6 %collective-permute-start.21 = (bf16[96,2560]{1,0:T(8,128)(2,1)}, bf16[96,2560]{1,0:T(8,128)(2,1)S(1)}, u32[]{:S(2)}, u32[]{:S(2)}) collective-permute-start(bf16[96,2560]{1,0:T(8,128)(2,1)} %pack.5.refs_0_), channel_id=1, source_target_pairs={{1,3},{3,5},{5,7},{7,6},{6,4},{4,2},{2,0},{0,1},{9,11},{11,13},{13... | collective-permute-start | bytes 1474568 | tf_op jit(solution)/shard_map/ppermute | solution.py:532
  17.0 20.5 %collective-permute-start.1 = (bf16[96,2432]{1,0:T(8,128)(2,1)S(1)}, bf16[96,2432]{1,0:T(8,128)(2,1)S(1)}, u32[]{:S(2)}, u32[]{:S(2)}) collective-permute-start(bf16[96,2432]{1,0:T(8,128)(2,1)S(1)} %collective-permute-done.refs_1_), channel_id=1, source_target_pairs={{1,3},{3,5},{5,7},{7,6},{6,4},{4,2},{2,0},{0,1},{9,11},{11,13},{13... | collective-permute-start | bytes 1400840 | tf_op jit(solution)/shard_map/ppermute | solution.py:532
  19.0 20.5 %collective-permute-start.25 = (bf16[96,2560]{1,0:T(8,128)(2,1)}, bf16[96,2560]{1,0:T(8,128)(2,1)S(1)}, u32[]{:S(2)}, u32[]{:S(2)}) collective-permute-start(bf16[96,2560]{1,0:T(8,128)(2,1)} %pack.5.refs_0_), channel_id=1, source_target_pairs={{1,0},{3,1},{5,3},{7,5},{6,7},{4,6},{2,4},{0,2},{9,8},{11,9},{13,1... | collective-permute-start | bytes 1474568 | tf_op jit(solution)/shard_map/ppermute | solution.py:532
  19.1 21.2 %collective-permute-start.9 = (bf16[96,2432]{1,0:T(8,128)(2,1)}, bf16[96,2432]{1,0:T(8,128)(2,1)S(1)}, u32[]{:S(2)}, u32[]{:S(2)}) collective-permute-start(bf16[96,2432]{1,0:T(8,128)(2,1)} %collective-permute-done.8.refs_4_), channel_id=1, source_target_pairs={{1,0},{3,1},{5,3},{7,5},{6,7},{4,6},{2,4},{0,2},{9,8},{11,9},{13,1... | collective-permute-start | bytes 1400840 | tf_op jit(solution)/shard_map/ppermute | solution.py:532
  27.6 20.5 %collective-permute-start.22 = (bf16[96,2560]{1,0:T(8,128)(2,1)S(1)}, bf16[96,2560]{1,0:T(8,128)(2,1)S(1)}, u32[]{:S(2)}, u32[]{:S(2)}) collective-permute-start(bf16[96,2560]{1,0:T(8,128)(2,1)S(1)} %collective-permute-done.21.refs_1_), channel_id=1, source_target_pairs={{1,3},{3,5},{5,7},{7,6},{6,4},{4,2},{2,0},{0,1},{9,11},{11,13},{13... | collective-permute-start | bytes 1474568 | tf_op jit(solution)/shard_map/ppermute | solution.py:532
  37.6 20.5 %collective-permute-start.2 = (bf16[96,2432]{1,0:T(8,128)(2,1)S(1)}, bf16[96,2432]{1,0:T(8,128)(2,1)S(1)}, u32[]{:S(2)}, u32[]{:S(2)}) collective-permute-start(bf16[96,2432]{1,0:T(8,128)(2,1)S(1)} %collective-permute-done.1.refs_2_), channel_id=1, source_target_pairs={{1,3},{3,5},{5,7},{7,6},{6,4},{4,2},{2,0},{0,1},{9,11},{11,13},{13... | collective-permute-start | bytes 1400840 | tf_op jit(solution)/shard_map/ppermute | solution.py:532
  39.6 20.5 %collective-permute-start.26 = (bf16[96,2560]{1,0:T(8,128)(2,1)S(1)}, bf16[96,2560]{1,0:T(8,128)(2,1)S(1)}, u32[]{:S(2)}, u32[]{:S(2)}) collective-permute-start(bf16[96,2560]{1,0:T(8,128)(2,1)S(1)} %collective-permute-done.25.refs_5_), channel_id=1, source_target_pairs={{1,0},{3,1},{5,3},{7,5},{6,7},{4,6},{2,4},{0,2},{9,8},{11,9},{13,1... | collective-permute-start | bytes 1474568 | tf_op jit(solution)/shard_map/ppermute | solution.py:532
  40.3 20.5 %collective-permute-start.10 = (bf16[96,2432]{1,0:T(8,128)(2,1)S(1)}, bf16[96,2432]{1,0:T(8,128)(2,1)S(1)}, u32[]{:S(2)}, u32[]{:S(2)}) collective-permute-start(bf16[96,2432]{1,0:T(8,128)(2,1)S(1)} %collective-permute-done.9.refs_5_), channel_id=1, source_target_pairs={{1,0},{3,1},{5,3},{7,5},{6,7},{4,6},{2,4},{0,2},{9,8},{11,9},{13,1... | collective-permute-start | bytes 1400840 | tf_op jit(solution)/shard_map/ppermute | solution.py:532
  48.1 20.5 %collective-permute-start.23 = (bf16[96,2560]{1,0:T(8,128)(2,1)S(1)}, bf16[96,2560]{1,0:T(8,128)(2,1)S(1)}, u32[]{:S(2)}, u32[]{:S(2)}) collective-permute-start(bf16[96,2560]{1,0:T(8,128)(2,1)S(1)} %collective-permute-done.22.refs_2_), channel_id=1, source_target_pairs={{1,3},{3,5},{5,7},{7,6},{6,4},{4,2},{2,0},{0,1},{9,11},{11,13},{13... | collective-permute-start | bytes 1474568 | tf_op jit(solution)/shard_map/ppermute | solution.py:532
  58.1 20.5 %collective-permute-start.3 = (bf16[96,2432]{1,0:T(8,128)(2,1)S(1)}, bf16[96,2432]{1,0:T(8,128)(2,1)S(1)}, u32[]{:S(2)}, u32[]{:S(2)}) collective-permute-start(bf16[96,2432]{1,0:T(8,128)(2,1)S(1)} %get-tuple-element.83.refs_0_), channel_id=1, source_target_pairs={{1,3},{3,5},{5,7},{7,6},{6,4},{4,2},{2,0},{0,1},{9,11},{11,13},{13... | collective-permute-start | bytes 1400840 | tf_op jit(solution)/shard_map/ppermute | solution.py:532
  60.1 24.2 %collective-permute-start.27 = (bf16[96,2560]{1,0:T(8,128)(2,1)S(1)}, bf16[96,2560]{1,0:T(8,128)(2,1)S(1)}, u32[]{:S(2)}, u32[]{:S(2)}) collective-permute-start(bf16[96,2560]{1,0:T(8,128)(2,1)S(1)} %collective-permute-done.26.refs_6_), channel_id=1, source_target_pairs={{1,0},{3,1},{5,3},{7,5},{6,7},{4,6},{2,4},{0,2},{9,8},{11,9},{13,1... | collective-permute-start | bytes 1474568 | tf_op jit(solution)/shard_map/ppermute | solution.py:532
  60.8 23.5 %collective-permute-start.11 = (bf16[96,2432]{1,0:T(8,128)(2,1)S(1)}, bf16[96,2432]{1,0:T(8,128)(2,1)S(1)}, u32[]{:S(2)}, u32[]{:S(2)}) collective-permute-start(bf16[96,2432]{1,0:T(8,128)(2,1)S(1)} %get-tuple-element.83.refs_0_), channel_id=1, source_target_pairs={{1,0},{3,1},{5,3},{7,5},{6,7},{4,6},{2,4},{0,2},{9,8},{11,9},{13,1... | collective-permute-start | bytes 1400840 | tf_op jit(solution)/shard_map/ppermute | solution.py:532
  68.6 25.6 %collective-permute-start.24 = (bf16[96,2560]{1,0:T(8,128)(2,1)S(1)}, bf16[96,2560]{1,0:T(8,128)(2,1)S(1)}, u32[]{:S(2)}, u32[]{:S(2)}) collective-permute-start(bf16[96,2560]{1,0:T(8,128)(2,1)S(1)} %collective-permute-done.23.refs_3_), channel_id=1, source_target_pairs={{1,3},{3,5},{5,7},{7,6},{6,4},{4,2},{2,0},{0,1},{9,11},{11,13},{13... | collective-permute-start | bytes 1474568 | tf_op jit(solution)/shard_map/ppermute | solution.py:532
  70.6 23.6 %collective-permute-start.20 = (bf16[96,2432]{1,0:T(8,128)(2,1)S(1)}, bf16[96,2432]{1,0:T(8,128)(2,1)S(1)}, u32[]{:S(2)}, u32[]{:S(2)}) collective-permute-start(bf16[96,2432]{1,0:T(8,128)(2,1)S(1)} %collective-permute-done.10.refs_6_), channel_id=1, source_target_pairs={{1,0},{3,1},{5,3},{7,5},{6,7},{4,6},{2,4},{0,2},{9,8},{11,9},{13,1... | collective-permute-start | bytes 1400840 | tf_op jit(solution)/shard_map/ppermute | solution.py:532
  78.6 19.7 %collective-permute-start.4 = (bf16[96,2432]{1,0:T(8,128)(2,1)S(1)}, bf16[96,2432]{1,0:T(8,128)(2,1)S(1)}, u32[]{:S(2)}, u32[]{:S(2)}) collective-permute-start(bf16[96,2432]{1,0:T(8,128)(2,1)S(1)} %collective-permute-done.3.refs_1_), channel_id=1, source_target_pairs={{1,3},{3,5},{5,7},{7,6},{6,4},{4,2},{2,0},{0,1},{9,11},{11,13},{13... | collective-permute-start | bytes 1400840 | tf_op jit(solution)/shard_map/ppermute | solution.py:532
  84.3 20.0 %collective-permute-start.18 = (bf16[96,2432]{1,0:T(8,128)(2,1)S(1)}, bf16[96,2432]{1,0:T(8,128)(2,1)S(1)}, u32[]{:S(2)}, u32[]{:S(2)}) collective-permute-start(bf16[96,2432]{1,0:T(8,128)(2,1)S(1)} %collective-permute-done.11.refs_5_), channel_id=1, source_target_pairs={{1,0},{3,1},{5,3},{7,5},{6,7},{4,6},{2,4},{0,2},{9,8},{11,9},{13,1... | collective-permute-start | bytes 1400840 | tf_op jit(solution)/shard_map/ppermute | solution.py:532
  84.3 29.9 %collective-permute-start.12 = (bf16[96,2432]{1,0:T(8,128)(2,1)S(1)}, bf16[96,2432]{1,0:T(8,128)(2,1)S(1)}, u32[]{:S(2)}, u32[]{:S(2)}) collective-permute-start(bf16[96,2432]{1,0:T(8,128)(2,1)S(1)} %get-tuple-element.79.refs_0_), channel_id=1, source_target_pairs={{1,0},{3,1},{5,3},{7,5},{6,7},{4,6},{2,4},{0,2},{9,8},{11,9},{13,1... | collective-permute-start | bytes 1400840 | tf_op jit(solution)/shard_map/ppermute | solution.py:532
  94.4 37.4 %copy-start.3 = (bf16[96,2432]{1,0:T(8,128)(2,1)S(1)}, bf16[96,2432]{1,0:T(8,128)(2,1)}, u32[]{:S(2)}) copy-start(bf16[96,2432]{1,0:T(8,128)(2,1)} %pack.4.refs_0_) | copy-start | bytes 1400836
  94.4 11.4 %collective-permute-start.28 = (bf16[8,96,128]{2,1,0:T(8,128)(2,1)S(1)}, bf16[8,96,128]{2,1,0:T(8,128)(2,1)S(1)}, u32[]{:S(2)}, u32[]{:S(2)}) collective-permute-start(bf16[8,96,128]{2,1,0:T(8,128)(2,1)S(1)} %collect.1.refs_11_), channel_id=1, source_target_pairs={{0,24},{1,25},{2,26},{3,27},{4,28},{5,29},{6,30},{7,31}} | collective-permute-start | bytes 589832 | tf_op jit(solution)/shard_map/ppermute | solution.py:569
  95.9 11.6 %collective-permute-start.29 = (bf16[8,96,128]{2,1,0:T(8,128)(2,1)S(1)}, bf16[8,96,128]{2,1,0:T(8,128)(2,1)S(1)}, u32[]{:S(2)}, u32[]{:S(2)}) collective-permute-start(bf16[8,96,128]{2,1,0:T(8,128)(2,1)S(1)} %collect.1.refs_11_), channel_id=1, source_target_pairs={{8,24},{9,25},{10,26},{11,27},{12,28},{13,29},{14,30},{15,31}} | collective-permute-start | bytes 589832 | tf_op jit(solution)/shard_map/ppermute | solution.py:569
  98.4 16.0 %collective-permute-start.30 = (bf16[8,96,128]{2,1,0:T(8,128)(2,1)S(1)}, bf16[8,96,128]{2,1,0:T(8,128)(2,1)S(1)}, u32[]{:S(2)}, u32[]{:S(2)}) collective-permute-start(bf16[8,96,128]{2,1,0:T(8,128)(2,1)S(1)} %collect.1.refs_11_), channel_id=1, source_target_pairs={{16,24},{17,25},{18,26},{19,27},{20,28},{21,29},{22,30},{23,31}} | collective-permute-start | bytes 589832 | tf_op jit(solution)/shard_map/ppermute | solution.py:569
  104.3 16.1 %collective-permute-start.16 = (bf16[96,2432]{1,0:T(8,128)(2,1)S(1)}, bf16[96,2432]{1,0:T(8,128)(2,1)S(1)}, u32[]{:S(2)}, u32[]{:S(2)}) collective-permute-start(bf16[96,2432]{1,0:T(8,128)(2,1)S(1)} %collective-permute-done.4.refs_2_), channel_id=1, source_target_pairs={{1,3},{3,5},{5,7},{7,6},{6,4},{4,2},{2,0},{0,1},{9,11},{11,13},{13... | collective-permute-start | bytes 1400840 | tf_op jit(solution)/shard_map/ppermute | solution.py:532
  105.9 20.0 %collective-permute-start.5 = (bf16[96,2432]{1,0:T(8,128)(2,1)S(1)}, bf16[96,2432]{1,0:T(8,128)(2,1)S(1)}, u32[]{:S(2)}, u32[]{:S(2)}) collective-permute-start(bf16[96,2432]{1,0:T(8,128)(2,1)S(1)} %get-tuple-element.79.refs_0_), channel_id=1, source_target_pairs={{1,3},{3,5},{5,7},{7,6},{6,4},{4,2},{2,0},{0,1},{9,11},{11,13},{13... | collective-permute-start | bytes 1400840 | tf_op jit(solution)/shard_map/ppermute | solution.py:532
  107.4 16.9 %collective-permute-start.19 = (bf16[96,2432]{1,0:T(8,128)(2,1)S(1)}, bf16[96,2432]{1,0:T(8,128)(2,1)S(1)}, u32[]{:S(2)}, u32[]{:S(2)}) collective-permute-start(bf16[96,2432]{1,0:T(8,128)(2,1)S(1)} %collective-permute-done.18.refs_6_), channel_id=1, source_target_pairs={{1,0},{3,1},{5,3},{7,5},{6,7},{4,6},{2,4},{0,2},{9,8},{11,9},{13,1... | collective-permute-start | bytes 1400840 | tf_op jit(solution)/shard_map/ppermute | solution.py:532
  114.3 17.2 %collective-permute-start.13 = (bf16[96,2432]{1,0:T(8,128)(2,1)S(1)}, bf16[96,2432]{1,0:T(8,128)(2,1)S(1)}, u32[]{:S(2)}, u32[]{:S(2)}) collective-permute-start(bf16[96,2432]{1,0:T(8,128)(2,1)S(1)} %collective-permute-done.12.refs_4_), channel_id=1, source_target_pairs={{1,0},{3,1},{5,3},{7,5},{6,7},{4,6},{2,4},{0,2},{9,8},{11,9},{13,1... | collective-permute-start | bytes 1400840 | tf_op jit(solution)/shard_map/ppermute | solution.py:532
  124.3 15.1 %collective-permute-start.17 = (bf16[96,2432]{1,0:T(8,128)(2,1)S(1)}, bf16[96,2432]{1,0:T(8,128)(2,1)S(1)}, u32[]{:S(2)}, u32[]{:S(2)}) collective-permute-start(bf16[96,2432]{1,0:T(8,128)(2,1)S(1)} %collective-permute-done.16.refs_3_), channel_id=1, source_target_pairs={{1,3},{3,5},{5,7},{7,6},{6,4},{4,2},{2,0},{0,1},{9,11},{11,13},{13... | collective-permute-start | bytes 1400840 | tf_op jit(solution)/shard_map/ppermute | solution.py:532
  125.9 16.2 %collective-permute-start.6 = (bf16[96,2432]{1,0:T(8,128)(2,1)S(1)}, bf16[96,2432]{1,0:T(8,128)(2,1)S(1)}, u32[]{:S(2)}, u32[]{:S(2)}) collective-permute-start(bf16[96,2432]{1,0:T(8,128)(2,1)S(1)} %collective-permute-done.5.refs_1_), channel_id=1, source_target_pairs={{1,3},{3,5},{5,7},{7,6},{6,4},{4,2},{2,0},{0,1},{9,11},{11,13},{13... | collective-permute-start | bytes 1400840 | tf_op jit(solution)/shard_map/ppermute | solution.py:532
  131.5 10.6 %collective-permute-start.14 = (bf16[96,2432]{1,0:T(8,128)(2,1)S(1)}, bf16[96,2432]{1,0:T(8,128)(2,1)S(1)}, u32[]{:S(2)}, u32[]{:S(2)}) collective-permute-start(bf16[96,2432]{1,0:T(8,128)(2,1)S(1)} %collective-permute-done.13.refs_5_), channel_id=1, source_target_pairs={{1,0},{3,1},{5,3},{7,5},{6,7},{4,6},{2,4},{0,2},{9,8},{11,9},{13,1... | collective-permute-start | bytes 1400840 | tf_op jit(solution)/shard_map/ppermute | solution.py:532
  142.1 8.9 %collective-permute-start.7 = (bf16[96,2432]{1,0:T(8,128)(2,1)S(1)}, bf16[96,2432]{1,0:T(8,128)(2,1)S(1)}, u32[]{:S(2)}, u32[]{:S(2)}) collective-permute-start(bf16[96,2432]{1,0:T(8,128)(2,1)S(1)} %collective-permute-done.6.refs_2_), channel_id=1, source_target_pairs={{1,3},{3,5},{5,7},{7,6},{6,4},{4,2},{2,0},{0,1},{9,11},{11,13},{13... | collective-permute-start | bytes 1400840 | tf_op jit(solution)/shard_map/ppermute | solution.py:532
  143.3 8.6 %collective-permute-start.15 = (bf16[96,2432]{1,0:T(8,128)(2,1)S(1)}, bf16[96,2432]{1,0:T(8,128)(2,1)S(1)}, u32[]{:S(2)}, u32[]{:S(2)}) collective-permute-start(bf16[96,2432]{1,0:T(8,128)(2,1)S(1)} %collective-permute-done.14.refs_6_), channel_id=1, source_target_pairs={{1,0},{3,1},{5,3},{7,5},{6,7},{4,6},{2,4},{0,2},{9,8},{11,9},{13,1... | collective-permute-start | bytes 1400840 | tf_op jit(solution)/shard_map/ppermute | solution.py:532
  156.5 3.0 %collective-permute-start.31 = (bf16[21,128,128]{2,1,0:T(8,128)(2,1)S(1)}, bf16[21,128,128]{2,1,0:T(8,128)(2,1)S(1)}, u32[]{:S(2)}, u32[]{:S(2)}) collective-permute-start(bf16[21,128,128]{2,1,0:T(8,128)(2,1)S(1)} %get-tuple-element.128), channel_id=1, source_target_pairs={{24,16},{25,17},{26,18},{27,19},{28,20},{29,21},{30,22},{31,23}} | collective-permute-start | bytes 2064392 | tf_op jit(solution)/shard_map/ppermute | solution.py:591
  161.7 5.3 %collective-permute-start.32 = (bf16[21,128,128]{2,1,0:T(8,128)(2,1)S(1)}, bf16[21,128,128]{2,1,0:T(8,128)(2,1)S(1)}, u32[]{:S(2)}, u32[]{:S(2)}) collective-permute-start(bf16[21,128,128]{2,1,0:T(8,128)(2,1)S(1)} %hop.2), channel_id=1, source_target_pairs={{16,8},{17,9},{18,10},{19,11},{20,12},{21,13},{22,14},{23,15}} | collective-permute-start | bytes 2064392 | tf_op jit(solution)/shard_map/ppermute | solution.py:591
  169.3 11.3 %collective-permute-start.33 = (bf16[21,128,128]{2,1,0:T(8,128)(2,1)S(1)}, bf16[21,128,128]{2,1,0:T(8,128)(2,1)S(1)}, u32[]{:S(2)}, u32[]{:S(2)}) collective-permute-start(bf16[21,128,128]{2,1,0:T(8,128)(2,1)S(1)} %hop.3), channel_id=1, source_target_pairs={{8,0},{9,1},{10,2},{11,3},{12,4},{13,5},{14,6},{15,7}} | collective-permute-start | bytes 2064392 | tf_op jit(solution)/shard_map/ppermute | solution.py:591

commit v20 on v19

--- a/solution.py
+++ b/solution.py
@@ -546,7 +546,7 @@
             source = array
             if turn > 1:
                 before = found[turn - 1][way]
-                gate = count // 2 - 1 if turn == 2 else len(before) - 3
+                gate = count // 2 - 1 if turn == 2 else len(before) - 3 - (way == 1)
                 source, before[gate] = lax.optimization_barrier((source, before[gate]))
                 for n in range(gate + 1, len(before)):
                     before[n] = passed(before[n - 1], way)

time: 186 us -> 184 us (0.989)
  starting transfers between devices: 41 us -> 38.5 us
    ppermute x28, starting transfers between devices: 35.3 us -> 32.9 us  [passed(): lax.ppermute(array, 'tile', [(cycle[n], cycle[(n + way) % count]) for n i...]
  transfers between devices with their start and end apart: 34 -> 34, of which waited for: 20 -> 23; matrix products, arithmetic and copies ran while one was open for 0% -> 0% of each run, Pallas kernels for 16% -> 17%
where the time goes in v20:
time: 184 us
  waiting for transfers between devices  98.2 us (53%)
  Pallas kernels  46.7 us (25%)
  starting transfers between devices  38.5 us (21%)
    ppermute x28, waiting for transfers between devices, passed(): lax.ppermute(array, 'tile', [(cycle[n], cycle[(n + way) % count]) for n i...  89.4 us
    ppermute x28, starting transfers between devices, passed(): lax.ppermute(array, 'tile', [(cycle[n], cycle[(n + way) % count]) for n i...  32.9 us
    pallas_call x3, Pallas kernels, compose(): pl.pallas_call(functools.partial(compose_kernel, cycle, right, turns, fir...  20.2 us
    ppermute x3, waiting for transfers between devices, local(): packed.append(lax.ppermute(before, 'tm', [(turn, turn - 1)]))  8.77 us
    pallas_call x3, Pallas kernels, pack(): pl.pallas_call(functools.partial(pack_kernel, count, ranges), grid_spec=p...  5.58 us
    pallas_call x1, Pallas kernels, finish(): pl.pallas_call(functools.partial(finish_kernel, len(packed)), in_specs=[v...  5.07 us
    pallas_call x1, Pallas kernels, chain(): pl.pallas_call(functools.partial(chain_kernel, cycle, right, turns), in_s...  4.63 us
    pallas_call x2, Pallas kernels, hop(): pl.pallas_call(functools.partial(hop_kernel, len(packed)), in_specs=[vmem...  4.39 us
  transfers between devices with their start and end apart: 34, of which 23 were waited for; matrix products, arithmetic and copies ran while one was open for 0% of the time, Pallas kernels for 17%

profile of v20, /device:TPU:0, one launch (start us, length us, event | category | flops | bytes accessed | tf_op | source)
XLA Modules:
  0.0 183.8 jit_solution(11437142814291984230)
XLA Ops:
  0.0 2.3 %pack.4.refs_0_ = bf16[96,2432]{1,0:T(8,128)(2,1)} custom-call(s32[1]{0:T(128)} %bitcast.place_ref, s32[1]{0:T(128)} %bitcast.1.block_ref, bf16[8,96,768]{2,1,0:T(8,128)(2,1)} %gain_ref.5, f32[8,96,768]{2,1,0:T(8,128)} %increment_ref.5), custom_call_target="tpu_custom_call" | custom-call | tf_op jit(solution)/shard_map/pack/pallas_call | solution.py:80
  2.3 3.0 %collective-permute-start.7 = (bf16[96,2432]{1,0:T(8,128)(2,1)}, bf16[96,2432]{1,0:T(8,128)(2,1)S(1)}, u32[]{:S(2)}, u32[]{:S(2)}) collective-permute-start(bf16[96,2432]{1,0:T(8,128)(2,1)} %pack.4.refs_0_), channel_id=1, source_target_pairs={{1,0},{3,1},{5,3},{7,5},{6,7},{4,6},{2,4},{0,2},{9,8},{11,9},{13,1... | collective-permute-start | bytes 1400840 | tf_op jit(solution)/shard_map/ppermute | solution.py:532
  5.3 2.6 %pack.5.refs_0_ = bf16[96,2560]{1,0:T(8,128)(2,1)} custom-call(s32[1]{0:T(128)} %bitcast.place_ref, s32[1]{0:T(128)} %bitcast.1.block_ref, bf16[8,96,768]{2,1,0:T(8,128)(2,1)} %gain_ref.5, f32[8,96,768]{2,1,0:T(8,128)} %increment_ref.5, f32[96,768]{1,0:T(8,128)} %refs_0_.1), custom_call_target="tpu_custom_call" | custom-call | tf_op jit(solution)/shard_map/pack/pallas_call | solution.py:80
  7.9 2.0 %collective-permute-start.21 = (bf16[96,2560]{1,0:T(8,128)(2,1)}, bf16[96,2560]{1,0:T(8,128)(2,1)S(1)}, u32[]{:S(2)}, u32[]{:S(2)}) collective-permute-start(bf16[96,2560]{1,0:T(8,128)(2,1)} %pack.5.refs_0_), channel_id=1, source_target_pairs={{1,3},{3,5},{5,7},{7,6},{6,4},{4,2},{2,0},{0,1},{9,11},{11,13},{13... | collective-permute-start | bytes 1474568 | tf_op jit(solution)/shard_map/ppermute | solution.py:532
  9.9 6.3 %collective-permute-done.7.refs_4_ = bf16[96,2432]{1,0:T(8,128)(2,1)S(1)} collective-permute-done((bf16[96,2432]{1,0:T(8,128)(2,1)}, bf16[96,2432]{1,0:T(8,128)(2,1)S(1)}, u32[]{:S(2)}, u32[]{:S(2)}) %collective-permute-start.7) | collective-permute-done | bytes 466976 | tf_op jit(solution)/shard_map/ppermute | solution.py:532
  16.1 1.8 collective-permute-start.8
  17.9 1.3 collective-permute-done.refs_1_
  19.2 2.0 %collective-permute-start.25 = (bf16[96,2560]{1,0:T(8,128)(2,1)}, bf16[96,2560]{1,0:T(8,128)(2,1)S(1)}, u32[]{:S(2)}, u32[]{:S(2)}) collective-permute-start(bf16[96,2560]{1,0:T(8,128)(2,1)} %pack.5.refs_0_), channel_id=1, source_target_pairs={{1,0},{3,1},{5,3},{7,5},{6,7},{4,6},{2,4},{0,2},{9,8},{11,9},{13,1... | collective-permute-start | bytes 1474568 | tf_op jit(solution)/shard_map/ppermute | solution.py:532
  21.3 8.4 %collective-permute-done.21.refs_1_ = bf16[96,2560]{1,0:T(8,128)(2,1)S(1)} collective-permute-done((bf16[96,2560]{1,0:T(8,128)(2,1)}, bf16[96,2560]{1,0:T(8,128)(2,1)S(1)}, u32[]{:S(2)}, u32[]{:S(2)}) %collective-permute-start.21) | collective-permute-done | bytes 491552 | tf_op jit(solution)/shard_map/ppermute | solution.py:532
  29.8 1.9 %collective-permute-start.9 = (bf16[96,2432]{1,0:T(8,128)(2,1)S(1)}, bf16[96,2432]{1,0:T(8,128)(2,1)S(1)}, u32[]{:S(2)}, u32[]{:S(2)}) collective-permute-start(bf16[96,2432]{1,0:T(8,128)(2,1)S(1)} %collective-permute-done.8.refs_5_), channel_id=1, source_target_pairs={{1,0},{3,1},{5,3},{7,5},{6,7},{4,6},{2,4},{0,2},{9,8},{11,9},{13,1... | collective-permute-start | bytes 1400840 | tf_op jit(solution)/shard_map/ppermute | solution.py:532
  31.7 8.0 %collective-permute-done.1.refs_2_ = bf16[96,2432]{1,0:T(8,128)(2,1)S(1)} collective-permute-done((bf16[96,2432]{1,0:T(8,128)(2,1)}, bf16[96,2432]{1,0:T(8,128)(2,1)S(1)}, u32[]{:S(2)}, u32[]{:S(2)}) %collective-permute-start.1) | collective-permute-done | bytes 466976 | tf_op jit(solution)/shard_map/ppermute | solution.py:532
  40.3 1.8 collective-permute-start.26
  42.1 8.1 %collective-permute-done.22.refs_2_ = bf16[96,2560]{1,0:T(8,128)(2,1)S(1)} collective-permute-done((bf16[96,2560]{1,0:T(8,128)(2,1)S(1)}, bf16[96,2560]{1,0:T(8,128)(2,1)S(1)}, u32[]{:S(2)}, u32[]{:S(2)}) %collective-permute-start.22) | collective-permute-done | bytes 491552 | tf_op jit(solution)/shard_map/ppermute | solution.py:532
  50.2 0.7 pack.3
  50.9 2.1 %collective-permute-start.10 = (bf16[96,2432]{1,0:T(8,128)(2,1)S(1)}, bf16[96,2432]{1,0:T(8,128)(2,1)S(1)}, u32[]{:S(2)}, u32[]{:S(2)}) collective-permute-start(bf16[96,2432]{1,0:T(8,128)(2,1)S(1)} %get-tuple-element.83.refs_0_), channel_id=1, source_target_pairs={{1,0},{3,1},{5,3},{7,5},{6,7},{4,6},{2,4},{0,2},{9,8},{11,9},{13,1... | collective-permute-start | bytes 1400840 | tf_op jit(solution)/shard_map/ppermute | solution.py:532
  53.0 7.2 %collective-permute-done.2.refs_3_ = bf16[96,2432]{1,0:T(8,128)(2,1)S(1)} collective-permute-done((bf16[96,2432]{1,0:T(8,128)(2,1)S(1)}, bf16[96,2432]{1,0:T(8,128)(2,1)S(1)}, u32[]{:S(2)}, u32[]{:S(2)}) %collective-permute-start.2) | collective-permute-done | bytes 466976 | tf_op jit(solution)/shard_map/ppermute | solution.py:532
  60.8 1.8 collective-permute-start.27
  62.6 1.6 collective-permute-start.20
  64.2 6.5 %collective-permute-done.23.refs_3_ = bf16[96,2560]{1,0:T(8,128)(2,1)S(1)} collective-permute-done((bf16[96,2560]{1,0:T(8,128)(2,1)S(1)}, bf16[96,2560]{1,0:T(8,128)(2,1)S(1)}, u32[]{:S(2)}, u32[]{:S(2)}) %collective-permute-start.23) | collective-permute-done | bytes 491552 | tf_op jit(solution)/shard_map/ppermute | solution.py:532
  70.8 1.9 %collective-permute-start.18 = (bf16[96,2432]{1,0:T(8,128)(2,1)S(1)}, bf16[96,2432]{1,0:T(8,128)(2,1)S(1)}, u32[]{:S(2)}, u32[]{:S(2)}) collective-permute-start(bf16[96,2432]{1,0:T(8,128)(2,1)S(1)} %collective-permute-done.10.refs_5_), channel_id=1, source_target_pairs={{1,0},{3,1},{5,3},{7,5},{6,7},{4,6},{2,4},{0,2},{9,8},{11,9},{13,1... | collective-permute-start | bytes 1400840 | tf_op jit(solution)/shard_map/ppermute | solution.py:532
  72.8 8.0 %collective-permute-done.3.refs_1_ = bf16[96,2432]{1,0:T(8,128)(2,1)S(1)} collective-permute-done((bf16[96,2432]{1,0:T(8,128)(2,1)S(1)}, bf16[96,2432]{1,0:T(8,128)(2,1)S(1)}, u32[]{:S(2)}, u32[]{:S(2)}) %collective-permute-start.3) | collective-permute-done | bytes 466976 | tf_op jit(solution)/shard_map/ppermute | solution.py:532
  81.4 1.8 collective-permute-start.11
  83.2 8.2 %collective-permute-done.20.refs_7_ = bf16[96,2432]{1,0:T(8,128)(2,1)S(1)} collective-permute-done((bf16[96,2432]{1,0:T(8,128)(2,1)S(1)}, bf16[96,2432]{1,0:T(8,128)(2,1)S(1)}, u32[]{:S(2)}, u32[]{:S(2)}) %collective-permute-start.20) | collective-permute-done | bytes 466976 | tf_op jit(solution)/shard_map/ppermute | solution.py:532
  91.4 1.7 collective-permute-start.4
  93.3 1.4 collective-permute-start.28
  94.7 6.7 %collective-permute-done.18.refs_6_ = bf16[96,2432]{1,0:T(8,128)(2,1)S(1)} collective-permute-done((bf16[96,2432]{1,0:T(8,128)(2,1)S(1)}, bf16[96,2432]{1,0:T(8,128)(2,1)S(1)}, u32[]{:S(2)}, u32[]{:S(2)}) %collective-permute-start.18) | collective-permute-done | bytes 466976 | tf_op jit(solution)/shard_map/ppermute | solution.py:532
  102.8 1.8 collective-permute-start.16
  104.8 6.6 %collective-permute-done.11.refs_4_ = bf16[96,2432]{1,0:T(8,128)(2,1)S(1)} collective-permute-done((bf16[96,2432]{1,0:T(8,128)(2,1)S(1)}, bf16[96,2432]{1,0:T(8,128)(2,1)S(1)}, u32[]{:S(2)}, u32[]{:S(2)}) %collective-permute-start.11) | collective-permute-done | bytes 466976 | tf_op jit(solution)/shard_map/ppermute | solution.py:532
  111.4 1.8 collective-permute-start.12
  113.4 6.0 %compose.3 = (bf16[8,768,768]{2,1,0:T(8,128)(2,1)S(1)}, bf16[8,96,768]{2,1,0:T(8,128)(2,1)S(1)}, bf16[2,768,768]{2,1,0:T(8,128)(2,1)S(1)}, bf16[768,768]{1,0:T(8,128)(2,1)S(1)}) custom-call(s32[1]{0:T(128)S(6)} %convert_element_type.3.last_ref, s32[1]{0:T(128)} %bitcast.place_ref, bf16[96,2560]{1,0:T(8,128)(2,1)S(1)} %copy-done.2, ...), custom_call_target="tpu_custom_call" | custom-call | flops 5435817984 | bytes 9437184 | tf_op jit(solution)/shard_map/compose/pallas_call | solution.py:259
  119.5 1.8 collective-permute-done.16.refs_3_
  121.4 1.7 collective-permute-start.17
  123.2 6.6 %collective-permute-done.12.refs_5_ = bf16[96,2432]{1,0:T(8,128)(2,1)S(1)} collective-permute-done((bf16[96,2432]{1,0:T(8,128)(2,1)S(1)}, bf16[96,2432]{1,0:T(8,128)(2,1)S(1)}, u32[]{:S(2)}, u32[]{:S(2)}) %collective-permute-start.12) | collective-permute-done | bytes 466976 | tf_op jit(solution)/shard_map/ppermute | solution.py:532
  129.8 1.5 collective-permute-start.13
  131.8 7.6 %compose.4 = (bf16[8,768,768]{2,1,0:T(8,128)(2,1)S(1)}, bf16[8,96,768]{2,1,0:T(8,128)(2,1)S(1)}, bf16[2,768,768]{2,1,0:T(8,128)(2,1)S(1)}, bf16[768,768]{1,0:T(8,128)(2,1)S(1)}) custom-call(s32[1]{0:T(128)S(6)} %convert_element_type.3.last_ref, s32[1]{0:T(128)} %bitcast.place_ref, ...), custom_call_target="tpu_custom_call", output_to_operand_aliasing={{0}: (11, {}), {1}: (12, {})} | custom-call | flops 5435817984 | bytes 9437184 | tf_op jit(solution)/shard_map/compose/pallas_call | solution.py:259
  139.4 1.9 %collective-permute-done.17.refs_4_ = bf16[96,2432]{1,0:T(8,128)(2,1)S(1)} collective-permute-done((bf16[96,2432]{1,0:T(8,128)(2,1)S(1)}, bf16[96,2432]{1,0:T(8,128)(2,1)S(1)}, u32[]{:S(2)}, u32[]{:S(2)}) %collective-permute-start.17) | collective-permute-done | bytes 466976 | tf_op jit(solution)/shard_map/ppermute | solution.py:532
  141.3 1.6 collective-permute-start.14
  142.9 6.6 %compose.5 = (bf16[8,768,768]{2,1,0:T(8,128)(2,1)S(1)}, bf16[8,96,768]{2,1,0:T(8,128)(2,1)S(1)}, bf16[2,768,768]{2,1,0:T(8,128)(2,1)S(1)}, bf16[768,768]{1,0:T(8,128)(2,1)S(1)}) custom-call(s32[1]{0:T(128)S(6)} %convert_element_type.3.last_ref, s32[1]{0:T(128)} %bitcast.place_ref, ...), custom_call_target="tpu_custom_call", output_to_operand_aliasing={{0}: (11, {}), {1}: (12, {})} | custom-call | flops 5435817984 | bytes 9437184 | tf_op jit(solution)/shard_map/compose/pallas_call | solution.py:259
  149.8 1.2 collective-permute-done.14.refs_7_
  151.1 4.6 %chain.1 = (bf16[2,768,768]{2,1,0:T(8,128)(2,1)S(1)}, bf16[2,768,768]{2,1,0:T(8,128)(2,1)S(1)}, bf16[21,128,128]{2,1,0:T(8,128)(2,1)S(1)}) custom-call(s32[1]{0:T(128)} %bitcast.place_ref, bf16[96,2432]{1,0:T(8,128)(2,1)S(1)} %get-tuple-element.79.refs_0_, bf16[96,2432]{1,0:T(8,128)(2,1)S(1)} %collective-permute-done.4.refs_1_, ...), custom_call_target="tpu_custom_call" | custom-call | flops 3623878656 | bytes 9437184 | tf_op jit(solution)/shard_map/chain/pallas_call | solution.py:303
  156.4 2.3 %extend_factors.1 = (bf16[8,768,768]{2,1,0:T(8,128)(2,1)S(1)}, bf16[8,96,768]{2,1,0:T(8,128)(2,1)S(1)}) custom-call(s32[1]{0:T(128)} %bitcast.place_ref, bf16[2,768,768]{2,1,0:T(8,128)(2,1)S(1)} %get-tuple-element.124.gain_ref, bf16[8,768,768]{2,1,0:T(8,128)(2,1)S(1)} %get-tuple-element.125.factor_in, ...), custom_call_target="tpu_custom_call", output_to_operand_aliasing={{0}: (2, {}), {1}: (3, {})} | custom-call | flops 1811939328 | bytes 4718592 | tf_op jit(solution)/shard_map/extend_factors/pallas_call | solution.py:343
  158.8 2.2 %hop.2 = bf16[21,128,128]{2,1,0:T(8,128)(2,1)S(1)} custom-call(bf16[8,768,768]{2,1,0:T(8,128)(2,1)S(1)} %get-tuple-element.127.factor_ref, bf16[2,768,768]{2,1,0:T(8,128)(2,1)S(1)} %get-tuple-element.133.half_ref.refs_0_, bf16[21,128,128]{2,1,0:T(8,128)(2,1)S(1)} %collective-permute-done.31.refs_0_), custom_call_target="tpu_custom_call" | custom-call | flops 1811939328 | bytes 5898240 | tf_op jit(solution)/shard_map/hop/pallas_call | solution.py:452
  160.9 0.9 collective-permute-start.32
  161.9 4.4 %own_rows.1.own_ref = f32[8,96,768]{2,1,0:T(8,128)S(1)} custom-call(s32[1]{0:T(128)} %bitcast.place_ref, bf16[2,768,768]{2,1,0:T(8,128)(2,1)S(1)} %get-tuple-element.133.half_ref.refs_0_, bf16[2,768,768]{2,1,0:T(8,128)(2,1)S(1)} %get-tuple-element.134.refs_1_, bf16[2,768,768]{2,1,0:T(8,128)(2,1)S(1)} %get-tuple-element.135.refs_2_, ...), custom_call_target="tpu_custom_call" | custom-call | flops 905969664 | bytes 9437184 | tf_op jit(solution)/shard_map/own_rows/pallas_call | solution.py:382
  166.3 2.2 %hop.3 = bf16[21,128,128]{2,1,0:T(8,128)(2,1)S(1)} custom-call(bf16[8,768,768]{2,1,0:T(8,128)(2,1)S(1)} %get-tuple-element.127.factor_ref, bf16[2,768,768]{2,1,0:T(8,128)(2,1)S(1)} %get-tuple-element.133.half_ref.refs_0_, bf16[21,128,128]{2,1,0:T(8,128)(2,1)S(1)} %collective-permute-done.31.refs_0_, bf16[21,128,128]{2,1,0:T(8,128)(2,1)S(1)} %collective-permute-done.32.refs_1_), custom_call_target="tpu_custom_call" | custom-call | flops 1811939328 | bytes 5898240 | tf_op jit(solution)/shard_map/hop/pallas_call | solution.py:452
  168.5 1.3 collective-permute-start.33
  169.8 8.8 %collective-permute-done.33.refs_2_ = bf16[21,128,128]{2,1,0:T(8,128)(2,1)S(1)} collective-permute-done((bf16[21,128,128]{2,1,0:T(8,128)(2,1)S(1)}, bf16[21,128,128]{2,1,0:T(8,128)(2,1)S(1)}, u32[]{:S(2)}, u32[]{:S(2)}) %collective-permute-start.33) | collective-permute-done | bytes 688160 | tf_op jit(solution)/shard_map/ppermute | solution.py:591
  178.6 5.1 %finish.1 = f32[8,96,768]{2,1,0:T(8,128)} custom-call(bf16[8,768,768]{2,1,0:T(8,128)(2,1)S(1)} %get-tuple-element.127.factor_ref, f32[8,96,768]{2,1,0:T(8,128)S(1)} %own_rows.1.own_ref, bf16[8,96,768]{2,1,0:T(8,128)(2,1)S(1)} %get-tuple-element.138.mine_ref, bf16[21,128,128]{2,1,0:T(8,128)(2,1)S(1)} %collective-permute-done.31.refs_0_, ...), custom_call_target="tpu_custom_call" | custom-call | tf_op jit(solution)/shard_map/finish/pallas_call | solution.py:492
  (41 shorter events, 5.9 us)
Async XLA Ops:
  2.3 47.9 %copy-start = (f32[8,96,768]{2,1,0:T(8,128)S(1)}, f32[8,96,768]{2,1,0:T(8,128)}, u32[]{:S(2)}) copy-start(f32[8,96,768]{2,1,0:T(8,128)} %increment_ref.5) | copy-start | bytes 7077892
  2.3 47.9 %copy-start.1 = (bf16[8,96,768]{2,1,0:T(8,128)(2,1)S(1)}, bf16[8,96,768]{2,1,0:T(8,128)(2,1)}, u32[]{:S(2)}) copy-start(bf16[8,96,768]{2,1,0:T(8,128)(2,1)} %gain_ref.5) | copy-start | bytes 3538948
  2.3 13.9 %collective-permute-start.7 = (bf16[96,2432]{1,0:T(8,128)(2,1)}, bf16[96,2432]{1,0:T(8,128)(2,1)S(1)}, u32[]{:S(2)}, u32[]{:S(2)}) collective-permute-start(bf16[96,2432]{1,0:T(8,128)(2,1)} %pack.4.refs_0_), channel_id=1, source_target_pairs={{1,0},{3,1},{5,3},{7,5},{6,7},{4,6},{2,4},{0,2},{9,8},{11,9},{13,1... | collective-permute-start | bytes 1400840 | tf_op jit(solution)/shard_map/ppermute | solution.py:532
  5.3 13.9 %collective-permute-start = (bf16[96,2432]{1,0:T(8,128)(2,1)}, bf16[96,2432]{1,0:T(8,128)(2,1)}, u32[]{:S(2)}, u32[]{:S(2)}) collective-permute-start(bf16[96,2432]{1,0:T(8,128)(2,1)} %pack.4.refs_0_), channel_id=1, source_target_pairs={{1,3},{3,5},{5,7},{7,6},{6,4},{4,2},{2,0},{0,1},{9,11},{11,13},{13... | collective-permute-start | bytes 1400840 | tf_op jit(solution)/shard_map/ppermute | solution.py:532
  7.9 85.3 %copy-start.2 = (bf16[96,2560]{1,0:T(8,128)(2,1)S(1)}, bf16[96,2560]{1,0:T(8,128)(2,1)}, u32[]{:S(2)}) copy-start(bf16[96,2560]{1,0:T(8,128)(2,1)} %pack.5.refs_0_) | copy-start | bytes 1474564
  7.9 21.8 %collective-permute-start.21 = (bf16[96,2560]{1,0:T(8,128)(2,1)}, bf16[96,2560]{1,0:T(8,128)(2,1)S(1)}, u32[]{:S(2)}, u32[]{:S(2)}) collective-permute-start(bf16[96,2560]{1,0:T(8,128)(2,1)} %pack.5.refs_0_), channel_id=1, source_target_pairs={{1,3},{3,5},{5,7},{7,6},{6,4},{4,2},{2,0},{0,1},{9,11},{11,13},{13... | collective-permute-start | bytes 1474568 | tf_op jit(solution)/shard_map/ppermute | solution.py:532
  16.1 13.6 %collective-permute-start.8 = (bf16[96,2432]{1,0:T(8,128)(2,1)S(1)}, bf16[96,2432]{1,0:T(8,128)(2,1)S(1)}, u32[]{:S(2)}, u32[]{:S(2)}) collective-permute-start(bf16[96,2432]{1,0:T(8,128)(2,1)S(1)} %collective-permute-done.7.refs_4_), channel_id=1, source_target_pairs={{1,0},{3,1},{5,3},{7,5},{6,7},{4,6},{2,4},{0,2},{9,8},{11,9},{13,1... | collective-permute-start | bytes 1400840 | tf_op jit(solution)/shard_map/ppermute | solution.py:532
  19.2 20.4 %collective-permute-start.1 = (bf16[96,2432]{1,0:T(8,128)(2,1)}, bf16[96,2432]{1,0:T(8,128)(2,1)S(1)}, u32[]{:S(2)}, u32[]{:S(2)}) collective-permute-start(bf16[96,2432]{1,0:T(8,128)(2,1)} %collective-permute-done.refs_1_), channel_id=1, source_target_pairs={{1,3},{3,5},{5,7},{7,6},{6,4},{4,2},{2,0},{0,1},{9,11},{11,13},{13... | collective-permute-start | bytes 1400840 | tf_op jit(solution)/shard_map/ppermute | solution.py:532
  19.2 21.1 %collective-permute-start.25 = (bf16[96,2560]{1,0:T(8,128)(2,1)}, bf16[96,2560]{1,0:T(8,128)(2,1)S(1)}, u32[]{:S(2)}, u32[]{:S(2)}) collective-permute-start(bf16[96,2560]{1,0:T(8,128)(2,1)} %pack.5.refs_0_), channel_id=1, source_target_pairs={{1,0},{3,1},{5,3},{7,5},{6,7},{4,6},{2,4},{0,2},{9,8},{11,9},{13,1... | collective-permute-start | bytes 1474568 | tf_op jit(solution)/shard_map/ppermute | solution.py:532
  29.7 20.5 %collective-permute-start.22 = (bf16[96,2560]{1,0:T(8,128)(2,1)S(1)}, bf16[96,2560]{1,0:T(8,128)(2,1)S(1)}, u32[]{:S(2)}, u32[]{:S(2)}) collective-permute-start(bf16[96,2560]{1,0:T(8,128)(2,1)S(1)} %collective-permute-done.21.refs_1_), channel_id=1, source_target_pairs={{1,3},{3,5},{5,7},{7,6},{6,4},{4,2},{2,0},{0,1},{9,11},{11,13},{13... | collective-permute-start | bytes 1474568 | tf_op jit(solution)/shard_map/ppermute | solution.py:532
  29.8 21.2 %collective-permute-start.9 = (bf16[96,2432]{1,0:T(8,128)(2,1)S(1)}, bf16[96,2432]{1,0:T(8,128)(2,1)S(1)}, u32[]{:S(2)}, u32[]{:S(2)}) collective-permute-start(bf16[96,2432]{1,0:T(8,128)(2,1)S(1)} %collective-permute-done.8.refs_5_), channel_id=1, source_target_pairs={{1,0},{3,1},{5,3},{7,5},{6,7},{4,6},{2,4},{0,2},{9,8},{11,9},{13,1... | collective-permute-start | bytes 1400840 | tf_op jit(solution)/shard_map/ppermute | solution.py:532
  39.7 20.5 %collective-permute-start.2 = (bf16[96,2432]{1,0:T(8,128)(2,1)S(1)}, bf16[96,2432]{1,0:T(8,128)(2,1)S(1)}, u32[]{:S(2)}, u32[]{:S(2)}) collective-permute-start(bf16[96,2432]{1,0:T(8,128)(2,1)S(1)} %collective-permute-done.1.refs_2_), channel_id=1, source_target_pairs={{1,3},{3,5},{5,7},{7,6},{6,4},{4,2},{2,0},{0,1},{9,11},{11,13},{13... | collective-permute-start | bytes 1400840 | tf_op jit(solution)/shard_map/ppermute | solution.py:532
  40.3 20.5 %collective-permute-start.26 = (bf16[96,2560]{1,0:T(8,128)(2,1)S(1)}, bf16[96,2560]{1,0:T(8,128)(2,1)S(1)}, u32[]{:S(2)}, u32[]{:S(2)}) collective-permute-start(bf16[96,2560]{1,0:T(8,128)(2,1)S(1)} %collective-permute-done.25.refs_5_), channel_id=1, source_target_pairs={{1,0},{3,1},{5,3},{7,5},{6,7},{4,6},{2,4},{0,2},{9,8},{11,9},{13,1... | collective-permute-start | bytes 1474568 | tf_op jit(solution)/shard_map/ppermute | solution.py:532
  50.2 20.5 %collective-permute-start.23 = (bf16[96,2560]{1,0:T(8,128)(2,1)S(1)}, bf16[96,2560]{1,0:T(8,128)(2,1)S(1)}, u32[]{:S(2)}, u32[]{:S(2)}) collective-permute-start(bf16[96,2560]{1,0:T(8,128)(2,1)S(1)} %collective-permute-done.22.refs_2_), channel_id=1, source_target_pairs={{1,3},{3,5},{5,7},{7,6},{6,4},{4,2},{2,0},{0,1},{9,11},{11,13},{13... | collective-permute-start | bytes 1474568 | tf_op jit(solution)/shard_map/ppermute | solution.py:532
  50.9 19.9 %collective-permute-start.10 = (bf16[96,2432]{1,0:T(8,128)(2,1)S(1)}, bf16[96,2432]{1,0:T(8,128)(2,1)S(1)}, u32[]{:S(2)}, u32[]{:S(2)}) collective-permute-start(bf16[96,2432]{1,0:T(8,128)(2,1)S(1)} %get-tuple-element.83.refs_0_), channel_id=1, source_target_pairs={{1,0},{3,1},{5,3},{7,5},{6,7},{4,6},{2,4},{0,2},{9,8},{11,9},{13,1... | collective-permute-start | bytes 1400840 | tf_op jit(solution)/shard_map/ppermute | solution.py:532
  60.2 20.5 %collective-permute-start.3 = (bf16[96,2432]{1,0:T(8,128)(2,1)S(1)}, bf16[96,2432]{1,0:T(8,128)(2,1)S(1)}, u32[]{:S(2)}, u32[]{:S(2)}) collective-permute-start(bf16[96,2432]{1,0:T(8,128)(2,1)S(1)} %get-tuple-element.83.refs_0_), channel_id=1, source_target_pairs={{1,3},{3,5},{5,7},{7,6},{6,4},{4,2},{2,0},{0,1},{9,11},{11,13},{13... | collective-permute-start | bytes 1400840 | tf_op jit(solution)/shard_map/ppermute | solution.py:532
  60.8 20.5 %collective-permute-start.27 = (bf16[96,2560]{1,0:T(8,128)(2,1)S(1)}, bf16[96,2560]{1,0:T(8,128)(2,1)S(1)}, u32[]{:S(2)}, u32[]{:S(2)}) collective-permute-start(bf16[96,2560]{1,0:T(8,128)(2,1)S(1)} %collective-permute-done.26.refs_6_), channel_id=1, source_target_pairs={{1,0},{3,1},{5,3},{7,5},{6,7},{4,6},{2,4},{0,2},{9,8},{11,9},{13,1... | collective-permute-start | bytes 1474568 | tf_op jit(solution)/shard_map/ppermute | solution.py:532
  62.6 28.7 %collective-permute-start.20 = (bf16[96,2432]{1,0:T(8,128)(2,1)S(1)}, bf16[96,2432]{1,0:T(8,128)(2,1)S(1)}, u32[]{:S(2)}, u32[]{:S(2)}) collective-permute-start(bf16[96,2432]{1,0:T(8,128)(2,1)S(1)} %collective-permute-done.9.refs_6_), channel_id=1, source_target_pairs={{1,0},{3,1},{5,3},{7,5},{6,7},{4,6},{2,4},{0,2},{9,8},{11,9},{13,1... | collective-permute-start | bytes 1400840 | tf_op jit(solution)/shard_map/ppermute | solution.py:532
  70.7 22.4 %collective-permute-start.24 = (bf16[96,2560]{1,0:T(8,128)(2,1)S(1)}, bf16[96,2560]{1,0:T(8,128)(2,1)S(1)}, u32[]{:S(2)}, u32[]{:S(2)}) collective-permute-start(bf16[96,2560]{1,0:T(8,128)(2,1)S(1)} %collective-permute-done.23.refs_3_), channel_id=1, source_target_pairs={{1,3},{3,5},{5,7},{7,6},{6,4},{4,2},{2,0},{0,1},{9,11},{11,13},{13... | collective-permute-start | bytes 1474568 | tf_op jit(solution)/shard_map/ppermute | solution.py:532
  70.8 30.5 %collective-permute-start.18 = (bf16[96,2432]{1,0:T(8,128)(2,1)S(1)}, bf16[96,2432]{1,0:T(8,128)(2,1)S(1)}, u32[]{:S(2)}, u32[]{:S(2)}) collective-permute-start(bf16[96,2432]{1,0:T(8,128)(2,1)S(1)} %collective-permute-done.10.refs_5_), channel_id=1, source_target_pairs={{1,0},{3,1},{5,3},{7,5},{6,7},{4,6},{2,4},{0,2},{9,8},{11,9},{13,1... | collective-permute-start | bytes 1400840 | tf_op jit(solution)/shard_map/ppermute | solution.py:532
  80.7 21.3 %collective-permute-start.15 = (bf16[96,2432]{1,0:T(8,128)(2,1)S(1)}, bf16[96,2432]{1,0:T(8,128)(2,1)S(1)}, u32[]{:S(2)}, u32[]{:S(2)}) collective-permute-start(bf16[96,2432]{1,0:T(8,128)(2,1)S(1)} %collective-permute-done.3.refs_1_), channel_id=1, source_target_pairs={{1,3},{3,5},{5,7},{7,6},{6,4},{4,2},{2,0},{0,1},{9,11},{11,13},{13... | collective-permute-start | bytes 1400840 | tf_op jit(solution)/shard_map/ppermute | solution.py:532
  81.4 30.0 %collective-permute-start.11 = (bf16[96,2432]{1,0:T(8,128)(2,1)S(1)}, bf16[96,2432]{1,0:T(8,128)(2,1)S(1)}, u32[]{:S(2)}, u32[]{:S(2)}) collective-permute-start(bf16[96,2432]{1,0:T(8,128)(2,1)S(1)} %get-tuple-element.79.refs_0_), channel_id=1, source_target_pairs={{1,0},{3,1},{5,3},{7,5},{6,7},{4,6},{2,4},{0,2},{9,8},{11,9},{13,1... | collective-permute-start | bytes 1400840 | tf_op jit(solution)/shard_map/ppermute | solution.py:532
  91.4 21.8 %collective-permute-start.4 = (bf16[96,2432]{1,0:T(8,128)(2,1)S(1)}, bf16[96,2432]{1,0:T(8,128)(2,1)S(1)}, u32[]{:S(2)}, u32[]{:S(2)}) collective-permute-start(bf16[96,2432]{1,0:T(8,128)(2,1)S(1)} %get-tuple-element.79.refs_0_), channel_id=1, source_target_pairs={{1,3},{3,5},{5,7},{7,6},{6,4},{4,2},{2,0},{0,1},{9,11},{11,13},{13... | collective-permute-start | bytes 1400840 | tf_op jit(solution)/shard_map/ppermute | solution.py:532
  93.3 38.5 %copy-start.3 = (bf16[96,2432]{1,0:T(8,128)(2,1)S(1)}, bf16[96,2432]{1,0:T(8,128)(2,1)}, u32[]{:S(2)}) copy-start(bf16[96,2432]{1,0:T(8,128)(2,1)} %pack.4.refs_0_) | copy-start | bytes 1400836
  93.3 9.5 %collective-permute-start.28 = (bf16[8,96,128]{2,1,0:T(8,128)(2,1)S(1)}, bf16[8,96,128]{2,1,0:T(8,128)(2,1)S(1)}, u32[]{:S(2)}, u32[]{:S(2)}) collective-permute-start(bf16[8,96,128]{2,1,0:T(8,128)(2,1)S(1)} %collect.1.refs_11_), channel_id=1, source_target_pairs={{0,24},{1,25},{2,26},{3,27},{4,28},{5,29},{6,30},{7,31}} | collective-permute-start | bytes 589832 | tf_op jit(solution)/shard_map/ppermute | solution.py:569
  101.4 3.2 %collective-permute-start.29 = (bf16[8,96,128]{2,1,0:T(8,128)(2,1)S(1)}, bf16[8,96,128]{2,1,0:T(8,128)(2,1)S(1)}, u32[]{:S(2)}, u32[]{:S(2)}) collective-permute-start(bf16[8,96,128]{2,1,0:T(8,128)(2,1)S(1)} %collect.1.refs_11_), channel_id=1, source_target_pairs={{8,24},{9,25},{10,26},{11,27},{12,28},{13,29},{14,30},{15,31}} | collective-permute-start | bytes 589832 | tf_op jit(solution)/shard_map/ppermute | solution.py:569
  102.1 11.4 %collective-permute-start.30 = (bf16[8,96,128]{2,1,0:T(8,128)(2,1)S(1)}, bf16[8,96,128]{2,1,0:T(8,128)(2,1)S(1)}, u32[]{:S(2)}, u32[]{:S(2)}) collective-permute-start(bf16[8,96,128]{2,1,0:T(8,128)(2,1)S(1)} %collect.1.refs_11_), channel_id=1, source_target_pairs={{16,24},{17,25},{18,26},{19,27},{20,28},{21,29},{22,30},{23,31}} | collective-permute-start | bytes 589832 | tf_op jit(solution)/shard_map/ppermute | solution.py:569
  102.8 18.5 %collective-permute-start.16 = (bf16[96,2432]{1,0:T(8,128)(2,1)S(1)}, bf16[96,2432]{1,0:T(8,128)(2,1)S(1)}, u32[]{:S(2)}, u32[]{:S(2)}) collective-permute-start(bf16[96,2432]{1,0:T(8,128)(2,1)S(1)} %collective-permute-done.15.refs_2_), channel_id=1, source_target_pairs={{1,3},{3,5},{5,7},{7,6},{6,4},{4,2},{2,0},{0,1},{9,11},{11,13},{13... | collective-permute-start | bytes 1400840 | tf_op jit(solution)/shard_map/ppermute | solution.py:532
  104.6 16.8 %collective-permute-start.19 = (bf16[96,2432]{1,0:T(8,128)(2,1)S(1)}, bf16[96,2432]{1,0:T(8,128)(2,1)S(1)}, u32[]{:S(2)}, u32[]{:S(2)}) collective-permute-start(bf16[96,2432]{1,0:T(8,128)(2,1)S(1)} %collective-permute-done.18.refs_6_), channel_id=1, source_target_pairs={{1,0},{3,1},{5,3},{7,5},{6,7},{4,6},{2,4},{0,2},{9,8},{11,9},{13,1... | collective-permute-start | bytes 1400840 | tf_op jit(solution)/shard_map/ppermute | solution.py:532
  111.4 18.4 %collective-permute-start.12 = (bf16[96,2432]{1,0:T(8,128)(2,1)S(1)}, bf16[96,2432]{1,0:T(8,128)(2,1)S(1)}, u32[]{:S(2)}, u32[]{:S(2)}) collective-permute-start(bf16[96,2432]{1,0:T(8,128)(2,1)S(1)} %collective-permute-done.11.refs_4_), channel_id=1, source_target_pairs={{1,0},{3,1},{5,3},{7,5},{6,7},{4,6},{2,4},{0,2},{9,8},{11,9},{13,1... | collective-permute-start | bytes 1400840 | tf_op jit(solution)/shard_map/ppermute | solution.py:532
  113.2 18.1 %collective-permute-start.5 = (bf16[96,2432]{1,0:T(8,128)(2,1)S(1)}, bf16[96,2432]{1,0:T(8,128)(2,1)S(1)}, u32[]{:S(2)}, u32[]{:S(2)}) collective-permute-start(bf16[96,2432]{1,0:T(8,128)(2,1)S(1)} %collective-permute-done.4.refs_1_), channel_id=1, source_target_pairs={{1,3},{3,5},{5,7},{7,6},{6,4},{4,2},{2,0},{0,1},{9,11},{11,13},{13... | collective-permute-start | bytes 1400840 | tf_op jit(solution)/shard_map/ppermute | solution.py:532
  121.4 19.9 %collective-permute-start.17 = (bf16[96,2432]{1,0:T(8,128)(2,1)S(1)}, bf16[96,2432]{1,0:T(8,128)(2,1)S(1)}, u32[]{:S(2)}, u32[]{:S(2)}) collective-permute-start(bf16[96,2432]{1,0:T(8,128)(2,1)S(1)} %collective-permute-done.16.refs_3_), channel_id=1, source_target_pairs={{1,3},{3,5},{5,7},{7,6},{6,4},{4,2},{2,0},{0,1},{9,11},{11,13},{13... | collective-permute-start | bytes 1400840 | tf_op jit(solution)/shard_map/ppermute | solution.py:532
  129.8 11.5 %collective-permute-start.13 = (bf16[96,2432]{1,0:T(8,128)(2,1)S(1)}, bf16[96,2432]{1,0:T(8,128)(2,1)S(1)}, u32[]{:S(2)}, u32[]{:S(2)}) collective-permute-start(bf16[96,2432]{1,0:T(8,128)(2,1)S(1)} %collective-permute-done.12.refs_5_), channel_id=1, source_target_pairs={{1,0},{3,1},{5,3},{7,5},{6,7},{4,6},{2,4},{0,2},{9,8},{11,9},{13,1... | collective-permute-start | bytes 1400840 | tf_op jit(solution)/shard_map/ppermute | solution.py:532
  131.3 18.5 %collective-permute-start.6 = (bf16[96,2432]{1,0:T(8,128)(2,1)S(1)}, bf16[96,2432]{1,0:T(8,128)(2,1)S(1)}, u32[]{:S(2)}, u32[]{:S(2)}) collective-permute-start(bf16[96,2432]{1,0:T(8,128)(2,1)S(1)} %collective-permute-done.5.refs_2_), channel_id=1, source_target_pairs={{1,3},{3,5},{5,7},{7,6},{6,4},{4,2},{2,0},{0,1},{9,11},{11,13},{13... | collective-permute-start | bytes 1400840 | tf_op jit(solution)/shard_map/ppermute | solution.py:532
  141.3 9.8 %collective-permute-start.14 = (bf16[96,2432]{1,0:T(8,128)(2,1)S(1)}, bf16[96,2432]{1,0:T(8,128)(2,1)S(1)}, u32[]{:S(2)}, u32[]{:S(2)}) collective-permute-start(bf16[96,2432]{1,0:T(8,128)(2,1)S(1)} %collective-permute-done.13.refs_6_), channel_id=1, source_target_pairs={{1,0},{3,1},{5,3},{7,5},{6,7},{4,6},{2,4},{0,2},{9,8},{11,9},{13,1... | collective-permute-start | bytes 1400840 | tf_op jit(solution)/shard_map/ppermute | solution.py:532
  155.7 3.0 %collective-permute-start.31 = (bf16[21,128,128]{2,1,0:T(8,128)(2,1)S(1)}, bf16[21,128,128]{2,1,0:T(8,128)(2,1)S(1)}, u32[]{:S(2)}, u32[]{:S(2)}) collective-permute-start(bf16[21,128,128]{2,1,0:T(8,128)(2,1)S(1)} %get-tuple-element.128), channel_id=1, source_target_pairs={{24,16},{25,17},{26,18},{27,19},{28,20},{29,21},{30,22},{31,23}} | collective-permute-start | bytes 2064392 | tf_op jit(solution)/shard_map/ppermute | solution.py:591
  160.9 5.3 %collective-permute-start.32 = (bf16[21,128,128]{2,1,0:T(8,128)(2,1)S(1)}, bf16[21,128,128]{2,1,0:T(8,128)(2,1)S(1)}, u32[]{:S(2)}, u32[]{:S(2)}) collective-permute-start(bf16[21,128,128]{2,1,0:T(8,128)(2,1)S(1)} %hop.2), channel_id=1, source_target_pairs={{16,8},{17,9},{18,10},{19,11},{20,12},{21,13},{22,14},{23,15}} | collective-permute-start | bytes 2064392 | tf_op jit(solution)/shard_map/ppermute | solution.py:591
  168.5 10.1 %collective-permute-start.33 = (bf16[21,128,128]{2,1,0:T(8,128)(2,1)S(1)}, bf16[21,128,128]{2,1,0:T(8,128)(2,1)S(1)}, u32[]{:S(2)}, u32[]{:S(2)}) collective-permute-start(bf16[21,128,128]{2,1,0:T(8,128)(2,1)S(1)} %hop.3), channel_id=1, source_target_pairs={{8,0},{9,1},{10,2},{11,3},{12,4},{13,5},{14,6},{15,7}} | collective-permute-start | bytes 2064392 | tf_op jit(solution)/shard_map/ppermute | solution.py:591
